TPU v7x, 32 devices: a whole 2x2x4 slice. The times are simulated.
32 devices in a mesh: dp: 8 (over z, x), ctx: 4 (over y, core).
Axes of the slice: x: 2, y: 2, z: 4, core: 2. Of those that a mesh axis runs over, the one named last changes fastest.
Arguments:
- tokens: float32 [8, 1024, 1024], P('dp', 'ctx'), may hold values from -6 to 6
- segment_ids: int32 [8, 1024], P('dp'), may hold values from 0 to 6, as said below
- cotangent: float32 [8, 1024, 1024], P('dp', 'ctx'), may hold values from -12 to 12
- in_weight: float32 [1024, 4352], P('dp'), may hold values from -0.1875 to 0.1875
- dt_weight: float32 [32, 1024], P(None, 'dp'), may hold values from -0.1875 to 0.1875
- out_weight: float32 [2048, 1024], P('dp'), may hold values from -0.125 to 0.125
- conv_params: float32 [5, 2304], P(None, 'dp'), may hold values from -0.5 to 0.5
- gains: float32 [3072], P('dp'), may hold values from 0.5 to 1.5
- head_params: float32 [3, 32], replicated, may hold values from -9 to 1.5
- in_first: float32 [1024, 4352], P('dp')
- in_second: float32 [1024, 4352], P('dp'), as said below
- dt_first: float32 [32, 1024], P(None, 'dp')
- dt_second: float32 [32, 1024], P(None, 'dp'), as said below
- out_first: float32 [2048, 1024], P('dp')
- out_second: float32 [2048, 1024], P('dp'), as said below
- conv_first: float32 [5, 2304], P(None, 'dp')
- conv_second: float32 [5, 2304], P(None, 'dp'), as said below
- gain_first: float32 [3072], P('dp')
- gain_second: float32 [3072], P('dp'), as said below
- head_first: float32 [3, 32], replicated
- head_second: float32 [3, 32], replicated, as said below
Outputs:
- block_output: float32 [8, 1024, 1024], P('dp', 'ctx')
- input_grad: float32 [8, 1024, 1024], P('dp', 'ctx')
- in_weight_new: float32 [1024, 4352], P('dp')
- in_first_new: float32 [1024, 4352], P('dp')
- in_second_new: float32 [1024, 4352], P('dp')
- dt_weight_new: float32 [32, 1024], P(None, 'dp')
- dt_first_new: float32 [32, 1024], P(None, 'dp')
- dt_second_new: float32 [32, 1024], P(None, 'dp')
- out_weight_new: float32 [2048, 1024], P('dp')
- out_first_new: float32 [2048, 1024], P('dp')
- out_second_new: float32 [2048, 1024], P('dp')
- conv_params_new: float32 [5, 2304], P(None, 'dp')
- conv_first_new: float32 [5, 2304], P(None, 'dp')
- conv_second_new: float32 [5, 2304], P(None, 'dp')
- gains_new: float32 [3072], P('dp')
- gain_first_new: float32 [3072], P('dp')
- gain_second_new: float32 [3072], P('dp')
- head_params_new: float32 [3, 32], replicated
- head_first_new: float32 [3, 32], replicated
- head_second_new: float32 [3, 32], replicated
Inputs may be any that keep to these rules, and one draw needn't show every extreme that they name: `segment_ids`: along each row the ids never fall; in each row one document starts within the first 256 positions and ends within the last 256. `in_second`: Positive. `dt_second`: Positive. `out_second`: Positive. `conv_second`: Positive. `gain_second`: Positive. `head_second`: Positive.
All inputs are finite; a program needn't handle non-finite values.
Results may differ from a plain program's by a relative error of at most 0.009.
The roundings to bfloat16 on the way count: a program that leaves them out, or rounds other values in their place, can miss the bound.
Values may be sent and summed in bfloat16 or wider, within the bound.
No kernel may reach another device: no remote copies, remote signals or barrier semaphores. Data moves between devices by JAX's collectives and lax.ppermute only.
A program may use at most 256 MiB of HBM per device.

v0:
```python
import jax
import jax.numpy as jnp
from jax import lax
from jax.sharding import PartitionSpec as P

INNER = 2048
HEADS = 32
HEAD_DIM = 64
STATE = 128
CONV = 4
STEP = 10


HIGHEST = lax.Precision.HIGHEST
NORM_EPS = 1e-05
BETA_ONE = 0.9
BETA_TWO = 0.95
ADAM_EPS = 1e-08
WEIGHT_DECAY = 0.1
block_span = 64


def shifted(value, axis, steps):
    count = lax.axis_size(axis)
    first, last = (max(0, -steps), min(count, count - steps))
    return lax.ppermute(value, axis, [(source, source + steps) for source in range(first, last)])


def prefix(value, axis, join, neutral, backward):
    count, mine = (lax.axis_size(axis), lax.axis_index(axis))
    pieces = jax.tree.map(lambda part: lax.all_gather(part, axis), value)
    if backward:
        pieces = jax.tree.map(lambda part: part[::-1], pieces)
        mine = count - 1 - mine
    total = jax.tree.map(
        lambda part, zero: jnp.full_like(part, 0) + jnp.asarray(zero, part.dtype), value, neutral
    )

    def hop(position, total):
        longer = join(total, jax.tree.map(lambda part: part[position], pieces))
        return jax.tree.map(lambda new, old: jnp.where(position < mine, new, old), longer, total)

    return lax.fori_loop(0, count - 1, hop, total)


def rounded(value):
    return value + lax.stop_gradient(value.astype(jnp.bfloat16).astype(jnp.float32) - value)


def pre_norm(block_in, gain_pre):
    return (
        block_in
        * lax.rsqrt(jnp.mean(block_in * block_in, axis=-1, keepdims=True) + NORM_EPS)
        * gain_pre
    )


def prepare(conv_in, edge_rows, step_raw, conv_weights, head_rows, seg_ext):
    piece_len = conv_in.shape[1]
    joined = jnp.concatenate([edge_rows, conv_in], axis=1)
    seg_here = seg_ext[:, CONV - 1 :]
    conv_sum = conv_weights[CONV]
    for tap_index in range(CONV):
        same_doc = (seg_ext[:, tap_index : tap_index + piece_len] == seg_here)[:, :, None]
        conv_sum = conv_sum + conv_weights[tap_index] * jnp.where(
            same_doc, joined[:, tap_index : tap_index + piece_len], 0.0
        )
    mixed_out = rounded(jax.nn.silu(conv_sum))
    head_values = mixed_out[:, :, :INNER].reshape(mixed_out.shape[0], piece_len, HEADS, HEAD_DIM)
    write_map = mixed_out[:, :, INNER : INNER + STATE]
    read_map = mixed_out[:, :, INNER + STATE :]
    step_size = jax.nn.softplus(step_raw + head_rows[1])
    log_decay = jnp.cumsum(-step_size * jnp.exp(head_rows[0]), axis=1)
    tail_scale = (
        jnp.where(
            (seg_here == seg_here[:, -1:])[:, :, None],
            jnp.exp(log_decay[:, -1:, :] - log_decay),
            0.0,
        )
        * step_size
    )
    local_state = jnp.einsum(
        "sqhp,sqn->shpn", tail_scale[:, :, :, None] * head_values, write_map, precision=HIGHEST
    )
    carry_keep = jnp.where(
        (seg_here[:, -1] == seg_ext[:, CONV - 2])[:, None], jnp.exp(log_decay[:, -1, :]), 0.0
    )
    return ((carry_keep, local_state), (head_values, write_map, read_map, step_size, log_decay))


def mix_tokens(prepared, state_in, gate_half, gain_gate, skip_gain, seg_ext):
    head_values, write_map, read_map, step_size, log_decay = prepared
    seg_here = seg_ext[:, CONV - 1 :]
    seq_count, piece_len = seg_here.shape
    span = min(block_span, piece_len)
    count = piece_len // span

    def split(value):
        return value.reshape((seq_count, count, span) + value.shape[2:])

    values_b = split(head_values)
    write_b = split(write_map)
    read_b = split(read_map)
    step_b = split(step_size)
    decay_b = split(log_decay)
    seg_b = split(seg_here)
    positions = jnp.arange(span)
    visible = (
        (seg_b[:, :, :, None] == seg_b[:, :, None, :]) & (positions[:, None] >= positions[None, :])
    )[:, :, None]
    decay_rows = jnp.moveaxis(decay_b, 3, 2)
    log_gap = decay_rows[:, :, :, :, None] - decay_rows[:, :, :, None, :]
    decay_map = jnp.where(visible, jnp.exp(jnp.where(visible, log_gap, 0.0)), 0.0)
    scores = jnp.einsum("sbtn,sbun->sbtu", read_b, write_b, precision=HIGHEST)
    weights = scores[:, :, None] * decay_map * jnp.moveaxis(step_b, 3, 2)[:, :, :, None, :]
    inner_out = jnp.einsum("sbhtu,sbuhp->sbthp", weights, values_b, precision=HIGHEST)
    last_decay = decay_b[:, :, -1, :]
    last_seg = seg_b[:, :, -1]
    tail = (
        jnp.where(
            (seg_b == last_seg[:, :, None])[:, :, :, None],
            jnp.exp(last_decay[:, :, None, :] - decay_b),
            0.0,
        )
        * step_b
    )
    block_state = jnp.einsum(
        "sbqhp,sbqn->sbhpn", tail[:, :, :, :, None] * values_b, write_b, precision=HIGHEST
    )
    ref_decay = jnp.concatenate([jnp.zeros_like(last_decay[:, :1]), last_decay[:, :-1]], axis=1)
    ref_seg = jnp.concatenate([seg_ext[:, CONV - 2 : CONV - 1], last_seg[:, :-1]], axis=1)
    keep = jnp.where((last_seg == ref_seg)[:, :, None], jnp.exp(last_decay - ref_decay), 0.0)
    starts = []
    current = state_in
    for index in range(count):
        starts.append(current)
        current = keep[:, index, :, None, None] * current + block_state[:, index]
    start_states = jnp.stack(starts, axis=1)
    enter = jnp.where(
        (seg_b == ref_seg[:, :, None])[:, :, :, None],
        jnp.exp(decay_b - ref_decay[:, :, None, :]),
        0.0,
    )
    inner_out = inner_out + enter[:, :, :, :, None] * jnp.einsum(
        "sbtn,sbhpn->sbthp", read_b, start_states, precision=HIGHEST
    )
    inner_out = (
        inner_out.reshape(seq_count, piece_len, HEADS, HEAD_DIM) + skip_gain[:, None] * head_values
    )
    gated_out = inner_out.reshape(gate_half.shape) * jax.nn.silu(gate_half)
    return (
        gated_out
        * lax.rsqrt(jnp.mean(gated_out * gated_out, axis=-1, keepdims=True) + NORM_EPS)
        * gain_gate
    )


def chain_step(earlier, later):
    return (earlier[0] * later[0], later[0][:, :, None, None] * earlier[1] + later[1])


def adam_step(weight, moment_one, second, gradient, step_rate, decay_rate):
    moment_new = BETA_ONE * moment_one + (1.0 - BETA_ONE) * gradient
    second_new = BETA_TWO * second + (1.0 - BETA_TWO) * gradient * gradient
    first_hat = moment_new / (1.0 - BETA_ONE**STEP)
    second_hat = second_new / (1.0 - BETA_TWO**STEP)
    weight_new = weight - step_rate * (
        first_hat / (jnp.sqrt(second_hat) + ADAM_EPS) + decay_rate * weight
    )
    return (weight_new, moment_new, second_new)


def shards(
    tokens,
    segment_ids,
    cotangent,
    in_weight,
    dt_weight,
    out_weight,
    conv_params,
    gains,
    head_params,
    in_first,
    in_second,
    dt_first,
    dt_second,
    out_first,
    out_second,
    conv_first,
    conv_second,
    gain_first,
    gain_second,
    head_first,
    head_second,
):
    seq_count, piece_len, model_width = tokens.shape
    w_in, w_dt, w_out, conv_low, gain_low = (
        lax.all_gather(in_weight.astype(jnp.bfloat16), "dp", axis=0, tiled=True),
        lax.all_gather(dt_weight.astype(jnp.bfloat16), "dp", axis=1, tiled=True),
        lax.all_gather(out_weight.astype(jnp.bfloat16), "dp", axis=0, tiled=True),
        lax.all_gather(conv_params.astype(jnp.bfloat16), "dp", axis=1, tiled=True),
        lax.all_gather(gains.astype(jnp.bfloat16), "dp", axis=0, tiled=True),
    )
    conv_full = conv_low.astype(jnp.float32)
    gain_full = gain_low.astype(jnp.float32)
    padded_ids = jnp.concatenate(
        [jnp.full((seq_count, CONV - 1), -1, jnp.int32), segment_ids], axis=1
    )
    seg_ext = lax.dynamic_slice_in_dim(
        padded_ids, lax.axis_index("ctx") * piece_len, piece_len + CONV - 1, 1
    )
    hidden, pre_pull = jax.vjp(pre_norm, tokens, gain_full[:model_width])
    hidden_low = hidden.astype(jnp.bfloat16)
    projected = jnp.einsum(
        "sqd,dk->sqk", hidden_low, w_in, preferred_element_type=jnp.float32
    ).astype(jnp.bfloat16)
    step_raw = jnp.einsum("sqd,hd->sqh", hidden_low, w_dt, preferred_element_type=jnp.float32)
    conv_low_in = projected[:, :, INNER:]
    edge_rows = shifted(conv_low_in[:, piece_len - CONV + 1 :, :], "ctx", 1)

    def prepare_here(conv_in, edge_in, raw_steps, conv_weights, head_rows):
        return prepare(conv_in, edge_in, raw_steps, conv_weights, head_rows, seg_ext)

    (summary, prepared), prep_pull = jax.vjp(
        prepare_here,
        conv_low_in.astype(jnp.float32),
        edge_rows.astype(jnp.float32),
        step_raw,
        conv_full,
        head_params,
    )
    carry_keep, local_state = summary
    identity_pair = (jnp.ones_like(carry_keep), jnp.zeros_like(local_state))
    state_in = prefix((carry_keep, local_state), "ctx", chain_step, identity_pair, False)[1]

    def mix_here(parts, state_now, gate_half, gain_gate, skip_gain):
        return mix_tokens(parts, state_now, gate_half, gain_gate, skip_gain, seg_ext)

    normed, mix_pull = jax.vjp(
        mix_here,
        prepared,
        state_in,
        projected[:, :, :INNER].astype(jnp.float32),
        gain_full[model_width:],
        head_params[2],
    )
    normed_low = normed.astype(jnp.bfloat16)
    block_output = tokens + jnp.einsum(
        "sqk,kd->sqd", normed_low, w_out, preferred_element_type=jnp.float32
    )
    cot_low = cotangent.astype(jnp.bfloat16)
    out_grad = jnp.einsum("sqk,sqd->kd", normed_low, cot_low, preferred_element_type=jnp.float32)
    normed_grad = jnp.einsum("sqd,kd->sqk", cot_low, w_out, preferred_element_type=jnp.float32)
    prep_grad, direct_grad, gate_grad, gain_gate_grad, skip_grad = mix_pull(normed_grad)
    state_out_grad = prefix((carry_keep, direct_grad), "ctx", chain_step, identity_pair, True)[1]
    keep_grad = jnp.sum(state_out_grad * state_in, axis=(2, 3))
    conv_in_grad, edge_grad, raw_grad, conv_grad, head_grad = prep_pull(
        ((keep_grad, state_out_grad), prep_grad)
    )
    edge_back = shifted(edge_grad, "ctx", -1)
    conv_in_grad = conv_in_grad.at[:, piece_len - CONV + 1 :, :].add(edge_back)
    proj_grad = jnp.concatenate([gate_grad, conv_in_grad], axis=2).astype(jnp.bfloat16)
    raw_low = raw_grad.astype(jnp.bfloat16)
    hidden_grad = jnp.einsum("sqk,dk->sqd", proj_grad, w_in, preferred_element_type=jnp.float32)
    hidden_grad = hidden_grad + jnp.einsum(
        "sqh,hd->sqd", raw_low, w_dt, preferred_element_type=jnp.float32
    )
    input_part, gain_pre_grad = pre_pull(hidden_grad)
    input_grad = cotangent + input_part
    dt_grad = jnp.einsum("sqh,sqd->hd", raw_low, hidden_low, preferred_element_type=jnp.float32)
    gain_grad = jnp.concatenate([gain_pre_grad, gain_gate_grad], axis=0)
    head_total = head_grad + jnp.stack(
        [jnp.zeros_like(skip_grad), jnp.zeros_like(skip_grad), skip_grad]
    )
    head_sum = lax.psum(head_total, ("dp", "ctx"))
    in_part = lax.psum_scatter(
        jnp.einsum("sqd,sqk->dk", hidden_low, proj_grad, preferred_element_type=jnp.float32),
        "dp",
        scatter_dimension=0,
        tiled=True,
    )
    dt_part, out_part, conv_part, gain_part = (
        lax.psum_scatter(dt_grad, "dp", scatter_dimension=1, tiled=True),
        lax.psum_scatter(out_grad, "dp", scatter_dimension=0, tiled=True),
        lax.psum_scatter(conv_grad, "dp", scatter_dimension=1, tiled=True),
        lax.psum_scatter(gain_grad, "dp", scatter_dimension=0, tiled=True),
    )
    in_total, dt_total, out_total, conv_total, gain_total = lax.psum(
        (in_part, dt_part, out_part, conv_part, gain_part), "ctx"
    )
    in_new = adam_step(in_weight, in_first, in_second, in_total, 0.03, WEIGHT_DECAY)
    dt_new = adam_step(dt_weight, dt_first, dt_second, dt_total, 0.03, WEIGHT_DECAY)
    out_new = adam_step(out_weight, out_first, out_second, out_total, 0.02, WEIGHT_DECAY)
    conv_new = adam_step(conv_params, conv_first, conv_second, conv_total, 0.3, 0.0)
    gain_new = adam_step(gains, gain_first, gain_second, gain_total, 0.5, 0.0)
    head_new = adam_step(head_params, head_first, head_second, head_sum, 2.0, 0.0)
    return (
        block_output,
        input_grad,
        in_new[0],
        in_new[1],
        in_new[2],
        dt_new[0],
        dt_new[1],
        dt_new[2],
        out_new[0],
        out_new[1],
        out_new[2],
        conv_new[0],
        conv_new[1],
        conv_new[2],
        gain_new[0],
        gain_new[1],
        gain_new[2],
        head_new[0],
        head_new[1],
        head_new[2],
    )


def solution(mesh):
    return jax.shard_map(
        shards,
        mesh=mesh,
        in_specs=(
            P("dp", "ctx", None),
            P("dp", None),
            P("dp", "ctx", None),
            P("dp", None),
            P(None, "dp"),
            P("dp", None),
            P(None, "dp"),
            P("dp"),
            P(),
            P("dp", None),
            P("dp", None),
            P(None, "dp"),
            P(None, "dp"),
            P("dp", None),
            P("dp", None),
            P(None, "dp"),
            P(None, "dp"),
            P("dp"),
            P("dp"),
            P(),
            P(),
        ),
        out_specs=(
            P("dp", "ctx", None),
            P("dp", "ctx", None),
            P("dp", None),
            P("dp", None),
            P("dp", None),
            P(None, "dp"),
            P(None, "dp"),
            P(None, "dp"),
            P("dp", None),
            P("dp", None),
            P("dp", None),
            P(None, "dp"),
            P(None, "dp"),
            P(None, "dp"),
            P("dp"),
            P("dp"),
            P("dp"),
            P(),
            P(),
            P(),
        ),
        check_vma=False,
    )
```

profile of v0, /device:TPU:0, one launch (start us, length us, event | category | flops | bytes accessed | tf_op | source)
XLA Modules:
  0.0 1018.6 jit_solution(1033067762730447475)
XLA Ops:
  7.3 2.8 convert_element_type.64
  10.3 28.1 %all-gather.2 = bf16[8,1,384]{2,1,0:T(2,128)(2,1)S(1)} all-gather(bf16[1,1,384]{2,1,0:T(2,128)(2,1)S(1)} %reshape.1101), channel_id=1, replica_groups=mesh['dp'=8,'ctx'=4] {'dp'}, dimensions={0}, use_global_device_ids=true | all-gather | bytes 6912 | tf_op jit(solution)/shard_map/all_gather | solution.py:202
  39.0 31.0 %all-gather.1 = bf16[8,288,5]{1,2,0:T(8,128)(2,1)S(1)} all-gather(bf16[1,288,5]{1,2,0:T(8,128)(2,1)S(1)} %convert_bitcast_fusion), channel_id=1, replica_groups=mesh['dp'=8,'ctx'=4] {'dp'}, dimensions={0}, use_global_device_ids=true | all-gather | bytes 25920 | tf_op jit(solution)/shard_map/all_gather | solution.py:201
  70.1 26.9 %all_gather.34 = bf16[32,1024]{1,0:T(8,128)(2,1)S(1)} all-gather(bf16[32,128]{1,0:T(8,128)(2,1)S(1)} %convert_element_type.71), channel_id=1, replica_groups=mesh['dp'=8,'ctx'=4] {'dp'}, dimensions={1}, use_global_device_ids=true | all-gather | bytes 73728 | tf_op jit(solution)/shard_map/all_gather | solution.py:199
  105.3 1.8 copy.250
  107.3 39.4 %all-gather.8.cloned.1.call-done = bf16[1024,4352]{1,0:T(8,128)(2,1)} async-done(((bf16[128,4352]{1,0:T(8,128)(2,1)}), bf16[1024,4352]{1,0:T(8,128)(2,1)}) %all-gather.8.cloned.1.call-update) | async-done | bytes 8912912 | tf_op jit(solution)/shard_map/all_gather | solution.py:198
  146.7 6.0 fusion.2
  155.0 3.7 subtract_add_fusion
  158.8 2.8 slice_multiply_fusion
  161.5 2.9 copy.251
  164.5 4.4 fusion.121
  178.6 7.7 all_gather.35
  190.8 4.9 reshape.1059
  196.3 12.4 %fusion.41 = f32[1,4,32,64,128]{4,3,2,1,0:T(8,128)} fusion(f32[4,64,128,1]{2,1,3,0:T(8,128)S(1)} %bitcast.464, f32[4,64,32,64]{3,2,1,0:T(8,128)} %reshape.1059, f32[4,64,32]{1,2,0:T(8,128)} %get-tuple-element.404), kind=kOutput, calls=%fused_computation.80 | convolution fusion | flops 805830656 | bytes 6455296 | tf_op jit(solution)/shard_map/jvp(sbqhp,sbqn->sbhpn)/dot_general | solution.py:127
  208.8 4.5 while.29
  213.4 2.4 fusion.99
  215.9 4.1 fusion.29
  220.0 2.0 copy-done.2
  222.0 11.8 %bitcast_add_fusion.3 = f32[1,4,64,32,64]{2,4,3,1,0:T(8,128)} fusion(f32[4,64,32,64]{1,3,2,0:T(8,128)S(1)} %fusion.29, f32[4,64,32]{1,2,0:T(8,128)S(1)} %copy-done.54, f32[4,32,64]{2,1,0:T(8,128)S(1)} %copy-done.51, f32[4,32,64]{2,1,0:T(8,128)S(1)} %copy-done.41, f32[4,64,64]{2,1,0:T(8,128)S(1)} %fusion.187, pred[4,64,64]{2,1,0:T(8,128)(4,1)S(1)} %copy-done.65, ...), kind=kOutput, calls=%fused_computation.10 | convolution fusion | flops 406323200 | bytes 6471680 | tf_op jit(solution)/shard_map/jvp(sbhtu,sbuhp->sbthp)/dot_general | solution.py:116
  233.8 6.2 copy.258
  240.0 4.9 reshape.1074
  245.0 3.4 multiply_reduce_fusion.8
  248.4 32.4 %all-gather.10.cloned.1.call-done = bf16[2048,1024]{1,0:T(8,128)(2,1)} async-done(((bf16[256,1024]{1,0:T(8,128)(2,1)}), bf16[2048,1024]{1,0:T(8,128)(2,1)}) %all-gather.10.cloned.1.call-update) | async-done | bytes 4194320 | tf_op jit(solution)/shard_map/all_gather | solution.py:200
  280.8 4.9 fusion.53
  285.7 4.5 multiply_reduce_fusion.7
  290.2 4.9 reshape.1077
  295.1 5.8 copy.259
  300.9 5.7 fusion.44
  306.7 2.3 slice_add_fusion
  310.1 6.1 fusion.114
  316.8 3.2 copy.272
  320.1 4.9 reshape.1087
  325.0 5.8 copy.270
  330.8 2.9 copy.266
  333.7 4.9 reshape.1078
  338.6 5.8 copy.261
  344.5 7.0 fusion.3
  351.5 6.5 bitcast_add_fusion.2
  358.0 5.5 copy.267
  363.5 5.8 reshape.1085
  369.4 10.0 fusion.86
  379.5 13.4 %fusion.40 = (f32[4,32,64]{2,1,0:T(8,128)}, f32[4,32,64]{2,1,0:T(8,128)}, f32[4,32,64]{2,1,0:T(8,128)}, f32[4,64,64]{2,1,0:T(8,128)S(1)}) fusion(f32[4,32,64]{2,1,0:T(8,128)S(1)} %copy-done.51, f32[4,32,64]{2,1,0:T(8,128)S(1)} %copy-done.41, f32[4,64,64]{2,1,0:T(8,128)S(1)} %copy-done.46, pred[4,64,64]{2,1,0:T(8,128)(4,1)S(1)} %copy-done.67, ...), kind=kOutput, calls=%fused_computation.79 | convolution fusion | flops 410476544 | bytes 4505600 | tf_op jit(solution)/shard_map/transpose(jvp(sbhtu,sbuhp->sbthp))/dot_general | solution.py:116
  393.2 6.4 fusion.89
  400.0 4.8 rev.7
  404.7 6.5 while.30
  411.2 6.9 fusion.54
  418.1 3.1 copy.268
  421.3 5.2 fusion.85
  426.5 5.6 multiply_reduce_fusion.6
  437.9 10.3 %fusion.81 = f32[1024,4352]{1,0:T(8,128)} fusion(bf16[256,1024]{1,0:T(8,128)(2,1)S(1)} %copy-done.26, bf16[256,2304]{1,0:T(8,128)(2,1)} %scatter-add.4, bf16[256,2048]{1,0:T(8,128)(2,1)} %get-tuple-element.388), kind=kOutput, calls=%fused_computation.118 | convolution fusion | flops 2286157824 | bytes 20578304 | tf_op jit(solution)/shard_map/sqd,sqk->dk/dot_general | solution.py:277
  450.9 4.9 multiply_reduce_fusion
  456.7 2.3 fusion.83
  467.2 2.5 reduce-window.16
  472.8 40.6 %psum.47 = f32[3,32]{1,0:T(4,128)S(1)} all-reduce(f32[3,32]{1,0:T(4,128)S(1)} %pad_add_fusion.6), channel_id=1, replica_groups=mesh['dp'=8,'ctx'=4] {'dp','ctx'}, use_global_device_ids=true, to_apply=%region_47.48 | all-reduce | flops 96 | bytes 768 | tf_op jit(solution)/shard_map/psum | solution.py:275
  515.4 282.0 %reduce-scatter.7.cloned.1.call-done = f32[128,4352]{1,0:T(8,128)} async-done(((f32[1024,4352]{1,0:T(8,128)}), f32[128,4352]{1,0:T(8,128)}) %reduce-scatter.7.cloned.1.call-update) | async-done | bytes 2228240 | tf_op jit(solution)/shard_map/reduce_scatter | solution.py:276
  797.5 7.7 fusion.102
  805.3 35.4 %all-reduce.27 = f32[3072]{0:T(1024)S(1)} all-reduce(f32[3072]{0:T(1024)S(1)} %pad_maximum_fusion.6), channel_id=7, replica_groups=mesh['dp'=8,'ctx'=4] {'dp'}, use_global_device_ids=true, to_apply=%region_41.42.clone | all-reduce | flops 3072 | bytes 24576
  840.8 2.5 fusion.95
  843.3 21.3 %reduce-scatter.13.cloned.1.call-done = f32[288,5]{1,0:T(8,128)} async-done(((f32[2304,5]{1,0:T(8,128)}), f32[288,5]{1,0:T(8,128)}) %reduce-scatter.13.cloned.1.call-update) | async-done | bytes 5776
  865.5 63.2 %reduce-scatter.9.cloned.1.call-done = f32[32,128]{1,0:T(8,128)} async-done(((f32[32,1024]{1,0:T(8,128)}), f32[32,128]{1,0:T(8,128)}) %reduce-scatter.9.cloned.1.call-update) | async-done | bytes 16400 | tf_op jit(solution)/shard_map/reduce_scatter | solution.py:283
  928.7 11.0 %all-reduce.28 = (f32[32,128]{1,0:T(8,128)S(1)}, f32[5,288]{1,0:T(8,128)S(1)}, f32[384]{0:T(512)S(1)}) all-reduce(f32[32,128]{1,0:T(8,128)} %reduce-scatter.9.cloned.1.call-done, f32[5,288]{1,0:T(8,128)S(1)} %copy.297, f32[384]{0:T(512)S(1)} %dynamic-slice.9), channel_id=1, replica_groups=mesh['dp'=8,'ctx'=4] {'ctx'}, use_global_device_ids=true, to_apply=%region_29.30 | all-reduce | flops 5920 | bytes 47360 | tf_op jit(solution)/shard_map/psum | solution.py:288
  941.6 59.5 %all-reduce.32.cloned.1.call-done = (f32[128,4352]{1,0:T(8,128)}, f32[256,1024]{1,0:T(8,128)}) async-done(((f32[128,4352]{1,0:T(8,128)}, f32[256,1024]{1,0:T(8,128)}), (f32[128,4352]{1,0:T(8,128)}, f32[256,1024]{1,0:T(8,128)})) %all-reduce.32.cloned.1.call-update) | async-done | bytes 3276816 | tf_op jit(solution)/shard_map/psum | solution.py:288
  1001.2 4.3 multiply_subtract_fusion.1
  1006.1 5.5 multiply_subtract_fusion
  (435 shorter events, 63.3 us)
Async XLA Ops:
  7.2 31.8 %copy-start.84 = (f32[5,288]{1,0:T(8,128)S(1)}, f32[5,288]{1,0:T(8,128)}, u32[]{:S(2)}) copy-start(f32[5,288]{1,0:T(8,128)} %param.33) | copy-start | bytes 17284
  7.2 89.7 %copy-start.13 = (f32[1,256,1024]{2,1,0:T(8,128)S(1)}, f32[1,256,1024]{2,1,0:T(8,128)}, u32[]{:S(2)}) copy-start(f32[1,256,1024]{2,1,0:T(8,128)} %param.27) | copy-start | bytes 3145732
  7.2 89.9 %copy-start.124 = (f32[3,32]{1,0:T(4,128)S(1)}, f32[3,32]{1,0:T(4,128)}, u32[]{:S(2)}) copy-start(f32[3,32]{1,0:T(4,128)} %param.35) | copy-start | bytes 1156
  7.2 139.4 %all-gather.8.cloned.1.call-start = ((), (), s32[]{:S(2)}) async-start(), calls=%async_computation.4 | async-start | bytes 10027008 | tf_op jit(solution)/shard_map/all_gather | solution.py:198
  10.1 89.1 %copy-start.88 = (s32[1,1024]{1,0:T(1,128)S(1)}, s32[1,1024]{1,0:T(1,128)}, u32[]{:S(2)}) copy-start(s32[1,1024]{1,0:T(1,128)} %param.28) | copy-start | bytes 12292
  10.1 198.6 %all-gather.14.cloned.1.call-start = ((), (), s32[]{:S(2)}) async-start(), calls=%async_computation.10 | async-start | bytes 5242880 | tf_op jit(solution)/shard_map/all_gather | solution.py:31
  39.0 58.8 %copy-start.86 = (f32[1024]{0:T(1024)}, f32[1024]{0:T(1024)S(1)}, u32[]{:S(2)}) copy-start(f32[1024]{0:T(1024)S(1)} %slice.195) | copy-start | bytes 12292
  96.9 8.1 copy-start.57
  97.8 48.9 %copy-start.25 = (bf16[256,1024]{1,0:T(8,128)(2,1)}, bf16[256,1024]{1,0:T(8,128)(2,1)S(1)}, u32[]{:S(2)}) copy-start(bf16[256,1024]{1,0:T(8,128)(2,1)S(1)} %fusion.113) | copy-start | bytes 1572868
  98.1 9.0 copy-start.49
  104.2 50.7 %copy-start.106 = (pred[256]{0:T(512)(128)(4,1)}, pred[256]{0:T(512)(128)(4,1)S(1)}, u32[]{:S(2)}) copy-start(pred[256]{0:T(512)(128)(4,1)S(1)} %get-tuple-element.320) | copy-start | bytes 772
  104.2 50.7 %copy-start.108 = (pred[256]{0:T(512)(128)(4,1)}, pred[256]{0:T(512)(128)(4,1)S(1)}, u32[]{:S(2)}) copy-start(pred[256]{0:T(512)(128)(4,1)S(1)} %get-tuple-element.321) | copy-start | bytes 772
  104.2 65.8 %copy-start.42 = (f32[1,256,32]{1,2,0:T(8,128)}, f32[1,256,32]{1,2,0:T(8,128)S(1)}, u32[]{:S(2)}) copy-start(f32[1,256,32]{1,2,0:T(8,128)S(1)} %fusion.136) | copy-start | bytes 98308
  107.3 47.7 %copy-start.69 = (f32[2304]{0:T(1024)}, f32[2304]{0:T(1024)S(1)}, u32[]{:S(2)}) copy-start(f32[2304]{0:T(1024)S(1)} %get-tuple-element.314) | copy-start | bytes 27652
  107.3 47.7 %copy-start.71 = (f32[2304]{0:T(1024)}, f32[2304]{0:T(1024)S(1)}, u32[]{:S(2)}) copy-start(f32[2304]{0:T(1024)S(1)} %get-tuple-element.315) | copy-start | bytes 27652
  107.3 47.7 %copy-start.73 = (f32[2304]{0:T(1024)}, f32[2304]{0:T(1024)S(1)}, u32[]{:S(2)}) copy-start(f32[2304]{0:T(1024)S(1)} %get-tuple-element.316) | copy-start | bytes 27652
  107.3 47.7 %copy-start.75 = (f32[2304]{0:T(1024)}, f32[2304]{0:T(1024)S(1)}, u32[]{:S(2)}) copy-start(f32[2304]{0:T(1024)S(1)} %get-tuple-element.317) | copy-start | bytes 27652
  152.7 2.2 collective-permute-start
  158.8 36.9 %copy-start.5 = (f32[1,256,2304]{2,1,0:T(8,128)}, f32[1,256,2304]{2,1,0:T(8,128)S(1)}, u32[]{:S(2)}) copy-start(f32[1,256,2304]{2,1,0:T(8,128)S(1)} %get-tuple-element.386) | copy-start | bytes 7077892
  168.9 111.8 %all-gather.10.cloned.1.call-start = ((), (), s32[]{:S(2)}) async-start(), calls=%async_computation.5 | async-start | bytes 4718592 | tf_op jit(solution)/shard_map/all_gather | solution.py:200
  169.9 230.0 %all-gather.12.cloned.1.call-start = ((), (), s32[]{:S(2)}) async-start(), calls=%async_computation.6 | async-start | bytes 5242880 | tf_op jit(solution)/shard_map/all_gather | solution.py:31
  170.1 20.7 %copy-start.47 = (f32[1,4,64,32]{2,1,3,0:T(4,128)}, f32[1,4,64,32]{2,1,3,0:T(4,128)S(1)}, u32[]{:S(2)}) copy-start(f32[1,4,64,32]{2,1,3,0:T(4,128)S(1)} %reshape.1067) | copy-start | bytes 98308
  188.4 25.0 %copy-start.112 = (f32[32]{0:T(128)}, f32[32]{0:T(128)S(1)}, u32[]{:S(2)}) copy-start(f32[32]{0:T(128)S(1)} %get-tuple-element.419) | copy-start | bytes 388
  196.0 24.0 %copy-start.44 = (f32[4,64,64]{2,1,0:T(8,128)}, f32[4,64,64]{2,1,0:T(8,128)S(1)}, u32[]{:S(2)}) copy-start(f32[4,64,64]{2,1,0:T(8,128)S(1)} %fusion.187) | copy-start | bytes 196612
  196.3 12.5 %copy-start.123 = (f32[4,1,32]{2,1,0:T(1,128)S(1)}, f32[4,1,32]{2,1,0:T(1,128)}, u32[]{:S(2)}) copy-start(f32[4,1,32]{2,1,0:T(1,128)} %all_gather.35) | copy-start | bytes 1540
  248.3 61.7 %copy-start = (f32[1,256,2048]{2,1,0:T(8,128)}, f32[1,256,2048]{2,1,0:T(8,128)S(1)}, u32[]{:S(2)}) copy-start(f32[1,256,2048]{2,1,0:T(8,128)S(1)} %get-tuple-element.380) | copy-start | bytes 6291460
  310.0 205.4 %reduce-scatter.11.cloned.1.call-start = ((), (), s32[]{:S(2)}) async-start(), calls=%async_computation.9 | async-start | bytes 9437184 | tf_op jit(solution)/shard_map/reduce_scatter | solution.py:284
  316.2 481.2 %reduce-scatter.7.cloned.1.call-start = ((), (), s32[]{:S(2)}) async-start(), calls=%async_computation.7 | async-start | bytes 20054016 | tf_op jit(solution)/shard_map/reduce_scatter | solution.py:276
  369.3 10.1 copy-start.4
  369.3 10.1 copy-start.16
  369.3 10.1 copy-start.46
  369.3 10.1 copy-start.67
  379.4 13.7 %copy-start.31 = (f32[1,1,32,64,128]{4,3,2,1,0:T(8,128)S(1)}, f32[1,1,32,64,128]{4,3,2,1,0:T(8,128)}, u32[]{:S(2)}) copy-start(f32[1,1,32,64,128]{4,3,2,1,0:T(8,128)} %get-tuple-element.377) | copy-start | bytes 3145732
  379.4 13.7 %copy-start.32 = (f32[1,1,32,64,128]{4,3,2,1,0:T(8,128)S(1)}, f32[1,1,32,64,128]{4,3,2,1,0:T(8,128)}, u32[]{:S(2)}) copy-start(f32[1,1,32,64,128]{4,3,2,1,0:T(8,128)} %get-tuple-element.378) | copy-start | bytes 3145732
  379.5 13.7 %copy-start.33 = (f32[1,1,32,64,128]{4,3,2,1,0:T(8,128)S(1)}, f32[1,1,32,64,128]{4,3,2,1,0:T(8,128)}, u32[]{:S(2)}) copy-start(f32[1,1,32,64,128]{4,3,2,1,0:T(8,128)} %get-tuple-element.389) | copy-start | bytes 3145732
  379.5 13.7 %copy-start.53 = (f32[4,64,32]{1,2,0:T(8,128)S(1)}, f32[4,64,32]{1,2,0:T(8,128)}, u32[]{:S(2)}) copy-start(f32[4,64,32]{1,2,0:T(8,128)} %get-tuple-element.404) | copy-start | bytes 98308
  433.1 3.3 collective-permute-start.1
  448.2 416.3 %reduce-scatter.13.cloned.1.call-start = ((), (), s32[]{:S(2)}) async-start(), calls=%async_computation.11 | async-start | bytes 1327104
  461.4 10.2 copy-start.103
  461.4 10.2 copy-start.105
  461.4 10.1 copy-start.127
  461.4 10.3 %copy-start.125 = (f32[3,32]{1,0:T(4,128)S(1)}, f32[3,32]{1,0:T(4,128)}, u32[]{:S(2)}) copy-start(f32[3,32]{1,0:T(4,128)} %param.35) | copy-start | bytes 1156
  461.5 10.3 %copy-start.27 = (bf16[256,1024]{1,0:T(8,128)(2,1)S(1)}, bf16[256,1024]{1,0:T(8,128)(2,1)}, u32[]{:S(2)}) copy-start(bf16[256,1024]{1,0:T(8,128)(2,1)} %copy-done.25) | copy-start | bytes 1572868
  463.5 9.3 copy-start.137
  463.5 50.0 %copy-start.133 = (f32[3,32]{1,0:T(4,128)S(1)}, f32[3,32]{1,0:T(4,128)}, u32[]{:S(2)}) copy-start(f32[3,32]{1,0:T(4,128)} %param.46) | copy-start | bytes 1156
  463.5 49.9 %copy-start.134 = (f32[3,32]{1,0:T(4,128)S(1)}, f32[3,32]{1,0:T(4,128)}, u32[]{:S(2)}) copy-start(f32[3,32]{1,0:T(4,128)} %param.47) | copy-start | bytes 1156
  463.6 50.6 %copy-start.58 = (bf16[32,1024]{1,0:T(8,128)(2,1)S(1)}, bf16[32,1024]{1,0:T(8,128)(2,1)}, u32[]{:S(2)}) copy-start(bf16[32,1024]{1,0:T(8,128)(2,1)} %copy-done.57) | copy-start | bytes 196612
  472.7 324.7 %copy-start.29 = (bf16[256,2048]{1,0:T(8,128)(2,1)S(1)}, bf16[256,2048]{1,0:T(8,128)(2,1)}, u32[]{:S(2)}) copy-start(bf16[256,2048]{1,0:T(8,128)(2,1)} %get-tuple-element.388) | copy-start | bytes 3145732
  472.7 324.7 %copy-start.87 = (f32[1024]{0:T(1024)S(1)}, f32[1024]{0:T(1024)}, u32[]{:S(2)}) copy-start(f32[1024]{0:T(1024)} %copy-done.86) | copy-start | bytes 12292
  472.7 324.7 %copy-start.101 = (f32[256]{0:T(256)S(1)}, f32[256]{0:T(256)}, u32[]{:S(2)}) copy-start(f32[256]{0:T(256)} %copy-done.100) | copy-start | bytes 3076
  472.7 456.0 %reduce-scatter.9.cloned.1.call-start = ((), (), s32[]{:S(2)}) async-start(), calls=%async_computation.8 | async-start | bytes 147456 | tf_op jit(solution)/shard_map/reduce_scatter | solution.py:283
  513.4 487.7 %all-reduce.32.cloned.1.call-start = ((), (), s32[]{:S(2)}) async-start(), calls=%async_computation.12 | async-start | bytes 6553600 | tf_op jit(solution)/shard_map/psum | solution.py:288
  797.4 43.3 %copy-start.99 = (f32[256]{0:T(256)S(1)}, f32[256]{0:T(256)}, u32[]{:S(2)}) copy-start(f32[256]{0:T(256)} %copy-done.98) | copy-start | bytes 3076
  797.4 43.3 %copy-start.17 = (f32[1,256,1024]{2,1,0:T(8,128)S(1)}, f32[1,256,1024]{2,1,0:T(8,128)}, u32[]{:S(2)}) copy-start(f32[1,256,1024]{2,1,0:T(8,128)} %param.29) | copy-start | bytes 3145732
  805.2 134.5 %copy-start.122 = (f32[384]{0:T(512)S(1)}, f32[384]{0:T(512)}, u32[]{:S(2)}) copy-start(f32[384]{0:T(512)} %param.34) | copy-start | bytes 4612
  805.2 134.5 %copy-start.135 = (f32[384]{0:T(512)S(1)}, f32[384]{0:T(512)}, u32[]{:S(2)}) copy-start(f32[384]{0:T(512)} %param.44) | copy-start | bytes 4612
  805.2 134.5 %copy-start.136 = (f32[384]{0:T(512)S(1)}, f32[384]{0:T(512)}, u32[]{:S(2)}) copy-start(f32[384]{0:T(512)} %param.45) | copy-start | bytes 4612
  805.2 135.1 %copy-start.85 = (f32[5,288]{1,0:T(8,128)S(1)}, f32[5,288]{1,0:T(8,128)}, u32[]{:S(2)}) copy-start(f32[5,288]{1,0:T(8,128)} %param.33) | copy-start | bytes 17284
  805.2 135.1 %copy-start.96 = (f32[5,288]{1,0:T(8,128)S(1)}, f32[5,288]{1,0:T(8,128)}, u32[]{:S(2)}) copy-start(f32[5,288]{1,0:T(8,128)} %param.42) | copy-start | bytes 17284
  805.2 135.1 %copy-start.97 = (f32[5,288]{1,0:T(8,128)S(1)}, f32[5,288]{1,0:T(8,128)}, u32[]{:S(2)}) copy-start(f32[5,288]{1,0:T(8,128)} %param.43) | copy-start | bytes 17284
  805.2 135.8 %copy-start.79 = (f32[32,128]{1,0:T(8,128)S(1)}, f32[32,128]{1,0:T(8,128)}, u32[]{:S(2)}) copy-start(f32[32,128]{1,0:T(8,128)} %param.31) | copy-start | bytes 49156
  805.2 135.7 %copy-start.94 = (f32[32,128]{1,0:T(8,128)S(1)}, f32[32,128]{1,0:T(8,128)}, u32[]{:S(2)}) copy-start(f32[32,128]{1,0:T(8,128)} %param.38) | copy-start | bytes 49156
  805.3 135.7 %copy-start.95 = (f32[32,128]{1,0:T(8,128)S(1)}, f32[32,128]{1,0:T(8,128)}, u32[]{:S(2)}) copy-start(f32[32,128]{1,0:T(8,128)} %param.39) | copy-start | bytes 49156
  805.3 195.9 %copy-start.35 = (f32[256,1024]{1,0:T(8,128)S(1)}, f32[256,1024]{1,0:T(8,128)}, u32[]{:S(2)}) copy-start(f32[256,1024]{1,0:T(8,128)} %param.32) | copy-start | bytes 3145732
  (86 other events, 373.8 us)
Sparse Core Ops, SparseCore 0:
  10.8 135.7 all-gather.7
  169.1 35.5 all-gather.13
  207.3 73.3 all-gather.9
  310.1 32.7 all-gather.11
  346.4 149.3 reduce-scatter.10
  500.1 297.2 reduce-scatter.6
  801.3 63.1 reduce-scatter.12
  868.4 60.2 reduce-scatter.8
  931.2 69.8 all-reduce.31
where the time goes:
time: 1030 us; the launch traced here: 1020 us
  waiting for transfers between devices  499 us (48%)
  blocking collectives  181 us (18%)
  matrix products  135 us (13%)
  local copies, waits for them, and re-layouts  109 us (11%)
  other arithmetic  73.8 us (7%)
  between operations  18.2 us (2%)
    reduce_scatter x1, waiting for transfers between devices, shards(): lax.psum_scatter(jnp.einsum('sqd,sqk->dk', hidden_low, proj_grad, preferr...  282 us
    reduce_scatter x1, waiting for transfers between devices, shards(): lax.psum_scatter(dt_grad, 'dp', scatter_dimension=1, tiled=True)  63.2 us
    psum x1, waiting for transfers between devices, shards(): lax.psum((in_part, dt_part, out_part, conv_part, gain_part), 'ctx')  59.5 us
    psum x1, blocking collectives, shards(): head_sum = lax.psum(head_total, ('dp', 'ctx'))  40.6 us
    all_gather x1, waiting for transfers between devices, shards(): lax.all_gather(in_weight.astype(jnp.bfloat16), 'dp', axis=0, tiled=True)  39.4 us
    unnamed x1, blocking collectives  35.4 us
    all_gather x1, waiting for transfers between devices, shards(): lax.all_gather(out_weight.astype(jnp.bfloat16), 'dp', axis=0, tiled=True)  32.4 us
    dot_general x3, matrix products, mix_tokens(): jnp.einsum('sbhtu,sbuhp->sbthp', weights, values_b, precision=HIGHEST)  31.6 us
  transfers between devices with their start and end apart: 11, of which 7 were waited for; matrix products, arithmetic and copies ran while one was open for 25% of the time, Pallas kernels for 0%

commit v1 on v0

v1 whole, which is shorter than its diff:
```python
import jax
import jax.numpy as jnp
from jax import lax
from jax.experimental import pallas as pl
from jax.experimental.pallas import tpu as pltpu
from jax.sharding import PartitionSpec as P

INNER = 2048
HEADS = 32
HEAD_DIM = 64
STATE = 128
CONV = 4
STEP = 10

F32 = jnp.float32
BF16 = jnp.bfloat16
HIGHEST = lax.Precision.HIGHEST
NORM_EPS = 1e-05
BETA_ONE = 0.9
BETA_TWO = 0.95
ADAM_EPS = 1e-08
WEIGHT_DECAY = 0.1
VMEM_LIMIT = 56 * 1024 * 1024


def nn(a, b, precision=None):
    return lax.dot_general(
        a, b, (((1,), (0,)), ((), ())), precision=precision, preferred_element_type=F32
    )


def nt(a, b, precision=None):
    return lax.dot_general(
        a, b, (((1,), (1,)), ((), ())), precision=precision, preferred_element_type=F32
    )


def tn(a, b, precision=None):
    return lax.dot_general(
        a, b, (((0,), (0,)), ((), ())), precision=precision, preferred_element_type=F32
    )


def halves(value):
    high = value.astype(BF16)
    return high, (value - high.astype(F32)).astype(BF16)


def spread(value, width):
    heads = value.shape[1]
    row = lax.broadcasted_iota(jnp.int32, (heads, width), 0)
    col = lax.broadcasted_iota(jnp.int32, (heads, width), 1)
    table = jnp.where(col // HEAD_DIM == row, 1.0, 0.0).astype(BF16)
    high, low = halves(value)
    return nn(high, table) + nn(low, table)


def gather_heads(value, heads):
    width = value.shape[1]
    row = lax.broadcasted_iota(jnp.int32, (width, heads), 0)
    col = lax.broadcasted_iota(jnp.int32, (width, heads), 1)
    table = jnp.where(row // HEAD_DIM == col, 1.0, 0.0).astype(BF16)
    high, low = halves(value)
    return nn(high, table) + nn(low, table)


def softplus(value):
    return jnp.maximum(value, 0.0) + jnp.log1p(jnp.exp(-jnp.abs(value)))


def sigmoid(value):
    return 1.0 / (1.0 + jnp.exp(-value))


def silu_grad(value):
    sig = sigmoid(value)
    return sig * (1.0 + value * (1.0 - sig))


def triangle(size, lower):
    row = lax.broadcasted_iota(jnp.int32, (size, size), 0)
    col = lax.broadcasted_iota(jnp.int32, (size, size), 1)
    keep = row >= col if lower else row <= col
    return jnp.where(keep, 1.0, 0.0).astype(F32)


def params(*semantics):
    return pltpu.CompilerParams(
        dimension_semantics=semantics or None, vmem_limit_bytes=VMEM_LIMIT
    )


def norm_kernel(tok_ref, gain_ref, hid_ref):
    tok = tok_ref[...]
    scale = lax.rsqrt(jnp.mean(tok * tok, axis=-1, keepdims=True) + NORM_EPS)
    hid_ref[...] = (tok * scale * gain_ref[...]).astype(BF16)


def scan_forward_kernel(
    perm_ref,
    hid_ref,
    w1_ref,
    wdt_ref,
    conv_ref,
    hrow_ref,
    hcol_ref,
    segc_ref,
    segr_ref,
    mixed_ref,
    convin_ref,
    convsum_ref,
    inner_ref,
    raw_ref,
    stepc_ref,
    logc_ref,
    stepr_ref,
    logr_ref,
    start_ref,
    ext_ref,
    seg_ref,
    state_ref,
):
    step = pl.program_id(0)
    span = hid_ref.shape[1]
    heads = wdt_ref.shape[0]
    width = heads * HEAD_DIM

    @pl.when(step == 0)
    def _():
        ext_ref[0:8] = jnp.zeros((8, ext_ref.shape[1]), F32)
        state_ref[...] = jnp.zeros_like(state_ref)

    hid = hid_ref[0]
    proj = nn(hid, w1_ref[...]).astype(BF16)
    convin_ref[...] = proj
    ext_ref[8 : 8 + span] = proj.astype(F32)
    seg_ref[...] = segc_ref[pl.ds(pl.multiple_of(step * span, 8), span + 8), :]
    seg_here = seg_ref[8 : 8 + span]
    total = conv_ref[CONV : CONV + 1]
    for tap in range(CONV):
        at = 8 - (CONV - 1) + tap
        same = seg_ref[at : at + span] == seg_here
        total = total + conv_ref[tap : tap + 1] * jnp.where(same, ext_ref[at : at + span], 0.0)
    ext_ref[0:8] = ext_ref[span : span + 8]
    convsum_ref[...] = total
    mixed = (total * sigmoid(total)).astype(BF16)
    mixed_ref[...] = mixed

    raw_c = nt(hid, wdt_ref[...]) + hrow_ref[1:2]
    raw_r = nt(wdt_ref[...], hid) + hcol_ref[:, 1:2]
    step_c = softplus(raw_c)
    step_r = softplus(raw_r)
    log_c = nn(triangle(span, True), -step_c * jnp.exp(hrow_ref[0:1]), HIGHEST)
    log_r = nn(-step_r * jnp.exp(hcol_ref[:, 0:1]), triangle(span, False), HIGHEST)
    raw_ref[...] = raw_c
    stepc_ref[...] = step_c
    logc_ref[...] = log_c
    stepr_ref[...] = step_r
    logr_ref[...] = log_r

    values = mixed[:, :width]
    write = mixed[:, width : width + STATE]
    read = mixed[:, width + STATE :]
    row = lax.broadcasted_iota(jnp.int32, (span, span), 0)
    col = lax.broadcasted_iota(jnp.int32, (span, span), 1)
    visible = (seg_here == segr_ref[...]) & (row >= col)
    scores = jnp.where(visible, nt(read, write), 0.0)
    lane = lax.broadcasted_iota(jnp.int32, (span, 2 * HEAD_DIM), 1)

    seg_prev = seg_ref[7:8]
    seg_last = seg_ref[span + 7 : span + 8]
    last = log_c[span - 1 : span]
    enter = jnp.where(seg_here == seg_prev, jnp.exp(log_c), 0.0)
    tail = jnp.where(seg_here == seg_last, jnp.exp(last - log_c), 0.0) * step_c
    keep = jnp.where(seg_last == seg_prev, jnp.exp(last), 0.0)
    state = state_ref[...]
    start_ref[0] = state
    values_f = values.astype(F32)
    base = spread(enter, width) * nn(read, state.astype(BF16)) + spread(
        hrow_ref[2:3] + jnp.zeros((8, heads), F32), width
    )[0:1] * values_f
    for pair in range(heads // 2):
        lanes = slice(pair * 2 * HEAD_DIM, (pair + 1) * 2 * HEAD_DIM)
        pieces = []
        for head in (2 * pair, 2 * pair + 1):
            gap = jnp.minimum(log_c[:, head : head + 1] - log_r[head : head + 1], 0.0)
            weights = scores * jnp.exp(gap) * step_r[head : head + 1]
            pieces.append(nn(weights.astype(BF16), values[:, lanes]))
        inner_ref[:, lanes] = base[:, lanes] + jnp.where(lane < HEAD_DIM, pieces[0], pieces[1])
    moved = (spread(tail, width) * values_f).astype(BF16)
    state_ref[...] = spread(keep + jnp.zeros((8, heads), F32), width)[0:1] * state + tn(
        write, moved
    )


def gate_kernel(perm_ref, hid_ref, wg_ref, inner_ref, cot_ref, wout_ref, gain_ref, gate_ref, ng_ref, stat_ref):
    gate = nn(hid_ref[0], wg_ref[...]).astype(BF16)
    gate_ref[...] = gate
    gate = gate.astype(F32)
    grad = nt(cot_ref[0], wout_ref[...])
    ng_ref[...] = grad
    gated = inner_ref[...] * (gate * sigmoid(gate))
    ones = jnp.ones((8, gated.shape[1]), F32)
    squares = nt(ones, gated * gated, HIGHEST)
    crossed = nt(ones, gated * (grad * gain_ref[...]), HIGHEST)
    at = lax.broadcasted_iota(jnp.int32, squares.shape, 0)
    stat_ref[...] = jnp.where(at == 0, squares, crossed)


def norm_back_kernel(
    perm_ref,
    hid_ref,
    inner_ref,
    gate_ref,
    ng_ref,
    stat_ref,
    gain_ref,
    cot_ref,
    wout_ref,
    mixed_ref,
    block_ref,
    outg_ref,
    ing_ref,
    dy_ref,
    dgate_ref,
    sums_ref,
    outacc_ref,
    inacc_ref,
):
    step = pl.program_id(0)
    span, width = inner_ref.shape

    @pl.when(step == 0)
    def _():
        outacc_ref[...] = jnp.zeros_like(outacc_ref)
        inacc_ref[...] = jnp.zeros_like(inacc_ref)
        sums_ref[...] = jnp.zeros_like(sums_ref)

    row = lax.broadcasted_iota(jnp.int32, (span, span), 0)
    col = lax.broadcasted_iota(jnp.int32, (span, span), 1)
    eye = jnp.where(row == col, 1.0, 0.0).astype(F32)
    stats = nt(eye, stat_ref[...], HIGHEST)
    inv = lax.rsqrt(stats[:, 0:1] * (1.0 / INNER) + NORM_EPS)
    cross = stats[:, 1:2]
    gate = gate_ref[...].astype(F32)
    sig = sigmoid(gate)
    silu = gate * sig
    inner = inner_ref[...]
    gated = inner * silu
    unit = gated * inv
    normed = (unit * gain_ref[...]).astype(BF16)
    cot = cot_ref[0]
    block_ref[0] = nn(normed, wout_ref[...]).astype(BF16)
    outacc_ref[...] += tn(normed, cot)
    grad = ng_ref[...]
    dgated = inv * (grad * gain_ref[...] - unit * (cross * inv * (1.0 / INNER)))
    dy = dgated * silu
    dy_ref[...] = dy
    dgate = (dgated * inner * (sig * (1.0 + gate * (1.0 - sig)))).astype(BF16)
    dgate_ref[...] = dgate
    inacc_ref[...] += tn(hid_ref[0], dgate)
    gain_sum = jnp.sum(grad * unit, axis=0, keepdims=True)
    skip_sum = jnp.sum(dy * mixed_ref[...].astype(F32), axis=0, keepdims=True)
    at = lax.broadcasted_iota(jnp.int32, (8, width), 0)
    sums_ref[...] += jnp.where(at == 0, gain_sum, jnp.where(at == 1, skip_sum, 0.0))

    @pl.when(step == pl.num_programs(0) - 1)
    def _():
        outg_ref[...] = outacc_ref[...].astype(BF16)
        ing_ref[...] = inacc_ref[...].astype(BF16)


def scan_back_kernel(
    perm_ref,
    hid_ref,
    dy_ref,
    mixed_ref,
    convin_ref,
    convsum_ref,
    raw_ref,
    stepc_ref,
    logc_ref,
    stepr_ref,
    logr_ref,
    start_ref,
    conv_ref,
    hrow_ref,
    segc_ref,
    segr_ref,
    ing_ref,
    dval_ref,
    dbc_ref,
    dstep_ref,
    convg_ref,
    dtg_ref,
    headg_ref,
    ext_ref,
    seg_ref,
    grad_ref,
    inacc_ref,
    dx_ref,
):
    step = pl.program_id(0)
    chunk = pl.num_programs(0) - 1 - step
    span = hid_ref.shape[1]
    heads = stepc_ref.shape[1]
    width = heads * HEAD_DIM

    @pl.when(step == 0)
    def _():
        ext_ref[span : span + 8] = jnp.zeros((8, width), F32)
        grad_ref[...] = jnp.zeros_like(grad_ref)
        inacc_ref[...] = jnp.zeros_like(inacc_ref)
        convg_ref[...] = jnp.zeros_like(convg_ref)
        dtg_ref[...] = jnp.zeros_like(dtg_ref)
        headg_ref[...] = jnp.zeros_like(headg_ref)

    seg_ref[...] = segc_ref[pl.ds(pl.multiple_of(chunk * span, 8), span + 16), :]
    seg_here = seg_ref[8 : 8 + span]
    seg_prev = seg_ref[7:8]
    seg_last = seg_ref[span + 7 : span + 8]
    mixed = mixed_ref[...]
    values = mixed[:, :width]
    write = mixed[:, width : width + STATE]
    read = mixed[:, width + STATE :]
    values_f = values.astype(F32)
    dy = dy_ref[...]
    dy_low = dy.astype(BF16)
    step_c = stepc_ref[...]
    log_c = logc_ref[...]
    step_r = stepr_ref[...]
    log_r = logr_ref[...]
    last = log_c[span - 1 : span]
    enter = jnp.where(seg_here == seg_prev, jnp.exp(log_c), 0.0)
    tail_raw = jnp.where(seg_here == seg_last, jnp.exp(last - log_c), 0.0)
    tail = tail_raw * step_c
    keep = jnp.where(seg_last == seg_prev, jnp.exp(last), 0.0)
    enter_w = spread(enter, width)
    tail_w = spread(tail, width)
    wide = spread(
        jnp.concatenate([hrow_ref[2:3] + jnp.zeros((8, heads), F32), keep + jnp.zeros((8, heads), F32)], axis=0),
        width,
    )
    skip_w = wide[0:1]
    keep_w = wide[8:9]
    state = start_ref[0]
    state_low = state.astype(BF16)
    later = grad_ref[...]
    later_low = later.astype(BF16)

    row = lax.broadcasted_iota(jnp.int32, (span, span), 0)
    col = lax.broadcasted_iota(jnp.int32, (span, span), 1)
    visible = (seg_here == segr_ref[...]) & (row >= col)
    scores = jnp.where(visible, nt(read, write), 0.0)
    lane = lax.broadcasted_iota(jnp.int32, (span, 2 * HEAD_DIM), 1)
    head_at = lax.broadcasted_iota(jnp.int32, (8, span), 0)
    lane_at = lax.broadcasted_iota(jnp.int32, (span, heads), 1)

    entered = enter_w * dy
    entered_low = entered.astype(BF16)
    inter = enter_w * nn(read, state_low)
    from_later = nn(write, later_low)
    moved_low = (tail_w * values_f).astype(BF16)
    dread = nt(entered_low, state_low)
    dwrite = nt(moved_low, later_low)
    dlog_c = gather_heads(dy * inter, heads)
    tail_dot = gather_heads(values_f * from_later, heads)
    dlog_c = dlog_c - tail_dot * tail
    dstep_c = tail_dot * tail_raw
    carried = gather_heads(jnp.sum(later * state, axis=0, keepdims=True) + jnp.zeros((8, width), F32), heads)[0:1]
    at_last = lax.broadcasted_iota(jnp.int32, (span, heads), 0) == span - 1
    dlog_c = dlog_c + jnp.where(
        at_last, jnp.sum(tail_dot * tail, axis=0, keepdims=True) + keep * carried, 0.0
    )
    grad_ref[...] = keep_w * later + tn(read, entered_low)
    dx_ref[...] = tail_w * from_later + skip_w * dy

    dscores = jnp.zeros((span, span), F32)
    dstep_r = jnp.zeros((8, span), F32)
    for pair in range(heads // 2):
        lanes = slice(pair * 2 * HEAD_DIM, (pair + 1) * 2 * HEAD_DIM)
        dy_pair = dy_low[:, lanes]
        pieces = []
        for head in (2 * pair, 2 * pair + 1):
            mine = lane < HEAD_DIM if head % 2 == 0 else lane >= HEAD_DIM
            gap = jnp.minimum(log_c[:, head : head + 1] - log_r[head : head + 1], 0.0)
            decay = jnp.exp(gap)
            outer = nt(jnp.where(mine, dy_pair, jnp.zeros_like(dy_pair)), values[:, lanes])
            fade = decay * step_r[head : head + 1]
            dscores = dscores + outer * fade
            flow = outer * scores
            base = flow * decay
            dstep_r = dstep_r + jnp.where(head_at == head, jnp.sum(base, axis=0, keepdims=True), 0.0)
            dlog_c = dlog_c + jnp.where(
                lane_at == head, jnp.sum(flow * fade, axis=1, keepdims=True), 0.0
            )
            pieces.append(tn((scores * fade).astype(BF16), dy_pair))
        dx_ref[:, lanes] += jnp.where(lane < HEAD_DIM, pieces[0], pieces[1])
    dscores = jnp.where(visible, dscores, 0.0).astype(BF16)
    dread = dread + nn(dscores, write)
    dwrite = dwrite + tn(dscores, read)
    dbc_ref[:, :STATE] = dwrite.astype(BF16)
    dbc_ref[:, STATE:] = dread.astype(BF16)

    upper = triangle(span, False)
    eye = jnp.where(row == col, 1.0, 0.0).astype(F32)
    dalpha = nn(upper, dlog_c, HIGHEST) - nt(upper, dstep_r * step_r, HIGHEST)[:, :heads]
    dstep = dstep_c + nt(eye, dstep_r, HIGHEST)[:, :heads]
    rate = jnp.exp(hrow_ref[0:1])
    draw = (dstep - rate * dalpha) * sigmoid(raw_ref[...])
    draw_low = draw.astype(BF16)
    dstep_ref[...] = draw_low
    hid = hid_ref[0]
    dtg_ref[...] += tn(draw_low, hid)
    rate_sum = jnp.sum(-dalpha * step_c * rate, axis=0, keepdims=True)
    bias_sum = jnp.sum(draw, axis=0, keepdims=True)
    at = lax.broadcasted_iota(jnp.int32, (8, heads), 0)
    headg_ref[...] += jnp.where(at == 0, rate_sum, jnp.where(at == 1, bias_sum, 0.0))

    ext_ref[0:span] = dx_ref[...] * silu_grad(convsum_ref[...])
    back = jnp.zeros((span, width), F32)
    conv_in = convin_ref[...].astype(F32)
    at = lax.broadcasted_iota(jnp.int32, (8, width), 0)
    sums = jnp.where(at == CONV, jnp.sum(ext_ref[0:span], axis=0, keepdims=True), 0.0)
    for tap in range(CONV):
        ahead = CONV - 1 - tap
        same = seg_ref[8 + ahead : 8 + ahead + span] == seg_here
        term = jnp.where(same, ext_ref[ahead : ahead + span], 0.0)
        back = back + conv_ref[tap : tap + 1] * term
        sums = sums + jnp.where(at == tap, jnp.sum(conv_in * term, axis=0, keepdims=True), 0.0)
    convg_ref[...] += sums
    ext_ref[span : span + 8] = ext_ref[0:8]
    dval = back.astype(BF16)
    dval_ref[...] = dval
    inacc_ref[...] += tn(hid, dval)

    @pl.when(step == pl.num_programs(0) - 1)
    def _():
        ing_ref[...] = inacc_ref[...].astype(BF16)


def hidden_back_kernel(perm_ref, dgate_ref, dval_ref, dstep_ref, wg_ref, wv_ref, wdt_ref, out_ref):
    total = nt(dgate_ref[...], wg_ref[...]) + nt(dval_ref[...], wv_ref[...])
    out_ref[0] = (total + nn(dstep_ref[...], wdt_ref[...])).astype(BF16)


def maps_back_kernel(dbc_ref, convsum_ref, convin_ref, conv_ref, segc_ref, hid_ref, dmap_ref, convg_ref, ing_ref, ext_ref):
    size, width = dmap_ref.shape
    ext_ref[0:size] = dbc_ref[...] * silu_grad(convsum_ref[...])
    ext_ref[size : size + 8] = jnp.zeros((8, width), F32)
    back = jnp.zeros((size, width), F32)
    conv_in = convin_ref[...].astype(F32)
    at = lax.broadcasted_iota(jnp.int32, (8, width), 0)
    sums = jnp.where(at == CONV, jnp.sum(ext_ref[0:size], axis=0, keepdims=True), 0.0)
    seg_here = segc_ref[8 : 8 + size]
    for tap in range(CONV):
        ahead = CONV - 1 - tap
        same = segc_ref[8 + ahead : 8 + ahead + size] == seg_here
        term = jnp.where(same, ext_ref[ahead : ahead + size], 0.0)
        back = back + conv_ref[tap : tap + 1] * term
        sums = sums + jnp.where(at == tap, jnp.sum(conv_in * term, axis=0, keepdims=True), 0.0)
    convg_ref[...] = sums
    dmap = back.astype(BF16)
    dmap_ref[...] = dmap
    ing_ref[...] = tn(hid_ref[...], dmap).astype(BF16)


def input_back_kernel(hg_ref, dmap_ref, wbc_ref, tok_ref, gain_ref, cot_ref, out_ref, gsum_ref):
    grad = hg_ref[...] + nt(dmap_ref[...], wbc_ref[...])
    tok = tok_ref[...]
    scale = lax.rsqrt(jnp.mean(tok * tok, axis=-1, keepdims=True) + NORM_EPS)
    unit = tok * scale
    gsum_ref[...] = jnp.sum(grad * unit, axis=0, keepdims=True) + jnp.zeros(gsum_ref.shape, F32)
    scaled = grad * gain_ref[...]
    mean = jnp.mean(scaled * unit, axis=-1, keepdims=True)
    out_ref[...] = cot_ref[...] + scale * (scaled - unit * mean)


def swap(value, axis, bit):
    count = lax.axis_size(axis)
    return lax.ppermute(value, axis, [(at, at ^ bit) for at in range(count)])


def gather_ctx(value):
    two = jnp.stack([value, swap(value, "ctx", 2)])
    return jnp.concatenate([two, swap(two, "ctx", 1)])


def scatter_ctx(value):
    near = value[0:2].astype(F32) + swap(value[2:4], "ctx", 1).astype(F32)
    return near[0] + swap(near[1].astype(BF16), "ctx", 2).astype(F32)


def sum_ctx(value):
    pair = value.astype(F32) + swap(value, "ctx", 1).astype(F32)
    pair = pair.astype(BF16)
    return pair.astype(F32) + swap(pair, "ctx", 2).astype(F32)


def adam_step(weight, moment_one, second, gradient, step_rate, decay_rate):
    moment_new = BETA_ONE * moment_one + (1.0 - BETA_ONE) * gradient
    second_new = BETA_TWO * second + (1.0 - BETA_TWO) * gradient * gradient
    first_hat = moment_new / (1.0 - BETA_ONE**STEP)
    second_hat = second_new / (1.0 - BETA_TWO**STEP)
    weight_new = weight - step_rate * (
        first_hat / (jnp.sqrt(second_hat) + ADAM_EPS) + decay_rate * weight
    )
    return (weight_new, moment_new, second_new)


def full(shape):
    return pl.BlockSpec(shape, lambda *_: (0,) * len(shape))


def shape_of(*shape, dtype=F32):
    return jax.ShapeDtypeStruct(shape, dtype)


def shards(
    tokens,
    segment_ids,
    cotangent,
    in_weight,
    dt_weight,
    out_weight,
    conv_params,
    gains,
    head_params,
    in_first,
    in_second,
    dt_first,
    dt_second,
    out_first,
    out_second,
    conv_first,
    conv_second,
    gain_first,
    gain_second,
    head_first,
    head_second,
):
    _, span, model = tokens.shape
    length = segment_ids.shape[1]
    ndp, nctx = lax.axis_size("dp"), lax.axis_size("ctx")
    d, c = lax.axis_index("dp"), lax.axis_index("ctx")
    heads = HEADS // nctx
    width = INNER // nctx
    maps = 2 * STATE
    wide = width + maps
    chunks = nctx
    rows_in = in_weight.shape[0]
    rows_out = out_weight.shape[0]
    cols_out = model // nctx
    conv_cols = conv_params.shape[1]
    gain_len = gains.shape[0]
    dt_cols = dt_weight.shape[1]

    tok = tokens[0]
    lanes = max(-(-max(gain_len, conv_cols, dt_cols) // 128) * 128, 128)

    def padded(value):
        return jnp.pad(value.astype(BF16), ((0, 0), (0, lanes - value.shape[1])))

    small = jnp.concatenate(
        [padded(dt_weight), padded(conv_params), padded(gains[None]), jnp.zeros((10, lanes), BF16)]
    )
    small_all = lax.all_gather(small, "dp", axis=0)
    gain_full = small_all[:, HEADS + CONV + 1, :gain_len].astype(F32).reshape(1, -1)
    conv_full = jnp.moveaxis(
        small_all[:, HEADS : HEADS + CONV + 1, :conv_cols].astype(F32), 0, 1
    ).reshape(CONV + 1, -1)
    dt_mine = lax.dynamic_slice_in_dim(small_all[:, :HEADS, :dt_cols], c * heads, heads, 1)
    dt_mine = jnp.moveaxis(dt_mine, 0, 1).reshape(heads, model)
    gain_pre = gain_full[:, :model]
    gain_mine = lax.dynamic_slice_in_dim(gain_full, model + c * width, width, 1)
    conv_mine = jnp.concatenate(
        [lax.dynamic_slice_in_dim(conv_full, c * width, width, 1), conv_full[:, INNER:]], axis=1
    )
    conv_mine = jnp.pad(conv_mine, ((0, 8 - CONV - 1), (0, 0)))

    value_part = lax.dynamic_slice_in_dim(in_weight, INNER + c * width, width, 1)
    w1 = lax.all_gather(
        jnp.concatenate([value_part, in_weight[:, 2 * INNER :]], axis=1).astype(BF16),
        "dp",
        axis=0,
        tiled=True,
    )
    wout = lax.all_gather(
        lax.dynamic_slice_in_dim(out_weight, c * cols_out, cols_out, 1).astype(BF16),
        "dp",
        axis=0,
        tiled=True,
    )
    wout = lax.all_to_all(wout, "ctx", split_axis=0, concat_axis=1, tiled=True)
    wg = lax.all_gather(
        lax.dynamic_slice_in_dim(in_weight, c * width, width, 1).astype(BF16),
        "dp",
        axis=0,
        tiled=True,
    )

    order = jnp.asarray([0, 2, 1, 3], jnp.int32)
    perm = order[jnp.arange(nctx, dtype=jnp.int32) ^ c]
    cot_all = gather_ctx(cotangent[0].astype(BF16))
    hid_own = pl.pallas_call(
        norm_kernel, out_shape=shape_of(span, model, dtype=BF16), compiler_params=params(), name="pre_norm"
    )(tok, gain_pre)
    hid_all = gather_ctx(hid_own)

    ids = segment_ids[0]
    seg_col = jnp.pad(ids, (8, 8), constant_values=-1)[:, None]
    seg_row = segment_ids
    head_mine = lax.dynamic_slice_in_dim(head_params, c * heads, heads, 1)
    head_col = head_mine.T

    slot_rows = pl.BlockSpec((1, span, model), lambda i, p: (p[i], 0, 0))
    rows = lambda cols: pl.BlockSpec((span, cols), lambda i, p: (i, 0))
    row_of = pl.BlockSpec((heads, span), lambda i, p: (0, i))

    mixed, conv_in, conv_sum, inner, raw, step_c, log_c, step_r, log_r, starts = pl.pallas_call(
        scan_forward_kernel,
        grid_spec=pltpu.PrefetchScalarGridSpec(
            num_scalar_prefetch=1,
            grid=(chunks,),
            in_specs=[
                slot_rows,
                full((model, wide)),
                full((heads, model)),
                full((8, wide)),
                full((3, heads)),
                full((heads, 3)),
                full((length + 16, 1)),
                pl.BlockSpec((1, span), lambda i, p: (0, i)),
            ],
            out_specs=[
                rows(wide),
                rows(wide),
                rows(wide),
                rows(width),
                rows(heads),
                rows(heads),
                rows(heads),
                row_of,
                row_of,
                pl.BlockSpec((1, STATE, width), lambda i, p: (i, 0, 0)),
            ],
            scratch_shapes=[
                pltpu.VMEM((span + 8, wide), F32),
                pltpu.VMEM((span + 8, 1), jnp.int32),
                pltpu.VMEM((STATE, width), F32),
            ],
        ),
        out_shape=[
            shape_of(length, wide, dtype=BF16),
            shape_of(length, wide, dtype=BF16),
            shape_of(length, wide),
            shape_of(length, width),
            shape_of(length, heads),
            shape_of(length, heads),
            shape_of(length, heads),
            shape_of(heads, length),
            shape_of(heads, length),
            shape_of(chunks, STATE, width),
        ],
        compiler_params=params("arbitrary"),
        name="scan_forward",
    )(perm, hid_all, w1, dt_mine, conv_mine, head_mine, head_col, seg_col, seg_row)

    gate, normed_grad, stats = pl.pallas_call(
        gate_kernel,
        grid_spec=pltpu.PrefetchScalarGridSpec(
            num_scalar_prefetch=1,
            grid=(chunks,),
            in_specs=[
                slot_rows,
                full((model, width)),
                rows(width),
                slot_rows,
                full((width, model)),
                full((1, width)),
            ],
            out_specs=[rows(width), rows(width), pl.BlockSpec((8, span), lambda i, p: (0, i))],
        ),
        out_shape=[
            shape_of(length, width, dtype=BF16),
            shape_of(length, width),
            shape_of(8, length),
        ],
        compiler_params=params("arbitrary"),
        name="gate",
    )(perm, hid_all, wg, inner, cot_all, wout, gain_mine)
    stats = stats + swap(stats, "ctx", 1)
    stats = stats + swap(stats, "ctx", 2)

    block_part, out_grad, gate_in_grad, dy, dgate, col_sums = pl.pallas_call(
        norm_back_kernel,
        grid_spec=pltpu.PrefetchScalarGridSpec(
            num_scalar_prefetch=1,
            grid=(chunks,),
            in_specs=[
                slot_rows,
                rows(width),
                rows(width),
                rows(width),
                pl.BlockSpec((8, span), lambda i, p: (0, i)),
                full((1, width)),
                slot_rows,
                full((width, model)),
                rows(width),
            ],
            out_specs=[
                slot_rows,
                full((width, model)),
                full((model, width)),
                rows(width),
                rows(width),
                full((8, width)),
            ],
            scratch_shapes=[pltpu.VMEM((width, model), F32), pltpu.VMEM((model, width), F32)],
        ),
        out_shape=[
            shape_of(nctx, span, model, dtype=BF16),
            shape_of(width, model, dtype=BF16),
            shape_of(model, width, dtype=BF16),
            shape_of(length, width),
            shape_of(length, width, dtype=BF16),
            shape_of(8, width),
        ],
        compiler_params=params("arbitrary"),
        name="norm_back",
    )(perm, hid_all, inner, gate, normed_grad, stats, gain_mine, cot_all, wout, mixed)

    block_output = tok + scatter_ctx(block_part)
    out_cols = lax.all_to_all(out_grad, "ctx", split_axis=1, concat_axis=0, tiled=True)
    out_shard = lax.psum_scatter(out_cols, "dp", scatter_dimension=0, tiled=True)
    gate_shard = lax.psum_scatter(gate_in_grad, "dp", scatter_dimension=0, tiled=True)

    back = lambda cols: pl.BlockSpec((span, cols), lambda i, p: (chunks - 1 - i, 0))
    back_row = pl.BlockSpec((heads, span), lambda i, p: (0, chunks - 1 - i))
    value_in_grad, dval, dbc, dstep, conv_grad, dt_grad, head_grad = pl.pallas_call(
        scan_back_kernel,
        grid_spec=pltpu.PrefetchScalarGridSpec(
            num_scalar_prefetch=1,
            grid=(chunks,),
            in_specs=[
                pl.BlockSpec((1, span, model), lambda i, p: (p[chunks - 1 - i], 0, 0)),
                back(width),
                back(wide),
                back(width),
                back(width),
                back(heads),
                back(heads),
                back(heads),
                back_row,
                back_row,
                pl.BlockSpec((1, STATE, width), lambda i, p: (chunks - 1 - i, 0, 0)),
                full((8, width)),
                full((3, heads)),
                full((length + 16, 1)),
                pl.BlockSpec((1, span), lambda i, p: (0, chunks - 1 - i)),
            ],
            out_specs=[
                full((model, width)),
                back(width),
                back(maps),
                back(heads),
                full((8, width)),
                full((heads, model)),
                full((8, heads)),
            ],
            scratch_shapes=[
                pltpu.VMEM((span + 8, width), F32),
                pltpu.VMEM((span + 16, 1), jnp.int32),
                pltpu.VMEM((STATE, width), F32),
                pltpu.VMEM((model, width), F32),
                pltpu.VMEM((span, width), F32),
            ],
        ),
        out_shape=[
            shape_of(model, width, dtype=BF16),
            shape_of(length, width, dtype=BF16),
            shape_of(length, maps, dtype=BF16),
            shape_of(length, heads, dtype=BF16),
            shape_of(8, width),
            shape_of(heads, model),
            shape_of(8, heads),
        ],
        compiler_params=params("arbitrary"),
        name="scan_back",
    )(
        perm, hid_all, dy, mixed, conv_in, conv_sum, raw, step_c, log_c, step_r, log_r, starts,
        conv_mine, head_mine, seg_col, seg_row,
    )
    value_shard = lax.psum_scatter(value_in_grad, "dp", scatter_dimension=0, tiled=True)
    dbc_total = sum_ctx(dbc)

    hidden_part = pl.pallas_call(
        hidden_back_kernel,
        grid_spec=pltpu.PrefetchScalarGridSpec(
            num_scalar_prefetch=1,
            grid=(chunks,),
            in_specs=[
                rows(width),
                rows(width),
                rows(heads),
                full((model, width)),
                full((model, width)),
                full((heads, model)),
            ],
            out_specs=[slot_rows],
        ),
        out_shape=[shape_of(nctx, span, model, dtype=BF16)],
        compiler_params=params("arbitrary"),
        name="hidden_back",
    )(perm, dgate, dval, dstep, wg, w1, dt_mine)[0]
    hidden_grad = scatter_ctx(hidden_part)

    hid_order = jnp.concatenate(
        [lax.dynamic_index_in_dim(hid_all, perm[at], 0, keepdims=False) for at in range(nctx)]
    )
    dmap, map_conv_grad, map_in_grad = pl.pallas_call(
        maps_back_kernel,
        out_shape=[
            shape_of(length, maps, dtype=BF16),
            shape_of(8, maps),
            shape_of(model, maps, dtype=BF16),
        ],
        scratch_shapes=[pltpu.VMEM((length + 8, maps), F32)],
        compiler_params=params(),
        name="maps_back",
    )(dbc_total, conv_sum[:, width:], conv_in[:, width:], conv_mine[:, width:], seg_col, hid_order)
    map_rows = rows_in // nctx
    map_part = lax.dynamic_index_in_dim(
        map_in_grad.reshape(ndp, nctx, map_rows, maps), c, 1, keepdims=False
    )
    map_shard = lax.psum_scatter(map_part, "dp", scatter_dimension=0, tiled=True)[0]

    input_grad, gain_sum = pl.pallas_call(
        input_back_kernel,
        out_shape=[shape_of(span, model), shape_of(8, model)],
        compiler_params=params(),
        name="input_back",
    )(
        hidden_grad,
        lax.dynamic_slice_in_dim(dmap, c * span, span, 0),
        w1[:, width:],
        tok,
        gain_pre,
        cotangent[0],
    )

    def row_block(value):
        return jnp.pad(value, ((0, 0), (0, width - value.shape[1])))

    half = model // width
    packed = jnp.concatenate(
        [conv_grad, col_sums, row_block(map_conv_grad), row_block(head_grad)]
        + [dt_grad[:, at * width : (at + 1) * width] for at in range(half)]
        + [gain_sum[:, at * width : (at + 1) * width] for at in range(half)]
    )
    packed = lax.all_gather(lax.psum(packed, "dp"), "ctx", axis=0)
    conv_total = jnp.concatenate(
        [packed[at, : CONV + 1] for at in range(nctx)] + [packed[0, 16 : 16 + CONV + 1, :maps]], axis=1
    )
    conv_total = lax.dynamic_slice_in_dim(conv_total, d * conv_cols, conv_cols, 1)
    dt_total = jnp.concatenate(
        [packed[:, 32 + 8 * at : 40 + 8 * at].reshape(HEADS, width) for at in range(half)], axis=1
    )
    dt_total = lax.dynamic_slice_in_dim(dt_total, d * dt_cols, dt_cols, 1)
    first_gain = 32 + 8 * half
    pre_total = [
        jnp.sum(packed[:, first_gain + 8 * at], axis=0) for at in range(half)
    ]
    gain_total = jnp.concatenate(pre_total + [packed[:, 8].reshape(-1)])
    gain_total = lax.dynamic_slice_in_dim(gain_total, d * gain_len, gain_len, 0)
    head_total = jnp.stack(
        [
            packed[:, 24, :heads].reshape(-1),
            packed[:, 25, :heads].reshape(-1),
            jnp.sum(packed[:, 9].reshape(HEADS, HEAD_DIM), axis=1),
        ]
    )

    columns = lax.all_gather(jnp.stack([gate_shard, value_shard]).astype(BF16), "ctx", axis=0)
    map_total = lax.all_gather(map_shard.astype(BF16), "ctx", axis=0, tiled=True)
    in_total = jnp.concatenate(
        [columns[at, 0] for at in range(nctx)] + [columns[at, 1] for at in range(nctx)] + [map_total],
        axis=1,
    ).astype(F32)
    out_total = lax.all_gather(out_shard.astype(BF16), "ctx", axis=1, tiled=True).astype(F32)

    in_new = adam_step(in_weight, in_first, in_second, in_total, 0.03, WEIGHT_DECAY)
    dt_new = adam_step(dt_weight, dt_first, dt_second, dt_total, 0.03, WEIGHT_DECAY)
    out_new = adam_step(out_weight, out_first, out_second, out_total, 0.02, WEIGHT_DECAY)
    conv_new = adam_step(conv_params, conv_first, conv_second, conv_total, 0.3, 0.0)
    gain_new = adam_step(gains, gain_first, gain_second, gain_total, 0.5, 0.0)
    head_new = adam_step(head_params, head_first, head_second, head_total, 2.0, 0.0)
    return (block_output[None], input_grad[None]) + in_new + dt_new + out_new + conv_new + gain_new + head_new


def solution(mesh):
    tokens, rows, cols = P("dp", "ctx", None), P("dp", None), P(None, "dp")
    return jax.shard_map(
        shards,
        mesh=mesh,
        in_specs=(tokens, rows, tokens, rows, cols, rows, cols, P("dp"), P())
        + (rows, rows, cols, cols, rows, rows, cols, cols, P("dp"), P("dp"), P(), P()),
        out_specs=(tokens, tokens)
        + (rows,) * 3
        + (cols,) * 3
        + (rows,) * 3
        + (cols,) * 3
        + (P("dp"),) * 3
        + (P(),) * 3,
        check_vma=False,
    )
```

time: 1030 us -> 607 us (0.59)
  waiting for transfers between devices: 499 us -> 357 us
  matrix products: 135 us -> 0 us
  blocking collectives: 181 us -> 53.1 us
  Pallas kernels: 0 us -> 79.6 us
  local copies, waits for them, and re-layouts: 109 us -> 38.7 us
  other arithmetic: 73.8 us -> 37.3 us
  starting transfers between devices: 3.27 us -> 17.3 us
    reduce_scatter x3 -> x4, waiting for transfers between devices: 345 us -> 200 us  [the longest x1 65.8 us: shards(): lax.psum_scatter(gate_in_grad, 'dp', scatter_dimension=0, tiled=True)]
    dot_general x24 -> x0, matrix products: 135 us -> none  [the longest x3 31.6 us: mix_tokens(): jnp.einsum('sbhtu,sbuhp->sbthp', weights, values_b, precision=HIGHEST)]
    pallas_call x0 -> x8, Pallas kernels: none -> 79.6 us  [the longest x1 21.7 us: shards(): pl.pallas_call(scan_back_kernel, grid_spec=pltpu.PrefetchScalarGridSpec(n...]
    psum x2 -> x0, blocking collectives: 51.6 us -> none  [the longest x1 40.6 us: shards(): head_sum = lax.psum(head_total, ('dp', 'ctx'))]
    reshape x17 -> x3, local copies, waits for them, and re-layouts: 48.5 us -> 1.42 us  [the longest x1 1.32 us: shards(): dt_mine = jnp.moveaxis(dt_mine, 0, 1).reshape(heads, model)]
    all_gather x4, blocking collectives: 93.7 us -> 53.1 us  [the longest x1 33 us: shards(): small_all = lax.all_gather(small, 'dp', axis=0)]
    unnamed x1 -> x0, blocking collectives: 35.4 us -> none
    ppermute x2 -> x12, waiting for transfers between devices: 0.65 us -> 34.8 us  [swap(): return lax.ppermute(value, axis, [(at, at ^ bit) for at in range(count)])]
  transfers between devices with their start and end apart: 11 -> 23, of which waited for: 7 -> 16; matrix products, arithmetic and copies ran while one was open for 25% -> 10% of each run, Pallas kernels for 0% -> 6%
where the time goes in v1:
time: 607 us; the launch traced here: 605 us
  waiting for transfers between devices  357 us (59%)
  Pallas kernels  79.6 us (13%)
  blocking collectives  53.1 us (9%)
  local copies, waits for them, and re-layouts  38.7 us (6%)
  other arithmetic  37.3 us (6%)
  between operations  22.2 us (4%)
  starting transfers between devices  17.3 us (3%)
    reduce_scatter x1, waiting for transfers between devices, shards(): lax.psum_scatter(gate_in_grad, 'dp', scatter_dimension=0, tiled=True)  65.8 us
    psum x1, waiting for transfers between devices, shards(): packed = lax.all_gather(lax.psum(packed, 'dp'), 'ctx', axis=0)  64.7 us
    reduce_scatter x1, waiting for transfers between devices, shards(): lax.psum_scatter(out_cols, 'dp', scatter_dimension=0, tiled=True)  62.4 us
    reduce_scatter x1, waiting for transfers between devices, shards(): lax.psum_scatter(value_in_grad, 'dp', scatter_dimension=0, tiled=True)  58.5 us
    ppermute x12, waiting for transfers between devices, swap(): return lax.ppermute(value, axis, [(at, at ^ bit) for at in range(count)])  34.8 us
    all_gather x1, blocking collectives, shards(): small_all = lax.all_gather(small, 'dp', axis=0)  33 us
    all_gather x1, waiting for transfers between devices, shards(): lax.all_gather(lax.dynamic_slice_in_dim(in_weight, c * width, width, 1).a...  26.8 us
    pallas_call x1, Pallas kernels, shards(): pl.pallas_call(scan_back_kernel, grid_spec=pltpu.PrefetchScalarGridSpec(n...  21.7 us
  transfers between devices with their start and end apart: 23, of which 16 were waited for; matrix products, arithmetic and copies ran while one was open for 10% of the time, Pallas kernels for 6%

profile of v1, /device:TPU:0, one launch (start us, length us, event | category | flops | bytes accessed | tf_op | source)
XLA Modules:
  0.0 605.3 jit_solution(3992696780217832365)
XLA Ops:
  7.3 1.7 dynamic-slice_convert_fusion
  9.9 1.7 dynamic-slice_convert_fusion.1
  14.7 33.0 %all-gather = bf16[384,384]{1,0:T(8,128)(2,1)S(1)} all-gather(bf16[48,384]{1,0:T(8,128)(2,1)S(1)} %fusion.23), channel_id=2, replica_groups=mesh['dp'=8,'ctx'=4] {'dp'}, dimensions={0}, use_global_device_ids=true | all-gather | bytes 331776 | tf_op jit(solution)/shard_map/all_gather | solution.py:567
  48.4 2.2 pre_norm.1
  50.6 1.5 collective-permute-start
  52.1 0.9 fusion.40
  53.6 10.2 %collective-permute-done = bf16[256,1024]{1,0:T(8,128)(2,1)S(1)} collective-permute-done((bf16[256,1024]{1,0:T(8,128)(2,1)}, bf16[256,1024]{1,0:T(8,128)(2,1)S(1)}, u32[]{:S(2)}, u32[]{:S(2)}) %collective-permute-start) | collective-permute-done | bytes 524320 | tf_op jit(solution)/shard_map/ppermute | solution.py:481
  63.8 1.1 pad_maximum_fusion.3
  64.9 4.5 collective-permute-done.2
  69.4 1.1 pad_maximum_fusion.4
  71.2 3.5 all-to-all-start
  76.3 1.0 broadcast_in_dim.18.segc_ref
  77.4 1.1 gather_fusion
  79.1 1.3 dynamic-slice_bitcast_fusion.5.wdt_ref
  81.0 2.7 pad_maximum_fusion.hid_ref
  83.8 2.7 pad_maximum_fusion.1.cot_ref
  86.5 2.6 all-to-all-done
  89.1 1.1 copy.66
  90.3 10.2 %all-gather.8.cloned.1.call-done.w1_ref.wv_ref = bf16[1024,768]{1,0:T(8,128)(2,1)} async-done(((bf16[128,768]{1,0:T(8,128)(2,1)}), bf16[1024,768]{1,0:T(8,128)(2,1)}) %all-gather.8.cloned.1.call-update) | async-done | bytes 1572880 | tf_op jit(solution)/shard_map/all_gather | solution.py:582
  100.4 14.9 %scan_forward.1 = (bf16[1024,768]{1,0:T(8,128)(2,1)}, bf16[1024,768]{1,0:T(8,128)(2,1)}, f32[1024,768]{1,0:T(8,128)}, f32[1024,512]{1,0:T(8,128)}, f32[1024,8]{1...) custom-call(s32[4]{0:T(128)} %gather_fusion, ...), custom_call_target="tpu_custom_call" | custom-call | tf_op jit(solution)/shard_map/scan_forward/pallas_call | solution.py:620
  115.4 26.8 %all-gather.10.cloned.1.call-done.wg_ref = bf16[1024,512]{1,0:T(8,128)(2,1)} async-done(((bf16[128,512]{1,0:T(8,128)(2,1)}), bf16[1024,512]{1,0:T(8,128)(2,1)}) %all-gather.10.cloned.1.call-update) | async-done | bytes 1048592 | tf_op jit(solution)/shard_map/all_gather | solution.py:595
  142.2 10.7 %gate.1 = (bf16[1024,512]{1,0:T(8,128)(2,1)}, f32[1024,512]{1,0:T(8,128)}, f32[8,1024]{1,0:T(8,128)}) custom-call(s32[4]{0:T(128)} %gather_fusion, bf16[4,256,1024]{2,1,0:T(8,128)(2,1)} %pad_maximum_fusion.hid_ref, bf16[1024,512]{1,0:T(8,128)(2,1)} %all-gather.10.cloned.1.call-done.wg_ref, f32[1024,512]{1,0:T(8,128)} %get-tuple-element.51.inner_ref, ...), custom_call_target="tpu_custom_call" | custom-call | tf_op jit(solution)/shard_map/gate/pallas_call | solution.py:669
  152.8 1.4 collective-permute-done.4
  155.0 1.5 collective-permute-start.5
  156.5 2.4 collective-permute-done.5
  159.5 13.2 %norm_back.1 = (bf16[4,256,1024]{2,1,0:T(8,128)(2,1)}, bf16[512,1024]{1,0:T(8,128)(2,1)}, bf16[1024,512]{1,0:T(8,128)(2,1)}, f32[1024,512]{1,0:T(8,128)}, bf16[1024,512]{1,0:T(8,128)(2,1)}, /*index=5*/f32[8,512]{1,0:T(8,128)}) custom-call(s32[4]{0:T(128)} %gather_fusion, bf16[4,256,1024]{2,1,0:T(8,128)(2,1)} %pad_maximum_fusion.hid_ref, ...), custom_call_target="tpu_custom_call" | custom-call | tf_op jit(solution)/shard_map/norm_back/pallas_call | solution.py:695
  172.7 21.7 %scan_back.1 = (bf16[1024,512]{1,0:T(8,128)(2,1)}, bf16[1024,512]{1,0:T(8,128)(2,1)}, bf16[1024,256]{1,0:T(8,128)(2,1)}, bf16[1024,8]{1,0:T(8,128)(2,1)}, f32[8,...) custom-call(s32[4]{0:T(128)} %gather_fusion, bf16[4,256,1024]{2,1,0:T(8,128)(2,1)} %pad_maximum_fusion.hid_ref, ...), custom_call_target="tpu_custom_call" | custom-call | tf_op jit(solution)/shard_map/scan_back/pallas_call | solution.py:740
  200.3 1.3 slice.205.conv_ref
  204.2 7.4 %hidden_back.1 = bf16[4,256,1024]{2,1,0:T(8,128)(2,1)} custom-call(s32[4]{0:T(128)} %gather_fusion, bf16[1024,512]{1,0:T(8,128)(2,1)} %get-tuple-element.57.dgate_ref, bf16[1024,512]{1,0:T(8,128)(2,1)} %get-tuple-element.67.dval_ref, bf16[1024,8]{1,0:T(8,128)(2,1)} %get-tuple-element.68.dstep_ref, bf16[1024,512]{1,0:T(8,128)(2,1)} %all-gather.10.cloned.1.call-done.wg_ref, ...), custom_call_target="tpu_custom_call" | custom-call | tf_op jit(solution)/shard_map/hidden_back/pallas_call | solution.py:797
  211.6 1.4 slice.202
  213.7 1.5 collective-permute-start.11
  215.4 1.5 pad_maximum_fusion.2.hid_ref
  216.9 2.3 slice.158.convsum_ref
  219.2 1.9 slice.159.convin_ref
  221.1 1.9 slice.206.wbc_ref
  223.0 4.7 collective-permute-done.11
  227.7 1.1 convert_add_fusion.2.dbc_ref
  228.7 5.6 maps_back.1
  234.4 1.6 dynamic-slice_bitcast_fusion.4
  236.7 1.6 constant_dynamic-slice_fusion.dmap_ref
  238.3 1.6 convert_add_fusion
  240.0 1.5 collective-permute-start.9
  241.6 11.5 %collective-permute-done.9 = bf16[256,1024]{1,0:T(8,128)(2,1)S(1)} collective-permute-done((bf16[256,1024]{1,0:T(8,128)(2,1)S(1)}, bf16[256,1024]{1,0:T(8,128)(2,1)S(1)}, u32[]{:S(2)}, u32[]{:S(2)}) %collective-permute-start.9) | collective-permute-done | bytes 524320 | tf_op jit(solution)/shard_map/ppermute | solution.py:481
  253.1 1.1 fusion.4.hg_ref
  254.2 3.9 input_back.1
  260.9 1.0 slice.151
  261.9 1.0 copy.71
  263.0 4.3 all-to-all-start.1
  267.3 1.9 convert_add_fusion.1
  270.1 1.9 collective-permute-start.7
  272.0 10.2 %all-to-all-done.1 = bf16[512,4,256]{2,0,1:T(8,128)(2,1)} async-done(((bf16[512,4,256]{2,0,1:T(8,128)(2,1)}), bf16[512,4,256]{2,0,1:T(8,128)(2,1)}, u32[]{:S(2)}, u32[]{:S(2)}) %all-to-all-start.1) | async-done | bytes 1048608 | tf_op jit(solution)/shard_map/all_to_all | solution.py:734
  282.3 13.4 %reduce-scatter.9.cloned.1.call-done = bf16[1,32,256]{2,1,0:T(8,128)(2,1)} async-done(((bf16[8,32,256]{2,1,0:T(8,128)(2,1)}), bf16[1,32,256]{2,1,0:T(8,128)(2,1)}) %reduce-scatter.9.cloned.1.call-update) | async-done | bytes 16400 | tf_op jit(solution)/shard_map/reduce_scatter | solution.py:836
  295.7 5.4 all-gather.2
  301.3 2.3 fusion.7
  303.6 64.7 %all-reduce.8.cloned.1.call-done = f32[1,64,512]{2,1,0:T(8,128)} async-done(((f32[1,64,512]{2,1,0:T(8,128)}), f32[1,64,512]{2,1,0:T(8,128)}) %all-reduce.8.cloned.1.call-update) | async-done | bytes 131088 | tf_op jit(solution)/shard_map/psum | solution.py:861
  368.3 7.3 %all_gather.42 = f32[4,64,512]{2,1,0:T(8,128)S(1)} all-gather(f32[1,64,512]{2,1,0:T(8,128)} %all-reduce.8.cloned.1.call-done), channel_id=1, replica_groups=mesh['dp'=8,'ctx'=4] {'ctx'}, dimensions={0}, use_global_device_ids=true | all-gather | bytes 655360 | tf_op jit(solution)/shard_map/all_gather | solution.py:861
  376.8 58.5 %reduce-scatter.7.cloned.1.call-done = bf16[128,512]{1,0:T(8,128)(2,1)} async-done(((bf16[1024,512]{1,0:T(8,128)(2,1)}), bf16[128,512]{1,0:T(8,128)(2,1)}) %reduce-scatter.7.cloned.1.call-update) | async-done | bytes 131088 | tf_op jit(solution)/shard_map/reduce_scatter | solution.py:794
  435.3 65.8 %reduce-scatter.5.cloned.1.call-done = bf16[128,512]{1,0:T(8,128)(2,1)} async-done(((bf16[1024,512]{1,0:T(8,128)(2,1)}), bf16[128,512]{1,0:T(8,128)(2,1)}) %reduce-scatter.5.cloned.1.call-update) | async-done | bytes 131088 | tf_op jit(solution)/shard_map/reduce_scatter | solution.py:736
  501.1 1.7 pad_maximum_fusion.5
  504.9 62.4 %reduce-scatter.11.cloned.1.call-done = bf16[256,256]{1,0:T(8,128)(2,1)} async-done(((bf16[2048,256]{1,0:T(8,128)(2,1)}), bf16[256,256]{1,0:T(8,128)(2,1)}) %reduce-scatter.11.cloned.1.call-update) | async-done | bytes 131088 | tf_op jit(solution)/shard_map/reduce_scatter | solution.py:735
  567.3 7.4 %all_gather.43 = bf16[256,1024]{1,0:T(8,128)(2,1)S(1)} all-gather(bf16[256,256]{1,0:T(8,128)(2,1)} %reduce-scatter.11.cloned.1.call-done), channel_id=1, replica_groups=mesh['dp'=8,'ctx'=4] {'ctx'}, dimensions={1}, use_global_device_ids=true | all-gather | bytes 655360 | tf_op jit(solution)/shard_map/all_gather | solution.py:890
  574.7 3.5 multiply_subtract_fusion.1
  578.2 7.0 %all-gather.14.cloned.1.call-done = bf16[8,128,512]{2,1,0:T(8,128)(2,1)} async-done(((bf16[2,128,512]{2,1,0:T(8,128)(2,1)}), bf16[8,128,512]{2,1,0:T(8,128)(2,1)}) %all-gather.14.cloned.1.call-update) | async-done | bytes 1048592 | tf_op jit(solution)/shard_map/all_gather | solution.py:884
  592.6 6.2 %multiply_subtract_fusion = (f32[128,4352]{1,0:T(8,128)}, f32[128,4352]{1,0:T(8,128)}, f32[128,4352]{1,0:T(8,128)}) fusion(f32[128,4352]{1,0:T(8,128)S(1)} %copy-done.6, bf16[128,4352]{1,0:T(8,128)(2,1)S(1)} %bitcast_dynamic-update-slice_fusion, f32[128,4352]{1,0:T(8,128)} %param.31, f32[128,4352]{1,0:T(8,128)} %param.32), kind=kLoop, calls=%fused_computation.5 | loop fusion | flops 8912896 | bytes 14483456 | tf_op jit(solution)/shard_map/sub | solution.py:505
  (161 shorter events, 26.7 us)
Async XLA Ops:
  7.2 44.9 %copy-start.5 = (f32[1,256,1024]{2,1,0:T(8,128)S(1)}, f32[1,256,1024]{2,1,0:T(8,128)}, u32[]{:S(2)}) copy-start(f32[1,256,1024]{2,1,0:T(8,128)} %param.24) | copy-start | bytes 3145732
  7.2 64.0 %all-gather.12.cloned.1.call-start = ((), (), s32[]{:S(2)}) async-start(), calls=%async_computation.8 | async-start | bytes 1179648 | tf_op jit(solution)/shard_map/all_gather | solution.py:588
  9.0 91.5 %all-gather.8.cloned.1.call-start = ((), (), s32[]{:S(2)}) async-start(), calls=%async_computation.6 | async-start | bytes 1769472 | tf_op jit(solution)/shard_map/all_gather | solution.py:582
  12.4 129.8 %all-gather.10.cloned.1.call-start = ((), (), s32[]{:S(2)}) async-start(), calls=%async_computation.7 | async-start | bytes 1179648 | tf_op jit(solution)/shard_map/all_gather | solution.py:595
  50.6 13.2 %copy-start.4 = (bf16[256,1024]{1,0:T(8,128)(2,1)S(1)}, bf16[256,1024]{1,0:T(8,128)(2,1)}, u32[]{:S(2)}) copy-start(bf16[256,1024]{1,0:T(8,128)(2,1)} %pre_norm.1) | copy-start | bytes 1572868
  50.6 13.2 %collective-permute-start = (bf16[256,1024]{1,0:T(8,128)(2,1)}, bf16[256,1024]{1,0:T(8,128)(2,1)S(1)}, u32[]{:S(2)}, u32[]{:S(2)}) collective-permute-start(bf16[256,1024]{1,0:T(8,128)(2,1)} %pre_norm.1), channel_id=1, source_target_pairs={{0,2},{1,3},{2,0},{3,1},{4,6},{5,7},{6,4},{7,5},{8,10},{9,11},{10,... | collective-permute-start | bytes 1572872 | tf_op jit(solution)/shard_map/ppermute | solution.py:481
  53.0 16.4 %collective-permute-start.2 = (bf16[256,1024]{1,0:T(8,128)(2,1)}, bf16[256,1024]{1,0:T(8,128)(2,1)S(1)}, u32[]{:S(2)}, u32[]{:S(2)}) collective-permute-start(bf16[256,1024]{1,0:T(8,128)(2,1)} %get-tuple-element.112), channel_id=1, source_target_pairs={{0,2},{1,3},{2,0},{3,1},{4,6},{5,7},{6,4},{7,5},{8,10},{9,11},{10,... | collective-permute-start | bytes 1572872 | tf_op jit(solution)/shard_map/ppermute | solution.py:481
  63.8 6.7 %copy-start.18 = (f32[3,32]{1,0:T(4,128)S(1)}, f32[3,32]{1,0:T(4,128)}, u32[]{:S(2)}) copy-start(f32[3,32]{1,0:T(4,128)} %param.30) | copy-start | bytes 1156
  64.9 16.1 %collective-permute-start.1 = (bf16[2,256,1024]{2,1,0:T(8,128)(2,1)}, bf16[2,256,1024]{2,1,0:T(8,128)(2,1)}, u32[]{:S(2)}, u32[]{:S(2)}) collective-permute-start(bf16[2,256,1024]{2,1,0:T(8,128)(2,1)} %pad_maximum_fusion.3), channel_id=1, source_target_pairs={{0,1},{1,0},{2,3},{3,2},{4,5},{5,4},{6,7},{7,6},{8,9},{9,8},{10,11... | collective-permute-start | bytes 3145736 | tf_op jit(solution)/shard_map/ppermute | solution.py:481
  69.4 6.8 %copy-start.16 = (s32[1,1024]{1,0:T(1,128)S(1)}, s32[1,1024]{1,0:T(1,128)}, u32[]{:S(2)}) copy-start(s32[1,1024]{1,0:T(1,128)} %segr_ref.3) | copy-start | bytes 12292
  69.4 7.9 %copy-start = (s32[4]{0:T(128)S(1)}, s32[4]{0:T(128)}, u32[]{:S(2)}) copy-start(s32[4]{0:T(128)} %constant.69.clone) | copy-start | bytes 52
  70.5 13.3 %collective-permute-start.3 = (bf16[2,256,1024]{2,1,0:T(8,128)(2,1)}, bf16[2,256,1024]{2,1,0:T(8,128)(2,1)}, u32[]{:S(2)}, u32[]{:S(2)}) collective-permute-start(bf16[2,256,1024]{2,1,0:T(8,128)(2,1)} %pad_maximum_fusion.4), channel_id=1, source_target_pairs={{0,1},{1,0},{2,3},{3,2},{4,5},{5,4},{6,7},{7,6},{8,9},{9,8},{10,11... | collective-permute-start | bytes 3145736 | tf_op jit(solution)/shard_map/ppermute | solution.py:481
  71.2 18.0 %all-to-all-start = ((bf16[4,512,256]{2,1,0:T(8,128)(2,1)}), bf16[4,512,256]{2,1,0:T(8,128)(2,1)S(1)}, u32[]{:S(2)}, u32[]{:S(2)}) async-start(bf16[4,512,256]{2,1,0:T(8,128)(2,1)} %bitcast.153), calls=%async_computation | async-start | bytes 2097152 | tf_op jit(solution)/shard_map/all_to_all | solution.py:594
  74.7 221.0 %reduce-scatter.9.cloned.1.call-start = ((), (), s32[]{:S(2)}) async-start(), calls=%async_computation.11 | async-start | bytes 147456 | tf_op jit(solution)/shard_map/reduce_scatter | solution.py:836
  152.8 1.4 collective-permute-start.4
  155.0 3.9 collective-permute-start.5
  172.7 21.8 %copy-start.14 = (s32[4]{0:T(128)S(1)}, s32[4]{0:T(128)}, u32[]{:S(2)}) copy-start(s32[4]{0:T(128)} %gather_fusion) | copy-start | bytes 52
  194.4 19.1 %collective-permute-start.10 = (bf16[1024,256]{1,0:T(8,128)(2,1)}, bf16[1024,256]{1,0:T(8,128)(2,1)S(1)}, u32[]{:S(2)}, u32[]{:S(2)}) collective-permute-start(bf16[1024,256]{1,0:T(8,128)(2,1)} %get-tuple-element.69), channel_id=1, source_target_pairs={{0,1},{1,0},{2,3},{3,2},{4,5},{5,4},{6,7},{7,6},{8,9},{9,8},{10,11... | collective-permute-start | bytes 1572872 | tf_op jit(solution)/shard_map/ppermute | solution.py:481
  204.2 9.4 %copy-start.11 = (bf16[1024,256]{1,0:T(8,128)(2,1)S(1)}, bf16[1024,256]{1,0:T(8,128)(2,1)}, u32[]{:S(2)}) copy-start(bf16[1024,256]{1,0:T(8,128)(2,1)} %get-tuple-element.69) | copy-start | bytes 1572868
  211.6 3.7 copy-start.1
  213.0 25.3 %collective-permute-start.8 = (bf16[2,256,1024]{2,1,0:T(8,128)(2,1)S(1)}, bf16[2,256,1024]{2,1,0:T(8,128)(2,1)}, u32[]{:S(2)}, u32[]{:S(2)}) collective-permute-start(bf16[2,256,1024]{2,1,0:T(8,128)(2,1)S(1)} %slice.202), channel_id=1, source_target_pairs={{0,1},{1,0},{2,3},{3,2},{4,5},{5,4},{6,7},{7,6},{8,9},{9,8},{10,11... | collective-permute-start | bytes 3145736 | tf_op jit(solution)/shard_map/ppermute | solution.py:481
  213.7 13.9 %collective-permute-start.11 = (bf16[1024,256]{1,0:T(8,128)(2,1)S(1)}, bf16[1024,256]{1,0:T(8,128)(2,1)S(1)}, u32[]{:S(2)}, u32[]{:S(2)}) collective-permute-start(bf16[1024,256]{1,0:T(8,128)(2,1)S(1)} %add_convert_fusion), channel_id=1, source_target_pairs={{0,2},{1,3},{2,0},{3,1},{4,6},{5,7},{6,4},{7,5},{8,10},{9,11},{10,... | collective-permute-start | bytes 1572872 | tf_op jit(solution)/shard_map/ppermute | solution.py:481
  216.9 6.0 copy-start.22
  216.9 6.0 copy-start.21
  228.7 9.6 %copy-start.3 = (bf16[4,256,1024]{2,1,0:T(8,128)(2,1)S(1)}, bf16[4,256,1024]{2,1,0:T(8,128)(2,1)}, u32[]{:S(2)}) copy-start(bf16[4,256,1024]{2,1,0:T(8,128)(2,1)} %hidden_back.1) | copy-start | bytes 6291460
  236.0 132.3 %all-reduce.8.cloned.1.call-start = ((), (), s32[]{:S(2)}) async-start(), calls=%async_computation.12 | async-start | bytes 262144 | tf_op jit(solution)/shard_map/psum | solution.py:861
  238.3 3.2 copy-start.26
  238.3 3.3 copy-start.17
  240.0 13.1 %collective-permute-start.9 = (bf16[256,1024]{1,0:T(8,128)(2,1)S(1)}, bf16[256,1024]{1,0:T(8,128)(2,1)S(1)}, u32[]{:S(2)}, u32[]{:S(2)}) collective-permute-start(bf16[256,1024]{1,0:T(8,128)(2,1)S(1)} %fusion.9), channel_id=1, source_target_pairs={{0,2},{1,3},{2,0},{3,1},{4,6},{5,7},{6,4},{7,5},{8,10},{9,11},{10,... | collective-permute-start | bytes 1572872 | tf_op jit(solution)/shard_map/ppermute | solution.py:481
  254.2 6.6 %copy-start.7 = (bf16[4,256,1024]{2,1,0:T(8,128)(2,1)S(1)}, bf16[4,256,1024]{2,1,0:T(8,128)(2,1)}, u32[]{:S(2)}) copy-start(bf16[4,256,1024]{2,1,0:T(8,128)(2,1)} %get-tuple-element.56) | copy-start | bytes 6291460
  259.5 0.7 copy-start.12
  260.2 175.1 %reduce-scatter.7.cloned.1.call-start = ((), (), s32[]{:S(2)}) async-start(), calls=%async_computation.10 | async-start | bytes 1179648 | tf_op jit(solution)/shard_map/reduce_scatter | solution.py:794
  260.3 1.7 copy-start.9
  260.8 240.3 %reduce-scatter.5.cloned.1.call-start = ((), (), s32[]{:S(2)}) async-start(), calls=%async_computation.9 | async-start | bytes 1179648 | tf_op jit(solution)/shard_map/reduce_scatter | solution.py:736
  261.9 5.4 collective-permute-start.6
  263.0 19.3 %all-to-all-start.1 = ((bf16[512,4,256]{2,0,1:T(8,128)(2,1)}), bf16[512,4,256]{2,0,1:T(8,128)(2,1)}, u32[]{:S(2)}, u32[]{:S(2)}) async-start(bf16[512,4,256]{2,0,1:T(8,128)(2,1)} %bitcast.131), calls=%async_computation.4 | async-start | bytes 2097152 | tf_op jit(solution)/shard_map/all_to_all | solution.py:734
  267.2 300.1 %reduce-scatter.11.cloned.1.call-start = ((), (), s32[]{:S(2)}) async-start(), calls=%async_computation.13 | async-start | bytes 1179648 | tf_op jit(solution)/shard_map/reduce_scatter | solution.py:735
  269.2 32.1 %copy-start.2 = (f32[1,256,1024]{2,1,0:T(8,128)S(1)}, f32[1,256,1024]{2,1,0:T(8,128)}, u32[]{:S(2)}) copy-start(f32[1,256,1024]{2,1,0:T(8,128)} %param.22) | copy-start | bytes 3145732
  270.1 31.2 %collective-permute-start.7 = (bf16[256,1024]{1,0:T(8,128)(2,1)}, bf16[256,1024]{1,0:T(8,128)(2,1)}, u32[]{:S(2)}, u32[]{:S(2)}) collective-permute-start(bf16[256,1024]{1,0:T(8,128)(2,1)} %fusion.8), channel_id=1, source_target_pairs={{0,2},{1,3},{2,0},{3,1},{4,6},{5,7},{6,4},{7,5},{8,10},{9,11},{10,... | collective-permute-start | bytes 1572872 | tf_op jit(solution)/shard_map/ppermute | solution.py:481
  282.3 303.0 %all-gather.14.cloned.1.call-start = ((), (), s32[]{:S(2)}) async-start(), calls=%async_computation.14 | async-start | bytes 1310720 | tf_op jit(solution)/shard_map/all_gather | solution.py:884
  301.2 74.9 %copy-start.27 = (f32[3,32]{1,0:T(4,128)S(1)}, f32[3,32]{1,0:T(4,128)}, u32[]{:S(2)}) copy-start(f32[3,32]{1,0:T(4,128)} %param.41) | copy-start | bytes 1156
  301.2 74.9 %copy-start.28 = (f32[3,32]{1,0:T(4,128)S(1)}, f32[3,32]{1,0:T(4,128)}, u32[]{:S(2)}) copy-start(f32[3,32]{1,0:T(4,128)} %param.42) | copy-start | bytes 1156
  301.2 201.6 %copy-start.25 = (f32[384]{0:T(512)S(1)}, f32[384]{0:T(512)}, u32[]{:S(2)}) copy-start(f32[384]{0:T(512)} %param.29) | copy-start | bytes 4612
  301.2 201.6 %copy-start.29 = (f32[384]{0:T(512)S(1)}, f32[384]{0:T(512)}, u32[]{:S(2)}) copy-start(f32[384]{0:T(512)} %param.39) | copy-start | bytes 4612
  301.2 201.6 %copy-start.30 = (f32[384]{0:T(512)S(1)}, f32[384]{0:T(512)}, u32[]{:S(2)}) copy-start(f32[384]{0:T(512)} %param.40) | copy-start | bytes 4612
  301.2 202.3 %copy-start.15 = (f32[5,288]{1,0:T(8,128)S(1)}, f32[5,288]{1,0:T(8,128)}, u32[]{:S(2)}) copy-start(f32[5,288]{1,0:T(8,128)} %param.28) | copy-start | bytes 17284
  301.2 202.3 %copy-start.23 = (f32[5,288]{1,0:T(8,128)S(1)}, f32[5,288]{1,0:T(8,128)}, u32[]{:S(2)}) copy-start(f32[5,288]{1,0:T(8,128)} %param.37) | copy-start | bytes 17284
  301.2 202.3 %copy-start.24 = (f32[5,288]{1,0:T(8,128)S(1)}, f32[5,288]{1,0:T(8,128)}, u32[]{:S(2)}) copy-start(f32[5,288]{1,0:T(8,128)} %param.38) | copy-start | bytes 17284
  301.2 203.0 %copy-start.13 = (f32[32,128]{1,0:T(8,128)S(1)}, f32[32,128]{1,0:T(8,128)}, u32[]{:S(2)}) copy-start(f32[32,128]{1,0:T(8,128)} %param.26) | copy-start | bytes 49156
  301.3 203.0 %copy-start.19 = (f32[32,128]{1,0:T(8,128)S(1)}, f32[32,128]{1,0:T(8,128)}, u32[]{:S(2)}) copy-start(f32[32,128]{1,0:T(8,128)} %param.33) | copy-start | bytes 49156
  301.3 203.0 %copy-start.20 = (f32[32,128]{1,0:T(8,128)S(1)}, f32[32,128]{1,0:T(8,128)}, u32[]{:S(2)}) copy-start(f32[32,128]{1,0:T(8,128)} %param.34) | copy-start | bytes 49156
  303.6 271.1 %copy-start.8 = (f32[256,1024]{1,0:T(8,128)S(1)}, f32[256,1024]{1,0:T(8,128)}, u32[]{:S(2)}) copy-start(f32[256,1024]{1,0:T(8,128)} %param.27) | copy-start | bytes 3145732
  303.6 271.1 %copy-start.10 = (f32[256,1024]{1,0:T(8,128)S(1)}, f32[256,1024]{1,0:T(8,128)}, u32[]{:S(2)}) copy-start(f32[256,1024]{1,0:T(8,128)} %param.35) | copy-start | bytes 3145732
  578.2 14.4 %copy-start.6 = (f32[128,4352]{1,0:T(8,128)S(1)}, f32[128,4352]{1,0:T(8,128)}, u32[]{:S(2)}) copy-start(f32[128,4352]{1,0:T(8,128)} %param.25) | copy-start | bytes 6684676
Sparse Core Ops, SparseCore 0:
  10.7 43.8 all-gather.11
  57.4 43.0 all-gather.7
  103.2 38.9 all-gather.9
  236.1 59.5 reduce-scatter.8
  299.5 68.7 all-reduce.7
  372.5 62.6 reduce-scatter.6
  438.7 62.3 reduce-scatter.4
  504.8 62.4 reduce-scatter.10
  569.5 15.7 all-gather.13

commit v2 on v1

--- a/solution.py
+++ b/solution.py
@@ -90,6 +90,28 @@
     )
 
 
+def place(pieces, at_ref, target, sems, first=0):
+    copies = []
+    for index, piece in enumerate(pieces):
+        rows = piece.shape[0]
+        start = pl.multiple_of(at_ref[index] * rows, 16)
+        copies.append(
+            pltpu.make_async_copy(piece, target.at[pl.ds(start, rows), :], sems.at[first + index])
+        )
+    for copy in copies:
+        copy.start()
+    return copies
+
+
+def part_rows(total, own_bit, keep_ref, send_ref):
+    count, rows, _ = keep_ref.shape
+    for at in range(count):
+        low = total[2 * at * rows : (2 * at + 1) * rows].astype(BF16)
+        high = total[(2 * at + 1) * rows : (2 * at + 2) * rows].astype(BF16)
+        keep_ref[at] = jnp.where(own_bit == 0, low, high)
+        send_ref[at] = jnp.where(own_bit == 0, high, low)
+
+
 def norm_kernel(tok_ref, gain_ref, hid_ref):
     tok = tok_ref[...]
     scale = lax.rsqrt(jnp.mean(tok * tok, axis=-1, keepdims=True) + NORM_EPS)
@@ -98,8 +120,9 @@
 
 def scan_forward_kernel(
     perm_ref,
+    at_ref,
     hid_ref,
-    w1_ref,
+    w1_pieces,
     wdt_ref,
     conv_ref,
     hrow_ref,
@@ -119,6 +142,8 @@
     ext_ref,
     seg_ref,
     state_ref,
+    w1_ref,
+    sems,
 ):
     step = pl.program_id(0)
     span = hid_ref.shape[1]
@@ -127,8 +152,11 @@
 
     @pl.when(step == 0)
     def _():
+        copies = place(w1_pieces, at_ref, w1_ref, sems)
         ext_ref[0:8] = jnp.zeros((8, ext_ref.shape[1]), F32)
         state_ref[...] = jnp.zeros_like(state_ref)
+        for copy in copies:
+            copy.wait()
 
     hid = hid_ref[0]
     proj = nn(hid, w1_ref[...]).astype(BF16)
@@ -193,7 +221,26 @@
     )
 
 
-def gate_kernel(perm_ref, hid_ref, wg_ref, inner_ref, cot_ref, wout_ref, gain_ref, gate_ref, ng_ref, stat_ref):
+def gate_kernel(
+    perm_ref,
+    at_ref,
+    hid_ref,
+    wg_pieces,
+    inner_ref,
+    cot_ref,
+    wout_ref,
+    gain_ref,
+    gate_ref,
+    ng_ref,
+    stat_ref,
+    wg_ref,
+    sems,
+):
+    @pl.when(pl.program_id(0) == 0)
+    def _():
+        for copy in place(wg_pieces, at_ref, wg_ref, sems):
+            copy.wait()
+
     gate = nn(hid_ref[0], wg_ref[...]).astype(BF16)
     gate_ref[...] = gate
     gate = gate.astype(F32)
@@ -209,6 +256,7 @@
 
 def norm_back_kernel(
     perm_ref,
+    here_ref,
     hid_ref,
     inner_ref,
     gate_ref,
@@ -219,8 +267,9 @@
     wout_ref,
     mixed_ref,
     block_ref,
-    outg_ref,
-    ing_ref,
+    outg_refs,
+    keep_ref,
+    send_ref,
     dy_ref,
     dgate_ref,
     sums_ref,
@@ -266,12 +315,16 @@
 
     @pl.when(step == pl.num_programs(0) - 1)
     def _():
-        outg_ref[...] = outacc_ref[...].astype(BF16)
-        ing_ref[...] = inacc_ref[...].astype(BF16)
+        cols = outg_refs[0].shape[1]
+        for at, outg_ref in enumerate(outg_refs):
+            start = pl.multiple_of((here_ref[2] ^ at) * cols, 128)
+            outg_ref[...] = outacc_ref[:, pl.ds(start, cols)].astype(BF16)
+        part_rows(inacc_ref, here_ref[0], keep_ref, send_ref)
 
 
 def scan_back_kernel(
     perm_ref,
+    here_ref,
     hid_ref,
     dy_ref,
     mixed_ref,
@@ -287,7 +340,8 @@
     hrow_ref,
     segc_ref,
     segr_ref,
-    ing_ref,
+    keep_ref,
+    send_ref,
     dval_ref,
     dbc_ref,
     dstep_ref,
@@ -436,15 +490,66 @@
 
     @pl.when(step == pl.num_programs(0) - 1)
     def _():
-        ing_ref[...] = inacc_ref[...].astype(BF16)
-
-
-def hidden_back_kernel(perm_ref, dgate_ref, dval_ref, dstep_ref, wg_ref, wv_ref, wdt_ref, out_ref):
-    total = nt(dgate_ref[...], wg_ref[...]) + nt(dval_ref[...], wv_ref[...])
-    out_ref[0] = (total + nn(dstep_ref[...], wdt_ref[...])).astype(BF16)
-
-
-def maps_back_kernel(dbc_ref, convsum_ref, convin_ref, conv_ref, segc_ref, hid_ref, dmap_ref, convg_ref, ing_ref, ext_ref):
+        part_rows(inacc_ref, here_ref[0], keep_ref, send_ref)
+
+
+def hidden_back_kernel(
+    perm_ref,
+    at_ref,
+    dgate_ref,
+    dval_ref,
+    dstep_ref,
+    wg_pieces,
+    w1_pieces,
+    wdt_ref,
+    hid_ref,
+    gain_ref,
+    out_ref,
+    gsum_ref,
+    wg_ref,
+    wv_ref,
+    sems,
+):
+    @pl.when(pl.program_id(0) == 0)
+    def _():
+        copies = place(wg_pieces, at_ref, wg_ref, sems)
+        copies += place(w1_pieces, at_ref, wv_ref, sems, len(wg_pieces))
+        gsum_ref[...] = jnp.zeros_like(gsum_ref)
+        for copy in copies:
+            copy.wait()
+
+    width = wg_ref.shape[1]
+    total = nt(dgate_ref[...], wg_ref[...]) + nt(dval_ref[...], wv_ref[:, :width])
+    total = total + nn(dstep_ref[...], wdt_ref[...])
+    out_ref[0] = total.astype(BF16)
+    unit = hid_ref[0].astype(F32) / gain_ref[...]
+    gsum_ref[...] += jnp.sum(total * unit, axis=0, keepdims=True) + jnp.zeros(gsum_ref.shape, F32)
+
+
+def maps_back_kernel(
+    perm_ref,
+    at_ref,
+    here_ref,
+    dbc_ref,
+    convsum_ref,
+    convin_ref,
+    conv_ref,
+    segc_ref,
+    hid_ref,
+    w1_pieces,
+    gain_ref,
+    convg_ref,
+    keep_ref,
+    send_ref,
+    own_ref,
+    gsum_ref,
+    ext_ref,
+    acc_ref,
+    dmap_ref,
+    w1_ref,
+    sems,
+):
+    copies = place(w1_pieces, at_ref, w1_ref, sems)
     size, width = dmap_ref.shape
     ext_ref[0:size] = dbc_ref[...] * silu_grad(convsum_ref[...])
     ext_ref[size : size + 8] = jnp.zeros((8, width), F32)
@@ -460,20 +565,90 @@
         back = back + conv_ref[tap : tap + 1] * term
         sums = sums + jnp.where(at == tap, jnp.sum(conv_in * term, axis=0, keepdims=True), 0.0)
     convg_ref[...] = sums
-    dmap = back.astype(BF16)
-    dmap_ref[...] = dmap
-    ing_ref[...] = tn(hid_ref[...], dmap).astype(BF16)
-
-
-def input_back_kernel(hg_ref, dmap_ref, wbc_ref, tok_ref, gain_ref, cot_ref, out_ref, gsum_ref):
-    grad = hg_ref[...] + nt(dmap_ref[...], wbc_ref[...])
+    dmap_ref[...] = back.astype(BF16)
+    pieces, span, _ = hid_ref.shape
+    total = None
+    for index in range(pieces):
+        part = tn(hid_ref[perm_ref[index]], dmap_ref[index * span : (index + 1) * span])
+        total = part if total is None else total + part
+    acc_ref[...] = total
+    count, rows, _ = keep_ref.shape
+    for at_block in range(count):
+        start = pl.multiple_of((2 * at_block * pieces + here_ref[2]) * rows, 8)
+        low = acc_ref[pl.ds(start, rows), :].astype(BF16)
+        start = pl.multiple_of(((2 * at_block + 1) * pieces + here_ref[2]) * rows, 8)
+        high = acc_ref[pl.ds(start, rows), :].astype(BF16)
+        keep_ref[at_block] = jnp.where(here_ref[0] == 0, low, high)
+        send_ref[at_block] = jnp.where(here_ref[0] == 0, high, low)
+    own = dmap_ref[pl.ds(pl.multiple_of(here_ref[2] * span, 16), span), :]
+    for copy in copies:
+        copy.wait()
+    grad = nt(own, w1_ref[:, w1_ref.shape[1] - width :])
+    own_ref[...] = grad
+    unit = hid_ref[0].astype(F32) / gain_ref[...]
+    gsum_ref[...] = jnp.sum(grad * unit, axis=0, keepdims=True) + jnp.zeros(gsum_ref.shape, F32)
+
+
+def input_back_kernel(hg_ref, own_ref, tok_ref, gain_ref, cot_ref, out_ref):
+    grad = hg_ref[...] + own_ref[...]
     tok = tok_ref[...]
     scale = lax.rsqrt(jnp.mean(tok * tok, axis=-1, keepdims=True) + NORM_EPS)
     unit = tok * scale
-    gsum_ref[...] = jnp.sum(grad * unit, axis=0, keepdims=True) + jnp.zeros(gsum_ref.shape, F32)
     scaled = grad * gain_ref[...]
     mean = jnp.mean(scaled * unit, axis=-1, keepdims=True)
     out_ref[...] = cot_ref[...] + scale * (scaled - unit * mean)
+
+
+def split_kernel(here_ref, part_refs, keep_ref, send_ref):
+    rows = keep_ref.shape[1]
+    for at, part_ref in enumerate(part_refs):
+        place_at = here_ref[2] ^ at
+        low, high = part_ref[0:rows], part_ref[rows : 2 * rows]
+        keep_ref[pl.ds(place_at, 1)] = jnp.where(here_ref[0] == 0, low, high)[None]
+        send_ref[pl.ds(place_at, 1)] = jnp.where(here_ref[0] == 0, high, low)[None]
+
+
+def pair_sum_kernel(here_ref, keep_ref, came_ref, out_refs):
+    for at, out_ref in enumerate(out_refs):
+        index = pl.ds(here_ref[1] ^ at, 1)
+        out_ref[...] = (keep_ref[index].astype(F32) + came_ref[index].astype(F32))[0].astype(BF16)
+
+
+def adam_in_kernel(
+    here_ref, weight_ref, first_ref, second_ref, gate_refs, value_refs, map_refs, *rest
+):
+    new_refs, (cols_ref, maps_ref) = rest[:3], rest[3:]
+    step = pl.program_id(0)
+    pieces = len(gate_refs)
+    rows, width = gate_refs[0].shape
+    block = weight_ref.shape[1]
+    per = width // block
+
+    @pl.when(step == 0)
+    def _():
+        for at in range(pieces):
+            owner = here_ref[2] ^ at
+            cols_ref[pl.ds(owner, 1)] = gate_refs[at][...][None]
+            cols_ref[pl.ds(pieces + owner, 1)] = value_refs[at][...][None]
+            some = map_refs[at].shape[0]
+            maps_ref[pl.ds(pl.multiple_of(owner * some, some), some), :] = map_refs[at][...]
+
+    last = pl.num_programs(0) - 1
+
+    @pl.when(step < last)
+    def _():
+        grad = cols_ref[step // per, :, pl.ds(pl.multiple_of((step % per) * block, 128), block)]
+        news = adam_step(weight_ref[...], first_ref[...], second_ref[...], grad.astype(F32), 0.03, WEIGHT_DECAY)
+        for ref, new in zip(new_refs, news):
+            ref[...] = new
+
+    @pl.when(step == last)
+    def _():
+        news = adam_step(
+            weight_ref[...], first_ref[...], second_ref[...], maps_ref[...].astype(F32), 0.03, WEIGHT_DECAY
+        )
+        for ref, new in zip(new_refs, news):
+            ref[...] = new
 
 
 def swap(value, axis, bit):
@@ -495,6 +670,50 @@
     pair = value.astype(F32) + swap(value, "ctx", 1).astype(F32)
     pair = pair.astype(BF16)
     return pair.astype(F32) + swap(pair, "ctx", 2).astype(F32)
+
+
+def gather_dp(value):
+    count, here = lax.axis_size("dp"), lax.axis_index("dp")
+    if count > 8 or count & (count - 1) or value.shape[0] % 16:
+        return [lax.all_gather(value, "dp", axis=0, tiled=True)], jnp.zeros((1,), jnp.int32)
+    pieces = [(value, 0)] + [(swap(value, "dp", bit), bit) for bit in range(2, count, 2)]
+    if count > 1:
+        pieces += [(swap(piece, "dp", 1), bit + 1) for piece, bit in pieces]
+    return [piece for piece, _ in pieces], here ^ jnp.asarray([bit for _, bit in pieces], jnp.int32)
+
+
+def scatter_dp(keep, send, here, name):
+    count, rows, cols = keep.shape
+    if 2 * count != lax.axis_size("dp"):
+        return keep[0]
+    came = swap(send, "dp", 1)
+    if count > 4 or rows % 16:
+        part = keep.astype(F32) + came.astype(F32)
+        stride, high = 2, here[1]
+        while part.shape[0] > 1:
+            size = min(4, part.shape[0])
+            low = part.astype(BF16).reshape(part.shape[0] // size, size, rows, cols)
+            part = 0.0
+            for at in range(size):
+                term = lax.dynamic_index_in_dim(low, (high % size) ^ at, 1, keepdims=False)
+                part = part + (swap(term, "dp", stride * at) if at else term).astype(F32)
+            stride, high = stride * size, high // size
+        return part[0].astype(BF16)
+    parts = pl.pallas_call(
+        pair_sum_kernel,
+        in_specs=[pl.BlockSpec(memory_space=pltpu.SMEM)] + [pl.BlockSpec(memory_space=pltpu.VMEM)] * 2,
+        out_shape=[[shape_of(rows, cols, dtype=BF16)] * count],
+        compiler_params=params(),
+        name="pair_sum_" + name,
+    )(here, keep, came)[0]
+    total = parts[0].astype(F32)
+    for at in range(1, count):
+        total = total + swap(parts[at], "dp", 2 * at).astype(F32)
+    return total.astype(BF16)
+
+
+def fan_ctx(value):
+    return [value] + [swap(value, "ctx", bit) for bit in range(1, lax.axis_size("ctx"))]
 
 
 def adam_step(weight, moment_one, second, gradient, step_rate, decay_rate):
@@ -579,11 +798,8 @@
     conv_mine = jnp.pad(conv_mine, ((0, 8 - CONV - 1), (0, 0)))
 
     value_part = lax.dynamic_slice_in_dim(in_weight, INNER + c * width, width, 1)
-    w1 = lax.all_gather(
-        jnp.concatenate([value_part, in_weight[:, 2 * INNER :]], axis=1).astype(BF16),
-        "dp",
-        axis=0,
-        tiled=True,
+    w1, at_rows = gather_dp(
+        jnp.concatenate([value_part, in_weight[:, 2 * INNER :]], axis=1).astype(BF16)
     )
     wout = lax.all_gather(
         lax.dynamic_slice_in_dim(out_weight, c * cols_out, cols_out, 1).astype(BF16),
@@ -592,12 +808,8 @@
         tiled=True,
     )
     wout = lax.all_to_all(wout, "ctx", split_axis=0, concat_axis=1, tiled=True)
-    wg = lax.all_gather(
-        lax.dynamic_slice_in_dim(in_weight, c * width, width, 1).astype(BF16),
-        "dp",
-        axis=0,
-        tiled=True,
-    )
+    wg, _ = gather_dp(lax.dynamic_slice_in_dim(in_weight, c * width, width, 1).astype(BF16))
+    here = jnp.stack([d & 1, d >> 1, c]).astype(jnp.int32)
 
     order = jnp.asarray([0, 2, 1, 3], jnp.int32)
     perm = order[jnp.arange(nctx, dtype=jnp.int32) ^ c]
@@ -613,24 +825,26 @@
     head_mine = lax.dynamic_slice_in_dim(head_params, c * heads, heads, 1)
     head_col = head_mine.T
 
-    slot_rows = pl.BlockSpec((1, span, model), lambda i, p: (p[i], 0, 0))
-    rows = lambda cols: pl.BlockSpec((span, cols), lambda i, p: (i, 0))
-    row_of = pl.BlockSpec((heads, span), lambda i, p: (0, i))
+    anywhere = lambda pieces: [pl.BlockSpec(memory_space=pl.ANY)] * len(pieces)
+    blocks_of = lambda rows, cols: [shape_of(ndp // 2, rows, cols, dtype=BF16)] * 2
+    slot_rows = pl.BlockSpec((1, span, model), lambda i, p, *_: (p[i], 0, 0))
+    rows = lambda cols: pl.BlockSpec((span, cols), lambda i, *_: (i, 0))
+    row_of = pl.BlockSpec((heads, span), lambda i, *_: (0, i))
 
     mixed, conv_in, conv_sum, inner, raw, step_c, log_c, step_r, log_r, starts = pl.pallas_call(
         scan_forward_kernel,
         grid_spec=pltpu.PrefetchScalarGridSpec(
-            num_scalar_prefetch=1,
+            num_scalar_prefetch=2,
             grid=(chunks,),
             in_specs=[
                 slot_rows,
-                full((model, wide)),
+                anywhere(w1),
                 full((heads, model)),
                 full((8, wide)),
                 full((3, heads)),
                 full((heads, 3)),
                 full((length + 16, 1)),
-                pl.BlockSpec((1, span), lambda i, p: (0, i)),
+                pl.BlockSpec((1, span), lambda i, *_: (0, i)),
             ],
             out_specs=[
                 rows(wide),
@@ -642,12 +856,14 @@
                 rows(heads),
                 row_of,
                 row_of,
-                pl.BlockSpec((1, STATE, width), lambda i, p: (i, 0, 0)),
+                pl.BlockSpec((1, STATE, width), lambda i, *_: (i, 0, 0)),
             ],
             scratch_shapes=[
                 pltpu.VMEM((span + 8, wide), F32),
                 pltpu.VMEM((span + 8, 1), jnp.int32),
                 pltpu.VMEM((STATE, width), F32),
+                pltpu.VMEM((model, wide), BF16),
+                pltpu.SemaphoreType.DMA((len(w1),)),
             ],
         ),
         out_shape=[
@@ -664,22 +880,23 @@
         ],
         compiler_params=params("arbitrary"),
         name="scan_forward",
-    )(perm, hid_all, w1, dt_mine, conv_mine, head_mine, head_col, seg_col, seg_row)
+    )(perm, at_rows, hid_all, w1, dt_mine, conv_mine, head_mine, head_col, seg_col, seg_row)
 
     gate, normed_grad, stats = pl.pallas_call(
         gate_kernel,
         grid_spec=pltpu.PrefetchScalarGridSpec(
-            num_scalar_prefetch=1,
+            num_scalar_prefetch=2,
             grid=(chunks,),
             in_specs=[
                 slot_rows,
-                full((model, width)),
+                anywhere(wg),
                 rows(width),
                 slot_rows,
                 full((width, model)),
                 full((1, width)),
             ],
-            out_specs=[rows(width), rows(width), pl.BlockSpec((8, span), lambda i, p: (0, i))],
+            out_specs=[rows(width), rows(width), pl.BlockSpec((8, span), lambda i, *_: (0, i))],
+            scratch_shapes=[pltpu.VMEM((model, width), BF16), pltpu.SemaphoreType.DMA((len(wg),))],
         ),
         out_shape=[
             shape_of(length, width, dtype=BF16),
@@ -688,21 +905,20 @@
         ],
         compiler_params=params("arbitrary"),
         name="gate",
-    )(perm, hid_all, wg, inner, cot_all, wout, gain_mine)
-    stats = stats + swap(stats, "ctx", 1)
-    stats = stats + swap(stats, "ctx", 2)
-
-    block_part, out_grad, gate_in_grad, dy, dgate, col_sums = pl.pallas_call(
+    )(perm, at_rows, hid_all, wg, inner, cot_all, wout, gain_mine)
+    stats = sum(fan_ctx(stats))
+
+    block_part, out_grads, gate_keep, gate_send, dy, dgate, col_sums = pl.pallas_call(
         norm_back_kernel,
         grid_spec=pltpu.PrefetchScalarGridSpec(
-            num_scalar_prefetch=1,
+            num_scalar_prefetch=2,
             grid=(chunks,),
             in_specs=[
                 slot_rows,
                 rows(width),
                 rows(width),
                 rows(width),
-                pl.BlockSpec((8, span), lambda i, p: (0, i)),
+                pl.BlockSpec((8, span), lambda i, *_: (0, i)),
                 full((1, width)),
                 slot_rows,
                 full((width, model)),
@@ -710,8 +926,9 @@
             ],
             out_specs=[
                 slot_rows,
-                full((width, model)),
-                full((model, width)),
+                [full((width, cols_out))] * nctx,
+                full((ndp // 2, rows_in, width)),
+                full((ndp // 2, rows_in, width)),
                 rows(width),
                 rows(width),
                 full((8, width)),
@@ -720,30 +937,49 @@
         ),
         out_shape=[
             shape_of(nctx, span, model, dtype=BF16),
-            shape_of(width, model, dtype=BF16),
-            shape_of(model, width, dtype=BF16),
+            [shape_of(width, cols_out, dtype=BF16)] * nctx,
+            *blocks_of(rows_in, width),
             shape_of(length, width),
             shape_of(length, width, dtype=BF16),
             shape_of(8, width),
         ],
         compiler_params=params("arbitrary"),
         name="norm_back",
-    )(perm, hid_all, inner, gate, normed_grad, stats, gain_mine, cot_all, wout, mixed)
+    )(perm, here, hid_all, inner, gate, normed_grad, stats, gain_mine, cot_all, wout, mixed)
 
     block_output = tok + scatter_ctx(block_part)
-    out_cols = lax.all_to_all(out_grad, "ctx", split_axis=1, concat_axis=0, tiled=True)
-    out_shard = lax.psum_scatter(out_cols, "dp", scatter_dimension=0, tiled=True)
-    gate_shard = lax.psum_scatter(gate_in_grad, "dp", scatter_dimension=0, tiled=True)
-
-    back = lambda cols: pl.BlockSpec((span, cols), lambda i, p: (chunks - 1 - i, 0))
-    back_row = pl.BlockSpec((heads, span), lambda i, p: (0, chunks - 1 - i))
-    value_in_grad, dval, dbc, dstep, conv_grad, dt_grad, head_grad = pl.pallas_call(
+    gate_shard = scatter_dp(gate_keep, gate_send, here, "gate")
+    if ndp == 2 * nctx:
+        out_grads = [
+            swap(part, "ctx", bit) if bit else part for bit, part in enumerate(out_grads)
+        ]
+        out_keep, out_send = pl.pallas_call(
+            split_kernel,
+            in_specs=[
+                pl.BlockSpec(memory_space=pltpu.SMEM),
+                [pl.BlockSpec(memory_space=pltpu.VMEM)] * nctx,
+            ],
+            out_shape=blocks_of(rows_out, cols_out),
+            compiler_params=params(),
+            name="out_split",
+        )(here, out_grads)
+        out_shard = scatter_dp(out_keep, out_send, here, "out")
+    else:
+        natural = [lax.dynamic_index_in_dim(jnp.stack(out_grads), c ^ at, 0, False) for at in range(nctx)]
+        out_grad = lax.all_to_all(
+            jnp.concatenate(natural, axis=1), "ctx", split_axis=1, concat_axis=0, tiled=True
+        )
+        out_shard = lax.psum_scatter(out_grad, "dp", scatter_dimension=0, tiled=True)
+
+    back = lambda cols: pl.BlockSpec((span, cols), lambda i, *_: (chunks - 1 - i, 0))
+    back_row = pl.BlockSpec((heads, span), lambda i, *_: (0, chunks - 1 - i))
+    value_keep, value_send, dval, dbc, dstep, conv_grad, dt_grad, head_grad = pl.pallas_call(
         scan_back_kernel,
         grid_spec=pltpu.PrefetchScalarGridSpec(
-            num_scalar_prefetch=1,
+            num_scalar_prefetch=2,
             grid=(chunks,),
             in_specs=[
-                pl.BlockSpec((1, span, model), lambda i, p: (p[chunks - 1 - i], 0, 0)),
+                pl.BlockSpec((1, span, model), lambda i, p, *_: (p[chunks - 1 - i], 0, 0)),
                 back(width),
                 back(wide),
                 back(width),
@@ -753,14 +989,15 @@
                 back(heads),
                 back_row,
                 back_row,
-                pl.BlockSpec((1, STATE, width), lambda i, p: (chunks - 1 - i, 0, 0)),
+                pl.BlockSpec((1, STATE, width), lambda i, *_: (chunks - 1 - i, 0, 0)),
                 full((8, width)),
                 full((3, heads)),
                 full((length + 16, 1)),
-                pl.BlockSpec((1, span), lambda i, p: (0, chunks - 1 - i)),
+                pl.BlockSpec((1, span), lambda i, *_: (0, chunks - 1 - i)),
             ],
             out_specs=[
-                full((model, width)),
+                full((ndp // 2, rows_in, width)),
+                full((ndp // 2, rows_in, width)),
                 back(width),
                 back(maps),
                 back(heads),
@@ -777,7 +1014,7 @@
             ],
         ),
         out_shape=[
-            shape_of(model, width, dtype=BF16),
+            *blocks_of(rows_in, width),
             shape_of(length, width, dtype=BF16),
             shape_of(length, maps, dtype=BF16),
             shape_of(length, heads, dtype=BF16),
@@ -788,108 +1025,164 @@
         compiler_params=params("arbitrary"),
         name="scan_back",
     )(
-        perm, hid_all, dy, mixed, conv_in, conv_sum, raw, step_c, log_c, step_r, log_r, starts,
+        perm, here, hid_all, dy, mixed, conv_in, conv_sum, raw, step_c, log_c, step_r, log_r, starts,
         conv_mine, head_mine, seg_col, seg_row,
     )
-    value_shard = lax.psum_scatter(value_in_grad, "dp", scatter_dimension=0, tiled=True)
+    value_shard = scatter_dp(value_keep, value_send, here, "value")
     dbc_total = sum_ctx(dbc)
 
-    hidden_part = pl.pallas_call(
+    hidden_part, gain_sum = pl.pallas_call(
         hidden_back_kernel,
         grid_spec=pltpu.PrefetchScalarGridSpec(
-            num_scalar_prefetch=1,
+            num_scalar_prefetch=2,
             grid=(chunks,),
             in_specs=[
                 rows(width),
                 rows(width),
                 rows(heads),
-                full((model, width)),
-                full((model, width)),
+                anywhere(wg),
+                anywhere(w1),
                 full((heads, model)),
+                slot_rows,
+                full((1, model)),
             ],
-            out_specs=[slot_rows],
+            out_specs=[slot_rows, full((8, model))],
+            scratch_shapes=[
+                pltpu.VMEM((model, width), BF16),
+                pltpu.VMEM((model, wide), BF16),
+                pltpu.SemaphoreType.DMA((len(wg) + len(w1),)),
+            ],
         ),
-        out_shape=[shape_of(nctx, span, model, dtype=BF16)],
+        out_shape=[shape_of(nctx, span, model, dtype=BF16), shape_of(8, model)],
         compiler_params=params("arbitrary"),
         name="hidden_back",
-    )(perm, dgate, dval, dstep, wg, w1, dt_mine)[0]
+    )(perm, at_rows, dgate, dval, dstep, wg, w1, dt_mine, hid_all, gain_pre)
     hidden_grad = scatter_ctx(hidden_part)
 
-    hid_order = jnp.concatenate(
-        [lax.dynamic_index_in_dim(hid_all, perm[at], 0, keepdims=False) for at in range(nctx)]
-    )
-    dmap, map_conv_grad, map_in_grad = pl.pallas_call(
+    map_rows = rows_in // nctx
+    in_smem = pl.BlockSpec(memory_space=pltpu.SMEM)
+    in_vmem = pl.BlockSpec(memory_space=pltpu.VMEM)
+    map_conv_grad, map_keep, map_send, hidden_own, gain_own = pl.pallas_call(
         maps_back_kernel,
+        in_specs=[in_smem] * 3 + [in_vmem] * 6 + [anywhere(w1), in_vmem],
         out_shape=[
-            shape_of(length, maps, dtype=BF16),
             shape_of(8, maps),
-            shape_of(model, maps, dtype=BF16),
+            *blocks_of(map_rows, maps),
+            shape_of(span, model),
+            shape_of(8, model),
         ],
-        scratch_shapes=[pltpu.VMEM((length + 8, maps), F32)],
+        scratch_shapes=[
+            pltpu.VMEM((length + 8, maps), F32),
+            pltpu.VMEM((model, maps), F32),
+            pltpu.VMEM((length, maps), BF16),
+            pltpu.VMEM((model, wide), BF16),
+            pltpu.SemaphoreType.DMA((len(w1),)),
+        ],
         compiler_params=params(),
         name="maps_back",
-    )(dbc_total, conv_sum[:, width:], conv_in[:, width:], conv_mine[:, width:], seg_col, hid_order)
-    map_rows = rows_in // nctx
-    map_part = lax.dynamic_index_in_dim(
-        map_in_grad.reshape(ndp, nctx, map_rows, maps), c, 1, keepdims=False
-    )
-    map_shard = lax.psum_scatter(map_part, "dp", scatter_dimension=0, tiled=True)[0]
-
-    input_grad, gain_sum = pl.pallas_call(
+    )(
+        perm,
+        at_rows,
+        here,
+        dbc_total,
+        conv_sum[:, width:],
+        conv_in[:, width:],
+        conv_mine[:, width:],
+        seg_col,
+        hid_all,
+        w1,
+        gain_pre,
+    )
+    map_shard = scatter_dp(map_keep, map_send, here, "map")
+
+    input_grad = pl.pallas_call(
         input_back_kernel,
-        out_shape=[shape_of(span, model), shape_of(8, model)],
+        out_shape=shape_of(span, model),
         compiler_params=params(),
         name="input_back",
-    )(
-        hidden_grad,
-        lax.dynamic_slice_in_dim(dmap, c * span, span, 0),
-        w1[:, width:],
-        tok,
-        gain_pre,
-        cotangent[0],
-    )
+    )(hidden_grad, hidden_own, tok, gain_pre, cotangent[0])
 
     def row_block(value):
         return jnp.pad(value, ((0, 0), (0, width - value.shape[1])))
 
     half = model // width
+    gain_sum = gain_sum + gain_own
     packed = jnp.concatenate(
-        [conv_grad, col_sums, row_block(map_conv_grad), row_block(head_grad)]
+        [conv_grad[: CONV + 1], col_sums[:2], row_block(head_grad[:2]), row_block(map_conv_grad[: CONV + 1])]
+        + [gain_sum[:1, at * width : (at + 1) * width] for at in range(half)]
         + [dt_grad[:, at * width : (at + 1) * width] for at in range(half)]
-        + [gain_sum[:, at * width : (at + 1) * width] for at in range(half)]
-    )
-    packed = lax.all_gather(lax.psum(packed, "dp"), "ctx", axis=0)
+    )
+    packed = jnp.pad(packed, ((0, -packed.shape[0] % 8), (0, 0)))
+    if ndp > 8 or ndp & (ndp - 1):
+        packed = lax.psum(packed, "dp")
+    else:
+        packed = packed + swap(packed, "dp", 1)
+        others = [swap(packed, "dp", bit) for bit in range(2, ndp, 2)]
+        others = jnp.stack([packed] + others)[here[1] ^ jnp.arange(ndp // 2)]
+        packed = sum(others[at] for at in range(ndp // 2))
+    packed = jnp.stack(fan_ctx(packed))[c ^ jnp.arange(nctx)]
+    map_at = CONV + 5
+    gain_at = map_at + CONV + 1
+    dt_at = gain_at + half
     conv_total = jnp.concatenate(
-        [packed[at, : CONV + 1] for at in range(nctx)] + [packed[0, 16 : 16 + CONV + 1, :maps]], axis=1
+        [packed[at, : CONV + 1] for at in range(nctx)] + [packed[0, map_at:gain_at, :maps]], axis=1
     )
     conv_total = lax.dynamic_slice_in_dim(conv_total, d * conv_cols, conv_cols, 1)
     dt_total = jnp.concatenate(
-        [packed[:, 32 + 8 * at : 40 + 8 * at].reshape(HEADS, width) for at in range(half)], axis=1
+        [packed[:, dt_at + heads * at : dt_at + heads * (at + 1)].reshape(HEADS, width) for at in range(half)],
+        axis=1,
     )
     dt_total = lax.dynamic_slice_in_dim(dt_total, d * dt_cols, dt_cols, 1)
-    first_gain = 32 + 8 * half
-    pre_total = [
-        jnp.sum(packed[:, first_gain + 8 * at], axis=0) for at in range(half)
+    pre_total = jnp.sum(packed[:, gain_at:dt_at], axis=0).reshape(-1)
+    gain_total = jnp.concatenate([pre_total, packed[:, CONV + 1].reshape(-1)])
+    gain_total = lax.dynamic_slice_in_dim(gain_total, d * gain_len, gain_len, 0)
+    head_total = jnp.concatenate(
+        [
+            jnp.moveaxis(packed[:, CONV + 3 : CONV + 5, :heads], 0, 1).reshape(2, HEADS),
+            jnp.sum(packed[:, CONV + 2].reshape(HEADS, HEAD_DIM), axis=1)[None],
+        ]
+    )
+
+    gates, values, maps_in, outs = [
+        fan_ctx(shard) for shard in (gate_shard, value_shard, map_shard, out_shard)
     ]
-    gain_total = jnp.concatenate(pre_total + [packed[:, 8].reshape(-1)])
-    gain_total = lax.dynamic_slice_in_dim(gain_total, d * gain_len, gain_len, 0)
-    head_total = jnp.stack(
-        [
-            packed[:, 24, :heads].reshape(-1),
-            packed[:, 25, :heads].reshape(-1),
-            jnp.sum(packed[:, 9].reshape(HEADS, HEAD_DIM), axis=1),
+    if rows_in % 64 == 0:
+        block = maps
+        steps = in_weight.shape[1] // block
+        part = pl.BlockSpec((rows_in, block), lambda i, *_: (0, i))
+        in_new = pl.pallas_call(
+            adam_in_kernel,
+            grid_spec=pltpu.PrefetchScalarGridSpec(
+                num_scalar_prefetch=1,
+                grid=(steps,),
+                in_specs=[part] * 3
+                + [
+                    [full((rows_in, width))] * nctx,
+                    [full((rows_in, width))] * nctx,
+                    [full((map_rows, maps))] * nctx,
+                ],
+                out_specs=[part] * 3,
+                scratch_shapes=[
+                    pltpu.VMEM((2 * nctx, rows_in, width), BF16),
+                    pltpu.VMEM((rows_in, maps), BF16),
+                ],
+            ),
+            out_shape=[shape_of(*in_weight.shape)] * 3,
+            compiler_params=params("arbitrary"),
+            name="adam_in",
+        )(here, in_weight, in_first, in_second, gates, values, maps_in)
+        in_new = tuple(in_new)
+    else:
+        natural = lambda parts: [
+            lax.dynamic_index_in_dim(jnp.stack(parts), c ^ at, 0, False) for at in range(nctx)
         ]
-    )
-
-    columns = lax.all_gather(jnp.stack([gate_shard, value_shard]).astype(BF16), "ctx", axis=0)
-    map_total = lax.all_gather(map_shard.astype(BF16), "ctx", axis=0, tiled=True)
-    in_total = jnp.concatenate(
-        [columns[at, 0] for at in range(nctx)] + [columns[at, 1] for at in range(nctx)] + [map_total],
-        axis=1,
-    ).astype(F32)
-    out_total = lax.all_gather(out_shard.astype(BF16), "ctx", axis=1, tiled=True).astype(F32)
-
-    in_new = adam_step(in_weight, in_first, in_second, in_total, 0.03, WEIGHT_DECAY)
+        in_total = jnp.concatenate(
+            natural(gates) + natural(values) + [jnp.concatenate(natural(maps_in))], axis=1
+        ).astype(F32)
+        in_new = adam_step(in_weight, in_first, in_second, in_total, 0.03, WEIGHT_DECAY)
+    out_total = jnp.stack(outs)[c ^ jnp.arange(nctx)]
+    out_total = jnp.concatenate([out_total[at] for at in range(nctx)], axis=1).astype(F32)
+
     dt_new = adam_step(dt_weight, dt_first, dt_second, dt_total, 0.03, WEIGHT_DECAY)
     out_new = adam_step(out_weight, out_first, out_second, out_total, 0.02, WEIGHT_DECAY)
     conv_new = adam_step(conv_params, conv_first, conv_second, conv_total, 0.3, 0.0)

time: 607 us -> 361 us (0.59)
  waiting for transfers between devices: 357 us -> 67.5 us
  starting transfers between devices: 17.3 us -> 72.2 us
  Pallas kernels: 79.6 us -> 109 us
  blocking collectives: 53.1 us -> 32.1 us
  local copies, waits for them, and re-layouts: 38.7 us -> 30.9 us
  between operations: 22.2 us -> 15.1 us
    reduce_scatter x4 -> x0, waiting for transfers between devices: 200 us -> none  [the longest x1 65.8 us: shards(): lax.psum_scatter(gate_in_grad, 'dp', scatter_dimension=0, tiled=True)]
    psum x1 -> x0, waiting for transfers between devices: 64.7 us -> none  [shards(): packed = lax.all_gather(lax.psum(packed, 'dp'), 'ctx', axis=0)]
    ppermute x12 -> x65, starting transfers between devices: 9.14 us -> 68.7 us  [swap(): return lax.ppermute(value, axis, [(at, at ^ bit) for at in range(count)])]
    all_gather x3 -> x0, waiting for transfers between devices: 44 us -> none  [the longest x1 26.8 us: shards(): lax.all_gather(lax.dynamic_slice_in_dim(in_weight, c * width, width, 1).a...]
    ppermute x12 -> x65, waiting for transfers between devices: 34.8 us -> 67.5 us  [swap(): return lax.ppermute(value, axis, [(at, at ^ bit) for at in range(count)])]
    pallas_call x2 -> x8, Pallas kernels: 9.52 us -> 35.1 us  [the longest x1 13.9 us: shards(): pl.pallas_call(adam_in_kernel, grid_spec=pltpu.PrefetchScalarGridSpec(num...]
    all_gather x3 -> x0, blocking collectives: 20.1 us -> none  [the longest x1 7.35 us: shards(): lax.all_gather(out_shard.astype(BF16), 'ctx', axis=1, tiled=True)]
    all_to_all x1 -> x0, waiting for transfers between devices: 10.2 us -> none  [shards(): lax.all_to_all(out_grad, 'ctx', split_axis=1, concat_axis=0, tiled=True)]
  transfers between devices with their start and end apart: 23 -> 67, of which waited for: 16 -> 19; matrix products, arithmetic and copies ran while one was open for 10% -> 16% of each run, Pallas kernels for 6% -> 23%
where the time goes in v2:
time: 361 us; the launch traced here: 359 us
  Pallas kernels  109 us (30%)
  starting transfers between devices  72.2 us (20%)
  waiting for transfers between devices  67.5 us (19%)
  other arithmetic  32.8 us (9%)
  blocking collectives  32.1 us (9%)
  local copies, waits for them, and re-layouts  30.9 us (9%)
  between operations  15.1 us (4%)
    ppermute x65, starting transfers between devices, swap(): return lax.ppermute(value, axis, [(at, at ^ bit) for at in range(count)])  68.7 us
    ppermute x65, waiting for transfers between devices, swap(): return lax.ppermute(value, axis, [(at, at ^ bit) for at in range(count)])  67.5 us
    all_gather x1, blocking collectives, shards(): small_all = lax.all_gather(small, 'dp', axis=0)  32.1 us
    pallas_call x1, Pallas kernels, shards(): pl.pallas_call(scan_back_kernel, grid_spec=pltpu.PrefetchScalarGridSpec(n...  22 us
    pallas_call x1, Pallas kernels, shards(): pl.pallas_call(scan_forward_kernel, grid_spec=pltpu.PrefetchScalarGridSpe...  15.7 us
    pallas_call x1, Pallas kernels, shards(): pl.pallas_call(adam_in_kernel, grid_spec=pltpu.PrefetchScalarGridSpec(num...  13.9 us
    pallas_call x1, Pallas kernels, shards(): pl.pallas_call(norm_back_kernel, grid_spec=pltpu.PrefetchScalarGridSpec(n...  13.2 us
    pallas_call x1, Pallas kernels, shards(): pl.pallas_call(gate_kernel, grid_spec=pltpu.PrefetchScalarGridSpec(num_sc...  11.7 us
  transfers between devices with their start and end apart: 67, of which 19 were waited for; matrix products, arithmetic and copies ran while one was open for 16% of the time, Pallas kernels for 23%

profile of v2, /device:TPU:0, one launch (start us, length us, event | category | flops | bytes accessed | tf_op | source)
XLA Modules:
  0.0 359.5 jit_solution(5015485144336910494)
XLA Ops:
  7.3 1.8 dynamic-slice_convert_fusion.1
  9.0 3.0 collective-permute-start.9
  12.1 2.6 collective-permute-start.10
  14.7 1.6 dynamic-slice_convert_fusion
  18.6 32.1 %all-gather = bf16[384,384]{1,0:T(8,128)(2,1)S(1)} all-gather(bf16[48,384]{1,0:T(8,128)(2,1)S(1)} %fusion.13), channel_id=2, replica_groups=mesh['dp'=8,'ctx'=4] {'dp'}, dimensions={0}, use_global_device_ids=true | all-gather | bytes 331776 | tf_op jit(solution)/shard_map/all_gather | solution.py:786
  51.4 2.2 pre_norm.1
  53.6 1.4 collective-permute-start
  56.6 8.9 %collective-permute-done = bf16[256,1024]{1,0:T(8,128)(2,1)S(1)} collective-permute-done((bf16[256,1024]{1,0:T(8,128)(2,1)}, bf16[256,1024]{1,0:T(8,128)(2,1)S(1)}, u32[]{:S(2)}, u32[]{:S(2)}) %collective-permute-start) | collective-permute-done | bytes 524320 | tf_op jit(solution)/shard_map/ppermute | solution.py:656
  66.7 4.4 %collective-permute-done.16 = bf16[256,1024]{1,0:T(8,128)(2,1)S(1)} collective-permute-done((bf16[256,1024]{1,0:T(8,128)(2,1)}, bf16[256,1024]{1,0:T(8,128)(2,1)S(1)}, u32[]{:S(2)}, u32[]{:S(2)}) %collective-permute-start.16) | collective-permute-done | bytes 524320 | tf_op jit(solution)/shard_map/ppermute | solution.py:656
  74.1 3.5 all-to-all-start
  79.9 3.2 collective-permute-start.4
  84.3 4.2 %collective-permute-done.2.w1_pieces_1_ = bf16[128,768]{1,0:T(8,128)(2,1)S(1)} collective-permute-done((bf16[128,768]{1,0:T(8,128)(2,1)S(1)}, bf16[128,768]{1,0:T(8,128)(2,1)S(1)}, u32[]{:S(2)}, u32[]{:S(2)}) %collective-permute-start.2) | collective-permute-done | bytes 196640 | tf_op jit(solution)/shard_map/ppermute | solution.py:656
  88.5 3.3 collective-permute-start.5
  91.8 4.2 %collective-permute-done.3.w1_pieces_2_ = bf16[128,768]{1,0:T(8,128)(2,1)} collective-permute-done((bf16[128,768]{1,0:T(8,128)(2,1)S(1)}, bf16[128,768]{1,0:T(8,128)(2,1)}, u32[]{:S(2)}, u32[]{:S(2)}) %collective-permute-start.3) | collective-permute-done | bytes 196640 | tf_op jit(solution)/shard_map/ppermute | solution.py:656
  96.0 2.4 collective-permute-start.6
  98.4 2.0 collective-permute-start.8
  104.6 2.7 pad_maximum_fusion.hid_ref
  107.5 2.0 collective-permute-start.13
  109.5 3.2 collective-permute-done.8.w1_pieces_7_
  113.2 15.7 %scan_forward.1 = (bf16[1024,768]{1,0:T(8,128)(2,1)}, bf16[1024,768]{1,0:T(8,128)(2,1)}, f32[1024,768]{1,0:T(8,128)}, f32[1024,512]{1,0:T(8,128)}, f32[1024,8]{1...) custom-call(s32[4]{0:T(128)} %gather_fusion, ...), custom_call_target="tpu_custom_call" | custom-call | tf_op jit(solution)/shard_map/scan_forward/pallas_call | solution.py:834
  128.9 2.7 pad_maximum_fusion.1.cot_ref
  133.6 11.7 %gate.1 = (bf16[1024,512]{1,0:T(8,128)(2,1)}, f32[1024,512]{1,0:T(8,128)}, f32[8,1024]{1,0:T(8,128)}) custom-call(s32[4]{0:T(128)} %gather_fusion, s32[8]{0:T(128)} %broadcast_xor_fusion.at_ref, bf16[4,256,1024]{2,1,0:T(8,128)(2,1)} %pad_maximum_fusion.hid_ref, bf16[128,512]{1,0:T(8,128)(2,1)} %get-tuple-element.153.wg_pieces_0_, ...), custom_call_target="tpu_custom_call" | custom-call | tf_op jit(solution)/shard_map/gate/pallas_call | solution.py:885
  145.4 1.7 collective-permute-start.19
  147.9 1.7 collective-permute-done.19
  150.6 1.4 add_add_fusion.stat_ref
  152.0 13.2 %norm_back.1 = (bf16[4,256,1024]{2,1,0:T(8,128)(2,1)}, bf16[512,256]{1,0:T(8,128)(2,1)}, bf16[512,256]{1,0:T(8,128)(2,1)}, bf16[512,256]{1,0:T(8,128)(2,1)}, bf1...) custom-call(s32[4]{0:T(128)} %gather_fusion, ...), custom_call_target="tpu_custom_call" | custom-call | tf_op jit(solution)/shard_map/norm_back/pallas_call | solution.py:911
  165.5 22.0 %scan_back.1 = (bf16[4,128,512]{2,1,0:T(8,128)(2,1)}, bf16[4,128,512]{2,1,0:T(8,128)(2,1)}, bf16[1024,512]{1,0:T(8,128)(2,1)}, bf16[1024,256]{1,0:T(8,128)(2,1)}...) custom-call(s32[4]{0:T(128)} %gather_fusion, s32[3]{0:T(128)} %pad_add_fusion.here_ref, ...), custom_call_target="tpu_custom_call" | custom-call | tf_op jit(solution)/shard_map/scan_back/pallas_call | solution.py:976
  187.5 2.1 collective-permute-start.34
  192.2 1.3 slice.197.conv_ref
  193.5 2.3 slice.149.convsum_ref
  195.8 1.9 slice.150.convin_ref
  198.8 4.8 %collective-permute-done.57.part_refs_3_ = bf16[512,256]{1,0:T(8,128)(2,1)S(1)} collective-permute-done((bf16[512,256]{1,0:T(8,128)(2,1)S(1)}, bf16[512,256]{1,0:T(8,128)(2,1)S(1)}, u32[]{:S(2)}, u32[]{:S(2)}) %collective-permute-start.57) | collective-permute-done | bytes 262176 | tf_op jit(solution)/shard_map/ppermute | solution.py:656
  204.3 2.3 out_split.1
  207.8 1.3 slice.153
  209.1 8.8 %hidden_back.1 = (bf16[4,256,1024]{2,1,0:T(8,128)(2,1)}, f32[8,1024]{1,0:T(8,128)}) custom-call(s32[4]{0:T(128)} %gather_fusion, s32[8]{0:T(128)} %broadcast_xor_fusion.at_ref, bf16[1024,512]{1,0:T(8,128)(2,1)} %get-tuple-element.85.dgate_ref, bf16[1024,512]{1,0:T(8,128)(2,1)} %get-tuple-element.95.dval_ref, bf16[1024,8]{1,0:T(8,128)(2,1)} %get-tuple-element.96.dstep_ref, ...), custom_call_target="tpu_custom_call" | custom-call | tf_op jit(solution)/shard_map/hidden_back/pallas_call | solution.py:1034
  217.9 1.4 slice.146
  220.5 2.1 pair_sum_value.1
  223.3 4.3 %collective-permute-start.36 = (bf16[128,512]{1,0:T(8,128)(2,1)}, bf16[128,512]{1,0:T(8,128)(2,1)S(1)}, u32[]{:S(2)}, u32[]{:S(2)}) collective-permute-start(bf16[128,512]{1,0:T(8,128)(2,1)} %get-tuple-element.110), channel_id=1, source_target_pairs={{0,16},{4,20},{8,24},{12,28},{16,0},{20,4},{24,8},{28,12},{1,17},{... | collective-permute-start | bytes 393224 | tf_op jit(solution)/shard_map/ppermute | solution.py:656
  228.6 2.0 pair_sum_gate.1
  231.2 6.6 %collective-permute-done.36 = bf16[128,512]{1,0:T(8,128)(2,1)S(1)} collective-permute-done((bf16[128,512]{1,0:T(8,128)(2,1)}, bf16[128,512]{1,0:T(8,128)(2,1)S(1)}, u32[]{:S(2)}, u32[]{:S(2)}) %collective-permute-start.36) | collective-permute-done | bytes 131104 | tf_op jit(solution)/shard_map/ppermute | solution.py:656
  237.9 3.0 collective-permute-start.30
  241.7 2.1 pair_sum_out.1
  243.8 7.5 %collective-permute-start.59 = (bf16[256,256]{1,0:T(8,128)(2,1)}, bf16[256,256]{1,0:T(8,128)(2,1)S(1)}, u32[]{:S(2)}, u32[]{:S(2)}) collective-permute-start(bf16[256,256]{1,0:T(8,128)(2,1)} %get-tuple-element.135), channel_id=1, source_target_pairs={{0,8},{4,12},{8,0},{12,4},{16,24},{20,28},{24,16},{28,20},{1,9},{5... | collective-permute-start | bytes 393224 | tf_op jit(solution)/shard_map/ppermute | solution.py:656
  251.4 2.4 collective-permute-start.61
  255.8 8.2 %collective-permute-done.60 = bf16[256,256]{1,0:T(8,128)(2,1)S(1)} collective-permute-done((bf16[256,256]{1,0:T(8,128)(2,1)}, bf16[256,256]{1,0:T(8,128)(2,1)S(1)}, u32[]{:S(2)}, u32[]{:S(2)}) %collective-permute-start.60) | collective-permute-done | bytes 131104 | tf_op jit(solution)/shard_map/ppermute | solution.py:656
  268.3 3.1 collective-permute-done.63
  274.1 7.5 %maps_back.1 = (f32[8,256]{1,0:T(8,128)}, bf16[4,32,256]{2,1,0:T(8,128)(2,1)}, bf16[4,32,256]{2,1,0:T(8,128)(2,1)}, f32[256,1024]{1,0:T(8,128)}, f32[8,1024]{1,0:T(8,128)}) custom-call(s32[4]{0:T(128)} %gather_fusion, s32[8]{0:T(128)} %broadcast_xor_fusion.at_ref, s32[3]{0:T(128)} %pad_add_fusion.here_ref, f32[1024,256]{1,0:T(8,128)} %convert_add_fusion.2.dbc_ref, ...), custom_call_target="tpu_custom_call" | custom-call | tf_op jit(solution)/shard_map/maps_back/pallas_call | solution.py:1065
  282.4 3.1 convert_add_fusion
  285.5 2.3 multiply_subtract_fusion
  287.8 1.6 convert_add_fusion.1
  290.2 1.5 pair_sum_map.1
  291.7 2.4 collective-permute-start.42
  294.1 2.4 collective-permute-start.44
  297.0 2.1 collective-permute-done.43
  299.9 1.4 collective-permute-start.48
  304.3 2.1 fusion.7
  306.6 2.8 collective-permute-start.50
  309.4 1.5 collective-permute-start.51
  312.7 2.0 collective-permute-done.46.map_refs_2_
  315.3 1.5 collective-permute-start.22
  316.8 13.9 %adam_in.1 = (f32[128,4352]{1,0:T(8,128)}, f32[128,4352]{1,0:T(8,128)}, f32[128,4352]{1,0:T(8,128)}) custom-call(s32[3]{0:T(128)} %pad_add_fusion.here_ref, f32[128,4352]{1,0:T(8,128)} %weight_ref.1, f32[128,4352]{1,0:T(8,128)} %first_ref.1, f32[128,4352]{1,0:T(8,128)} %second_ref.1, bf16[128,512]{1,0:T(8,128)(2,1)} %copy-done.13, ...), custom_call_target="tpu_custom_call" | custom-call | tf_op jit(solution)/shard_map/adam_in/pallas_call | solution.py:1153
  333.6 7.7 %collective-permute-done.53 = f32[32,512]{1,0:T(8,128)S(1)} collective-permute-done((f32[32,512]{1,0:T(8,128)S(1)}, f32[32,512]{1,0:T(8,128)S(1)}, u32[]{:S(2)}, u32[]{:S(2)}) %collective-permute-start.53) | collective-permute-done | bytes 65568 | tf_op jit(solution)/shard_map/ppermute | solution.py:656
  345.2 2.5 fusion.2.hg_ref
  347.7 3.7 %input_back.1 = f32[256,1024]{1,0:T(8,128)} custom-call(f32[256,1024]{1,0:T(8,128)} %fusion.2.hg_ref, f32[256,1024]{1,0:T(8,128)} %get-tuple-element.99.own_ref, f32[256,1024]{1,0:T(8,128)} %bitcast.105, f32[1,1024]{1,0:T(1,128)} %slice.188.gain_ref, f32[256,1024]{1,0:T(8,128)} %bitcast.111), custom_call_target="tpu_custom_call" | custom-call | tf_op jit(solution)/shard_map/input_back/pallas_call | solution.py:1098
  (305 shorter events, 56.0 us)
Async XLA Ops:
  7.2 66.9 %all-gather.3.cloned.1.call-start = ((), (), s32[]{:S(2)}) async-start(), calls=%async_computation.1 | async-start | bytes 1179648 | tf_op jit(solution)/shard_map/all_gather | solution.py:804
  9.0 69.6 %collective-permute-start.9 = (bf16[128,512]{1,0:T(8,128)(2,1)}, bf16[128,512]{1,0:T(8,128)(2,1)}, u32[]{:S(2)}, u32[]{:S(2)}) collective-permute-start(bf16[128,512]{1,0:T(8,128)(2,1)} %get-tuple-element.153.wg_pieces_0_), channel_id=1, source_target_pairs={{0,8},{4,12},{8,0},{12,4},{16,24},{20,28},{24,16},{28,20},{1,9},{5... | collective-permute-start | bytes 393224 | tf_op jit(solution)/shard_map/ppermute | solution.py:656
  12.1 66.6 %collective-permute-start.10 = (bf16[128,512]{1,0:T(8,128)(2,1)}, bf16[128,512]{1,0:T(8,128)(2,1)}, u32[]{:S(2)}, u32[]{:S(2)}) collective-permute-start(bf16[128,512]{1,0:T(8,128)(2,1)} %get-tuple-element.153.wg_pieces_0_), channel_id=1, source_target_pairs={{0,16},{4,20},{8,24},{12,28},{16,0},{20,4},{24,8},{28,12},{1,17},{... | collective-permute-start | bytes 393224 | tf_op jit(solution)/shard_map/ppermute | solution.py:656
  14.7 65.3 %collective-permute-start.11 = (bf16[128,512]{1,0:T(8,128)(2,1)}, bf16[128,512]{1,0:T(8,128)(2,1)}, u32[]{:S(2)}, u32[]{:S(2)}) collective-permute-start(bf16[128,512]{1,0:T(8,128)(2,1)} %get-tuple-element.153.wg_pieces_0_), channel_id=1, source_target_pairs={{0,24},{4,28},{8,16},{12,20},{16,8},{20,12},{24,0},{28,4},{1,25},{... | collective-permute-start | bytes 393224 | tf_op jit(solution)/shard_map/ppermute | solution.py:656
  53.6 11.9 %collective-permute-start = (bf16[256,1024]{1,0:T(8,128)(2,1)}, bf16[256,1024]{1,0:T(8,128)(2,1)S(1)}, u32[]{:S(2)}, u32[]{:S(2)}) collective-permute-start(bf16[256,1024]{1,0:T(8,128)(2,1)} %pre_norm.1), channel_id=1, source_target_pairs={{0,2},{1,3},{2,0},{3,1},{4,6},{5,7},{6,4},{7,5},{8,10},{9,11},{10,... | collective-permute-start | bytes 1572872 | tf_op jit(solution)/shard_map/ppermute | solution.py:656
  56.0 15.2 %collective-permute-start.16 = (bf16[256,1024]{1,0:T(8,128)(2,1)}, bf16[256,1024]{1,0:T(8,128)(2,1)S(1)}, u32[]{:S(2)}, u32[]{:S(2)}) collective-permute-start(bf16[256,1024]{1,0:T(8,128)(2,1)} %get-tuple-element.156), channel_id=1, source_target_pairs={{0,2},{1,3},{2,0},{3,1},{4,6},{5,7},{6,4},{7,5},{8,10},{9,11},{10,... | collective-permute-start | bytes 1572872 | tf_op jit(solution)/shard_map/ppermute | solution.py:656
  66.6 31.8 %collective-permute-start.1 = (bf16[2,256,1024]{2,1,0:T(8,128)(2,1)}, bf16[2,256,1024]{2,1,0:T(8,128)(2,1)}, u32[]{:S(2)}, u32[]{:S(2)}) collective-permute-start(bf16[2,256,1024]{2,1,0:T(8,128)(2,1)} %pad_maximum_fusion.2), channel_id=1, source_target_pairs={{0,1},{1,0},{2,3},{3,2},{4,5},{5,4},{6,7},{7,6},{8,9},{9,8},{10,11... | collective-permute-start | bytes 3145736 | tf_op jit(solution)/shard_map/ppermute | solution.py:656
  72.2 56.7 %collective-permute-start.17 = (bf16[2,256,1024]{2,1,0:T(8,128)(2,1)}, bf16[2,256,1024]{2,1,0:T(8,128)(2,1)}, u32[]{:S(2)}, u32[]{:S(2)}) collective-permute-start(bf16[2,256,1024]{2,1,0:T(8,128)(2,1)} %pad_maximum_fusion.3), channel_id=1, source_target_pairs={{0,1},{1,0},{2,3},{3,2},{4,5},{5,4},{6,7},{7,6},{8,9},{9,8},{10,11... | collective-permute-start | bytes 3145736 | tf_op jit(solution)/shard_map/ppermute | solution.py:656
  74.1 57.6 %all-to-all-start = ((bf16[4,512,256]{2,1,0:T(8,128)(2,1)}), bf16[4,512,256]{2,1,0:T(8,128)(2,1)S(1)}, u32[]{:S(2)}, u32[]{:S(2)}) async-start(bf16[4,512,256]{2,1,0:T(8,128)(2,1)} %bitcast.116), calls=%async_computation | async-start | bytes 2097152 | tf_op jit(solution)/shard_map/all_to_all | solution.py:810
  78.6 9.8 %collective-permute-start.2 = (bf16[128,768]{1,0:T(8,128)(2,1)S(1)}, bf16[128,768]{1,0:T(8,128)(2,1)S(1)}, u32[]{:S(2)}, u32[]{:S(2)}) collective-permute-start(bf16[128,768]{1,0:T(8,128)(2,1)S(1)} %pad_maximum_fusion.8.w1_pieces_0_), channel_id=1, source_target_pairs={{0,8},{4,12},{8,0},{12,4},{16,24},{20,28},{24,16},{28,20},{1,9},{5... | collective-permute-start | bytes 589832 | tf_op jit(solution)/shard_map/ppermute | solution.py:656
  78.7 17.2 %collective-permute-start.3 = (bf16[128,768]{1,0:T(8,128)(2,1)S(1)}, bf16[128,768]{1,0:T(8,128)(2,1)}, u32[]{:S(2)}, u32[]{:S(2)}) collective-permute-start(bf16[128,768]{1,0:T(8,128)(2,1)S(1)} %pad_maximum_fusion.8.w1_pieces_0_), channel_id=1, source_target_pairs={{0,16},{4,20},{8,24},{12,28},{16,0},{20,4},{24,8},{28,12},{1,17},{... | collective-permute-start | bytes 589832 | tf_op jit(solution)/shard_map/ppermute | solution.py:656
  79.9 18.4 %collective-permute-start.4 = (bf16[128,768]{1,0:T(8,128)(2,1)S(1)}, bf16[128,768]{1,0:T(8,128)(2,1)}, u32[]{:S(2)}, u32[]{:S(2)}) collective-permute-start(bf16[128,768]{1,0:T(8,128)(2,1)S(1)} %pad_maximum_fusion.8.w1_pieces_0_), channel_id=1, source_target_pairs={{0,24},{4,28},{8,16},{12,20},{16,8},{20,12},{24,0},{28,4},{1,25},{... | collective-permute-start | bytes 589832 | tf_op jit(solution)/shard_map/ppermute | solution.py:656
  88.5 18.9 %collective-permute-start.5 = (bf16[128,768]{1,0:T(8,128)(2,1)S(1)}, bf16[128,768]{1,0:T(8,128)(2,1)}, u32[]{:S(2)}, u32[]{:S(2)}) collective-permute-start(bf16[128,768]{1,0:T(8,128)(2,1)S(1)} %pad_maximum_fusion.8.w1_pieces_0_), channel_id=1, source_target_pairs={{0,4},{4,0},{8,12},{12,8},{16,20},{20,16},{24,28},{28,24},{1,5},{5... | collective-permute-start | bytes 589832 | tf_op jit(solution)/shard_map/ppermute | solution.py:656
  96.0 11.5 %collective-permute-start.6 = (bf16[128,768]{1,0:T(8,128)(2,1)S(1)}, bf16[128,768]{1,0:T(8,128)(2,1)}, u32[]{:S(2)}, u32[]{:S(2)}) collective-permute-start(bf16[128,768]{1,0:T(8,128)(2,1)S(1)} %collective-permute-done.2.w1_pieces_1_), channel_id=1, source_target_pairs={{0,4},{4,0},{8,12},{12,8},{16,20},{20,16},{24,28},{28,24},{1,5},{5... | collective-permute-start | bytes 589832 | tf_op jit(solution)/shard_map/ppermute | solution.py:656
  98.4 11.0 %collective-permute-start.7 = (bf16[128,768]{1,0:T(8,128)(2,1)}, bf16[128,768]{1,0:T(8,128)(2,1)}, u32[]{:S(2)}, u32[]{:S(2)}) collective-permute-start(bf16[128,768]{1,0:T(8,128)(2,1)} %collective-permute-done.3.w1_pieces_2_), channel_id=1, source_target_pairs={{0,4},{4,0},{8,12},{12,8},{16,20},{20,16},{24,28},{28,24},{1,5},{5... | collective-permute-start | bytes 589832 | tf_op jit(solution)/shard_map/ppermute | solution.py:656
  98.4 14.3 %collective-permute-start.8 = (bf16[128,768]{1,0:T(8,128)(2,1)}, bf16[128,768]{1,0:T(8,128)(2,1)}, u32[]{:S(2)}, u32[]{:S(2)}) collective-permute-start(bf16[128,768]{1,0:T(8,128)(2,1)} %collective-permute-done.4.w1_pieces_3_), channel_id=1, source_target_pairs={{0,4},{4,0},{8,12},{12,8},{16,20},{20,16},{24,28},{28,24},{1,5},{5... | collective-permute-start | bytes 589832 | tf_op jit(solution)/shard_map/ppermute | solution.py:656
  107.3 25.5 %collective-permute-start.12 = (bf16[128,512]{1,0:T(8,128)(2,1)}, bf16[128,512]{1,0:T(8,128)(2,1)S(1)}, u32[]{:S(2)}, u32[]{:S(2)}) collective-permute-start(bf16[128,512]{1,0:T(8,128)(2,1)} %get-tuple-element.153.wg_pieces_0_), channel_id=1, source_target_pairs={{0,4},{4,0},{8,12},{12,8},{16,20},{20,16},{24,28},{28,24},{1,5},{5... | collective-permute-start | bytes 393224 | tf_op jit(solution)/shard_map/ppermute | solution.py:656
  107.5 25.3 %collective-permute-start.13 = (bf16[128,512]{1,0:T(8,128)(2,1)}, bf16[128,512]{1,0:T(8,128)(2,1)S(1)}, u32[]{:S(2)}, u32[]{:S(2)}) collective-permute-start(bf16[128,512]{1,0:T(8,128)(2,1)} %collective-permute-done.9.wg_pieces_1_), channel_id=1, source_target_pairs={{0,4},{4,0},{8,12},{12,8},{16,20},{20,16},{24,28},{28,24},{1,5},{5... | collective-permute-start | bytes 393224 | tf_op jit(solution)/shard_map/ppermute | solution.py:656
  109.4 23.4 %collective-permute-start.14 = (bf16[128,512]{1,0:T(8,128)(2,1)}, bf16[128,512]{1,0:T(8,128)(2,1)S(1)}, u32[]{:S(2)}, u32[]{:S(2)}) collective-permute-start(bf16[128,512]{1,0:T(8,128)(2,1)} %collective-permute-done.10.wg_pieces_2_), channel_id=1, source_target_pairs={{0,4},{4,0},{8,12},{12,8},{16,20},{20,16},{24,28},{28,24},{1,5},{5... | collective-permute-start | bytes 393224 | tf_op jit(solution)/shard_map/ppermute | solution.py:656
  112.7 20.1 %collective-permute-start.15 = (bf16[128,512]{1,0:T(8,128)(2,1)}, bf16[128,512]{1,0:T(8,128)(2,1)S(1)}, u32[]{:S(2)}, u32[]{:S(2)}) collective-permute-start(bf16[128,512]{1,0:T(8,128)(2,1)} %collective-permute-done.11.wg_pieces_3_), channel_id=1, source_target_pairs={{0,4},{4,0},{8,12},{12,8},{16,20},{20,16},{24,28},{28,24},{1,5},{5... | collective-permute-start | bytes 393224 | tf_op jit(solution)/shard_map/ppermute | solution.py:656
  145.4 4.2 %collective-permute-start.19 = (f32[8,1024]{1,0:T(8,128)}, f32[8,1024]{1,0:T(8,128)S(1)}, u32[]{:S(2)}, u32[]{:S(2)}) collective-permute-start(f32[8,1024]{1,0:T(8,128)} %get-tuple-element.82), channel_id=1, source_target_pairs={{0,2},{1,3},{2,0},{3,1},{4,6},{5,7},{6,4},{7,5},{8,10},{9,11},{10,... | collective-permute-start | bytes 98312 | tf_op jit(solution)/shard_map/ppermute | solution.py:656
  147.0 3.6 collective-permute-start.20
  165.2 26.3 %collective-permute-start.55 = (bf16[512,256]{1,0:T(8,128)(2,1)}, bf16[512,256]{1,0:T(8,128)(2,1)S(1)}, u32[]{:S(2)}, u32[]{:S(2)}) collective-permute-start(bf16[512,256]{1,0:T(8,128)(2,1)} %get-tuple-element.129), channel_id=1, source_target_pairs={{0,1},{1,0},{2,3},{3,2},{4,5},{5,4},{6,7},{7,6},{8,9},{9,8},{10,11... | collective-permute-start | bytes 786440 | tf_op jit(solution)/shard_map/ppermute | solution.py:656
  187.5 33.0 %collective-permute-start.34 = (bf16[4,128,512]{2,1,0:T(8,128)(2,1)}, bf16[4,128,512]{2,1,0:T(8,128)(2,1)}, u32[]{:S(2)}, u32[]{:S(2)}) collective-permute-start(bf16[4,128,512]{2,1,0:T(8,128)(2,1)} %get-tuple-element.107), channel_id=1, source_target_pairs={{0,4},{4,0},{8,12},{12,8},{16,20},{20,16},{24,28},{28,24},{1,5},{5... | collective-permute-start | bytes 1572872 | tf_op jit(solution)/shard_map/ppermute | solution.py:656
  189.6 38.0 %collective-permute-start.25 = (bf16[1024,256]{1,0:T(8,128)(2,1)}, bf16[1024,256]{1,0:T(8,128)(2,1)S(1)}, u32[]{:S(2)}, u32[]{:S(2)}) collective-permute-start(bf16[1024,256]{1,0:T(8,128)(2,1)} %get-tuple-element.98), channel_id=1, source_target_pairs={{0,1},{1,0},{2,3},{3,2},{4,5},{5,4},{6,7},{7,6},{8,9},{9,8},{10,11... | collective-permute-start | bytes 1572872 | tf_op jit(solution)/shard_map/ppermute | solution.py:656
  189.6 9.1 %collective-permute-start.56 = (bf16[512,256]{1,0:T(8,128)(2,1)S(1)}, bf16[512,256]{1,0:T(8,128)(2,1)S(1)}, u32[]{:S(2)}, u32[]{:S(2)}) collective-permute-start(bf16[512,256]{1,0:T(8,128)(2,1)S(1)} %copy-done.60), channel_id=1, source_target_pairs={{0,2},{1,3},{2,0},{3,1},{4,6},{5,7},{6,4},{7,5},{8,10},{9,11},{10,... | collective-permute-start | bytes 786440 | tf_op jit(solution)/shard_map/ppermute | solution.py:656
  190.4 13.1 %collective-permute-start.57 = (bf16[512,256]{1,0:T(8,128)(2,1)S(1)}, bf16[512,256]{1,0:T(8,128)(2,1)S(1)}, u32[]{:S(2)}, u32[]{:S(2)}) collective-permute-start(bf16[512,256]{1,0:T(8,128)(2,1)S(1)} %copy-done.59), channel_id=1, source_target_pairs={{0,3},{1,2},{2,1},{3,0},{4,7},{5,6},{6,5},{7,4},{8,11},{9,10},{10,... | collective-permute-start | bytes 786440 | tf_op jit(solution)/shard_map/ppermute | solution.py:656
  191.5 36.3 %collective-permute-start.27 = (bf16[4,128,512]{2,1,0:T(8,128)(2,1)}, bf16[4,128,512]{2,1,0:T(8,128)(2,1)S(1)}, u32[]{:S(2)}, u32[]{:S(2)}) collective-permute-start(bf16[4,128,512]{2,1,0:T(8,128)(2,1)} %get-tuple-element.101), channel_id=1, source_target_pairs={{0,4},{4,0},{8,12},{12,8},{16,20},{20,16},{24,28},{28,24},{1,5},{5... | collective-permute-start | bytes 1572872 | tf_op jit(solution)/shard_map/ppermute | solution.py:656
  206.5 34.4 %collective-permute-start.58 = (bf16[4,256,256]{2,1,0:T(8,128)(2,1)}, bf16[4,256,256]{2,1,0:T(8,128)(2,1)S(1)}, u32[]{:S(2)}, u32[]{:S(2)}) collective-permute-start(bf16[4,256,256]{2,1,0:T(8,128)(2,1)} %get-tuple-element.133), channel_id=1, source_target_pairs={{0,4},{4,0},{8,12},{12,8},{16,20},{20,16},{24,28},{28,24},{1,5},{5... | collective-permute-start | bytes 1572872 | tf_op jit(solution)/shard_map/ppermute | solution.py:656
  222.6 8.0 %collective-permute-start.35 = (bf16[128,512]{1,0:T(8,128)(2,1)}, bf16[128,512]{1,0:T(8,128)(2,1)S(1)}, u32[]{:S(2)}, u32[]{:S(2)}) collective-permute-start(bf16[128,512]{1,0:T(8,128)(2,1)} %get-tuple-element.109), channel_id=1, source_target_pairs={{0,8},{4,12},{8,0},{12,4},{16,24},{20,28},{24,16},{28,20},{1,9},{5... | collective-permute-start | bytes 393224 | tf_op jit(solution)/shard_map/ppermute | solution.py:656
  223.3 14.5 %collective-permute-start.36 = (bf16[128,512]{1,0:T(8,128)(2,1)}, bf16[128,512]{1,0:T(8,128)(2,1)S(1)}, u32[]{:S(2)}, u32[]{:S(2)}) collective-permute-start(bf16[128,512]{1,0:T(8,128)(2,1)} %get-tuple-element.110), channel_id=1, source_target_pairs={{0,16},{4,20},{8,24},{12,28},{16,0},{20,4},{24,8},{28,12},{1,17},{... | collective-permute-start | bytes 393224 | tf_op jit(solution)/shard_map/ppermute | solution.py:656
  227.7 10.2 %collective-permute-start.37 = (bf16[128,512]{1,0:T(8,128)(2,1)}, bf16[128,512]{1,0:T(8,128)(2,1)S(1)}, u32[]{:S(2)}, u32[]{:S(2)}) collective-permute-start(bf16[128,512]{1,0:T(8,128)(2,1)} %get-tuple-element.111), channel_id=1, source_target_pairs={{0,24},{4,28},{8,16},{12,20},{16,8},{20,12},{24,0},{28,4},{1,25},{... | collective-permute-start | bytes 393224 | tf_op jit(solution)/shard_map/ppermute | solution.py:656
  227.8 38.0 %collective-permute-start.26 = (bf16[1024,256]{1,0:T(8,128)(2,1)S(1)}, bf16[1024,256]{1,0:T(8,128)(2,1)S(1)}, u32[]{:S(2)}, u32[]{:S(2)}) collective-permute-start(bf16[1024,256]{1,0:T(8,128)(2,1)S(1)} %add_convert_fusion), channel_id=1, source_target_pairs={{0,2},{1,3},{2,0},{3,1},{4,6},{5,7},{6,4},{7,5},{8,10},{9,11},{10,... | collective-permute-start | bytes 1572872 | tf_op jit(solution)/shard_map/ppermute | solution.py:656
  230.7 13.2 %collective-permute-start.28 = (bf16[128,512]{1,0:T(8,128)(2,1)}, bf16[128,512]{1,0:T(8,128)(2,1)S(1)}, u32[]{:S(2)}, u32[]{:S(2)}) collective-permute-start(bf16[128,512]{1,0:T(8,128)(2,1)} %get-tuple-element.103), channel_id=1, source_target_pairs={{0,8},{4,12},{8,0},{12,4},{16,24},{20,28},{24,16},{28,20},{1,9},{5... | collective-permute-start | bytes 393224 | tf_op jit(solution)/shard_map/ppermute | solution.py:656
  237.9 13.5 %collective-permute-start.29 = (bf16[128,512]{1,0:T(8,128)(2,1)}, bf16[128,512]{1,0:T(8,128)(2,1)S(1)}, u32[]{:S(2)}, u32[]{:S(2)}) collective-permute-start(bf16[128,512]{1,0:T(8,128)(2,1)} %get-tuple-element.104), channel_id=1, source_target_pairs={{0,16},{4,20},{8,24},{12,28},{16,0},{20,4},{24,8},{28,12},{1,17},{... | collective-permute-start | bytes 393224 | tf_op jit(solution)/shard_map/ppermute | solution.py:656
  237.9 13.5 %collective-permute-start.30 = (bf16[128,512]{1,0:T(8,128)(2,1)}, bf16[128,512]{1,0:T(8,128)(2,1)S(1)}, u32[]{:S(2)}, u32[]{:S(2)}) collective-permute-start(bf16[128,512]{1,0:T(8,128)(2,1)} %get-tuple-element.105), channel_id=1, source_target_pairs={{0,24},{4,28},{8,16},{12,20},{16,8},{20,12},{24,0},{28,4},{1,25},{... | collective-permute-start | bytes 393224 | tf_op jit(solution)/shard_map/ppermute | solution.py:656
  240.9 41.4 %collective-permute-start.23 = (bf16[2,256,1024]{2,1,0:T(8,128)(2,1)S(1)}, bf16[2,256,1024]{2,1,0:T(8,128)(2,1)}, u32[]{:S(2)}, u32[]{:S(2)}) collective-permute-start(bf16[2,256,1024]{2,1,0:T(8,128)(2,1)S(1)} %slice.146), channel_id=1, source_target_pairs={{0,1},{1,0},{2,3},{3,2},{4,5},{5,4},{6,7},{7,6},{8,9},{9,8},{10,11... | collective-permute-start | bytes 3145736 | tf_op jit(solution)/shard_map/ppermute | solution.py:656
  243.8 12.0 %collective-permute-start.59 = (bf16[256,256]{1,0:T(8,128)(2,1)}, bf16[256,256]{1,0:T(8,128)(2,1)S(1)}, u32[]{:S(2)}, u32[]{:S(2)}) collective-permute-start(bf16[256,256]{1,0:T(8,128)(2,1)} %get-tuple-element.135), channel_id=1, source_target_pairs={{0,8},{4,12},{8,0},{12,4},{16,24},{20,28},{24,16},{28,20},{1,9},{5... | collective-permute-start | bytes 393224 | tf_op jit(solution)/shard_map/ppermute | solution.py:656
  251.4 12.6 %collective-permute-start.60 = (bf16[256,256]{1,0:T(8,128)(2,1)}, bf16[256,256]{1,0:T(8,128)(2,1)S(1)}, u32[]{:S(2)}, u32[]{:S(2)}) collective-permute-start(bf16[256,256]{1,0:T(8,128)(2,1)} %get-tuple-element.136), channel_id=1, source_target_pairs={{0,16},{4,20},{8,24},{12,28},{16,0},{20,4},{24,8},{28,12},{1,17},{... | collective-permute-start | bytes 393224 | tf_op jit(solution)/shard_map/ppermute | solution.py:656
  251.4 12.6 %collective-permute-start.61 = (bf16[256,256]{1,0:T(8,128)(2,1)}, bf16[256,256]{1,0:T(8,128)(2,1)S(1)}, u32[]{:S(2)}, u32[]{:S(2)}) collective-permute-start(bf16[256,256]{1,0:T(8,128)(2,1)} %get-tuple-element.137), channel_id=1, source_target_pairs={{0,24},{4,28},{8,16},{12,20},{16,8},{20,12},{24,0},{28,4},{1,25},{... | collective-permute-start | bytes 393224 | tf_op jit(solution)/shard_map/ppermute | solution.py:656
  255.8 32.0 %collective-permute-start.21 = (bf16[2,256,1024]{2,1,0:T(8,128)(2,1)S(1)}, bf16[2,256,1024]{2,1,0:T(8,128)(2,1)}, u32[]{:S(2)}, u32[]{:S(2)}) collective-permute-start(bf16[2,256,1024]{2,1,0:T(8,128)(2,1)S(1)} %slice.142), channel_id=1, source_target_pairs={{0,1},{1,0},{2,3},{3,2},{4,5},{5,4},{6,7},{7,6},{8,9},{9,8},{10,11... | collective-permute-start | bytes 3145736 | tf_op jit(solution)/shard_map/ppermute | solution.py:656
  265.0 6.4 %collective-permute-start.63 = (bf16[256,256]{1,0:T(8,128)(2,1)S(1)}, bf16[256,256]{1,0:T(8,128)(2,1)S(1)}, u32[]{:S(2)}, u32[]{:S(2)}) collective-permute-start(bf16[256,256]{1,0:T(8,128)(2,1)S(1)} %add_convert_fusion.1), channel_id=1, source_target_pairs={{0,2},{1,3},{2,0},{3,1},{4,6},{5,7},{6,4},{7,5},{8,10},{9,11},{10,... | collective-permute-start | bytes 393224 | tf_op jit(solution)/shard_map/ppermute | solution.py:656
  265.8 7.5 %collective-permute-start.64 = (bf16[256,256]{1,0:T(8,128)(2,1)S(1)}, bf16[256,256]{1,0:T(8,128)(2,1)S(1)}, u32[]{:S(2)}, u32[]{:S(2)}) collective-permute-start(bf16[256,256]{1,0:T(8,128)(2,1)S(1)} %add_convert_fusion.1), channel_id=1, source_target_pairs={{0,3},{1,2},{2,1},{3,0},{4,7},{5,6},{6,5},{7,4},{8,11},{9,10},{10,... | collective-permute-start | bytes 393224 | tf_op jit(solution)/shard_map/ppermute | solution.py:656
  268.0 34.1 %collective-permute-start.38 = (bf16[128,512]{1,0:T(8,128)(2,1)S(1)}, bf16[128,512]{1,0:T(8,128)(2,1)S(1)}, u32[]{:S(2)}, u32[]{:S(2)}) collective-permute-start(bf16[128,512]{1,0:T(8,128)(2,1)S(1)} %add_convert_fusion.2.value_refs_0_), channel_id=1, source_target_pairs={{0,1},{1,0},{2,3},{3,2},{4,5},{5,4},{6,7},{7,6},{8,9},{9,8},{10,11... | collective-permute-start | bytes 393224 | tf_op jit(solution)/shard_map/ppermute | solution.py:656
  271.4 31.4 %collective-permute-start.39 = (bf16[128,512]{1,0:T(8,128)(2,1)S(1)}, bf16[128,512]{1,0:T(8,128)(2,1)}, u32[]{:S(2)}, u32[]{:S(2)}) collective-permute-start(bf16[128,512]{1,0:T(8,128)(2,1)S(1)} %add_convert_fusion.2.value_refs_0_), channel_id=1, source_target_pairs={{0,2},{1,3},{2,0},{3,1},{4,6},{5,7},{6,4},{7,5},{8,10},{9,11},{10,... | collective-permute-start | bytes 393224 | tf_op jit(solution)/shard_map/ppermute | solution.py:656
  281.6 7.9 %collective-permute-start.41 = (bf16[4,32,256]{2,1,0:T(8,128)(2,1)}, bf16[4,32,256]{2,1,0:T(8,128)(2,1)S(1)}, u32[]{:S(2)}, u32[]{:S(2)}) collective-permute-start(bf16[4,32,256]{2,1,0:T(8,128)(2,1)} %get-tuple-element.113), channel_id=1, source_target_pairs={{0,4},{4,0},{8,12},{12,8},{16,20},{20,16},{24,28},{28,24},{1,5},{5... | collective-permute-start | bytes 196616 | tf_op jit(solution)/shard_map/ppermute | solution.py:656
  291.7 5.0 %collective-permute-start.42 = (bf16[32,256]{1,0:T(8,128)(2,1)}, bf16[32,256]{1,0:T(8,128)(2,1)S(1)}, u32[]{:S(2)}, u32[]{:S(2)}) collective-permute-start(bf16[32,256]{1,0:T(8,128)(2,1)} %get-tuple-element.115), channel_id=1, source_target_pairs={{0,8},{4,12},{8,0},{12,4},{16,24},{20,28},{24,16},{28,20},{1,9},{5... | collective-permute-start | bytes 49160 | tf_op jit(solution)/shard_map/ppermute | solution.py:656
  294.1 5.0 %collective-permute-start.43 = (bf16[32,256]{1,0:T(8,128)(2,1)}, bf16[32,256]{1,0:T(8,128)(2,1)S(1)}, u32[]{:S(2)}, u32[]{:S(2)}) collective-permute-start(bf16[32,256]{1,0:T(8,128)(2,1)} %get-tuple-element.116), channel_id=1, source_target_pairs={{0,16},{4,20},{8,24},{12,28},{16,0},{20,4},{24,8},{28,12},{1,17},{... | collective-permute-start | bytes 49160 | tf_op jit(solution)/shard_map/ppermute | solution.py:656
  294.1 5.7 %collective-permute-start.44 = (bf16[32,256]{1,0:T(8,128)(2,1)}, bf16[32,256]{1,0:T(8,128)(2,1)S(1)}, u32[]{:S(2)}, u32[]{:S(2)}) collective-permute-start(bf16[32,256]{1,0:T(8,128)(2,1)} %get-tuple-element.117), channel_id=1, source_target_pairs={{0,24},{4,28},{8,16},{12,20},{16,8},{20,12},{24,0},{28,4},{1,25},{... | collective-permute-start | bytes 49160 | tf_op jit(solution)/shard_map/ppermute | solution.py:656
  296.7 9.7 %collective-permute-start.40 = (bf16[128,512]{1,0:T(8,128)(2,1)S(1)}, bf16[128,512]{1,0:T(8,128)(2,1)S(1)}, u32[]{:S(2)}, u32[]{:S(2)}) collective-permute-start(bf16[128,512]{1,0:T(8,128)(2,1)S(1)} %add_convert_fusion.2.value_refs_0_), channel_id=1, source_target_pairs={{0,3},{1,2},{2,1},{3,0},{4,7},{5,6},{6,5},{7,4},{8,11},{9,10},{10,... | collective-permute-start | bytes 393224 | tf_op jit(solution)/shard_map/ppermute | solution.py:656
  299.1 7.5 %collective-permute-start.31 = (bf16[128,512]{1,0:T(8,128)(2,1)S(1)}, bf16[128,512]{1,0:T(8,128)(2,1)S(1)}, u32[]{:S(2)}, u32[]{:S(2)}) collective-permute-start(bf16[128,512]{1,0:T(8,128)(2,1)S(1)} %add_convert_fusion.3.gate_refs_0_), channel_id=1, source_target_pairs={{0,1},{1,0},{2,3},{3,2},{4,5},{5,4},{6,7},{7,6},{8,9},{9,8},{10,11... | collective-permute-start | bytes 393224 | tf_op jit(solution)/shard_map/ppermute | solution.py:656
  299.9 4.3 %collective-permute-start.48 = (f32[32,512]{1,0:T(8,128)S(1)}, f32[32,512]{1,0:T(8,128)S(1)}, u32[]{:S(2)}, u32[]{:S(2)}) collective-permute-start(f32[32,512]{1,0:T(8,128)S(1)} %concatenate.41), channel_id=1, source_target_pairs={{0,4},{4,0},{8,12},{12,8},{16,20},{20,16},{24,28},{28,24},{1,5},{5... | collective-permute-start | bytes 196616 | tf_op jit(solution)/shard_map/ppermute | solution.py:656
  302.0 7.4 %collective-permute-start.32 = (bf16[128,512]{1,0:T(8,128)(2,1)S(1)}, bf16[128,512]{1,0:T(8,128)(2,1)S(1)}, u32[]{:S(2)}, u32[]{:S(2)}) collective-permute-start(bf16[128,512]{1,0:T(8,128)(2,1)S(1)} %add_convert_fusion.3.gate_refs_0_), channel_id=1, source_target_pairs={{0,2},{1,3},{2,0},{3,1},{4,6},{5,7},{6,4},{7,5},{8,10},{9,11},{10,... | collective-permute-start | bytes 393224 | tf_op jit(solution)/shard_map/ppermute | solution.py:656
  302.8 8.1 %collective-permute-start.33 = (bf16[128,512]{1,0:T(8,128)(2,1)S(1)}, bf16[128,512]{1,0:T(8,128)(2,1)S(1)}, u32[]{:S(2)}, u32[]{:S(2)}) collective-permute-start(bf16[128,512]{1,0:T(8,128)(2,1)S(1)} %add_convert_fusion.3.gate_refs_0_), channel_id=1, source_target_pairs={{0,3},{1,2},{2,1},{3,0},{4,7},{5,6},{6,5},{7,4},{8,11},{9,10},{10,... | collective-permute-start | bytes 393224 | tf_op jit(solution)/shard_map/ppermute | solution.py:656
  304.1 7.4 %collective-permute-start.45 = (bf16[32,256]{1,0:T(8,128)(2,1)S(1)}, bf16[32,256]{1,0:T(8,128)(2,1)S(1)}, u32[]{:S(2)}, u32[]{:S(2)}) collective-permute-start(bf16[32,256]{1,0:T(8,128)(2,1)S(1)} %add_convert_fusion.4.map_refs_0_), channel_id=1, source_target_pairs={{0,1},{1,0},{2,3},{3,2},{4,5},{5,4},{6,7},{7,6},{8,9},{9,8},{10,11... | collective-permute-start | bytes 49160 | tf_op jit(solution)/shard_map/ppermute | solution.py:656
  306.4 24.4 %collective-permute-start.49 = (f32[32,512]{1,0:T(8,128)S(1)}, f32[32,512]{1,0:T(8,128)S(1)}, u32[]{:S(2)}, u32[]{:S(2)}) collective-permute-start(f32[32,512]{1,0:T(8,128)S(1)} %add.261), channel_id=1, source_target_pairs={{0,8},{4,12},{8,0},{12,4},{16,24},{20,28},{24,16},{28,20},{1,9},{5... | collective-permute-start | bytes 196616 | tf_op jit(solution)/shard_map/ppermute | solution.py:656
  306.6 24.2 %collective-permute-start.50 = (f32[32,512]{1,0:T(8,128)S(1)}, f32[32,512]{1,0:T(8,128)S(1)}, u32[]{:S(2)}, u32[]{:S(2)}) collective-permute-start(f32[32,512]{1,0:T(8,128)S(1)} %add.261), channel_id=1, source_target_pairs={{0,16},{4,20},{8,24},{12,28},{16,0},{20,4},{24,8},{28,12},{1,17},{... | collective-permute-start | bytes 196616 | tf_op jit(solution)/shard_map/ppermute | solution.py:656
  309.4 21.4 %collective-permute-start.51 = (f32[32,512]{1,0:T(8,128)S(1)}, f32[32,512]{1,0:T(8,128)S(1)}, u32[]{:S(2)}, u32[]{:S(2)}) collective-permute-start(f32[32,512]{1,0:T(8,128)S(1)} %add.261), channel_id=1, source_target_pairs={{0,24},{4,28},{8,16},{12,20},{16,8},{20,12},{24,0},{28,4},{1,25},{... | collective-permute-start | bytes 196616 | tf_op jit(solution)/shard_map/ppermute | solution.py:656
  310.9 3.8 %collective-permute-start.46 = (bf16[32,256]{1,0:T(8,128)(2,1)S(1)}, bf16[32,256]{1,0:T(8,128)(2,1)S(1)}, u32[]{:S(2)}, u32[]{:S(2)}) collective-permute-start(bf16[32,256]{1,0:T(8,128)(2,1)S(1)} %add_convert_fusion.4.map_refs_0_), channel_id=1, source_target_pairs={{0,2},{1,3},{2,0},{3,1},{4,6},{5,7},{6,4},{7,5},{8,10},{9,11},{10,... | collective-permute-start | bytes 49160 | tf_op jit(solution)/shard_map/ppermute | solution.py:656
  311.6 3.7 %collective-permute-start.47 = (bf16[32,256]{1,0:T(8,128)(2,1)S(1)}, bf16[32,256]{1,0:T(8,128)(2,1)S(1)}, u32[]{:S(2)}, u32[]{:S(2)}) collective-permute-start(bf16[32,256]{1,0:T(8,128)(2,1)S(1)} %add_convert_fusion.4.map_refs_0_), channel_id=1, source_target_pairs={{0,3},{1,2},{2,1},{3,0},{4,7},{5,6},{6,5},{7,4},{8,11},{9,10},{10,... | collective-permute-start | bytes 49160 | tf_op jit(solution)/shard_map/ppermute | solution.py:656
  314.7 30.5 %collective-permute-start.24 = (bf16[256,1024]{1,0:T(8,128)(2,1)}, bf16[256,1024]{1,0:T(8,128)(2,1)}, u32[]{:S(2)}, u32[]{:S(2)}) collective-permute-start(bf16[256,1024]{1,0:T(8,128)(2,1)} %fusion.7), channel_id=1, source_target_pairs={{0,2},{1,3},{2,0},{3,1},{4,6},{5,7},{6,4},{7,5},{8,10},{9,11},{10,... | collective-permute-start | bytes 1572872 | tf_op jit(solution)/shard_map/ppermute | solution.py:656
  315.3 36.1 %collective-permute-start.22 = (bf16[256,1024]{1,0:T(8,128)(2,1)}, bf16[256,1024]{1,0:T(8,128)(2,1)S(1)}, u32[]{:S(2)}, u32[]{:S(2)}) collective-permute-start(bf16[256,1024]{1,0:T(8,128)(2,1)} %fusion.6), channel_id=1, source_target_pairs={{0,2},{1,3},{2,0},{3,1},{4,6},{5,7},{6,4},{7,5},{8,10},{9,11},{10,... | collective-permute-start | bytes 1572872 | tf_op jit(solution)/shard_map/ppermute | solution.py:656
  331.7 9.6 %collective-permute-start.53 = (f32[32,512]{1,0:T(8,128)S(1)}, f32[32,512]{1,0:T(8,128)S(1)}, u32[]{:S(2)}, u32[]{:S(2)}) collective-permute-start(f32[32,512]{1,0:T(8,128)S(1)} %fusion.35), channel_id=1, source_target_pairs={{0,2},{1,3},{2,0},{3,1},{4,6},{5,7},{6,4},{7,5},{8,10},{9,11},{10,... | collective-permute-start | bytes 196616 | tf_op jit(solution)/shard_map/ppermute | solution.py:656
  332.3 9.0 %collective-permute-start.54 = (f32[32,512]{1,0:T(8,128)S(1)}, f32[32,512]{1,0:T(8,128)S(1)}, u32[]{:S(2)}, u32[]{:S(2)}) collective-permute-start(f32[32,512]{1,0:T(8,128)S(1)} %fusion.35), channel_id=1, source_target_pairs={{0,3},{1,2},{2,1},{3,0},{4,7},{5,6},{6,5},{7,4},{8,11},{9,10},{10,... | collective-permute-start | bytes 196616 | tf_op jit(solution)/shard_map/ppermute | solution.py:656
  (64 other events, 749.6 us)
Sparse Core Ops, SparseCore 0:
  16.4 42.2 all-gather.2

commit v3 on v1

--- a/solution.py
+++ b/solution.py
@@ -1,3 +1,5 @@
+import functools
+
 import jax
 import jax.numpy as jnp
 from jax import lax
@@ -90,22 +92,97 @@
     )
 
 
-def norm_kernel(tok_ref, gain_ref, hid_ref):
-    tok = tok_ref[...]
-    scale = lax.rsqrt(jnp.mean(tok * tok, axis=-1, keepdims=True) + NORM_EPS)
-    hid_ref[...] = (tok * scale * gain_ref[...]).astype(BF16)
+def place(pieces, at_ref, sems, targets):
+    copies = []
+    for index, piece in enumerate(pieces):
+        for block in range(piece.shape[0]):
+            for first, rows, target in targets:
+                copies.append(
+                    pltpu.make_async_copy(
+                        piece.at[block, first : first + rows],
+                        target(at_ref[index] + block),
+                        sems.at[len(copies)],
+                    )
+                )
+    for copy in copies:
+        copy.start()
+    return copies
+
+
+def copies_of(pieces, targets):
+    return sum(piece.shape[0] for piece in pieces) * targets
+
+
+def rows_of(ref, rows):
+    return lambda at: ref.at[pl.ds(pl.multiple_of(at * rows, 16), rows)]
+
+
+def part_of(block, own_bit, keep_ref, send_ref, first=0):
+    for at in range(keep_ref.shape[0]):
+        low, high = block(2 * at).astype(BF16), block(2 * at + 1).astype(BF16)
+        rows = slice(first, first + low.shape[0])
+        keep_ref[at, rows] = jnp.where(own_bit == 0, low, high)
+        send_ref[at, rows] = jnp.where(own_bit == 0, high, low)
+
+
+def pick_heads(ref, base, ctx, heads):
+    first = pl.multiple_of(base + (ctx >> 1) * 2 * HEAD_DIM, 2 * HEAD_DIM)
+    wide = ref[:, pl.ds(first, 2 * HEAD_DIM)]
+    low = lax.broadcasted_iota(jnp.int32, wide.shape, 1) < HEAD_DIM
+    odd = (ctx & 1) == 1
+    out = []
+    for pair in range(heads // 2):
+        parts = []
+        for head in (2 * pair, 2 * pair + 1):
+            first = pl.multiple_of(base + head * 4 * HEAD_DIM + (ctx >> 1) * 2 * HEAD_DIM, 2 * HEAD_DIM)
+            parts.append(ref[:, pl.ds(first, 2 * HEAD_DIM)])
+        even = jnp.where(low, parts[0], pltpu.roll(parts[1], HEAD_DIM, 1))
+        other = jnp.where(low, pltpu.roll(parts[0], HEAD_DIM, 1), parts[1])
+        out.append(jnp.where(odd, other, even))
+    return out
+
+
+def pack_kernel(here_ref, win_ref, wout_ref, dt_ref, conv_ref, gain_ref, cot_ref, w1_ref, g2_ref, cotl_ref, tmp_ref):
+    ctx = here_ref[2]
+    rows = win_ref.shape[0]
+    heads = HEADS // 4
+    width = heads * HEAD_DIM
+    for at, part in enumerate(pick_heads(win_ref, INNER, ctx, heads)):
+        w1_ref[0:rows, at * 128 : (at + 1) * 128] = part.astype(BF16)
+    w1_ref[0:rows, width:] = win_ref[:, 2 * INNER :].astype(BF16)
+    tmp_ref[...] = jnp.zeros_like(tmp_ref)
+    row = lax.broadcasted_iota(jnp.int32, (heads, HEADS), 0)
+    col = lax.broadcasted_iota(jnp.int32, (heads, HEADS), 1)
+    table = jnp.where(col == 4 * row + ctx, 1.0, 0.0).astype(BF16)
+    tmp_ref[0:heads, 384 : 384 + dt_ref.shape[1]] = nn(table, dt_ref[...].astype(BF16))
+    tmp_ref[8 : 8 + CONV + 1, 0 : conv_ref.shape[1]] = conv_ref[...]
+    tmp_ref[8 + CONV + 1 : 8 + CONV + 2, 0 : gain_ref.shape[1]] = gain_ref[...]
+    w1_ref[rows : rows + 16, :] = tmp_ref[...].astype(BF16)
+    for at, part in enumerate(pick_heads(win_ref, 0, ctx, heads)):
+        g2_ref[0:rows, at * 128 : (at + 1) * 128] = part.astype(BF16)
+    if g2_ref.shape[0] > rows:
+        some = wout_ref.shape[0] // 4
+        mine = wout_ref[pl.ds(pl.multiple_of(ctx * some, 8), some), :].astype(BF16)
+        g2_ref[rows : rows + some] = mine[:, :width]
+        g2_ref[rows + some : rows + 2 * some] = mine[:, width:]
+    cotl_ref[...] = cot_ref[...].astype(BF16)
 
 
 def scan_forward_kernel(
-    perm_ref,
-    hid_ref,
-    w1_ref,
-    wdt_ref,
-    conv_ref,
+    here_ref,
+    at_ref,
+    tok_pieces,
+    w1_pieces,
     hrow_ref,
     hcol_ref,
     segc_ref,
     segr_ref,
+    hid_ref,
+    conv_ref,
+    gpre_ref,
+    gmine_ref,
+    wdt_ref,
+    w1_ref,
     mixed_ref,
     convin_ref,
     convsum_ref,
@@ -119,18 +196,61 @@
     ext_ref,
     seg_ref,
     state_ref,
+    small_ref,
+    tok_ref,
+    conv_all,
+    gain_all,
+    sems,
+    tok_sems,
 ):
     step = pl.program_id(0)
-    span = hid_ref.shape[1]
+    span, model = hid_ref.shape
     heads = wdt_ref.shape[0]
     width = heads * HEAD_DIM
+    shards = small_ref.shape[0]
+    rows = model // shards
 
     @pl.when(step == 0)
     def _():
+        copies = place(
+            w1_pieces,
+            at_ref,
+            sems,
+            [(0, rows, rows_of(w1_ref, rows)), (rows, 16, lambda at: small_ref.at[at])],
+        )
+        tokens = [
+            pltpu.make_async_copy(piece, tok_ref.at[here_ref[2] ^ index], tok_sems.at[index])
+            for index, piece in enumerate(tok_pieces)
+        ]
+        for copy in tokens:
+            copy.start()
         ext_ref[0:8] = jnp.zeros((8, ext_ref.shape[1]), F32)
         state_ref[...] = jnp.zeros_like(state_ref)
-
-    hid = hid_ref[0]
+        conv_all[...] = jnp.zeros_like(conv_all)
+        for copy in copies:
+            copy.wait()
+        conv_cols = conv_all.shape[1] // shards
+        gain_len = gain_all.shape[1] // shards
+        for shard in range(shards):
+            small = small_ref[shard].astype(F32)
+            wdt_ref[:, shard * rows : (shard + 1) * rows] = small[0:8, 384 : 384 + rows].astype(BF16)
+            conv_all[0 : CONV + 1, shard * conv_cols : (shard + 1) * conv_cols] = small[
+                8 : 8 + CONV + 1, :conv_cols
+            ]
+            gain_all[:, shard * gain_len : (shard + 1) * gain_len] = small[13:14, :gain_len]
+        for at, part in enumerate(pick_heads(conv_all, 0, here_ref[2], heads)):
+            conv_ref[:, at * 128 : (at + 1) * 128] = part
+        conv_ref[:, width:] = conv_all[:, INNER:]
+        gpre_ref[...] = gain_all[:, :model]
+        for at, part in enumerate(pick_heads(gain_all, model, here_ref[2], heads)):
+            gmine_ref[:, at * 128 : (at + 1) * 128] = part
+        for copy in tokens:
+            copy.wait()
+
+    tok = tok_ref[step]
+    scale = lax.rsqrt(jnp.mean(tok * tok, axis=-1, keepdims=True) + NORM_EPS)
+    hid = (tok * scale * gpre_ref[...]).astype(BF16)
+    hid_ref[...] = hid
     proj = nn(hid, w1_ref[...]).astype(BF16)
     convin_ref[...] = proj
     ext_ref[8 : 8 + span] = proj.astype(F32)
@@ -193,11 +313,53 @@
     )
 
 
-def gate_kernel(perm_ref, hid_ref, wg_ref, inner_ref, cot_ref, wout_ref, gain_ref, gate_ref, ng_ref, stat_ref):
-    gate = nn(hid_ref[0], wg_ref[...]).astype(BF16)
+def gate_kernel(
+    here_ref,
+    at_ref,
+    hid_ref,
+    g2_pieces,
+    cot_pieces,
+    inner_ref,
+    gain_ref,
+    wg_ref,
+    wout_ref,
+    cot_ref,
+    gate_ref,
+    ng_ref,
+    stat_ref,
+    sems,
+    cot_sems,
+):
+    step = pl.program_id(0)
+    rows = wg_ref.shape[0] // (wout_ref.shape[0] // HEAD_DIM)
+    width = wg_ref.shape[1]
+
+    @pl.when(step == 0)
+    def _():
+        some = rows_of(wout_ref, HEAD_DIM)
+        copies = place(
+            g2_pieces,
+            at_ref,
+            sems,
+            [
+                (0, rows, rows_of(wg_ref, rows)),
+                (rows, HEAD_DIM, lambda at: some(at).at[:, 0:width]),
+                (rows + HEAD_DIM, HEAD_DIM, lambda at: some(at).at[:, width : 2 * width]),
+            ],
+        )
+        cots = [
+            pltpu.make_async_copy(piece, cot_ref.at[here_ref[2] ^ index], cot_sems.at[index])
+            for index, piece in enumerate(cot_pieces)
+        ]
+        for copy in cots:
+            copy.start()
+        for copy in copies + cots:
+            copy.wait()
+
+    gate = nn(hid_ref[...], wg_ref[...]).astype(BF16)
     gate_ref[...] = gate
     gate = gate.astype(F32)
-    grad = nt(cot_ref[0], wout_ref[...])
+    grad = nt(cot_ref[step], wout_ref[...])
     ng_ref[...] = grad
     gated = inner_ref[...] * (gate * sigmoid(gate))
     ones = jnp.ones((8, gated.shape[1]), F32)
@@ -209,18 +371,19 @@
 
 def norm_back_kernel(
     perm_ref,
+    here_ref,
     hid_ref,
     inner_ref,
     gate_ref,
     ng_ref,
     stat_ref,
     gain_ref,
+    mixed_ref,
+    wout_ref,
     cot_ref,
-    wout_ref,
-    mixed_ref,
     block_ref,
-    outg_ref,
-    ing_ref,
+    keep_ref,
+    send_ref,
     dy_ref,
     dgate_ref,
     sums_ref,
@@ -249,7 +412,7 @@
     gated = inner * silu
     unit = gated * inv
     normed = (unit * gain_ref[...]).astype(BF16)
-    cot = cot_ref[0]
+    cot = cot_ref[step]
     block_ref[0] = nn(normed, wout_ref[...]).astype(BF16)
     outacc_ref[...] += tn(normed, cot)
     grad = ng_ref[...]
@@ -258,7 +421,7 @@
     dy_ref[...] = dy
     dgate = (dgated * inner * (sig * (1.0 + gate * (1.0 - sig)))).astype(BF16)
     dgate_ref[...] = dgate
-    inacc_ref[...] += tn(hid_ref[0], dgate)
+    inacc_ref[...] += tn(hid_ref[...], dgate)
     gain_sum = jnp.sum(grad * unit, axis=0, keepdims=True)
     skip_sum = jnp.sum(dy * mixed_ref[...].astype(F32), axis=0, keepdims=True)
     at = lax.broadcasted_iota(jnp.int32, (8, width), 0)
@@ -266,12 +429,17 @@
 
     @pl.when(step == pl.num_programs(0) - 1)
     def _():
-        outg_ref[...] = outacc_ref[...].astype(BF16)
-        ing_ref[...] = inacc_ref[...].astype(BF16)
+        own = here_ref[0]
+        rows = inacc_ref.shape[0] // (2 * keep_ref.shape[0])
+        part_of(lambda at: inacc_ref[at * rows : (at + 1) * rows], own, keep_ref, send_ref)
+        outs = lambda at: outacc_ref[at * HEAD_DIM : (at + 1) * HEAD_DIM]
+        part_of(lambda at: outs(at)[:, :width], own, keep_ref, send_ref, rows)
+        part_of(lambda at: outs(at)[:, width:], own, keep_ref, send_ref, rows + HEAD_DIM)
 
 
 def scan_back_kernel(
     perm_ref,
+    here_ref,
     hid_ref,
     dy_ref,
     mixed_ref,
@@ -287,7 +455,8 @@
     hrow_ref,
     segc_ref,
     segr_ref,
-    ing_ref,
+    keep_ref,
+    send_ref,
     dval_ref,
     dbc_ref,
     dstep_ref,
@@ -302,7 +471,7 @@
 ):
     step = pl.program_id(0)
     chunk = pl.num_programs(0) - 1 - step
-    span = hid_ref.shape[1]
+    span = hid_ref.shape[0]
     heads = stepc_ref.shape[1]
     width = heads * HEAD_DIM
 
@@ -410,7 +579,7 @@
     draw = (dstep - rate * dalpha) * sigmoid(raw_ref[...])
     draw_low = draw.astype(BF16)
     dstep_ref[...] = draw_low
-    hid = hid_ref[0]
+    hid = hid_ref[...]
     dtg_ref[...] += tn(draw_low, hid)
     rate_sum = jnp.sum(-dalpha * step_c * rate, axis=0, keepdims=True)
     bias_sum = jnp.sum(draw, axis=0, keepdims=True)
@@ -436,15 +605,57 @@
 
     @pl.when(step == pl.num_programs(0) - 1)
     def _():
-        ing_ref[...] = inacc_ref[...].astype(BF16)
-
-
-def hidden_back_kernel(perm_ref, dgate_ref, dval_ref, dstep_ref, wg_ref, wv_ref, wdt_ref, out_ref):
+        rows = inacc_ref.shape[0] // (2 * keep_ref.shape[0])
+        part_of(lambda at: inacc_ref[at * rows : (at + 1) * rows], here_ref[0], keep_ref, send_ref)
+
+
+def hidden_back_kernel(
+    perm_ref,
+    dgate_ref,
+    dval_ref,
+    dstep_ref,
+    wg_ref,
+    wv_ref,
+    wdt_ref,
+    hid_ref,
+    gain_ref,
+    out_ref,
+    gsum_ref,
+):
+    @pl.when(pl.program_id(0) == 0)
+    def _():
+        gsum_ref[...] = jnp.zeros_like(gsum_ref)
+
     total = nt(dgate_ref[...], wg_ref[...]) + nt(dval_ref[...], wv_ref[...])
-    out_ref[0] = (total + nn(dstep_ref[...], wdt_ref[...])).astype(BF16)
-
-
-def maps_back_kernel(dbc_ref, convsum_ref, convin_ref, conv_ref, segc_ref, hid_ref, dmap_ref, convg_ref, ing_ref, ext_ref):
+    total = total + nn(dstep_ref[...], wdt_ref[...])
+    out_ref[0] = total.astype(BF16)
+    unit = hid_ref[...].astype(F32) / gain_ref[...]
+    gsum_ref[...] += jnp.sum(total * unit, axis=0, keepdims=True) + jnp.zeros(gsum_ref.shape, F32)
+
+
+def maps_back_kernel(
+    here_ref,
+    dbc_ref,
+    convsum_ref,
+    convin_ref,
+    conv_ref,
+    segc_ref,
+    hid_ref,
+    w1_ref,
+    gain_ref,
+    convg_ref,
+    sums_ref,
+    headg_ref,
+    dtg_ref,
+    gall_ref,
+    keep_ref,
+    send_ref,
+    own_ref,
+    ext_ref,
+    acc_ref,
+    dmap_ref,
+    small_ref,
+):
     size, width = dmap_ref.shape
     ext_ref[0:size] = dbc_ref[...] * silu_grad(convsum_ref[...])
     ext_ref[size : size + 8] = jnp.zeros((8, width), F32)
@@ -459,31 +670,164 @@
         term = jnp.where(same, ext_ref[ahead : ahead + size], 0.0)
         back = back + conv_ref[tap : tap + 1] * term
         sums = sums + jnp.where(at == tap, jnp.sum(conv_in * term, axis=0, keepdims=True), 0.0)
-    convg_ref[...] = sums
-    dmap = back.astype(BF16)
-    dmap_ref[...] = dmap
-    ing_ref[...] = tn(hid_ref[...], dmap).astype(BF16)
-
-
-def input_back_kernel(hg_ref, dmap_ref, wbc_ref, tok_ref, gain_ref, cot_ref, out_ref, gsum_ref):
-    grad = hg_ref[...] + nt(dmap_ref[...], wbc_ref[...])
+    dmap_ref[...] = back.astype(BF16)
+    ctx = here_ref[2]
+    acc_ref[...] = tn(hid_ref[...], dmap_ref[...])
+    span = own_ref.shape[0]
+    own = pl.ds(pl.multiple_of(ctx * span, 16), span)
+    grad = nt(dmap_ref[own, :], w1_ref[:, w1_ref.shape[1] - width :])
+    own_ref[...] = grad
+    unit = hid_ref[own, :].astype(F32) / gain_ref[...]
+    gain_sum = gall_ref[0:1] + jnp.sum(grad * unit, axis=0, keepdims=True)
+    half = small_ref.shape[1]
+    heads = headg_ref.shape[1]
+    small_ref[...] = jnp.zeros_like(small_ref)
+    small_ref[0 : CONV + 1] = convg_ref[0 : CONV + 1]
+    small_ref[CONV + 1 : CONV + 3] = sums_ref[0:2]
+    small_ref[7:8, 0:heads] = headg_ref[0:1]
+    small_ref[7:8, 128 : 128 + heads] = headg_ref[1:2]
+    small_ref[8 : 8 + CONV + 1, 0:width] = sums[0 : CONV + 1]
+    small_ref[13:14] = gain_sum[:, :half]
+    small_ref[14:15] = gain_sum[:, half:]
+    small_ref[15:16] = small_ref[7:8] - small_ref[7:8].astype(BF16).astype(F32)
+    small_ref[16:24] = dtg_ref[:, :half]
+    small_ref[24:32] = dtg_ref[:, half:]
+    small = small_ref[...].astype(BF16)
+    count = keep_ref.shape[0] // 32 - 1
+    block = acc_ref.shape[0] // (2 * count)
+    some = block // 4
+    keep_ref[0:32] = small
+    send_ref[0:32] = small
+    for at in range(count):
+        start = pl.multiple_of(2 * at * block + ctx * some, 8)
+        low = acc_ref[pl.ds(start, some), :].astype(BF16)
+        start = pl.multiple_of((2 * at + 1) * block + ctx * some, 8)
+        high = acc_ref[pl.ds(start, some), :].astype(BF16)
+        keep_ref[32 + 32 * at : 64 + 32 * at, 0:width] = jnp.where(here_ref[0] == 0, low, high)
+        send_ref[32 + 32 * at : 64 + 32 * at, 0:width] = jnp.where(here_ref[0] == 0, high, low)
+
+
+def input_back_kernel(hg_ref, own_ref, tok_ref, gain_ref, cot_ref, out_ref):
+    grad = hg_ref[...] + own_ref[...]
     tok = tok_ref[...]
     scale = lax.rsqrt(jnp.mean(tok * tok, axis=-1, keepdims=True) + NORM_EPS)
     unit = tok * scale
-    gsum_ref[...] = jnp.sum(grad * unit, axis=0, keepdims=True) + jnp.zeros(gsum_ref.shape, F32)
     scaled = grad * gain_ref[...]
     mean = jnp.mean(scaled * unit, axis=-1, keepdims=True)
     out_ref[...] = cot_ref[...] + scale * (scaled - unit * mean)
 
 
+def pair_sum_kernel(here_ref, keep_ref, came_ref, out_refs):
+    for at, out_ref in enumerate(out_refs):
+        index = pl.ds(here_ref[1] ^ at, 1)
+        out_ref[...] = (keep_ref[index].astype(F32) + came_ref[index].astype(F32))[0].astype(BF16)
+
+
+def pair_sum_late_kernel(here_ref, keep_ref, came_ref, mkeep_ref, mcame_ref, out_refs):
+    rows, width = keep_ref.shape[1:]
+    small = (mkeep_ref[0:32].astype(F32) + mcame_ref[0:32].astype(F32))
+    row = lax.broadcasted_iota(jnp.int32, small.shape, 0)
+    head = small[7:8] + small[15:16]
+    rest = head - head.astype(BF16).astype(F32)
+    small = jnp.where(row == 7, head, jnp.where(row == 15, rest, small)).astype(BF16)
+    for at, out_ref in enumerate(out_refs):
+        block = here_ref[1] ^ at
+        index = pl.ds(block, 1)
+        out_ref[0:rows] = (keep_ref[index].astype(F32) + came_ref[index].astype(F32))[0].astype(BF16)
+        out_ref[rows : rows + 32] = small
+        index = pl.ds(pl.multiple_of(32 + 32 * block, 32), 32)
+        out_ref[rows + 32 : rows + 64] = (
+            mkeep_ref[index].astype(F32) + mcame_ref[index].astype(F32)
+        ).astype(BF16)
+
+
+def sum_kernel(late, part_refs, out_ref):
+    terms = [ref[...].astype(F32) for ref in part_refs]
+    while len(terms) > 1:
+        terms = [terms[at] + terms[at + 1] for at in range(0, len(terms), 2)]
+    total = terms[0]
+    if late:
+        first = out_ref.shape[0] - 64
+        row = lax.broadcasted_iota(jnp.int32, total.shape, 0)
+        head = total[first + 7 : first + 8] + total[first + 15 : first + 16]
+        rest = head - head.astype(BF16).astype(F32)
+        total = jnp.where(row == first + 7, head, jnp.where(row == first + 15, rest, total))
+    out_ref[...] = total.astype(out_ref.dtype)
+
+
+def adam_kernel(
+    here_ref,
+    win_ref,
+    wfirst_ref,
+    wsecond_ref,
+    oin_ref,
+    ofirst_ref,
+    osecond_ref,
+    early_refs,
+    late_refs,
+    win_new,
+    wfirst_new,
+    wsecond_new,
+    out_new,
+    ofirst_new,
+    osecond_new,
+    early_ref,
+    late_ref,
+):
+    step = pl.program_id(0)
+    pieces = len(early_refs)
+    rows = win_ref.shape[0]
+    width = early_ref.shape[2]
+    block = pieces * HEAD_DIM
+
+    @pl.when(step == 0)
+    def _():
+        for at in range(pieces):
+            owner = pl.ds(here_ref[2] ^ at, 1)
+            early_ref[owner] = early_refs[at][...][None]
+            late_ref[owner] = late_refs[at][...][None]
+
+    here = pl.ds(pl.multiple_of(step * rows, rows), rows)
+    low = lax.broadcasted_iota(jnp.int32, (rows, 2 * HEAD_DIM), 1) < HEAD_DIM
+
+    def update(lanes, grad):
+        news = adam_step(
+            win_ref[:, lanes], wfirst_ref[:, lanes], wsecond_ref[:, lanes], grad, 0.03, WEIGHT_DECAY
+        )
+        win_new[:, lanes], wfirst_new[:, lanes], wsecond_new[:, lanes] = news
+
+    for base, ref in ((0, early_ref), (INNER, late_ref)):
+        for pair in range(width // (2 * HEAD_DIM)):
+            lanes = slice(pair * 2 * HEAD_DIM, (pair + 1) * 2 * HEAD_DIM)
+            for at in range(0, pieces, 2):
+                first = ref[at, here, lanes].astype(F32)
+                second = ref[at + 1, here, lanes].astype(F32)
+                start = base + 2 * pair * block + at * HEAD_DIM
+                even = jnp.where(low, first, pltpu.roll(second, HEAD_DIM, 1))
+                update(slice(start, start + 2 * HEAD_DIM), even)
+                start = start + block
+                odd = jnp.where(low, pltpu.roll(first, HEAD_DIM, 1), second)
+                update(slice(start, start + 2 * HEAD_DIM), odd)
+    first = late_ref.shape[1] - 32
+    update(slice(2 * INNER, 2 * INNER + 2 * STATE), late_ref[step, first : first + 32, 0 : 2 * STATE].astype(F32))
+    first = rows * pieces
+    for at in range(2):
+        lanes = slice(at * width, (at + 1) * width)
+        grad = early_ref[step, first + at * HEAD_DIM : first + (at + 1) * HEAD_DIM].astype(F32)
+        news = adam_step(
+            oin_ref[:, lanes], ofirst_ref[:, lanes], osecond_ref[:, lanes], grad, 0.02, WEIGHT_DECAY
+        )
+        out_new[:, lanes], ofirst_new[:, lanes], osecond_new[:, lanes] = news
+
+
 def swap(value, axis, bit):
     count = lax.axis_size(axis)
     return lax.ppermute(value, axis, [(at, at ^ bit) for at in range(count)])
 
 
 def gather_ctx(value):
-    two = jnp.stack([value, swap(value, "ctx", 2)])
-    return jnp.concatenate([two, swap(two, "ctx", 1)])
+    far = swap(value, "ctx", 2)
+    return [value, swap(value, "ctx", 1), far, swap(far, "ctx", 1)]
 
 
 def scatter_ctx(value):
@@ -495,6 +839,24 @@
     pair = value.astype(F32) + swap(value, "ctx", 1).astype(F32)
     pair = pair.astype(BF16)
     return pair.astype(F32) + swap(pair, "ctx", 2).astype(F32)
+
+
+def gather_dp(value):
+    count, here = lax.axis_size("dp"), lax.axis_index("dp")
+    if count != 8:
+        return [lax.all_gather(value, "dp", axis=0)], jnp.zeros((1,), jnp.int32)
+    value = value[None]
+    pieces = [(value, 0)] + [(swap(value, "dp", bit), bit) for bit in range(2, count, 2)]
+    pieces += [(swap(piece, "dp", 1), bit + 1) for piece, bit in pieces]
+    return [piece for piece, _ in pieces], here ^ jnp.asarray([bit for _, bit in pieces], jnp.int32)
+
+
+def spread_dp(parts):
+    return [parts[0]] + [swap(part, "dp", 2 * at) for at, part in enumerate(parts) if at]
+
+
+def fan_ctx(value):
+    return [value] + [swap(value, "ctx", bit) for bit in range(1, lax.axis_size("ctx"))]
 
 
 def adam_step(weight, moment_one, second, gradient, step_rate, decay_rate):
@@ -549,90 +911,78 @@
     wide = width + maps
     chunks = nctx
     rows_in = in_weight.shape[0]
-    rows_out = out_weight.shape[0]
-    cols_out = model // nctx
     conv_cols = conv_params.shape[1]
     gain_len = gains.shape[0]
     dt_cols = dt_weight.shape[1]
-
+    near = ndp == heads
+    high = heads // 2
+    block_in = model // heads
     tok = tokens[0]
-    lanes = max(-(-max(gain_len, conv_cols, dt_cols) // 128) * 128, 128)
-
-    def padded(value):
-        return jnp.pad(value.astype(BF16), ((0, 0), (0, lanes - value.shape[1])))
-
-    small = jnp.concatenate(
-        [padded(dt_weight), padded(conv_params), padded(gains[None]), jnp.zeros((10, lanes), BF16)]
-    )
-    small_all = lax.all_gather(small, "dp", axis=0)
-    gain_full = small_all[:, HEADS + CONV + 1, :gain_len].astype(F32).reshape(1, -1)
-    conv_full = jnp.moveaxis(
-        small_all[:, HEADS : HEADS + CONV + 1, :conv_cols].astype(F32), 0, 1
-    ).reshape(CONV + 1, -1)
-    dt_mine = lax.dynamic_slice_in_dim(small_all[:, :HEADS, :dt_cols], c * heads, heads, 1)
-    dt_mine = jnp.moveaxis(dt_mine, 0, 1).reshape(heads, model)
-    gain_pre = gain_full[:, :model]
-    gain_mine = lax.dynamic_slice_in_dim(gain_full, model + c * width, width, 1)
-    conv_mine = jnp.concatenate(
-        [lax.dynamic_slice_in_dim(conv_full, c * width, width, 1), conv_full[:, INNER:]], axis=1
-    )
-    conv_mine = jnp.pad(conv_mine, ((0, 8 - CONV - 1), (0, 0)))
-
-    value_part = lax.dynamic_slice_in_dim(in_weight, INNER + c * width, width, 1)
-    w1 = lax.all_gather(
-        jnp.concatenate([value_part, in_weight[:, 2 * INNER :]], axis=1).astype(BF16),
-        "dp",
-        axis=0,
-        tiled=True,
-    )
-    wout = lax.all_gather(
-        lax.dynamic_slice_in_dim(out_weight, c * cols_out, cols_out, 1).astype(BF16),
-        "dp",
-        axis=0,
-        tiled=True,
-    )
-    wout = lax.all_to_all(wout, "ctx", split_axis=0, concat_axis=1, tiled=True)
-    wg = lax.all_gather(
-        lax.dynamic_slice_in_dim(in_weight, c * width, width, 1).astype(BF16),
-        "dp",
-        axis=0,
-        tiled=True,
-    )
-
+    bits = jnp.stack([d & 1, d >> 1, c] if near else [0 * d, 0 * d, c]).astype(jnp.int32)
     order = jnp.asarray([0, 2, 1, 3], jnp.int32)
     perm = order[jnp.arange(nctx, dtype=jnp.int32) ^ c]
-    cot_all = gather_ctx(cotangent[0].astype(BF16))
-    hid_own = pl.pallas_call(
-        norm_kernel, out_shape=shape_of(span, model, dtype=BF16), compiler_params=params(), name="pre_norm"
-    )(tok, gain_pre)
-    hid_all = gather_ctx(hid_own)
+    smem = pl.BlockSpec(memory_space=pltpu.SMEM)
+    vmem = pl.BlockSpec(memory_space=pltpu.VMEM)
+    anywhere = lambda pieces: [pl.BlockSpec(memory_space=pl.ANY)] * len(pieces)
+
+    w1, g2, cot_low = pl.pallas_call(
+        pack_kernel,
+        in_specs=[smem] + [vmem] * 6,
+        out_shape=[
+            shape_of(rows_in + 16, wide, dtype=BF16),
+            shape_of(rows_in + (2 * HEAD_DIM if near else 0), width, dtype=BF16),
+            shape_of(span, model, dtype=BF16),
+        ],
+        scratch_shapes=[pltpu.VMEM((16, wide), F32)],
+        compiler_params=params(),
+        name="pack",
+    )(bits, in_weight, out_weight, dt_weight, conv_params, gains[None], cotangent[0])
+    toks = gather_ctx(tok)
+    w1, at_rows = gather_dp(w1)
+    if near:
+        g2, at_g2 = gather_dp(g2)
+    else:
+        wg = lax.all_gather(g2, "dp", axis=0, tiled=True).reshape(heads, block_in, width)
+        wout = lax.all_gather(out_weight.astype(BF16), "dp", axis=0, tiled=True)
+        wout = lax.dynamic_index_in_dim(wout.reshape(heads, nctx, HEAD_DIM, model), c, 1, False)
+        g2 = [jnp.concatenate([wg, wout[:, :, :width], wout[:, :, width:]], axis=1)]
+        at_g2 = at_rows
+    cots = gather_ctx(cot_low)
 
     ids = segment_ids[0]
     seg_col = jnp.pad(ids, (8, 8), constant_values=-1)[:, None]
     seg_row = segment_ids
-    head_mine = lax.dynamic_slice_in_dim(head_params, c * heads, heads, 1)
+    head_mine = lax.dynamic_index_in_dim(head_params.reshape(3, heads, nctx), c, 2, False)
     head_col = head_mine.T
 
-    slot_rows = pl.BlockSpec((1, span, model), lambda i, p: (p[i], 0, 0))
-    rows = lambda cols: pl.BlockSpec((span, cols), lambda i, p: (i, 0))
-    row_of = pl.BlockSpec((heads, span), lambda i, p: (0, i))
-
-    mixed, conv_in, conv_sum, inner, raw, step_c, log_c, step_r, log_r, starts = pl.pallas_call(
+    rows = lambda cols: pl.BlockSpec((span, cols), lambda i, *_: (i, 0))
+    row_of = pl.BlockSpec((heads, span), lambda i, *_: (0, i))
+    slot_rows = pl.BlockSpec((1, span, model), lambda i, p, *_: (p[i], 0, 0))
+    shards_in = sum(piece.shape[0] for piece in w1)
+
+    (
+        hid, conv_mine, gain_pre, gain_mine, dt_mine, w1, mixed, conv_in, conv_sum, inner, raw,
+        step_c, log_c, step_r, log_r, starts,
+    ) = pl.pallas_call(
         scan_forward_kernel,
         grid_spec=pltpu.PrefetchScalarGridSpec(
-            num_scalar_prefetch=1,
+            num_scalar_prefetch=2,
             grid=(chunks,),
             in_specs=[
-                slot_rows,
-                full((model, wide)),
-                full((heads, model)),
-                full((8, wide)),
+                anywhere(toks),
+                anywhere(w1),
                 full((3, heads)),
                 full((heads, 3)),
                 full((length + 16, 1)),
-                pl.BlockSpec((1, span), lambda i, p: (0, i)),
+                pl.BlockSpec((1, span), lambda i, *_: (0, i)),
             ],
             out_specs=[
+                rows(model),
+                full((8, wide)),
+                full((1, model)),
+                full((1, width)),
+                full((heads, model)),
+                full((model, wide)),
                 rows(wide),
                 rows(wide),
                 rows(wide),
@@ -642,15 +992,27 @@
                 rows(heads),
                 row_of,
                 row_of,
-                pl.BlockSpec((1, STATE, width), lambda i, p: (i, 0, 0)),
+                pl.BlockSpec((1, STATE, width), lambda i, *_: (i, 0, 0)),
             ],
             scratch_shapes=[
                 pltpu.VMEM((span + 8, wide), F32),
                 pltpu.VMEM((span + 8, 1), jnp.int32),
                 pltpu.VMEM((STATE, width), F32),
+                pltpu.VMEM((shards_in, 16, wide), BF16),
+                pltpu.VMEM((nctx, span, model), F32),
+                pltpu.VMEM((8, INNER + maps), F32),
+                pltpu.VMEM((1, model + INNER), F32),
+                pltpu.SemaphoreType.DMA((copies_of(w1, 2),)),
+                pltpu.SemaphoreType.DMA((nctx,)),
             ],
         ),
         out_shape=[
+            shape_of(length, model, dtype=BF16),
+            shape_of(8, wide),
+            shape_of(1, model),
+            shape_of(1, width),
+            shape_of(heads, model, dtype=BF16),
+            shape_of(model, wide, dtype=BF16),
             shape_of(length, wide, dtype=BF16),
             shape_of(length, wide, dtype=BF16),
             shape_of(length, wide),
@@ -664,54 +1026,61 @@
         ],
         compiler_params=params("arbitrary"),
         name="scan_forward",
-    )(perm, hid_all, w1, dt_mine, conv_mine, head_mine, head_col, seg_col, seg_row)
-
-    gate, normed_grad, stats = pl.pallas_call(
+    )(bits, at_rows, toks, w1, head_mine, head_col, seg_col, seg_row)
+
+    wg, wout, cot_all, gate, normed_grad, stats = pl.pallas_call(
         gate_kernel,
         grid_spec=pltpu.PrefetchScalarGridSpec(
-            num_scalar_prefetch=1,
+            num_scalar_prefetch=2,
             grid=(chunks,),
-            in_specs=[
-                slot_rows,
+            in_specs=[rows(model), anywhere(g2), anywhere(cots), rows(width), full((1, width))],
+            out_specs=[
                 full((model, width)),
+                full((width, model)),
+                full((nctx, span, model)),
                 rows(width),
-                slot_rows,
-                full((width, model)),
-                full((1, width)),
+                rows(width),
+                pl.BlockSpec((8, span), lambda i, *_: (0, i)),
             ],
-            out_specs=[rows(width), rows(width), pl.BlockSpec((8, span), lambda i, p: (0, i))],
+            scratch_shapes=[
+                pltpu.SemaphoreType.DMA((copies_of(g2, 3),)),
+                pltpu.SemaphoreType.DMA((nctx,)),
+            ],
         ),
         out_shape=[
+            shape_of(model, width, dtype=BF16),
+            shape_of(width, model, dtype=BF16),
+            shape_of(nctx, span, model, dtype=BF16),
             shape_of(length, width, dtype=BF16),
             shape_of(length, width),
             shape_of(8, length),
         ],
         compiler_params=params("arbitrary"),
         name="gate",
-    )(perm, hid_all, wg, inner, cot_all, wout, gain_mine)
-    stats = stats + swap(stats, "ctx", 1)
-    stats = stats + swap(stats, "ctx", 2)
-
-    block_part, out_grad, gate_in_grad, dy, dgate, col_sums = pl.pallas_call(
+    )(bits, at_g2, hid, g2, cots, inner, gain_mine)
+    stats = sum(fan_ctx(stats))
+
+    early_rows = block_in + 2 * HEAD_DIM
+    block_part, early_keep, early_send, dy, dgate, col_sums = pl.pallas_call(
         norm_back_kernel,
         grid_spec=pltpu.PrefetchScalarGridSpec(
-            num_scalar_prefetch=1,
+            num_scalar_prefetch=2,
             grid=(chunks,),
             in_specs=[
-                slot_rows,
+                rows(model),
                 rows(width),
                 rows(width),
                 rows(width),
-                pl.BlockSpec((8, span), lambda i, p: (0, i)),
+                pl.BlockSpec((8, span), lambda i, *_: (0, i)),
                 full((1, width)),
-                slot_rows,
+                rows(width),
                 full((width, model)),
-                rows(width),
+                full((nctx, span, model)),
             ],
             out_specs=[
                 slot_rows,
-                full((width, model)),
-                full((model, width)),
+                full((high, early_rows, width)),
+                full((high, early_rows, width)),
                 rows(width),
                 rows(width),
                 full((8, width)),
@@ -720,30 +1089,28 @@
         ),
         out_shape=[
             shape_of(nctx, span, model, dtype=BF16),
-            shape_of(width, model, dtype=BF16),
-            shape_of(model, width, dtype=BF16),
+            shape_of(high, early_rows, width, dtype=BF16),
+            shape_of(high, early_rows, width, dtype=BF16),
             shape_of(length, width),
             shape_of(length, width, dtype=BF16),
             shape_of(8, width),
         ],
         compiler_params=params("arbitrary"),
         name="norm_back",
-    )(perm, hid_all, inner, gate, normed_grad, stats, gain_mine, cot_all, wout, mixed)
-
+    )(perm, bits, hid, inner, gate, normed_grad, stats, gain_mine, mixed, wout, cot_all)
     block_output = tok + scatter_ctx(block_part)
-    out_cols = lax.all_to_all(out_grad, "ctx", split_axis=1, concat_axis=0, tiled=True)
-    out_shard = lax.psum_scatter(out_cols, "dp", scatter_dimension=0, tiled=True)
-    gate_shard = lax.psum_scatter(gate_in_grad, "dp", scatter_dimension=0, tiled=True)
-
-    back = lambda cols: pl.BlockSpec((span, cols), lambda i, p: (chunks - 1 - i, 0))
-    back_row = pl.BlockSpec((heads, span), lambda i, p: (0, chunks - 1 - i))
-    value_in_grad, dval, dbc, dstep, conv_grad, dt_grad, head_grad = pl.pallas_call(
+    if near:
+        early_came = swap(early_send, "dp", 1)
+
+    back = lambda cols: pl.BlockSpec((span, cols), lambda i, *_: (chunks - 1 - i, 0))
+    back_row = pl.BlockSpec((heads, span), lambda i, *_: (0, chunks - 1 - i))
+    late_keep, late_send, dval, dbc, dstep, conv_grad, dt_grad, head_grad = pl.pallas_call(
         scan_back_kernel,
         grid_spec=pltpu.PrefetchScalarGridSpec(
-            num_scalar_prefetch=1,
+            num_scalar_prefetch=2,
             grid=(chunks,),
             in_specs=[
-                pl.BlockSpec((1, span, model), lambda i, p: (p[chunks - 1 - i], 0, 0)),
+                back(model),
                 back(width),
                 back(wide),
                 back(width),
@@ -753,14 +1120,15 @@
                 back(heads),
                 back_row,
                 back_row,
-                pl.BlockSpec((1, STATE, width), lambda i, p: (chunks - 1 - i, 0, 0)),
+                pl.BlockSpec((1, STATE, width), lambda i, *_: (chunks - 1 - i, 0, 0)),
                 full((8, width)),
                 full((3, heads)),
                 full((length + 16, 1)),
-                pl.BlockSpec((1, span), lambda i, p: (0, chunks - 1 - i)),
+                pl.BlockSpec((1, span), lambda i, *_: (0, chunks - 1 - i)),
             ],
             out_specs=[
-                full((model, width)),
+                full((high, block_in, width)),
+                full((high, block_in, width)),
                 back(width),
                 back(maps),
                 back(heads),
@@ -777,7 +1145,8 @@
             ],
         ),
         out_shape=[
-            shape_of(model, width, dtype=BF16),
+            shape_of(high, block_in, width, dtype=BF16),
+            shape_of(high, block_in, width, dtype=BF16),
             shape_of(length, width, dtype=BF16),
             shape_of(length, maps, dtype=BF16),
             shape_of(length, heads, dtype=BF16),
@@ -788,13 +1157,22 @@
         compiler_params=params("arbitrary"),
         name="scan_back",
     )(
-        perm, hid_all, dy, mixed, conv_in, conv_sum, raw, step_c, log_c, step_r, log_r, starts,
+        perm, bits, hid, dy, mixed, conv_in, conv_sum, raw, step_c, log_c, step_r, log_r, starts,
         conv_mine, head_mine, seg_col, seg_row,
     )
-    value_shard = lax.psum_scatter(value_in_grad, "dp", scatter_dimension=0, tiled=True)
     dbc_total = sum_ctx(dbc)
-
-    hidden_part = pl.pallas_call(
+    if near:
+        late_came = swap(late_send, "dp", 1)
+        early_parts = pl.pallas_call(
+            pair_sum_kernel,
+            in_specs=[smem, vmem, vmem],
+            out_shape=[[shape_of(early_rows, width, dtype=BF16)] * high],
+            compiler_params=params(),
+            name="pair_sum_early",
+        )(bits, early_keep, early_came)[0]
+        early_parts = spread_dp(early_parts)
+
+    hidden_part, gain_sum = pl.pallas_call(
         hidden_back_kernel,
         grid_spec=pltpu.PrefetchScalarGridSpec(
             num_scalar_prefetch=1,
@@ -806,92 +1184,156 @@
                 full((model, width)),
                 full((model, width)),
                 full((heads, model)),
+                rows(model),
+                full((1, model)),
             ],
-            out_specs=[slot_rows],
+            out_specs=[slot_rows, full((8, model))],
         ),
-        out_shape=[shape_of(nctx, span, model, dtype=BF16)],
+        out_shape=[shape_of(nctx, span, model, dtype=BF16), shape_of(8, model)],
         compiler_params=params("arbitrary"),
         name="hidden_back",
-    )(perm, dgate, dval, dstep, wg, w1, dt_mine)[0]
+    )(perm, dgate, dval, dstep, wg, w1, dt_mine, hid, gain_pre)
     hidden_grad = scatter_ctx(hidden_part)
 
-    hid_order = jnp.concatenate(
-        [lax.dynamic_index_in_dim(hid_all, perm[at], 0, keepdims=False) for at in range(nctx)]
-    )
-    dmap, map_conv_grad, map_in_grad = pl.pallas_call(
+    map_rows = 32 + 32 * high
+    map_keep, map_send, hidden_own = pl.pallas_call(
         maps_back_kernel,
+        in_specs=[smem] + [vmem] * 13,
         out_shape=[
-            shape_of(length, maps, dtype=BF16),
-            shape_of(8, maps),
-            shape_of(model, maps, dtype=BF16),
+            shape_of(map_rows, width, dtype=BF16),
+            shape_of(map_rows, width, dtype=BF16),
+            shape_of(span, model),
         ],
-        scratch_shapes=[pltpu.VMEM((length + 8, maps), F32)],
+        scratch_shapes=[
+            pltpu.VMEM((length + 8, maps), F32),
+            pltpu.VMEM((model, maps), F32),
+            pltpu.VMEM((length, maps), BF16),
+            pltpu.VMEM((32, width), F32),
+        ],
         compiler_params=params(),
         name="maps_back",
-    )(dbc_total, conv_sum[:, width:], conv_in[:, width:], conv_mine[:, width:], seg_col, hid_order)
-    map_rows = rows_in // nctx
-    map_part = lax.dynamic_index_in_dim(
-        map_in_grad.reshape(ndp, nctx, map_rows, maps), c, 1, keepdims=False
+    )(
+        bits,
+        dbc_total,
+        conv_sum[:, width:],
+        conv_in[:, width:],
+        conv_mine[:, width:],
+        seg_col,
+        hid,
+        w1,
+        gain_pre,
+        conv_grad,
+        col_sums,
+        head_grad,
+        dt_grad,
+        gain_sum,
     )
-    map_shard = lax.psum_scatter(map_part, "dp", scatter_dimension=0, tiled=True)[0]
-
-    input_grad, gain_sum = pl.pallas_call(
+
+    input_grad = pl.pallas_call(
         input_back_kernel,
-        out_shape=[shape_of(span, model), shape_of(8, model)],
+        out_shape=shape_of(span, model),
         compiler_params=params(),
         name="input_back",
-    )(
-        hidden_grad,
-        lax.dynamic_slice_in_dim(dmap, c * span, span, 0),
-        w1[:, width:],
-        tok,
-        gain_pre,
-        cotangent[0],
-    )
-
-    def row_block(value):
-        return jnp.pad(value, ((0, 0), (0, width - value.shape[1])))
-
-    half = model // width
-    packed = jnp.concatenate(
-        [conv_grad, col_sums, row_block(map_conv_grad), row_block(head_grad)]
-        + [dt_grad[:, at * width : (at + 1) * width] for at in range(half)]
-        + [gain_sum[:, at * width : (at + 1) * width] for at in range(half)]
-    )
-    packed = lax.all_gather(lax.psum(packed, "dp"), "ctx", axis=0)
-    conv_total = jnp.concatenate(
-        [packed[at, : CONV + 1] for at in range(nctx)] + [packed[0, 16 : 16 + CONV + 1, :maps]], axis=1
-    )
+    )(hidden_grad, hidden_own, tok, gain_pre, cotangent[0])
+
+    late_rows = block_in + 64
+    if near:
+        map_came = swap(map_send, "dp", 1)
+        late_parts = pl.pallas_call(
+            pair_sum_late_kernel,
+            in_specs=[smem] + [vmem] * 4,
+            out_shape=[[shape_of(late_rows, width, dtype=BF16)] * high],
+            compiler_params=params(),
+            name="pair_sum_late",
+        )(bits, late_keep, late_came, map_keep, map_came)[0]
+        late_parts = spread_dp(late_parts)
+        early, late = [
+            pl.pallas_call(
+                functools.partial(sum_kernel, name == "late"),
+                in_specs=[[vmem] * high],
+                out_shape=shape_of(*parts[0].shape, dtype=BF16),
+                compiler_params=params(),
+                name="sum_" + name,
+            )(parts)
+            for name, parts in (("early", early_parts), ("late", late_parts))
+        ]
+        early, late = fan_ctx(early), fan_ctx(late)
+        row_block = lambda ref_rows, cols: pl.BlockSpec((ref_rows, cols), lambda i, *_: (i, 0))
+        in_block = row_block(rows_in // nctx, in_weight.shape[1])
+        out_block = row_block(out_weight.shape[0] // nctx, model)
+        news = pl.pallas_call(
+            adam_kernel,
+            grid_spec=pltpu.PrefetchScalarGridSpec(
+                num_scalar_prefetch=1,
+                grid=(nctx,),
+                in_specs=[in_block] * 3
+                + [out_block] * 3
+                + [[full((early_rows, width))] * nctx, [full((late_rows, width))] * nctx],
+                out_specs=[in_block] * 3 + [out_block] * 3,
+                scratch_shapes=[
+                    pltpu.VMEM((nctx, early_rows, width), BF16),
+                    pltpu.VMEM((nctx, late_rows, width), BF16),
+                ],
+            ),
+            out_shape=[shape_of(*in_weight.shape)] * 3 + [shape_of(*out_weight.shape)] * 3,
+            compiler_params=params("arbitrary"),
+            name="adam",
+        )(bits, in_weight, in_first, in_second, out_weight, out_first, out_second, early, late)
+        in_new, out_new = tuple(news[:3]), tuple(news[3:])
+        small = jnp.stack([part[block_in : block_in + 32] for part in late])[c ^ jnp.arange(nctx)]
+        small = small.astype(F32)
+    else:
+        blocks = lambda keep, send: jnp.stack([keep, send], axis=1).reshape((heads,) + keep.shape[1:])
+        early = blocks(early_keep, early_send).astype(F32)
+        late = blocks(late_keep, late_send).astype(F32)
+        part = lambda value: value[32:].reshape(high, 32, width)[:, :, :maps]
+        map_blocks = blocks(part(map_keep), part(map_send)).astype(F32)
+
+        def total(value):
+            return lax.psum_scatter(value, "dp", scatter_dimension=0, tiled=True)
+
+        def spaced(value):
+            place_at = (jnp.arange(nctx) == c).astype(F32).reshape((1, nctx, 1, 1))
+            value = value[:, None] * place_at
+            return lax.psum(total(value.reshape(-1, value.shape[-1])), "ctx")
+
+        def by_head(value):
+            value = lax.all_gather(total(value.reshape(model, width)), "ctx", axis=0)
+            value = value.reshape(nctx, rows_in, heads, HEAD_DIM)
+            return jnp.transpose(value, (1, 2, 0, 3)).reshape(rows_in, INNER)
+
+        in_total = jnp.concatenate(
+            [by_head(early[:, :block_in]), by_head(late), spaced(map_blocks)], axis=1
+        )
+        out_total = spaced(
+            jnp.concatenate([early[:, block_in : block_in + HEAD_DIM], early[:, block_in + HEAD_DIM :]], axis=2)
+        )
+        in_new = adam_step(in_weight, in_first, in_second, in_total, 0.03, WEIGHT_DECAY)
+        out_new = adam_step(out_weight, out_first, out_second, out_total, 0.02, WEIGHT_DECAY)
+        small = lax.all_gather(lax.psum(map_keep[:32].astype(F32), "dp"), "ctx", axis=0)
+
+    def in_order(value):
+        return jnp.swapaxes(value.reshape(nctx, -1, heads, HEAD_DIM), 0, 1).swapaxes(1, 2).reshape(-1, INNER)
+
+    columns = in_order(small[:, : CONV + 2])
+    conv_total = jnp.concatenate([columns[: CONV + 1], small[0, 8 : 8 + CONV + 1, :maps]], axis=1)
     conv_total = lax.dynamic_slice_in_dim(conv_total, d * conv_cols, conv_cols, 1)
-    dt_total = jnp.concatenate(
-        [packed[:, 32 + 8 * at : 40 + 8 * at].reshape(HEADS, width) for at in range(half)], axis=1
-    )
+    dt_total = small[:, 16:32].reshape(nctx, 2, heads, width)
+    dt_total = jnp.transpose(dt_total, (2, 0, 1, 3)).reshape(HEADS, model)
     dt_total = lax.dynamic_slice_in_dim(dt_total, d * dt_cols, dt_cols, 1)
-    first_gain = 32 + 8 * half
-    pre_total = [
-        jnp.sum(packed[:, first_gain + 8 * at], axis=0) for at in range(half)
-    ]
-    gain_total = jnp.concatenate(pre_total + [packed[:, 8].reshape(-1)])
+    pre_total = jnp.sum(small[:, 13:15], axis=0).reshape(-1)
+    gain_total = jnp.concatenate([pre_total, columns[CONV + 1]])
     gain_total = lax.dynamic_slice_in_dim(gain_total, d * gain_len, gain_len, 0)
+    head_row = small[:, 7] + small[:, 15]
     head_total = jnp.stack(
         [
-            packed[:, 24, :heads].reshape(-1),
-            packed[:, 25, :heads].reshape(-1),
-            jnp.sum(packed[:, 9].reshape(HEADS, HEAD_DIM), axis=1),
+            head_row[:, :heads].T.reshape(-1),
+            head_row[:, 128 : 128 + heads].T.reshape(-1),
+            jnp.sum(small[:, CONV + 2].reshape(nctx, heads, HEAD_DIM), axis=2).T.reshape(-1),
         ]
     )
 
-    columns = lax.all_gather(jnp.stack([gate_shard, value_shard]).astype(BF16), "ctx", axis=0)
-    map_total = lax.all_gather(map_shard.astype(BF16), "ctx", axis=0, tiled=True)
-    in_total = jnp.concatenate(
-        [columns[at, 0] for at in range(nctx)] + [columns[at, 1] for at in range(nctx)] + [map_total],
-        axis=1,
-    ).astype(F32)
-    out_total = lax.all_gather(out_shard.astype(BF16), "ctx", axis=1, tiled=True).astype(F32)
-
-    in_new = adam_step(in_weight, in_first, in_second, in_total, 0.03, WEIGHT_DECAY)
     dt_new = adam_step(dt_weight, dt_first, dt_second, dt_total, 0.03, WEIGHT_DECAY)
-    out_new = adam_step(out_weight, out_first, out_second, out_total, 0.02, WEIGHT_DECAY)
     conv_new = adam_step(conv_params, conv_first, conv_second, conv_total, 0.3, 0.0)
     gain_new = adam_step(gains, gain_first, gain_second, gain_total, 0.5, 0.0)
     head_new = adam_step(head_params, head_first, head_second, head_total, 2.0, 0.0)

time: 607 us -> 258 us (0.43)
  waiting for transfers between devices: 357 us -> 59.3 us
  blocking collectives: 53.1 us -> 0 us
  starting transfers between devices: 17.3 us -> 54.6 us
  Pallas kernels: 79.6 us -> 107 us
  other arithmetic: 37.3 us -> 13.2 us
  between operations: 22.2 us -> 1.44 us
  local copies, waits for them, and re-layouts: 38.7 us -> 21.7 us
    reduce_scatter x4 -> x0, waiting for transfers between devices: 200 us -> none  [the longest x1 65.8 us: shards(): lax.psum_scatter(gate_in_grad, 'dp', scatter_dimension=0, tiled=True)]
    psum x1 -> x0, waiting for transfers between devices: 64.7 us -> none  [shards(): packed = lax.all_gather(lax.psum(packed, 'dp'), 'ctx', axis=0)]
    all_gather x4 -> x0, blocking collectives: 53.1 us -> none  [the longest x1 33 us: shards(): small_all = lax.all_gather(small, 'dp', axis=0)]
    ppermute x12 -> x44, starting transfers between devices: 9.14 us -> 54.6 us  [swap(): return lax.ppermute(value, axis, [(at, at ^ bit) for at in range(count)])]
    all_gather x4 -> x0, waiting for transfers between devices: 44 us -> none  [the longest x1 26.8 us: shards(): lax.all_gather(lax.dynamic_slice_in_dim(in_weight, c * width, width, 1).a...]
    ppermute x12 -> x44, waiting for transfers between devices: 34.8 us -> 59.3 us  [swap(): return lax.ppermute(value, axis, [(at, at ^ bit) for at in range(count)])]
    pallas_call x3 -> x8, Pallas kernels: 11.7 us -> 32.7 us  [the longest x1 9.97 us: shards(): pl.pallas_call(adam_kernel, grid_spec=pltpu.PrefetchScalarGridSpec(num_sc...]
    all_to_all x2 -> x0, waiting for transfers between devices: 12.8 us -> none  [the longest x1 10.2 us: shards(): lax.all_to_all(out_grad, 'ctx', split_axis=1, concat_axis=0, tiled=True)]
  transfers between devices with their start and end apart: 23 -> 44, of which waited for: 16 -> 16; matrix products, arithmetic and copies ran while one was open for 10% -> 11% of each run, Pallas kernels for 6% -> 28%
where the time goes in v3:
time: 258 us; the launch traced here: 257 us
  Pallas kernels  107 us (41%)
  waiting for transfers between devices  59.3 us (23%)
  starting transfers between devices  54.6 us (21%)
  local copies, waits for them, and re-layouts  21.7 us (8%)
  other arithmetic  13.2 us (5%)
    ppermute x44, waiting for transfers between devices, swap(): return lax.ppermute(value, axis, [(at, at ^ bit) for at in range(count)])  59.3 us
    ppermute x44, starting transfers between devices, swap(): return lax.ppermute(value, axis, [(at, at ^ bit) for at in range(count)])  54.6 us
    pallas_call x1, Pallas kernels, shards(): pl.pallas_call(scan_back_kernel, grid_spec=pltpu.PrefetchScalarGridSpec(n...  21.7 us
    pallas_call x1, Pallas kernels, shards(): pl.pallas_call(scan_forward_kernel, grid_spec=pltpu.PrefetchScalarGridSpe...  18.5 us
    pallas_call x1, Pallas kernels, shards(): pl.pallas_call(norm_back_kernel, grid_spec=pltpu.PrefetchScalarGridSpec(n...  13.5 us
    pallas_call x1, Pallas kernels, shards(): pl.pallas_call(gate_kernel, grid_spec=pltpu.PrefetchScalarGridSpec(num_sc...  12.3 us
    pallas_call x1, Pallas kernels, shards(): pl.pallas_call(adam_kernel, grid_spec=pltpu.PrefetchScalarGridSpec(num_sc...  9.97 us
    pallas_call x1, Pallas kernels, shards(): pl.pallas_call(hidden_back_kernel, grid_spec=pltpu.PrefetchScalarGridSpec...  7.9 us
  transfers between devices with their start and end apart: 44, of which 16 were waited for; matrix products, arithmetic and copies ran while one was open for 11% of the time, Pallas kernels for 28%

profile of v3, /device:TPU:0, one launch (start us, length us, event | category | flops | bytes accessed | tf_op | source)
XLA Modules:
  0.0 256.7 jit_solution(15171549360029658086)
XLA Ops:
  0.7 3.0 %collective-permute-start.1 = (f32[256,1024]{1,0:T(8,128)}, f32[256,1024]{1,0:T(8,128)S(1)}, u32[]{:S(2)}, u32[]{:S(2)}) collective-permute-start(f32[256,1024]{1,0:T(8,128)} %bitcast.61), channel_id=1, source_target_pairs={{0,2},{1,3},{2,0},{3,1},{4,6},{5,7},{6,4},{7,5},{8,10},{9,11},{10,... | collective-permute-start | bytes 3145736 | tf_op jit(solution)/shard_map/ppermute | solution.py:825
  3.7 1.2 broadcast_in_dim.20.gain_ref
  5.5 3.5 %pack.1 = (bf16[144,768]{1,0:T(8,128)(2,1)}, bf16[256,512]{1,0:T(8,128)(2,1)}, bf16[256,1024]{1,0:T(8,128)(2,1)}) custom-call(s32[3]{0:T(128)} %pad_add_fusion.here_ref, f32[128,4352]{1,0:T(8,128)} %win_ref.3, f32[256,1024]{1,0:T(8,128)} %oin_ref.1, f32[32,128]{1,0:T(8,128)} %dt_ref.1, f32[5,288]{1,0:T(8,128)} %conv_ref.1, ...), custom_call_target="tpu_custom_call" | custom-call | tf_op jit(solution)/shard_map/pack/pallas_call | solution.py:928
  9.0 1.6 collective-permute-start.3
  10.6 2.6 %collective-permute-start.4 = (bf16[1,144,768]{2,1,0:T(8,128)(2,1)}, bf16[1,144,768]{2,1,0:T(8,128)(2,1)S(1)}, u32[]{:S(2)}, u32[]{:S(2)}) collective-permute-start(bf16[1,144,768]{2,1,0:T(8,128)(2,1)} %bitcast.77), channel_id=1, source_target_pairs={{0,16},{4,20},{8,24},{12,28},{16,0},{20,4},{24,8},{28,12},{1,17},{... | collective-permute-start | bytes 663560 | tf_op jit(solution)/shard_map/ppermute | solution.py:825
  13.4 13.7 %collective-permute-done.1.tok_pieces_2_ = f32[256,1024]{1,0:T(8,128)S(1)} collective-permute-done((f32[256,1024]{1,0:T(8,128)}, f32[256,1024]{1,0:T(8,128)S(1)}, u32[]{:S(2)}, u32[]{:S(2)}) %collective-permute-start.1) | collective-permute-done | bytes 1048608 | tf_op jit(solution)/shard_map/ppermute | solution.py:825
  27.1 1.9 collective-permute-start.10
  29.5 2.0 collective-permute-start.11
  31.5 1.5 collective-permute-start.6
  33.0 5.9 %collective-permute-done.6.w1_pieces_4_ = bf16[1,144,768]{2,1,0:T(8,128)(2,1)S(1)} collective-permute-done((bf16[1,144,768]{2,1,0:T(8,128)(2,1)}, bf16[1,144,768]{2,1,0:T(8,128)(2,1)S(1)}, u32[]{:S(2)}, u32[]{:S(2)}) %collective-permute-start.6) | collective-permute-done | bytes 221216 | tf_op jit(solution)/shard_map/ppermute | solution.py:825
  39.7 1.5 collective-permute-start.18
  41.5 2.7 %collective-permute-start.12 = (bf16[1,256,512]{2,1,0:T(8,128)(2,1)}, bf16[1,256,512]{2,1,0:T(8,128)(2,1)}, u32[]{:S(2)}, u32[]{:S(2)}) collective-permute-start(bf16[1,256,512]{2,1,0:T(8,128)(2,1)} %bitcast.73), channel_id=1, source_target_pairs={{0,24},{4,28},{8,16},{12,20},{16,8},{20,12},{24,0},{28,4},{1,25},{... | collective-permute-start | bytes 786440 | tf_op jit(solution)/shard_map/ppermute | solution.py:825
  44.3 1.5 collective-permute-start.13
  45.8 6.0 %collective-permute-done.12.g2_pieces_3_ = bf16[1,256,512]{2,1,0:T(8,128)(2,1)} collective-permute-done((bf16[1,256,512]{2,1,0:T(8,128)(2,1)}, bf16[1,256,512]{2,1,0:T(8,128)(2,1)}, u32[]{:S(2)}, u32[]{:S(2)}) %collective-permute-start.12) | collective-permute-done | bytes 262176 | tf_op jit(solution)/shard_map/ppermute | solution.py:825
  51.8 1.6 collective-permute-start.7
  53.8 6.3 %collective-permute-done.7.w1_pieces_5_ = bf16[1,144,768]{2,1,0:T(8,128)(2,1)S(1)} collective-permute-done((bf16[1,144,768]{2,1,0:T(8,128)(2,1)S(1)}, bf16[1,144,768]{2,1,0:T(8,128)(2,1)S(1)}, u32[]{:S(2)}, u32[]{:S(2)}) %collective-permute-start.7) | collective-permute-done | bytes 221216 | tf_op jit(solution)/shard_map/ppermute | solution.py:825
  60.2 1.6 collective-permute-start.9
  61.8 3.1 %collective-permute-done.8.w1_pieces_6_ = bf16[1,144,768]{2,1,0:T(8,128)(2,1)S(1)} collective-permute-done((bf16[1,144,768]{2,1,0:T(8,128)(2,1)S(1)}, bf16[1,144,768]{2,1,0:T(8,128)(2,1)S(1)}, u32[]{:S(2)}, u32[]{:S(2)}) %collective-permute-start.8) | collective-permute-done | bytes 221216 | tf_op jit(solution)/shard_map/ppermute | solution.py:825
  65.4 2.1 collective-permute-done.9.w1_pieces_7_
  67.5 1.6 collective-permute-start.14
  69.5 1.0 copy-done.9
  70.5 1.6 collective-permute-start.16
  73.1 1.0 broadcast_in_dim.26.segc_ref
  74.7 18.5 %scan_forward.1 = (bf16[1024,1024]{1,0:T(8,128)(2,1)}, f32[8,768]{1,0:T(8,128)}, f32[1,1024]{1,0:T(1,128)}, f32[1,512]{1,0:T(1,128)}, bf16[8,1024]{1,0:T(8,128)(...) custom-call(s32[3]{0:T(128)} %pad_add_fusion.here_ref, ...), custom_call_target="tpu_custom_call" | custom-call | tf_op jit(solution)/shard_map/scan_forward/pallas_call | solution.py:966
  94.0 12.3 %gate.1 = (bf16[1024,512]{1,0:T(8,128)(2,1)}, bf16[512,1024]{1,0:T(8,128)(2,1)}, bf16[4,256,1024]{2,1,0:T(8,128)(2,1)}, bf16[1024,512]{1,0:T(8,128)(2,1)}, f32[1024,512]{1,0:T(8,128)}, /*index=5*/f32[8,1024]{1,0:T(8,128)}) custom-call(s32[3]{0:T(128)} %pad_add_fusion.here_ref, s32[8]{0:T(128)} %broadcast_xor_fusion.at_ref, ...), custom_call_target="tpu_custom_call" | custom-call | tf_op jit(solution)/shard_map/gate/pallas_call | solution.py:1031
  106.4 1.6 collective-permute-start.21
  108.3 1.1 gather_fusion
  109.4 1.2 collective-permute-done.21
  110.6 1.0 collective-permute-done.22
  111.5 1.4 add_add_fusion.stat_ref
  112.9 13.5 %norm_back.1 = (bf16[4,256,1024]{2,1,0:T(8,128)(2,1)}, bf16[4,256,512]{2,1,0:T(8,128)(2,1)}, bf16[4,256,512]{2,1,0:T(8,128)(2,1)}, f32[1024,512]{1,0:T(8,128)}, ...) custom-call(s32[4]{0:T(128)} %gather_fusion, s32[3]{0:T(128)} %pad_add_fusion.here_ref, ...), custom_call_target="tpu_custom_call" | custom-call | tf_op jit(solution)/shard_map/norm_back/pallas_call | solution.py:1064
  127.0 21.7 %scan_back.1 = (bf16[4,128,512]{2,1,0:T(8,128)(2,1)}, bf16[4,128,512]{2,1,0:T(8,128)(2,1)}, bf16[1024,512]{1,0:T(8,128)(2,1)}, bf16[1024,256]{1,0:T(8,128)(2,1)}...) custom-call(s32[4]{0:T(128)} %gather_fusion, s32[3]{0:T(128)} %pad_add_fusion.here_ref, ...), custom_call_target="tpu_custom_call" | custom-call | tf_op jit(solution)/shard_map/scan_back/pallas_call | solution.py:1107
  148.7 7.9 %hidden_back.1 = (bf16[4,256,1024]{2,1,0:T(8,128)(2,1)}, f32[8,1024]{1,0:T(8,128)}) custom-call(s32[4]{0:T(128)} %gather_fusion, bf16[1024,512]{1,0:T(8,128)(2,1)} %get-tuple-element.91.dgate_ref, bf16[1024,512]{1,0:T(8,128)(2,1)} %get-tuple-element.102.dval_ref, bf16[1024,8]{1,0:T(8,128)(2,1)} %get-tuple-element.103.dstep_ref, ...), custom_call_target="tpu_custom_call" | custom-call | tf_op jit(solution)/shard_map/hidden_back/pallas_call | solution.py:1175
  156.6 1.4 slice.89
  158.5 2.3 slice.92.convsum_ref
  160.8 1.9 slice.93.convin_ref
  162.7 1.3 slice.94.conv_ref
  164.0 1.5 collective-permute-start.36
  166.8 1.0 copy-done.10
  167.7 2.7 %pair_sum_early.1 = (bf16[256,512]{1,0:T(8,128)(2,1)}, bf16[256,512]{1,0:T(8,128)(2,1)}, bf16[256,512]{1,0:T(8,128)(2,1)}, bf16[256,512]{1,0:T(8,128)(2,1)}) custom-call(s32[3]{0:T(128)} %pad_add_fusion.here_ref, bf16[4,256,512]{2,1,0:T(8,128)(2,1)} %get-tuple-element.116.keep_ref, bf16[4,256,512]{2,1,0:T(8,128)(2,1)} %copy-done.10), custom_call_target="tpu_custom_call" | custom-call | tf_op jit(solution)/shard_map/pair_sum_early/pallas_call | solution.py:1166
  170.4 4.7 %collective-permute-start.30 = (bf16[256,512]{1,0:T(8,128)(2,1)}, bf16[256,512]{1,0:T(8,128)(2,1)S(1)}, u32[]{:S(2)}, u32[]{:S(2)}) collective-permute-start(bf16[256,512]{1,0:T(8,128)(2,1)} %get-tuple-element.119), channel_id=1, source_target_pairs={{0,8},{4,12},{8,0},{12,4},{16,24},{20,28},{24,16},{28,20},{1,9},{5... | collective-permute-start | bytes 786440 | tf_op jit(solution)/shard_map/ppermute | solution.py:825
  176.1 1.6 convert_add_fusion
  177.7 1.3 copy-done.3
  181.2 2.1 convert_add_fusion.2.dbc_ref
  183.3 6.4 %maps_back.1 = (bf16[160,512]{1,0:T(8,128)(2,1)}, bf16[160,512]{1,0:T(8,128)(2,1)}, f32[256,1024]{1,0:T(8,128)}) custom-call(s32[3]{0:T(128)} %pad_add_fusion.here_ref, f32[1024,256]{1,0:T(8,128)} %convert_add_fusion.2.dbc_ref, f32[1024,256]{1,0:T(8,128)} %slice.92.convsum_ref, bf16[1024,256]{1,0:T(8,128)(2,1)} %slice.93.convin_ref, ...), custom_call_target="tpu_custom_call" | custom-call | tf_op jit(solution)/shard_map/maps_back/pallas_call | solution.py:1199
  190.2 1.6 convert_add_fusion.1
  191.9 2.6 %collective-permute-start.32 = (bf16[256,512]{1,0:T(8,128)(2,1)S(1)}, bf16[256,512]{1,0:T(8,128)(2,1)S(1)}, u32[]{:S(2)}, u32[]{:S(2)}) collective-permute-start(bf16[256,512]{1,0:T(8,128)(2,1)S(1)} %copy-done.45), channel_id=1, source_target_pairs={{0,24},{4,28},{8,16},{12,20},{16,8},{20,12},{24,0},{28,4},{1,25},{... | collective-permute-start | bytes 786440 | tf_op jit(solution)/shard_map/ppermute | solution.py:825
  194.5 1.1 collective-permute-done.37.mcame_ref
  196.3 2.3 pair_sum_late.1
  198.6 4.6 %collective-permute-start.38 = (bf16[192,512]{1,0:T(8,128)(2,1)}, bf16[192,512]{1,0:T(8,128)(2,1)}, u32[]{:S(2)}, u32[]{:S(2)}) collective-permute-start(bf16[192,512]{1,0:T(8,128)(2,1)} %get-tuple-element.127), channel_id=1, source_target_pairs={{0,8},{4,12},{8,0},{12,4},{16,24},{20,28},{24,16},{28,20},{1,9},{5... | collective-permute-start | bytes 589832 | tf_op jit(solution)/shard_map/ppermute | solution.py:825
  204.2 1.5 collective-permute-start.40
  207.2 1.3 collective-permute-start.24
  208.5 2.2 sum_early.1.early_refs_0_
  210.7 9.3 %collective-permute-done.39.part_refs_2_ = bf16[192,512]{1,0:T(8,128)(2,1)} collective-permute-done((bf16[192,512]{1,0:T(8,128)(2,1)}, bf16[192,512]{1,0:T(8,128)(2,1)}, u32[]{:S(2)}, u32[]{:S(2)}) %collective-permute-start.39) | collective-permute-done | bytes 196640 | tf_op jit(solution)/shard_map/ppermute | solution.py:825
  220.0 1.2 collective-permute-start.34
  221.2 2.0 sum_late.1.late_refs_0_
  224.0 1.7 collective-permute-start.43
  225.7 1.2 fusion.hg_ref
  226.9 3.7 %input_back.1 = f32[256,1024]{1,0:T(8,128)} custom-call(f32[256,1024]{1,0:T(8,128)} %fusion.hg_ref, f32[256,1024]{1,0:T(8,128)} %get-tuple-element.115.own_ref, f32[256,1024]{1,0:T(8,128)} %bitcast.63, f32[1,1024]{1,0:T(1,128)} %get-tuple-element.107.gain_ref, f32[256,1024]{1,0:T(8,128)} %bitcast.66), custom_call_target="tpu_custom_call" | custom-call | tf_op jit(solution)/shard_map/input_back/pallas_call | solution.py:1232
  231.4 1.2 fusion.3
  232.7 5.4 %collective-permute-done.43.late_refs_3_ = bf16[192,512]{1,0:T(8,128)(2,1)S(1)} collective-permute-done((bf16[192,512]{1,0:T(8,128)(2,1)}, bf16[192,512]{1,0:T(8,128)(2,1)S(1)}, u32[]{:S(2)}, u32[]{:S(2)}) %collective-permute-start.43) | collective-permute-done | bytes 196640 | tf_op jit(solution)/shard_map/ppermute | solution.py:825
  238.1 1.0 collective-permute-start.41
  239.1 2.7 %collective-permute-done.42.late_refs_2_ = bf16[192,512]{1,0:T(8,128)(2,1)S(1)} collective-permute-done((bf16[192,512]{1,0:T(8,128)(2,1)S(1)}, bf16[192,512]{1,0:T(8,128)(2,1)S(1)}, u32[]{:S(2)}, u32[]{:S(2)}) %collective-permute-start.42) | collective-permute-done | bytes 196640 | tf_op jit(solution)/shard_map/ppermute | solution.py:825
  246.6 10.0 %adam.1 = (f32[128,4352]{1,0:T(8,128)}, f32[128,4352]{1,0:T(8,128)}, f32[128,4352]{1,0:T(8,128)}, f32[256,1024]{1,0:T(8,128)}, f32[256,1024]{1,0:T(8,128)}, /*index=5*/f32[256,1024]{1,0:T(8,128)}) custom-call(s32[3]{0:T(128)} %pad_add_fusion.here_ref, f32[128,4352]{1,0:T(8,128)} %win_ref.3, f32[128,4352]{1,0:T(8,128)} %wfirst_ref.1, ...), custom_call_target="tpu_custom_call" | custom-call | tf_op jit(solution)/shard_map/adam/pallas_call | solution.py:1264
  (193 shorter events, 22.0 us)
Async XLA Ops:
  0.7 26.4 %collective-permute-start.1 = (f32[256,1024]{1,0:T(8,128)}, f32[256,1024]{1,0:T(8,128)S(1)}, u32[]{:S(2)}, u32[]{:S(2)}) collective-permute-start(f32[256,1024]{1,0:T(8,128)} %bitcast.61), channel_id=1, source_target_pairs={{0,2},{1,3},{2,0},{3,1},{4,6},{5,7},{6,4},{7,5},{8,10},{9,11},{10,... | collective-permute-start | bytes 3145736 | tf_op jit(solution)/shard_map/ppermute | solution.py:825
  5.5 66.6 %copy-start.39 = (f32[3,32]{1,0:T(4,128)S(1)}, f32[3,32]{1,0:T(4,128)}, u32[]{:S(2)}) copy-start(f32[3,32]{1,0:T(4,128)} %param.32) | copy-start | bytes 1156
  5.5 67.6 %copy-start.33 = (s32[1,1024]{1,0:T(1,128)S(1)}, s32[1,1024]{1,0:T(1,128)}, u32[]{:S(2)}) copy-start(s32[1,1024]{1,0:T(1,128)} %segr_ref.3) | copy-start | bytes 12292
  5.5 68.7 %copy-start.46 = (s32[8]{0:T(128)S(1)}, s32[8]{0:T(128)}, u32[]{:S(2)}) copy-start(s32[8]{0:T(128)} %constant.53.clone) | copy-start | bytes 100
  9.0 18.1 %collective-permute-start.3 = (bf16[1,144,768]{2,1,0:T(8,128)(2,1)}, bf16[1,144,768]{2,1,0:T(8,128)(2,1)S(1)}, u32[]{:S(2)}, u32[]{:S(2)}) collective-permute-start(bf16[1,144,768]{2,1,0:T(8,128)(2,1)} %bitcast.76), channel_id=1, source_target_pairs={{0,8},{4,12},{8,0},{12,4},{16,24},{20,28},{24,16},{28,20},{1,9},{5... | collective-permute-start | bytes 663560 | tf_op jit(solution)/shard_map/ppermute | solution.py:825
  10.6 19.0 %collective-permute-start.4 = (bf16[1,144,768]{2,1,0:T(8,128)(2,1)}, bf16[1,144,768]{2,1,0:T(8,128)(2,1)S(1)}, u32[]{:S(2)}, u32[]{:S(2)}) collective-permute-start(bf16[1,144,768]{2,1,0:T(8,128)(2,1)} %bitcast.77), channel_id=1, source_target_pairs={{0,16},{4,20},{8,24},{12,28},{16,0},{20,4},{24,8},{28,12},{1,17},{... | collective-permute-start | bytes 663560 | tf_op jit(solution)/shard_map/ppermute | solution.py:825
  13.2 18.4 %collective-permute-start.5 = (bf16[1,144,768]{2,1,0:T(8,128)(2,1)}, bf16[1,144,768]{2,1,0:T(8,128)(2,1)S(1)}, u32[]{:S(2)}, u32[]{:S(2)}) collective-permute-start(bf16[1,144,768]{2,1,0:T(8,128)(2,1)} %bitcast.78), channel_id=1, source_target_pairs={{0,24},{4,28},{8,16},{12,20},{16,8},{20,12},{24,0},{28,4},{1,25},{... | collective-permute-start | bytes 663560 | tf_op jit(solution)/shard_map/ppermute | solution.py:825
  13.4 55.7 %collective-permute-start = (f32[256,1024]{1,0:T(8,128)S(1)}, f32[256,1024]{1,0:T(8,128)S(1)}, u32[]{:S(2)}, u32[]{:S(2)}) collective-permute-start(f32[256,1024]{1,0:T(8,128)S(1)} %bitcast.64), channel_id=1, source_target_pairs={{0,1},{1,0},{2,3},{3,2},{4,5},{5,4},{6,7},{7,6},{8,9},{9,8},{10,11... | collective-permute-start | bytes 3145736 | tf_op jit(solution)/shard_map/ppermute | solution.py:825
  27.1 47.6 %copy-start.7 = (f32[256,1024]{1,0:T(8,128)}, f32[256,1024]{1,0:T(8,128)S(1)}, u32[]{:S(2)}) copy-start(f32[256,1024]{1,0:T(8,128)S(1)} %collective-permute-done.1.tok_pieces_2_) | copy-start | bytes 3145732
  27.1 42.5 %collective-permute-start.2 = (f32[256,1024]{1,0:T(8,128)S(1)}, f32[256,1024]{1,0:T(8,128)S(1)}, u32[]{:S(2)}, u32[]{:S(2)}) collective-permute-start(f32[256,1024]{1,0:T(8,128)S(1)} %collective-permute-done.1.tok_pieces_2_), channel_id=1, source_target_pairs={{0,1},{1,0},{2,3},{3,2},{4,5},{5,4},{6,7},{7,6},{8,9},{9,8},{10,11... | collective-permute-start | bytes 3145736 | tf_op jit(solution)/shard_map/ppermute | solution.py:825
  27.1 34.7 %copy-start.23 = (bf16[1,144,768]{2,1,0:T(8,128)(2,1)}, bf16[1,144,768]{2,1,0:T(8,128)(2,1)S(1)}, u32[]{:S(2)}) copy-start(bf16[1,144,768]{2,1,0:T(8,128)(2,1)S(1)} %collective-permute-done.3.w1_pieces_1_) | copy-start | bytes 663556
  27.1 14.5 %collective-permute-start.10 = (bf16[1,256,512]{2,1,0:T(8,128)(2,1)}, bf16[1,256,512]{2,1,0:T(8,128)(2,1)S(1)}, u32[]{:S(2)}, u32[]{:S(2)}) collective-permute-start(bf16[1,256,512]{2,1,0:T(8,128)(2,1)} %bitcast.71), channel_id=1, source_target_pairs={{0,8},{4,12},{8,0},{12,4},{16,24},{20,28},{24,16},{28,20},{1,9},{5... | collective-permute-start | bytes 786440 | tf_op jit(solution)/shard_map/ppermute | solution.py:825
  29.5 42.6 %copy-start.24 = (bf16[1,144,768]{2,1,0:T(8,128)(2,1)}, bf16[1,144,768]{2,1,0:T(8,128)(2,1)S(1)}, u32[]{:S(2)}) copy-start(bf16[1,144,768]{2,1,0:T(8,128)(2,1)S(1)} %collective-permute-done.4.w1_pieces_2_) | copy-start | bytes 663556
  29.5 14.7 %collective-permute-start.11 = (bf16[1,256,512]{2,1,0:T(8,128)(2,1)}, bf16[1,256,512]{2,1,0:T(8,128)(2,1)}, u32[]{:S(2)}, u32[]{:S(2)}) collective-permute-start(bf16[1,256,512]{2,1,0:T(8,128)(2,1)} %bitcast.72), channel_id=1, source_target_pairs={{0,16},{4,20},{8,24},{12,28},{16,0},{20,4},{24,8},{28,12},{1,17},{... | collective-permute-start | bytes 786440 | tf_op jit(solution)/shard_map/ppermute | solution.py:825
  31.5 40.6 %copy-start.25 = (bf16[1,144,768]{2,1,0:T(8,128)(2,1)}, bf16[1,144,768]{2,1,0:T(8,128)(2,1)S(1)}, u32[]{:S(2)}) copy-start(bf16[1,144,768]{2,1,0:T(8,128)(2,1)S(1)} %collective-permute-done.5.w1_pieces_3_) | copy-start | bytes 663556
  31.5 7.4 %collective-permute-start.6 = (bf16[1,144,768]{2,1,0:T(8,128)(2,1)}, bf16[1,144,768]{2,1,0:T(8,128)(2,1)S(1)}, u32[]{:S(2)}, u32[]{:S(2)}) collective-permute-start(bf16[1,144,768]{2,1,0:T(8,128)(2,1)} %bitcast.79), channel_id=1, source_target_pairs={{0,4},{4,0},{8,12},{12,8},{16,20},{20,16},{24,28},{28,24},{1,5},{5... | collective-permute-start | bytes 663560 | tf_op jit(solution)/shard_map/ppermute | solution.py:825
  39.7 25.2 %collective-permute-start.18 = (bf16[256,1024]{1,0:T(8,128)(2,1)}, bf16[256,1024]{1,0:T(8,128)(2,1)S(1)}, u32[]{:S(2)}, u32[]{:S(2)}) collective-permute-start(bf16[256,1024]{1,0:T(8,128)(2,1)} %get-tuple-element.82.cot_pieces_0_), channel_id=1, source_target_pairs={{0,2},{1,3},{2,0},{3,1},{4,6},{5,7},{6,4},{7,5},{8,10},{9,11},{10,... | collective-permute-start | bytes 1572872 | tf_op jit(solution)/shard_map/ppermute | solution.py:825
  41.5 51.7 %copy-start.18 = (bf16[1,256,512]{2,1,0:T(8,128)(2,1)}, bf16[1,256,512]{2,1,0:T(8,128)(2,1)S(1)}, u32[]{:S(2)}) copy-start(bf16[1,256,512]{2,1,0:T(8,128)(2,1)S(1)} %collective-permute-done.10.g2_pieces_1_) | copy-start | bytes 786436
  41.5 10.2 %collective-permute-start.12 = (bf16[1,256,512]{2,1,0:T(8,128)(2,1)}, bf16[1,256,512]{2,1,0:T(8,128)(2,1)}, u32[]{:S(2)}, u32[]{:S(2)}) collective-permute-start(bf16[1,256,512]{2,1,0:T(8,128)(2,1)} %bitcast.73), channel_id=1, source_target_pairs={{0,24},{4,28},{8,16},{12,20},{16,8},{20,12},{24,0},{28,4},{1,25},{... | collective-permute-start | bytes 786440 | tf_op jit(solution)/shard_map/ppermute | solution.py:825
  44.3 9.1 %collective-permute-start.13 = (bf16[1,256,512]{2,1,0:T(8,128)(2,1)}, bf16[1,256,512]{2,1,0:T(8,128)(2,1)S(1)}, u32[]{:S(2)}, u32[]{:S(2)}) collective-permute-start(bf16[1,256,512]{2,1,0:T(8,128)(2,1)} %bitcast.74), channel_id=1, source_target_pairs={{0,4},{4,0},{8,12},{12,8},{16,20},{20,16},{24,28},{28,24},{1,5},{5... | collective-permute-start | bytes 786440 | tf_op jit(solution)/shard_map/ppermute | solution.py:825
  51.8 8.4 %collective-permute-start.7 = (bf16[1,144,768]{2,1,0:T(8,128)(2,1)S(1)}, bf16[1,144,768]{2,1,0:T(8,128)(2,1)S(1)}, u32[]{:S(2)}, u32[]{:S(2)}) collective-permute-start(bf16[1,144,768]{2,1,0:T(8,128)(2,1)S(1)} %collective-permute-done.3.w1_pieces_1_), channel_id=1, source_target_pairs={{0,4},{4,0},{8,12},{12,8},{16,20},{20,16},{24,28},{28,24},{1,5},{5... | collective-permute-start | bytes 663560 | tf_op jit(solution)/shard_map/ppermute | solution.py:825
  53.4 11.5 %collective-permute-start.8 = (bf16[1,144,768]{2,1,0:T(8,128)(2,1)S(1)}, bf16[1,144,768]{2,1,0:T(8,128)(2,1)S(1)}, u32[]{:S(2)}, u32[]{:S(2)}) collective-permute-start(bf16[1,144,768]{2,1,0:T(8,128)(2,1)S(1)} %collective-permute-done.4.w1_pieces_2_), channel_id=1, source_target_pairs={{0,4},{4,0},{8,12},{12,8},{16,20},{20,16},{24,28},{28,24},{1,5},{5... | collective-permute-start | bytes 663560 | tf_op jit(solution)/shard_map/ppermute | solution.py:825
  60.1 12.0 %copy-start.27 = (bf16[1,144,768]{2,1,0:T(8,128)(2,1)}, bf16[1,144,768]{2,1,0:T(8,128)(2,1)S(1)}, u32[]{:S(2)}) copy-start(bf16[1,144,768]{2,1,0:T(8,128)(2,1)S(1)} %collective-permute-done.7.w1_pieces_5_) | copy-start | bytes 663556
  60.2 7.4 %collective-permute-start.9 = (bf16[1,144,768]{2,1,0:T(8,128)(2,1)S(1)}, bf16[1,144,768]{2,1,0:T(8,128)(2,1)S(1)}, u32[]{:S(2)}, u32[]{:S(2)}) collective-permute-start(bf16[1,144,768]{2,1,0:T(8,128)(2,1)S(1)} %collective-permute-done.5.w1_pieces_3_), channel_id=1, source_target_pairs={{0,4},{4,0},{8,12},{12,8},{16,20},{20,16},{24,28},{28,24},{1,5},{5... | collective-permute-start | bytes 663560 | tf_op jit(solution)/shard_map/ppermute | solution.py:825
  64.9 28.3 %collective-permute-start.17 = (bf16[256,1024]{1,0:T(8,128)(2,1)}, bf16[256,1024]{1,0:T(8,128)(2,1)S(1)}, u32[]{:S(2)}, u32[]{:S(2)}) collective-permute-start(bf16[256,1024]{1,0:T(8,128)(2,1)} %get-tuple-element.82.cot_pieces_0_), channel_id=1, source_target_pairs={{0,1},{1,0},{2,3},{3,2},{4,5},{5,4},{6,7},{7,6},{8,9},{9,8},{10,11... | collective-permute-start | bytes 1572872 | tf_op jit(solution)/shard_map/ppermute | solution.py:825
  64.9 28.3 %copy-start.12 = (bf16[256,1024]{1,0:T(8,128)(2,1)}, bf16[256,1024]{1,0:T(8,128)(2,1)S(1)}, u32[]{:S(2)}) copy-start(bf16[256,1024]{1,0:T(8,128)(2,1)S(1)} %collective-permute-done.18.cot_pieces_2_) | copy-start | bytes 1572868
  64.9 28.3 %collective-permute-start.19 = (bf16[256,1024]{1,0:T(8,128)(2,1)S(1)}, bf16[256,1024]{1,0:T(8,128)(2,1)}, u32[]{:S(2)}, u32[]{:S(2)}) collective-permute-start(bf16[256,1024]{1,0:T(8,128)(2,1)S(1)} %collective-permute-done.18.cot_pieces_2_), channel_id=1, source_target_pairs={{0,1},{1,0},{2,3},{3,2},{4,5},{5,4},{6,7},{7,6},{8,9},{9,8},{10,11... | collective-permute-start | bytes 1572872 | tf_op jit(solution)/shard_map/ppermute | solution.py:825
  67.5 25.6 %collective-permute-start.14 = (bf16[1,256,512]{2,1,0:T(8,128)(2,1)S(1)}, bf16[1,256,512]{2,1,0:T(8,128)(2,1)}, u32[]{:S(2)}, u32[]{:S(2)}) collective-permute-start(bf16[1,256,512]{2,1,0:T(8,128)(2,1)S(1)} %collective-permute-done.10.g2_pieces_1_), channel_id=1, source_target_pairs={{0,4},{4,0},{8,12},{12,8},{16,20},{20,16},{24,28},{28,24},{1,5},{5... | collective-permute-start | bytes 786440 | tf_op jit(solution)/shard_map/ppermute | solution.py:825
  69.1 24.1 %collective-permute-start.15 = (bf16[1,256,512]{2,1,0:T(8,128)(2,1)}, bf16[1,256,512]{2,1,0:T(8,128)(2,1)}, u32[]{:S(2)}, u32[]{:S(2)}) collective-permute-start(bf16[1,256,512]{2,1,0:T(8,128)(2,1)} %collective-permute-done.11.g2_pieces_2_), channel_id=1, source_target_pairs={{0,4},{4,0},{8,12},{12,8},{16,20},{20,16},{24,28},{28,24},{1,5},{5... | collective-permute-start | bytes 786440 | tf_op jit(solution)/shard_map/ppermute | solution.py:825
  70.5 22.7 %collective-permute-start.16 = (bf16[1,256,512]{2,1,0:T(8,128)(2,1)}, bf16[1,256,512]{2,1,0:T(8,128)(2,1)}, u32[]{:S(2)}, u32[]{:S(2)}) collective-permute-start(bf16[1,256,512]{2,1,0:T(8,128)(2,1)} %collective-permute-done.12.g2_pieces_3_), channel_id=1, source_target_pairs={{0,4},{4,0},{8,12},{12,8},{16,20},{20,16},{24,28},{28,24},{1,5},{5... | collective-permute-start | bytes 786440 | tf_op jit(solution)/shard_map/ppermute | solution.py:825
  94.0 14.3 %copy-start = (s32[4]{0:T(128)S(1)}, s32[4]{0:T(128)}, u32[]{:S(2)}) copy-start(s32[4]{0:T(128)} %constant.52.clone) | copy-start | bytes 52
  106.3 3.1 %collective-permute-start.20 = (f32[8,1024]{1,0:T(8,128)}, f32[8,1024]{1,0:T(8,128)S(1)}, u32[]{:S(2)}, u32[]{:S(2)}) collective-permute-start(f32[8,1024]{1,0:T(8,128)} %get-tuple-element.86), channel_id=1, source_target_pairs={{0,1},{1,0},{2,3},{3,2},{4,5},{5,4},{6,7},{7,6},{8,9},{9,8},{10,11... | collective-permute-start | bytes 98312 | tf_op jit(solution)/shard_map/ppermute | solution.py:825
  106.4 4.2 %collective-permute-start.21 = (f32[8,1024]{1,0:T(8,128)}, f32[8,1024]{1,0:T(8,128)S(1)}, u32[]{:S(2)}, u32[]{:S(2)}) collective-permute-start(f32[8,1024]{1,0:T(8,128)} %get-tuple-element.86), channel_id=1, source_target_pairs={{0,2},{1,3},{2,0},{3,1},{4,6},{5,7},{6,4},{7,5},{8,10},{9,11},{10,... | collective-permute-start | bytes 98312 | tf_op jit(solution)/shard_map/ppermute | solution.py:825
  108.0 3.6 %collective-permute-start.22 = (f32[8,1024]{1,0:T(8,128)}, f32[8,1024]{1,0:T(8,128)S(1)}, u32[]{:S(2)}, u32[]{:S(2)}) collective-permute-start(f32[8,1024]{1,0:T(8,128)} %get-tuple-element.86), channel_id=1, source_target_pairs={{0,3},{1,2},{2,1},{3,0},{4,7},{5,6},{6,5},{7,4},{8,11},{9,10},{10,... | collective-permute-start | bytes 98312 | tf_op jit(solution)/shard_map/ppermute | solution.py:825
  126.4 40.4 %collective-permute-start.29 = (bf16[4,256,512]{2,1,0:T(8,128)(2,1)}, bf16[4,256,512]{2,1,0:T(8,128)(2,1)S(1)}, u32[]{:S(2)}, u32[]{:S(2)}) collective-permute-start(bf16[4,256,512]{2,1,0:T(8,128)(2,1)} %get-tuple-element.117), channel_id=1, source_target_pairs={{0,4},{4,0},{8,12},{12,8},{16,20},{20,16},{24,28},{28,24},{1,5},{5... | collective-permute-start | bytes 3145736 | tf_op jit(solution)/shard_map/ppermute | solution.py:825
  158.0 17.2 %collective-permute-start.25 = (bf16[2,256,1024]{2,1,0:T(8,128)(2,1)S(1)}, bf16[2,256,1024]{2,1,0:T(8,128)(2,1)}, u32[]{:S(2)}, u32[]{:S(2)}) collective-permute-start(bf16[2,256,1024]{2,1,0:T(8,128)(2,1)S(1)} %slice.89), channel_id=1, source_target_pairs={{0,1},{1,0},{2,3},{3,2},{4,5},{5,4},{6,7},{7,6},{8,9},{9,8},{10,11... | collective-permute-start | bytes 3145736 | tf_op jit(solution)/shard_map/ppermute | solution.py:825
  158.0 7.6 %collective-permute-start.27 = (bf16[1024,256]{1,0:T(8,128)(2,1)S(1)}, bf16[1024,256]{1,0:T(8,128)(2,1)S(1)}, u32[]{:S(2)}, u32[]{:S(2)}) collective-permute-start(bf16[1024,256]{1,0:T(8,128)(2,1)S(1)} %copy-done.14), channel_id=1, source_target_pairs={{0,1},{1,0},{2,3},{3,2},{4,5},{5,4},{6,7},{7,6},{8,9},{9,8},{10,11... | collective-permute-start | bytes 1572872 | tf_op jit(solution)/shard_map/ppermute | solution.py:825
  164.0 27.8 %collective-permute-start.36 = (bf16[4,128,512]{2,1,0:T(8,128)(2,1)}, bf16[4,128,512]{2,1,0:T(8,128)(2,1)}, u32[]{:S(2)}, u32[]{:S(2)}) collective-permute-start(bf16[4,128,512]{2,1,0:T(8,128)(2,1)} %get-tuple-element.123), channel_id=1, source_target_pairs={{0,4},{4,0},{8,12},{12,8},{16,20},{20,16},{24,28},{28,24},{1,5},{5... | collective-permute-start | bytes 1572872 | tf_op jit(solution)/shard_map/ppermute | solution.py:825
  165.6 24.1 %collective-permute-start.23 = (bf16[2,256,1024]{2,1,0:T(8,128)(2,1)S(1)}, bf16[2,256,1024]{2,1,0:T(8,128)(2,1)}, u32[]{:S(2)}, u32[]{:S(2)}) collective-permute-start(bf16[2,256,1024]{2,1,0:T(8,128)(2,1)S(1)} %slice.85), channel_id=1, source_target_pairs={{0,1},{1,0},{2,3},{3,2},{4,5},{5,4},{6,7},{7,6},{8,9},{9,8},{10,11... | collective-permute-start | bytes 3145736 | tf_op jit(solution)/shard_map/ppermute | solution.py:825
  165.8 14.5 %collective-permute-start.28 = (bf16[1024,256]{1,0:T(8,128)(2,1)S(1)}, bf16[1024,256]{1,0:T(8,128)(2,1)}, u32[]{:S(2)}, u32[]{:S(2)}) collective-permute-start(bf16[1024,256]{1,0:T(8,128)(2,1)S(1)} %add_convert_fusion), channel_id=1, source_target_pairs={{0,2},{1,3},{2,0},{3,1},{4,6},{5,7},{6,4},{7,5},{8,10},{9,11},{10,... | collective-permute-start | bytes 1572872 | tf_op jit(solution)/shard_map/ppermute | solution.py:825
  170.4 32.8 %collective-permute-start.30 = (bf16[256,512]{1,0:T(8,128)(2,1)}, bf16[256,512]{1,0:T(8,128)(2,1)S(1)}, u32[]{:S(2)}, u32[]{:S(2)}) collective-permute-start(bf16[256,512]{1,0:T(8,128)(2,1)} %get-tuple-element.119), channel_id=1, source_target_pairs={{0,8},{4,12},{8,0},{12,4},{16,24},{20,28},{24,16},{28,20},{1,9},{5... | collective-permute-start | bytes 786440 | tf_op jit(solution)/shard_map/ppermute | solution.py:825
  175.2 29.0 %collective-permute-start.31 = (bf16[256,512]{1,0:T(8,128)(2,1)}, bf16[256,512]{1,0:T(8,128)(2,1)S(1)}, u32[]{:S(2)}, u32[]{:S(2)}) collective-permute-start(bf16[256,512]{1,0:T(8,128)(2,1)} %get-tuple-element.120), channel_id=1, source_target_pairs={{0,16},{4,20},{8,24},{12,28},{16,0},{20,4},{24,8},{28,12},{1,17},{... | collective-permute-start | bytes 786440 | tf_op jit(solution)/shard_map/ppermute | solution.py:825
  180.3 43.6 %collective-permute-start.26 = (bf16[256,1024]{1,0:T(8,128)(2,1)}, bf16[256,1024]{1,0:T(8,128)(2,1)S(1)}, u32[]{:S(2)}, u32[]{:S(2)}) collective-permute-start(bf16[256,1024]{1,0:T(8,128)(2,1)} %fusion.5), channel_id=1, source_target_pairs={{0,2},{1,3},{2,0},{3,1},{4,6},{5,7},{6,4},{7,5},{8,10},{9,11},{10,... | collective-permute-start | bytes 1572872 | tf_op jit(solution)/shard_map/ppermute | solution.py:825
  189.7 5.9 %collective-permute-start.37 = (bf16[160,512]{1,0:T(8,128)(2,1)}, bf16[160,512]{1,0:T(8,128)(2,1)S(1)}, u32[]{:S(2)}, u32[]{:S(2)}) collective-permute-start(bf16[160,512]{1,0:T(8,128)(2,1)} %get-tuple-element.125), channel_id=1, source_target_pairs={{0,4},{4,0},{8,12},{12,8},{16,20},{20,16},{24,28},{28,24},{1,5},{5... | collective-permute-start | bytes 491528 | tf_op jit(solution)/shard_map/ppermute | solution.py:825
  191.9 14.7 %collective-permute-start.32 = (bf16[256,512]{1,0:T(8,128)(2,1)S(1)}, bf16[256,512]{1,0:T(8,128)(2,1)S(1)}, u32[]{:S(2)}, u32[]{:S(2)}) collective-permute-start(bf16[256,512]{1,0:T(8,128)(2,1)S(1)} %copy-done.45), channel_id=1, source_target_pairs={{0,24},{4,28},{8,16},{12,20},{16,8},{20,12},{24,0},{28,4},{1,25},{... | collective-permute-start | bytes 786440 | tf_op jit(solution)/shard_map/ppermute | solution.py:825
  198.6 12.1 %collective-permute-start.38 = (bf16[192,512]{1,0:T(8,128)(2,1)}, bf16[192,512]{1,0:T(8,128)(2,1)}, u32[]{:S(2)}, u32[]{:S(2)}) collective-permute-start(bf16[192,512]{1,0:T(8,128)(2,1)} %get-tuple-element.127), channel_id=1, source_target_pairs={{0,8},{4,12},{8,0},{12,4},{16,24},{20,28},{24,16},{28,20},{1,9},{5... | collective-permute-start | bytes 589832 | tf_op jit(solution)/shard_map/ppermute | solution.py:825
  203.2 16.8 %collective-permute-start.39 = (bf16[192,512]{1,0:T(8,128)(2,1)}, bf16[192,512]{1,0:T(8,128)(2,1)}, u32[]{:S(2)}, u32[]{:S(2)}) collective-permute-start(bf16[192,512]{1,0:T(8,128)(2,1)} %get-tuple-element.128), channel_id=1, source_target_pairs={{0,16},{4,20},{8,24},{12,28},{16,0},{20,4},{24,8},{28,12},{1,17},{... | collective-permute-start | bytes 589832 | tf_op jit(solution)/shard_map/ppermute | solution.py:825
  204.2 17.0 %collective-permute-start.40 = (bf16[192,512]{1,0:T(8,128)(2,1)}, bf16[192,512]{1,0:T(8,128)(2,1)}, u32[]{:S(2)}, u32[]{:S(2)}) collective-permute-start(bf16[192,512]{1,0:T(8,128)(2,1)} %get-tuple-element.129), channel_id=1, source_target_pairs={{0,24},{4,28},{8,16},{12,20},{16,8},{20,12},{24,0},{28,4},{1,25},{... | collective-permute-start | bytes 589832 | tf_op jit(solution)/shard_map/ppermute | solution.py:825
  207.2 23.3 %collective-permute-start.24 = (bf16[256,1024]{1,0:T(8,128)(2,1)}, bf16[256,1024]{1,0:T(8,128)(2,1)S(1)}, u32[]{:S(2)}, u32[]{:S(2)}) collective-permute-start(bf16[256,1024]{1,0:T(8,128)(2,1)} %fusion.4), channel_id=1, source_target_pairs={{0,2},{1,3},{2,0},{3,1},{4,6},{5,7},{6,4},{7,5},{8,10},{9,11},{10,... | collective-permute-start | bytes 1572872 | tf_op jit(solution)/shard_map/ppermute | solution.py:825
  208.5 17.2 %copy-start.4 = (f32[2,256,1024]{2,1,0:T(8,128)S(1)}, f32[2,256,1024]{2,1,0:T(8,128)}, u32[]{:S(2)}) copy-start(f32[2,256,1024]{2,1,0:T(8,128)} %copy-done.3) | copy-start | bytes 6291460
  210.7 35.9 %collective-permute-start.33 = (bf16[256,512]{1,0:T(8,128)(2,1)}, bf16[256,512]{1,0:T(8,128)(2,1)}, u32[]{:S(2)}, u32[]{:S(2)}) collective-permute-start(bf16[256,512]{1,0:T(8,128)(2,1)} %sum_early.1.early_refs_0_), channel_id=1, source_target_pairs={{0,1},{1,0},{2,3},{3,2},{4,5},{5,4},{6,7},{7,6},{8,9},{9,8},{10,11... | collective-permute-start | bytes 786440 | tf_op jit(solution)/shard_map/ppermute | solution.py:825
  220.0 26.5 %collective-permute-start.34 = (bf16[256,512]{1,0:T(8,128)(2,1)}, bf16[256,512]{1,0:T(8,128)(2,1)}, u32[]{:S(2)}, u32[]{:S(2)}) collective-permute-start(bf16[256,512]{1,0:T(8,128)(2,1)} %sum_early.1.early_refs_0_), channel_id=1, source_target_pairs={{0,2},{1,3},{2,0},{3,1},{4,6},{5,7},{6,4},{7,5},{8,10},{9,11},{10,... | collective-permute-start | bytes 786440 | tf_op jit(solution)/shard_map/ppermute | solution.py:825
  221.2 25.3 %collective-permute-start.35 = (bf16[256,512]{1,0:T(8,128)(2,1)}, bf16[256,512]{1,0:T(8,128)(2,1)}, u32[]{:S(2)}, u32[]{:S(2)}) collective-permute-start(bf16[256,512]{1,0:T(8,128)(2,1)} %sum_early.1.early_refs_0_), channel_id=1, source_target_pairs={{0,3},{1,2},{2,1},{3,0},{4,7},{5,6},{6,5},{7,4},{8,11},{9,10},{10,... | collective-permute-start | bytes 786440 | tf_op jit(solution)/shard_map/ppermute | solution.py:825
  224.0 14.1 %collective-permute-start.43 = (bf16[192,512]{1,0:T(8,128)(2,1)}, bf16[192,512]{1,0:T(8,128)(2,1)S(1)}, u32[]{:S(2)}, u32[]{:S(2)}) collective-permute-start(bf16[192,512]{1,0:T(8,128)(2,1)} %sum_late.1.late_refs_0_), channel_id=1, source_target_pairs={{0,3},{1,2},{2,1},{3,0},{4,7},{5,6},{6,5},{7,4},{8,11},{9,10},{10,... | collective-permute-start | bytes 589832 | tf_op jit(solution)/shard_map/ppermute | solution.py:825
  230.6 11.2 %collective-permute-start.42 = (bf16[192,512]{1,0:T(8,128)(2,1)S(1)}, bf16[192,512]{1,0:T(8,128)(2,1)S(1)}, u32[]{:S(2)}, u32[]{:S(2)}) collective-permute-start(bf16[192,512]{1,0:T(8,128)(2,1)S(1)} %copy-done.11), channel_id=1, source_target_pairs={{0,2},{1,3},{2,0},{3,1},{4,6},{5,7},{6,4},{7,5},{8,10},{9,11},{10,... | collective-permute-start | bytes 589832 | tf_op jit(solution)/shard_map/ppermute | solution.py:825
  232.6 11.7 %copy-start.32 = (f32[5,288]{1,0:T(8,128)S(1)}, f32[5,288]{1,0:T(8,128)}, u32[]{:S(2)}) copy-start(f32[5,288]{1,0:T(8,128)} %conv_ref.1) | copy-start | bytes 17284
  232.6 11.7 %copy-start.37 = (f32[5,288]{1,0:T(8,128)S(1)}, f32[5,288]{1,0:T(8,128)}, u32[]{:S(2)}) copy-start(f32[5,288]{1,0:T(8,128)} %param.39) | copy-start | bytes 17284
  232.6 12.4 %copy-start.40 = (f32[384]{0:T(512)S(1)}, f32[384]{0:T(512)}, u32[]{:S(2)}) copy-start(f32[384]{0:T(512)} %param.31) | copy-start | bytes 4612
  232.7 12.4 %copy-start.43 = (f32[384]{0:T(512)S(1)}, f32[384]{0:T(512)}, u32[]{:S(2)}) copy-start(f32[384]{0:T(512)} %param.41) | copy-start | bytes 4612
  232.7 12.4 %copy-start.44 = (f32[384]{0:T(512)S(1)}, f32[384]{0:T(512)}, u32[]{:S(2)}) copy-start(f32[384]{0:T(512)} %param.42) | copy-start | bytes 4612
  232.7 13.2 %copy-start.31 = (f32[32,128]{1,0:T(8,128)S(1)}, f32[32,128]{1,0:T(8,128)}, u32[]{:S(2)}) copy-start(f32[32,128]{1,0:T(8,128)} %dt_ref.1) | copy-start | bytes 49156
  232.7 13.2 %copy-start.35 = (f32[32,128]{1,0:T(8,128)S(1)}, f32[32,128]{1,0:T(8,128)}, u32[]{:S(2)}) copy-start(f32[32,128]{1,0:T(8,128)} %param.35) | copy-start | bytes 49156
  232.7 13.2 %copy-start.36 = (f32[32,128]{1,0:T(8,128)S(1)}, f32[32,128]{1,0:T(8,128)}, u32[]{:S(2)}) copy-start(f32[32,128]{1,0:T(8,128)} %param.36) | copy-start | bytes 49156
  238.1 3.7 %collective-permute-start.41 = (bf16[192,512]{1,0:T(8,128)(2,1)S(1)}, bf16[192,512]{1,0:T(8,128)(2,1)S(1)}, u32[]{:S(2)}, u32[]{:S(2)}) collective-permute-start(bf16[192,512]{1,0:T(8,128)(2,1)S(1)} %copy-done.11), channel_id=1, source_target_pairs={{0,1},{1,0},{2,3},{3,2},{4,5},{5,4},{6,7},{7,6},{8,9},{9,8},{10,11... | collective-permute-start | bytes 589832 | tf_op jit(solution)/shard_map/ppermute | solution.py:825
  (27 other events, 131.4 us)

commit v4 on v3

--- a/solution.py
+++ b/solution.py
@@ -79,11 +79,22 @@
     return sig * (1.0 + value * (1.0 - sig))
 
 
+def diagonal(size):
+    row = lax.broadcasted_iota(jnp.int32, (size, size), 0)
+    return row == lax.broadcasted_iota(jnp.int32, (size, size), 1)
+
+
 def triangle(size, lower):
     row = lax.broadcasted_iota(jnp.int32, (size, size), 0)
     col = lax.broadcasted_iota(jnp.int32, (size, size), 1)
     keep = row >= col if lower else row <= col
     return jnp.where(keep, 1.0, 0.0).astype(F32)
+
+
+def cost(micros):
+    return pl.CostEstimate(
+        flops=int(micros * 1.1e9), bytes_accessed=int(micros * 3.6e6), transcendentals=0
+    )
 
 
 def params(*semantics):
@@ -142,7 +153,7 @@
     return out
 
 
-def pack_kernel(here_ref, win_ref, wout_ref, dt_ref, conv_ref, gain_ref, cot_ref, w1_ref, g2_ref, cotl_ref, tmp_ref):
+def pack_kernel(here_ref, win_ref, wout_ref, dt_ref, conv_ref, gain_ref, w1_ref, g2_ref, tmp_ref):
     ctx = here_ref[2]
     rows = win_ref.shape[0]
     heads = HEADS // 4
@@ -156,7 +167,7 @@
     table = jnp.where(col == 4 * row + ctx, 1.0, 0.0).astype(BF16)
     tmp_ref[0:heads, 384 : 384 + dt_ref.shape[1]] = nn(table, dt_ref[...].astype(BF16))
     tmp_ref[8 : 8 + CONV + 1, 0 : conv_ref.shape[1]] = conv_ref[...]
-    tmp_ref[8 + CONV + 1 : 8 + CONV + 2, 0 : gain_ref.shape[1]] = gain_ref[...]
+    tmp_ref[8 + CONV + 1 : 8 + CONV + 2, 0 : gain_ref.shape[0]] = gain_ref[...].reshape(1, -1)
     w1_ref[rows : rows + 16, :] = tmp_ref[...].astype(BF16)
     for at, part in enumerate(pick_heads(win_ref, 0, ctx, heads)):
         g2_ref[0:rows, at * 128 : (at + 1) * 128] = part.astype(BF16)
@@ -165,7 +176,6 @@
         mine = wout_ref[pl.ds(pl.multiple_of(ctx * some, 8), some), :].astype(BF16)
         g2_ref[rows : rows + some] = mine[:, :width]
         g2_ref[rows + some : rows + 2 * some] = mine[:, width:]
-    cotl_ref[...] = cot_ref[...].astype(BF16)
 
 
 def scan_forward_kernel(
@@ -362,10 +372,12 @@
     grad = nt(cot_ref[step], wout_ref[...])
     ng_ref[...] = grad
     gated = inner_ref[...] * (gate * sigmoid(gate))
-    ones = jnp.ones((8, gated.shape[1]), F32)
-    squares = nt(ones, gated * gated, HIGHEST)
-    crossed = nt(ones, gated * (grad * gain_ref[...]), HIGHEST)
-    at = lax.broadcasted_iota(jnp.int32, squares.shape, 0)
+    squares = jnp.sum(gated * gated, axis=1, keepdims=True)
+    crossed = jnp.sum(gated * (grad * gain_ref[...]), axis=1, keepdims=True)
+    same = diagonal(gated.shape[0])
+    squares = jnp.sum(jnp.where(same, squares, 0.0), axis=0, keepdims=True)
+    crossed = jnp.sum(jnp.where(same, crossed, 0.0), axis=0, keepdims=True)
+    at = lax.broadcasted_iota(jnp.int32, stat_ref.shape, 0)
     stat_ref[...] = jnp.where(at == 0, squares, crossed)
 
 
@@ -381,7 +393,8 @@
     mixed_ref,
     wout_ref,
     cot_ref,
-    block_ref,
+    bkeep_ref,
+    bsend_ref,
     keep_ref,
     send_ref,
     dy_ref,
@@ -399,12 +412,10 @@
         inacc_ref[...] = jnp.zeros_like(inacc_ref)
         sums_ref[...] = jnp.zeros_like(sums_ref)
 
-    row = lax.broadcasted_iota(jnp.int32, (span, span), 0)
-    col = lax.broadcasted_iota(jnp.int32, (span, span), 1)
-    eye = jnp.where(row == col, 1.0, 0.0).astype(F32)
-    stats = nt(eye, stat_ref[...], HIGHEST)
-    inv = lax.rsqrt(stats[:, 0:1] * (1.0 / INNER) + NORM_EPS)
-    cross = stats[:, 1:2]
+    same = diagonal(span)
+    squares = jnp.sum(jnp.where(same, stat_ref[0:1], 0.0), axis=1, keepdims=True)
+    cross = jnp.sum(jnp.where(same, stat_ref[1:2], 0.0), axis=1, keepdims=True)
+    inv = lax.rsqrt(squares * (1.0 / INNER) + NORM_EPS)
     gate = gate_ref[...].astype(F32)
     sig = sigmoid(gate)
     silu = gate * sig
@@ -412,8 +423,17 @@
     gated = inner * silu
     unit = gated * inv
     normed = (unit * gain_ref[...]).astype(BF16)
-    cot = cot_ref[step]
-    block_ref[0] = nn(normed, wout_ref[...]).astype(BF16)
+    cot = cot_ref[perm_ref[step]]
+    block = nn(normed, wout_ref[...]).astype(BF16)
+
+    @pl.when(step < 2)
+    def _():
+        bsend_ref[0] = block
+
+    @pl.when(step >= 2)
+    def _():
+        bkeep_ref[0] = block
+
     outacc_ref[...] += tn(normed, cot)
     grad = ng_ref[...]
     dgated = inv * (grad * gain_ref[...] - unit * (cross * inv * (1.0 / INNER)))
@@ -619,7 +639,8 @@
     wdt_ref,
     hid_ref,
     gain_ref,
-    out_ref,
+    keep_ref,
+    send_ref,
     gsum_ref,
 ):
     @pl.when(pl.program_id(0) == 0)
@@ -628,7 +649,16 @@
 
     total = nt(dgate_ref[...], wg_ref[...]) + nt(dval_ref[...], wv_ref[...])
     total = total + nn(dstep_ref[...], wdt_ref[...])
-    out_ref[0] = total.astype(BF16)
+    step = pl.program_id(0)
+
+    @pl.when(step < 2)
+    def _():
+        send_ref[0] = total.astype(BF16)
+
+    @pl.when(step >= 2)
+    def _():
+        keep_ref[0] = total.astype(BF16)
+
     unit = hid_ref[...].astype(F32) / gain_ref[...]
     gsum_ref[...] += jnp.sum(total * unit, axis=0, keepdims=True) + jnp.zeros(gsum_ref.shape, F32)
 
@@ -636,6 +666,7 @@
 def maps_back_kernel(
     here_ref,
     dbc_ref,
+    dbcfar_ref,
     convsum_ref,
     convin_ref,
     conv_ref,
@@ -657,7 +688,8 @@
     small_ref,
 ):
     size, width = dmap_ref.shape
-    ext_ref[0:size] = dbc_ref[...] * silu_grad(convsum_ref[...])
+    total = dbc_ref[...].astype(F32) + dbcfar_ref[...].astype(F32)
+    ext_ref[0:size] = total * silu_grad(convsum_ref[...])
     ext_ref[size : size + 8] = jnp.zeros((8, width), F32)
     back = jnp.zeros((size, width), F32)
     conv_in = convin_ref[...].astype(F32)
@@ -675,7 +707,7 @@
     acc_ref[...] = tn(hid_ref[...], dmap_ref[...])
     span = own_ref.shape[0]
     own = pl.ds(pl.multiple_of(ctx * span, 16), span)
-    grad = nt(dmap_ref[own, :], w1_ref[:, w1_ref.shape[1] - width :])
+    grad = nt(dmap_ref[own, :], w1_ref[...])
     own_ref[...] = grad
     unit = hid_ref[own, :].astype(F32) / gain_ref[...]
     gain_sum = gall_ref[0:1] + jnp.sum(grad * unit, axis=0, keepdims=True)
@@ -707,8 +739,8 @@
         send_ref[32 + 32 * at : 64 + 32 * at, 0:width] = jnp.where(here_ref[0] == 0, high, low)
 
 
-def input_back_kernel(hg_ref, own_ref, tok_ref, gain_ref, cot_ref, out_ref):
-    grad = hg_ref[...] + own_ref[...]
+def input_back_kernel(keep_ref, came_ref, far_ref, own_ref, tok_ref, gain_ref, cot_ref, out_ref):
+    grad = keep_ref[0].astype(F32) + came_ref[0].astype(F32) + far_ref[...].astype(F32) + own_ref[...]
     tok = tok_ref[...]
     scale = lax.rsqrt(jnp.mean(tok * tok, axis=-1, keepdims=True) + NORM_EPS)
     unit = tok * scale
@@ -755,28 +787,33 @@
     out_ref[...] = total.astype(out_ref.dtype)
 
 
-def adam_kernel(
-    here_ref,
-    win_ref,
-    wfirst_ref,
-    wsecond_ref,
-    oin_ref,
-    ofirst_ref,
-    osecond_ref,
-    early_refs,
-    late_refs,
-    win_new,
-    wfirst_new,
-    wsecond_new,
-    out_new,
-    ofirst_new,
-    osecond_new,
-    early_ref,
-    late_ref,
-):
+def adam_out_kernel(here_ref, weight_ref, first_ref, second_ref, early_refs, *rest):
+    new_refs, early_ref = rest[:3], rest[3]
+    step = pl.program_id(0)
+
+    @pl.when(step == 0)
+    def _():
+        for at, ref in enumerate(early_refs):
+            early_ref[pl.ds(here_ref[2] ^ at, 1)] = ref[...][None]
+
+    rows = weight_ref.shape[0]
+    width = early_ref.shape[2]
+    first = early_ref.shape[1] - 2 * rows
+    for at in range(2):
+        lanes = slice(at * width, (at + 1) * width)
+        grad = early_ref[step, first + at * rows : first + (at + 1) * rows].astype(F32)
+        news = adam_step(
+            weight_ref[:, lanes], first_ref[:, lanes], second_ref[:, lanes], grad, 0.02, WEIGHT_DECAY
+        )
+        for ref, new in zip(new_refs, news):
+            ref[:, lanes] = new
+
+
+def adam_in_kernel(here_ref, weight_ref, first_ref, second_ref, early_refs, late_refs, *rest):
+    new_refs, (early_ref, late_ref) = rest[:3], rest[3:]
     step = pl.program_id(0)
     pieces = len(early_refs)
-    rows = win_ref.shape[0]
+    rows = weight_ref.shape[0]
     width = early_ref.shape[2]
     block = pieces * HEAD_DIM
 
@@ -792,9 +829,10 @@
 
     def update(lanes, grad):
         news = adam_step(
-            win_ref[:, lanes], wfirst_ref[:, lanes], wsecond_ref[:, lanes], grad, 0.03, WEIGHT_DECAY
+            weight_ref[:, lanes], first_ref[:, lanes], second_ref[:, lanes], grad, 0.03, WEIGHT_DECAY
         )
-        win_new[:, lanes], wfirst_new[:, lanes], wsecond_new[:, lanes] = news
+        for ref, new in zip(new_refs, news):
+            ref[:, lanes] = new
 
     for base, ref in ((0, early_ref), (INNER, late_ref)):
         for pair in range(width // (2 * HEAD_DIM)):
@@ -809,15 +847,10 @@
                 odd = jnp.where(low, pltpu.roll(first, HEAD_DIM, 1), second)
                 update(slice(start, start + 2 * HEAD_DIM), odd)
     first = late_ref.shape[1] - 32
-    update(slice(2 * INNER, 2 * INNER + 2 * STATE), late_ref[step, first : first + 32, 0 : 2 * STATE].astype(F32))
-    first = rows * pieces
-    for at in range(2):
-        lanes = slice(at * width, (at + 1) * width)
-        grad = early_ref[step, first + at * HEAD_DIM : first + (at + 1) * HEAD_DIM].astype(F32)
-        news = adam_step(
-            oin_ref[:, lanes], ofirst_ref[:, lanes], osecond_ref[:, lanes], grad, 0.02, WEIGHT_DECAY
-        )
-        out_new[:, lanes], ofirst_new[:, lanes], osecond_new[:, lanes] = news
+    update(
+        slice(2 * INNER, 2 * INNER + 2 * STATE),
+        late_ref[step, first : first + 32, 0 : 2 * STATE].astype(F32),
+    )
 
 
 def swap(value, axis, bit):
@@ -828,17 +861,6 @@
 def gather_ctx(value):
     far = swap(value, "ctx", 2)
     return [value, swap(value, "ctx", 1), far, swap(far, "ctx", 1)]
-
-
-def scatter_ctx(value):
-    near = value[0:2].astype(F32) + swap(value[2:4], "ctx", 1).astype(F32)
-    return near[0] + swap(near[1].astype(BF16), "ctx", 2).astype(F32)
-
-
-def sum_ctx(value):
-    pair = value.astype(F32) + swap(value, "ctx", 1).astype(F32)
-    pair = pair.astype(BF16)
-    return pair.astype(F32) + swap(pair, "ctx", 2).astype(F32)
 
 
 def gather_dp(value):
@@ -919,35 +941,36 @@
     block_in = model // heads
     tok = tokens[0]
     bits = jnp.stack([d & 1, d >> 1, c] if near else [0 * d, 0 * d, c]).astype(jnp.int32)
-    order = jnp.asarray([0, 2, 1, 3], jnp.int32)
-    perm = order[jnp.arange(nctx, dtype=jnp.int32) ^ c]
+    perm = c ^ jnp.asarray([1, 3, 0, 2], jnp.int32)
     smem = pl.BlockSpec(memory_space=pltpu.SMEM)
     vmem = pl.BlockSpec(memory_space=pltpu.VMEM)
     anywhere = lambda pieces: [pl.BlockSpec(memory_space=pl.ANY)] * len(pieces)
 
-    w1, g2, cot_low = pl.pallas_call(
+    w1, g2 = pl.pallas_call(
         pack_kernel,
-        in_specs=[smem] + [vmem] * 6,
+        in_specs=[smem] + [vmem] * 5,
         out_shape=[
             shape_of(rows_in + 16, wide, dtype=BF16),
             shape_of(rows_in + (2 * HEAD_DIM if near else 0), width, dtype=BF16),
-            shape_of(span, model, dtype=BF16),
         ],
         scratch_shapes=[pltpu.VMEM((16, wide), F32)],
         compiler_params=params(),
+        cost_estimate=cost(3),
         name="pack",
-    )(bits, in_weight, out_weight, dt_weight, conv_params, gains[None], cotangent[0])
-    toks = gather_ctx(tok)
+    )(bits, in_weight, out_weight, dt_weight, conv_params, gains)
+    tok_sent, w1 = lax.optimization_barrier((tok, w1))
     w1, at_rows = gather_dp(w1)
+    toks = gather_ctx(tok_sent)
     if near:
-        g2, at_g2 = gather_dp(g2)
+        g2 = [lax.all_gather(g2, "dp", axis=0)]
     else:
         wg = lax.all_gather(g2, "dp", axis=0, tiled=True).reshape(heads, block_in, width)
         wout = lax.all_gather(out_weight.astype(BF16), "dp", axis=0, tiled=True)
         wout = lax.dynamic_index_in_dim(wout.reshape(heads, nctx, HEAD_DIM, model), c, 1, False)
         g2 = [jnp.concatenate([wg, wout[:, :, :width], wout[:, :, width:]], axis=1)]
-        at_g2 = at_rows
-    cots = gather_ctx(cot_low)
+    at_g2 = jnp.zeros((1,), jnp.int32)
+    cot_low, w1 = lax.optimization_barrier((cotangent[0].astype(BF16), w1))
+    cots = fan_ctx(cot_low)
 
     ids = segment_ids[0]
     seg_col = jnp.pad(ids, (8, 8), constant_values=-1)[:, None]
@@ -957,7 +980,9 @@
 
     rows = lambda cols: pl.BlockSpec((span, cols), lambda i, *_: (i, 0))
     row_of = pl.BlockSpec((heads, span), lambda i, *_: (0, i))
-    slot_rows = pl.BlockSpec((1, span, model), lambda i, p, *_: (p[i], 0, 0))
+    rows_at = lambda cols: pl.BlockSpec((span, cols), lambda i, p, *_: (p[i], 0))
+    sent = pl.BlockSpec((1, span, model), lambda i, *_: (jnp.minimum(i, 1), 0, 0))
+    kept = pl.BlockSpec((1, span, model), lambda i, *_: (jnp.maximum(i - 2, 0), 0, 0))
     shards_in = sum(piece.shape[0] for piece in w1)
 
     (
@@ -1025,6 +1050,7 @@
             shape_of(chunks, STATE, width),
         ],
         compiler_params=params("arbitrary"),
+        cost_estimate=cost(18),
         name="scan_forward",
     )(bits, at_rows, toks, w1, head_mine, head_col, seg_col, seg_row)
 
@@ -1056,39 +1082,42 @@
             shape_of(8, length),
         ],
         compiler_params=params("arbitrary"),
+        cost_estimate=cost(12),
         name="gate",
     )(bits, at_g2, hid, g2, cots, inner, gain_mine)
     stats = sum(fan_ctx(stats))
 
     early_rows = block_in + 2 * HEAD_DIM
-    block_part, early_keep, early_send, dy, dgate, col_sums = pl.pallas_call(
+    block_keep, block_send, early_keep, early_send, dy, dgate, col_sums = pl.pallas_call(
         norm_back_kernel,
         grid_spec=pltpu.PrefetchScalarGridSpec(
             num_scalar_prefetch=2,
             grid=(chunks,),
             in_specs=[
-                rows(model),
-                rows(width),
-                rows(width),
-                rows(width),
-                pl.BlockSpec((8, span), lambda i, *_: (0, i)),
+                rows_at(model),
+                rows_at(width),
+                rows_at(width),
+                rows_at(width),
+                pl.BlockSpec((8, span), lambda i, p, *_: (0, p[i])),
                 full((1, width)),
-                rows(width),
+                rows_at(width),
                 full((width, model)),
                 full((nctx, span, model)),
             ],
             out_specs=[
-                slot_rows,
+                kept,
+                sent,
                 full((high, early_rows, width)),
                 full((high, early_rows, width)),
-                rows(width),
-                rows(width),
+                rows_at(width),
+                rows_at(width),
                 full((8, width)),
             ],
             scratch_shapes=[pltpu.VMEM((width, model), F32), pltpu.VMEM((model, width), F32)],
         ),
         out_shape=[
-            shape_of(nctx, span, model, dtype=BF16),
+            shape_of(2, span, model, dtype=BF16),
+            shape_of(2, span, model, dtype=BF16),
             shape_of(high, early_rows, width, dtype=BF16),
             shape_of(high, early_rows, width, dtype=BF16),
             shape_of(length, width),
@@ -1096,9 +1125,10 @@
             shape_of(8, width),
         ],
         compiler_params=params("arbitrary"),
+        cost_estimate=cost(13),
         name="norm_back",
     )(perm, bits, hid, inner, gate, normed_grad, stats, gain_mine, mixed, wout, cot_all)
-    block_output = tok + scatter_ctx(block_part)
+    block_came = swap(block_send, "ctx", 1)
     if near:
         early_came = swap(early_send, "dp", 1)
 
@@ -1155,12 +1185,14 @@
             shape_of(8, heads),
         ],
         compiler_params=params("arbitrary"),
+        cost_estimate=cost(21),
         name="scan_back",
     )(
         perm, bits, hid, dy, mixed, conv_in, conv_sum, raw, step_c, log_c, step_r, log_r, starts,
         conv_mine, head_mine, seg_col, seg_row,
     )
-    dbc_total = sum_ctx(dbc)
+    block_far = (block_keep[1].astype(F32) + block_came[1].astype(F32)).astype(BF16)
+    dbc_came = swap(dbc, "ctx", 1)
     if near:
         late_came = swap(late_send, "dp", 1)
         early_parts = pl.pallas_call(
@@ -1168,37 +1200,67 @@
             in_specs=[smem, vmem, vmem],
             out_shape=[[shape_of(early_rows, width, dtype=BF16)] * high],
             compiler_params=params(),
+            cost_estimate=cost(3),
             name="pair_sum_early",
         )(bits, early_keep, early_came)[0]
+        dval, early_parts = lax.optimization_barrier((dval, early_parts))
         early_parts = spread_dp(early_parts)
-
-    hidden_part, gain_sum = pl.pallas_call(
+    dbc = (dbc.astype(F32) + dbc_came.astype(F32)).astype(BF16)
+    dbc_far = swap(dbc, "ctx", 2)
+
+    hidden_keep, hidden_send, gain_sum = pl.pallas_call(
         hidden_back_kernel,
         grid_spec=pltpu.PrefetchScalarGridSpec(
             num_scalar_prefetch=1,
             grid=(chunks,),
             in_specs=[
-                rows(width),
-                rows(width),
-                rows(heads),
+                rows_at(width),
+                rows_at(width),
+                rows_at(heads),
                 full((model, width)),
                 full((model, width)),
                 full((heads, model)),
-                rows(model),
+                rows_at(model),
                 full((1, model)),
             ],
-            out_specs=[slot_rows, full((8, model))],
+            out_specs=[kept, sent, full((8, model))],
         ),
-        out_shape=[shape_of(nctx, span, model, dtype=BF16), shape_of(8, model)],
+        out_shape=[
+            shape_of(2, span, model, dtype=BF16),
+            shape_of(2, span, model, dtype=BF16),
+            shape_of(8, model),
+        ],
         compiler_params=params("arbitrary"),
+        cost_estimate=cost(8),
         name="hidden_back",
     )(perm, dgate, dval, dstep, wg, w1, dt_mine, hid, gain_pre)
-    hidden_grad = scatter_ctx(hidden_part)
+    hidden_came = swap(hidden_send, "ctx", 1)
+    hidden_far = (hidden_keep[1].astype(F32) + hidden_came[1].astype(F32)).astype(BF16)
+    hidden_far = swap(hidden_far, "ctx", 2)
 
     map_rows = 32 + 32 * high
+    map_cols = lambda size: pl.BlockSpec((size, maps), lambda i: (0, width // maps))
     map_keep, map_send, hidden_own = pl.pallas_call(
         maps_back_kernel,
-        in_specs=[smem] + [vmem] * 13,
+        grid=(1,),
+        in_specs=[
+            smem,
+            full((length, maps)),
+            full((length, maps)),
+            map_cols(length),
+            map_cols(length),
+            map_cols(8),
+            full((length + 16, 1)),
+            full((length, model)),
+            map_cols(model),
+            full((1, model)),
+            full((8, width)),
+            full((8, width)),
+            full((8, heads)),
+            full((heads, model)),
+            full((8, model)),
+        ],
+        out_specs=[full((map_rows, width)), full((map_rows, width)), full((span, model))],
         out_shape=[
             shape_of(map_rows, width, dtype=BF16),
             shape_of(map_rows, width, dtype=BF16),
@@ -1210,14 +1272,16 @@
             pltpu.VMEM((length, maps), BF16),
             pltpu.VMEM((32, width), F32),
         ],
-        compiler_params=params(),
+        compiler_params=params("arbitrary"),
+        cost_estimate=cost(6),
         name="maps_back",
     )(
         bits,
-        dbc_total,
-        conv_sum[:, width:],
-        conv_in[:, width:],
-        conv_mine[:, width:],
+        dbc,
+        dbc_far,
+        conv_sum,
+        conv_in,
+        conv_mine,
         seg_col,
         hid,
         w1,
@@ -1229,12 +1293,21 @@
         gain_sum,
     )
 
+    mine = pl.BlockSpec((1, span, model), lambda i: (0, 0, 0))
     input_grad = pl.pallas_call(
         input_back_kernel,
+        grid=(1,),
+        in_specs=[mine, mine] + [full((span, model))] * 3 + [full((1, model)), full((span, model))],
+        out_specs=full((span, model)),
         out_shape=shape_of(span, model),
-        compiler_params=params(),
+        compiler_params=params("arbitrary"),
+        cost_estimate=cost(4),
         name="input_back",
-    )(hidden_grad, hidden_own, tok, gain_pre, cotangent[0])
+    )(hidden_keep, hidden_came, hidden_far, hidden_own, tok, gain_pre, cotangent[0])
+    block_far = swap(block_far, "ctx", 2)
+    block_output = tok + (
+        block_keep[0].astype(F32) + block_came[0].astype(F32) + block_far.astype(F32)
+    )
 
     late_rows = block_in + 64
     if near:
@@ -1244,7 +1317,8 @@
             in_specs=[smem] + [vmem] * 4,
             out_shape=[[shape_of(late_rows, width, dtype=BF16)] * high],
             compiler_params=params(),
-            name="pair_sum_late",
+            cost_estimate=cost(2),
+        name="pair_sum_late",
         )(bits, late_keep, late_came, map_keep, map_came)[0]
         late_parts = spread_dp(late_parts)
         early, late = [
@@ -1253,6 +1327,7 @@
                 in_specs=[[vmem] * high],
                 out_shape=shape_of(*parts[0].shape, dtype=BF16),
                 compiler_params=params(),
+                cost_estimate=cost(2),
                 name="sum_" + name,
             )(parts)
             for name, parts in (("early", early_parts), ("late", late_parts))
@@ -1261,25 +1336,37 @@
         row_block = lambda ref_rows, cols: pl.BlockSpec((ref_rows, cols), lambda i, *_: (i, 0))
         in_block = row_block(rows_in // nctx, in_weight.shape[1])
         out_block = row_block(out_weight.shape[0] // nctx, model)
-        news = pl.pallas_call(
-            adam_kernel,
+        early_spec = [full((early_rows, width))] * nctx
+        early_scratch = pltpu.VMEM((nctx, early_rows, width), BF16)
+        out_new = pl.pallas_call(
+            adam_out_kernel,
             grid_spec=pltpu.PrefetchScalarGridSpec(
                 num_scalar_prefetch=1,
                 grid=(nctx,),
-                in_specs=[in_block] * 3
-                + [out_block] * 3
-                + [[full((early_rows, width))] * nctx, [full((late_rows, width))] * nctx],
-                out_specs=[in_block] * 3 + [out_block] * 3,
-                scratch_shapes=[
-                    pltpu.VMEM((nctx, early_rows, width), BF16),
-                    pltpu.VMEM((nctx, late_rows, width), BF16),
-                ],
+                in_specs=[out_block] * 3 + [early_spec],
+                out_specs=[out_block] * 3,
+                scratch_shapes=[early_scratch],
             ),
-            out_shape=[shape_of(*in_weight.shape)] * 3 + [shape_of(*out_weight.shape)] * 3,
+            out_shape=[shape_of(*out_weight.shape)] * 3,
             compiler_params=params("arbitrary"),
-            name="adam",
-        )(bits, in_weight, in_first, in_second, out_weight, out_first, out_second, early, late)
-        in_new, out_new = tuple(news[:3]), tuple(news[3:])
+            cost_estimate=cost(4),
+            name="adam_out",
+        )(bits, out_weight, out_first, out_second, early)
+        in_new = pl.pallas_call(
+            adam_in_kernel,
+            grid_spec=pltpu.PrefetchScalarGridSpec(
+                num_scalar_prefetch=1,
+                grid=(nctx,),
+                in_specs=[in_block] * 3 + [early_spec, [full((late_rows, width))] * nctx],
+                out_specs=[in_block] * 3,
+                scratch_shapes=[early_scratch, pltpu.VMEM((nctx, late_rows, width), BF16)],
+            ),
+            out_shape=[shape_of(*in_weight.shape)] * 3,
+            compiler_params=params("arbitrary"),
+            cost_estimate=cost(7),
+            name="adam_in",
+        )(bits, in_weight, in_first, in_second, early, late)
+        in_new, out_new = tuple(in_new), tuple(out_new)
         small = jnp.stack([part[block_in : block_in + 32] for part in late])[c ^ jnp.arange(nctx)]
         small = small.astype(F32)
     else:

time: 258 us -> 286 us (1.11)
  waiting for transfers between devices: 59.3 us -> 104 us
  between operations: 1.44 us -> 14.7 us
  starting transfers between devices: 54.6 us -> 41.4 us
  local copies, waits for them, and re-layouts: 21.7 us -> 8.64 us
  other arithmetic: 13.2 us -> 8.83 us
    ppermute x44 -> x37, waiting for transfers between devices: 59.3 us -> 104 us  [swap(): return lax.ppermute(value, axis, [(at, at ^ bit) for at in range(count)])]
    ppermute x44 -> x37, starting transfers between devices: 54.6 us -> 41.4 us  [swap(): return lax.ppermute(value, axis, [(at, at ^ bit) for at in range(count)])]
    slice x5 -> x0, local copies, waits for them, and re-layouts: 6.9 us -> none  [the longest x1 2.3 us: shards(): conv_sum[:, width:]]
    add x4 -> x0, other arithmetic: 6.5 us -> none  [the longest x2 3.22 us: scatter_ctx(): near = value[0:2].astype(F32) + swap(value[2:4], 'ctx', 1).astype(F32)]
    pallas_call x4 -> x5, Pallas kernels: 23.6 us -> 27.1 us  [the longest x1 8.29 us: shards(): pl.pallas_call(adam_in_kernel, grid_spec=pltpu.PrefetchScalarGridSpec(num...]
    unnamed x97 -> x111, local copies, waits for them, and re-layouts: 6.29 us -> 4.18 us
  transfers between devices with their start and end apart: 44 -> 38, of which waited for: 16 -> 20; matrix products, arithmetic and copies ran while one was open for 11% -> 4% of each run, Pallas kernels for 28% -> 27%
where the time goes in v4:
time: 286 us
  Pallas kernels  108 us (38%)
  waiting for transfers between devices  104 us (36%)
  starting transfers between devices  41.4 us (14%)
  between operations  14.7 us (5%)
  other arithmetic  8.83 us (3%)
  local copies, waits for them, and re-layouts  8.64 us (3%)
    ppermute x37, waiting for transfers between devices, swap(): return lax.ppermute(value, axis, [(at, at ^ bit) for at in range(count)])  104 us
    ppermute x37, starting transfers between devices, swap(): return lax.ppermute(value, axis, [(at, at ^ bit) for at in range(count)])  41.4 us
    pallas_call x1, Pallas kernels, shards(): pl.pallas_call(scan_back_kernel, grid_spec=pltpu.PrefetchScalarGridSpec(n...  21.8 us
    pallas_call x1, Pallas kernels, shards(): pl.pallas_call(scan_forward_kernel, grid_spec=pltpu.PrefetchScalarGridSpe...  18.2 us
    pallas_call x1, Pallas kernels, shards(): pl.pallas_call(norm_back_kernel, grid_spec=pltpu.PrefetchScalarGridSpec(n...  13.1 us
    pallas_call x1, Pallas kernels, shards(): pl.pallas_call(gate_kernel, grid_spec=pltpu.PrefetchScalarGridSpec(num_sc...  10.1 us
    pallas_call x1, Pallas kernels, shards(): pl.pallas_call(adam_in_kernel, grid_spec=pltpu.PrefetchScalarGridSpec(num...  8.29 us
    pallas_call x1, Pallas kernels, shards(): pl.pallas_call(hidden_back_kernel, grid_spec=pltpu.PrefetchScalarGridSpec...  8.27 us
  transfers between devices with their start and end apart: 38, of which 20 were waited for; matrix products, arithmetic and copies ran while one was open for 4% of the time, Pallas kernels for 27%

profile of v4, /device:TPU:0, one launch (start us, length us, event | category | flops | bytes accessed | tf_op | source)
XLA Modules:
  0.0 285.5 jit_solution(7550758332049412983)
XLA Ops:
  7.9 3.1 %pack.1 = (bf16[144,768]{1,0:T(8,128)(2,1)}, bf16[256,512]{1,0:T(8,128)(2,1)}) custom-call(s32[3]{0:T(128)} %pad_add_fusion.here_ref, f32[128,4352]{1,0:T(8,128)} %weight_ref.2, f32[256,1024]{1,0:T(8,128)} %weight_ref.3, f32[32,128]{1,0:T(8,128)} %dt_ref.1, f32[5,288]{1,0:T(8,128)} %conv_ref.1, f32[384]{0:T(512)} %gain_ref.1), custom_call_target="tpu_custom_call" | custom-call | flops 3300000000 | bytes 10800000 | tf_op jit(solution)/shard_map/pack/pallas_call | solution.py:949
  11.0 3.0 %collective-permute-start.1 = (f32[256,1024]{1,0:T(8,128)S(1)}, f32[256,1024]{1,0:T(8,128)S(1)}, u32[]{:S(2)}, u32[]{:S(2)}) collective-permute-start(f32[256,1024]{1,0:T(8,128)S(1)} %bitcast.58), channel_id=1, source_target_pairs={{0,2},{1,3},{2,0},{3,1},{4,6},{5,7},{6,4},{7,5},{8,10},{9,11},{10,... | collective-permute-start | bytes 3145736 | tf_op jit(solution)/shard_map/ppermute | solution.py:858
  14.1 23.1 %collective-permute-done.1.tok_pieces_2_ = f32[256,1024]{1,0:T(8,128)S(1)} collective-permute-done((f32[256,1024]{1,0:T(8,128)S(1)}, f32[256,1024]{1,0:T(8,128)S(1)}, u32[]{:S(2)}, u32[]{:S(2)}) %collective-permute-start.1) | collective-permute-done | bytes 1048608 | tf_op jit(solution)/shard_map/ppermute | solution.py:858
  37.1 1.8 collective-permute-start.3
  38.9 2.6 collective-permute-start.4
  41.8 0.7 copy.67
  42.5 1.0 broadcast_in_dim.17.segc_ref
  43.6 10.8 %collective-permute-done.3.w1_pieces_1_ = bf16[1,144,768]{2,1,0:T(8,128)(2,1)S(1)} collective-permute-done((bf16[1,144,768]{2,1,0:T(8,128)(2,1)}, bf16[1,144,768]{2,1,0:T(8,128)(2,1)S(1)}, u32[]{:S(2)}, u32[]{:S(2)}) %collective-permute-start.3) | collective-permute-done | bytes 221216 | tf_op jit(solution)/shard_map/ppermute | solution.py:858
  54.3 1.9 collective-permute-start.6
  56.3 10.5 %collective-permute-done.4.w1_pieces_2_ = bf16[1,144,768]{2,1,0:T(8,128)(2,1)} collective-permute-done((bf16[1,144,768]{2,1,0:T(8,128)(2,1)}, bf16[1,144,768]{2,1,0:T(8,128)(2,1)}, u32[]{:S(2)}, u32[]{:S(2)}) %collective-permute-start.4) | collective-permute-done | bytes 221216 | tf_op jit(solution)/shard_map/ppermute | solution.py:858
  66.8 1.5 collective-permute-start.7
  68.2 1.0 collective-permute-done.5.w1_pieces_3_
  69.2 1.5 collective-permute-start.8
  71.8 2.7 collective-permute-done.7.w1_pieces_5_
  74.5 4.7 %collective-permute-done.8.w1_pieces_6_ = bf16[1,144,768]{2,1,0:T(8,128)(2,1)S(1)} collective-permute-done((bf16[1,144,768]{2,1,0:T(8,128)(2,1)}, bf16[1,144,768]{2,1,0:T(8,128)(2,1)S(1)}, u32[]{:S(2)}, u32[]{:S(2)}) %collective-permute-start.8) | collective-permute-done | bytes 221216 | tf_op jit(solution)/shard_map/ppermute | solution.py:858
  79.2 2.9 %collective-permute-done.9.w1_pieces_7_ = bf16[1,144,768]{2,1,0:T(8,128)(2,1)S(1)} collective-permute-done((bf16[1,144,768]{2,1,0:T(8,128)(2,1)}, bf16[1,144,768]{2,1,0:T(8,128)(2,1)S(1)}, u32[]{:S(2)}, u32[]{:S(2)}) %collective-permute-start.9) | collective-permute-done | bytes 221216 | tf_op jit(solution)/shard_map/ppermute | solution.py:858
  82.2 1.6 collective-permute-start.11
  84.1 18.2 %scan_forward.1 = (bf16[1024,1024]{1,0:T(8,128)(2,1)}, f32[8,768]{1,0:T(8,128)}, f32[1,1024]{1,0:T(1,128)}, f32[1,512]{1,0:T(1,128)}, bf16[8,1024]{1,0:T(8,128)(...) custom-call(s32[3]{0:T(128)} %pad_add_fusion.here_ref, ...), custom_call_target="tpu_custom_call" | custom-call | flops 19800000512 | bytes 64800000 | tf_op jit(solution)/shard_map/scan_forward/pallas_call | solution.py:991
  102.4 5.1 %collective-permute-done.12.cot_pieces_3_ = bf16[256,1024]{1,0:T(8,128)(2,1)} collective-permute-done((bf16[256,1024]{1,0:T(8,128)(2,1)S(1)}, bf16[256,1024]{1,0:T(8,128)(2,1)}, u32[]{:S(2)}, u32[]{:S(2)}) %collective-permute-start.12) | collective-permute-done | bytes 524320 | tf_op jit(solution)/shard_map/ppermute | solution.py:858
  107.5 10.1 %gate.1 = (bf16[1024,512]{1,0:T(8,128)(2,1)}, bf16[512,1024]{1,0:T(8,128)(2,1)}, bf16[4,256,1024]{2,1,0:T(8,128)(2,1)}, bf16[1024,512]{1,0:T(8,128)(2,1)}, f32[1024,512]{1,0:T(8,128)}, /*index=5*/f32[8,1024]{1,0:T(8,128)}) custom-call(s32[3]{0:T(128)} %pad_add_fusion.here_ref, s32[1]{0:T(128)} %constant.35.clone.1.at_ref, ...), custom_call_target="tpu_custom_call" | custom-call | flops 13200000000 | bytes 43200000 | tf_op jit(solution)/shard_map/gate/pallas_call | solution.py:1057
  117.9 1.6 collective-permute-start.14
  120.1 1.9 collective-permute-done.14
  122.0 1.2 collective-permute-done.15
  123.2 1.4 add_add_fusion.stat_ref
  124.6 13.1 %norm_back.1 = (bf16[2,256,1024]{2,1,0:T(8,128)(2,1)}, bf16[2,256,1024]{2,1,0:T(8,128)(2,1)}, bf16[4,256,512]{2,1,0:T(8,128)(2,1)}, bf16[4,256,512]{2,1,0:T(8,12...) custom-call(s32[4]{0:T(128)} %broadcast_xor_fusion.1.perm_ref, s32[3]{0:T(128)} %pad_add_fusion.here_ref, ...), custom_call_target="tpu_custom_call" | custom-call | flops 14300000256 | bytes 46800000 | tf_op jit(solution)/shard_map/norm_back/pallas_call | solution.py:1091
  137.7 1.6 collective-permute-start.18
  139.3 21.8 %scan_back.1 = (bf16[4,128,512]{2,1,0:T(8,128)(2,1)}, bf16[4,128,512]{2,1,0:T(8,128)(2,1)}, bf16[1024,512]{1,0:T(8,128)(2,1)}, bf16[1024,256]{1,0:T(8,128)(2,1)}...) custom-call(s32[4]{0:T(128)} %broadcast_xor_fusion.1.perm_ref, ...), custom_call_target="tpu_custom_call" | custom-call | flops 23100000256 | bytes 75600000 | tf_op jit(solution)/shard_map/scan_back/pallas_call | solution.py:1137
  162.0 1.3 collective-permute-done.21
  163.3 1.2 add_convert_fusion.dbc_ref
  165.1 1.0 copy-done.28
  166.1 2.7 pair_sum_early.1
  168.8 8.3 %hidden_back.1 = (bf16[2,256,1024]{2,1,0:T(8,128)(2,1)}, bf16[2,256,1024]{2,1,0:T(8,128)(2,1)}, f32[8,1024]{1,0:T(8,128)}) custom-call(s32[4]{0:T(128)} %broadcast_xor_fusion.1.perm_ref, bf16[1024,512]{1,0:T(8,128)(2,1)} %get-tuple-element.119.dgate_ref, bf16[1024,512]{1,0:T(8,128)(2,1)} %get-tuple-element.137.dval_ref, ...), custom_call_target="tpu_custom_call" | custom-call | flops 8800000000 | bytes 28800000 | tf_op jit(solution)/shard_map/hidden_back/pallas_call | solution.py:1211
  177.1 1.5 collective-permute-done.22.dbcfar_ref
  178.5 0.8 copy-done.32
  179.3 6.3 %maps_back.1 = (bf16[160,512]{1,0:T(8,128)(2,1)}, bf16[160,512]{1,0:T(8,128)(2,1)}, f32[256,1024]{1,0:T(8,128)}) custom-call(s32[3]{0:T(128)} %pad_add_fusion.here_ref, bf16[1024,256]{1,0:T(8,128)(2,1)} %copy-done.5, bf16[1024,256]{1,0:T(8,128)(2,1)} %copy-done.32, f32[1024,768]{1,0:T(8,128)} %get-tuple-element.122.convsum_ref, ...), custom_call_target="tpu_custom_call" | custom-call | flops 6600000000 | bytes 21600000 | tf_op jit(solution)/shard_map/maps_back/pallas_call | solution.py:1243
  186.1 8.4 %collective-permute-start.23 = (bf16[256,512]{1,0:T(8,128)(2,1)S(1)}, bf16[256,512]{1,0:T(8,128)(2,1)S(1)}, u32[]{:S(2)}, u32[]{:S(2)}) collective-permute-start(bf16[256,512]{1,0:T(8,128)(2,1)S(1)} %copy-done.39), channel_id=1, source_target_pairs={{0,8},{4,12},{8,0},{12,4},{16,24},{20,28},{24,16},{28,20},{1,9},{5... | collective-permute-start | bytes 786440 | tf_op jit(solution)/shard_map/ppermute | solution.py:858
  194.5 2.0 collective-permute-start.24
  196.5 1.5 collective-permute-start.25
  198.3 0.8 collective-permute-start.17
  199.1 2.3 pair_sum_late.1
  201.3 3.4 %collective-permute-done.23.part_refs_1_ = bf16[256,512]{1,0:T(8,128)(2,1)S(1)} collective-permute-done((bf16[256,512]{1,0:T(8,128)(2,1)S(1)}, bf16[256,512]{1,0:T(8,128)(2,1)S(1)}, u32[]{:S(2)}, u32[]{:S(2)}) %collective-permute-start.23) | collective-permute-done | bytes 262176 | tf_op jit(solution)/shard_map/ppermute | solution.py:858
  204.8 10.7 %collective-permute-done.24.part_refs_2_ = bf16[256,512]{1,0:T(8,128)(2,1)S(1)} collective-permute-done((bf16[256,512]{1,0:T(8,128)(2,1)S(1)}, bf16[256,512]{1,0:T(8,128)(2,1)S(1)}, u32[]{:S(2)}, u32[]{:S(2)}) %collective-permute-start.24) | collective-permute-done | bytes 262176 | tf_op jit(solution)/shard_map/ppermute | solution.py:858
  215.5 0.9 collective-permute-done.25.part_refs_3_
  216.4 4.5 %collective-permute-start.33 = (bf16[192,512]{1,0:T(8,128)(2,1)}, bf16[192,512]{1,0:T(8,128)(2,1)S(1)}, u32[]{:S(2)}, u32[]{:S(2)}) collective-permute-start(bf16[192,512]{1,0:T(8,128)(2,1)} %get-tuple-element.163), channel_id=1, source_target_pairs={{0,24},{4,28},{8,16},{12,20},{16,8},{20,12},{24,0},{28,4},{1,25},{... | collective-permute-start | bytes 589832 | tf_op jit(solution)/shard_map/ppermute | solution.py:858
  220.9 2.0 sum_early.1.early_refs_0_
  222.9 11.2 %collective-permute-done.32.part_refs_2_ = bf16[192,512]{1,0:T(8,128)(2,1)S(1)} collective-permute-done((bf16[192,512]{1,0:T(8,128)(2,1)}, bf16[192,512]{1,0:T(8,128)(2,1)S(1)}, u32[]{:S(2)}, u32[]{:S(2)}) %collective-permute-start.32) | collective-permute-done | bytes 196640 | tf_op jit(solution)/shard_map/ppermute | solution.py:858
  234.1 0.7 collective-permute-start.27
  235.5 2.1 sum_late.1.late_refs_0_
  237.5 0.8 slice_bitcast_fusion.4
  238.4 1.1 collective-permute-start.36
  239.5 1.3 fusion.1
  240.8 1.4 collective-permute-start.35
  242.1 1.2 collective-permute-done.27.early_refs_2_
  243.3 3.4 %collective-permute-done.28.early_refs_3_ = bf16[256,512]{1,0:T(8,128)(2,1)S(1)} collective-permute-done((bf16[256,512]{1,0:T(8,128)(2,1)}, bf16[256,512]{1,0:T(8,128)(2,1)S(1)}, u32[]{:S(2)}, u32[]{:S(2)}) %collective-permute-start.28) | collective-permute-done | bytes 262176 | tf_op jit(solution)/shard_map/ppermute | solution.py:858
  246.7 0.7 copy-done.36
  247.4 5.5 %adam_out.1 = (f32[256,1024]{1,0:T(8,128)}, f32[256,1024]{1,0:T(8,128)}, f32[256,1024]{1,0:T(8,128)}) custom-call(s32[3]{0:T(128)} %pad_add_fusion.here_ref, f32[256,1024]{1,0:T(8,128)} %weight_ref.3, f32[256,1024]{1,0:T(8,128)} %first_ref.3, f32[256,1024]{1,0:T(8,128)} %second_ref.3, bf16[256,512]{1,0:T(8,128)(2,1)} %sum_early.1.early_refs_0_, ...), custom_call_target="tpu_custom_call" | custom-call | flops 4400000000 | bytes 14400000 | tf_op jit(solution)/shard_map/adam_out/pallas_call | solution.py:1341
  253.1 1.6 collective-permute-done.35.late_refs_2_
  257.3 0.7 multiply_subtract_fusion.3
  258.0 0.7 multiply_subtract_fusion.1
  259.6 0.8 collective-permute-start.20
  260.4 8.3 %adam_in.1 = (f32[128,4352]{1,0:T(8,128)}, f32[128,4352]{1,0:T(8,128)}, f32[128,4352]{1,0:T(8,128)}) custom-call(s32[3]{0:T(128)} %pad_add_fusion.here_ref, f32[128,4352]{1,0:T(8,128)} %weight_ref.2, f32[128,4352]{1,0:T(8,128)} %first_ref.2, f32[128,4352]{1,0:T(8,128)} %second_ref.2, bf16[256,512]{1,0:T(8,128)(2,1)} %sum_early.1.early_refs_0_, ...), custom_call_target="tpu_custom_call" | custom-call | flops 7699999744 | bytes 25200000 | tf_op jit(solution)/shard_map/adam_in/pallas_call | solution.py:1355
  268.7 5.3 %collective-permute-done.20.far_ref = bf16[256,1024]{1,0:T(8,128)(2,1)S(1)} collective-permute-done((bf16[256,1024]{1,0:T(8,128)(2,1)S(1)}, bf16[256,1024]{1,0:T(8,128)(2,1)S(1)}, u32[]{:S(2)}, u32[]{:S(2)}) %collective-permute-start.20) | collective-permute-done | bytes 524320 | tf_op jit(solution)/shard_map/ppermute | solution.py:858
  274.0 0.8 copy-done.33
  274.8 3.9 %input_back.1 = f32[256,1024]{1,0:T(8,128)} custom-call(bf16[2,256,1024]{2,1,0:T(8,128)(2,1)} %get-tuple-element.143.keep_ref, bf16[2,256,1024]{2,1,0:T(8,128)(2,1)} %copy-done.7, bf16[256,1024]{1,0:T(8,128)(2,1)} %copy-done.33, f32[256,1024]{1,0:T(8,128)} %get-tuple-element.151.own_ref, f32[256,1024]{1,0:T(8,128)} %bitcast.57, ...), custom_call_target="tpu_custom_call" | custom-call | flops 4400000000 | bytes 14400000 | tf_op jit(solution)/shard_map/input_back/pallas_call | solution.py:1297
  (188 shorter events, 9.8 us)
Async XLA Ops:
  7.2 100.3 %all-gather.3.cloned.1.call-start = ((), (), s32[]{:S(2)}) async-start(), calls=%async_computation | async-start | bytes 2359296 | tf_op jit(solution)/shard_map/all_gather | solution.py:965
  7.9 33.7 %copy-start.14 = (f32[3,32]{1,0:T(4,128)S(1)}, f32[3,32]{1,0:T(4,128)}, u32[]{:S(2)}) copy-start(f32[3,32]{1,0:T(4,128)} %param.31) | copy-start | bytes 1156
  7.9 34.6 %copy-start.20 = (s32[1,1024]{1,0:T(1,128)S(1)}, s32[1,1024]{1,0:T(1,128)}, u32[]{:S(2)}) copy-start(s32[1,1024]{1,0:T(1,128)} %segr_ref.3) | copy-start | bytes 12292
  7.9 48.3 %copy-start.3 = (f32[1,256,1024]{2,1,0:T(8,128)S(1)}, f32[1,256,1024]{2,1,0:T(8,128)}, u32[]{:S(2)}) copy-start(f32[1,256,1024]{2,1,0:T(8,128)} %param.25) | copy-start | bytes 3145732
  11.0 60.3 %copy-start.53 = (s32[8]{0:T(128)S(1)}, s32[8]{0:T(128)}, u32[]{:S(2)}) copy-start(s32[8]{0:T(128)} %constant.15.clone) | copy-start | bytes 100
  11.0 26.2 %collective-permute-start.1 = (f32[256,1024]{1,0:T(8,128)S(1)}, f32[256,1024]{1,0:T(8,128)S(1)}, u32[]{:S(2)}, u32[]{:S(2)}) collective-permute-start(f32[256,1024]{1,0:T(8,128)S(1)} %bitcast.58), channel_id=1, source_target_pairs={{0,2},{1,3},{2,0},{3,1},{4,6},{5,7},{6,4},{7,5},{8,10},{9,11},{10,... | collective-permute-start | bytes 3145736 | tf_op jit(solution)/shard_map/ppermute | solution.py:858
  14.0 70.1 %collective-permute-start = (f32[256,1024]{1,0:T(8,128)S(1)}, f32[256,1024]{1,0:T(8,128)}, u32[]{:S(2)}, u32[]{:S(2)}) collective-permute-start(f32[256,1024]{1,0:T(8,128)S(1)} %bitcast.59), channel_id=1, source_target_pairs={{0,1},{1,0},{2,3},{3,2},{4,5},{5,4},{6,7},{7,6},{8,9},{9,8},{10,11... | collective-permute-start | bytes 3145736 | tf_op jit(solution)/shard_map/ppermute | solution.py:858
  37.1 46.9 %copy-start.27 = (f32[256,1024]{1,0:T(8,128)}, f32[256,1024]{1,0:T(8,128)S(1)}, u32[]{:S(2)}) copy-start(f32[256,1024]{1,0:T(8,128)S(1)} %collective-permute-done.1.tok_pieces_2_) | copy-start | bytes 3145732
  37.1 46.9 %collective-permute-start.2 = (f32[256,1024]{1,0:T(8,128)S(1)}, f32[256,1024]{1,0:T(8,128)}, u32[]{:S(2)}, u32[]{:S(2)}) collective-permute-start(f32[256,1024]{1,0:T(8,128)S(1)} %collective-permute-done.1.tok_pieces_2_), channel_id=1, source_target_pairs={{0,1},{1,0},{2,3},{3,2},{4,5},{5,4},{6,7},{7,6},{8,9},{9,8},{10,11... | collective-permute-start | bytes 3145736 | tf_op jit(solution)/shard_map/ppermute | solution.py:858
  37.1 17.2 %collective-permute-start.3 = (bf16[1,144,768]{2,1,0:T(8,128)(2,1)}, bf16[1,144,768]{2,1,0:T(8,128)(2,1)S(1)}, u32[]{:S(2)}, u32[]{:S(2)}) collective-permute-start(bf16[1,144,768]{2,1,0:T(8,128)(2,1)} %bitcast.72), channel_id=1, source_target_pairs={{0,8},{4,12},{8,0},{12,4},{16,24},{20,28},{24,16},{28,20},{1,9},{5... | collective-permute-start | bytes 663560 | tf_op jit(solution)/shard_map/ppermute | solution.py:858
  38.9 27.8 %collective-permute-start.4 = (bf16[1,144,768]{2,1,0:T(8,128)(2,1)}, bf16[1,144,768]{2,1,0:T(8,128)(2,1)}, u32[]{:S(2)}, u32[]{:S(2)}) collective-permute-start(bf16[1,144,768]{2,1,0:T(8,128)(2,1)} %bitcast.73), channel_id=1, source_target_pairs={{0,16},{4,20},{8,24},{12,28},{16,0},{20,4},{24,8},{28,12},{1,17},{... | collective-permute-start | bytes 663560 | tf_op jit(solution)/shard_map/ppermute | solution.py:858
  41.5 27.7 %collective-permute-start.5 = (bf16[1,144,768]{2,1,0:T(8,128)(2,1)}, bf16[1,144,768]{2,1,0:T(8,128)(2,1)}, u32[]{:S(2)}, u32[]{:S(2)}) collective-permute-start(bf16[1,144,768]{2,1,0:T(8,128)(2,1)} %bitcast.74), channel_id=1, source_target_pairs={{0,24},{4,28},{8,16},{12,20},{16,8},{20,12},{24,0},{28,4},{1,25},{... | collective-permute-start | bytes 663560 | tf_op jit(solution)/shard_map/ppermute | solution.py:858
  41.8 42.3 %copy-start.15 = (f32[3,8]{1,0:T(4,128)}, f32[3,8]{1,0:T(4,128)S(1)}, u32[]{:S(2)}) copy-start(f32[3,8]{1,0:T(4,128)S(1)} %dynamic-slice_reduce_fusion.hrow_ref) | copy-start | bytes 292
  54.3 29.8 %copy-start.43 = (bf16[1,144,768]{2,1,0:T(8,128)(2,1)}, bf16[1,144,768]{2,1,0:T(8,128)(2,1)S(1)}, u32[]{:S(2)}) copy-start(bf16[1,144,768]{2,1,0:T(8,128)(2,1)S(1)} %collective-permute-done.3.w1_pieces_1_) | copy-start | bytes 663556
  54.3 16.4 %collective-permute-start.6 = (bf16[1,144,768]{2,1,0:T(8,128)(2,1)}, bf16[1,144,768]{2,1,0:T(8,128)(2,1)S(1)}, u32[]{:S(2)}, u32[]{:S(2)}) collective-permute-start(bf16[1,144,768]{2,1,0:T(8,128)(2,1)} %bitcast.75), channel_id=1, source_target_pairs={{0,4},{4,0},{8,12},{12,8},{16,20},{20,16},{24,28},{28,24},{1,5},{5... | collective-permute-start | bytes 663560 | tf_op jit(solution)/shard_map/ppermute | solution.py:858
  56.3 46.0 %copy-start.4 = (bf16[256,1024]{1,0:T(8,128)(2,1)}, bf16[256,1024]{1,0:T(8,128)(2,1)S(1)}, u32[]{:S(2)}) copy-start(bf16[256,1024]{1,0:T(8,128)(2,1)S(1)} %bitcast_convert_fusion.cot_pieces_0_) | copy-start | bytes 1572868
  66.8 7.7 %collective-permute-start.7 = (bf16[1,144,768]{2,1,0:T(8,128)(2,1)S(1)}, bf16[1,144,768]{2,1,0:T(8,128)(2,1)S(1)}, u32[]{:S(2)}, u32[]{:S(2)}) collective-permute-start(bf16[1,144,768]{2,1,0:T(8,128)(2,1)S(1)} %collective-permute-done.3.w1_pieces_1_), channel_id=1, source_target_pairs={{0,4},{4,0},{8,12},{12,8},{16,20},{20,16},{24,28},{28,24},{1,5},{5... | collective-permute-start | bytes 663560 | tf_op jit(solution)/shard_map/ppermute | solution.py:858
  69.2 10.0 %collective-permute-start.8 = (bf16[1,144,768]{2,1,0:T(8,128)(2,1)}, bf16[1,144,768]{2,1,0:T(8,128)(2,1)S(1)}, u32[]{:S(2)}, u32[]{:S(2)}) collective-permute-start(bf16[1,144,768]{2,1,0:T(8,128)(2,1)} %collective-permute-done.4.w1_pieces_2_), channel_id=1, source_target_pairs={{0,4},{4,0},{8,12},{12,8},{16,20},{20,16},{24,28},{28,24},{1,5},{5... | collective-permute-start | bytes 663560 | tf_op jit(solution)/shard_map/ppermute | solution.py:858
  70.7 13.4 %copy-start.44 = (bf16[1,144,768]{2,1,0:T(8,128)(2,1)}, bf16[1,144,768]{2,1,0:T(8,128)(2,1)S(1)}, u32[]{:S(2)}) copy-start(bf16[1,144,768]{2,1,0:T(8,128)(2,1)S(1)} %collective-permute-done.6.w1_pieces_4_) | copy-start | bytes 663556
  70.7 11.5 %collective-permute-start.9 = (bf16[1,144,768]{2,1,0:T(8,128)(2,1)}, bf16[1,144,768]{2,1,0:T(8,128)(2,1)S(1)}, u32[]{:S(2)}, u32[]{:S(2)}) collective-permute-start(bf16[1,144,768]{2,1,0:T(8,128)(2,1)} %collective-permute-done.5.w1_pieces_3_), channel_id=1, source_target_pairs={{0,4},{4,0},{8,12},{12,8},{16,20},{20,16},{24,28},{28,24},{1,5},{5... | collective-permute-start | bytes 663560 | tf_op jit(solution)/shard_map/ppermute | solution.py:858
  74.5 9.6 %copy-start.45 = (bf16[1,144,768]{2,1,0:T(8,128)(2,1)}, bf16[1,144,768]{2,1,0:T(8,128)(2,1)S(1)}, u32[]{:S(2)}) copy-start(bf16[1,144,768]{2,1,0:T(8,128)(2,1)S(1)} %collective-permute-done.7.w1_pieces_5_) | copy-start | bytes 663556
  82.2 20.2 %collective-permute-start.10 = (bf16[256,1024]{1,0:T(8,128)(2,1)S(1)}, bf16[256,1024]{1,0:T(8,128)(2,1)S(1)}, u32[]{:S(2)}, u32[]{:S(2)}) collective-permute-start(bf16[256,1024]{1,0:T(8,128)(2,1)S(1)} %bitcast_convert_fusion.cot_pieces_0_), channel_id=1, source_target_pairs={{0,1},{1,0},{2,3},{3,2},{4,5},{5,4},{6,7},{7,6},{8,9},{9,8},{10,11... | collective-permute-start | bytes 1572872 | tf_op jit(solution)/shard_map/ppermute | solution.py:858
  82.2 20.2 %collective-permute-start.11 = (bf16[256,1024]{1,0:T(8,128)(2,1)S(1)}, bf16[256,1024]{1,0:T(8,128)(2,1)S(1)}, u32[]{:S(2)}, u32[]{:S(2)}) collective-permute-start(bf16[256,1024]{1,0:T(8,128)(2,1)S(1)} %bitcast_convert_fusion.cot_pieces_0_), channel_id=1, source_target_pairs={{0,2},{1,3},{2,0},{3,1},{4,6},{5,7},{6,4},{7,5},{8,10},{9,11},{10,... | collective-permute-start | bytes 1572872 | tf_op jit(solution)/shard_map/ppermute | solution.py:858
  83.8 23.7 %collective-permute-start.12 = (bf16[256,1024]{1,0:T(8,128)(2,1)S(1)}, bf16[256,1024]{1,0:T(8,128)(2,1)}, u32[]{:S(2)}, u32[]{:S(2)}) collective-permute-start(bf16[256,1024]{1,0:T(8,128)(2,1)S(1)} %bitcast_convert_fusion.cot_pieces_0_), channel_id=1, source_target_pairs={{0,3},{1,2},{2,1},{3,0},{4,7},{5,6},{6,5},{7,4},{8,11},{9,10},{10,... | collective-permute-start | bytes 1572872 | tf_op jit(solution)/shard_map/ppermute | solution.py:858
  107.5 12.1 %copy-start.52 = (s32[4]{0:T(128)S(1)}, s32[4]{0:T(128)}, u32[]{:S(2)}) copy-start(s32[4]{0:T(128)} %constant.54.clone) | copy-start | bytes 52
  117.6 2.5 collective-permute-start.13
  117.9 4.1 %collective-permute-start.14 = (f32[8,1024]{1,0:T(8,128)}, f32[8,1024]{1,0:T(8,128)S(1)}, u32[]{:S(2)}, u32[]{:S(2)}) collective-permute-start(f32[8,1024]{1,0:T(8,128)} %get-tuple-element.113), channel_id=1, source_target_pairs={{0,2},{1,3},{2,0},{3,1},{4,6},{5,7},{6,4},{7,5},{8,10},{9,11},{10,... | collective-permute-start | bytes 98312 | tf_op jit(solution)/shard_map/ppermute | solution.py:858
  119.5 3.7 %collective-permute-start.15 = (f32[8,1024]{1,0:T(8,128)}, f32[8,1024]{1,0:T(8,128)S(1)}, u32[]{:S(2)}, u32[]{:S(2)}) collective-permute-start(f32[8,1024]{1,0:T(8,128)} %get-tuple-element.113), channel_id=1, source_target_pairs={{0,3},{1,2},{2,1},{3,0},{4,7},{5,6},{6,5},{7,4},{8,11},{9,10},{10,... | collective-permute-start | bytes 98312 | tf_op jit(solution)/shard_map/ppermute | solution.py:858
  137.7 27.4 %collective-permute-start.18 = (bf16[4,256,512]{2,1,0:T(8,128)(2,1)}, bf16[4,256,512]{2,1,0:T(8,128)(2,1)S(1)}, u32[]{:S(2)}, u32[]{:S(2)}) collective-permute-start(bf16[4,256,512]{2,1,0:T(8,128)(2,1)} %get-tuple-element.132), channel_id=1, source_target_pairs={{0,4},{4,0},{8,12},{12,8},{16,20},{20,16},{24,28},{28,24},{1,5},{5... | collective-permute-start | bytes 3145736 | tf_op jit(solution)/shard_map/ppermute | solution.py:858
  139.3 22.5 %copy-start.26 = (bf16[2,256,1024]{2,1,0:T(8,128)(2,1)S(1)}, bf16[2,256,1024]{2,1,0:T(8,128)(2,1)}, u32[]{:S(2)}) copy-start(bf16[2,256,1024]{2,1,0:T(8,128)(2,1)} %get-tuple-element.118) | copy-start | bytes 3145732
  161.1 2.2 collective-permute-start.21
  161.2 37.0 %collective-permute-start.29 = (bf16[4,128,512]{2,1,0:T(8,128)(2,1)}, bf16[4,128,512]{2,1,0:T(8,128)(2,1)S(1)}, u32[]{:S(2)}, u32[]{:S(2)}) collective-permute-start(bf16[4,128,512]{2,1,0:T(8,128)(2,1)} %get-tuple-element.157), channel_id=1, source_target_pairs={{0,4},{4,0},{8,12},{12,8},{16,20},{20,16},{24,28},{28,24},{1,5},{5... | collective-permute-start | bytes 1572872 | tf_op jit(solution)/shard_map/ppermute | solution.py:858
  161.8 34.7 %collective-permute-start.16 = (bf16[2,256,1024]{2,1,0:T(8,128)(2,1)S(1)}, bf16[2,256,1024]{2,1,0:T(8,128)(2,1)S(1)}, u32[]{:S(2)}, u32[]{:S(2)}) collective-permute-start(bf16[2,256,1024]{2,1,0:T(8,128)(2,1)S(1)} %copy-done.26), channel_id=1, source_target_pairs={{0,1},{1,0},{2,3},{3,2},{4,5},{5,4},{6,7},{7,6},{8,9},{9,8},{10,11... | collective-permute-start | bytes 3145736 | tf_op jit(solution)/shard_map/ppermute | solution.py:858
  164.5 14.0 %collective-permute-start.22 = (bf16[1024,256]{1,0:T(8,128)(2,1)S(1)}, bf16[1024,256]{1,0:T(8,128)(2,1)S(1)}, u32[]{:S(2)}, u32[]{:S(2)}) collective-permute-start(bf16[1024,256]{1,0:T(8,128)(2,1)S(1)} %add_convert_fusion.dbc_ref), channel_id=1, source_target_pairs={{0,2},{1,3},{2,0},{3,1},{4,6},{5,7},{6,4},{7,5},{8,10},{9,11},{10,... | collective-permute-start | bytes 1572872 | tf_op jit(solution)/shard_map/ppermute | solution.py:858
  179.3 6.8 %copy-start.39 = (bf16[256,512]{1,0:T(8,128)(2,1)S(1)}, bf16[256,512]{1,0:T(8,128)(2,1)}, u32[]{:S(2)}) copy-start(bf16[256,512]{1,0:T(8,128)(2,1)} %get-tuple-element.153) | copy-start | bytes 786436
  179.3 15.2 %copy-start.38 = (bf16[256,512]{1,0:T(8,128)(2,1)S(1)}, bf16[256,512]{1,0:T(8,128)(2,1)}, u32[]{:S(2)}) copy-start(bf16[256,512]{1,0:T(8,128)(2,1)} %get-tuple-element.154) | copy-start | bytes 786436
  179.3 17.2 %copy-start.37 = (bf16[256,512]{1,0:T(8,128)(2,1)S(1)}, bf16[256,512]{1,0:T(8,128)(2,1)}, u32[]{:S(2)}) copy-start(bf16[256,512]{1,0:T(8,128)(2,1)} %get-tuple-element.155) | copy-start | bytes 786436
  179.3 18.7 %copy-start.2 = (bf16[2,256,1024]{2,1,0:T(8,128)(2,1)S(1)}, bf16[2,256,1024]{2,1,0:T(8,128)(2,1)}, u32[]{:S(2)}) copy-start(bf16[2,256,1024]{2,1,0:T(8,128)(2,1)} %get-tuple-element.117) | copy-start | bytes 3145732
  185.6 12.7 %collective-permute-start.30 = (bf16[160,512]{1,0:T(8,128)(2,1)}, bf16[160,512]{1,0:T(8,128)(2,1)S(1)}, u32[]{:S(2)}, u32[]{:S(2)}) collective-permute-start(bf16[160,512]{1,0:T(8,128)(2,1)} %get-tuple-element.159), channel_id=1, source_target_pairs={{0,4},{4,0},{8,12},{12,8},{16,20},{20,16},{24,28},{28,24},{1,5},{5... | collective-permute-start | bytes 491528 | tf_op jit(solution)/shard_map/ppermute | solution.py:858
  186.1 18.6 %collective-permute-start.23 = (bf16[256,512]{1,0:T(8,128)(2,1)S(1)}, bf16[256,512]{1,0:T(8,128)(2,1)S(1)}, u32[]{:S(2)}, u32[]{:S(2)}) collective-permute-start(bf16[256,512]{1,0:T(8,128)(2,1)S(1)} %copy-done.39), channel_id=1, source_target_pairs={{0,8},{4,12},{8,0},{12,4},{16,24},{20,28},{24,16},{28,20},{1,9},{5... | collective-permute-start | bytes 786440 | tf_op jit(solution)/shard_map/ppermute | solution.py:858
  194.5 21.0 %collective-permute-start.24 = (bf16[256,512]{1,0:T(8,128)(2,1)S(1)}, bf16[256,512]{1,0:T(8,128)(2,1)S(1)}, u32[]{:S(2)}, u32[]{:S(2)}) collective-permute-start(bf16[256,512]{1,0:T(8,128)(2,1)S(1)} %copy-done.38), channel_id=1, source_target_pairs={{0,16},{4,20},{8,24},{12,28},{16,0},{20,4},{24,8},{28,12},{1,17},{... | collective-permute-start | bytes 786440 | tf_op jit(solution)/shard_map/ppermute | solution.py:858
  196.5 19.9 %collective-permute-start.25 = (bf16[256,512]{1,0:T(8,128)(2,1)S(1)}, bf16[256,512]{1,0:T(8,128)(2,1)S(1)}, u32[]{:S(2)}, u32[]{:S(2)}) collective-permute-start(bf16[256,512]{1,0:T(8,128)(2,1)S(1)} %copy-done.37), channel_id=1, source_target_pairs={{0,24},{4,28},{8,16},{12,20},{16,8},{20,12},{24,0},{28,4},{1,25},{... | collective-permute-start | bytes 786440 | tf_op jit(solution)/shard_map/ppermute | solution.py:858
  198.2 61.2 %collective-permute-start.19 = (bf16[2,256,1024]{2,1,0:T(8,128)(2,1)}, bf16[2,256,1024]{2,1,0:T(8,128)(2,1)S(1)}, u32[]{:S(2)}, u32[]{:S(2)}) collective-permute-start(bf16[2,256,1024]{2,1,0:T(8,128)(2,1)} %get-tuple-element.144), channel_id=1, source_target_pairs={{0,1},{1,0},{2,3},{3,2},{4,5},{5,4},{6,7},{7,6},{8,9},{9,8},{10,11... | collective-permute-start | bytes 3145736 | tf_op jit(solution)/shard_map/ppermute | solution.py:858
  198.3 40.1 %collective-permute-start.17 = (bf16[256,1024]{1,0:T(8,128)(2,1)S(1)}, bf16[256,1024]{1,0:T(8,128)(2,1)S(1)}, u32[]{:S(2)}, u32[]{:S(2)}) collective-permute-start(bf16[256,1024]{1,0:T(8,128)(2,1)S(1)} %fusion.2), channel_id=1, source_target_pairs={{0,2},{1,3},{2,0},{3,1},{4,6},{5,7},{6,4},{7,5},{8,10},{9,11},{10,... | collective-permute-start | bytes 1572872 | tf_op jit(solution)/shard_map/ppermute | solution.py:858
  204.8 16.1 %copy-start.40 = (bf16[256,512]{1,0:T(8,128)(2,1)}, bf16[256,512]{1,0:T(8,128)(2,1)S(1)}, u32[]{:S(2)}) copy-start(bf16[256,512]{1,0:T(8,128)(2,1)S(1)} %collective-permute-done.23.part_refs_1_) | copy-start | bytes 786436
  204.8 18.1 %collective-permute-start.31 = (bf16[192,512]{1,0:T(8,128)(2,1)}, bf16[192,512]{1,0:T(8,128)(2,1)S(1)}, u32[]{:S(2)}, u32[]{:S(2)}) collective-permute-start(bf16[192,512]{1,0:T(8,128)(2,1)} %get-tuple-element.161), channel_id=1, source_target_pairs={{0,8},{4,12},{8,0},{12,4},{16,24},{20,28},{24,16},{28,20},{1,9},{5... | collective-permute-start | bytes 589832 | tf_op jit(solution)/shard_map/ppermute | solution.py:858
  215.5 5.4 %copy-start.41 = (bf16[256,512]{1,0:T(8,128)(2,1)}, bf16[256,512]{1,0:T(8,128)(2,1)S(1)}, u32[]{:S(2)}) copy-start(bf16[256,512]{1,0:T(8,128)(2,1)S(1)} %collective-permute-done.24.part_refs_2_) | copy-start | bytes 786436
  215.5 18.6 %collective-permute-start.32 = (bf16[192,512]{1,0:T(8,128)(2,1)}, bf16[192,512]{1,0:T(8,128)(2,1)S(1)}, u32[]{:S(2)}, u32[]{:S(2)}) collective-permute-start(bf16[192,512]{1,0:T(8,128)(2,1)} %get-tuple-element.162), channel_id=1, source_target_pairs={{0,16},{4,20},{8,24},{12,28},{16,0},{20,4},{24,8},{28,12},{1,17},{... | collective-permute-start | bytes 589832 | tf_op jit(solution)/shard_map/ppermute | solution.py:858
  216.4 18.4 %collective-permute-start.33 = (bf16[192,512]{1,0:T(8,128)(2,1)}, bf16[192,512]{1,0:T(8,128)(2,1)S(1)}, u32[]{:S(2)}, u32[]{:S(2)}) collective-permute-start(bf16[192,512]{1,0:T(8,128)(2,1)} %get-tuple-element.163), channel_id=1, source_target_pairs={{0,24},{4,28},{8,16},{12,20},{16,8},{20,12},{24,0},{28,4},{1,25},{... | collective-permute-start | bytes 589832 | tf_op jit(solution)/shard_map/ppermute | solution.py:858
  222.9 11.9 %copy-start.48 = (bf16[192,512]{1,0:T(8,128)(2,1)}, bf16[192,512]{1,0:T(8,128)(2,1)S(1)}, u32[]{:S(2)}) copy-start(bf16[192,512]{1,0:T(8,128)(2,1)S(1)} %collective-permute-done.31.part_refs_1_) | copy-start | bytes 589828
  222.9 17.9 %collective-permute-start.26 = (bf16[256,512]{1,0:T(8,128)(2,1)}, bf16[256,512]{1,0:T(8,128)(2,1)S(1)}, u32[]{:S(2)}, u32[]{:S(2)}) collective-permute-start(bf16[256,512]{1,0:T(8,128)(2,1)} %sum_early.1.early_refs_0_), channel_id=1, source_target_pairs={{0,1},{1,0},{2,3},{3,2},{4,5},{5,4},{6,7},{7,6},{8,9},{9,8},{10,11... | collective-permute-start | bytes 786440 | tf_op jit(solution)/shard_map/ppermute | solution.py:858
  234.1 9.2 %collective-permute-start.27 = (bf16[256,512]{1,0:T(8,128)(2,1)}, bf16[256,512]{1,0:T(8,128)(2,1)S(1)}, u32[]{:S(2)}, u32[]{:S(2)}) collective-permute-start(bf16[256,512]{1,0:T(8,128)(2,1)} %sum_early.1.early_refs_0_), channel_id=1, source_target_pairs={{0,2},{1,3},{2,0},{3,1},{4,6},{5,7},{6,4},{7,5},{8,10},{9,11},{10,... | collective-permute-start | bytes 786440 | tf_op jit(solution)/shard_map/ppermute | solution.py:858
  234.8 11.9 %collective-permute-start.28 = (bf16[256,512]{1,0:T(8,128)(2,1)}, bf16[256,512]{1,0:T(8,128)(2,1)S(1)}, u32[]{:S(2)}, u32[]{:S(2)}) collective-permute-start(bf16[256,512]{1,0:T(8,128)(2,1)} %sum_early.1.early_refs_0_), channel_id=1, source_target_pairs={{0,3},{1,2},{2,1},{3,0},{4,7},{5,6},{6,5},{7,4},{8,11},{9,10},{10,... | collective-permute-start | bytes 786440 | tf_op jit(solution)/shard_map/ppermute | solution.py:858
  238.4 14.7 %collective-permute-start.36 = (bf16[192,512]{1,0:T(8,128)(2,1)}, bf16[192,512]{1,0:T(8,128)(2,1)S(1)}, u32[]{:S(2)}, u32[]{:S(2)}) collective-permute-start(bf16[192,512]{1,0:T(8,128)(2,1)} %sum_late.1.late_refs_0_), channel_id=1, source_target_pairs={{0,3},{1,2},{2,1},{3,0},{4,7},{5,6},{6,5},{7,4},{8,11},{9,10},{10,... | collective-permute-start | bytes 589832 | tf_op jit(solution)/shard_map/ppermute | solution.py:858
  240.8 6.0 %copy-start.34 = (bf16[256,512]{1,0:T(8,128)(2,1)}, bf16[256,512]{1,0:T(8,128)(2,1)S(1)}, u32[]{:S(2)}) copy-start(bf16[256,512]{1,0:T(8,128)(2,1)S(1)} %collective-permute-done.26.early_refs_1_) | copy-start | bytes 786436
  240.8 13.9 %collective-permute-start.35 = (bf16[192,512]{1,0:T(8,128)(2,1)S(1)}, bf16[192,512]{1,0:T(8,128)(2,1)S(1)}, u32[]{:S(2)}, u32[]{:S(2)}) collective-permute-start(bf16[192,512]{1,0:T(8,128)(2,1)S(1)} %copy-done.16), channel_id=1, source_target_pairs={{0,2},{1,3},{2,0},{3,1},{4,6},{5,7},{6,4},{7,5},{8,10},{9,11},{10,... | collective-permute-start | bytes 589832 | tf_op jit(solution)/shard_map/ppermute | solution.py:858
  243.3 11.4 %collective-permute-start.34 = (bf16[192,512]{1,0:T(8,128)(2,1)S(1)}, bf16[192,512]{1,0:T(8,128)(2,1)S(1)}, u32[]{:S(2)}, u32[]{:S(2)}) collective-permute-start(bf16[192,512]{1,0:T(8,128)(2,1)S(1)} %copy-done.16), channel_id=1, source_target_pairs={{0,1},{1,0},{2,3},{3,2},{4,5},{5,4},{6,7},{7,6},{8,9},{9,8},{10,11... | collective-permute-start | bytes 589832 | tf_op jit(solution)/shard_map/ppermute | solution.py:858
  253.0 5.7 %copy-start.8 = (f32[32,128]{1,0:T(8,128)S(1)}, f32[32,128]{1,0:T(8,128)}, u32[]{:S(2)}) copy-start(f32[32,128]{1,0:T(8,128)} %dt_ref.1) | copy-start | bytes 49156
  253.0 5.7 %copy-start.9 = (f32[32,128]{1,0:T(8,128)S(1)}, f32[32,128]{1,0:T(8,128)}, u32[]{:S(2)}) copy-start(f32[32,128]{1,0:T(8,128)} %param.34) | copy-start | bytes 49156
  253.1 5.7 %copy-start.10 = (f32[32,128]{1,0:T(8,128)S(1)}, f32[32,128]{1,0:T(8,128)}, u32[]{:S(2)}) copy-start(f32[32,128]{1,0:T(8,128)} %param.35) | copy-start | bytes 49156
  253.1 6.3 %copy-start.6 = (bf16[2,256,1024]{2,1,0:T(8,128)(2,1)S(1)}, bf16[2,256,1024]{2,1,0:T(8,128)(2,1)}, u32[]{:S(2)}) copy-start(bf16[2,256,1024]{2,1,0:T(8,128)(2,1)} %get-tuple-element.143.keep_ref) | copy-start | bytes 3145732
  253.1 6.5 %copy-start.17 = (bf16[192,512]{1,0:T(8,128)(2,1)}, bf16[192,512]{1,0:T(8,128)(2,1)S(1)}, u32[]{:S(2)}) copy-start(bf16[192,512]{1,0:T(8,128)(2,1)S(1)} %collective-permute-done.36.late_refs_3_) | copy-start | bytes 589828
  259.4 9.3 %copy-start.7 = (bf16[2,256,1024]{2,1,0:T(8,128)(2,1)}, bf16[2,256,1024]{2,1,0:T(8,128)(2,1)S(1)}, u32[]{:S(2)}) copy-start(bf16[2,256,1024]{2,1,0:T(8,128)(2,1)S(1)} %collective-permute-done.19.came_ref) | copy-start | bytes 3145732
  259.6 14.4 %collective-permute-start.20 = (bf16[256,1024]{1,0:T(8,128)(2,1)S(1)}, bf16[256,1024]{1,0:T(8,128)(2,1)S(1)}, u32[]{:S(2)}, u32[]{:S(2)}) collective-permute-start(bf16[256,1024]{1,0:T(8,128)(2,1)S(1)} %fusion.3), channel_id=1, source_target_pairs={{0,2},{1,3},{2,0},{3,1},{4,6},{5,7},{6,4},{7,5},{8,10},{9,11},{10,... | collective-permute-start | bytes 1572872 | tf_op jit(solution)/shard_map/ppermute | solution.py:858
  (28 other events, 91.3 us)
Sparse Core Ops, SparseCore 0:
  14.1 64.8 all-gather.2

commit v5 on v4

--- a/solution.py
+++ b/solution.py
@@ -91,19 +91,13 @@
     return jnp.where(keep, 1.0, 0.0).astype(F32)
 
 
-def cost(micros):
-    return pl.CostEstimate(
-        flops=int(micros * 1.1e9), bytes_accessed=int(micros * 3.6e6), transcendentals=0
-    )
-
-
 def params(*semantics):
     return pltpu.CompilerParams(
         dimension_semantics=semantics or None, vmem_limit_bytes=VMEM_LIMIT
     )
 
 
-def place(pieces, at_ref, sems, targets):
+def place(pieces, at_ref, stride, sems, targets):
     copies = []
     for index, piece in enumerate(pieces):
         for block in range(piece.shape[0]):
@@ -111,7 +105,7 @@
                 copies.append(
                     pltpu.make_async_copy(
                         piece.at[block, first : first + rows],
-                        target(at_ref[index] + block),
+                        target(at_ref[index] + stride * block),
                         sems.at[len(copies)],
                     )
                 )
@@ -158,9 +152,14 @@
     rows = win_ref.shape[0]
     heads = HEADS // 4
     width = heads * HEAD_DIM
+    copies = range(w1_ref.shape[0])
     for at, part in enumerate(pick_heads(win_ref, INNER, ctx, heads)):
-        w1_ref[0:rows, at * 128 : (at + 1) * 128] = part.astype(BF16)
-    w1_ref[0:rows, width:] = win_ref[:, 2 * INNER :].astype(BF16)
+        part = part.astype(BF16)
+        for copy in copies:
+            w1_ref[copy, 0:rows, at * 128 : (at + 1) * 128] = part
+    part = win_ref[:, 2 * INNER :].astype(BF16)
+    for copy in copies:
+        w1_ref[copy, 0:rows, width:] = part
     tmp_ref[...] = jnp.zeros_like(tmp_ref)
     row = lax.broadcasted_iota(jnp.int32, (heads, HEADS), 0)
     col = lax.broadcasted_iota(jnp.int32, (heads, HEADS), 1)
@@ -168,7 +167,8 @@
     tmp_ref[0:heads, 384 : 384 + dt_ref.shape[1]] = nn(table, dt_ref[...].astype(BF16))
     tmp_ref[8 : 8 + CONV + 1, 0 : conv_ref.shape[1]] = conv_ref[...]
     tmp_ref[8 + CONV + 1 : 8 + CONV + 2, 0 : gain_ref.shape[0]] = gain_ref[...].reshape(1, -1)
-    w1_ref[rows : rows + 16, :] = tmp_ref[...].astype(BF16)
+    for copy in copies:
+        w1_ref[copy, rows : rows + 16, :] = tmp_ref[...].astype(BF16)
     for at, part in enumerate(pick_heads(win_ref, 0, ctx, heads)):
         g2_ref[0:rows, at * 128 : (at + 1) * 128] = part.astype(BF16)
     if g2_ref.shape[0] > rows:
@@ -225,6 +225,7 @@
         copies = place(
             w1_pieces,
             at_ref,
+            len(w1_pieces),
             sems,
             [(0, rows, rows_of(w1_ref, rows)), (rows, 16, lambda at: small_ref.at[at])],
         )
@@ -350,6 +351,7 @@
         copies = place(
             g2_pieces,
             at_ref,
+            len(g2_pieces),
             sems,
             [
                 (0, rows, rows_of(wg_ref, rows)),
@@ -749,42 +751,34 @@
     out_ref[...] = cot_ref[...] + scale * (scaled - unit * mean)
 
 
-def pair_sum_kernel(here_ref, keep_ref, came_ref, out_refs):
-    for at, out_ref in enumerate(out_refs):
-        index = pl.ds(here_ref[1] ^ at, 1)
-        out_ref[...] = (keep_ref[index].astype(F32) + came_ref[index].astype(F32))[0].astype(BF16)
-
-
-def pair_sum_late_kernel(here_ref, keep_ref, came_ref, mkeep_ref, mcame_ref, out_refs):
-    rows, width = keep_ref.shape[1:]
-    small = (mkeep_ref[0:32].astype(F32) + mcame_ref[0:32].astype(F32))
-    row = lax.broadcasted_iota(jnp.int32, small.shape, 0)
-    head = small[7:8] + small[15:16]
+def pair_sum_kernel(keep_ref, came_ref, out_ref):
+    out_ref[...] = (keep_ref[...].astype(F32) + came_ref[...].astype(F32)).astype(BF16)
+
+
+def with_rest(value, first):
+    row = lax.broadcasted_iota(jnp.int32, value.shape, 0)
+    head = value[first + 7 : first + 8] + value[first + 15 : first + 16]
     rest = head - head.astype(BF16).astype(F32)
-    small = jnp.where(row == 7, head, jnp.where(row == 15, rest, small)).astype(BF16)
-    for at, out_ref in enumerate(out_refs):
-        block = here_ref[1] ^ at
-        index = pl.ds(block, 1)
-        out_ref[0:rows] = (keep_ref[index].astype(F32) + came_ref[index].astype(F32))[0].astype(BF16)
-        out_ref[rows : rows + 32] = small
-        index = pl.ds(pl.multiple_of(32 + 32 * block, 32), 32)
-        out_ref[rows + 32 : rows + 64] = (
-            mkeep_ref[index].astype(F32) + mcame_ref[index].astype(F32)
+    return jnp.where(row == first + 7, head, jnp.where(row == first + 15, rest, value))
+
+
+def pair_sum_late_kernel(keep_ref, came_ref, mkeep_ref, mcame_ref, out_ref):
+    count, rows, width = keep_ref.shape
+    small = with_rest(mkeep_ref[0:32].astype(F32) + mcame_ref[0:32].astype(F32), 0).astype(BF16)
+    for block in range(count):
+        out_ref[block, 0:rows] = (keep_ref[block].astype(F32) + came_ref[block].astype(F32)).astype(BF16)
+        out_ref[block, rows : rows + 32] = small
+        at = slice(32 + 32 * block, 64 + 32 * block)
+        out_ref[block, rows + 32 : rows + 64] = (
+            mkeep_ref[at].astype(F32) + mcame_ref[at].astype(F32)
         ).astype(BF16)
 
 
-def sum_kernel(late, part_refs, out_ref):
-    terms = [ref[...].astype(F32) for ref in part_refs]
-    while len(terms) > 1:
-        terms = [terms[at] + terms[at + 1] for at in range(0, len(terms), 2)]
-    total = terms[0]
-    if late:
-        first = out_ref.shape[0] - 64
-        row = lax.broadcasted_iota(jnp.int32, total.shape, 0)
-        head = total[first + 7 : first + 8] + total[first + 15 : first + 16]
-        rest = head - head.astype(BF16).astype(F32)
-        total = jnp.where(row == first + 7, head, jnp.where(row == first + 15, rest, total))
-    out_ref[...] = total.astype(out_ref.dtype)
+def sum_late_kernel(parts_ref, out_ref):
+    total = parts_ref[0].astype(F32)
+    for at in range(1, parts_ref.shape[0]):
+        total = total + parts_ref[at].astype(F32)
+    out_ref[...] = with_rest(total, out_ref.shape[0] - 64).astype(BF16)
 
 
 def adam_out_kernel(here_ref, weight_ref, first_ref, second_ref, early_refs, *rest):
@@ -863,18 +857,10 @@
     return [value, swap(value, "ctx", 1), far, swap(far, "ctx", 1)]
 
 
-def gather_dp(value):
-    count, here = lax.axis_size("dp"), lax.axis_index("dp")
-    if count != 8:
-        return [lax.all_gather(value, "dp", axis=0)], jnp.zeros((1,), jnp.int32)
-    value = value[None]
-    pieces = [(value, 0)] + [(swap(value, "dp", bit), bit) for bit in range(2, count, 2)]
-    pieces += [(swap(piece, "dp", 1), bit + 1) for piece, bit in pieces]
-    return [piece for piece, _ in pieces], here ^ jnp.asarray([bit for _, bit in pieces], jnp.int32)
-
-
-def spread_dp(parts):
-    return [parts[0]] + [swap(part, "dp", 2 * at) for at, part in enumerate(parts) if at]
+def high_all_to_all(value):
+    count = lax.axis_size("dp")
+    groups = [list(range(low, count, 2)) for low in range(2)]
+    return lax.all_to_all(value, "dp", 0, 0, axis_index_groups=groups)
 
 
 def fan_ctx(value):
@@ -950,17 +936,24 @@
         pack_kernel,
         in_specs=[smem] + [vmem] * 5,
         out_shape=[
-            shape_of(rows_in + 16, wide, dtype=BF16),
+            shape_of(high if near else 1, rows_in + 16, wide, dtype=BF16),
             shape_of(rows_in + (2 * HEAD_DIM if near else 0), width, dtype=BF16),
         ],
         scratch_shapes=[pltpu.VMEM((16, wide), F32)],
         compiler_params=params(),
-        cost_estimate=cost(3),
         name="pack",
     )(bits, in_weight, out_weight, dt_weight, conv_params, gains)
     tok_sent, w1 = lax.optimization_barrier((tok, w1))
-    w1, at_rows = gather_dp(w1)
-    toks = gather_ctx(tok_sent)
+    tok_far = swap(tok_sent, "ctx", 2)
+    if near:
+        w1 = high_all_to_all(w1)
+        w1, tok_far, tok_sent = lax.optimization_barrier((w1, tok_far, tok_sent))
+        w1 = [w1, swap(w1, "dp", 1)]
+        at_rows = jnp.stack([d & 1, 1 - (d & 1)]).astype(jnp.int32)
+    else:
+        w1 = [lax.all_gather(w1[0], "dp", axis=0)]
+        at_rows = jnp.zeros((1,), jnp.int32)
+    toks = [tok, swap(tok_sent, "ctx", 1), tok_far, swap(tok_far, "ctx", 1)]
     if near:
         g2 = [lax.all_gather(g2, "dp", axis=0)]
     else:
@@ -970,7 +963,7 @@
         g2 = [jnp.concatenate([wg, wout[:, :, :width], wout[:, :, width:]], axis=1)]
     at_g2 = jnp.zeros((1,), jnp.int32)
     cot_low, w1 = lax.optimization_barrier((cotangent[0].astype(BF16), w1))
-    cots = fan_ctx(cot_low)
+    cots = gather_ctx(cot_low)
 
     ids = segment_ids[0]
     seg_col = jnp.pad(ids, (8, 8), constant_values=-1)[:, None]
@@ -1050,7 +1043,6 @@
             shape_of(chunks, STATE, width),
         ],
         compiler_params=params("arbitrary"),
-        cost_estimate=cost(18),
         name="scan_forward",
     )(bits, at_rows, toks, w1, head_mine, head_col, seg_col, seg_row)
 
@@ -1082,7 +1074,6 @@
             shape_of(8, length),
         ],
         compiler_params=params("arbitrary"),
-        cost_estimate=cost(12),
         name="gate",
     )(bits, at_g2, hid, g2, cots, inner, gain_mine)
     stats = sum(fan_ctx(stats))
@@ -1125,7 +1116,6 @@
             shape_of(8, width),
         ],
         compiler_params=params("arbitrary"),
-        cost_estimate=cost(13),
         name="norm_back",
     )(perm, bits, hid, inner, gate, normed_grad, stats, gain_mine, mixed, wout, cot_all)
     block_came = swap(block_send, "ctx", 1)
@@ -1185,26 +1175,25 @@
             shape_of(8, heads),
         ],
         compiler_params=params("arbitrary"),
-        cost_estimate=cost(21),
         name="scan_back",
     )(
         perm, bits, hid, dy, mixed, conv_in, conv_sum, raw, step_c, log_c, step_r, log_r, starts,
         conv_mine, head_mine, seg_col, seg_row,
     )
-    block_far = (block_keep[1].astype(F32) + block_came[1].astype(F32)).astype(BF16)
     dbc_came = swap(dbc, "ctx", 1)
     if near:
         late_came = swap(late_send, "dp", 1)
         early_parts = pl.pallas_call(
             pair_sum_kernel,
-            in_specs=[smem, vmem, vmem],
-            out_shape=[[shape_of(early_rows, width, dtype=BF16)] * high],
-            compiler_params=params(),
-            cost_estimate=cost(3),
+            grid=(high,),
+            in_specs=[pl.BlockSpec((1, early_rows, width), lambda i: (i, 0, 0))] * 2,
+            out_specs=pl.BlockSpec((1, early_rows, width), lambda i: (i, 0, 0)),
+            out_shape=shape_of(high, early_rows, width, dtype=BF16),
+            compiler_params=params("arbitrary"),
             name="pair_sum_early",
-        )(bits, early_keep, early_came)[0]
+        )(early_keep, early_came)
         dval, early_parts = lax.optimization_barrier((dval, early_parts))
-        early_parts = spread_dp(early_parts)
+        early_parts = high_all_to_all(early_parts)
     dbc = (dbc.astype(F32) + dbc_came.astype(F32)).astype(BF16)
     dbc_far = swap(dbc, "ctx", 2)
 
@@ -1231,13 +1220,9 @@
             shape_of(8, model),
         ],
         compiler_params=params("arbitrary"),
-        cost_estimate=cost(8),
         name="hidden_back",
     )(perm, dgate, dval, dstep, wg, w1, dt_mine, hid, gain_pre)
     hidden_came = swap(hidden_send, "ctx", 1)
-    hidden_far = (hidden_keep[1].astype(F32) + hidden_came[1].astype(F32)).astype(BF16)
-    hidden_far = swap(hidden_far, "ctx", 2)
-
     map_rows = 32 + 32 * high
     map_cols = lambda size: pl.BlockSpec((size, maps), lambda i: (0, width // maps))
     map_keep, map_send, hidden_own = pl.pallas_call(
@@ -1273,7 +1258,6 @@
             pltpu.VMEM((32, width), F32),
         ],
         compiler_params=params("arbitrary"),
-        cost_estimate=cost(6),
         name="maps_back",
     )(
         bits,
@@ -1293,6 +1277,10 @@
         gain_sum,
     )
 
+    map_send, hidden_came, block_came = lax.optimization_barrier((map_send, hidden_came, block_came))
+    hidden_far = (hidden_keep[1].astype(F32) + hidden_came[1].astype(F32)).astype(BF16)
+    hidden_far = swap(hidden_far, "ctx", 2)
+    block_far = (block_keep[1].astype(F32) + block_came[1].astype(F32)).astype(BF16)
     mine = pl.BlockSpec((1, span, model), lambda i: (0, 0, 0))
     input_grad = pl.pallas_call(
         input_back_kernel,
@@ -1301,7 +1289,6 @@
         out_specs=full((span, model)),
         out_shape=shape_of(span, model),
         compiler_params=params("arbitrary"),
-        cost_estimate=cost(4),
         name="input_back",
     )(hidden_keep, hidden_came, hidden_far, hidden_own, tok, gain_pre, cotangent[0])
     block_far = swap(block_far, "ctx", 2)
@@ -1314,24 +1301,21 @@
         map_came = swap(map_send, "dp", 1)
         late_parts = pl.pallas_call(
             pair_sum_late_kernel,
-            in_specs=[smem] + [vmem] * 4,
-            out_shape=[[shape_of(late_rows, width, dtype=BF16)] * high],
+            out_shape=shape_of(high, late_rows, width, dtype=BF16),
             compiler_params=params(),
-            cost_estimate=cost(2),
-        name="pair_sum_late",
-        )(bits, late_keep, late_came, map_keep, map_came)[0]
-        late_parts = spread_dp(late_parts)
-        early, late = [
-            pl.pallas_call(
-                functools.partial(sum_kernel, name == "late"),
-                in_specs=[[vmem] * high],
-                out_shape=shape_of(*parts[0].shape, dtype=BF16),
-                compiler_params=params(),
-                cost_estimate=cost(2),
-                name="sum_" + name,
-            )(parts)
-            for name, parts in (("early", early_parts), ("late", late_parts))
-        ]
+            name="pair_sum_late",
+        )(late_keep, late_came, map_keep, map_came)
+        late_parts = high_all_to_all(late_parts)
+        late_parts, input_grad, block_output = lax.optimization_barrier(
+            (late_parts, input_grad, block_output)
+        )
+        early = jnp.sum(early_parts.astype(F32), axis=0).astype(BF16)
+        late = pl.pallas_call(
+            sum_late_kernel,
+            out_shape=shape_of(late_rows, width, dtype=BF16),
+            compiler_params=params(),
+            name="sum_late",
+        )(late_parts)
         early, late = fan_ctx(early), fan_ctx(late)
         row_block = lambda ref_rows, cols: pl.BlockSpec((ref_rows, cols), lambda i, *_: (i, 0))
         in_block = row_block(rows_in // nctx, in_weight.shape[1])
@@ -1349,7 +1333,6 @@
             ),
             out_shape=[shape_of(*out_weight.shape)] * 3,
             compiler_params=params("arbitrary"),
-            cost_estimate=cost(4),
             name="adam_out",
         )(bits, out_weight, out_first, out_second, early)
         in_new = pl.pallas_call(
@@ -1363,7 +1346,6 @@
             ),
             out_shape=[shape_of(*in_weight.shape)] * 3,
             compiler_params=params("arbitrary"),
-            cost_estimate=cost(7),
             name="adam_in",
         )(bits, in_weight, in_first, in_second, early, late)
         in_new, out_new = tuple(in_new), tuple(out_new)

time: 286 us -> 300 us (1.049)
  waiting for transfers between devices: 104 us -> 119 us
  starting transfers between devices: 41.4 us -> 35.4 us
  other arithmetic: 8.83 us -> 12 us
    ppermute x37 -> x25, starting transfers between devices: 41.4 us -> 20.5 us  [swap(): return lax.ppermute(value, axis, [(at, at ^ bit) for at in range(count)])]
    all_to_all x0 -> x3, starting transfers between devices: none -> 14.9 us  [high_all_to_all(): return lax.all_to_all(value, 'dp', 0, 0, axis_index_groups=groups)]
    ppermute x37 -> x25, waiting for transfers between devices: 104 us -> 113 us  [swap(): return lax.ppermute(value, axis, [(at, at ^ bit) for at in range(count)])]
    all_to_all x0 -> x3, waiting for transfers between devices: none -> 5.92 us  [high_all_to_all(): return lax.all_to_all(value, 'dp', 0, 0, axis_index_groups=groups)]
    pallas_call x4 -> x3, Pallas kernels: 9.02 us -> 7.99 us  [the longest x1 3.68 us: shards(): pl.pallas_call(pair_sum_kernel, grid=(high,), in_specs=[pl.BlockSpec((1,...]
  transfers between devices with their start and end apart: 38 -> 29, of which waited for: 20 -> 15; matrix products, arithmetic and copies ran while one was open for 4% -> 3% of each run, Pallas kernels for 27% -> 22%
where the time goes in v5:
time: 300 us; the launch traced here: 299 us
  waiting for transfers between devices  119 us (40%)
  Pallas kernels  107 us (36%)
  starting transfers between devices  35.4 us (12%)
  between operations  14.6 us (5%)
  other arithmetic  12 us (4%)
  local copies, waits for them, and re-layouts  10.4 us (3%)
    ppermute x25, waiting for transfers between devices, swap(): return lax.ppermute(value, axis, [(at, at ^ bit) for at in range(count)])  113 us
    pallas_call x1, Pallas kernels, shards(): pl.pallas_call(scan_back_kernel, grid_spec=pltpu.PrefetchScalarGridSpec(n...  21.7 us
    ppermute x25, starting transfers between devices, swap(): return lax.ppermute(value, axis, [(at, at ^ bit) for at in range(count)])  20.5 us
    pallas_call x1, Pallas kernels, shards(): pl.pallas_call(scan_forward_kernel, grid_spec=pltpu.PrefetchScalarGridSpe...  18.2 us
    all_to_all x3, starting transfers between devices, high_all_to_all(): return lax.all_to_all(value, 'dp', 0, 0, axis_index_groups=groups)  14.9 us
    pallas_call x1, Pallas kernels, shards(): pl.pallas_call(norm_back_kernel, grid_spec=pltpu.PrefetchScalarGridSpec(n...  13.1 us
    pallas_call x1, Pallas kernels, shards(): pl.pallas_call(gate_kernel, grid_spec=pltpu.PrefetchScalarGridSpec(num_sc...  10.1 us
    pallas_call x1, Pallas kernels, shards(): pl.pallas_call(adam_in_kernel, grid_spec=pltpu.PrefetchScalarGridSpec(num...  8.29 us
  transfers between devices with their start and end apart: 29, of which 15 were waited for; matrix products, arithmetic and copies ran while one was open for 3% of the time, Pallas kernels for 22%

profile of v5, /device:TPU:0, one launch (start us, length us, event | category | flops | bytes accessed | tf_op | source)
XLA Modules:
  0.0 298.5 jit_solution(8552657485853538740)
XLA Ops:
  7.2 0.7 pad_add_fusion.here_ref
  7.9 3.3 %pack.1 = (bf16[4,144,768]{2,1,0:T(8,128)(2,1)}, bf16[256,512]{1,0:T(8,128)(2,1)}) custom-call(s32[3]{0:T(128)} %pad_add_fusion.here_ref, f32[128,4352]{1,0:T(8,128)} %weight_ref.2, f32[256,1024]{1,0:T(8,128)} %weight_ref.3, f32[32,128]{1,0:T(8,128)} %dt_ref.1, f32[5,288]{1,0:T(8,128)} %conv_ref.1, f32[384]{0:T(512)} %gain_ref.1), custom_call_target="tpu_custom_call" | custom-call | tf_op jit(solution)/shard_map/pack/pallas_call | solution.py:935
  11.3 6.3 %all-to-all-start = ((bf16[4,144,768]{2,1,0:T(8,128)(2,1)}), bf16[4,144,768]{2,1,0:T(8,128)(2,1)S(1)}, u32[]{:S(2)}, u32[]{:S(2)}) async-start(bf16[4,144,768]{2,1,0:T(8,128)(2,1)} %get-tuple-element.88), calls=%async_computation | async-start | bytes 1769472 | tf_op jit(solution)/shard_map/all_to_all | solution.py:863
  17.6 1.5 collective-permute-start
  19.1 23.2 %collective-permute-done.tok_pieces_2_ = f32[256,1024]{1,0:T(8,128)} collective-permute-done((f32[256,1024]{1,0:T(8,128)S(1)}, f32[256,1024]{1,0:T(8,128)}, u32[]{:S(2)}, u32[]{:S(2)}) %collective-permute-start) | collective-permute-done | bytes 1048608 | tf_op jit(solution)/shard_map/ppermute | solution.py:852
  42.3 5.9 %all-to-all-done.w1_pieces_0_ = bf16[4,144,768]{2,1,0:T(8,128)(2,1)S(1)} async-done(((bf16[4,144,768]{2,1,0:T(8,128)(2,1)}), bf16[4,144,768]{2,1,0:T(8,128)(2,1)S(1)}, u32[]{:S(2)}, u32[]{:S(2)}) %all-to-all-start) | async-done | bytes 884768 | tf_op jit(solution)/shard_map/all_to_all | solution.py:863
  48.2 1.5 collective-permute-start.3
  50.4 29.5 %collective-permute-done.3.w1_pieces_1_ = bf16[4,144,768]{2,1,0:T(8,128)(2,1)S(1)} collective-permute-done((bf16[4,144,768]{2,1,0:T(8,128)(2,1)S(1)}, bf16[4,144,768]{2,1,0:T(8,128)(2,1)S(1)}, u32[]{:S(2)}, u32[]{:S(2)}) %collective-permute-start.3) | collective-permute-done | bytes 884768 | tf_op jit(solution)/shard_map/ppermute | solution.py:852
  79.9 1.5 collective-permute-start.5
  81.4 10.4 %collective-permute-done.5.cot_pieces_2_ = bf16[256,1024]{1,0:T(8,128)(2,1)} collective-permute-done((bf16[256,1024]{1,0:T(8,128)(2,1)S(1)}, bf16[256,1024]{1,0:T(8,128)(2,1)}, u32[]{:S(2)}, u32[]{:S(2)}) %collective-permute-start.5) | collective-permute-done | bytes 524320 | tf_op jit(solution)/shard_map/ppermute | solution.py:852
  92.1 0.7 copy.66
  92.8 1.0 broadcast_in_dim.13.segc_ref
  94.4 0.9 copy-done.13
  95.4 18.2 %scan_forward.1 = (bf16[1024,1024]{1,0:T(8,128)(2,1)}, f32[8,768]{1,0:T(8,128)}, f32[1,1024]{1,0:T(1,128)}, f32[1,512]{1,0:T(1,128)}, bf16[8,1024]{1,0:T(8,128)(...) custom-call(s32[3]{0:T(128)} %pad_add_fusion.here_ref, ...), custom_call_target="tpu_custom_call" | custom-call | tf_op jit(solution)/shard_map/scan_forward/pallas_call | solution.py:984
  113.7 10.1 %gate.1 = (bf16[1024,512]{1,0:T(8,128)(2,1)}, bf16[512,1024]{1,0:T(8,128)(2,1)}, bf16[4,256,1024]{2,1,0:T(8,128)(2,1)}, bf16[1024,512]{1,0:T(8,128)(2,1)}, f32[1024,512]{1,0:T(8,128)}, /*index=5*/f32[8,1024]{1,0:T(8,128)}) custom-call(s32[3]{0:T(128)} %pad_add_fusion.here_ref, s32[1]{0:T(128)} %constant.35.clone.1.at_ref, ...), custom_call_target="tpu_custom_call" | custom-call | tf_op jit(solution)/shard_map/gate/pallas_call | solution.py:1049
  124.4 1.5 collective-permute-start.8
  126.4 2.1 collective-permute-done.8
  128.5 1.3 collective-permute-done.9
  129.8 1.4 add_add_fusion.stat_ref
  131.2 13.1 %norm_back.1 = (bf16[2,256,1024]{2,1,0:T(8,128)(2,1)}, bf16[2,256,1024]{2,1,0:T(8,128)(2,1)}, bf16[4,256,512]{2,1,0:T(8,128)(2,1)}, bf16[4,256,512]{2,1,0:T(8,12...) custom-call(s32[4]{0:T(128)} %broadcast_xor_fusion.perm_ref, s32[3]{0:T(128)} %pad_add_fusion.here_ref, ...), custom_call_target="tpu_custom_call" | custom-call | tf_op jit(solution)/shard_map/norm_back/pallas_call | solution.py:1082
  144.3 1.6 collective-permute-start.13
  145.9 21.7 %scan_back.1 = (bf16[4,128,512]{2,1,0:T(8,128)(2,1)}, bf16[4,128,512]{2,1,0:T(8,128)(2,1)}, bf16[1024,512]{1,0:T(8,128)(2,1)}, bf16[1024,256]{1,0:T(8,128)(2,1)}...) custom-call(s32[4]{0:T(128)} %broadcast_xor_fusion.perm_ref, ...), custom_call_target="tpu_custom_call" | custom-call | tf_op jit(solution)/shard_map/scan_back/pallas_call | solution.py:1127
  167.6 2.1 collective-permute-done.13.came_ref
  169.7 1.0 copy-done.14
  170.7 3.7 %pair_sum_early.1 = bf16[4,256,512]{2,1,0:T(8,128)(2,1)} custom-call(bf16[4,256,512]{2,1,0:T(8,128)(2,1)} %get-tuple-element.127.keep_ref, bf16[4,256,512]{2,1,0:T(8,128)(2,1)} %copy-done.14), custom_call_target="tpu_custom_call" | custom-call | tf_op jit(solution)/shard_map/pair_sum_early/pallas_call | solution.py:1186
  174.4 3.5 %all-to-all-start.2 = ((bf16[4,256,512]{2,1,0:T(8,128)(2,1)}), bf16[4,256,512]{2,1,0:T(8,128)(2,1)S(1)}, u32[]{:S(2)}, u32[]{:S(2)}) async-start(bf16[4,256,512]{2,1,0:T(8,128)(2,1)} %pair_sum_early.1), calls=%async_computation.2 | async-start | bytes 2097152 | tf_op jit(solution)/shard_map/all_to_all | solution.py:863
  178.5 8.2 %hidden_back.1 = (bf16[2,256,1024]{2,1,0:T(8,128)(2,1)}, bf16[2,256,1024]{2,1,0:T(8,128)(2,1)}, f32[8,1024]{1,0:T(8,128)}) custom-call(s32[4]{0:T(128)} %broadcast_xor_fusion.perm_ref, bf16[1024,512]{1,0:T(8,128)(2,1)} %get-tuple-element.125.dgate_ref, bf16[1024,512]{1,0:T(8,128)(2,1)} %get-tuple-element.129.dval_ref, ...), custom_call_target="tpu_custom_call" | custom-call | tf_op jit(solution)/shard_map/hidden_back/pallas_call | solution.py:1200
  187.0 0.7 collective-permute-start.12
  187.7 1.5 collective-permute-start.10
  189.2 12.1 %collective-permute-done.12.dbcfar_ref = bf16[1024,256]{1,0:T(8,128)(2,1)S(1)} collective-permute-done((bf16[1024,256]{1,0:T(8,128)(2,1)S(1)}, bf16[1024,256]{1,0:T(8,128)(2,1)S(1)}, u32[]{:S(2)}, u32[]{:S(2)}) %collective-permute-start.12) | collective-permute-done | bytes 524320 | tf_op jit(solution)/shard_map/ppermute | solution.py:852
  201.3 0.8 copy-done.21
  202.1 6.2 %maps_back.1 = (bf16[160,512]{1,0:T(8,128)(2,1)}, bf16[160,512]{1,0:T(8,128)(2,1)}, f32[256,1024]{1,0:T(8,128)}) custom-call(s32[3]{0:T(128)} %pad_add_fusion.here_ref, bf16[1024,256]{1,0:T(8,128)(2,1)} %copy-done.9, bf16[1024,256]{1,0:T(8,128)(2,1)} %copy-done.21, f32[1024,768]{1,0:T(8,128)} %get-tuple-element.108.convsum_ref, ...), custom_call_target="tpu_custom_call" | custom-call | tf_op jit(solution)/shard_map/maps_back/pallas_call | solution.py:1228
  208.4 1.6 collective-permute-start.16
  209.9 4.5 %collective-permute-done.16.mcame_ref = bf16[160,512]{1,0:T(8,128)(2,1)S(1)} collective-permute-done((bf16[160,512]{1,0:T(8,128)(2,1)}, bf16[160,512]{1,0:T(8,128)(2,1)S(1)}, u32[]{:S(2)}, u32[]{:S(2)}) %collective-permute-start.16) | collective-permute-done | bytes 163872 | tf_op jit(solution)/shard_map/ppermute | solution.py:852
  214.4 0.6 copy-done.26
  215.1 2.4 pair_sum_late.1
  217.5 5.0 %all-to-all-start.1 = ((bf16[4,192,512]{2,1,0:T(8,128)(2,1)}), bf16[4,192,512]{2,1,0:T(8,128)(2,1)S(1)}, u32[]{:S(2)}, u32[]{:S(2)}) async-start(bf16[4,192,512]{2,1,0:T(8,128)(2,1)} %pair_sum_late.1), calls=%async_computation.1 | async-start | bytes 1572864 | tf_op jit(solution)/shard_map/all_to_all | solution.py:863
  222.5 2.0 fusion.1
  224.5 0.6 collective-permute-start.17
  225.2 2.2 fusion.2
  227.4 1.4 collective-permute-start.18
  229.1 0.7 collective-permute-start.20
  229.8 1.2 collective-permute-start.21
  231.0 8.6 %collective-permute-done.17.far_ref = bf16[256,1024]{1,0:T(8,128)(2,1)S(1)} collective-permute-done((bf16[256,1024]{1,0:T(8,128)(2,1)}, bf16[256,1024]{1,0:T(8,128)(2,1)S(1)}, u32[]{:S(2)}, u32[]{:S(2)}) %collective-permute-start.17) | collective-permute-done | bytes 524320 | tf_op jit(solution)/shard_map/ppermute | solution.py:852
  239.6 0.8 copy-done.19
  240.4 4.1 %input_back.1 = f32[256,1024]{1,0:T(8,128)} custom-call(bf16[2,256,1024]{2,1,0:T(8,128)(2,1)} %get-tuple-element.139.keep_ref, bf16[2,256,1024]{2,1,0:T(8,128)(2,1)} %copy-done.7, bf16[256,1024]{1,0:T(8,128)(2,1)} %copy-done.19, f32[256,1024]{1,0:T(8,128)} %get-tuple-element.141.own_ref, f32[256,1024]{1,0:T(8,128)} %bitcast.54, ...), custom_call_target="tpu_custom_call" | custom-call | tf_op jit(solution)/shard_map/input_back/pallas_call | solution.py:1285
  244.5 6.3 %collective-permute-done.18 = bf16[256,1024]{1,0:T(8,128)(2,1)S(1)} collective-permute-done((bf16[256,1024]{1,0:T(8,128)(2,1)}, bf16[256,1024]{1,0:T(8,128)(2,1)S(1)}, u32[]{:S(2)}, u32[]{:S(2)}) %collective-permute-start.18) | collective-permute-done | bytes 524320 | tf_op jit(solution)/shard_map/ppermute | solution.py:852
  250.8 1.3 fusion
  252.1 4.3 %collective-permute-done.20.early_refs_2_ = bf16[256,512]{1,0:T(8,128)(2,1)S(1)} collective-permute-done((bf16[256,512]{1,0:T(8,128)(2,1)S(1)}, bf16[256,512]{1,0:T(8,128)(2,1)S(1)}, u32[]{:S(2)}, u32[]{:S(2)}) %collective-permute-start.20) | collective-permute-done | bytes 262176 | tf_op jit(solution)/shard_map/ppermute | solution.py:852
  256.5 1.3 collective-permute-done.21.early_refs_3_
  257.7 0.7 copy-done.17
  258.5 5.5 %adam_out.1 = (f32[256,1024]{1,0:T(8,128)}, f32[256,1024]{1,0:T(8,128)}, f32[256,1024]{1,0:T(8,128)}) custom-call(s32[3]{0:T(128)} %pad_add_fusion.here_ref, f32[256,1024]{1,0:T(8,128)} %weight_ref.3, f32[256,1024]{1,0:T(8,128)} %first_ref.3, f32[256,1024]{1,0:T(8,128)} %second_ref.3, bf16[256,512]{1,0:T(8,128)(2,1)} %copy-done.5, ...), custom_call_target="tpu_custom_call" | custom-call | tf_op jit(solution)/shard_map/adam_out/pallas_call | solution.py:1325
  264.1 0.9 copy-done.4
  265.0 1.9 sum_late.1.late_refs_0_
  266.9 1.9 collective-permute-start.24
  268.8 1.4 collective-permute-start.23
  270.2 0.8 slice_bitcast_fusion.4
  271.0 3.4 %collective-permute-done.24.late_refs_3_ = bf16[192,512]{1,0:T(8,128)(2,1)S(1)} collective-permute-done((bf16[192,512]{1,0:T(8,128)(2,1)}, bf16[192,512]{1,0:T(8,128)(2,1)S(1)}, u32[]{:S(2)}, u32[]{:S(2)}) %collective-permute-start.24) | collective-permute-done | bytes 196640 | tf_op jit(solution)/shard_map/ppermute | solution.py:852
  274.4 4.3 %collective-permute-done.23.late_refs_2_ = bf16[192,512]{1,0:T(8,128)(2,1)S(1)} collective-permute-done((bf16[192,512]{1,0:T(8,128)(2,1)}, bf16[192,512]{1,0:T(8,128)(2,1)S(1)}, u32[]{:S(2)}, u32[]{:S(2)}) %collective-permute-start.23) | collective-permute-done | bytes 196640 | tf_op jit(solution)/shard_map/ppermute | solution.py:852
  280.7 0.6 multiply_subtract_fusion
  281.3 0.6 multiply_subtract_fusion.2
  281.9 0.7 multiply_subtract_fusion.3
  282.6 0.7 multiply_subtract_fusion.1
  283.4 8.3 %adam_in.1 = (f32[128,4352]{1,0:T(8,128)}, f32[128,4352]{1,0:T(8,128)}, f32[128,4352]{1,0:T(8,128)}) custom-call(s32[3]{0:T(128)} %pad_add_fusion.here_ref, f32[128,4352]{1,0:T(8,128)} %weight_ref.2, f32[128,4352]{1,0:T(8,128)} %first_ref.2, f32[128,4352]{1,0:T(8,128)} %second_ref.2, bf16[256,512]{1,0:T(8,128)(2,1)} %copy-done.5, ...), custom_call_target="tpu_custom_call" | custom-call | tf_op jit(solution)/shard_map/adam_in/pallas_call | solution.py:1338
  (148 shorter events, 5.9 us)
Async XLA Ops:
  7.2 106.5 %all-gather.3.cloned.1.call-start = ((), (), s32[]{:S(2)}) async-start(), calls=%async_computation.3 | async-start | bytes 2359296 | tf_op jit(solution)/shard_map/all_gather | solution.py:958
  7.9 9.7 %copy-start = (f32[1,256,1024]{2,1,0:T(8,128)S(1)}, f32[1,256,1024]{2,1,0:T(8,128)}, u32[]{:S(2)}) copy-start(f32[1,256,1024]{2,1,0:T(8,128)} %param.22) | copy-start | bytes 3145732
  7.9 41.8 %copy-start.2 = (f32[1,256,1024]{2,1,0:T(8,128)S(1)}, f32[1,256,1024]{2,1,0:T(8,128)}, u32[]{:S(2)}) copy-start(f32[1,256,1024]{2,1,0:T(8,128)} %param.24) | copy-start | bytes 3145732
  11.2 80.6 %copy-start.36 = (f32[3,32]{1,0:T(4,128)S(1)}, f32[3,32]{1,0:T(4,128)}, u32[]{:S(2)}) copy-start(f32[3,32]{1,0:T(4,128)} %param.30) | copy-start | bytes 1156
  11.2 81.5 %copy-start.29 = (s32[1,1024]{1,0:T(1,128)S(1)}, s32[1,1024]{1,0:T(1,128)}, u32[]{:S(2)}) copy-start(s32[1,1024]{1,0:T(1,128)} %segr_ref.3) | copy-start | bytes 12292
  11.3 37.0 %all-to-all-start = ((bf16[4,144,768]{2,1,0:T(8,128)(2,1)}), bf16[4,144,768]{2,1,0:T(8,128)(2,1)S(1)}, u32[]{:S(2)}, u32[]{:S(2)}) async-start(bf16[4,144,768]{2,1,0:T(8,128)(2,1)} %get-tuple-element.88), calls=%async_computation | async-start | bytes 1769472 | tf_op jit(solution)/shard_map/all_to_all | solution.py:863
  17.6 24.7 %collective-permute-start = (f32[256,1024]{1,0:T(8,128)S(1)}, f32[256,1024]{1,0:T(8,128)}, u32[]{:S(2)}, u32[]{:S(2)}) collective-permute-start(f32[256,1024]{1,0:T(8,128)S(1)} %bitcast.55), channel_id=1, source_target_pairs={{0,2},{1,3},{2,0},{3,1},{4,6},{5,7},{6,4},{7,5},{8,10},{9,11},{10,... | collective-permute-start | bytes 3145736 | tf_op jit(solution)/shard_map/ppermute | solution.py:852
  48.2 46.2 %copy-start.3 = (bf16[4,144,768]{2,1,0:T(8,128)(2,1)}, bf16[4,144,768]{2,1,0:T(8,128)(2,1)S(1)}, u32[]{:S(2)}) copy-start(bf16[4,144,768]{2,1,0:T(8,128)(2,1)S(1)} %all-to-all-done.w1_pieces_0_) | copy-start | bytes 2654212
  48.2 31.7 %collective-permute-start.3 = (bf16[4,144,768]{2,1,0:T(8,128)(2,1)S(1)}, bf16[4,144,768]{2,1,0:T(8,128)(2,1)S(1)}, u32[]{:S(2)}, u32[]{:S(2)}) collective-permute-start(bf16[4,144,768]{2,1,0:T(8,128)(2,1)S(1)} %all-to-all-done.w1_pieces_0_), channel_id=1, source_target_pairs={{0,4},{4,0},{8,12},{12,8},{16,20},{20,16},{24,28},{28,24},{1,5},{5... | collective-permute-start | bytes 2654216 | tf_op jit(solution)/shard_map/ppermute | solution.py:852
  49.8 63.8 %copy-start.8 = (bf16[256,1024]{1,0:T(8,128)(2,1)}, bf16[256,1024]{1,0:T(8,128)(2,1)S(1)}, u32[]{:S(2)}) copy-start(bf16[256,1024]{1,0:T(8,128)(2,1)S(1)} %bitcast_convert_fusion.cot_pieces_0_) | copy-start | bytes 1572868
  49.8 44.6 %collective-permute-start.2 = (f32[256,1024]{1,0:T(8,128)}, f32[256,1024]{1,0:T(8,128)S(1)}, u32[]{:S(2)}, u32[]{:S(2)}) collective-permute-start(f32[256,1024]{1,0:T(8,128)} %collective-permute-done.tok_pieces_2_), channel_id=1, source_target_pairs={{0,1},{1,0},{2,3},{3,2},{4,5},{5,4},{6,7},{7,6},{8,9},{9,8},{10,11... | collective-permute-start | bytes 3145736 | tf_op jit(solution)/shard_map/ppermute | solution.py:852
  49.9 44.5 %collective-permute-start.1 = (f32[256,1024]{1,0:T(8,128)S(1)}, f32[256,1024]{1,0:T(8,128)}, u32[]{:S(2)}, u32[]{:S(2)}) collective-permute-start(f32[256,1024]{1,0:T(8,128)S(1)} %bitcast.56), channel_id=1, source_target_pairs={{0,1},{1,0},{2,3},{3,2},{4,5},{5,4},{6,7},{7,6},{8,9},{9,8},{10,11... | collective-permute-start | bytes 3145736 | tf_op jit(solution)/shard_map/ppermute | solution.py:852
  79.9 11.9 %copy-start.18 = (bf16[4,144,768]{2,1,0:T(8,128)(2,1)}, bf16[4,144,768]{2,1,0:T(8,128)(2,1)S(1)}, u32[]{:S(2)}) copy-start(bf16[4,144,768]{2,1,0:T(8,128)(2,1)S(1)} %collective-permute-done.3.w1_pieces_1_) | copy-start | bytes 2654212
  79.9 11.9 %collective-permute-start.5 = (bf16[256,1024]{1,0:T(8,128)(2,1)S(1)}, bf16[256,1024]{1,0:T(8,128)(2,1)}, u32[]{:S(2)}, u32[]{:S(2)}) collective-permute-start(bf16[256,1024]{1,0:T(8,128)(2,1)S(1)} %bitcast_convert_fusion.cot_pieces_0_), channel_id=1, source_target_pairs={{0,2},{1,3},{2,0},{3,1},{4,6},{5,7},{6,4},{7,5},{8,10},{9,11},{10,... | collective-permute-start | bytes 1572872 | tf_op jit(solution)/shard_map/ppermute | solution.py:852
  81.4 32.2 %collective-permute-start.4 = (bf16[256,1024]{1,0:T(8,128)(2,1)S(1)}, bf16[256,1024]{1,0:T(8,128)(2,1)}, u32[]{:S(2)}, u32[]{:S(2)}) collective-permute-start(bf16[256,1024]{1,0:T(8,128)(2,1)S(1)} %bitcast_convert_fusion.cot_pieces_0_), channel_id=1, source_target_pairs={{0,1},{1,0},{2,3},{3,2},{4,5},{5,4},{6,7},{7,6},{8,9},{9,8},{10,11... | collective-permute-start | bytes 1572872 | tf_op jit(solution)/shard_map/ppermute | solution.py:852
  91.8 21.8 %collective-permute-start.6 = (bf16[256,1024]{1,0:T(8,128)(2,1)}, bf16[256,1024]{1,0:T(8,128)(2,1)}, u32[]{:S(2)}, u32[]{:S(2)}) collective-permute-start(bf16[256,1024]{1,0:T(8,128)(2,1)} %collective-permute-done.5.cot_pieces_2_), channel_id=1, source_target_pairs={{0,1},{1,0},{2,3},{3,2},{4,5},{5,4},{6,7},{7,6},{8,9},{9,8},{10,11... | collective-permute-start | bytes 1572872 | tf_op jit(solution)/shard_map/ppermute | solution.py:852
  92.1 2.4 copy-start.30
  113.7 12.2 %copy-start.42 = (s32[4]{0:T(128)S(1)}, s32[4]{0:T(128)}, u32[]{:S(2)}) copy-start(s32[4]{0:T(128)} %constant.16.clone) | copy-start | bytes 52
  123.8 2.6 collective-permute-start.7
  124.4 4.1 %collective-permute-start.8 = (f32[8,1024]{1,0:T(8,128)}, f32[8,1024]{1,0:T(8,128)S(1)}, u32[]{:S(2)}, u32[]{:S(2)}) collective-permute-start(f32[8,1024]{1,0:T(8,128)} %get-tuple-element.102), channel_id=1, source_target_pairs={{0,2},{1,3},{2,0},{3,1},{4,6},{5,7},{6,4},{7,5},{8,10},{9,11},{10,... | collective-permute-start | bytes 98312 | tf_op jit(solution)/shard_map/ppermute | solution.py:852
  125.9 3.9 %collective-permute-start.9 = (f32[8,1024]{1,0:T(8,128)}, f32[8,1024]{1,0:T(8,128)S(1)}, u32[]{:S(2)}, u32[]{:S(2)}) collective-permute-start(f32[8,1024]{1,0:T(8,128)} %get-tuple-element.102), channel_id=1, source_target_pairs={{0,3},{1,2},{2,1},{3,0},{4,7},{5,6},{6,5},{7,4},{8,11},{9,10},{10,... | collective-permute-start | bytes 98312 | tf_op jit(solution)/shard_map/ppermute | solution.py:852
  144.3 25.4 %collective-permute-start.13 = (bf16[4,256,512]{2,1,0:T(8,128)(2,1)}, bf16[4,256,512]{2,1,0:T(8,128)(2,1)S(1)}, u32[]{:S(2)}, u32[]{:S(2)}) collective-permute-start(bf16[4,256,512]{2,1,0:T(8,128)(2,1)} %get-tuple-element.128), channel_id=1, source_target_pairs={{0,4},{4,0},{8,12},{12,8},{16,20},{20,16},{24,28},{28,24},{1,5},{5... | collective-permute-start | bytes 3145736 | tf_op jit(solution)/shard_map/ppermute | solution.py:852
  170.7 7.2 %copy-start.20 = (bf16[1024,256]{1,0:T(8,128)(2,1)S(1)}, bf16[1024,256]{1,0:T(8,128)(2,1)}, u32[]{:S(2)}) copy-start(bf16[1024,256]{1,0:T(8,128)(2,1)} %get-tuple-element.118) | copy-start | bytes 1572868
  174.4 43.1 %all-to-all-start.2 = ((bf16[4,256,512]{2,1,0:T(8,128)(2,1)}), bf16[4,256,512]{2,1,0:T(8,128)(2,1)S(1)}, u32[]{:S(2)}, u32[]{:S(2)}) async-start(bf16[4,256,512]{2,1,0:T(8,128)(2,1)} %pair_sum_early.1), calls=%async_computation.2 | async-start | bytes 2097152 | tf_op jit(solution)/shard_map/all_to_all | solution.py:863
  177.9 8.9 %collective-permute-start.11 = (bf16[1024,256]{1,0:T(8,128)(2,1)S(1)}, bf16[1024,256]{1,0:T(8,128)(2,1)S(1)}, u32[]{:S(2)}, u32[]{:S(2)}) collective-permute-start(bf16[1024,256]{1,0:T(8,128)(2,1)S(1)} %copy-done.20), channel_id=1, source_target_pairs={{0,1},{1,0},{2,3},{3,2},{4,5},{5,4},{6,7},{7,6},{8,9},{9,8},{10,11... | collective-permute-start | bytes 1572872 | tf_op jit(solution)/shard_map/ppermute | solution.py:852
  178.0 30.3 %collective-permute-start.15 = (bf16[2,256,1024]{2,1,0:T(8,128)(2,1)}, bf16[2,256,1024]{2,1,0:T(8,128)(2,1)S(1)}, u32[]{:S(2)}, u32[]{:S(2)}) collective-permute-start(bf16[2,256,1024]{2,1,0:T(8,128)(2,1)} %get-tuple-element.137), channel_id=1, source_target_pairs={{0,1},{1,0},{2,3},{3,2},{4,5},{5,4},{6,7},{7,6},{8,9},{9,8},{10,11... | collective-permute-start | bytes 3145736 | tf_op jit(solution)/shard_map/ppermute | solution.py:852
  178.5 9.2 %copy-start.41 = (bf16[4,128,512]{2,1,0:T(8,128)(2,1)S(1)}, bf16[4,128,512]{2,1,0:T(8,128)(2,1)}, u32[]{:S(2)}) copy-start(bf16[4,128,512]{2,1,0:T(8,128)(2,1)} %get-tuple-element.117) | copy-start | bytes 1572868
  186.7 21.7 %collective-permute-start.14 = (bf16[2,256,1024]{2,1,0:T(8,128)(2,1)}, bf16[2,256,1024]{2,1,0:T(8,128)(2,1)S(1)}, u32[]{:S(2)}, u32[]{:S(2)}) collective-permute-start(bf16[2,256,1024]{2,1,0:T(8,128)(2,1)} %get-tuple-element.136), channel_id=1, source_target_pairs={{0,1},{1,0},{2,3},{3,2},{4,5},{5,4},{6,7},{7,6},{8,9},{9,8},{10,11... | collective-permute-start | bytes 3145736 | tf_op jit(solution)/shard_map/ppermute | solution.py:852
  187.0 14.4 %copy-start.9 = (bf16[1024,256]{1,0:T(8,128)(2,1)}, bf16[1024,256]{1,0:T(8,128)(2,1)S(1)}, u32[]{:S(2)}) copy-start(bf16[1024,256]{1,0:T(8,128)(2,1)S(1)} %add_convert_fusion.2.dbc_ref) | copy-start | bytes 1572868
  187.0 14.3 %collective-permute-start.12 = (bf16[1024,256]{1,0:T(8,128)(2,1)S(1)}, bf16[1024,256]{1,0:T(8,128)(2,1)S(1)}, u32[]{:S(2)}, u32[]{:S(2)}) collective-permute-start(bf16[1024,256]{1,0:T(8,128)(2,1)S(1)} %add_convert_fusion.2.dbc_ref), channel_id=1, source_target_pairs={{0,2},{1,3},{2,0},{3,1},{4,6},{5,7},{6,4},{7,5},{8,10},{9,11},{10,... | collective-permute-start | bytes 1572872 | tf_op jit(solution)/shard_map/ppermute | solution.py:852
  187.7 22.2 %collective-permute-start.10 = (bf16[4,128,512]{2,1,0:T(8,128)(2,1)S(1)}, bf16[4,128,512]{2,1,0:T(8,128)(2,1)S(1)}, u32[]{:S(2)}, u32[]{:S(2)}) collective-permute-start(bf16[4,128,512]{2,1,0:T(8,128)(2,1)S(1)} %copy-done.41), channel_id=1, source_target_pairs={{0,4},{4,0},{8,12},{12,8},{16,20},{20,16},{24,28},{28,24},{1,5},{5... | collective-permute-start | bytes 1572872 | tf_op jit(solution)/shard_map/ppermute | solution.py:852
  208.3 14.2 %copy-start.6 = (bf16[2,256,1024]{2,1,0:T(8,128)(2,1)S(1)}, bf16[2,256,1024]{2,1,0:T(8,128)(2,1)}, u32[]{:S(2)}) copy-start(bf16[2,256,1024]{2,1,0:T(8,128)(2,1)} %get-tuple-element.139.keep_ref) | copy-start | bytes 3145732
  208.3 6.1 %copy-start.11 = (bf16[2,256,1024]{2,1,0:T(8,128)(2,1)}, bf16[2,256,1024]{2,1,0:T(8,128)(2,1)S(1)}, u32[]{:S(2)}) copy-start(bf16[2,256,1024]{2,1,0:T(8,128)(2,1)S(1)} %collective-permute-done.15) | copy-start | bytes 3145732
  208.4 6.1 %copy-start.7 = (bf16[2,256,1024]{2,1,0:T(8,128)(2,1)}, bf16[2,256,1024]{2,1,0:T(8,128)(2,1)S(1)}, u32[]{:S(2)}) copy-start(bf16[2,256,1024]{2,1,0:T(8,128)(2,1)S(1)} %collective-permute-done.14.came_ref) | copy-start | bytes 3145732
  208.4 6.0 %collective-permute-start.16 = (bf16[160,512]{1,0:T(8,128)(2,1)}, bf16[160,512]{1,0:T(8,128)(2,1)S(1)}, u32[]{:S(2)}, u32[]{:S(2)}) collective-permute-start(bf16[160,512]{1,0:T(8,128)(2,1)} %get-tuple-element.138), channel_id=1, source_target_pairs={{0,4},{4,0},{8,12},{12,8},{16,20},{20,16},{24,28},{28,24},{1,5},{5... | collective-permute-start | bytes 491528 | tf_op jit(solution)/shard_map/ppermute | solution.py:852
  209.9 4.5 %copy-start.22 = (bf16[4,128,512]{2,1,0:T(8,128)(2,1)}, bf16[4,128,512]{2,1,0:T(8,128)(2,1)S(1)}, u32[]{:S(2)}) copy-start(bf16[4,128,512]{2,1,0:T(8,128)(2,1)S(1)} %collective-permute-done.10.came_ref) | copy-start | bytes 1572868
  217.5 46.6 %all-to-all-start.1 = ((bf16[4,192,512]{2,1,0:T(8,128)(2,1)}), bf16[4,192,512]{2,1,0:T(8,128)(2,1)S(1)}, u32[]{:S(2)}, u32[]{:S(2)}) async-start(bf16[4,192,512]{2,1,0:T(8,128)(2,1)} %pair_sum_late.1), calls=%async_computation.1 | async-start | bytes 1572864 | tf_op jit(solution)/shard_map/all_to_all | solution.py:863
  224.5 15.1 %collective-permute-start.17 = (bf16[256,1024]{1,0:T(8,128)(2,1)}, bf16[256,1024]{1,0:T(8,128)(2,1)S(1)}, u32[]{:S(2)}, u32[]{:S(2)}) collective-permute-start(bf16[256,1024]{1,0:T(8,128)(2,1)} %fusion.1), channel_id=1, source_target_pairs={{0,2},{1,3},{2,0},{3,1},{4,6},{5,7},{6,4},{7,5},{8,10},{9,11},{10,... | collective-permute-start | bytes 1572872 | tf_op jit(solution)/shard_map/ppermute | solution.py:852
  227.4 23.5 %collective-permute-start.18 = (bf16[256,1024]{1,0:T(8,128)(2,1)}, bf16[256,1024]{1,0:T(8,128)(2,1)S(1)}, u32[]{:S(2)}, u32[]{:S(2)}) collective-permute-start(bf16[256,1024]{1,0:T(8,128)(2,1)} %fusion.2), channel_id=1, source_target_pairs={{0,2},{1,3},{2,0},{3,1},{4,6},{5,7},{6,4},{7,5},{8,10},{9,11},{10,... | collective-permute-start | bytes 1572872 | tf_op jit(solution)/shard_map/ppermute | solution.py:852
  229.0 15.5 %copy-start.5 = (bf16[256,512]{1,0:T(8,128)(2,1)}, bf16[256,512]{1,0:T(8,128)(2,1)S(1)}, u32[]{:S(2)}) copy-start(bf16[256,512]{1,0:T(8,128)(2,1)S(1)} %reduce_sum.30.early_refs_0_) | copy-start | bytes 786436
  229.0 23.1 %collective-permute-start.19 = (bf16[256,512]{1,0:T(8,128)(2,1)S(1)}, bf16[256,512]{1,0:T(8,128)(2,1)S(1)}, u32[]{:S(2)}, u32[]{:S(2)}) collective-permute-start(bf16[256,512]{1,0:T(8,128)(2,1)S(1)} %reduce_sum.30.early_refs_0_), channel_id=1, source_target_pairs={{0,1},{1,0},{2,3},{3,2},{4,5},{5,4},{6,7},{7,6},{8,9},{9,8},{10,11... | collective-permute-start | bytes 786440 | tf_op jit(solution)/shard_map/ppermute | solution.py:852
  229.1 27.4 %collective-permute-start.20 = (bf16[256,512]{1,0:T(8,128)(2,1)S(1)}, bf16[256,512]{1,0:T(8,128)(2,1)S(1)}, u32[]{:S(2)}, u32[]{:S(2)}) collective-permute-start(bf16[256,512]{1,0:T(8,128)(2,1)S(1)} %reduce_sum.30.early_refs_0_), channel_id=1, source_target_pairs={{0,2},{1,3},{2,0},{3,1},{4,6},{5,7},{6,4},{7,5},{8,10},{9,11},{10,... | collective-permute-start | bytes 786440 | tf_op jit(solution)/shard_map/ppermute | solution.py:852
  229.8 27.9 %collective-permute-start.21 = (bf16[256,512]{1,0:T(8,128)(2,1)S(1)}, bf16[256,512]{1,0:T(8,128)(2,1)S(1)}, u32[]{:S(2)}, u32[]{:S(2)}) collective-permute-start(bf16[256,512]{1,0:T(8,128)(2,1)S(1)} %reduce_sum.30.early_refs_0_), channel_id=1, source_target_pairs={{0,3},{1,2},{2,1},{3,0},{4,7},{5,6},{6,5},{7,4},{8,11},{9,10},{10,... | collective-permute-start | bytes 786440 | tf_op jit(solution)/shard_map/ppermute | solution.py:852
  240.4 10.4 %copy-start.1 = (f32[1,256,1024]{2,1,0:T(8,128)S(1)}, f32[1,256,1024]{2,1,0:T(8,128)}, u32[]{:S(2)}) copy-start(f32[1,256,1024]{2,1,0:T(8,128)} %param.22) | copy-start | bytes 3145732
  240.4 10.4 %copy-start.10 = (bf16[2,256,1024]{2,1,0:T(8,128)(2,1)S(1)}, bf16[2,256,1024]{2,1,0:T(8,128)(2,1)}, u32[]{:S(2)}) copy-start(bf16[2,256,1024]{2,1,0:T(8,128)(2,1)} %get-tuple-element.142) | copy-start | bytes 3145732
  240.4 10.4 %copy-start.12 = (bf16[2,256,1024]{2,1,0:T(8,128)(2,1)S(1)}, bf16[2,256,1024]{2,1,0:T(8,128)(2,1)}, u32[]{:S(2)}) copy-start(bf16[2,256,1024]{2,1,0:T(8,128)(2,1)} %copy-done.11) | copy-start | bytes 3145732
  252.1 5.6 %copy-start.15 = (bf16[256,512]{1,0:T(8,128)(2,1)}, bf16[256,512]{1,0:T(8,128)(2,1)S(1)}, u32[]{:S(2)}) copy-start(bf16[256,512]{1,0:T(8,128)(2,1)S(1)} %collective-permute-done.19.early_refs_1_) | copy-start | bytes 786436
  263.9 16.7 %copy-start.27 = (f32[32,128]{1,0:T(8,128)S(1)}, f32[32,128]{1,0:T(8,128)}, u32[]{:S(2)}) copy-start(f32[32,128]{1,0:T(8,128)} %dt_ref.1) | copy-start | bytes 49156
  263.9 16.7 %copy-start.31 = (f32[32,128]{1,0:T(8,128)S(1)}, f32[32,128]{1,0:T(8,128)}, u32[]{:S(2)}) copy-start(f32[32,128]{1,0:T(8,128)} %param.33) | copy-start | bytes 49156
  264.0 16.7 %copy-start.32 = (f32[32,128]{1,0:T(8,128)S(1)}, f32[32,128]{1,0:T(8,128)}, u32[]{:S(2)}) copy-start(f32[32,128]{1,0:T(8,128)} %param.34) | copy-start | bytes 49156
  264.0 17.3 %copy-start.37 = (f32[3,32]{1,0:T(4,128)S(1)}, f32[3,32]{1,0:T(4,128)}, u32[]{:S(2)}) copy-start(f32[3,32]{1,0:T(4,128)} %param.41) | copy-start | bytes 1156
  264.0 17.3 %copy-start.38 = (f32[3,32]{1,0:T(4,128)S(1)}, f32[3,32]{1,0:T(4,128)}, u32[]{:S(2)}) copy-start(f32[3,32]{1,0:T(4,128)} %param.42) | copy-start | bytes 1156
  264.0 17.9 %copy-start.35 = (f32[384]{0:T(512)S(1)}, f32[384]{0:T(512)}, u32[]{:S(2)}) copy-start(f32[384]{0:T(512)} %gain_ref.1) | copy-start | bytes 4612
  264.0 17.9 %copy-start.39 = (f32[384]{0:T(512)S(1)}, f32[384]{0:T(512)}, u32[]{:S(2)}) copy-start(f32[384]{0:T(512)} %param.39) | copy-start | bytes 4612
  264.0 17.9 %copy-start.40 = (f32[384]{0:T(512)S(1)}, f32[384]{0:T(512)}, u32[]{:S(2)}) copy-start(f32[384]{0:T(512)} %param.40) | copy-start | bytes 4612
  264.0 18.6 %copy-start.28 = (f32[5,288]{1,0:T(8,128)S(1)}, f32[5,288]{1,0:T(8,128)}, u32[]{:S(2)}) copy-start(f32[5,288]{1,0:T(8,128)} %conv_ref.1) | copy-start | bytes 17284
  264.0 18.6 %copy-start.33 = (f32[5,288]{1,0:T(8,128)S(1)}, f32[5,288]{1,0:T(8,128)}, u32[]{:S(2)}) copy-start(f32[5,288]{1,0:T(8,128)} %param.37) | copy-start | bytes 17284
  264.1 18.6 %copy-start.34 = (f32[5,288]{1,0:T(8,128)S(1)}, f32[5,288]{1,0:T(8,128)}, u32[]{:S(2)}) copy-start(f32[5,288]{1,0:T(8,128)} %param.38) | copy-start | bytes 17284
  266.9 7.5 %collective-permute-start.24 = (bf16[192,512]{1,0:T(8,128)(2,1)}, bf16[192,512]{1,0:T(8,128)(2,1)S(1)}, u32[]{:S(2)}, u32[]{:S(2)}) collective-permute-start(bf16[192,512]{1,0:T(8,128)(2,1)} %sum_late.1.late_refs_0_), channel_id=1, source_target_pairs={{0,3},{1,2},{2,1},{3,0},{4,7},{5,6},{6,5},{7,4},{8,11},{9,10},{10,... | collective-permute-start | bytes 589832 | tf_op jit(solution)/shard_map/ppermute | solution.py:852
  268.8 9.9 %collective-permute-start.23 = (bf16[192,512]{1,0:T(8,128)(2,1)}, bf16[192,512]{1,0:T(8,128)(2,1)S(1)}, u32[]{:S(2)}, u32[]{:S(2)}) collective-permute-start(bf16[192,512]{1,0:T(8,128)(2,1)} %sum_late.1.late_refs_0_), channel_id=1, source_target_pairs={{0,2},{1,3},{2,0},{3,1},{4,6},{5,7},{6,4},{7,5},{8,10},{9,11},{10,... | collective-permute-start | bytes 589832 | tf_op jit(solution)/shard_map/ppermute | solution.py:852
  270.2 8.5 %collective-permute-start.22 = (bf16[192,512]{1,0:T(8,128)(2,1)}, bf16[192,512]{1,0:T(8,128)(2,1)S(1)}, u32[]{:S(2)}, u32[]{:S(2)}) collective-permute-start(bf16[192,512]{1,0:T(8,128)(2,1)} %sum_late.1.late_refs_0_), channel_id=1, source_target_pairs={{0,1},{1,0},{2,3},{3,2},{4,5},{5,4},{6,7},{7,6},{8,9},{9,8},{10,11... | collective-permute-start | bytes 589832 | tf_op jit(solution)/shard_map/ppermute | solution.py:852
  274.4 9.0 %copy-start.23 = (bf16[192,512]{1,0:T(8,128)(2,1)}, bf16[192,512]{1,0:T(8,128)(2,1)S(1)}, u32[]{:S(2)}) copy-start(bf16[192,512]{1,0:T(8,128)(2,1)S(1)} %collective-permute-done.24.late_refs_3_) | copy-start | bytes 589828
  278.7 4.7 %copy-start.24 = (bf16[192,512]{1,0:T(8,128)(2,1)}, bf16[192,512]{1,0:T(8,128)(2,1)S(1)}, u32[]{:S(2)}) copy-start(bf16[192,512]{1,0:T(8,128)(2,1)S(1)} %collective-permute-done.23.late_refs_2_) | copy-start | bytes 589828
  278.7 4.7 %copy-start.25 = (bf16[192,512]{1,0:T(8,128)(2,1)}, bf16[192,512]{1,0:T(8,128)(2,1)S(1)}, u32[]{:S(2)}) copy-start(bf16[192,512]{1,0:T(8,128)(2,1)S(1)} %collective-permute-done.22.late_refs_1_) | copy-start | bytes 589828
  (8 other events, 7.1 us)
Sparse Core Ops, SparseCore 0:
  11.4 73.7 all-gather.2

commit v6 on v5

--- a/solution.py
+++ b/solution.py
@@ -169,13 +169,17 @@
     tmp_ref[8 + CONV + 1 : 8 + CONV + 2, 0 : gain_ref.shape[0]] = gain_ref[...].reshape(1, -1)
     for copy in copies:
         w1_ref[copy, rows : rows + 16, :] = tmp_ref[...].astype(BF16)
+    copies = range(g2_ref.shape[0])
     for at, part in enumerate(pick_heads(win_ref, 0, ctx, heads)):
-        g2_ref[0:rows, at * 128 : (at + 1) * 128] = part.astype(BF16)
-    if g2_ref.shape[0] > rows:
+        part = part.astype(BF16)
+        for copy in copies:
+            g2_ref[copy, 0:rows, at * 128 : (at + 1) * 128] = part
+    if g2_ref.shape[1] > rows:
         some = wout_ref.shape[0] // 4
         mine = wout_ref[pl.ds(pl.multiple_of(ctx * some, 8), some), :].astype(BF16)
-        g2_ref[rows : rows + some] = mine[:, :width]
-        g2_ref[rows + some : rows + 2 * some] = mine[:, width:]
+        for copy in copies:
+            g2_ref[copy, rows : rows + some] = mine[:, :width]
+            g2_ref[copy, rows + some : rows + 2 * some] = mine[:, width:]
 
 
 def scan_forward_kernel(
@@ -787,8 +791,7 @@
 
     @pl.when(step == 0)
     def _():
-        for at, ref in enumerate(early_refs):
-            early_ref[pl.ds(here_ref[2] ^ at, 1)] = ref[...][None]
+        by_owner(early_refs, here_ref[2], early_ref)
 
     rows = weight_ref.shape[0]
     width = early_ref.shape[2]
@@ -803,23 +806,34 @@
             ref[:, lanes] = new
 
 
-def adam_in_kernel(here_ref, weight_ref, first_ref, second_ref, early_refs, late_refs, *rest):
-    new_refs, (early_ref, late_ref) = rest[:3], rest[3:]
+def by_owner(refs, ctx, natural_ref):
+    for at, ref in enumerate(refs):
+        natural_ref[pl.ds(ctx ^ at, 1)] = ref[...][None]
+
+
+def mixed_columns(ref, pair, odd):
+    lanes = slice(pair * 2 * HEAD_DIM, (pair + 1) * 2 * HEAD_DIM)
+    out = []
+    for at in range(0, ref.shape[0], 2):
+        first = ref[at, :, lanes].astype(F32)
+        second = ref[at + 1, :, lanes].astype(F32)
+        low = lax.broadcasted_iota(jnp.int32, first.shape, 1) < HEAD_DIM
+        if odd:
+            out.append(jnp.where(low, pltpu.roll(first, HEAD_DIM, 1), second))
+        else:
+            out.append(jnp.where(low, first, pltpu.roll(second, HEAD_DIM, 1)))
+    return out
+
+
+def adam_in_kernel(count, tail, here_ref, weight_ref, first_ref, second_ref, part_refs, *rest):
+    new_refs, (rows_ref, all_ref) = rest[-5:-2], rest[-2:]
     step = pl.program_id(0)
-    pieces = len(early_refs)
     rows = weight_ref.shape[0]
-    width = early_ref.shape[2]
-    block = pieces * HEAD_DIM
 
     @pl.when(step == 0)
     def _():
-        for at in range(pieces):
-            owner = pl.ds(here_ref[2] ^ at, 1)
-            early_ref[owner] = early_refs[at][...][None]
-            late_ref[owner] = late_refs[at][...][None]
-
-    here = pl.ds(pl.multiple_of(step * rows, rows), rows)
-    low = lax.broadcasted_iota(jnp.int32, (rows, 2 * HEAD_DIM), 1) < HEAD_DIM
+        by_owner(part_refs, here_ref[2], all_ref)
+        rows_ref[...] = all_ref[:, 0:rows, :]
 
     def update(lanes, grad):
         news = adam_step(
@@ -828,23 +842,27 @@
         for ref, new in zip(new_refs, news):
             ref[:, lanes] = new
 
-    for base, ref in ((0, early_ref), (INNER, late_ref)):
-        for pair in range(width // (2 * HEAD_DIM)):
-            lanes = slice(pair * 2 * HEAD_DIM, (pair + 1) * 2 * HEAD_DIM)
-            for at in range(0, pieces, 2):
-                first = ref[at, here, lanes].astype(F32)
-                second = ref[at + 1, here, lanes].astype(F32)
-                start = base + 2 * pair * block + at * HEAD_DIM
-                even = jnp.where(low, first, pltpu.roll(second, HEAD_DIM, 1))
-                update(slice(start, start + 2 * HEAD_DIM), even)
-                start = start + block
-                odd = jnp.where(low, pltpu.roll(first, HEAD_DIM, 1), second)
-                update(slice(start, start + 2 * HEAD_DIM), odd)
-    first = late_ref.shape[1] - 32
-    update(
-        slice(2 * INNER, 2 * INNER + 2 * STATE),
-        late_ref[step, first : first + 32, 0 : 2 * STATE].astype(F32),
-    )
+    for head in range(count):
+
+        @pl.when(step == head)
+        def _():
+            for at, grad in enumerate(mixed_columns(rows_ref, head // 2, head % 2)):
+                update(slice(at * 2 * HEAD_DIM, (at + 1) * 2 * HEAD_DIM), grad)
+
+    if tail:
+
+        @pl.when(step == count)
+        def _():
+            some = rows // all_ref.shape[0]
+            first = all_ref.shape[1] - 32
+            for at in range(all_ref.shape[0]):
+                grad = all_ref[at, first : first + some, 0 : 2 * STATE].astype(F32)
+                here = slice(at * some, (at + 1) * some)
+                news = adam_step(
+                    weight_ref[here], first_ref[here], second_ref[here], grad, 0.03, WEIGHT_DECAY
+                )
+                for ref, new in zip(new_refs, news):
+                    ref[here] = new
 
 
 def swap(value, axis, bit):
@@ -928,6 +946,7 @@
     tok = tokens[0]
     bits = jnp.stack([d & 1, d >> 1, c] if near else [0 * d, 0 * d, c]).astype(jnp.int32)
     perm = c ^ jnp.asarray([1, 3, 0, 2], jnp.int32)
+    perm_far = c ^ jnp.asarray([2, 3, 0, 1], jnp.int32)
     smem = pl.BlockSpec(memory_space=pltpu.SMEM)
     vmem = pl.BlockSpec(memory_space=pltpu.VMEM)
     anywhere = lambda pieces: [pl.BlockSpec(memory_space=pl.ANY)] * len(pieces)
@@ -937,33 +956,38 @@
         in_specs=[smem] + [vmem] * 5,
         out_shape=[
             shape_of(high if near else 1, rows_in + 16, wide, dtype=BF16),
-            shape_of(rows_in + (2 * HEAD_DIM if near else 0), width, dtype=BF16),
+            shape_of(high if near else 1, rows_in + (2 * HEAD_DIM if near else 0), width, dtype=BF16),
         ],
         scratch_shapes=[pltpu.VMEM((16, wide), F32)],
         compiler_params=params(),
         name="pack",
     )(bits, in_weight, out_weight, dt_weight, conv_params, gains)
-    tok_sent, w1 = lax.optimization_barrier((tok, w1))
-    tok_far = swap(tok_sent, "ctx", 2)
+    cot_low = cotangent[0].astype(BF16)
     if near:
+        tok_sent, w1 = lax.optimization_barrier((tok, w1))
+        tok_far = swap(tok_sent, "ctx", 2)
         w1 = high_all_to_all(w1)
-        w1, tok_far, tok_sent = lax.optimization_barrier((w1, tok_far, tok_sent))
-        w1 = [w1, swap(w1, "dp", 1)]
-        at_rows = jnp.stack([d & 1, 1 - (d & 1)]).astype(jnp.int32)
+        w1, tok_far, tok_sent, g2, cot_low = lax.optimization_barrier((w1, tok_far, tok_sent, g2, cot_low))
+        w1_came = swap(w1, "dp", 1)
+        toks = [tok, swap(tok_sent, "ctx", 1), tok_far, swap(tok_far, "ctx", 1)]
+        g2 = high_all_to_all(g2)
+        cot_far = swap(cot_low, "ctx", 2)
+        w1, w1_came, toks, g2, cot_far, cot_low = lax.optimization_barrier(
+            (w1, w1_came, toks, g2, cot_far, cot_low)
+        )
+        w1 = [w1, w1_came]
+        g2 = [g2, swap(g2, "dp", 1)]
+        cots = [cot_low, swap(cot_low, "ctx", 1), cot_far, swap(cot_far, "ctx", 1)]
+        at_rows = at_g2 = jnp.stack([d & 1, 1 - (d & 1)]).astype(jnp.int32)
     else:
         w1 = [lax.all_gather(w1[0], "dp", axis=0)]
-        at_rows = jnp.zeros((1,), jnp.int32)
-    toks = [tok, swap(tok_sent, "ctx", 1), tok_far, swap(tok_far, "ctx", 1)]
-    if near:
-        g2 = [lax.all_gather(g2, "dp", axis=0)]
-    else:
-        wg = lax.all_gather(g2, "dp", axis=0, tiled=True).reshape(heads, block_in, width)
+        toks = gather_ctx(tok)
+        cots = gather_ctx(cot_low)
+        wg = lax.all_gather(g2[0], "dp", axis=0, tiled=True).reshape(heads, block_in, width)
         wout = lax.all_gather(out_weight.astype(BF16), "dp", axis=0, tiled=True)
         wout = lax.dynamic_index_in_dim(wout.reshape(heads, nctx, HEAD_DIM, model), c, 1, False)
         g2 = [jnp.concatenate([wg, wout[:, :, :width], wout[:, :, width:]], axis=1)]
-    at_g2 = jnp.zeros((1,), jnp.int32)
-    cot_low, w1 = lax.optimization_barrier((cotangent[0].astype(BF16), w1))
-    cots = gather_ctx(cot_low)
+        at_rows = at_g2 = jnp.zeros((1,), jnp.int32)
 
     ids = segment_ids[0]
     seg_col = jnp.pad(ids, (8, 8), constant_values=-1)[:, None]
@@ -1117,8 +1141,8 @@
         ],
         compiler_params=params("arbitrary"),
         name="norm_back",
-    )(perm, bits, hid, inner, gate, normed_grad, stats, gain_mine, mixed, wout, cot_all)
-    block_came = swap(block_send, "ctx", 1)
+    )(perm_far, bits, hid, inner, gate, normed_grad, stats, gain_mine, mixed, wout, cot_all)
+    block_came = swap(block_send, "ctx", 2)
     if near:
         early_came = swap(early_send, "dp", 1)
 
@@ -1185,16 +1209,13 @@
         late_came = swap(late_send, "dp", 1)
         early_parts = pl.pallas_call(
             pair_sum_kernel,
-            grid=(high,),
-            in_specs=[pl.BlockSpec((1, early_rows, width), lambda i: (i, 0, 0))] * 2,
-            out_specs=pl.BlockSpec((1, early_rows, width), lambda i: (i, 0, 0)),
             out_shape=shape_of(high, early_rows, width, dtype=BF16),
-            compiler_params=params("arbitrary"),
+            compiler_params=params(),
             name="pair_sum_early",
         )(early_keep, early_came)
-        dval, early_parts = lax.optimization_barrier((dval, early_parts))
         early_parts = high_all_to_all(early_parts)
     dbc = (dbc.astype(F32) + dbc_came.astype(F32)).astype(BF16)
+    dval, dbc = lax.optimization_barrier((dval, dbc))
     dbc_far = swap(dbc, "ctx", 2)
 
     hidden_keep, hidden_send, gain_sum = pl.pallas_call(
@@ -1280,7 +1301,8 @@
     map_send, hidden_came, block_came = lax.optimization_barrier((map_send, hidden_came, block_came))
     hidden_far = (hidden_keep[1].astype(F32) + hidden_came[1].astype(F32)).astype(BF16)
     hidden_far = swap(hidden_far, "ctx", 2)
-    block_far = (block_keep[1].astype(F32) + block_came[1].astype(F32)).astype(BF16)
+    block_near = (block_keep[1].astype(F32) + block_came[1].astype(F32)).astype(BF16)
+    block_near = swap(block_near, "ctx", 1)
     mine = pl.BlockSpec((1, span, model), lambda i: (0, 0, 0))
     input_grad = pl.pallas_call(
         input_back_kernel,
@@ -1291,9 +1313,8 @@
         compiler_params=params("arbitrary"),
         name="input_back",
     )(hidden_keep, hidden_came, hidden_far, hidden_own, tok, gain_pre, cotangent[0])
-    block_far = swap(block_far, "ctx", 2)
     block_output = tok + (
-        block_keep[0].astype(F32) + block_came[0].astype(F32) + block_far.astype(F32)
+        block_keep[0].astype(F32) + block_came[0].astype(F32) + block_near.astype(F32)
     )
 
     late_rows = block_in + 64
@@ -1316,9 +1337,8 @@
             compiler_params=params(),
             name="sum_late",
         )(late_parts)
-        early, late = fan_ctx(early), fan_ctx(late)
+        early, late = gather_ctx(early), fan_ctx(late)
         row_block = lambda ref_rows, cols: pl.BlockSpec((ref_rows, cols), lambda i, *_: (i, 0))
-        in_block = row_block(rows_in // nctx, in_weight.shape[1])
         out_block = row_block(out_weight.shape[0] // nctx, model)
         early_spec = [full((early_rows, width))] * nctx
         early_scratch = pltpu.VMEM((nctx, early_rows, width), BF16)
@@ -1335,19 +1355,30 @@
             compiler_params=params("arbitrary"),
             name="adam_out",
         )(bits, out_weight, out_first, out_second, early)
-        in_new = pl.pallas_call(
-            adam_in_kernel,
-            grid_spec=pltpu.PrefetchScalarGridSpec(
-                num_scalar_prefetch=1,
-                grid=(nctx,),
-                in_specs=[in_block] * 3 + [early_spec, [full((late_rows, width))] * nctx],
-                out_specs=[in_block] * 3,
-                scratch_shapes=[early_scratch, pltpu.VMEM((nctx, late_rows, width), BF16)],
-            ),
-            out_shape=[shape_of(*in_weight.shape)] * 3,
-            compiler_params=params("arbitrary"),
-            name="adam_in",
-        )(bits, in_weight, in_first, in_second, early, late)
+
+        def adam_in(first_block, steps, tail, parts, part_rows, done, name):
+            part = pl.BlockSpec((rows_in, nctx * HEAD_DIM), lambda i, *_: (0, first_block + i))
+            return pl.pallas_call(
+                functools.partial(adam_in_kernel, heads, tail),
+                grid_spec=pltpu.PrefetchScalarGridSpec(
+                    num_scalar_prefetch=1,
+                    grid=(steps,),
+                    in_specs=[part] * 3 + [[full((part_rows, width))] * nctx] + anywhere(done),
+                    out_specs=[part] * 3,
+                    scratch_shapes=[
+                        pltpu.VMEM((nctx, rows_in, width), BF16),
+                        pltpu.VMEM((nctx, part_rows, width), BF16),
+                    ],
+                ),
+                out_shape=[shape_of(*in_weight.shape)] * 3,
+                input_output_aliases={4 + nctx + at: at for at in range(len(done))},
+                compiler_params=params("arbitrary"),
+                name=name,
+            )(bits, in_weight, in_first, in_second, parts, *done)
+
+        in_new = adam_in(0, heads, False, early, early_rows, [], "adam_gate")
+        late, in_new = lax.optimization_barrier((late, in_new))
+        in_new = adam_in(heads, heads + 1, True, late, late_rows, in_new, "adam_rest")
         in_new, out_new = tuple(in_new), tuple(out_new)
         small = jnp.stack([part[block_in : block_in + 32] for part in late])[c ^ jnp.arange(nctx)]
         small = small.astype(F32)

time: 300 us -> 273 us (0.910)
  waiting for transfers between devices: 119 us -> 87.4 us
  between operations: 14.6 us -> 1.22 us
  Pallas kernels: 107 us -> 115 us
  starting transfers between devices: 35.4 us -> 40.8 us
    ppermute x25 -> x26, waiting for transfers between devices: 113 us -> 87.1 us  [swap(): return lax.ppermute(value, axis, [(at, at ^ bit) for at in range(count)])]
    pallas_call x2 -> x3, Pallas kernels: 12 us -> 19.9 us  [the longest x2 17 us: adam_in(): pl.pallas_call(functools.partial(adam_in_kernel, heads, tail), grid_spec=...]
    all_to_all x3 -> x4, starting transfers between devices: 14.9 us -> 20.9 us  [high_all_to_all(): return lax.all_to_all(value, 'dp', 0, 0, axis_index_groups=groups)]
    all_to_all x3 -> x4, waiting for transfers between devices: 5.92 us -> 0.29 us  [high_all_to_all(): return lax.all_to_all(value, 'dp', 0, 0, axis_index_groups=groups)]
    unnamed x89 -> x91, local copies, waits for them, and re-layouts: 5.99 us -> 7.73 us
    ppermute x25 -> x26, starting transfers between devices: 20.5 us -> 19.9 us  [swap(): return lax.ppermute(value, axis, [(at, at ^ bit) for at in range(count)])]
  transfers between devices with their start and end apart: 29 -> 30, of which waited for: 15 -> 12; matrix products, arithmetic and copies ran while one was open for 3% -> 4% of each run, Pallas kernels for 22% -> 27%
where the time goes in v6:
time: 273 us; the launch traced here: 271 us
  Pallas kernels  115 us (42%)
  waiting for transfers between devices  87.4 us (32%)
  starting transfers between devices  40.8 us (15%)
  other arithmetic  14.1 us (5%)
  local copies, waits for them, and re-layouts  12.2 us (4%)
    ppermute x26, waiting for transfers between devices, swap(): return lax.ppermute(value, axis, [(at, at ^ bit) for at in range(count)])  87.1 us
    pallas_call x1, Pallas kernels, shards(): pl.pallas_call(scan_back_kernel, grid_spec=pltpu.PrefetchScalarGridSpec(n...  21.9 us
    all_to_all x4, starting transfers between devices, high_all_to_all(): return lax.all_to_all(value, 'dp', 0, 0, axis_index_groups=groups)  20.9 us
    ppermute x26, starting transfers between devices, swap(): return lax.ppermute(value, axis, [(at, at ^ bit) for at in range(count)])  19.9 us
    pallas_call x1, Pallas kernels, shards(): pl.pallas_call(scan_forward_kernel, grid_spec=pltpu.PrefetchScalarGridSpe...  18.2 us
    pallas_call x2, Pallas kernels, adam_in(): pl.pallas_call(functools.partial(adam_in_kernel, heads, tail), grid_spec=...  17 us
    pallas_call x1, Pallas kernels, shards(): pl.pallas_call(norm_back_kernel, grid_spec=pltpu.PrefetchScalarGridSpec(n...  13.2 us
    pallas_call x1, Pallas kernels, shards(): pl.pallas_call(gate_kernel, grid_spec=pltpu.PrefetchScalarGridSpec(num_sc...  10.6 us
  transfers between devices with their start and end apart: 30, of which 12 were waited for; matrix products, arithmetic and copies ran while one was open for 4% of the time, Pallas kernels for 27%

profile of v6, /device:TPU:0, one launch (start us, length us, event | category | flops | bytes accessed | tf_op | source)
XLA Modules:
  0.0 271.1 jit_solution(5864581973124050107)
XLA Ops:
  0.7 0.6 pad_add_fusion.here_ref
  1.3 3.6 %pack.1 = (bf16[4,144,768]{2,1,0:T(8,128)(2,1)}, bf16[4,256,512]{2,1,0:T(8,128)(2,1)}) custom-call(s32[3]{0:T(128)} %pad_add_fusion.here_ref, f32[128,4352]{1,0:T(8,128)} %weight_ref.4, f32[256,1024]{1,0:T(8,128)} %weight_ref.5, f32[32,128]{1,0:T(8,128)} %dt_ref.1, f32[5,288]{1,0:T(8,128)} %conv_ref.1, f32[384]{0:T(512)} %gain_ref.1), custom_call_target="tpu_custom_call" | custom-call | tf_op jit(solution)/shard_map/pack/pallas_call | solution.py:954
  4.8 6.3 %all-to-all-start = ((bf16[4,144,768]{2,1,0:T(8,128)(2,1)}), bf16[4,144,768]{2,1,0:T(8,128)(2,1)S(1)}, u32[]{:S(2)}, u32[]{:S(2)}) async-start(bf16[4,144,768]{2,1,0:T(8,128)(2,1)} %get-tuple-element.106), calls=%async_computation | async-start | bytes 1769472 | tf_op jit(solution)/shard_map/all_to_all | solution.py:881
  11.2 1.6 collective-permute-start
  12.8 23.1 %collective-permute-done.tok_pieces_2_ = f32[256,1024]{1,0:T(8,128)} collective-permute-done((f32[256,1024]{1,0:T(8,128)S(1)}, f32[256,1024]{1,0:T(8,128)}, u32[]{:S(2)}, u32[]{:S(2)}) %collective-permute-start) | collective-permute-done | bytes 1048608 | tf_op jit(solution)/shard_map/ppermute | solution.py:870
  36.0 4.8 %all-to-all-start.1 = ((bf16[4,256,512]{2,1,0:T(8,128)(2,1)}), bf16[4,256,512]{2,1,0:T(8,128)(2,1)S(1)}, u32[]{:S(2)}, u32[]{:S(2)}) async-start(bf16[4,256,512]{2,1,0:T(8,128)(2,1)} %get-tuple-element.112), calls=%async_computation.1 | async-start | bytes 2097152 | tf_op jit(solution)/shard_map/all_to_all | solution.py:881
  41.3 1.5 collective-permute-start.1
  42.8 1.5 collective-permute-start.4
  44.3 12.0 %collective-permute-done.4.cot_pieces_2_ = bf16[256,1024]{1,0:T(8,128)(2,1)S(1)} collective-permute-done((bf16[256,1024]{1,0:T(8,128)(2,1)S(1)}, bf16[256,1024]{1,0:T(8,128)(2,1)S(1)}, u32[]{:S(2)}, u32[]{:S(2)}) %collective-permute-start.4) | collective-permute-done | bytes 524320 | tf_op jit(solution)/shard_map/ppermute | solution.py:870
  56.3 6.5 %collective-permute-done.1.w1_pieces_1_ = bf16[4,144,768]{2,1,0:T(8,128)(2,1)S(1)} collective-permute-done((bf16[4,144,768]{2,1,0:T(8,128)(2,1)S(1)}, bf16[4,144,768]{2,1,0:T(8,128)(2,1)S(1)}, u32[]{:S(2)}, u32[]{:S(2)}) %collective-permute-start.1) | collective-permute-done | bytes 884768 | tf_op jit(solution)/shard_map/ppermute | solution.py:870
  62.8 0.9 copy-done.17
  63.7 1.0 copy-done.11
  65.0 1.5 collective-permute-start.5
  67.2 0.7 copy.70
  68.0 1.0 broadcast_in_dim.13.segc_ref
  69.0 0.6 pad_add_fusion.1.at_ref
  69.6 18.2 %scan_forward.1 = (bf16[1024,1024]{1,0:T(8,128)(2,1)}, f32[8,768]{1,0:T(8,128)}, f32[1,1024]{1,0:T(1,128)}, f32[1,512]{1,0:T(1,128)}, bf16[8,1024]{1,0:T(8,128)(...) custom-call(s32[3]{0:T(128)} %pad_add_fusion.here_ref, ...), custom_call_target="tpu_custom_call" | custom-call | tf_op jit(solution)/shard_map/scan_forward/pallas_call | solution.py:1008
  87.9 1.2 collective-permute-done.5.g2_pieces_1_
  89.1 1.0 copy-done.12
  90.1 10.6 %gate.1 = (bf16[1024,512]{1,0:T(8,128)(2,1)}, bf16[512,1024]{1,0:T(8,128)(2,1)}, bf16[4,256,1024]{2,1,0:T(8,128)(2,1)}, bf16[1024,512]{1,0:T(8,128)(2,1)}, f32[1024,512]{1,0:T(8,128)}, /*index=5*/f32[8,1024]{1,0:T(8,128)}) custom-call(s32[3]{0:T(128)} %pad_add_fusion.here_ref, s32[2]{0:T(128)} %pad_add_fusion.1.at_ref, ...), custom_call_target="tpu_custom_call" | custom-call | tf_op jit(solution)/shard_map/gate/pallas_call | solution.py:1073
  100.7 1.6 collective-permute-start.9
  103.1 1.4 collective-permute-done.10
  105.0 1.4 add_add_fusion.stat_ref
  106.4 13.2 %norm_back.1 = (bf16[2,256,1024]{2,1,0:T(8,128)(2,1)}, bf16[2,256,1024]{2,1,0:T(8,128)(2,1)}, bf16[4,256,512]{2,1,0:T(8,128)(2,1)}, bf16[4,256,512]{2,1,0:T(8,12...) custom-call(s32[4]{0:T(128)} %broadcast_xor_fusion.perm_ref, s32[3]{0:T(128)} %pad_add_fusion.here_ref, ...), custom_call_target="tpu_custom_call" | custom-call | tf_op jit(solution)/shard_map/norm_back/pallas_call | solution.py:1106
  119.6 1.6 collective-permute-start.22
  121.7 21.9 %scan_back.1 = (bf16[4,128,512]{2,1,0:T(8,128)(2,1)}, bf16[4,128,512]{2,1,0:T(8,128)(2,1)}, bf16[1024,512]{1,0:T(8,128)(2,1)}, bf16[1024,256]{1,0:T(8,128)(2,1)}...) custom-call(s32[4]{0:T(128)} %broadcast_xor_fusion.1.perm_ref, ...), custom_call_target="tpu_custom_call" | custom-call | tf_op jit(solution)/shard_map/scan_back/pallas_call | solution.py:1151
  143.7 1.6 collective-permute-done.22.came_ref
  145.3 1.0 copy-done.13
  146.3 2.9 %pair_sum_early.1 = bf16[4,256,512]{2,1,0:T(8,128)(2,1)} custom-call(bf16[4,256,512]{2,1,0:T(8,128)(2,1)} %get-tuple-element.172.keep_ref, bf16[4,256,512]{2,1,0:T(8,128)(2,1)} %copy-done.13), custom_call_target="tpu_custom_call" | custom-call | tf_op jit(solution)/shard_map/pair_sum_early/pallas_call | solution.py:1210
  149.2 5.0 %all-to-all-start.3 = ((bf16[4,256,512]{2,1,0:T(8,128)(2,1)}), bf16[4,256,512]{2,1,0:T(8,128)(2,1)S(1)}, u32[]{:S(2)}, u32[]{:S(2)}) async-start(bf16[4,256,512]{2,1,0:T(8,128)(2,1)} %pair_sum_early.1), calls=%async_computation.3 | async-start | bytes 2097152 | tf_op jit(solution)/shard_map/all_to_all | solution.py:881
  154.2 1.0 collective-permute-start.15
  155.3 8.2 %hidden_back.1 = (bf16[2,256,1024]{2,1,0:T(8,128)(2,1)}, bf16[2,256,1024]{2,1,0:T(8,128)(2,1)}, f32[8,1024]{1,0:T(8,128)}) custom-call(s32[4]{0:T(128)} %broadcast_xor_fusion.1.perm_ref, bf16[1024,512]{1,0:T(8,128)(2,1)} %get-tuple-element.153.dgate_ref, bf16[1024,512]{1,0:T(8,128)(2,1)} %get-tuple-element.154.dval_ref, ...), custom_call_target="tpu_custom_call" | custom-call | tf_op jit(solution)/shard_map/hidden_back/pallas_call | solution.py:1221
  163.6 1.1 collective-permute-start.13
  164.7 1.5 collective-permute-start.11
  166.2 23.5 %collective-permute-done.13.dbcfar_ref = bf16[1024,256]{1,0:T(8,128)(2,1)S(1)} collective-permute-done((bf16[1024,256]{1,0:T(8,128)(2,1)S(1)}, bf16[1024,256]{1,0:T(8,128)(2,1)S(1)}, u32[]{:S(2)}, u32[]{:S(2)}) %collective-permute-start.13) | collective-permute-done | bytes 524320 | tf_op jit(solution)/shard_map/ppermute | solution.py:870
  189.8 0.8 copy-done.20
  190.5 6.2 %maps_back.1 = (bf16[160,512]{1,0:T(8,128)(2,1)}, bf16[160,512]{1,0:T(8,128)(2,1)}, f32[256,1024]{1,0:T(8,128)}) custom-call(s32[3]{0:T(128)} %pad_add_fusion.here_ref, bf16[1024,256]{1,0:T(8,128)(2,1)} %copy-done.9, bf16[1024,256]{1,0:T(8,128)(2,1)} %copy-done.20, f32[1024,768]{1,0:T(8,128)} %get-tuple-element.134.convsum_ref, ...), custom_call_target="tpu_custom_call" | custom-call | tf_op jit(solution)/shard_map/maps_back/pallas_call | solution.py:1249
  196.8 1.5 collective-permute-start.16
  198.3 4.1 %collective-permute-done.16.mcame_ref = bf16[160,512]{1,0:T(8,128)(2,1)S(1)} collective-permute-done((bf16[160,512]{1,0:T(8,128)(2,1)}, bf16[160,512]{1,0:T(8,128)(2,1)S(1)}, u32[]{:S(2)}, u32[]{:S(2)}) %collective-permute-start.16) | collective-permute-done | bytes 163872 | tf_op jit(solution)/shard_map/ppermute | solution.py:870
  202.4 0.6 copy-done.25
  203.1 2.3 pair_sum_late.1
  205.4 4.8 %all-to-all-start.2 = ((bf16[4,192,512]{2,1,0:T(8,128)(2,1)}), bf16[4,192,512]{2,1,0:T(8,128)(2,1)S(1)}, u32[]{:S(2)}, u32[]{:S(2)}) async-start(bf16[4,192,512]{2,1,0:T(8,128)(2,1)} %pair_sum_late.1), calls=%async_computation.2 | async-start | bytes 1572864 | tf_op jit(solution)/shard_map/all_to_all | solution.py:881
  210.2 2.3 fusion.2
  212.7 0.8 collective-permute-start.24
  213.6 2.2 fusion.1
  215.8 1.3 collective-permute-start.17
  217.1 4.9 %collective-permute-done.24.part_refs_2_.early_refs_2_ = bf16[256,512]{1,0:T(8,128)(2,1)S(1)} collective-permute-done((bf16[256,512]{1,0:T(8,128)(2,1)S(1)}, bf16[256,512]{1,0:T(8,128)(2,1)S(1)}, u32[]{:S(2)}, u32[]{:S(2)}) %collective-permute-start.24) | collective-permute-done | bytes 262176 | tf_op jit(solution)/shard_map/ppermute | solution.py:870
  221.9 2.7 fusion
  224.6 8.2 %collective-permute-done.17.far_ref = bf16[256,1024]{1,0:T(8,128)(2,1)} collective-permute-done((bf16[256,1024]{1,0:T(8,128)(2,1)}, bf16[256,1024]{1,0:T(8,128)(2,1)}, u32[]{:S(2)}, u32[]{:S(2)}) %collective-permute-start.17) | collective-permute-done | bytes 524320 | tf_op jit(solution)/shard_map/ppermute | solution.py:870
  232.9 3.9 %input_back.1 = f32[256,1024]{1,0:T(8,128)} custom-call(bf16[2,256,1024]{2,1,0:T(8,128)(2,1)} %get-tuple-element.164.keep_ref, bf16[2,256,1024]{2,1,0:T(8,128)(2,1)} %copy-done.7, bf16[256,1024]{1,0:T(8,128)(2,1)} %collective-permute-done.17.far_ref, f32[256,1024]{1,0:T(8,128)} %get-tuple-element.166.own_ref, f32[256,1024]{1,0:T(8,128)} %bitcast.53, ...), custom_call_target="tpu_custom_call" | custom-call | tf_op jit(solution)/shard_map/input_back/pallas_call | solution.py:1307
  236.8 0.9 copy-done.5
  237.7 1.9 sum_late.1.part_refs_0_
  239.6 0.7 collective-permute-start.20
  240.3 1.1 collective-permute-start.21
  241.5 0.7 copy-done.15
  242.2 0.7 copy-done.16
  242.9 8.1 %adam_gate.1 = (f32[128,4352]{1,0:T(8,128)}, f32[128,4352]{1,0:T(8,128)}, f32[128,4352]{1,0:T(8,128)}) custom-call(s32[3]{0:T(128)} %pad_add_fusion.here_ref, f32[128,4352]{1,0:T(8,128)} %weight_ref.4, f32[128,4352]{1,0:T(8,128)} %first_ref.4, f32[128,4352]{1,0:T(8,128)} %second_ref.4, bf16[256,512]{1,0:T(8,128)(2,1)} %copy-done.6, ...), custom_call_target="tpu_custom_call" | custom-call | tf_op jit(solution)/shard_map/adam_gate/pallas_call | solution.py:1361
  251.1 0.8 slice_bitcast_fusion.3
  254.0 8.9 %adam_rest.1 = (f32[128,4352]{1,0:T(8,128)}, f32[128,4352]{1,0:T(8,128)}, f32[128,4352]{1,0:T(8,128)}) custom-call(s32[3]{0:T(128)} %pad_add_fusion.here_ref, f32[128,4352]{1,0:T(8,128)} %weight_ref.4, f32[128,4352]{1,0:T(8,128)} %first_ref.4, f32[128,4352]{1,0:T(8,128)} %second_ref.4, ...), custom_call_target="tpu_custom_call", output_to_operand_aliasing={{0}: (8, {}), {1}: (9, {}), {2}: (10, {})} | custom-call | tf_op jit(solution)/shard_map/adam_rest/pallas_call | solution.py:1361
  262.9 0.6 multiply_subtract_fusion
  263.6 0.7 multiply_subtract_fusion.1
  264.3 0.7 multiply_subtract_fusion.3
  265.0 0.6 multiply_subtract_fusion.2
  265.6 5.5 %adam_out.1 = (f32[256,1024]{1,0:T(8,128)}, f32[256,1024]{1,0:T(8,128)}, f32[256,1024]{1,0:T(8,128)}) custom-call(s32[3]{0:T(128)} %pad_add_fusion.here_ref, f32[256,1024]{1,0:T(8,128)} %weight_ref.5, f32[256,1024]{1,0:T(8,128)} %first_ref.5, f32[256,1024]{1,0:T(8,128)} %second_ref.5, bf16[256,512]{1,0:T(8,128)(2,1)} %copy-done.6, ...), custom_call_target="tpu_custom_call" | custom-call | tf_op jit(solution)/shard_map/adam_out/pallas_call | solution.py:1345
  (151 shorter events, 6.1 us)
Async XLA Ops:
  1.2 9.9 %copy-start = (f32[1,256,1024]{2,1,0:T(8,128)S(1)}, f32[1,256,1024]{2,1,0:T(8,128)}, u32[]{:S(2)}) copy-start(f32[1,256,1024]{2,1,0:T(8,128)} %param.23) | copy-start | bytes 3145732
  1.2 11.5 %copy-start.3 = (f32[1,256,1024]{2,1,0:T(8,128)S(1)}, f32[1,256,1024]{2,1,0:T(8,128)}, u32[]{:S(2)}) copy-start(f32[1,256,1024]{2,1,0:T(8,128)} %param.25) | copy-start | bytes 3145732
  4.8 31.1 %all-to-all-start = ((bf16[4,144,768]{2,1,0:T(8,128)(2,1)}), bf16[4,144,768]{2,1,0:T(8,128)(2,1)S(1)}, u32[]{:S(2)}, u32[]{:S(2)}) async-start(bf16[4,144,768]{2,1,0:T(8,128)(2,1)} %get-tuple-element.106), calls=%async_computation | async-start | bytes 1769472 | tf_op jit(solution)/shard_map/all_to_all | solution.py:881
  11.2 55.9 %copy-start.35 = (f32[3,32]{1,0:T(4,128)S(1)}, f32[3,32]{1,0:T(4,128)}, u32[]{:S(2)}) copy-start(f32[3,32]{1,0:T(4,128)} %param.31) | copy-start | bytes 1156
  11.2 56.8 %copy-start.28 = (s32[1,1024]{1,0:T(1,128)S(1)}, s32[1,1024]{1,0:T(1,128)}, u32[]{:S(2)}) copy-start(s32[1,1024]{1,0:T(1,128)} %segr_ref.3) | copy-start | bytes 12292
  11.2 24.8 %collective-permute-start = (f32[256,1024]{1,0:T(8,128)S(1)}, f32[256,1024]{1,0:T(8,128)}, u32[]{:S(2)}, u32[]{:S(2)}) collective-permute-start(f32[256,1024]{1,0:T(8,128)S(1)} %bitcast.54), channel_id=1, source_target_pairs={{0,2},{1,3},{2,0},{3,1},{4,6},{5,7},{6,4},{7,5},{8,10},{9,11},{10,... | collective-permute-start | bytes 3145736 | tf_op jit(solution)/shard_map/ppermute | solution.py:870
  12.8 75.0 %copy-start.8 = (bf16[256,1024]{1,0:T(8,128)(2,1)}, bf16[256,1024]{1,0:T(8,128)(2,1)S(1)}, u32[]{:S(2)}) copy-start(bf16[256,1024]{1,0:T(8,128)(2,1)S(1)} %bitcast_convert_fusion.cot_pieces_0_) | copy-start | bytes 1572868
  36.0 33.6 %copy-start.4 = (bf16[4,144,768]{2,1,0:T(8,128)(2,1)}, bf16[4,144,768]{2,1,0:T(8,128)(2,1)S(1)}, u32[]{:S(2)}) copy-start(bf16[4,144,768]{2,1,0:T(8,128)(2,1)S(1)} %all-to-all-done.w1_pieces_0_) | copy-start | bytes 2654212
  36.0 29.0 %all-to-all-start.1 = ((bf16[4,256,512]{2,1,0:T(8,128)(2,1)}), bf16[4,256,512]{2,1,0:T(8,128)(2,1)S(1)}, u32[]{:S(2)}, u32[]{:S(2)}) async-start(bf16[4,256,512]{2,1,0:T(8,128)(2,1)} %get-tuple-element.112), calls=%async_computation.1 | async-start | bytes 2097152 | tf_op jit(solution)/shard_map/all_to_all | solution.py:881
  40.8 22.1 %collective-permute-start.2 = (f32[256,1024]{1,0:T(8,128)S(1)}, f32[256,1024]{1,0:T(8,128)S(1)}, u32[]{:S(2)}, u32[]{:S(2)}) collective-permute-start(f32[256,1024]{1,0:T(8,128)S(1)} %bitcast.55), channel_id=1, source_target_pairs={{0,1},{1,0},{2,3},{3,2},{4,5},{5,4},{6,7},{7,6},{8,9},{9,8},{10,11... | collective-permute-start | bytes 3145736 | tf_op jit(solution)/shard_map/ppermute | solution.py:870
  40.8 23.9 %collective-permute-start.3 = (f32[256,1024]{1,0:T(8,128)}, f32[256,1024]{1,0:T(8,128)}, u32[]{:S(2)}, u32[]{:S(2)}) collective-permute-start(f32[256,1024]{1,0:T(8,128)} %collective-permute-done.tok_pieces_2_), channel_id=1, source_target_pairs={{0,1},{1,0},{2,3},{3,2},{4,5},{5,4},{6,7},{7,6},{8,9},{9,8},{10,11... | collective-permute-start | bytes 3145736 | tf_op jit(solution)/shard_map/ppermute | solution.py:870
  41.3 21.6 %collective-permute-start.1 = (bf16[4,144,768]{2,1,0:T(8,128)(2,1)S(1)}, bf16[4,144,768]{2,1,0:T(8,128)(2,1)S(1)}, u32[]{:S(2)}, u32[]{:S(2)}) collective-permute-start(bf16[4,144,768]{2,1,0:T(8,128)(2,1)S(1)} %all-to-all-done.w1_pieces_0_), channel_id=1, source_target_pairs={{0,4},{4,0},{8,12},{12,8},{16,20},{20,16},{24,28},{28,24},{1,5},{5... | collective-permute-start | bytes 2654216 | tf_op jit(solution)/shard_map/ppermute | solution.py:870
  42.8 13.6 %collective-permute-start.4 = (bf16[256,1024]{1,0:T(8,128)(2,1)S(1)}, bf16[256,1024]{1,0:T(8,128)(2,1)S(1)}, u32[]{:S(2)}, u32[]{:S(2)}) collective-permute-start(bf16[256,1024]{1,0:T(8,128)(2,1)S(1)} %bitcast_convert_fusion.cot_pieces_0_), channel_id=1, source_target_pairs={{0,2},{1,3},{2,0},{3,1},{4,6},{5,7},{6,4},{7,5},{8,10},{9,11},{10,... | collective-permute-start | bytes 1572872 | tf_op jit(solution)/shard_map/ppermute | solution.py:870
  56.3 6.5 %copy-start.18 = (bf16[256,1024]{1,0:T(8,128)(2,1)}, bf16[256,1024]{1,0:T(8,128)(2,1)S(1)}, u32[]{:S(2)}) copy-start(bf16[256,1024]{1,0:T(8,128)(2,1)S(1)} %collective-permute-done.4.cot_pieces_2_) | copy-start | bytes 1572868
  65.0 22.9 %copy-start.2 = (bf16[4,256,512]{2,1,0:T(8,128)(2,1)}, bf16[4,256,512]{2,1,0:T(8,128)(2,1)S(1)}, u32[]{:S(2)}) copy-start(bf16[4,256,512]{2,1,0:T(8,128)(2,1)S(1)} %all-to-all-done.1.g2_pieces_0_) | copy-start | bytes 3145732
  65.0 24.1 %collective-permute-start.5 = (bf16[4,256,512]{2,1,0:T(8,128)(2,1)S(1)}, bf16[4,256,512]{2,1,0:T(8,128)(2,1)S(1)}, u32[]{:S(2)}, u32[]{:S(2)}) collective-permute-start(bf16[4,256,512]{2,1,0:T(8,128)(2,1)S(1)} %all-to-all-done.1.g2_pieces_0_), channel_id=1, source_target_pairs={{0,4},{4,0},{8,12},{12,8},{16,20},{20,16},{24,28},{28,24},{1,5},{5... | collective-permute-start | bytes 3145736 | tf_op jit(solution)/shard_map/ppermute | solution.py:870
  66.5 21.4 %collective-permute-start.6 = (bf16[256,1024]{1,0:T(8,128)(2,1)S(1)}, bf16[256,1024]{1,0:T(8,128)(2,1)}, u32[]{:S(2)}, u32[]{:S(2)}) collective-permute-start(bf16[256,1024]{1,0:T(8,128)(2,1)S(1)} %bitcast_convert_fusion.cot_pieces_0_), channel_id=1, source_target_pairs={{0,1},{1,0},{2,3},{3,2},{4,5},{5,4},{6,7},{7,6},{8,9},{9,8},{10,11... | collective-permute-start | bytes 1572872 | tf_op jit(solution)/shard_map/ppermute | solution.py:870
  66.5 21.4 %collective-permute-start.7 = (bf16[256,1024]{1,0:T(8,128)(2,1)}, bf16[256,1024]{1,0:T(8,128)(2,1)}, u32[]{:S(2)}, u32[]{:S(2)}) collective-permute-start(bf16[256,1024]{1,0:T(8,128)(2,1)} %copy-done.18), channel_id=1, source_target_pairs={{0,1},{1,0},{2,3},{3,2},{4,5},{5,4},{6,7},{7,6},{8,9},{9,8},{10,11... | collective-permute-start | bytes 1572872 | tf_op jit(solution)/shard_map/ppermute | solution.py:870
  90.1 12.5 %copy-start.43 = (s32[4]{0:T(128)S(1)}, s32[4]{0:T(128)}, u32[]{:S(2)}) copy-start(s32[4]{0:T(128)} %constant.17.clone) | copy-start | bytes 52
  100.7 3.9 %collective-permute-start.10 = (f32[8,1024]{1,0:T(8,128)}, f32[8,1024]{1,0:T(8,128)S(1)}, u32[]{:S(2)}, u32[]{:S(2)}) collective-permute-start(f32[8,1024]{1,0:T(8,128)} %get-tuple-element.128), channel_id=1, source_target_pairs={{0,3},{1,2},{2,1},{3,0},{4,7},{5,6},{6,5},{7,4},{8,11},{9,10},{10,... | collective-permute-start | bytes 98312 | tf_op jit(solution)/shard_map/ppermute | solution.py:870
  100.7 4.2 %collective-permute-start.9 = (f32[8,1024]{1,0:T(8,128)}, f32[8,1024]{1,0:T(8,128)S(1)}, u32[]{:S(2)}, u32[]{:S(2)}) collective-permute-start(f32[8,1024]{1,0:T(8,128)} %get-tuple-element.128), channel_id=1, source_target_pairs={{0,2},{1,3},{2,0},{3,1},{4,6},{5,7},{6,4},{7,5},{8,10},{9,11},{10,... | collective-permute-start | bytes 98312 | tf_op jit(solution)/shard_map/ppermute | solution.py:870
  102.3 2.7 collective-permute-start.8
  106.4 14.8 %copy-start.42 = (s32[4]{0:T(128)S(1)}, s32[4]{0:T(128)}, u32[]{:S(2)}) copy-start(s32[4]{0:T(128)} %constant.16.clone) | copy-start | bytes 52
  119.6 25.7 %collective-permute-start.22 = (bf16[4,256,512]{2,1,0:T(8,128)(2,1)}, bf16[4,256,512]{2,1,0:T(8,128)(2,1)S(1)}, u32[]{:S(2)}, u32[]{:S(2)}) collective-permute-start(bf16[4,256,512]{2,1,0:T(8,128)(2,1)} %get-tuple-element.173), channel_id=1, source_target_pairs={{0,4},{4,0},{8,12},{12,8},{16,20},{20,16},{24,28},{28,24},{1,5},{5... | collective-permute-start | bytes 3145736 | tf_op jit(solution)/shard_map/ppermute | solution.py:870
  143.5 11.6 %collective-permute-start.12 = (bf16[1024,256]{1,0:T(8,128)(2,1)}, bf16[1024,256]{1,0:T(8,128)(2,1)S(1)}, u32[]{:S(2)}, u32[]{:S(2)}) collective-permute-start(bf16[1024,256]{1,0:T(8,128)(2,1)} %get-tuple-element.145), channel_id=1, source_target_pairs={{0,1},{1,0},{2,3},{3,2},{4,5},{5,4},{6,7},{7,6},{8,9},{9,8},{10,11... | collective-permute-start | bytes 1572872 | tf_op jit(solution)/shard_map/ppermute | solution.py:870
  146.3 7.9 %copy-start.40 = (bf16[2,256,1024]{2,1,0:T(8,128)(2,1)S(1)}, bf16[2,256,1024]{2,1,0:T(8,128)(2,1)}, u32[]{:S(2)}) copy-start(bf16[2,256,1024]{2,1,0:T(8,128)(2,1)} %get-tuple-element.162) | copy-start | bytes 3145732
  146.3 8.9 %copy-start.19 = (bf16[1024,256]{1,0:T(8,128)(2,1)S(1)}, bf16[1024,256]{1,0:T(8,128)(2,1)}, u32[]{:S(2)}) copy-start(bf16[1024,256]{1,0:T(8,128)(2,1)} %get-tuple-element.145) | copy-start | bytes 1572868
  149.2 56.2 %all-to-all-start.3 = ((bf16[4,256,512]{2,1,0:T(8,128)(2,1)}), bf16[4,256,512]{2,1,0:T(8,128)(2,1)S(1)}, u32[]{:S(2)}, u32[]{:S(2)}) async-start(bf16[4,256,512]{2,1,0:T(8,128)(2,1)} %pair_sum_early.1), calls=%async_computation.3 | async-start | bytes 2097152 | tf_op jit(solution)/shard_map/all_to_all | solution.py:881
  154.2 42.6 %collective-permute-start.15 = (bf16[2,256,1024]{2,1,0:T(8,128)(2,1)S(1)}, bf16[2,256,1024]{2,1,0:T(8,128)(2,1)S(1)}, u32[]{:S(2)}, u32[]{:S(2)}) collective-permute-start(bf16[2,256,1024]{2,1,0:T(8,128)(2,1)S(1)} %copy-done.40), channel_id=1, source_target_pairs={{0,2},{1,3},{2,0},{3,1},{4,6},{5,7},{6,4},{7,5},{8,10},{9,11},{10,... | collective-permute-start | bytes 3145736 | tf_op jit(solution)/shard_map/ppermute | solution.py:870
  155.3 8.3 %copy-start.9 = (bf16[1024,256]{1,0:T(8,128)(2,1)}, bf16[1024,256]{1,0:T(8,128)(2,1)S(1)}, u32[]{:S(2)}) copy-start(bf16[1024,256]{1,0:T(8,128)(2,1)S(1)} %add_convert_fusion.2.dbc_ref) | copy-start | bytes 1572868
  155.3 9.4 %copy-start.41 = (bf16[4,128,512]{2,1,0:T(8,128)(2,1)S(1)}, bf16[4,128,512]{2,1,0:T(8,128)(2,1)}, u32[]{:S(2)}) copy-start(bf16[4,128,512]{2,1,0:T(8,128)(2,1)} %get-tuple-element.143) | copy-start | bytes 1572868
  163.6 33.2 %collective-permute-start.14 = (bf16[2,256,1024]{2,1,0:T(8,128)(2,1)}, bf16[2,256,1024]{2,1,0:T(8,128)(2,1)S(1)}, u32[]{:S(2)}, u32[]{:S(2)}) collective-permute-start(bf16[2,256,1024]{2,1,0:T(8,128)(2,1)} %get-tuple-element.161), channel_id=1, source_target_pairs={{0,1},{1,0},{2,3},{3,2},{4,5},{5,4},{6,7},{7,6},{8,9},{9,8},{10,11... | collective-permute-start | bytes 3145736 | tf_op jit(solution)/shard_map/ppermute | solution.py:870
  163.6 26.1 %collective-permute-start.13 = (bf16[1024,256]{1,0:T(8,128)(2,1)S(1)}, bf16[1024,256]{1,0:T(8,128)(2,1)S(1)}, u32[]{:S(2)}, u32[]{:S(2)}) collective-permute-start(bf16[1024,256]{1,0:T(8,128)(2,1)S(1)} %add_convert_fusion.2.dbc_ref), channel_id=1, source_target_pairs={{0,2},{1,3},{2,0},{3,1},{4,6},{5,7},{6,4},{7,5},{8,10},{9,11},{10,... | collective-permute-start | bytes 1572872 | tf_op jit(solution)/shard_map/ppermute | solution.py:870
  164.7 33.6 %collective-permute-start.11 = (bf16[4,128,512]{2,1,0:T(8,128)(2,1)S(1)}, bf16[4,128,512]{2,1,0:T(8,128)(2,1)S(1)}, u32[]{:S(2)}, u32[]{:S(2)}) collective-permute-start(bf16[4,128,512]{2,1,0:T(8,128)(2,1)S(1)} %copy-done.41), channel_id=1, source_target_pairs={{0,4},{4,0},{8,12},{12,8},{16,20},{20,16},{24,28},{28,24},{1,5},{5... | collective-permute-start | bytes 1572872 | tf_op jit(solution)/shard_map/ppermute | solution.py:870
  196.8 5.6 %copy-start.10 = (bf16[2,256,1024]{2,1,0:T(8,128)(2,1)}, bf16[2,256,1024]{2,1,0:T(8,128)(2,1)S(1)}, u32[]{:S(2)}) copy-start(bf16[2,256,1024]{2,1,0:T(8,128)(2,1)S(1)} %collective-permute-done.15) | copy-start | bytes 3145732
  196.8 5.6 %copy-start.7 = (bf16[2,256,1024]{2,1,0:T(8,128)(2,1)}, bf16[2,256,1024]{2,1,0:T(8,128)(2,1)S(1)}, u32[]{:S(2)}) copy-start(bf16[2,256,1024]{2,1,0:T(8,128)(2,1)S(1)} %collective-permute-done.14.came_ref) | copy-start | bytes 3145732
  196.8 5.6 %collective-permute-start.16 = (bf16[160,512]{1,0:T(8,128)(2,1)}, bf16[160,512]{1,0:T(8,128)(2,1)S(1)}, u32[]{:S(2)}, u32[]{:S(2)}) collective-permute-start(bf16[160,512]{1,0:T(8,128)(2,1)} %get-tuple-element.163), channel_id=1, source_target_pairs={{0,4},{4,0},{8,12},{12,8},{16,20},{20,16},{24,28},{28,24},{1,5},{5... | collective-permute-start | bytes 491528 | tf_op jit(solution)/shard_map/ppermute | solution.py:870
  198.3 4.1 %copy-start.21 = (bf16[4,128,512]{2,1,0:T(8,128)(2,1)}, bf16[4,128,512]{2,1,0:T(8,128)(2,1)S(1)}, u32[]{:S(2)}) copy-start(bf16[4,128,512]{2,1,0:T(8,128)(2,1)S(1)} %collective-permute-done.11.came_ref) | copy-start | bytes 1572868
  205.4 31.4 %all-to-all-start.2 = ((bf16[4,192,512]{2,1,0:T(8,128)(2,1)}), bf16[4,192,512]{2,1,0:T(8,128)(2,1)S(1)}, u32[]{:S(2)}, u32[]{:S(2)}) async-start(bf16[4,192,512]{2,1,0:T(8,128)(2,1)} %pair_sum_late.1), calls=%async_computation.2 | async-start | bytes 1572864 | tf_op jit(solution)/shard_map/all_to_all | solution.py:881
  210.2 11.7 %copy-start.1 = (f32[1,256,1024]{2,1,0:T(8,128)S(1)}, f32[1,256,1024]{2,1,0:T(8,128)}, u32[]{:S(2)}) copy-start(f32[1,256,1024]{2,1,0:T(8,128)} %param.23) | copy-start | bytes 3145732
  212.5 9.4 %collective-permute-start.18 = (bf16[256,1024]{1,0:T(8,128)(2,1)}, bf16[256,1024]{1,0:T(8,128)(2,1)}, u32[]{:S(2)}, u32[]{:S(2)}) collective-permute-start(bf16[256,1024]{1,0:T(8,128)(2,1)} %fusion.2), channel_id=1, source_target_pairs={{0,1},{1,0},{2,3},{3,2},{4,5},{5,4},{6,7},{7,6},{8,9},{9,8},{10,11... | collective-permute-start | bytes 1572872 | tf_op jit(solution)/shard_map/ppermute | solution.py:870
  212.7 11.9 %copy-start.6 = (bf16[256,512]{1,0:T(8,128)(2,1)}, bf16[256,512]{1,0:T(8,128)(2,1)S(1)}, u32[]{:S(2)}) copy-start(bf16[256,512]{1,0:T(8,128)(2,1)S(1)} %reduce_sum.30.part_refs_0_.early_refs_0_) | copy-start | bytes 786436
  212.7 9.2 %collective-permute-start.24 = (bf16[256,512]{1,0:T(8,128)(2,1)S(1)}, bf16[256,512]{1,0:T(8,128)(2,1)S(1)}, u32[]{:S(2)}, u32[]{:S(2)}) collective-permute-start(bf16[256,512]{1,0:T(8,128)(2,1)S(1)} %reduce_sum.30.part_refs_0_.early_refs_0_), channel_id=1, source_target_pairs={{0,2},{1,3},{2,0},{3,1},{4,6},{5,7},{6,4},{7,5},{8,10},{9,11},{10,... | collective-permute-start | bytes 786440 | tf_op jit(solution)/shard_map/ppermute | solution.py:870
  215.8 17.1 %collective-permute-start.17 = (bf16[256,1024]{1,0:T(8,128)(2,1)}, bf16[256,1024]{1,0:T(8,128)(2,1)}, u32[]{:S(2)}, u32[]{:S(2)}) collective-permute-start(bf16[256,1024]{1,0:T(8,128)(2,1)} %fusion.1), channel_id=1, source_target_pairs={{0,2},{1,3},{2,0},{3,1},{4,6},{5,7},{6,4},{7,5},{8,10},{9,11},{10,... | collective-permute-start | bytes 1572872 | tf_op jit(solution)/shard_map/ppermute | solution.py:870
  217.1 24.4 %collective-permute-start.23 = (bf16[256,512]{1,0:T(8,128)(2,1)S(1)}, bf16[256,512]{1,0:T(8,128)(2,1)S(1)}, u32[]{:S(2)}, u32[]{:S(2)}) collective-permute-start(bf16[256,512]{1,0:T(8,128)(2,1)S(1)} %reduce_sum.30.part_refs_0_.early_refs_0_), channel_id=1, source_target_pairs={{0,1},{1,0},{2,3},{3,2},{4,5},{5,4},{6,7},{7,6},{8,9},{9,8},{10,11... | collective-permute-start | bytes 786440 | tf_op jit(solution)/shard_map/ppermute | solution.py:870
  221.9 14.9 %copy-start.14 = (bf16[256,512]{1,0:T(8,128)(2,1)}, bf16[256,512]{1,0:T(8,128)(2,1)S(1)}, u32[]{:S(2)}) copy-start(bf16[256,512]{1,0:T(8,128)(2,1)S(1)} %collective-permute-done.24.part_refs_2_.early_refs_2_) | copy-start | bytes 786436
  221.9 19.6 %collective-permute-start.25 = (bf16[256,512]{1,0:T(8,128)(2,1)S(1)}, bf16[256,512]{1,0:T(8,128)(2,1)S(1)}, u32[]{:S(2)}, u32[]{:S(2)}) collective-permute-start(bf16[256,512]{1,0:T(8,128)(2,1)S(1)} %collective-permute-done.24.part_refs_2_.early_refs_2_), channel_id=1, source_target_pairs={{0,1},{1,0},{2,3},{3,2},{4,5},{5,4},{6,7},{7,6},{8,9},{9,8},{10,11... | collective-permute-start | bytes 786440 | tf_op jit(solution)/shard_map/ppermute | solution.py:870
  239.6 11.4 %collective-permute-start.19 = (bf16[192,512]{1,0:T(8,128)(2,1)}, bf16[192,512]{1,0:T(8,128)(2,1)S(1)}, u32[]{:S(2)}, u32[]{:S(2)}) collective-permute-start(bf16[192,512]{1,0:T(8,128)(2,1)} %sum_late.1.part_refs_0_), channel_id=1, source_target_pairs={{0,1},{1,0},{2,3},{3,2},{4,5},{5,4},{6,7},{7,6},{8,9},{9,8},{10,11... | collective-permute-start | bytes 589832 | tf_op jit(solution)/shard_map/ppermute | solution.py:870
  239.6 11.4 %collective-permute-start.20 = (bf16[192,512]{1,0:T(8,128)(2,1)}, bf16[192,512]{1,0:T(8,128)(2,1)S(1)}, u32[]{:S(2)}, u32[]{:S(2)}) collective-permute-start(bf16[192,512]{1,0:T(8,128)(2,1)} %sum_late.1.part_refs_0_), channel_id=1, source_target_pairs={{0,2},{1,3},{2,0},{3,1},{4,6},{5,7},{6,4},{7,5},{8,10},{9,11},{10,... | collective-permute-start | bytes 589832 | tf_op jit(solution)/shard_map/ppermute | solution.py:870
  240.3 10.7 %collective-permute-start.21 = (bf16[192,512]{1,0:T(8,128)(2,1)}, bf16[192,512]{1,0:T(8,128)(2,1)S(1)}, u32[]{:S(2)}, u32[]{:S(2)}) collective-permute-start(bf16[192,512]{1,0:T(8,128)(2,1)} %sum_late.1.part_refs_0_), channel_id=1, source_target_pairs={{0,3},{1,2},{2,1},{3,0},{4,7},{5,6},{6,5},{7,4},{8,11},{9,10},{10,... | collective-permute-start | bytes 589832 | tf_op jit(solution)/shard_map/ppermute | solution.py:870
  251.0 2.8 %copy-start.22 = (bf16[192,512]{1,0:T(8,128)(2,1)}, bf16[192,512]{1,0:T(8,128)(2,1)S(1)}, u32[]{:S(2)}) copy-start(bf16[192,512]{1,0:T(8,128)(2,1)S(1)} %collective-permute-done.19.part_refs_1_) | copy-start | bytes 589828
  251.0 2.8 %copy-start.23 = (bf16[192,512]{1,0:T(8,128)(2,1)}, bf16[192,512]{1,0:T(8,128)(2,1)S(1)}, u32[]{:S(2)}) copy-start(bf16[192,512]{1,0:T(8,128)(2,1)S(1)} %collective-permute-done.20.part_refs_2_) | copy-start | bytes 589828
  251.0 2.8 %copy-start.24 = (bf16[192,512]{1,0:T(8,128)(2,1)}, bf16[192,512]{1,0:T(8,128)(2,1)S(1)}, u32[]{:S(2)}) copy-start(bf16[192,512]{1,0:T(8,128)(2,1)S(1)} %collective-permute-done.21.part_refs_3_) | copy-start | bytes 589828
  253.8 9.1 %copy-start.26 = (f32[32,128]{1,0:T(8,128)S(1)}, f32[32,128]{1,0:T(8,128)}, u32[]{:S(2)}) copy-start(f32[32,128]{1,0:T(8,128)} %dt_ref.1) | copy-start | bytes 49156
  253.8 9.1 %copy-start.30 = (f32[32,128]{1,0:T(8,128)S(1)}, f32[32,128]{1,0:T(8,128)}, u32[]{:S(2)}) copy-start(f32[32,128]{1,0:T(8,128)} %param.34) | copy-start | bytes 49156
  253.9 9.1 %copy-start.31 = (f32[32,128]{1,0:T(8,128)S(1)}, f32[32,128]{1,0:T(8,128)}, u32[]{:S(2)}) copy-start(f32[32,128]{1,0:T(8,128)} %param.35) | copy-start | bytes 49156
  253.9 9.7 %copy-start.27 = (f32[5,288]{1,0:T(8,128)S(1)}, f32[5,288]{1,0:T(8,128)}, u32[]{:S(2)}) copy-start(f32[5,288]{1,0:T(8,128)} %conv_ref.1) | copy-start | bytes 17284
  253.9 9.7 %copy-start.32 = (f32[5,288]{1,0:T(8,128)S(1)}, f32[5,288]{1,0:T(8,128)}, u32[]{:S(2)}) copy-start(f32[5,288]{1,0:T(8,128)} %param.38) | copy-start | bytes 17284
  253.9 9.7 %copy-start.33 = (f32[5,288]{1,0:T(8,128)S(1)}, f32[5,288]{1,0:T(8,128)}, u32[]{:S(2)}) copy-start(f32[5,288]{1,0:T(8,128)} %param.39) | copy-start | bytes 17284
  253.9 10.4 %copy-start.34 = (f32[384]{0:T(512)S(1)}, f32[384]{0:T(512)}, u32[]{:S(2)}) copy-start(f32[384]{0:T(512)} %gain_ref.1) | copy-start | bytes 4612
  253.9 10.4 %copy-start.36 = (f32[384]{0:T(512)S(1)}, f32[384]{0:T(512)}, u32[]{:S(2)}) copy-start(f32[384]{0:T(512)} %param.40) | copy-start | bytes 4612
  253.9 10.4 %copy-start.37 = (f32[384]{0:T(512)S(1)}, f32[384]{0:T(512)}, u32[]{:S(2)}) copy-start(f32[384]{0:T(512)} %param.41) | copy-start | bytes 4612
  253.9 11.1 %copy-start.38 = (f32[3,32]{1,0:T(4,128)S(1)}, f32[3,32]{1,0:T(4,128)}, u32[]{:S(2)}) copy-start(f32[3,32]{1,0:T(4,128)} %param.42) | copy-start | bytes 1156
  253.9 11.1 %copy-start.39 = (f32[3,32]{1,0:T(4,128)S(1)}, f32[3,32]{1,0:T(4,128)}, u32[]{:S(2)}) copy-start(f32[3,32]{1,0:T(4,128)} %param.43) | copy-start | bytes 1156
  (10 other events, 9.9 us)

commit v7 on v5

--- a/solution.py
+++ b/solution.py
@@ -169,13 +169,17 @@
     tmp_ref[8 + CONV + 1 : 8 + CONV + 2, 0 : gain_ref.shape[0]] = gain_ref[...].reshape(1, -1)
     for copy in copies:
         w1_ref[copy, rows : rows + 16, :] = tmp_ref[...].astype(BF16)
+    copies = range(g2_ref.shape[0])
     for at, part in enumerate(pick_heads(win_ref, 0, ctx, heads)):
-        g2_ref[0:rows, at * 128 : (at + 1) * 128] = part.astype(BF16)
-    if g2_ref.shape[0] > rows:
+        part = part.astype(BF16)
+        for copy in copies:
+            g2_ref[copy, 0:rows, at * 128 : (at + 1) * 128] = part
+    if g2_ref.shape[1] > rows:
         some = wout_ref.shape[0] // 4
         mine = wout_ref[pl.ds(pl.multiple_of(ctx * some, 8), some), :].astype(BF16)
-        g2_ref[rows : rows + some] = mine[:, :width]
-        g2_ref[rows + some : rows + 2 * some] = mine[:, width:]
+        for copy in copies:
+            g2_ref[copy, rows : rows + some] = mine[:, :width]
+            g2_ref[copy, rows + some : rows + 2 * some] = mine[:, width:]
 
 
 def scan_forward_kernel(
@@ -395,8 +399,7 @@
     mixed_ref,
     wout_ref,
     cot_ref,
-    bkeep_ref,
-    bsend_ref,
+    block_refs,
     keep_ref,
     send_ref,
     dy_ref,
@@ -428,13 +431,11 @@
     cot = cot_ref[perm_ref[step]]
     block = nn(normed, wout_ref[...]).astype(BF16)
 
-    @pl.when(step < 2)
-    def _():
-        bsend_ref[0] = block
-
-    @pl.when(step >= 2)
-    def _():
-        bkeep_ref[0] = block
+    for at, block_ref in enumerate(block_refs):
+
+        @pl.when(step == at)
+        def _():
+            block_ref[...] = block
 
     outacc_ref[...] += tn(normed, cot)
     grad = ng_ref[...]
@@ -641,8 +642,7 @@
     wdt_ref,
     hid_ref,
     gain_ref,
-    keep_ref,
-    send_ref,
+    out_refs,
     gsum_ref,
 ):
     @pl.when(pl.program_id(0) == 0)
@@ -653,13 +653,11 @@
     total = total + nn(dstep_ref[...], wdt_ref[...])
     step = pl.program_id(0)
 
-    @pl.when(step < 2)
-    def _():
-        send_ref[0] = total.astype(BF16)
-
-    @pl.when(step >= 2)
-    def _():
-        keep_ref[0] = total.astype(BF16)
+    for at, out_ref in enumerate(out_refs):
+
+        @pl.when(step == at)
+        def _():
+            out_ref[...] = total.astype(BF16)
 
     unit = hid_ref[...].astype(F32) / gain_ref[...]
     gsum_ref[...] += jnp.sum(total * unit, axis=0, keepdims=True) + jnp.zeros(gsum_ref.shape, F32)
@@ -741,18 +739,16 @@
         send_ref[32 + 32 * at : 64 + 32 * at, 0:width] = jnp.where(here_ref[0] == 0, high, low)
 
 
-def input_back_kernel(keep_ref, came_ref, far_ref, own_ref, tok_ref, gain_ref, cot_ref, out_ref):
-    grad = keep_ref[0].astype(F32) + came_ref[0].astype(F32) + far_ref[...].astype(F32) + own_ref[...]
+def input_back_kernel(part_refs, own_ref, tok_ref, gain_ref, cot_ref, out_ref):
+    grad = own_ref[...]
+    for ref in part_refs:
+        grad = grad + ref[...].astype(F32)
     tok = tok_ref[...]
     scale = lax.rsqrt(jnp.mean(tok * tok, axis=-1, keepdims=True) + NORM_EPS)
     unit = tok * scale
     scaled = grad * gain_ref[...]
     mean = jnp.mean(scaled * unit, axis=-1, keepdims=True)
     out_ref[...] = cot_ref[...] + scale * (scaled - unit * mean)
-
-
-def pair_sum_kernel(keep_ref, came_ref, out_ref):
-    out_ref[...] = (keep_ref[...].astype(F32) + came_ref[...].astype(F32)).astype(BF16)
 
 
 def with_rest(value, first):
@@ -787,8 +783,7 @@
 
     @pl.when(step == 0)
     def _():
-        for at, ref in enumerate(early_refs):
-            early_ref[pl.ds(here_ref[2] ^ at, 1)] = ref[...][None]
+        by_owner(early_refs, here_ref[2], early_ref)
 
     rows = weight_ref.shape[0]
     width = early_ref.shape[2]
@@ -803,6 +798,11 @@
             ref[:, lanes] = new
 
 
+def by_owner(refs, ctx, natural_ref):
+    for at, ref in enumerate(refs):
+        natural_ref[pl.ds(ctx ^ at, 1)] = ref[...][None]
+
+
 def adam_in_kernel(here_ref, weight_ref, first_ref, second_ref, early_refs, late_refs, *rest):
     new_refs, (early_ref, late_ref) = rest[:3], rest[3:]
     step = pl.program_id(0)
@@ -813,10 +813,8 @@
 
     @pl.when(step == 0)
     def _():
-        for at in range(pieces):
-            owner = pl.ds(here_ref[2] ^ at, 1)
-            early_ref[owner] = early_refs[at][...][None]
-            late_ref[owner] = late_refs[at][...][None]
+        by_owner(early_refs, here_ref[2], early_ref)
+        by_owner(late_refs, here_ref[2], late_ref)
 
     here = pl.ds(pl.multiple_of(step * rows, rows), rows)
     low = lax.broadcasted_iota(jnp.int32, (rows, 2 * HEAD_DIM), 1) < HEAD_DIM
@@ -840,11 +838,10 @@
                 start = start + block
                 odd = jnp.where(low, pltpu.roll(first, HEAD_DIM, 1), second)
                 update(slice(start, start + 2 * HEAD_DIM), odd)
-    first = late_ref.shape[1] - 32
-    update(
-        slice(2 * INNER, 2 * INNER + 2 * STATE),
-        late_ref[step, first : first + 32, 0 : 2 * STATE].astype(F32),
-    )
+    some = 32 // rows
+    first = pl.multiple_of(late_ref.shape[1] - 32 + (step % some) * rows, rows)
+    grad = late_ref[step // some, pl.ds(first, rows), 0 : 2 * STATE].astype(F32)
+    update(slice(2 * INNER, 2 * INNER + 2 * STATE), grad)
 
 
 def swap(value, axis, bit):
@@ -861,6 +858,11 @@
     count = lax.axis_size("dp")
     groups = [list(range(low, count, 2)) for low in range(2)]
     return lax.all_to_all(value, "dp", 0, 0, axis_index_groups=groups)
+
+
+def from_owners(parts):
+    count = len(parts)
+    return [swap(parts[bit - 1], "ctx", bit) for bit in range(1, count)] + [parts[-1]]
 
 
 def fan_ctx(value):
@@ -927,7 +929,7 @@
     block_in = model // heads
     tok = tokens[0]
     bits = jnp.stack([d & 1, d >> 1, c] if near else [0 * d, 0 * d, c]).astype(jnp.int32)
-    perm = c ^ jnp.asarray([1, 3, 0, 2], jnp.int32)
+    perm = c ^ jnp.asarray([1, 2, 3, 0], jnp.int32)
     smem = pl.BlockSpec(memory_space=pltpu.SMEM)
     vmem = pl.BlockSpec(memory_space=pltpu.VMEM)
     anywhere = lambda pieces: [pl.BlockSpec(memory_space=pl.ANY)] * len(pieces)
@@ -937,33 +939,37 @@
         in_specs=[smem] + [vmem] * 5,
         out_shape=[
             shape_of(high if near else 1, rows_in + 16, wide, dtype=BF16),
-            shape_of(rows_in + (2 * HEAD_DIM if near else 0), width, dtype=BF16),
+            shape_of(high if near else 1, rows_in + (2 * HEAD_DIM if near else 0), width, dtype=BF16),
         ],
         scratch_shapes=[pltpu.VMEM((16, wide), F32)],
         compiler_params=params(),
         name="pack",
     )(bits, in_weight, out_weight, dt_weight, conv_params, gains)
-    tok_sent, w1 = lax.optimization_barrier((tok, w1))
-    tok_far = swap(tok_sent, "ctx", 2)
+    cot_low = cotangent[0].astype(BF16)
     if near:
+        tok_far = swap(tok, "ctx", 2)
         w1 = high_all_to_all(w1)
-        w1, tok_far, tok_sent = lax.optimization_barrier((w1, tok_far, tok_sent))
-        w1 = [w1, swap(w1, "dp", 1)]
-        at_rows = jnp.stack([d & 1, 1 - (d & 1)]).astype(jnp.int32)
+        w1, tok_far, tok_sent, g2, cot_low = lax.optimization_barrier((w1, tok_far, tok, g2, cot_low))
+        w1_came = swap(w1, "dp", 1)
+        toks = [tok, swap(tok_sent, "ctx", 1), tok_far, swap(tok_far, "ctx", 1)]
+        g2 = high_all_to_all(g2)
+        cot_far = swap(cot_low, "ctx", 2)
+        w1, w1_came, toks, g2, cot_far, cot_low = lax.optimization_barrier(
+            (w1, w1_came, toks, g2, cot_far, cot_low)
+        )
+        w1 = [w1, w1_came]
+        g2 = [g2, swap(g2, "dp", 1)]
+        cots = [cot_low, swap(cot_low, "ctx", 1), cot_far, swap(cot_far, "ctx", 1)]
+        at_rows = at_g2 = jnp.stack([d & 1, 1 - (d & 1)]).astype(jnp.int32)
     else:
         w1 = [lax.all_gather(w1[0], "dp", axis=0)]
-        at_rows = jnp.zeros((1,), jnp.int32)
-    toks = [tok, swap(tok_sent, "ctx", 1), tok_far, swap(tok_far, "ctx", 1)]
-    if near:
-        g2 = [lax.all_gather(g2, "dp", axis=0)]
-    else:
-        wg = lax.all_gather(g2, "dp", axis=0, tiled=True).reshape(heads, block_in, width)
+        toks = gather_ctx(tok)
+        cots = gather_ctx(cot_low)
+        wg = lax.all_gather(g2[0], "dp", axis=0, tiled=True).reshape(heads, block_in, width)
         wout = lax.all_gather(out_weight.astype(BF16), "dp", axis=0, tiled=True)
         wout = lax.dynamic_index_in_dim(wout.reshape(heads, nctx, HEAD_DIM, model), c, 1, False)
         g2 = [jnp.concatenate([wg, wout[:, :, :width], wout[:, :, width:]], axis=1)]
-    at_g2 = jnp.zeros((1,), jnp.int32)
-    cot_low, w1 = lax.optimization_barrier((cotangent[0].astype(BF16), w1))
-    cots = gather_ctx(cot_low)
+        at_rows = at_g2 = jnp.zeros((1,), jnp.int32)
 
     ids = segment_ids[0]
     seg_col = jnp.pad(ids, (8, 8), constant_values=-1)[:, None]
@@ -974,8 +980,7 @@
     rows = lambda cols: pl.BlockSpec((span, cols), lambda i, *_: (i, 0))
     row_of = pl.BlockSpec((heads, span), lambda i, *_: (0, i))
     rows_at = lambda cols: pl.BlockSpec((span, cols), lambda i, p, *_: (p[i], 0))
-    sent = pl.BlockSpec((1, span, model), lambda i, *_: (jnp.minimum(i, 1), 0, 0))
-    kept = pl.BlockSpec((1, span, model), lambda i, *_: (jnp.maximum(i - 2, 0), 0, 0))
+    whole = full((span, model))
     shards_in = sum(piece.shape[0] for piece in w1)
 
     (
@@ -1079,7 +1084,7 @@
     stats = sum(fan_ctx(stats))
 
     early_rows = block_in + 2 * HEAD_DIM
-    block_keep, block_send, early_keep, early_send, dy, dgate, col_sums = pl.pallas_call(
+    blocks_out, early_keep, early_send, dy, dgate, col_sums = pl.pallas_call(
         norm_back_kernel,
         grid_spec=pltpu.PrefetchScalarGridSpec(
             num_scalar_prefetch=2,
@@ -1096,8 +1101,7 @@
                 full((nctx, span, model)),
             ],
             out_specs=[
-                kept,
-                sent,
+                [whole] * nctx,
                 full((high, early_rows, width)),
                 full((high, early_rows, width)),
                 rows_at(width),
@@ -1107,8 +1111,7 @@
             scratch_shapes=[pltpu.VMEM((width, model), F32), pltpu.VMEM((model, width), F32)],
         ),
         out_shape=[
-            shape_of(2, span, model, dtype=BF16),
-            shape_of(2, span, model, dtype=BF16),
+            [shape_of(span, model, dtype=BF16)] * nctx,
             shape_of(high, early_rows, width, dtype=BF16),
             shape_of(high, early_rows, width, dtype=BF16),
             shape_of(length, width),
@@ -1118,7 +1121,7 @@
         compiler_params=params("arbitrary"),
         name="norm_back",
     )(perm, bits, hid, inner, gate, normed_grad, stats, gain_mine, mixed, wout, cot_all)
-    block_came = swap(block_send, "ctx", 1)
+    blocks_out = from_owners(blocks_out)
     if near:
         early_came = swap(early_send, "dp", 1)
 
@@ -1183,21 +1186,16 @@
     dbc_came = swap(dbc, "ctx", 1)
     if near:
         late_came = swap(late_send, "dp", 1)
-        early_parts = pl.pallas_call(
-            pair_sum_kernel,
-            grid=(high,),
-            in_specs=[pl.BlockSpec((1, early_rows, width), lambda i: (i, 0, 0))] * 2,
-            out_specs=pl.BlockSpec((1, early_rows, width), lambda i: (i, 0, 0)),
-            out_shape=shape_of(high, early_rows, width, dtype=BF16),
-            compiler_params=params("arbitrary"),
-            name="pair_sum_early",
-        )(early_keep, early_came)
-        dval, early_parts = lax.optimization_barrier((dval, early_parts))
+        early_came, blocks_out, dval = lax.optimization_barrier((early_came, blocks_out, dval))
+        early_parts = (early_keep.astype(F32) + early_came.astype(F32)).astype(BF16)
         early_parts = high_all_to_all(early_parts)
     dbc = (dbc.astype(F32) + dbc_came.astype(F32)).astype(BF16)
+    dval, dbc = lax.optimization_barrier((dval, dbc))
     dbc_far = swap(dbc, "ctx", 2)
-
-    hidden_keep, hidden_send, gain_sum = pl.pallas_call(
+    if near:
+        dbc_far, late_came = lax.optimization_barrier((dbc_far, late_came))
+
+    hidden_out, gain_sum = pl.pallas_call(
         hidden_back_kernel,
         grid_spec=pltpu.PrefetchScalarGridSpec(
             num_scalar_prefetch=1,
@@ -1212,17 +1210,16 @@
                 rows_at(model),
                 full((1, model)),
             ],
-            out_specs=[kept, sent, full((8, model))],
+            out_specs=[[whole] * nctx, full((8, model))],
         ),
         out_shape=[
-            shape_of(2, span, model, dtype=BF16),
-            shape_of(2, span, model, dtype=BF16),
+            [shape_of(span, model, dtype=BF16)] * nctx,
             shape_of(8, model),
         ],
         compiler_params=params("arbitrary"),
         name="hidden_back",
     )(perm, dgate, dval, dstep, wg, w1, dt_mine, hid, gain_pre)
-    hidden_came = swap(hidden_send, "ctx", 1)
+    hidden_out = from_owners(hidden_out)
     map_rows = 32 + 32 * high
     map_cols = lambda size: pl.BlockSpec((size, maps), lambda i: (0, width // maps))
     map_keep, map_send, hidden_own = pl.pallas_call(
@@ -1277,24 +1274,14 @@
         gain_sum,
     )
 
-    map_send, hidden_came, block_came = lax.optimization_barrier((map_send, hidden_came, block_came))
-    hidden_far = (hidden_keep[1].astype(F32) + hidden_came[1].astype(F32)).astype(BF16)
-    hidden_far = swap(hidden_far, "ctx", 2)
-    block_far = (block_keep[1].astype(F32) + block_came[1].astype(F32)).astype(BF16)
-    mine = pl.BlockSpec((1, span, model), lambda i: (0, 0, 0))
     input_grad = pl.pallas_call(
         input_back_kernel,
-        grid=(1,),
-        in_specs=[mine, mine] + [full((span, model))] * 3 + [full((1, model)), full((span, model))],
-        out_specs=full((span, model)),
+        in_specs=[[vmem] * nctx] + [vmem] * 4,
         out_shape=shape_of(span, model),
-        compiler_params=params("arbitrary"),
+        compiler_params=params(),
         name="input_back",
-    )(hidden_keep, hidden_came, hidden_far, hidden_own, tok, gain_pre, cotangent[0])
-    block_far = swap(block_far, "ctx", 2)
-    block_output = tok + (
-        block_keep[0].astype(F32) + block_came[0].astype(F32) + block_far.astype(F32)
-    )
+    )(hidden_out, hidden_own, tok, gain_pre, cotangent[0])
+    block_output = tok + sum(part.astype(F32) for part in blocks_out)
 
     late_rows = block_in + 64
     if near:
@@ -1306,19 +1293,9 @@
             name="pair_sum_late",
         )(late_keep, late_came, map_keep, map_came)
         late_parts = high_all_to_all(late_parts)
-        late_parts, input_grad, block_output = lax.optimization_barrier(
-            (late_parts, input_grad, block_output)
-        )
         early = jnp.sum(early_parts.astype(F32), axis=0).astype(BF16)
-        late = pl.pallas_call(
-            sum_late_kernel,
-            out_shape=shape_of(late_rows, width, dtype=BF16),
-            compiler_params=params(),
-            name="sum_late",
-        )(late_parts)
-        early, late = fan_ctx(early), fan_ctx(late)
+        early = gather_ctx(early)
         row_block = lambda ref_rows, cols: pl.BlockSpec((ref_rows, cols), lambda i, *_: (i, 0))
-        in_block = row_block(rows_in // nctx, in_weight.shape[1])
         out_block = row_block(out_weight.shape[0] // nctx, model)
         early_spec = [full((early_rows, width))] * nctx
         early_scratch = pltpu.VMEM((nctx, early_rows, width), BF16)
@@ -1335,11 +1312,21 @@
             compiler_params=params("arbitrary"),
             name="adam_out",
         )(bits, out_weight, out_first, out_second, early)
+
+        late_parts, block_output, out_new = lax.optimization_barrier((late_parts, block_output, out_new))
+        late = pl.pallas_call(
+            sum_late_kernel,
+            out_shape=shape_of(late_rows, width, dtype=BF16),
+            compiler_params=params(),
+            name="sum_late",
+        )(late_parts)
+        late = fan_ctx(late)
+        in_block = row_block(16, in_weight.shape[1])
         in_new = pl.pallas_call(
             adam_in_kernel,
             grid_spec=pltpu.PrefetchScalarGridSpec(
                 num_scalar_prefetch=1,
-                grid=(nctx,),
+                grid=(rows_in // 16,),
                 in_specs=[in_block] * 3 + [early_spec, [full((late_rows, width))] * nctx],
                 out_specs=[in_block] * 3,
                 scratch_shapes=[early_scratch, pltpu.VMEM((nctx, late_rows, width), BF16)],

time: 300 us -> 262 us (0.87)
  waiting for transfers between devices: 119 us -> 88 us
  between operations: 14.6 us -> 1.34 us
  starting transfers between devices: 35.4 us -> 41.7 us
    ppermute x25 -> x28, waiting for transfers between devices: 113 us -> 87.7 us  [swap(): return lax.ppermute(value, axis, [(at, at ^ bit) for at in range(count)])]
    all_to_all x3 -> x4, starting transfers between devices: 14.9 us -> 21.2 us  [high_all_to_all(): return lax.all_to_all(value, 'dp', 0, 0, axis_index_groups=groups)]
    all_to_all x3 -> x4, waiting for transfers between devices: 5.92 us -> 0.29 us  [high_all_to_all(): return lax.all_to_all(value, 'dp', 0, 0, axis_index_groups=groups)]
    pallas_call x2 -> x1, Pallas kernels: 7.74 us -> 4.14 us  [shards(): pl.pallas_call(input_back_kernel, in_specs=[[vmem] * nctx] + [vmem] * 4,...]
    unnamed x89 -> x95, local copies, waits for them, and re-layouts: 5.99 us -> 8.32 us
    ppermute x25 -> x28, starting transfers between devices: 20.5 us -> 20.5 us  [swap(): return lax.ppermute(value, axis, [(at, at ^ bit) for at in range(count)])]
  transfers between devices with their start and end apart: 29 -> 32, of which waited for: 15 -> 17; matrix products, arithmetic and copies ran while one was open for 3% -> 3% of each run, Pallas kernels for 22% -> 26%
where the time goes in v7:
time: 262 us; the launch traced here: 261 us
  Pallas kernels  107 us (41%)
  waiting for transfers between devices  88 us (34%)
  starting transfers between devices  41.7 us (16%)
  local copies, waits for them, and re-layouts  12.8 us (5%)
  other arithmetic  10.6 us (4%)
    ppermute x28, waiting for transfers between devices, swap(): return lax.ppermute(value, axis, [(at, at ^ bit) for at in range(count)])  87.7 us
    pallas_call x1, Pallas kernels, shards(): pl.pallas_call(scan_back_kernel, grid_spec=pltpu.PrefetchScalarGridSpec(n...  22 us
    all_to_all x4, starting transfers between devices, high_all_to_all(): return lax.all_to_all(value, 'dp', 0, 0, axis_index_groups=groups)  21.2 us
    ppermute x28, starting transfers between devices, swap(): return lax.ppermute(value, axis, [(at, at ^ bit) for at in range(count)])  20.5 us
    pallas_call x1, Pallas kernels, shards(): pl.pallas_call(scan_forward_kernel, grid_spec=pltpu.PrefetchScalarGridSpe...  18.3 us
    pallas_call x1, Pallas kernels, shards(): pl.pallas_call(norm_back_kernel, grid_spec=pltpu.PrefetchScalarGridSpec(n...  13.3 us
    pallas_call x1, Pallas kernels, shards(): pl.pallas_call(gate_kernel, grid_spec=pltpu.PrefetchScalarGridSpec(num_sc...  10.6 us
    pallas_call x1, Pallas kernels, shards(): pl.pallas_call(adam_in_kernel, grid_spec=pltpu.PrefetchScalarGridSpec(num...  10.2 us
  transfers between devices with their start and end apart: 32, of which 17 were waited for; matrix products, arithmetic and copies ran while one was open for 3% of the time, Pallas kernels for 26%

profile of v7, /device:TPU:0, one launch (start us, length us, event | category | flops | bytes accessed | tf_op | source)
XLA Modules:
  0.0 261.0 jit_solution(7758254532378223901)
XLA Ops:
  0.7 0.6 pad_add_fusion.here_ref
  1.3 3.6 %pack.1 = (bf16[4,144,768]{2,1,0:T(8,128)(2,1)}, bf16[4,256,512]{2,1,0:T(8,128)(2,1)}) custom-call(s32[3]{0:T(128)} %pad_add_fusion.here_ref, f32[128,4352]{1,0:T(8,128)} %weight_ref.3, f32[256,1024]{1,0:T(8,128)} %weight_ref.2, f32[32,128]{1,0:T(8,128)} %dt_ref.1, f32[5,288]{1,0:T(8,128)} %conv_ref.1, f32[384]{0:T(512)} %gain_ref.1), custom_call_target="tpu_custom_call" | custom-call | tf_op jit(solution)/shard_map/pack/pallas_call | solution.py:937
  4.9 6.3 %all-to-all-start = ((bf16[4,144,768]{2,1,0:T(8,128)(2,1)}), bf16[4,144,768]{2,1,0:T(8,128)(2,1)S(1)}, u32[]{:S(2)}, u32[]{:S(2)}) async-start(bf16[4,144,768]{2,1,0:T(8,128)(2,1)} %get-tuple-element.104), calls=%async_computation | async-start | bytes 1769472 | tf_op jit(solution)/shard_map/all_to_all | solution.py:860
  11.2 1.6 collective-permute-start
  12.9 23.1 %collective-permute-done.tok_pieces_2_ = f32[256,1024]{1,0:T(8,128)} collective-permute-done((f32[256,1024]{1,0:T(8,128)S(1)}, f32[256,1024]{1,0:T(8,128)}, u32[]{:S(2)}, u32[]{:S(2)}) %collective-permute-start) | collective-permute-done | bytes 1048608 | tf_op jit(solution)/shard_map/ppermute | solution.py:849
  36.0 4.8 %all-to-all-start.1 = ((bf16[4,256,512]{2,1,0:T(8,128)(2,1)}), bf16[4,256,512]{2,1,0:T(8,128)(2,1)S(1)}, u32[]{:S(2)}, u32[]{:S(2)}) async-start(bf16[4,256,512]{2,1,0:T(8,128)(2,1)} %get-tuple-element.109), calls=%async_computation.1 | async-start | bytes 2097152 | tf_op jit(solution)/shard_map/all_to_all | solution.py:860
  41.3 1.5 collective-permute-start.1
  42.8 1.5 collective-permute-start.4
  44.3 12.0 %collective-permute-done.4.cot_pieces_2_ = bf16[256,1024]{1,0:T(8,128)(2,1)S(1)} collective-permute-done((bf16[256,1024]{1,0:T(8,128)(2,1)S(1)}, bf16[256,1024]{1,0:T(8,128)(2,1)S(1)}, u32[]{:S(2)}, u32[]{:S(2)}) %collective-permute-start.4) | collective-permute-done | bytes 524320 | tf_op jit(solution)/shard_map/ppermute | solution.py:849
  56.3 6.5 %collective-permute-done.1.w1_pieces_1_ = bf16[4,144,768]{2,1,0:T(8,128)(2,1)S(1)} collective-permute-done((bf16[4,144,768]{2,1,0:T(8,128)(2,1)S(1)}, bf16[4,144,768]{2,1,0:T(8,128)(2,1)S(1)}, u32[]{:S(2)}, u32[]{:S(2)}) %collective-permute-start.1) | collective-permute-done | bytes 884768 | tf_op jit(solution)/shard_map/ppermute | solution.py:849
  62.9 0.9 copy-done.15
  63.8 1.0 copy-done.9
  65.0 1.5 collective-permute-start.5
  67.3 0.7 copy.66
  68.0 1.0 broadcast_in_dim.13.segc_ref
  69.7 18.3 %scan_forward.1 = (bf16[1024,1024]{1,0:T(8,128)(2,1)}, f32[8,768]{1,0:T(8,128)}, f32[1,1024]{1,0:T(1,128)}, f32[1,512]{1,0:T(1,128)}, bf16[8,1024]{1,0:T(8,128)(...) custom-call(s32[3]{0:T(128)} %pad_add_fusion.here_ref, ...), custom_call_target="tpu_custom_call" | custom-call | tf_op jit(solution)/shard_map/scan_forward/pallas_call | solution.py:989
  88.0 1.2 collective-permute-done.5.g2_pieces_1_
  89.1 1.0 copy-done.10
  90.1 10.6 %gate.1 = (bf16[1024,512]{1,0:T(8,128)(2,1)}, bf16[512,1024]{1,0:T(8,128)(2,1)}, bf16[4,256,1024]{2,1,0:T(8,128)(2,1)}, bf16[1024,512]{1,0:T(8,128)(2,1)}, f32[1024,512]{1,0:T(8,128)}, /*index=5*/f32[8,1024]{1,0:T(8,128)}) custom-call(s32[3]{0:T(128)} %pad_add_fusion.here_ref, s32[2]{0:T(128)} %pad_add_fusion.1.at_ref, ...), custom_call_target="tpu_custom_call" | custom-call | tf_op jit(solution)/shard_map/gate/pallas_call | solution.py:1054
  100.8 1.6 collective-permute-start.8
  103.4 1.2 collective-permute-done.10
  104.6 2.0 collective-permute-done.9
  106.5 1.4 add_add_fusion.1.stat_ref
  107.9 13.3 %norm_back.1 = (bf16[256,1024]{1,0:T(8,128)(2,1)}, bf16[256,1024]{1,0:T(8,128)(2,1)}, bf16[256,1024]{1,0:T(8,128)(2,1)}, bf16[256,1024]{1,0:T(8,128)(2,1)}, bf16...) custom-call(s32[4]{0:T(128)} %broadcast_xor_fusion.perm_ref, ...), custom_call_target="tpu_custom_call" | custom-call | tf_op jit(solution)/shard_map/norm_back/pallas_call | solution.py:1087
  121.2 1.6 collective-permute-start.11
  123.3 1.4 collective-permute-start.14
  124.7 22.0 %scan_back.1 = (bf16[4,128,512]{2,1,0:T(8,128)(2,1)}, bf16[4,128,512]{2,1,0:T(8,128)(2,1)}, bf16[1024,512]{1,0:T(8,128)(2,1)}, bf16[1024,256]{1,0:T(8,128)(2,1)}...) custom-call(s32[4]{0:T(128)} %broadcast_xor_fusion.perm_ref, ...), custom_call_target="tpu_custom_call" | custom-call | tf_op jit(solution)/shard_map/scan_back/pallas_call | solution.py:1130
  146.7 1.5 collective-permute-done.14
  148.2 0.8 copy-done.22
  149.0 1.3 add_convert_fusion
  150.2 5.0 %all-to-all-start.3 = ((bf16[4,256,512]{2,1,0:T(8,128)(2,1)}), bf16[4,256,512]{2,1,0:T(8,128)(2,1)S(1)}, u32[]{:S(2)}, u32[]{:S(2)}) async-start(bf16[4,256,512]{2,1,0:T(8,128)(2,1)} %add_convert_fusion), calls=%async_computation.3 | async-start | bytes 2097152 | tf_op jit(solution)/shard_map/all_to_all | solution.py:860
  155.2 0.6 collective-permute-start.17
  155.8 1.3 collective-permute-done.15
  157.8 8.4 %hidden_back.1 = (bf16[256,1024]{1,0:T(8,128)(2,1)}, bf16[256,1024]{1,0:T(8,128)(2,1)}, bf16[256,1024]{1,0:T(8,128)(2,1)}, bf16[256,1024]{1,0:T(8,128)(2,1)}, f32[8,1024]{1,0:T(8,128)}) custom-call(s32[4]{0:T(128)} %broadcast_xor_fusion.perm_ref, bf16[1024,512]{1,0:T(8,128)(2,1)} %get-tuple-element.158.dgate_ref, ...), custom_call_target="tpu_custom_call" | custom-call | tf_op jit(solution)/shard_map/hidden_back/pallas_call | solution.py:1198
  166.2 3.4 %collective-permute-done.17.came_ref = bf16[4,128,512]{2,1,0:T(8,128)(2,1)S(1)} collective-permute-done((bf16[4,128,512]{2,1,0:T(8,128)(2,1)S(1)}, bf16[4,128,512]{2,1,0:T(8,128)(2,1)S(1)}, u32[]{:S(2)}, u32[]{:S(2)}) %collective-permute-start.17) | collective-permute-done | bytes 524320 | tf_op jit(solution)/shard_map/ppermute | solution.py:849
  169.6 1.7 collective-permute-done.16.dbcfar_ref
  171.3 0.8 copy-done.18
  172.1 6.2 %maps_back.1 = (bf16[160,512]{1,0:T(8,128)(2,1)}, bf16[160,512]{1,0:T(8,128)(2,1)}, f32[256,1024]{1,0:T(8,128)}) custom-call(s32[3]{0:T(128)} %pad_add_fusion.here_ref, bf16[1024,256]{1,0:T(8,128)(2,1)} %copy-done.8, bf16[1024,256]{1,0:T(8,128)(2,1)} %copy-done.18, f32[1024,768]{1,0:T(8,128)} %get-tuple-element.131.convsum_ref, ...), custom_call_target="tpu_custom_call" | custom-call | tf_op jit(solution)/shard_map/maps_back/pallas_call | solution.py:1225
  178.9 5.1 %collective-permute-done.18.mcame_ref = bf16[160,512]{1,0:T(8,128)(2,1)S(1)} collective-permute-done((bf16[160,512]{1,0:T(8,128)(2,1)}, bf16[160,512]{1,0:T(8,128)(2,1)S(1)}, u32[]{:S(2)}, u32[]{:S(2)}) %collective-permute-start.18) | collective-permute-done | bytes 163872 | tf_op jit(solution)/shard_map/ppermute | solution.py:849
  184.0 0.7 copy-done.29
  184.6 2.4 pair_sum_late.1
  187.0 5.1 %all-to-all-start.2 = ((bf16[4,192,512]{2,1,0:T(8,128)(2,1)}), bf16[4,192,512]{2,1,0:T(8,128)(2,1)S(1)}, u32[]{:S(2)}, u32[]{:S(2)}) async-start(bf16[4,192,512]{2,1,0:T(8,128)(2,1)} %pair_sum_late.1), calls=%async_computation.2 | async-start | bytes 1572864 | tf_op jit(solution)/shard_map/all_to_all | solution.py:860
  192.9 1.5 collective-permute-start.23
  195.2 6.2 %collective-permute-done.20.early_refs_2_ = bf16[256,512]{1,0:T(8,128)(2,1)S(1)} collective-permute-done((bf16[256,512]{1,0:T(8,128)(2,1)S(1)}, bf16[256,512]{1,0:T(8,128)(2,1)S(1)}, u32[]{:S(2)}, u32[]{:S(2)}) %collective-permute-start.20) | collective-permute-done | bytes 262176 | tf_op jit(solution)/shard_map/ppermute | solution.py:849
  201.4 3.0 %add_add_fusion = f32[256,1024]{1,0:T(8,128)} fusion(bf16[256,1024]{1,0:T(8,128)(2,1)} %get-tuple-element.169, bf16[256,1024]{1,0:T(8,128)(2,1)} %copy-done.22, bf16[256,1024]{1,0:T(8,128)(2,1)} %copy-done.21, bf16[256,1024]{1,0:T(8,128)(2,1)} %copy-done.20, f32[1,256,1024]{2,1,0:T(8,128)S(1)} %copy-done.1), kind=kLoop, calls=%fused_computation.2 | loop fusion | flops 2097152 | bytes 4194304 | tf_op jit(solution)/shard_map/add | solution.py:1284
  204.4 8.2 %collective-permute-done.23.part_refs_1_ = bf16[256,1024]{1,0:T(8,128)(2,1)S(1)} collective-permute-done((bf16[256,1024]{1,0:T(8,128)(2,1)}, bf16[256,1024]{1,0:T(8,128)(2,1)S(1)}, u32[]{:S(2)}, u32[]{:S(2)}) %collective-permute-start.23) | collective-permute-done | bytes 524320 | tf_op jit(solution)/shard_map/ppermute | solution.py:849
  212.6 6.8 %collective-permute-done.24.part_refs_2_ = bf16[256,1024]{1,0:T(8,128)(2,1)S(1)} collective-permute-done((bf16[256,1024]{1,0:T(8,128)(2,1)}, bf16[256,1024]{1,0:T(8,128)(2,1)S(1)}, u32[]{:S(2)}, u32[]{:S(2)}) %collective-permute-start.24) | collective-permute-done | bytes 524320 | tf_op jit(solution)/shard_map/ppermute | solution.py:849
  219.4 0.8 copy-done.25
  220.2 4.1 %input_back.1 = f32[256,1024]{1,0:T(8,128)} custom-call(bf16[256,1024]{1,0:T(8,128)(2,1)} %copy-done.23, bf16[256,1024]{1,0:T(8,128)(2,1)} %copy-done.24, bf16[256,1024]{1,0:T(8,128)(2,1)} %copy-done.25, bf16[256,1024]{1,0:T(8,128)(2,1)} %get-tuple-element.179.part_refs_3_, f32[256,1024]{1,0:T(8,128)} %get-tuple-element.180.own_ref, f32[256,1024]{1,0:T(8,128)} %bitcast.45, ...), custom_call_target="tpu_custom_call" | custom-call | tf_op jit(solution)/shard_map/input_back/pallas_call | solution.py:1277
  224.4 0.7 copy-done.13
  225.1 0.7 copy-done.14
  225.8 5.5 %adam_out.1 = (f32[256,1024]{1,0:T(8,128)}, f32[256,1024]{1,0:T(8,128)}, f32[256,1024]{1,0:T(8,128)}) custom-call(s32[3]{0:T(128)} %pad_add_fusion.here_ref, f32[256,1024]{1,0:T(8,128)} %weight_ref.2, f32[256,1024]{1,0:T(8,128)} %first_ref.2, f32[256,1024]{1,0:T(8,128)} %second_ref.2, bf16[256,512]{1,0:T(8,128)(2,1)} %copy-done.6, ...), custom_call_target="tpu_custom_call" | custom-call | tf_op jit(solution)/shard_map/adam_out/pallas_call | solution.py:1302
  231.3 0.9 copy-done.5
  232.2 2.0 sum_late.1.late_refs_0_
  234.2 1.8 collective-permute-start.27
  236.0 1.5 collective-permute-start.26
  237.6 0.8 slice_bitcast_fusion.4
  238.4 3.2 %collective-permute-done.27.late_refs_3_ = bf16[192,512]{1,0:T(8,128)(2,1)S(1)} collective-permute-done((bf16[192,512]{1,0:T(8,128)(2,1)}, bf16[192,512]{1,0:T(8,128)(2,1)S(1)}, u32[]{:S(2)}, u32[]{:S(2)}) %collective-permute-start.27) | collective-permute-done | bytes 196640 | tf_op jit(solution)/shard_map/ppermute | solution.py:849
  241.6 4.3 %collective-permute-done.26.late_refs_2_ = bf16[192,512]{1,0:T(8,128)(2,1)S(1)} collective-permute-done((bf16[192,512]{1,0:T(8,128)(2,1)}, bf16[192,512]{1,0:T(8,128)(2,1)S(1)}, u32[]{:S(2)}, u32[]{:S(2)}) %collective-permute-start.26) | collective-permute-done | bytes 196640 | tf_op jit(solution)/shard_map/ppermute | solution.py:849
  247.9 0.6 multiply_subtract_fusion
  248.6 0.6 multiply_subtract_fusion.2
  249.2 0.7 multiply_subtract_fusion.3
  249.9 0.7 multiply_subtract_fusion.1
  250.6 10.2 %adam_in.1 = (f32[128,4352]{1,0:T(8,128)}, f32[128,4352]{1,0:T(8,128)}, f32[128,4352]{1,0:T(8,128)}) custom-call(s32[3]{0:T(128)} %pad_add_fusion.here_ref, f32[128,4352]{1,0:T(8,128)} %weight_ref.3, f32[128,4352]{1,0:T(8,128)} %first_ref.3, f32[128,4352]{1,0:T(8,128)} %second_ref.3, bf16[256,512]{1,0:T(8,128)(2,1)} %copy-done.6, ...), custom_call_target="tpu_custom_call" | custom-call | tf_op jit(solution)/shard_map/adam_in/pallas_call | solution.py:1325
  (157 shorter events, 8.6 us)
Async XLA Ops:
  1.3 9.9 %copy-start = (f32[1,256,1024]{2,1,0:T(8,128)S(1)}, f32[1,256,1024]{2,1,0:T(8,128)}, u32[]{:S(2)}) copy-start(f32[1,256,1024]{2,1,0:T(8,128)} %param.22) | copy-start | bytes 3145732
  1.3 11.5 %copy-start.3 = (f32[1,256,1024]{2,1,0:T(8,128)S(1)}, f32[1,256,1024]{2,1,0:T(8,128)}, u32[]{:S(2)}) copy-start(f32[1,256,1024]{2,1,0:T(8,128)} %param.24) | copy-start | bytes 3145732
  4.9 31.1 %all-to-all-start = ((bf16[4,144,768]{2,1,0:T(8,128)(2,1)}), bf16[4,144,768]{2,1,0:T(8,128)(2,1)S(1)}, u32[]{:S(2)}, u32[]{:S(2)}) async-start(bf16[4,144,768]{2,1,0:T(8,128)(2,1)} %get-tuple-element.104), calls=%async_computation | async-start | bytes 1769472 | tf_op jit(solution)/shard_map/all_to_all | solution.py:860
  11.2 55.9 %copy-start.39 = (f32[3,32]{1,0:T(4,128)S(1)}, f32[3,32]{1,0:T(4,128)}, u32[]{:S(2)}) copy-start(f32[3,32]{1,0:T(4,128)} %param.30) | copy-start | bytes 1156
  11.2 56.8 %copy-start.32 = (s32[1,1024]{1,0:T(1,128)S(1)}, s32[1,1024]{1,0:T(1,128)}, u32[]{:S(2)}) copy-start(s32[1,1024]{1,0:T(1,128)} %segr_ref.3) | copy-start | bytes 12292
  11.2 24.8 %collective-permute-start = (f32[256,1024]{1,0:T(8,128)S(1)}, f32[256,1024]{1,0:T(8,128)}, u32[]{:S(2)}, u32[]{:S(2)}) collective-permute-start(f32[256,1024]{1,0:T(8,128)S(1)} %bitcast.46), channel_id=1, source_target_pairs={{0,2},{1,3},{2,0},{3,1},{4,6},{5,7},{6,4},{7,5},{8,10},{9,11},{10,... | collective-permute-start | bytes 3145736 | tf_op jit(solution)/shard_map/ppermute | solution.py:849
  12.9 75.1 %copy-start.7 = (bf16[256,1024]{1,0:T(8,128)(2,1)}, bf16[256,1024]{1,0:T(8,128)(2,1)S(1)}, u32[]{:S(2)}) copy-start(bf16[256,1024]{1,0:T(8,128)(2,1)S(1)} %bitcast_convert_fusion.cot_pieces_0_) | copy-start | bytes 1572868
  36.0 33.7 %copy-start.4 = (bf16[4,144,768]{2,1,0:T(8,128)(2,1)}, bf16[4,144,768]{2,1,0:T(8,128)(2,1)S(1)}, u32[]{:S(2)}) copy-start(bf16[4,144,768]{2,1,0:T(8,128)(2,1)S(1)} %all-to-all-done.w1_pieces_0_) | copy-start | bytes 2654212
  36.0 29.0 %all-to-all-start.1 = ((bf16[4,256,512]{2,1,0:T(8,128)(2,1)}), bf16[4,256,512]{2,1,0:T(8,128)(2,1)S(1)}, u32[]{:S(2)}, u32[]{:S(2)}) async-start(bf16[4,256,512]{2,1,0:T(8,128)(2,1)} %get-tuple-element.109), calls=%async_computation.1 | async-start | bytes 2097152 | tf_op jit(solution)/shard_map/all_to_all | solution.py:860
  40.8 22.1 %collective-permute-start.3 = (f32[256,1024]{1,0:T(8,128)}, f32[256,1024]{1,0:T(8,128)S(1)}, u32[]{:S(2)}, u32[]{:S(2)}) collective-permute-start(f32[256,1024]{1,0:T(8,128)} %collective-permute-done.tok_pieces_2_), channel_id=1, source_target_pairs={{0,1},{1,0},{2,3},{3,2},{4,5},{5,4},{6,7},{7,6},{8,9},{9,8},{10,11... | collective-permute-start | bytes 3145736 | tf_op jit(solution)/shard_map/ppermute | solution.py:849
  40.8 23.9 %collective-permute-start.2 = (f32[256,1024]{1,0:T(8,128)S(1)}, f32[256,1024]{1,0:T(8,128)}, u32[]{:S(2)}, u32[]{:S(2)}) collective-permute-start(f32[256,1024]{1,0:T(8,128)S(1)} %bitcast.47), channel_id=1, source_target_pairs={{0,1},{1,0},{2,3},{3,2},{4,5},{5,4},{6,7},{7,6},{8,9},{9,8},{10,11... | collective-permute-start | bytes 3145736 | tf_op jit(solution)/shard_map/ppermute | solution.py:849
  41.3 21.6 %collective-permute-start.1 = (bf16[4,144,768]{2,1,0:T(8,128)(2,1)S(1)}, bf16[4,144,768]{2,1,0:T(8,128)(2,1)S(1)}, u32[]{:S(2)}, u32[]{:S(2)}) collective-permute-start(bf16[4,144,768]{2,1,0:T(8,128)(2,1)S(1)} %all-to-all-done.w1_pieces_0_), channel_id=1, source_target_pairs={{0,4},{4,0},{8,12},{12,8},{16,20},{20,16},{24,28},{28,24},{1,5},{5... | collective-permute-start | bytes 2654216 | tf_op jit(solution)/shard_map/ppermute | solution.py:849
  42.8 13.6 %collective-permute-start.4 = (bf16[256,1024]{1,0:T(8,128)(2,1)S(1)}, bf16[256,1024]{1,0:T(8,128)(2,1)S(1)}, u32[]{:S(2)}, u32[]{:S(2)}) collective-permute-start(bf16[256,1024]{1,0:T(8,128)(2,1)S(1)} %bitcast_convert_fusion.cot_pieces_0_), channel_id=1, source_target_pairs={{0,2},{1,3},{2,0},{3,1},{4,6},{5,7},{6,4},{7,5},{8,10},{9,11},{10,... | collective-permute-start | bytes 1572872 | tf_op jit(solution)/shard_map/ppermute | solution.py:849
  56.3 6.5 %copy-start.16 = (bf16[256,1024]{1,0:T(8,128)(2,1)}, bf16[256,1024]{1,0:T(8,128)(2,1)S(1)}, u32[]{:S(2)}) copy-start(bf16[256,1024]{1,0:T(8,128)(2,1)S(1)} %collective-permute-done.4.cot_pieces_2_) | copy-start | bytes 1572868
  65.0 22.9 %copy-start.2 = (bf16[4,256,512]{2,1,0:T(8,128)(2,1)}, bf16[4,256,512]{2,1,0:T(8,128)(2,1)S(1)}, u32[]{:S(2)}) copy-start(bf16[4,256,512]{2,1,0:T(8,128)(2,1)S(1)} %all-to-all-done.1.g2_pieces_0_) | copy-start | bytes 3145732
  65.0 24.1 %collective-permute-start.5 = (bf16[4,256,512]{2,1,0:T(8,128)(2,1)S(1)}, bf16[4,256,512]{2,1,0:T(8,128)(2,1)S(1)}, u32[]{:S(2)}, u32[]{:S(2)}) collective-permute-start(bf16[4,256,512]{2,1,0:T(8,128)(2,1)S(1)} %all-to-all-done.1.g2_pieces_0_), channel_id=1, source_target_pairs={{0,4},{4,0},{8,12},{12,8},{16,20},{20,16},{24,28},{28,24},{1,5},{5... | collective-permute-start | bytes 3145736 | tf_op jit(solution)/shard_map/ppermute | solution.py:849
  66.5 21.4 %collective-permute-start.6 = (bf16[256,1024]{1,0:T(8,128)(2,1)S(1)}, bf16[256,1024]{1,0:T(8,128)(2,1)}, u32[]{:S(2)}, u32[]{:S(2)}) collective-permute-start(bf16[256,1024]{1,0:T(8,128)(2,1)S(1)} %bitcast_convert_fusion.cot_pieces_0_), channel_id=1, source_target_pairs={{0,1},{1,0},{2,3},{3,2},{4,5},{5,4},{6,7},{7,6},{8,9},{9,8},{10,11... | collective-permute-start | bytes 1572872 | tf_op jit(solution)/shard_map/ppermute | solution.py:849
  66.5 21.4 %collective-permute-start.7 = (bf16[256,1024]{1,0:T(8,128)(2,1)}, bf16[256,1024]{1,0:T(8,128)(2,1)}, u32[]{:S(2)}, u32[]{:S(2)}) collective-permute-start(bf16[256,1024]{1,0:T(8,128)(2,1)} %copy-done.16), channel_id=1, source_target_pairs={{0,1},{1,0},{2,3},{3,2},{4,5},{5,4},{6,7},{7,6},{8,9},{9,8},{10,11... | collective-permute-start | bytes 1572872 | tf_op jit(solution)/shard_map/ppermute | solution.py:849
  90.1 12.8 %copy-start.45 = (s32[4]{0:T(128)S(1)}, s32[4]{0:T(128)}, u32[]{:S(2)}) copy-start(s32[4]{0:T(128)} %constant.15.clone) | copy-start | bytes 52
  100.7 3.9 %collective-permute-start.10 = (f32[8,1024]{1,0:T(8,128)}, f32[8,1024]{1,0:T(8,128)S(1)}, u32[]{:S(2)}, u32[]{:S(2)}) collective-permute-start(f32[8,1024]{1,0:T(8,128)} %get-tuple-element.125), channel_id=1, source_target_pairs={{0,3},{1,2},{2,1},{3,0},{4,7},{5,6},{6,5},{7,4},{8,11},{9,10},{10,... | collective-permute-start | bytes 98312 | tf_op jit(solution)/shard_map/ppermute | solution.py:849
  100.8 3.8 %collective-permute-start.8 = (f32[8,1024]{1,0:T(8,128)}, f32[8,1024]{1,0:T(8,128)S(1)}, u32[]{:S(2)}, u32[]{:S(2)}) collective-permute-start(f32[8,1024]{1,0:T(8,128)} %get-tuple-element.125), channel_id=1, source_target_pairs={{0,1},{1,0},{2,3},{3,2},{4,5},{5,4},{6,7},{7,6},{8,9},{9,8},{10,11... | collective-permute-start | bytes 98312 | tf_op jit(solution)/shard_map/ppermute | solution.py:849
  102.4 4.1 %collective-permute-start.9 = (f32[8,1024]{1,0:T(8,128)}, f32[8,1024]{1,0:T(8,128)S(1)}, u32[]{:S(2)}, u32[]{:S(2)}) collective-permute-start(f32[8,1024]{1,0:T(8,128)} %get-tuple-element.125), channel_id=1, source_target_pairs={{0,2},{1,3},{2,0},{3,1},{4,6},{5,7},{6,4},{7,5},{8,10},{9,11},{10,... | collective-permute-start | bytes 98312 | tf_op jit(solution)/shard_map/ppermute | solution.py:849
  121.2 27.0 %collective-permute-start.11 = (bf16[4,256,512]{2,1,0:T(8,128)(2,1)}, bf16[4,256,512]{2,1,0:T(8,128)(2,1)S(1)}, u32[]{:S(2)}, u32[]{:S(2)}) collective-permute-start(bf16[4,256,512]{2,1,0:T(8,128)(2,1)} %get-tuple-element.140), channel_id=1, source_target_pairs={{0,4},{4,0},{8,12},{12,8},{16,20},{20,16},{24,28},{28,24},{1,5},{5... | collective-permute-start | bytes 3145736 | tf_op jit(solution)/shard_map/ppermute | solution.py:849
  122.8 23.9 %collective-permute-start.12 = (bf16[256,1024]{1,0:T(8,128)(2,1)}, bf16[256,1024]{1,0:T(8,128)(2,1)S(1)}, u32[]{:S(2)}, u32[]{:S(2)}) collective-permute-start(bf16[256,1024]{1,0:T(8,128)(2,1)} %get-tuple-element.141), channel_id=1, source_target_pairs={{0,1},{1,0},{2,3},{3,2},{4,5},{5,4},{6,7},{7,6},{8,9},{9,8},{10,11... | collective-permute-start | bytes 1572872 | tf_op jit(solution)/shard_map/ppermute | solution.py:849
  122.8 23.9 %collective-permute-start.13 = (bf16[256,1024]{1,0:T(8,128)(2,1)}, bf16[256,1024]{1,0:T(8,128)(2,1)S(1)}, u32[]{:S(2)}, u32[]{:S(2)}) collective-permute-start(bf16[256,1024]{1,0:T(8,128)(2,1)} %get-tuple-element.142), channel_id=1, source_target_pairs={{0,2},{1,3},{2,0},{3,1},{4,6},{5,7},{6,4},{7,5},{8,10},{9,11},{10,... | collective-permute-start | bytes 1572872 | tf_op jit(solution)/shard_map/ppermute | solution.py:849
  123.3 24.9 %collective-permute-start.14 = (bf16[256,1024]{1,0:T(8,128)(2,1)}, bf16[256,1024]{1,0:T(8,128)(2,1)S(1)}, u32[]{:S(2)}, u32[]{:S(2)}) collective-permute-start(bf16[256,1024]{1,0:T(8,128)(2,1)} %get-tuple-element.143), channel_id=1, source_target_pairs={{0,3},{1,2},{2,1},{3,0},{4,7},{5,6},{6,5},{7,4},{8,11},{9,10},{10,... | collective-permute-start | bytes 1572872 | tf_op jit(solution)/shard_map/ppermute | solution.py:849
  124.7 24.3 %copy-start.11 = (bf16[4,256,512]{2,1,0:T(8,128)(2,1)S(1)}, bf16[4,256,512]{2,1,0:T(8,128)(2,1)}, u32[]{:S(2)}) copy-start(bf16[4,256,512]{2,1,0:T(8,128)(2,1)} %get-tuple-element.170) | copy-start | bytes 3145732
  149.0 6.2 %copy-start.17 = (bf16[1024,256]{1,0:T(8,128)(2,1)S(1)}, bf16[1024,256]{1,0:T(8,128)(2,1)}, u32[]{:S(2)}) copy-start(bf16[1024,256]{1,0:T(8,128)(2,1)} %get-tuple-element.147) | copy-start | bytes 1572868
  149.0 6.2 %copy-start.44 = (bf16[4,128,512]{2,1,0:T(8,128)(2,1)S(1)}, bf16[4,128,512]{2,1,0:T(8,128)(2,1)}, u32[]{:S(2)}) copy-start(bf16[4,128,512]{2,1,0:T(8,128)(2,1)} %get-tuple-element.149) | copy-start | bytes 1572868
  150.2 36.8 %all-to-all-start.3 = ((bf16[4,256,512]{2,1,0:T(8,128)(2,1)}), bf16[4,256,512]{2,1,0:T(8,128)(2,1)S(1)}, u32[]{:S(2)}, u32[]{:S(2)}) async-start(bf16[4,256,512]{2,1,0:T(8,128)(2,1)} %add_convert_fusion), calls=%async_computation.3 | async-start | bytes 2097152 | tf_op jit(solution)/shard_map/all_to_all | solution.py:860
  155.2 1.9 collective-permute-start.15
  155.2 14.3 %collective-permute-start.17 = (bf16[4,128,512]{2,1,0:T(8,128)(2,1)S(1)}, bf16[4,128,512]{2,1,0:T(8,128)(2,1)S(1)}, u32[]{:S(2)}, u32[]{:S(2)}) collective-permute-start(bf16[4,128,512]{2,1,0:T(8,128)(2,1)S(1)} %copy-done.44), channel_id=1, source_target_pairs={{0,4},{4,0},{8,12},{12,8},{16,20},{20,16},{24,28},{28,24},{1,5},{5... | collective-permute-start | bytes 1572872 | tf_op jit(solution)/shard_map/ppermute | solution.py:849
  157.3 9.0 %copy-start.8 = (bf16[1024,256]{1,0:T(8,128)(2,1)}, bf16[1024,256]{1,0:T(8,128)(2,1)S(1)}, u32[]{:S(2)}) copy-start(bf16[1024,256]{1,0:T(8,128)(2,1)S(1)} %add_convert_fusion.1.dbc_ref) | copy-start | bytes 1572868
  157.3 14.0 %collective-permute-start.16 = (bf16[1024,256]{1,0:T(8,128)(2,1)S(1)}, bf16[1024,256]{1,0:T(8,128)(2,1)S(1)}, u32[]{:S(2)}, u32[]{:S(2)}) collective-permute-start(bf16[1024,256]{1,0:T(8,128)(2,1)S(1)} %add_convert_fusion.1.dbc_ref), channel_id=1, source_target_pairs={{0,2},{1,3},{2,0},{3,1},{4,6},{5,7},{6,4},{7,5},{8,10},{9,11},{10,... | collective-permute-start | bytes 1572872 | tf_op jit(solution)/shard_map/ppermute | solution.py:849
  169.6 14.4 %copy-start.19 = (bf16[4,128,512]{2,1,0:T(8,128)(2,1)}, bf16[4,128,512]{2,1,0:T(8,128)(2,1)S(1)}, u32[]{:S(2)}) copy-start(bf16[4,128,512]{2,1,0:T(8,128)(2,1)S(1)} %collective-permute-done.17.came_ref) | copy-start | bytes 1572868
  178.3 5.6 %collective-permute-start.18 = (bf16[160,512]{1,0:T(8,128)(2,1)}, bf16[160,512]{1,0:T(8,128)(2,1)S(1)}, u32[]{:S(2)}, u32[]{:S(2)}) collective-permute-start(bf16[160,512]{1,0:T(8,128)(2,1)} %get-tuple-element.165), channel_id=1, source_target_pairs={{0,4},{4,0},{8,12},{12,8},{16,20},{20,16},{24,28},{28,24},{1,5},{5... | collective-permute-start | bytes 491528 | tf_op jit(solution)/shard_map/ppermute | solution.py:849
  184.6 16.8 %copy-start.1 = (f32[1,256,1024]{2,1,0:T(8,128)S(1)}, f32[1,256,1024]{2,1,0:T(8,128)}, u32[]{:S(2)}) copy-start(f32[1,256,1024]{2,1,0:T(8,128)} %param.22) | copy-start | bytes 3145732
  187.0 44.2 %all-to-all-start.2 = ((bf16[4,192,512]{2,1,0:T(8,128)(2,1)}), bf16[4,192,512]{2,1,0:T(8,128)(2,1)S(1)}, u32[]{:S(2)}, u32[]{:S(2)}) async-start(bf16[4,192,512]{2,1,0:T(8,128)(2,1)} %pair_sum_late.1), calls=%async_computation.2 | async-start | bytes 1572864 | tf_op jit(solution)/shard_map/all_to_all | solution.py:860
  192.4 12.0 %copy-start.6 = (bf16[256,512]{1,0:T(8,128)(2,1)}, bf16[256,512]{1,0:T(8,128)(2,1)S(1)}, u32[]{:S(2)}) copy-start(bf16[256,512]{1,0:T(8,128)(2,1)S(1)} %reduce_sum.30.early_refs_0_) | copy-start | bytes 786436
  192.4 9.0 %collective-permute-start.20 = (bf16[256,512]{1,0:T(8,128)(2,1)S(1)}, bf16[256,512]{1,0:T(8,128)(2,1)S(1)}, u32[]{:S(2)}, u32[]{:S(2)}) collective-permute-start(bf16[256,512]{1,0:T(8,128)(2,1)S(1)} %reduce_sum.30.early_refs_0_), channel_id=1, source_target_pairs={{0,2},{1,3},{2,0},{3,1},{4,6},{5,7},{6,4},{7,5},{8,10},{9,11},{10,... | collective-permute-start | bytes 786440 | tf_op jit(solution)/shard_map/ppermute | solution.py:849
  192.9 11.4 %collective-permute-start.22 = (bf16[256,1024]{1,0:T(8,128)(2,1)}, bf16[256,1024]{1,0:T(8,128)(2,1)S(1)}, u32[]{:S(2)}, u32[]{:S(2)}) collective-permute-start(bf16[256,1024]{1,0:T(8,128)(2,1)} %get-tuple-element.176), channel_id=1, source_target_pairs={{0,1},{1,0},{2,3},{3,2},{4,5},{5,4},{6,7},{7,6},{8,9},{9,8},{10,11... | collective-permute-start | bytes 1572872 | tf_op jit(solution)/shard_map/ppermute | solution.py:849
  192.9 19.7 %collective-permute-start.23 = (bf16[256,1024]{1,0:T(8,128)(2,1)}, bf16[256,1024]{1,0:T(8,128)(2,1)S(1)}, u32[]{:S(2)}, u32[]{:S(2)}) collective-permute-start(bf16[256,1024]{1,0:T(8,128)(2,1)} %get-tuple-element.177), channel_id=1, source_target_pairs={{0,2},{1,3},{2,0},{3,1},{4,6},{5,7},{6,4},{7,5},{8,10},{9,11},{10,... | collective-permute-start | bytes 1572872 | tf_op jit(solution)/shard_map/ppermute | solution.py:849
  194.5 24.9 %collective-permute-start.24 = (bf16[256,1024]{1,0:T(8,128)(2,1)}, bf16[256,1024]{1,0:T(8,128)(2,1)S(1)}, u32[]{:S(2)}, u32[]{:S(2)}) collective-permute-start(bf16[256,1024]{1,0:T(8,128)(2,1)} %get-tuple-element.178), channel_id=1, source_target_pairs={{0,3},{1,2},{2,1},{3,0},{4,7},{5,6},{6,5},{7,4},{8,11},{9,10},{10,... | collective-permute-start | bytes 1572872 | tf_op jit(solution)/shard_map/ppermute | solution.py:849
  194.8 29.5 %collective-permute-start.19 = (bf16[256,512]{1,0:T(8,128)(2,1)S(1)}, bf16[256,512]{1,0:T(8,128)(2,1)S(1)}, u32[]{:S(2)}, u32[]{:S(2)}) collective-permute-start(bf16[256,512]{1,0:T(8,128)(2,1)S(1)} %reduce_sum.30.early_refs_0_), channel_id=1, source_target_pairs={{0,1},{1,0},{2,3},{3,2},{4,5},{5,4},{6,7},{7,6},{8,9},{9,8},{10,11... | collective-permute-start | bytes 786440 | tf_op jit(solution)/shard_map/ppermute | solution.py:849
  201.4 23.0 %collective-permute-start.21 = (bf16[256,512]{1,0:T(8,128)(2,1)S(1)}, bf16[256,512]{1,0:T(8,128)(2,1)S(1)}, u32[]{:S(2)}, u32[]{:S(2)}) collective-permute-start(bf16[256,512]{1,0:T(8,128)(2,1)S(1)} %collective-permute-done.20.early_refs_2_), channel_id=1, source_target_pairs={{0,1},{1,0},{2,3},{3,2},{4,5},{5,4},{6,7},{7,6},{8,9},{9,8},{10,11... | collective-permute-start | bytes 786440 | tf_op jit(solution)/shard_map/ppermute | solution.py:849
  204.4 15.0 %copy-start.23 = (bf16[256,1024]{1,0:T(8,128)(2,1)}, bf16[256,1024]{1,0:T(8,128)(2,1)S(1)}, u32[]{:S(2)}) copy-start(bf16[256,1024]{1,0:T(8,128)(2,1)S(1)} %collective-permute-done.22.part_refs_0_) | copy-start | bytes 1572868
  212.6 6.8 %copy-start.24 = (bf16[256,1024]{1,0:T(8,128)(2,1)}, bf16[256,1024]{1,0:T(8,128)(2,1)S(1)}, u32[]{:S(2)}) copy-start(bf16[256,1024]{1,0:T(8,128)(2,1)S(1)} %collective-permute-done.23.part_refs_1_) | copy-start | bytes 1572868
  231.2 16.6 %copy-start.30 = (f32[32,128]{1,0:T(8,128)S(1)}, f32[32,128]{1,0:T(8,128)}, u32[]{:S(2)}) copy-start(f32[32,128]{1,0:T(8,128)} %dt_ref.1) | copy-start | bytes 49156
  231.3 16.6 %copy-start.34 = (f32[32,128]{1,0:T(8,128)S(1)}, f32[32,128]{1,0:T(8,128)}, u32[]{:S(2)}) copy-start(f32[32,128]{1,0:T(8,128)} %param.33) | copy-start | bytes 49156
  231.3 16.6 %copy-start.35 = (f32[32,128]{1,0:T(8,128)S(1)}, f32[32,128]{1,0:T(8,128)}, u32[]{:S(2)}) copy-start(f32[32,128]{1,0:T(8,128)} %param.34) | copy-start | bytes 49156
  232.2 16.4 %copy-start.40 = (f32[3,32]{1,0:T(4,128)S(1)}, f32[3,32]{1,0:T(4,128)}, u32[]{:S(2)}) copy-start(f32[3,32]{1,0:T(4,128)} %param.41) | copy-start | bytes 1156
  232.2 16.4 %copy-start.41 = (f32[3,32]{1,0:T(4,128)S(1)}, f32[3,32]{1,0:T(4,128)}, u32[]{:S(2)}) copy-start(f32[3,32]{1,0:T(4,128)} %param.42) | copy-start | bytes 1156
  232.2 17.0 %copy-start.38 = (f32[384]{0:T(512)S(1)}, f32[384]{0:T(512)}, u32[]{:S(2)}) copy-start(f32[384]{0:T(512)} %gain_ref.1) | copy-start | bytes 4612
  232.2 17.0 %copy-start.42 = (f32[384]{0:T(512)S(1)}, f32[384]{0:T(512)}, u32[]{:S(2)}) copy-start(f32[384]{0:T(512)} %param.39) | copy-start | bytes 4612
  232.2 17.0 %copy-start.43 = (f32[384]{0:T(512)S(1)}, f32[384]{0:T(512)}, u32[]{:S(2)}) copy-start(f32[384]{0:T(512)} %param.40) | copy-start | bytes 4612
  232.2 17.7 %copy-start.31 = (f32[5,288]{1,0:T(8,128)S(1)}, f32[5,288]{1,0:T(8,128)}, u32[]{:S(2)}) copy-start(f32[5,288]{1,0:T(8,128)} %conv_ref.1) | copy-start | bytes 17284
  232.2 17.7 %copy-start.36 = (f32[5,288]{1,0:T(8,128)S(1)}, f32[5,288]{1,0:T(8,128)}, u32[]{:S(2)}) copy-start(f32[5,288]{1,0:T(8,128)} %param.37) | copy-start | bytes 17284
  232.2 17.7 %copy-start.37 = (f32[5,288]{1,0:T(8,128)S(1)}, f32[5,288]{1,0:T(8,128)}, u32[]{:S(2)}) copy-start(f32[5,288]{1,0:T(8,128)} %param.38) | copy-start | bytes 17284
  234.2 7.4 %collective-permute-start.27 = (bf16[192,512]{1,0:T(8,128)(2,1)}, bf16[192,512]{1,0:T(8,128)(2,1)S(1)}, u32[]{:S(2)}, u32[]{:S(2)}) collective-permute-start(bf16[192,512]{1,0:T(8,128)(2,1)} %sum_late.1.late_refs_0_), channel_id=1, source_target_pairs={{0,3},{1,2},{2,1},{3,0},{4,7},{5,6},{6,5},{7,4},{8,11},{9,10},{10,... | collective-permute-start | bytes 589832 | tf_op jit(solution)/shard_map/ppermute | solution.py:849
  236.0 9.9 %collective-permute-start.26 = (bf16[192,512]{1,0:T(8,128)(2,1)}, bf16[192,512]{1,0:T(8,128)(2,1)S(1)}, u32[]{:S(2)}, u32[]{:S(2)}) collective-permute-start(bf16[192,512]{1,0:T(8,128)(2,1)} %sum_late.1.late_refs_0_), channel_id=1, source_target_pairs={{0,2},{1,3},{2,0},{3,1},{4,6},{5,7},{6,4},{7,5},{8,10},{9,11},{10,... | collective-permute-start | bytes 589832 | tf_op jit(solution)/shard_map/ppermute | solution.py:849
  237.6 8.4 %collective-permute-start.25 = (bf16[192,512]{1,0:T(8,128)(2,1)}, bf16[192,512]{1,0:T(8,128)(2,1)S(1)}, u32[]{:S(2)}, u32[]{:S(2)}) collective-permute-start(bf16[192,512]{1,0:T(8,128)(2,1)} %sum_late.1.late_refs_0_), channel_id=1, source_target_pairs={{0,1},{1,0},{2,3},{3,2},{4,5},{5,4},{6,7},{7,6},{8,9},{9,8},{10,11... | collective-permute-start | bytes 589832 | tf_op jit(solution)/shard_map/ppermute | solution.py:849
  241.6 9.0 %copy-start.26 = (bf16[192,512]{1,0:T(8,128)(2,1)}, bf16[192,512]{1,0:T(8,128)(2,1)S(1)}, u32[]{:S(2)}) copy-start(bf16[192,512]{1,0:T(8,128)(2,1)S(1)} %collective-permute-done.27.late_refs_3_) | copy-start | bytes 589828
  245.9 4.7 %copy-start.27 = (bf16[192,512]{1,0:T(8,128)(2,1)}, bf16[192,512]{1,0:T(8,128)(2,1)S(1)}, u32[]{:S(2)}) copy-start(bf16[192,512]{1,0:T(8,128)(2,1)S(1)} %collective-permute-done.26.late_refs_2_) | copy-start | bytes 589828
  245.9 4.7 %copy-start.28 = (bf16[192,512]{1,0:T(8,128)(2,1)}, bf16[192,512]{1,0:T(8,128)(2,1)S(1)}, u32[]{:S(2)}) copy-start(bf16[192,512]{1,0:T(8,128)(2,1)S(1)} %collective-permute-done.25.late_refs_1_) | copy-start | bytes 589828
  (14 other events, 16.6 us)

commit v8 on v7

--- a/solution.py
+++ b/solution.py
@@ -13,6 +13,7 @@
 STATE = 128
 CONV = 4
 STEP = 10
+SPAN = 128
 
 F32 = jnp.float32
 BF16 = jnp.bfloat16
@@ -87,7 +88,7 @@
 def triangle(size, lower):
     row = lax.broadcasted_iota(jnp.int32, (size, size), 0)
     col = lax.broadcasted_iota(jnp.int32, (size, size), 1)
-    keep = row >= col if lower else row <= col
+    keep = (row >= col if lower else row <= col) & (row // SPAN == col // SPAN)
     return jnp.where(keep, 1.0, 0.0).astype(F32)
 
 
@@ -293,39 +294,43 @@
     stepr_ref[...] = step_r
     logr_ref[...] = log_r
 
-    values = mixed[:, :width]
-    write = mixed[:, width : width + STATE]
-    read = mixed[:, width + STATE :]
-    row = lax.broadcasted_iota(jnp.int32, (span, span), 0)
-    col = lax.broadcasted_iota(jnp.int32, (span, span), 1)
-    visible = (seg_here == segr_ref[...]) & (row >= col)
-    scores = jnp.where(visible, nt(read, write), 0.0)
-    lane = lax.broadcasted_iota(jnp.int32, (span, 2 * HEAD_DIM), 1)
-
-    seg_prev = seg_ref[7:8]
-    seg_last = seg_ref[span + 7 : span + 8]
-    last = log_c[span - 1 : span]
-    enter = jnp.where(seg_here == seg_prev, jnp.exp(log_c), 0.0)
-    tail = jnp.where(seg_here == seg_last, jnp.exp(last - log_c), 0.0) * step_c
-    keep = jnp.where(seg_last == seg_prev, jnp.exp(last), 0.0)
+    low = lax.broadcasted_iota(jnp.int32, (SPAN, 2 * HEAD_DIM), 1) < HEAD_DIM
+    earlier = lax.broadcasted_iota(jnp.int32, (SPAN, SPAN), 0) >= lax.broadcasted_iota(
+        jnp.int32, (SPAN, SPAN), 1
+    )
+    skip_w = spread(hrow_ref[2:3] + jnp.zeros((8, heads), F32), width)[0:1]
     state = state_ref[...]
-    start_ref[0] = state
-    values_f = values.astype(F32)
-    base = spread(enter, width) * nn(read, state.astype(BF16)) + spread(
-        hrow_ref[2:3] + jnp.zeros((8, heads), F32), width
-    )[0:1] * values_f
-    for pair in range(heads // 2):
-        lanes = slice(pair * 2 * HEAD_DIM, (pair + 1) * 2 * HEAD_DIM)
-        pieces = []
-        for head in (2 * pair, 2 * pair + 1):
-            gap = jnp.minimum(log_c[:, head : head + 1] - log_r[head : head + 1], 0.0)
-            weights = scores * jnp.exp(gap) * step_r[head : head + 1]
-            pieces.append(nn(weights.astype(BF16), values[:, lanes]))
-        inner_ref[:, lanes] = base[:, lanes] + jnp.where(lane < HEAD_DIM, pieces[0], pieces[1])
-    moved = (spread(tail, width) * values_f).astype(BF16)
-    state_ref[...] = spread(keep + jnp.zeros((8, heads), F32), width)[0:1] * state + tn(
-        write, moved
-    )
+    for block in range(span // SPAN):
+        here = slice(block * SPAN, (block + 1) * SPAN)
+        values = mixed[here, :width]
+        write = mixed[here, width : width + STATE]
+        read = mixed[here, width + STATE :]
+        seg = seg_here[here]
+        log = log_c[here]
+        log_row = log_r[:, here]
+        step_row = step_r[:, here]
+        scores = jnp.where((seg == segr_ref[:, here]) & earlier, nt(read, write), 0.0)
+        seg_prev = seg_ref[7 + block * SPAN : 8 + block * SPAN]
+        seg_last = seg_ref[7 + (block + 1) * SPAN : 8 + (block + 1) * SPAN]
+        last = log[SPAN - 1 : SPAN]
+        enter = jnp.where(seg == seg_prev, jnp.exp(log), 0.0)
+        tail = jnp.where(seg == seg_last, jnp.exp(last - log), 0.0) * step_c[here]
+        keep = jnp.where(seg_last == seg_prev, jnp.exp(last), 0.0)
+        start_ref[block] = state
+        values_f = values.astype(F32)
+        base = spread(enter, width) * nn(read, state.astype(BF16)) + skip_w * values_f
+        for pair in range(heads // 2):
+            lanes = slice(pair * 2 * HEAD_DIM, (pair + 1) * 2 * HEAD_DIM)
+            pieces = []
+            for head in (2 * pair, 2 * pair + 1):
+                gap = jnp.minimum(log[:, head : head + 1] - log_row[head : head + 1], 0.0)
+                weights = scores * jnp.exp(gap) * step_row[head : head + 1]
+                pieces.append(nn(weights.astype(BF16), values[:, lanes]))
+            inner_ref[here, lanes] = base[:, lanes] + jnp.where(low, pieces[0], pieces[1])
+        moved = (spread(tail, width) * values_f).astype(BF16)
+        keep_w = spread(keep + jnp.zeros((8, heads), F32), width)[0:1]
+        state = keep_w * state + tn(write, moved)
+    state_ref[...] = state
 
 
 def gate_kernel(
@@ -342,6 +347,7 @@
     gate_ref,
     ng_ref,
     stat_ref,
+    turned_ref,
     sems,
     cot_sems,
 ):
@@ -371,11 +377,12 @@
             copy.start()
         for copy in copies + cots:
             copy.wait()
+        turned_ref[...] = wout_ref[...].T
 
     gate = nn(hid_ref[...], wg_ref[...]).astype(BF16)
     gate_ref[...] = gate
     gate = gate.astype(F32)
-    grad = nt(cot_ref[step], wout_ref[...])
+    grad = nn(cot_ref[step], turned_ref[...])
     ng_ref[...] = grad
     gated = inner_ref[...] * (gate * sigmoid(gate))
     squares = jnp.sum(gated * gated, axis=1, keepdims=True)
@@ -509,95 +516,100 @@
 
     seg_ref[...] = segc_ref[pl.ds(pl.multiple_of(chunk * span, 8), span + 16), :]
     seg_here = seg_ref[8 : 8 + span]
-    seg_prev = seg_ref[7:8]
-    seg_last = seg_ref[span + 7 : span + 8]
-    mixed = mixed_ref[...]
-    values = mixed[:, :width]
-    write = mixed[:, width : width + STATE]
-    read = mixed[:, width + STATE :]
-    values_f = values.astype(F32)
-    dy = dy_ref[...]
-    dy_low = dy.astype(BF16)
+    low = lax.broadcasted_iota(jnp.int32, (SPAN, 2 * HEAD_DIM), 1) < HEAD_DIM
+    earlier = lax.broadcasted_iota(jnp.int32, (SPAN, SPAN), 0) >= lax.broadcasted_iota(
+        jnp.int32, (SPAN, SPAN), 1
+    )
+    head_at = lax.broadcasted_iota(jnp.int32, (heads, SPAN), 0)
+    lane_at = lax.broadcasted_iota(jnp.int32, (SPAN, heads), 1)
+    at_last = lax.broadcasted_iota(jnp.int32, (SPAN, heads), 0) == SPAN - 1
+    skip_w = spread(hrow_ref[2:3] + jnp.zeros((8, heads), F32), width)[0:1]
     step_c = stepc_ref[...]
-    log_c = logc_ref[...]
     step_r = stepr_ref[...]
-    log_r = logr_ref[...]
-    last = log_c[span - 1 : span]
-    enter = jnp.where(seg_here == seg_prev, jnp.exp(log_c), 0.0)
-    tail_raw = jnp.where(seg_here == seg_last, jnp.exp(last - log_c), 0.0)
-    tail = tail_raw * step_c
-    keep = jnp.where(seg_last == seg_prev, jnp.exp(last), 0.0)
-    enter_w = spread(enter, width)
-    tail_w = spread(tail, width)
-    wide = spread(
-        jnp.concatenate([hrow_ref[2:3] + jnp.zeros((8, heads), F32), keep + jnp.zeros((8, heads), F32)], axis=0),
-        width,
-    )
-    skip_w = wide[0:1]
-    keep_w = wide[8:9]
-    state = start_ref[0]
-    state_low = state.astype(BF16)
     later = grad_ref[...]
-    later_low = later.astype(BF16)
-
-    row = lax.broadcasted_iota(jnp.int32, (span, span), 0)
-    col = lax.broadcasted_iota(jnp.int32, (span, span), 1)
-    visible = (seg_here == segr_ref[...]) & (row >= col)
-    scores = jnp.where(visible, nt(read, write), 0.0)
-    lane = lax.broadcasted_iota(jnp.int32, (span, 2 * HEAD_DIM), 1)
-    head_at = lax.broadcasted_iota(jnp.int32, (8, span), 0)
-    lane_at = lax.broadcasted_iota(jnp.int32, (span, heads), 1)
-
-    entered = enter_w * dy
-    entered_low = entered.astype(BF16)
-    inter = enter_w * nn(read, state_low)
-    from_later = nn(write, later_low)
-    moved_low = (tail_w * values_f).astype(BF16)
-    dread = nt(entered_low, state_low)
-    dwrite = nt(moved_low, later_low)
-    dlog_c = gather_heads(dy * inter, heads)
-    tail_dot = gather_heads(values_f * from_later, heads)
-    dlog_c = dlog_c - tail_dot * tail
-    dstep_c = tail_dot * tail_raw
-    carried = gather_heads(jnp.sum(later * state, axis=0, keepdims=True) + jnp.zeros((8, width), F32), heads)[0:1]
-    at_last = lax.broadcasted_iota(jnp.int32, (span, heads), 0) == span - 1
-    dlog_c = dlog_c + jnp.where(
-        at_last, jnp.sum(tail_dot * tail, axis=0, keepdims=True) + keep * carried, 0.0
-    )
-    grad_ref[...] = keep_w * later + tn(read, entered_low)
-    dx_ref[...] = tail_w * from_later + skip_w * dy
-
-    dscores = jnp.zeros((span, span), F32)
-    dstep_r = jnp.zeros((8, span), F32)
-    for pair in range(heads // 2):
-        lanes = slice(pair * 2 * HEAD_DIM, (pair + 1) * 2 * HEAD_DIM)
-        dy_pair = dy_low[:, lanes]
-        pieces = []
-        for head in (2 * pair, 2 * pair + 1):
-            mine = lane < HEAD_DIM if head % 2 == 0 else lane >= HEAD_DIM
-            gap = jnp.minimum(log_c[:, head : head + 1] - log_r[head : head + 1], 0.0)
-            decay = jnp.exp(gap)
-            outer = nt(jnp.where(mine, dy_pair, jnp.zeros_like(dy_pair)), values[:, lanes])
-            fade = decay * step_r[head : head + 1]
-            dscores = dscores + outer * fade
-            flow = outer * scores
-            base = flow * decay
-            dstep_r = dstep_r + jnp.where(head_at == head, jnp.sum(base, axis=0, keepdims=True), 0.0)
-            dlog_c = dlog_c + jnp.where(
-                lane_at == head, jnp.sum(flow * fade, axis=1, keepdims=True), 0.0
-            )
-            pieces.append(tn((scores * fade).astype(BF16), dy_pair))
-        dx_ref[:, lanes] += jnp.where(lane < HEAD_DIM, pieces[0], pieces[1])
-    dscores = jnp.where(visible, dscores, 0.0).astype(BF16)
-    dread = dread + nn(dscores, write)
-    dwrite = dwrite + tn(dscores, read)
-    dbc_ref[:, :STATE] = dwrite.astype(BF16)
-    dbc_ref[:, STATE:] = dread.astype(BF16)
+    count = span // SPAN
+    dlogs, dsteps_c, dsteps_r = [None] * count, [None] * count, [None] * count
+    for block in reversed(range(count)):
+        here = slice(block * SPAN, (block + 1) * SPAN)
+        values = mixed_ref[here, :width]
+        write = mixed_ref[here, width : width + STATE]
+        read = mixed_ref[here, width + STATE :]
+        values_f = values.astype(F32)
+        seg = seg_here[here]
+        seg_prev = seg_ref[7 + block * SPAN : 8 + block * SPAN]
+        seg_last = seg_ref[7 + (block + 1) * SPAN : 8 + (block + 1) * SPAN]
+        dy = dy_ref[here]
+        dy_low = dy.astype(BF16)
+        log = logc_ref[here]
+        log_row = logr_ref[:, here]
+        step_row = step_r[:, here]
+        last = log[SPAN - 1 : SPAN]
+        enter = jnp.where(seg == seg_prev, jnp.exp(log), 0.0)
+        tail_raw = jnp.where(seg == seg_last, jnp.exp(last - log), 0.0)
+        tail = tail_raw * step_c[here]
+        keep = jnp.where(seg_last == seg_prev, jnp.exp(last), 0.0)
+        enter_w = spread(enter, width)
+        tail_w = spread(tail, width)
+        keep_w = spread(keep + jnp.zeros((8, heads), F32), width)[0:1]
+        state = start_ref[block]
+        state_low = state.astype(BF16)
+        later_low = later.astype(BF16)
+
+        entered_low = (enter_w * dy).astype(BF16)
+        inter = enter_w * nn(read, state_low)
+        from_later = nn(write, later_low)
+        moved_low = (tail_w * values_f).astype(BF16)
+        dread = nt(entered_low, state_low)
+        dwrite = nt(moved_low, later_low)
+        tail_dot = gather_heads(values_f * from_later, heads)
+        dlog = gather_heads(dy * inter, heads) - tail_dot * tail
+        dsteps_c[block] = tail_dot * tail_raw
+        carried = jnp.sum(later * state, axis=0, keepdims=True) + jnp.zeros((8, width), F32)
+        carried = gather_heads(carried, heads)[0:1]
+        dlog = dlog + jnp.where(
+            at_last, jnp.sum(tail_dot * tail, axis=0, keepdims=True) + keep * carried, 0.0
+        )
+        later = keep_w * later + tn(read, entered_low)
+        direct = tail_w * from_later + skip_w * dy
+
+        visible = (seg == segr_ref[:, here]) & earlier
+        scores = jnp.where(visible, nt(read, write), 0.0)
+        dscores = jnp.zeros((SPAN, SPAN), F32)
+        dstep = jnp.zeros((heads, SPAN), F32)
+        for pair in range(heads // 2):
+            lanes = slice(pair * 2 * HEAD_DIM, (pair + 1) * 2 * HEAD_DIM)
+            dy_pair = dy_low[:, lanes]
+            pieces = []
+            for head in (2 * pair, 2 * pair + 1):
+                mine = low if head % 2 == 0 else ~low
+                gap = jnp.minimum(log[:, head : head + 1] - log_row[head : head + 1], 0.0)
+                decay = jnp.exp(gap)
+                outer = nt(jnp.where(mine, dy_pair, jnp.zeros_like(dy_pair)), values[:, lanes])
+                fade = decay * step_row[head : head + 1]
+                dscores = dscores + outer * fade
+                weights = scores * fade
+                flow = outer * scores
+                dstep = dstep + jnp.where(
+                    head_at == head, jnp.sum(flow * decay, axis=0, keepdims=True), 0.0
+                )
+                dlog = dlog + jnp.where(
+                    lane_at == head, jnp.sum(outer * weights, axis=1, keepdims=True), 0.0
+                )
+                pieces.append(tn(weights.astype(BF16), dy_pair))
+            dx_ref[here, lanes] = direct[:, lanes] + jnp.where(low, pieces[0], pieces[1])
+        dscores = jnp.where(visible, dscores, 0.0).astype(BF16)
+        dbc_ref[here, :STATE] = (dwrite + tn(dscores, read)).astype(BF16)
+        dbc_ref[here, STATE:] = (dread + nn(dscores, write)).astype(BF16)
+        dlogs[block], dsteps_r[block] = dlog, dstep
+    grad_ref[...] = later
+    dlog_c = jnp.concatenate(dlogs, axis=0)
+    dstep_c = jnp.concatenate(dsteps_c, axis=0)
+    dstep_r = jnp.concatenate(dsteps_r, axis=1)
 
     upper = triangle(span, False)
-    eye = jnp.where(row == col, 1.0, 0.0).astype(F32)
-    dalpha = nn(upper, dlog_c, HIGHEST) - nt(upper, dstep_r * step_r, HIGHEST)[:, :heads]
-    dstep = dstep_c + nt(eye, dstep_r, HIGHEST)[:, :heads]
+    eye = jnp.where(diagonal(span), 1.0, 0.0).astype(F32)
+    dalpha = nn(upper, dlog_c, HIGHEST) - nt(upper, dstep_r * step_r, HIGHEST)
+    dstep = dstep_c + nt(eye, dstep_r, HIGHEST)
     rate = jnp.exp(hrow_ref[0:1])
     draw = (dstep - rate * dalpha) * sigmoid(raw_ref[...])
     draw_low = draw.astype(BF16)
@@ -644,12 +656,17 @@
     gain_ref,
     out_refs,
     gsum_ref,
+    turned_ref,
 ):
+    width = wg_ref.shape[1]
+
     @pl.when(pl.program_id(0) == 0)
     def _():
         gsum_ref[...] = jnp.zeros_like(gsum_ref)
-
-    total = nt(dgate_ref[...], wg_ref[...]) + nt(dval_ref[...], wv_ref[...])
+        turned_ref[0:width] = wg_ref[...].T
+        turned_ref[width:] = wv_ref[...].T
+
+    total = nn(dgate_ref[...], turned_ref[0:width]) + nn(dval_ref[...], turned_ref[width:])
     total = total + nn(dstep_ref[...], wdt_ref[...])
     step = pl.program_id(0)
 
@@ -948,12 +965,14 @@
     cot_low = cotangent[0].astype(BF16)
     if near:
         tok_far = swap(tok, "ctx", 2)
+        tok_core = swap(tok, "ctx", 1)
         w1 = high_all_to_all(w1)
-        w1, tok_far, tok_sent, g2, cot_low = lax.optimization_barrier((w1, tok_far, tok, g2, cot_low))
+        w1, g2, cot_low = lax.optimization_barrier((w1, g2, cot_low))
         w1_came = swap(w1, "dp", 1)
-        toks = [tok, swap(tok_sent, "ctx", 1), tok_far, swap(tok_far, "ctx", 1)]
         g2 = high_all_to_all(g2)
         cot_far = swap(cot_low, "ctx", 2)
+        w1, w1_came, tok_far = lax.optimization_barrier((w1, w1_came, tok_far))
+        toks = [tok, tok_core, tok_far, swap(tok_far, "ctx", 1)]
         w1, w1_came, toks, g2, cot_far, cot_low = lax.optimization_barrier(
             (w1, w1_came, toks, g2, cot_far, cot_low)
         )
@@ -1015,7 +1034,7 @@
                 rows(heads),
                 row_of,
                 row_of,
-                pl.BlockSpec((1, STATE, width), lambda i, *_: (i, 0, 0)),
+                pl.BlockSpec((span // SPAN, STATE, width), lambda i, *_: (i, 0, 0)),
             ],
             scratch_shapes=[
                 pltpu.VMEM((span + 8, wide), F32),
@@ -1045,7 +1064,7 @@
             shape_of(length, heads),
             shape_of(heads, length),
             shape_of(heads, length),
-            shape_of(chunks, STATE, width),
+            shape_of(length // SPAN, STATE, width),
         ],
         compiler_params=params("arbitrary"),
         name="scan_forward",
@@ -1066,6 +1085,7 @@
                 pl.BlockSpec((8, span), lambda i, *_: (0, i)),
             ],
             scratch_shapes=[
+                pltpu.VMEM((model, width), BF16),
                 pltpu.SemaphoreType.DMA((copies_of(g2, 3),)),
                 pltpu.SemaphoreType.DMA((nctx,)),
             ],
@@ -1143,7 +1163,7 @@
                 back(heads),
                 back_row,
                 back_row,
-                pl.BlockSpec((1, STATE, width), lambda i, *_: (chunks - 1 - i, 0, 0)),
+                pl.BlockSpec((span // SPAN, STATE, width), lambda i, *_: (chunks - 1 - i, 0, 0)),
                 full((8, width)),
                 full((3, heads)),
                 full((length + 16, 1)),
@@ -1187,12 +1207,14 @@
     if near:
         late_came = swap(late_send, "dp", 1)
         early_came, blocks_out, dval = lax.optimization_barrier((early_came, blocks_out, dval))
+    dbc = (dbc.astype(F32) + dbc_came.astype(F32)).astype(BF16)
+    if near:
+        early_came, dbc = lax.optimization_barrier((early_came, dbc))
         early_parts = (early_keep.astype(F32) + early_came.astype(F32)).astype(BF16)
-        early_parts = high_all_to_all(early_parts)
-    dbc = (dbc.astype(F32) + dbc_came.astype(F32)).astype(BF16)
-    dval, dbc = lax.optimization_barrier((dval, dbc))
     dbc_far = swap(dbc, "ctx", 2)
     if near:
+        dval, early_parts = lax.optimization_barrier((dval, early_parts))
+        early_parts = high_all_to_all(early_parts)
         dbc_far, late_came = lax.optimization_barrier((dbc_far, late_came))
 
     hidden_out, gain_sum = pl.pallas_call(
@@ -1211,6 +1233,7 @@
                 full((1, model)),
             ],
             out_specs=[[whole] * nctx, full((8, model))],
+            scratch_shapes=[pltpu.VMEM((2 * width, model), BF16)],
         ),
         out_shape=[
             [shape_of(span, model, dtype=BF16)] * nctx,
@@ -1274,14 +1297,15 @@
         gain_sum,
     )
 
-    input_grad = pl.pallas_call(
+    block_output = tok + sum(part.astype(F32) for part in blocks_out)
+
+    input_part = lambda parts, own: pl.pallas_call(
         input_back_kernel,
         in_specs=[[vmem] * nctx] + [vmem] * 4,
         out_shape=shape_of(span, model),
         compiler_params=params(),
         name="input_back",
-    )(hidden_out, hidden_own, tok, gain_pre, cotangent[0])
-    block_output = tok + sum(part.astype(F32) for part in blocks_out)
+    )(parts, own, tok, gain_pre, cotangent[0])
 
     late_rows = block_in + 64
     if near:
@@ -1320,13 +1344,16 @@
             compiler_params=params(),
             name="sum_late",
         )(late_parts)
+        late, hidden_out = lax.optimization_barrier((late, hidden_out))
         late = fan_ctx(late)
-        in_block = row_block(16, in_weight.shape[1])
+        input_grad = input_part(hidden_out, hidden_own)
+        late, input_grad = lax.optimization_barrier((late, input_grad))
+        in_block = row_block(32, in_weight.shape[1])
         in_new = pl.pallas_call(
             adam_in_kernel,
             grid_spec=pltpu.PrefetchScalarGridSpec(
                 num_scalar_prefetch=1,
-                grid=(rows_in // 16,),
+                grid=(rows_in // 32,),
                 in_specs=[in_block] * 3 + [early_spec, [full((late_rows, width))] * nctx],
                 out_specs=[in_block] * 3,
                 scratch_shapes=[early_scratch, pltpu.VMEM((nctx, late_rows, width), BF16)],
@@ -1339,6 +1366,7 @@
         small = jnp.stack([part[block_in : block_in + 32] for part in late])[c ^ jnp.arange(nctx)]
         small = small.astype(F32)
     else:
+        input_grad = input_part(hidden_out, hidden_own)
         blocks = lambda keep, send: jnp.stack([keep, send], axis=1).reshape((heads,) + keep.shape[1:])
         early = blocks(early_keep, early_send).astype(F32)
         late = blocks(late_keep, late_send).astype(F32)

time: 262 us -> 271 us (1.034)
  waiting for transfers between devices: 88 us -> 100 us
  starting transfers between devices: 41.7 us -> 38.8 us
    all_to_all x4, waiting for transfers between devices: 0.29 us -> 20.6 us  [high_all_to_all(): return lax.all_to_all(value, 'dp', 0, 0, axis_index_groups=groups)]
    ppermute x28, waiting for transfers between devices: 87.7 us -> 79.8 us  [swap(): return lax.ppermute(value, axis, [(at, at ^ bit) for at in range(count)])]
    all_to_all x4, starting transfers between devices: 21.2 us -> 17.8 us  [high_all_to_all(): return lax.all_to_all(value, 'dp', 0, 0, axis_index_groups=groups)]
    unnamed x95 -> x89, local copies, waits for them, and re-layouts: 8.32 us -> 6.65 us
  transfers between devices with their start and end apart: 32 -> 32, of which waited for: 17 -> 16; matrix products, arithmetic and copies ran while one was open for 3% -> 3% of each run, Pallas kernels for 26% -> 26%
where the time goes in v8:
time: 271 us; the launch traced here: 269 us
  Pallas kernels  106 us (39%)
  waiting for transfers between devices  100 us (37%)
  starting transfers between devices  38.8 us (14%)
  other arithmetic  11.6 us (4%)
  local copies, waits for them, and re-layouts  11 us (4%)
    ppermute x28, waiting for transfers between devices, swap(): return lax.ppermute(value, axis, [(at, at ^ bit) for at in range(count)])  79.8 us
    pallas_call x1, Pallas kernels, shards(): pl.pallas_call(scan_back_kernel, grid_spec=pltpu.PrefetchScalarGridSpec(n...  22.4 us
    ppermute x28, starting transfers between devices, swap(): return lax.ppermute(value, axis, [(at, at ^ bit) for at in range(count)])  21 us
    all_to_all x4, waiting for transfers between devices, high_all_to_all(): return lax.all_to_all(value, 'dp', 0, 0, axis_index_groups=groups)  20.6 us
    pallas_call x1, Pallas kernels, shards(): pl.pallas_call(scan_forward_kernel, grid_spec=pltpu.PrefetchScalarGridSpe...  18.4 us
    all_to_all x4, starting transfers between devices, high_all_to_all(): return lax.all_to_all(value, 'dp', 0, 0, axis_index_groups=groups)  17.8 us
    pallas_call x1, Pallas kernels, shards(): pl.pallas_call(norm_back_kernel, grid_spec=pltpu.PrefetchScalarGridSpec(n...  13.3 us
    pallas_call x1, Pallas kernels, shards(): pl.pallas_call(gate_kernel, grid_spec=pltpu.PrefetchScalarGridSpec(num_sc...  10.8 us
  transfers between devices with their start and end apart: 32, of which 16 were waited for; matrix products, arithmetic and copies ran while one was open for 3% of the time, Pallas kernels for 26%

profile of v8, /device:TPU:0, one launch (start us, length us, event | category | flops | bytes accessed | tf_op | source)
XLA Modules:
  0.0 269.1 jit_solution(7943584037720166861)
XLA Ops:
  0.7 0.6 pad_add_fusion.here_ref
  1.2 3.6 %pack.1 = (bf16[4,144,768]{2,1,0:T(8,128)(2,1)}, bf16[4,256,512]{2,1,0:T(8,128)(2,1)}) custom-call(s32[3]{0:T(128)} %pad_add_fusion.here_ref, f32[128,4352]{1,0:T(8,128)} %weight_ref.3, f32[256,1024]{1,0:T(8,128)} %weight_ref.2, f32[32,128]{1,0:T(8,128)} %dt_ref.1, f32[5,288]{1,0:T(8,128)} %conv_ref.1, f32[384]{0:T(512)} %gain_ref.1), custom_call_target="tpu_custom_call" | custom-call | tf_op jit(solution)/shard_map/pack/pallas_call | solution.py:954
  4.8 6.3 %all-to-all-start = ((bf16[4,144,768]{2,1,0:T(8,128)(2,1)}), bf16[4,144,768]{2,1,0:T(8,128)(2,1)}, u32[]{:S(2)}, u32[]{:S(2)}) async-start(bf16[4,144,768]{2,1,0:T(8,128)(2,1)} %get-tuple-element.117), calls=%async_computation | async-start | bytes 1769472 | tf_op jit(solution)/shard_map/all_to_all | solution.py:877
  11.1 1.6 collective-permute-start.1
  12.8 20.6 %all-to-all-done.w1_pieces_0_ = bf16[4,144,768]{2,1,0:T(8,128)(2,1)} async-done(((bf16[4,144,768]{2,1,0:T(8,128)(2,1)}), bf16[4,144,768]{2,1,0:T(8,128)(2,1)}, u32[]{:S(2)}, u32[]{:S(2)}) %all-to-all-start) | async-done | bytes 884768 | tf_op jit(solution)/shard_map/all_to_all | solution.py:877
  33.4 1.5 collective-permute-start
  34.9 3.5 %all-to-all-start.1 = ((bf16[4,256,512]{2,1,0:T(8,128)(2,1)}), bf16[4,256,512]{2,1,0:T(8,128)(2,1)S(1)}, u32[]{:S(2)}, u32[]{:S(2)}) async-start(bf16[4,256,512]{2,1,0:T(8,128)(2,1)} %get-tuple-element.123), calls=%async_computation.1 | async-start | bytes 2097152 | tf_op jit(solution)/shard_map/all_to_all | solution.py:877
  38.6 15.7 %collective-permute-done.w1_pieces_1_ = bf16[4,144,768]{2,1,0:T(8,128)(2,1)S(1)} collective-permute-done((bf16[4,144,768]{2,1,0:T(8,128)(2,1)}, bf16[4,144,768]{2,1,0:T(8,128)(2,1)S(1)}, u32[]{:S(2)}, u32[]{:S(2)}) %collective-permute-start) | collective-permute-done | bytes 884768 | tf_op jit(solution)/shard_map/ppermute | solution.py:866
  54.3 1.5 collective-permute-start.4
  55.8 1.0 copy-done.8
  56.8 11.9 %collective-permute-done.4.cot_pieces_2_ = bf16[256,1024]{1,0:T(8,128)(2,1)} collective-permute-done((bf16[256,1024]{1,0:T(8,128)(2,1)S(1)}, bf16[256,1024]{1,0:T(8,128)(2,1)}, u32[]{:S(2)}, u32[]{:S(2)}) %collective-permute-start.4) | collective-permute-done | bytes 524320 | tf_op jit(solution)/shard_map/ppermute | solution.py:866
  68.7 1.6 collective-permute-start.5
  71.0 0.7 copy.66
  71.8 1.0 broadcast_in_dim.13.segc_ref
  72.8 0.6 pad_add_fusion.1.at_ref
  73.4 18.4 %scan_forward.1 = (bf16[1024,1024]{1,0:T(8,128)(2,1)}, f32[8,768]{1,0:T(8,128)}, f32[1,1024]{1,0:T(1,128)}, f32[1,512]{1,0:T(1,128)}, bf16[8,1024]{1,0:T(8,128)(...) custom-call(s32[3]{0:T(128)} %pad_add_fusion.here_ref, ...), custom_call_target="tpu_custom_call" | custom-call | tf_op jit(solution)/shard_map/scan_forward/pallas_call | solution.py:1008
  91.8 1.8 collective-permute-done.5.g2_pieces_1_
  93.6 1.0 copy-done.10
  94.6 10.8 %gate.1 = (bf16[1024,512]{1,0:T(8,128)(2,1)}, bf16[512,1024]{1,0:T(8,128)(2,1)}, bf16[4,256,1024]{2,1,0:T(8,128)(2,1)}, bf16[1024,512]{1,0:T(8,128)(2,1)}, f32[1024,512]{1,0:T(8,128)}, /*index=5*/f32[8,1024]{1,0:T(8,128)}) custom-call(s32[3]{0:T(128)} %pad_add_fusion.here_ref, s32[2]{0:T(128)} %pad_add_fusion.1.at_ref, ...), custom_call_target="tpu_custom_call" | custom-call | tf_op jit(solution)/shard_map/gate/pallas_call | solution.py:1073
  105.5 1.6 collective-permute-start.8
  108.1 1.2 collective-permute-done.10
  109.3 1.9 collective-permute-done.9
  111.2 1.4 add_add_fusion.1.stat_ref
  112.6 13.3 %norm_back.1 = (bf16[256,1024]{1,0:T(8,128)(2,1)}, bf16[256,1024]{1,0:T(8,128)(2,1)}, bf16[256,1024]{1,0:T(8,128)(2,1)}, bf16[256,1024]{1,0:T(8,128)(2,1)}, bf16...) custom-call(s32[4]{0:T(128)} %broadcast_xor_fusion.perm_ref, ...), custom_call_target="tpu_custom_call" | custom-call | tf_op jit(solution)/shard_map/norm_back/pallas_call | solution.py:1107
  125.9 1.6 collective-permute-start.11
  127.5 22.4 %scan_back.1 = (bf16[4,128,512]{2,1,0:T(8,128)(2,1)}, bf16[4,128,512]{2,1,0:T(8,128)(2,1)}, bf16[1024,512]{1,0:T(8,128)(2,1)}, bf16[1024,256]{1,0:T(8,128)(2,1)}...) custom-call(s32[4]{0:T(128)} %broadcast_xor_fusion.perm_ref, ...), custom_call_target="tpu_custom_call" | custom-call | tf_op jit(solution)/shard_map/scan_back/pallas_call | solution.py:1150
  151.0 0.9 collective-permute-start.14
  152.1 1.2 add_convert_fusion.1.dbc_ref
  153.3 12.0 %collective-permute-done.13 = bf16[256,1024]{1,0:T(8,128)(2,1)S(1)} collective-permute-done((bf16[256,1024]{1,0:T(8,128)(2,1)S(1)}, bf16[256,1024]{1,0:T(8,128)(2,1)S(1)}, u32[]{:S(2)}, u32[]{:S(2)}) %collective-permute-start.13) | collective-permute-done | bytes 524320 | tf_op jit(solution)/shard_map/ppermute | solution.py:866
  165.3 9.5 %collective-permute-done.14 = bf16[256,1024]{1,0:T(8,128)(2,1)S(1)} collective-permute-done((bf16[256,1024]{1,0:T(8,128)(2,1)S(1)}, bf16[256,1024]{1,0:T(8,128)(2,1)S(1)}, u32[]{:S(2)}, u32[]{:S(2)}) %collective-permute-start.14) | collective-permute-done | bytes 524320 | tf_op jit(solution)/shard_map/ppermute | solution.py:866
  174.8 0.8 copy-done.19
  175.6 1.3 add_convert_fusion
  176.9 3.5 %all-to-all-start.3 = ((bf16[4,256,512]{2,1,0:T(8,128)(2,1)}), bf16[4,256,512]{2,1,0:T(8,128)(2,1)S(1)}, u32[]{:S(2)}, u32[]{:S(2)}) async-start(bf16[4,256,512]{2,1,0:T(8,128)(2,1)} %add_convert_fusion), calls=%async_computation.3 | async-start | bytes 2097152 | tf_op jit(solution)/shard_map/all_to_all | solution.py:877
  180.4 0.6 collective-permute-start.17
  181.5 9.0 %hidden_back.1 = (bf16[256,1024]{1,0:T(8,128)(2,1)}, bf16[256,1024]{1,0:T(8,128)(2,1)}, bf16[256,1024]{1,0:T(8,128)(2,1)}, bf16[256,1024]{1,0:T(8,128)(2,1)}, f32[8,1024]{1,0:T(8,128)}) custom-call(s32[4]{0:T(128)} %broadcast_xor_fusion.perm_ref, bf16[1024,512]{1,0:T(8,128)(2,1)} %get-tuple-element.172.dgate_ref, ...), custom_call_target="tpu_custom_call" | custom-call | tf_op jit(solution)/shard_map/hidden_back/pallas_call | solution.py:1220
  190.5 4.5 %collective-permute-done.17.came_ref = bf16[4,128,512]{2,1,0:T(8,128)(2,1)S(1)} collective-permute-done((bf16[4,128,512]{2,1,0:T(8,128)(2,1)S(1)}, bf16[4,128,512]{2,1,0:T(8,128)(2,1)S(1)}, u32[]{:S(2)}, u32[]{:S(2)}) %collective-permute-start.17) | collective-permute-done | bytes 524320 | tf_op jit(solution)/shard_map/ppermute | solution.py:866
  195.2 0.8 copy-done.15
  196.0 6.2 %maps_back.1 = (bf16[160,512]{1,0:T(8,128)(2,1)}, bf16[160,512]{1,0:T(8,128)(2,1)}, f32[256,1024]{1,0:T(8,128)}) custom-call(s32[3]{0:T(128)} %pad_add_fusion.here_ref, bf16[1024,256]{1,0:T(8,128)(2,1)} %copy-done.7, bf16[1024,256]{1,0:T(8,128)(2,1)} %copy-done.15, f32[1024,768]{1,0:T(8,128)} %get-tuple-element.145.convsum_ref, ...), custom_call_target="tpu_custom_call" | custom-call | tf_op jit(solution)/shard_map/maps_back/pallas_call | solution.py:1248
  202.2 1.5 collective-permute-start.18
  203.8 4.5 %collective-permute-done.18.mcame_ref = bf16[160,512]{1,0:T(8,128)(2,1)S(1)} collective-permute-done((bf16[160,512]{1,0:T(8,128)(2,1)}, bf16[160,512]{1,0:T(8,128)(2,1)S(1)}, u32[]{:S(2)}, u32[]{:S(2)}) %collective-permute-start.18) | collective-permute-done | bytes 163872 | tf_op jit(solution)/shard_map/ppermute | solution.py:866
  208.3 0.7 copy-done.23
  209.0 2.4 pair_sum_late.1
  211.4 4.4 %all-to-all-start.2 = ((bf16[4,192,512]{2,1,0:T(8,128)(2,1)}), bf16[4,192,512]{2,1,0:T(8,128)(2,1)S(1)}, u32[]{:S(2)}, u32[]{:S(2)}) async-start(bf16[4,192,512]{2,1,0:T(8,128)(2,1)} %pair_sum_late.1), calls=%async_computation.2 | async-start | bytes 1572864 | tf_op jit(solution)/shard_map/all_to_all | solution.py:877
  216.1 0.6 collective-permute-start.20
  216.6 1.5 collective-permute-start.23
  218.8 6.4 %collective-permute-done.20.early_refs_2_ = bf16[256,512]{1,0:T(8,128)(2,1)S(1)} collective-permute-done((bf16[256,512]{1,0:T(8,128)(2,1)S(1)}, bf16[256,512]{1,0:T(8,128)(2,1)S(1)}, u32[]{:S(2)}, u32[]{:S(2)}) %collective-permute-start.20) | collective-permute-done | bytes 262176 | tf_op jit(solution)/shard_map/ppermute | solution.py:866
  225.2 3.0 %add_add_fusion = f32[256,1024]{1,0:T(8,128)} fusion(bf16[256,1024]{1,0:T(8,128)(2,1)} %get-tuple-element.186, bf16[256,1024]{1,0:T(8,128)(2,1)} %copy-done.19, bf16[256,1024]{1,0:T(8,128)(2,1)} %copy-done.18, bf16[256,1024]{1,0:T(8,128)(2,1)} %copy-done.17, f32[1,256,1024]{2,1,0:T(8,128)S(1)} %copy-done.1), kind=kLoop, calls=%fused_computation.2 | loop fusion | flops 2097152 | bytes 4194304 | tf_op jit(solution)/shard_map/add | solution.py:1300
  228.2 0.7 copy-done.12
  228.9 0.7 copy-done.13
  229.6 5.5 %adam_out.1 = (f32[256,1024]{1,0:T(8,128)}, f32[256,1024]{1,0:T(8,128)}, f32[256,1024]{1,0:T(8,128)}) custom-call(s32[3]{0:T(128)} %pad_add_fusion.here_ref, f32[256,1024]{1,0:T(8,128)} %weight_ref.2, f32[256,1024]{1,0:T(8,128)} %first_ref.2, f32[256,1024]{1,0:T(8,128)} %second_ref.2, bf16[256,512]{1,0:T(8,128)(2,1)} %copy-done.5, ...), custom_call_target="tpu_custom_call" | custom-call | tf_op jit(solution)/shard_map/adam_out/pallas_call | solution.py:1326
  235.2 0.9 copy-done.4
  236.0 1.9 sum_late.1.late_refs_0_
  237.9 5.2 %collective-permute-done.24.part_refs_2_ = bf16[256,1024]{1,0:T(8,128)(2,1)} collective-permute-done((bf16[256,1024]{1,0:T(8,128)(2,1)}, bf16[256,1024]{1,0:T(8,128)(2,1)}, u32[]{:S(2)}, u32[]{:S(2)}) %collective-permute-start.24) | collective-permute-done | bytes 524320 | tf_op jit(solution)/shard_map/ppermute | solution.py:866
  243.2 1.8 collective-permute-start.25
  245.5 0.9 collective-permute-start.27
  246.3 4.1 %input_back.1 = f32[256,1024]{1,0:T(8,128)} custom-call(bf16[256,1024]{1,0:T(8,128)(2,1)} %collective-permute-done.22.part_refs_0_, bf16[256,1024]{1,0:T(8,128)(2,1)} %collective-permute-done.23.part_refs_1_, bf16[256,1024]{1,0:T(8,128)(2,1)} %collective-permute-done.24.part_refs_2_, bf16[256,1024]{1,0:T(8,128)(2,1)} %get-tuple-element.201.part_refs_3_, ...), custom_call_target="tpu_custom_call" | custom-call | tf_op jit(solution)/shard_map/input_back/pallas_call | solution.py:1302
  250.6 2.3 collective-permute-done.26.late_refs_2_
  253.0 2.3 collective-permute-done.27.late_refs_3_
  255.3 0.8 slice_bitcast_fusion.3
  258.0 0.6 multiply_subtract_fusion
  258.6 0.6 multiply_subtract_fusion.2
  259.3 0.7 multiply_subtract_fusion.3
  260.0 0.7 multiply_subtract_fusion.1
  260.7 8.3 %adam_in.1 = (f32[128,4352]{1,0:T(8,128)}, f32[128,4352]{1,0:T(8,128)}, f32[128,4352]{1,0:T(8,128)}) custom-call(s32[3]{0:T(128)} %pad_add_fusion.here_ref, f32[128,4352]{1,0:T(8,128)} %weight_ref.3, f32[128,4352]{1,0:T(8,128)} %first_ref.3, f32[128,4352]{1,0:T(8,128)} %second_ref.3, bf16[256,512]{1,0:T(8,128)(2,1)} %copy-done.5, ...), custom_call_target="tpu_custom_call" | custom-call | tf_op jit(solution)/shard_map/adam_in/pallas_call | solution.py:1352
  (149 shorter events, 7.5 us)
Async XLA Ops:
  1.2 9.9 %copy-start = (f32[1,256,1024]{2,1,0:T(8,128)S(1)}, f32[1,256,1024]{2,1,0:T(8,128)}, u32[]{:S(2)}) copy-start(f32[1,256,1024]{2,1,0:T(8,128)} %param.22) | copy-start | bytes 3145732
  1.2 11.5 %copy-start.3 = (f32[1,256,1024]{2,1,0:T(8,128)S(1)}, f32[1,256,1024]{2,1,0:T(8,128)}, u32[]{:S(2)}) copy-start(f32[1,256,1024]{2,1,0:T(8,128)} %param.24) | copy-start | bytes 3145732
  4.8 28.6 %all-to-all-start = ((bf16[4,144,768]{2,1,0:T(8,128)(2,1)}), bf16[4,144,768]{2,1,0:T(8,128)(2,1)}, u32[]{:S(2)}, u32[]{:S(2)}) async-start(bf16[4,144,768]{2,1,0:T(8,128)(2,1)} %get-tuple-element.117), calls=%async_computation | async-start | bytes 1769472 | tf_op jit(solution)/shard_map/all_to_all | solution.py:877
  11.1 59.7 %copy-start.33 = (f32[3,32]{1,0:T(4,128)S(1)}, f32[3,32]{1,0:T(4,128)}, u32[]{:S(2)}) copy-start(f32[3,32]{1,0:T(4,128)} %param.30) | copy-start | bytes 1156
  11.1 60.6 %copy-start.26 = (s32[1,1024]{1,0:T(1,128)S(1)}, s32[1,1024]{1,0:T(1,128)}, u32[]{:S(2)}) copy-start(s32[1,1024]{1,0:T(1,128)} %segr_ref.3) | copy-start | bytes 12292
  11.1 27.4 %collective-permute-start.1 = (f32[256,1024]{1,0:T(8,128)S(1)}, f32[256,1024]{1,0:T(8,128)}, u32[]{:S(2)}, u32[]{:S(2)}) collective-permute-start(f32[256,1024]{1,0:T(8,128)S(1)} %bitcast.46), channel_id=1, source_target_pairs={{0,2},{1,3},{2,0},{3,1},{4,6},{5,7},{6,4},{7,5},{8,10},{9,11},{10,... | collective-permute-start | bytes 3145736 | tf_op jit(solution)/shard_map/ppermute | solution.py:866
  12.8 79.0 %copy-start.6 = (bf16[256,1024]{1,0:T(8,128)(2,1)}, bf16[256,1024]{1,0:T(8,128)(2,1)S(1)}, u32[]{:S(2)}) copy-start(bf16[256,1024]{1,0:T(8,128)(2,1)S(1)} %bitcast_convert_fusion.cot_pieces_0_) | copy-start | bytes 1572868
  33.4 20.8 %collective-permute-start = (bf16[4,144,768]{2,1,0:T(8,128)(2,1)}, bf16[4,144,768]{2,1,0:T(8,128)(2,1)S(1)}, u32[]{:S(2)}, u32[]{:S(2)}) collective-permute-start(bf16[4,144,768]{2,1,0:T(8,128)(2,1)} %all-to-all-done.w1_pieces_0_), channel_id=1, source_target_pairs={{0,4},{4,0},{8,12},{12,8},{16,20},{20,16},{24,28},{28,24},{1,5},{5... | collective-permute-start | bytes 2654216 | tf_op jit(solution)/shard_map/ppermute | solution.py:866
  34.9 33.8 %all-to-all-start.1 = ((bf16[4,256,512]{2,1,0:T(8,128)(2,1)}), bf16[4,256,512]{2,1,0:T(8,128)(2,1)S(1)}, u32[]{:S(2)}, u32[]{:S(2)}) async-start(bf16[4,256,512]{2,1,0:T(8,128)(2,1)} %get-tuple-element.123), calls=%async_computation.1 | async-start | bytes 2097152 | tf_op jit(solution)/shard_map/all_to_all | solution.py:877
  38.5 17.3 %collective-permute-start.2 = (f32[256,1024]{1,0:T(8,128)S(1)}, f32[256,1024]{1,0:T(8,128)S(1)}, u32[]{:S(2)}, u32[]{:S(2)}) collective-permute-start(f32[256,1024]{1,0:T(8,128)S(1)} %bitcast.47), channel_id=1, source_target_pairs={{0,1},{1,0},{2,3},{3,2},{4,5},{5,4},{6,7},{7,6},{8,9},{9,8},{10,11... | collective-permute-start | bytes 3145736 | tf_op jit(solution)/shard_map/ppermute | solution.py:866
  54.3 19.1 %copy-start.14 = (bf16[4,144,768]{2,1,0:T(8,128)(2,1)}, bf16[4,144,768]{2,1,0:T(8,128)(2,1)S(1)}, u32[]{:S(2)}) copy-start(bf16[4,144,768]{2,1,0:T(8,128)(2,1)S(1)} %collective-permute-done.w1_pieces_1_) | copy-start | bytes 2654212
  54.3 14.5 %collective-permute-start.3 = (f32[256,1024]{1,0:T(8,128)}, f32[256,1024]{1,0:T(8,128)}, u32[]{:S(2)}, u32[]{:S(2)}) collective-permute-start(f32[256,1024]{1,0:T(8,128)} %collective-permute-done.1.tok_pieces_2_), channel_id=1, source_target_pairs={{0,1},{1,0},{2,3},{3,2},{4,5},{5,4},{6,7},{7,6},{8,9},{9,8},{10,11... | collective-permute-start | bytes 3145736 | tf_op jit(solution)/shard_map/ppermute | solution.py:866
  54.3 14.4 %collective-permute-start.4 = (bf16[256,1024]{1,0:T(8,128)(2,1)S(1)}, bf16[256,1024]{1,0:T(8,128)(2,1)}, u32[]{:S(2)}, u32[]{:S(2)}) collective-permute-start(bf16[256,1024]{1,0:T(8,128)(2,1)S(1)} %bitcast_convert_fusion.cot_pieces_0_), channel_id=1, source_target_pairs={{0,2},{1,3},{2,0},{3,1},{4,6},{5,7},{6,4},{7,5},{8,10},{9,11},{10,... | collective-permute-start | bytes 1572872 | tf_op jit(solution)/shard_map/ppermute | solution.py:866
  68.7 23.1 %copy-start.2 = (bf16[4,256,512]{2,1,0:T(8,128)(2,1)}, bf16[4,256,512]{2,1,0:T(8,128)(2,1)S(1)}, u32[]{:S(2)}) copy-start(bf16[4,256,512]{2,1,0:T(8,128)(2,1)S(1)} %all-to-all-done.1.g2_pieces_0_) | copy-start | bytes 3145732
  68.7 24.9 %collective-permute-start.5 = (bf16[4,256,512]{2,1,0:T(8,128)(2,1)S(1)}, bf16[4,256,512]{2,1,0:T(8,128)(2,1)S(1)}, u32[]{:S(2)}, u32[]{:S(2)}) collective-permute-start(bf16[4,256,512]{2,1,0:T(8,128)(2,1)S(1)} %all-to-all-done.1.g2_pieces_0_), channel_id=1, source_target_pairs={{0,4},{4,0},{8,12},{12,8},{16,20},{20,16},{24,28},{28,24},{1,5},{5... | collective-permute-start | bytes 3145736 | tf_op jit(solution)/shard_map/ppermute | solution.py:866
  70.3 21.5 %collective-permute-start.6 = (bf16[256,1024]{1,0:T(8,128)(2,1)S(1)}, bf16[256,1024]{1,0:T(8,128)(2,1)}, u32[]{:S(2)}, u32[]{:S(2)}) collective-permute-start(bf16[256,1024]{1,0:T(8,128)(2,1)S(1)} %bitcast_convert_fusion.cot_pieces_0_), channel_id=1, source_target_pairs={{0,1},{1,0},{2,3},{3,2},{4,5},{5,4},{6,7},{7,6},{8,9},{9,8},{10,11... | collective-permute-start | bytes 1572872 | tf_op jit(solution)/shard_map/ppermute | solution.py:866
  70.3 21.5 %collective-permute-start.7 = (bf16[256,1024]{1,0:T(8,128)(2,1)}, bf16[256,1024]{1,0:T(8,128)(2,1)}, u32[]{:S(2)}, u32[]{:S(2)}) collective-permute-start(bf16[256,1024]{1,0:T(8,128)(2,1)} %collective-permute-done.4.cot_pieces_2_), channel_id=1, source_target_pairs={{0,1},{1,0},{2,3},{3,2},{4,5},{5,4},{6,7},{7,6},{8,9},{9,8},{10,11... | collective-permute-start | bytes 1572872 | tf_op jit(solution)/shard_map/ppermute | solution.py:866
  94.6 13.0 %copy-start.42 = (s32[4]{0:T(128)S(1)}, s32[4]{0:T(128)}, u32[]{:S(2)}) copy-start(s32[4]{0:T(128)} %constant.15.clone) | copy-start | bytes 52
  105.4 3.9 %collective-permute-start.10 = (f32[8,1024]{1,0:T(8,128)}, f32[8,1024]{1,0:T(8,128)S(1)}, u32[]{:S(2)}, u32[]{:S(2)}) collective-permute-start(f32[8,1024]{1,0:T(8,128)} %get-tuple-element.139), channel_id=1, source_target_pairs={{0,3},{1,2},{2,1},{3,0},{4,7},{5,6},{6,5},{7,4},{8,11},{9,10},{10,... | collective-permute-start | bytes 98312 | tf_op jit(solution)/shard_map/ppermute | solution.py:866
  105.5 3.8 %collective-permute-start.8 = (f32[8,1024]{1,0:T(8,128)}, f32[8,1024]{1,0:T(8,128)S(1)}, u32[]{:S(2)}, u32[]{:S(2)}) collective-permute-start(f32[8,1024]{1,0:T(8,128)} %get-tuple-element.139), channel_id=1, source_target_pairs={{0,1},{1,0},{2,3},{3,2},{4,5},{5,4},{6,7},{7,6},{8,9},{9,8},{10,11... | collective-permute-start | bytes 98312 | tf_op jit(solution)/shard_map/ppermute | solution.py:866
  107.1 4.1 %collective-permute-start.9 = (f32[8,1024]{1,0:T(8,128)}, f32[8,1024]{1,0:T(8,128)S(1)}, u32[]{:S(2)}, u32[]{:S(2)}) collective-permute-start(f32[8,1024]{1,0:T(8,128)} %get-tuple-element.139), channel_id=1, source_target_pairs={{0,2},{1,3},{2,0},{3,1},{4,6},{5,7},{6,4},{7,5},{8,10},{9,11},{10,... | collective-permute-start | bytes 98312 | tf_op jit(solution)/shard_map/ppermute | solution.py:866
  125.9 48.9 %collective-permute-start.11 = (bf16[4,256,512]{2,1,0:T(8,128)(2,1)}, bf16[4,256,512]{2,1,0:T(8,128)(2,1)S(1)}, u32[]{:S(2)}, u32[]{:S(2)}) collective-permute-start(bf16[4,256,512]{2,1,0:T(8,128)(2,1)} %get-tuple-element.154), channel_id=1, source_target_pairs={{0,4},{4,0},{8,12},{12,8},{16,20},{20,16},{24,28},{28,24},{1,5},{5... | collective-permute-start | bytes 3145736 | tf_op jit(solution)/shard_map/ppermute | solution.py:866
  127.5 22.5 %copy-start.41 = (bf16[256,1024]{1,0:T(8,128)(2,1)S(1)}, bf16[256,1024]{1,0:T(8,128)(2,1)}, u32[]{:S(2)}) copy-start(bf16[256,1024]{1,0:T(8,128)(2,1)} %get-tuple-element.155) | copy-start | bytes 1572868
  127.5 23.0 %copy-start.40 = (bf16[256,1024]{1,0:T(8,128)(2,1)S(1)}, bf16[256,1024]{1,0:T(8,128)(2,1)}, u32[]{:S(2)}) copy-start(bf16[256,1024]{1,0:T(8,128)(2,1)} %get-tuple-element.156) | copy-start | bytes 1572868
  127.5 23.6 %copy-start.39 = (bf16[256,1024]{1,0:T(8,128)(2,1)S(1)}, bf16[256,1024]{1,0:T(8,128)(2,1)}, u32[]{:S(2)}) copy-start(bf16[256,1024]{1,0:T(8,128)(2,1)} %get-tuple-element.157) | copy-start | bytes 1572868
  149.9 25.7 %copy-start.9 = (bf16[4,256,512]{2,1,0:T(8,128)(2,1)S(1)}, bf16[4,256,512]{2,1,0:T(8,128)(2,1)}, u32[]{:S(2)}) copy-start(bf16[4,256,512]{2,1,0:T(8,128)(2,1)} %get-tuple-element.174) | copy-start | bytes 3145732
  149.9 2.2 collective-permute-start.15
  150.0 3.3 %collective-permute-start.12 = (bf16[256,1024]{1,0:T(8,128)(2,1)S(1)}, bf16[256,1024]{1,0:T(8,128)(2,1)S(1)}, u32[]{:S(2)}, u32[]{:S(2)}) collective-permute-start(bf16[256,1024]{1,0:T(8,128)(2,1)S(1)} %copy-done.41), channel_id=1, source_target_pairs={{0,1},{1,0},{2,3},{3,2},{4,5},{5,4},{6,7},{7,6},{8,9},{9,8},{10,11... | collective-permute-start | bytes 1572872 | tf_op jit(solution)/shard_map/ppermute | solution.py:866
  150.5 14.8 %collective-permute-start.13 = (bf16[256,1024]{1,0:T(8,128)(2,1)S(1)}, bf16[256,1024]{1,0:T(8,128)(2,1)S(1)}, u32[]{:S(2)}, u32[]{:S(2)}) collective-permute-start(bf16[256,1024]{1,0:T(8,128)(2,1)S(1)} %copy-done.40), channel_id=1, source_target_pairs={{0,2},{1,3},{2,0},{3,1},{4,6},{5,7},{6,4},{7,5},{8,10},{9,11},{10,... | collective-permute-start | bytes 1572872 | tf_op jit(solution)/shard_map/ppermute | solution.py:866
  151.0 23.8 %collective-permute-start.14 = (bf16[256,1024]{1,0:T(8,128)(2,1)S(1)}, bf16[256,1024]{1,0:T(8,128)(2,1)S(1)}, u32[]{:S(2)}, u32[]{:S(2)}) collective-permute-start(bf16[256,1024]{1,0:T(8,128)(2,1)S(1)} %copy-done.39), channel_id=1, source_target_pairs={{0,3},{1,2},{2,1},{3,0},{4,7},{5,6},{6,5},{7,4},{8,11},{9,10},{10,... | collective-permute-start | bytes 1572872 | tf_op jit(solution)/shard_map/ppermute | solution.py:866
  153.3 27.7 %copy-start.7 = (bf16[1024,256]{1,0:T(8,128)(2,1)}, bf16[1024,256]{1,0:T(8,128)(2,1)S(1)}, u32[]{:S(2)}) copy-start(bf16[1024,256]{1,0:T(8,128)(2,1)S(1)} %add_convert_fusion.1.dbc_ref) | copy-start | bytes 1572868
  153.3 21.5 %copy-start.17 = (bf16[256,1024]{1,0:T(8,128)(2,1)}, bf16[256,1024]{1,0:T(8,128)(2,1)S(1)}, u32[]{:S(2)}) copy-start(bf16[256,1024]{1,0:T(8,128)(2,1)S(1)} %collective-permute-done.12) | copy-start | bytes 1572868
  165.3 9.5 %copy-start.18 = (bf16[256,1024]{1,0:T(8,128)(2,1)}, bf16[256,1024]{1,0:T(8,128)(2,1)S(1)}, u32[]{:S(2)}) copy-start(bf16[256,1024]{1,0:T(8,128)(2,1)S(1)} %collective-permute-done.13) | copy-start | bytes 1572868
  176.9 34.5 %all-to-all-start.3 = ((bf16[4,256,512]{2,1,0:T(8,128)(2,1)}), bf16[4,256,512]{2,1,0:T(8,128)(2,1)S(1)}, u32[]{:S(2)}, u32[]{:S(2)}) async-start(bf16[4,256,512]{2,1,0:T(8,128)(2,1)} %add_convert_fusion), calls=%async_computation.3 | async-start | bytes 2097152 | tf_op jit(solution)/shard_map/all_to_all | solution.py:877
  180.4 14.6 %collective-permute-start.17 = (bf16[4,128,512]{2,1,0:T(8,128)(2,1)S(1)}, bf16[4,128,512]{2,1,0:T(8,128)(2,1)S(1)}, u32[]{:S(2)}, u32[]{:S(2)}) collective-permute-start(bf16[4,128,512]{2,1,0:T(8,128)(2,1)S(1)} %copy-done.38), channel_id=1, source_target_pairs={{0,4},{4,0},{8,12},{12,8},{16,20},{20,16},{24,28},{28,24},{1,5},{5... | collective-permute-start | bytes 1572872 | tf_op jit(solution)/shard_map/ppermute | solution.py:866
  181.0 14.3 %collective-permute-start.16 = (bf16[1024,256]{1,0:T(8,128)(2,1)S(1)}, bf16[1024,256]{1,0:T(8,128)(2,1)S(1)}, u32[]{:S(2)}, u32[]{:S(2)}) collective-permute-start(bf16[1024,256]{1,0:T(8,128)(2,1)S(1)} %add_convert_fusion.1.dbc_ref), channel_id=1, source_target_pairs={{0,2},{1,3},{2,0},{3,1},{4,6},{5,7},{6,4},{7,5},{8,10},{9,11},{10,... | collective-permute-start | bytes 1572872 | tf_op jit(solution)/shard_map/ppermute | solution.py:866
  195.0 13.3 %copy-start.16 = (bf16[4,128,512]{2,1,0:T(8,128)(2,1)}, bf16[4,128,512]{2,1,0:T(8,128)(2,1)S(1)}, u32[]{:S(2)}) copy-start(bf16[4,128,512]{2,1,0:T(8,128)(2,1)S(1)} %collective-permute-done.17.came_ref) | copy-start | bytes 1572868
  202.2 6.0 %collective-permute-start.18 = (bf16[160,512]{1,0:T(8,128)(2,1)}, bf16[160,512]{1,0:T(8,128)(2,1)S(1)}, u32[]{:S(2)}, u32[]{:S(2)}) collective-permute-start(bf16[160,512]{1,0:T(8,128)(2,1)} %get-tuple-element.182), channel_id=1, source_target_pairs={{0,4},{4,0},{8,12},{12,8},{16,20},{20,16},{24,28},{28,24},{1,5},{5... | collective-permute-start | bytes 491528 | tf_op jit(solution)/shard_map/ppermute | solution.py:866
  209.0 16.3 %copy-start.1 = (f32[1,256,1024]{2,1,0:T(8,128)S(1)}, f32[1,256,1024]{2,1,0:T(8,128)}, u32[]{:S(2)}) copy-start(f32[1,256,1024]{2,1,0:T(8,128)} %param.22) | copy-start | bytes 3145732
  211.4 23.8 %all-to-all-start.2 = ((bf16[4,192,512]{2,1,0:T(8,128)(2,1)}), bf16[4,192,512]{2,1,0:T(8,128)(2,1)S(1)}, u32[]{:S(2)}, u32[]{:S(2)}) async-start(bf16[4,192,512]{2,1,0:T(8,128)(2,1)} %pair_sum_late.1), calls=%async_computation.2 | async-start | bytes 1572864 | tf_op jit(solution)/shard_map/all_to_all | solution.py:877
  216.0 12.1 %copy-start.5 = (bf16[256,512]{1,0:T(8,128)(2,1)}, bf16[256,512]{1,0:T(8,128)(2,1)S(1)}, u32[]{:S(2)}) copy-start(bf16[256,512]{1,0:T(8,128)(2,1)S(1)} %reduce_sum.30.early_refs_0_) | copy-start | bytes 786436
  216.1 9.2 %collective-permute-start.20 = (bf16[256,512]{1,0:T(8,128)(2,1)S(1)}, bf16[256,512]{1,0:T(8,128)(2,1)S(1)}, u32[]{:S(2)}, u32[]{:S(2)}) collective-permute-start(bf16[256,512]{1,0:T(8,128)(2,1)S(1)} %reduce_sum.30.early_refs_0_), channel_id=1, source_target_pairs={{0,2},{1,3},{2,0},{3,1},{4,6},{5,7},{6,4},{7,5},{8,10},{9,11},{10,... | collective-permute-start | bytes 786440 | tf_op jit(solution)/shard_map/ppermute | solution.py:866
  216.6 21.3 %collective-permute-start.22 = (bf16[256,1024]{1,0:T(8,128)(2,1)}, bf16[256,1024]{1,0:T(8,128)(2,1)}, u32[]{:S(2)}, u32[]{:S(2)}) collective-permute-start(bf16[256,1024]{1,0:T(8,128)(2,1)} %get-tuple-element.193), channel_id=1, source_target_pairs={{0,1},{1,0},{2,3},{3,2},{4,5},{5,4},{6,7},{7,6},{8,9},{9,8},{10,11... | collective-permute-start | bytes 1572872 | tf_op jit(solution)/shard_map/ppermute | solution.py:866
  216.6 21.3 %collective-permute-start.23 = (bf16[256,1024]{1,0:T(8,128)(2,1)}, bf16[256,1024]{1,0:T(8,128)(2,1)}, u32[]{:S(2)}, u32[]{:S(2)}) collective-permute-start(bf16[256,1024]{1,0:T(8,128)(2,1)} %get-tuple-element.194), channel_id=1, source_target_pairs={{0,2},{1,3},{2,0},{3,1},{4,6},{5,7},{6,4},{7,5},{8,10},{9,11},{10,... | collective-permute-start | bytes 1572872 | tf_op jit(solution)/shard_map/ppermute | solution.py:866
  218.2 25.0 %collective-permute-start.24 = (bf16[256,1024]{1,0:T(8,128)(2,1)}, bf16[256,1024]{1,0:T(8,128)(2,1)}, u32[]{:S(2)}, u32[]{:S(2)}) collective-permute-start(bf16[256,1024]{1,0:T(8,128)(2,1)} %get-tuple-element.195), channel_id=1, source_target_pairs={{0,3},{1,2},{2,1},{3,0},{4,7},{5,6},{6,5},{7,4},{8,11},{9,10},{10,... | collective-permute-start | bytes 1572872 | tf_op jit(solution)/shard_map/ppermute | solution.py:866
  218.5 9.7 %collective-permute-start.19 = (bf16[256,512]{1,0:T(8,128)(2,1)S(1)}, bf16[256,512]{1,0:T(8,128)(2,1)S(1)}, u32[]{:S(2)}, u32[]{:S(2)}) collective-permute-start(bf16[256,512]{1,0:T(8,128)(2,1)S(1)} %reduce_sum.30.early_refs_0_), channel_id=1, source_target_pairs={{0,1},{1,0},{2,3},{3,2},{4,5},{5,4},{6,7},{7,6},{8,9},{9,8},{10,11... | collective-permute-start | bytes 786440 | tf_op jit(solution)/shard_map/ppermute | solution.py:866
  225.2 3.0 %collective-permute-start.21 = (bf16[256,512]{1,0:T(8,128)(2,1)S(1)}, bf16[256,512]{1,0:T(8,128)(2,1)S(1)}, u32[]{:S(2)}, u32[]{:S(2)}) collective-permute-start(bf16[256,512]{1,0:T(8,128)(2,1)S(1)} %collective-permute-done.20.early_refs_2_), channel_id=1, source_target_pairs={{0,1},{1,0},{2,3},{3,2},{4,5},{5,4},{6,7},{7,6},{8,9},{9,8},{10,11... | collective-permute-start | bytes 786440 | tf_op jit(solution)/shard_map/ppermute | solution.py:866
  243.2 7.4 %collective-permute-start.25 = (bf16[192,512]{1,0:T(8,128)(2,1)}, bf16[192,512]{1,0:T(8,128)(2,1)S(1)}, u32[]{:S(2)}, u32[]{:S(2)}) collective-permute-start(bf16[192,512]{1,0:T(8,128)(2,1)} %sum_late.1.late_refs_0_), channel_id=1, source_target_pairs={{0,1},{1,0},{2,3},{3,2},{4,5},{5,4},{6,7},{7,6},{8,9},{9,8},{10,11... | collective-permute-start | bytes 589832 | tf_op jit(solution)/shard_map/ppermute | solution.py:866
  245.0 8.0 %collective-permute-start.26 = (bf16[192,512]{1,0:T(8,128)(2,1)}, bf16[192,512]{1,0:T(8,128)(2,1)S(1)}, u32[]{:S(2)}, u32[]{:S(2)}) collective-permute-start(bf16[192,512]{1,0:T(8,128)(2,1)} %sum_late.1.late_refs_0_), channel_id=1, source_target_pairs={{0,2},{1,3},{2,0},{3,1},{4,6},{5,7},{6,4},{7,5},{8,10},{9,11},{10,... | collective-permute-start | bytes 589832 | tf_op jit(solution)/shard_map/ppermute | solution.py:866
  245.5 9.8 %collective-permute-start.27 = (bf16[192,512]{1,0:T(8,128)(2,1)}, bf16[192,512]{1,0:T(8,128)(2,1)S(1)}, u32[]{:S(2)}, u32[]{:S(2)}) collective-permute-start(bf16[192,512]{1,0:T(8,128)(2,1)} %sum_late.1.late_refs_0_), channel_id=1, source_target_pairs={{0,3},{1,2},{2,1},{3,0},{4,7},{5,6},{6,5},{7,4},{8,11},{9,10},{10,... | collective-permute-start | bytes 589832 | tf_op jit(solution)/shard_map/ppermute | solution.py:866
  250.5 7.5 %copy-start.24 = (f32[32,128]{1,0:T(8,128)S(1)}, f32[32,128]{1,0:T(8,128)}, u32[]{:S(2)}) copy-start(f32[32,128]{1,0:T(8,128)} %dt_ref.1) | copy-start | bytes 49156
  250.5 7.5 %copy-start.28 = (f32[32,128]{1,0:T(8,128)S(1)}, f32[32,128]{1,0:T(8,128)}, u32[]{:S(2)}) copy-start(f32[32,128]{1,0:T(8,128)} %param.33) | copy-start | bytes 49156
  250.5 7.5 %copy-start.29 = (f32[32,128]{1,0:T(8,128)S(1)}, f32[32,128]{1,0:T(8,128)}, u32[]{:S(2)}) copy-start(f32[32,128]{1,0:T(8,128)} %param.34) | copy-start | bytes 49156
  250.5 8.1 %copy-start.34 = (f32[3,32]{1,0:T(4,128)S(1)}, f32[3,32]{1,0:T(4,128)}, u32[]{:S(2)}) copy-start(f32[3,32]{1,0:T(4,128)} %param.41) | copy-start | bytes 1156
  250.5 8.1 %copy-start.35 = (f32[3,32]{1,0:T(4,128)S(1)}, f32[3,32]{1,0:T(4,128)}, u32[]{:S(2)}) copy-start(f32[3,32]{1,0:T(4,128)} %param.42) | copy-start | bytes 1156
  250.5 8.7 %copy-start.32 = (f32[384]{0:T(512)S(1)}, f32[384]{0:T(512)}, u32[]{:S(2)}) copy-start(f32[384]{0:T(512)} %gain_ref.1) | copy-start | bytes 4612
  250.5 8.7 %copy-start.36 = (f32[384]{0:T(512)S(1)}, f32[384]{0:T(512)}, u32[]{:S(2)}) copy-start(f32[384]{0:T(512)} %param.39) | copy-start | bytes 4612
  250.6 8.7 %copy-start.37 = (f32[384]{0:T(512)S(1)}, f32[384]{0:T(512)}, u32[]{:S(2)}) copy-start(f32[384]{0:T(512)} %param.40) | copy-start | bytes 4612
  250.6 9.4 %copy-start.25 = (f32[5,288]{1,0:T(8,128)S(1)}, f32[5,288]{1,0:T(8,128)}, u32[]{:S(2)}) copy-start(f32[5,288]{1,0:T(8,128)} %conv_ref.1) | copy-start | bytes 17284
  250.6 9.4 %copy-start.30 = (f32[5,288]{1,0:T(8,128)S(1)}, f32[5,288]{1,0:T(8,128)}, u32[]{:S(2)}) copy-start(f32[5,288]{1,0:T(8,128)} %param.37) | copy-start | bytes 17284
  250.6 9.4 %copy-start.31 = (f32[5,288]{1,0:T(8,128)S(1)}, f32[5,288]{1,0:T(8,128)}, u32[]{:S(2)}) copy-start(f32[5,288]{1,0:T(8,128)} %param.38) | copy-start | bytes 17284
  250.6 10.1 %copy-start.20 = (bf16[192,512]{1,0:T(8,128)(2,1)}, bf16[192,512]{1,0:T(8,128)(2,1)S(1)}, u32[]{:S(2)}) copy-start(bf16[192,512]{1,0:T(8,128)(2,1)S(1)} %collective-permute-done.25.late_refs_1_) | copy-start | bytes 589828
  253.0 7.7 %copy-start.21 = (bf16[192,512]{1,0:T(8,128)(2,1)}, bf16[192,512]{1,0:T(8,128)(2,1)S(1)}, u32[]{:S(2)}) copy-start(bf16[192,512]{1,0:T(8,128)(2,1)S(1)} %collective-permute-done.26.late_refs_2_) | copy-start | bytes 589828
  255.2 5.4 %copy-start.22 = (bf16[192,512]{1,0:T(8,128)(2,1)}, bf16[192,512]{1,0:T(8,128)(2,1)S(1)}, u32[]{:S(2)}) copy-start(bf16[192,512]{1,0:T(8,128)(2,1)S(1)} %collective-permute-done.27.late_refs_3_) | copy-start | bytes 589828
  (11 other events, 16.7 us)

commit v9 on v8

--- a/solution.py
+++ b/solution.py
@@ -146,6 +146,43 @@
         other = jnp.where(low, pltpu.roll(parts[0], HEAD_DIM, 1), parts[1])
         out.append(jnp.where(odd, other, even))
     return out
+
+
+def conv_back(size, width, grad, convsum_ref, convin_ref, conv_ref, ext_ref, seg, out_ref):
+    sums = [[jnp.zeros((1, 128), F32)] * (CONV + 1) for _ in range(0, width, 128)]
+    for first in range(0, size, 64):
+        here = slice(first, first + 64)
+        for strip, lane in enumerate(range(0, width, 128)):
+            lanes = slice(lane, lane + 128)
+            value = grad(here, lanes) * silu_grad(convsum_ref[here, lanes])
+            ext_ref[here, lanes] = value
+            sums[strip][CONV] = sums[strip][CONV] + jnp.sum(value, axis=0, keepdims=True)
+    for first in range(0, size, 64):
+        here = slice(first, first + 64)
+        ids = seg(first, 64)
+        same = [
+            jnp.broadcast_to(seg(first + CONV - 1 - tap, 64) == ids, (64, 128)) for tap in range(CONV - 1)
+        ]
+        for strip, lane in enumerate(range(0, width, 128)):
+            lanes = slice(lane, lane + 128)
+            conv_in = convin_ref[here, lanes].astype(F32)
+            back = jnp.zeros((64, 128), F32)
+            for tap in range(CONV):
+                at = first + CONV - 1 - tap
+                term = ext_ref[at : at + 64, lanes]
+                if tap < CONV - 1:
+                    term = jnp.where(same[tap], term, 0.0)
+                back = back + conv_ref[tap : tap + 1, lanes] * term
+                sums[strip][tap] = sums[strip][tap] + jnp.sum(conv_in * term, axis=0, keepdims=True)
+            out_ref[here, lanes] = back.astype(BF16)
+    row = lax.broadcasted_iota(jnp.int32, (8, 128), 0)
+    out = []
+    for strip in sums:
+        total = jnp.zeros((8, 128), F32)
+        for at, value in enumerate(strip):
+            total = jnp.where(row == at, value, total)
+        out.append(total)
+    return jnp.concatenate(out, axis=1)
 
 
 def pack_kernel(here_ref, win_ref, wout_ref, dt_ref, conv_ref, gain_ref, w1_ref, g2_ref, tmp_ref):
@@ -263,24 +300,31 @@
         for copy in tokens:
             copy.wait()
 
-    tok = tok_ref[step]
-    scale = lax.rsqrt(jnp.mean(tok * tok, axis=-1, keepdims=True) + NORM_EPS)
-    hid = (tok * scale * gpre_ref[...]).astype(BF16)
-    hid_ref[...] = hid
+    for first in range(0, span, 32):
+        tok = tok_ref[step, first : first + 32]
+        scale = lax.rsqrt(jnp.mean(tok * tok, axis=-1, keepdims=True) + NORM_EPS)
+        hid_ref[first : first + 32] = (tok * scale * gpre_ref[...]).astype(BF16)
+    hid = hid_ref[...]
     proj = nn(hid, w1_ref[...]).astype(BF16)
     convin_ref[...] = proj
     ext_ref[8 : 8 + span] = proj.astype(F32)
     seg_ref[...] = segc_ref[pl.ds(pl.multiple_of(step * span, 8), span + 8), :]
     seg_here = seg_ref[8 : 8 + span]
-    total = conv_ref[CONV : CONV + 1]
-    for tap in range(CONV):
-        at = 8 - (CONV - 1) + tap
-        same = seg_ref[at : at + span] == seg_here
-        total = total + conv_ref[tap : tap + 1] * jnp.where(same, ext_ref[at : at + span], 0.0)
+    for first in range(0, span, 64):
+        here = seg_ref[8 + first : 72 + first]
+        starts = [8 - (CONV - 1) + tap + first for tap in range(CONV)]
+        same = [jnp.broadcast_to(seg_ref[at : at + 64] == here, (64, 128)) for at in starts[:-1]]
+        for lane in range(0, convin_ref.shape[1], 128):
+            lanes = slice(lane, lane + 128)
+            total = conv_ref[CONV : CONV + 1, lanes]
+            for tap, at in enumerate(starts):
+                term = ext_ref[at : at + 64, lanes]
+                if tap < CONV - 1:
+                    term = jnp.where(same[tap], term, 0.0)
+                total = total + conv_ref[tap : tap + 1, lanes] * term
+            convsum_ref[first : first + 64, lanes] = total
+            mixed_ref[first : first + 64, lanes] = (total * sigmoid(total)).astype(BF16)
     ext_ref[0:8] = ext_ref[span : span + 8]
-    convsum_ref[...] = total
-    mixed = (total * sigmoid(total)).astype(BF16)
-    mixed_ref[...] = mixed
 
     raw_c = nt(hid, wdt_ref[...]) + hrow_ref[1:2]
     raw_r = nt(wdt_ref[...], hid) + hcol_ref[:, 1:2]
@@ -302,9 +346,9 @@
     state = state_ref[...]
     for block in range(span // SPAN):
         here = slice(block * SPAN, (block + 1) * SPAN)
-        values = mixed[here, :width]
-        write = mixed[here, width : width + STATE]
-        read = mixed[here, width + STATE :]
+        values = mixed_ref[here, :width]
+        write = mixed_ref[here, width : width + STATE]
+        read = mixed_ref[here, width + STATE :]
         seg = seg_here[here]
         log = log_c[here]
         log_row = log_r[:, here]
@@ -318,7 +362,8 @@
         keep = jnp.where(seg_last == seg_prev, jnp.exp(last), 0.0)
         start_ref[block] = state
         values_f = values.astype(F32)
-        base = spread(enter, width) * nn(read, state.astype(BF16)) + skip_w * values_f
+        enter_w = spread(enter, width)
+        inter = nn(read, state.astype(BF16))
         for pair in range(heads // 2):
             lanes = slice(pair * 2 * HEAD_DIM, (pair + 1) * 2 * HEAD_DIM)
             pieces = []
@@ -326,7 +371,8 @@
                 gap = jnp.minimum(log[:, head : head + 1] - log_row[head : head + 1], 0.0)
                 weights = scores * jnp.exp(gap) * step_row[head : head + 1]
                 pieces.append(nn(weights.astype(BF16), values[:, lanes]))
-            inner_ref[here, lanes] = base[:, lanes] + jnp.where(low, pieces[0], pieces[1])
+            base = enter_w[:, lanes] * inter[:, lanes] + skip_w[:, lanes] * values_f[:, lanes]
+            inner_ref[here, lanes] = base + jnp.where(low, pieces[0], pieces[1])
         moved = (spread(tail, width) * values_f).astype(BF16)
         keep_w = spread(keep + jnp.zeros((8, heads), F32), width)[0:1]
         state = keep_w * state + tn(write, moved)
@@ -379,15 +425,19 @@
             copy.wait()
         turned_ref[...] = wout_ref[...].T
 
-    gate = nn(hid_ref[...], wg_ref[...]).astype(BF16)
-    gate_ref[...] = gate
-    gate = gate.astype(F32)
-    grad = nn(cot_ref[step], turned_ref[...])
-    ng_ref[...] = grad
-    gated = inner_ref[...] * (gate * sigmoid(gate))
-    squares = jnp.sum(gated * gated, axis=1, keepdims=True)
-    crossed = jnp.sum(gated * (grad * gain_ref[...]), axis=1, keepdims=True)
-    same = diagonal(gated.shape[0])
+    gate_ref[...] = nn(hid_ref[...], wg_ref[...]).astype(BF16)
+    ng_ref[...] = nn(cot_ref[step], turned_ref[...])
+    span = gate_ref.shape[0]
+    squares, crossed = [], []
+    for first in range(0, span, 32):
+        here = slice(first, first + 32)
+        gate = gate_ref[here].astype(F32)
+        gated = inner_ref[here] * (gate * sigmoid(gate))
+        squares.append(jnp.sum(gated * gated, axis=1, keepdims=True))
+        crossed.append(jnp.sum(gated * (ng_ref[here] * gain_ref[...]), axis=1, keepdims=True))
+    squares = jnp.concatenate(squares, axis=0)
+    crossed = jnp.concatenate(crossed, axis=0)
+    same = diagonal(span)
     squares = jnp.sum(jnp.where(same, squares, 0.0), axis=0, keepdims=True)
     crossed = jnp.sum(jnp.where(same, crossed, 0.0), axis=0, keepdims=True)
     at = lax.broadcasted_iota(jnp.int32, stat_ref.shape, 0)
@@ -414,6 +464,7 @@
     sums_ref,
     outacc_ref,
     inacc_ref,
+    normed_ref,
 ):
     step = pl.program_id(0)
     span, width = inner_ref.shape
@@ -428,13 +479,25 @@
     squares = jnp.sum(jnp.where(same, stat_ref[0:1], 0.0), axis=1, keepdims=True)
     cross = jnp.sum(jnp.where(same, stat_ref[1:2], 0.0), axis=1, keepdims=True)
     inv = lax.rsqrt(squares * (1.0 / INNER) + NORM_EPS)
-    gate = gate_ref[...].astype(F32)
-    sig = sigmoid(gate)
-    silu = gate * sig
-    inner = inner_ref[...]
-    gated = inner * silu
-    unit = gated * inv
-    normed = (unit * gain_ref[...]).astype(BF16)
+    gain_sum = jnp.zeros((1, width), F32)
+    skip_sum = jnp.zeros((1, width), F32)
+    for first in range(0, span, 32):
+        here = slice(first, first + 32)
+        gate = gate_ref[here].astype(F32)
+        sig = sigmoid(gate)
+        silu = gate * sig
+        inner = inner_ref[here]
+        scale = inv[here]
+        unit = inner * silu * scale
+        normed_ref[here] = (unit * gain_ref[...]).astype(BF16)
+        grad = ng_ref[here]
+        dgated = scale * (grad * gain_ref[...] - unit * (cross[here] * scale * (1.0 / INNER)))
+        dy = dgated * silu
+        dy_ref[here] = dy
+        dgate_ref[here] = (dgated * inner * (sig * (1.0 + gate * (1.0 - sig)))).astype(BF16)
+        gain_sum = gain_sum + jnp.sum(grad * unit, axis=0, keepdims=True)
+        skip_sum = skip_sum + jnp.sum(dy * mixed_ref[here].astype(F32), axis=0, keepdims=True)
+    normed = normed_ref[...]
     cot = cot_ref[perm_ref[step]]
     block = nn(normed, wout_ref[...]).astype(BF16)
 
@@ -445,15 +508,7 @@
             block_ref[...] = block
 
     outacc_ref[...] += tn(normed, cot)
-    grad = ng_ref[...]
-    dgated = inv * (grad * gain_ref[...] - unit * (cross * inv * (1.0 / INNER)))
-    dy = dgated * silu
-    dy_ref[...] = dy
-    dgate = (dgated * inner * (sig * (1.0 + gate * (1.0 - sig)))).astype(BF16)
-    dgate_ref[...] = dgate
-    inacc_ref[...] += tn(hid_ref[...], dgate)
-    gain_sum = jnp.sum(grad * unit, axis=0, keepdims=True)
-    skip_sum = jnp.sum(dy * mixed_ref[...].astype(F32), axis=0, keepdims=True)
+    inacc_ref[...] += tn(hid_ref[...], dgate_ref[...])
     at = lax.broadcasted_iota(jnp.int32, (8, width), 0)
     sums_ref[...] += jnp.where(at == 0, gain_sum, jnp.where(at == 1, skip_sum, 0.0))
 
@@ -621,22 +676,19 @@
     at = lax.broadcasted_iota(jnp.int32, (8, heads), 0)
     headg_ref[...] += jnp.where(at == 0, rate_sum, jnp.where(at == 1, bias_sum, 0.0))
 
-    ext_ref[0:span] = dx_ref[...] * silu_grad(convsum_ref[...])
-    back = jnp.zeros((span, width), F32)
-    conv_in = convin_ref[...].astype(F32)
-    at = lax.broadcasted_iota(jnp.int32, (8, width), 0)
-    sums = jnp.where(at == CONV, jnp.sum(ext_ref[0:span], axis=0, keepdims=True), 0.0)
-    for tap in range(CONV):
-        ahead = CONV - 1 - tap
-        same = seg_ref[8 + ahead : 8 + ahead + span] == seg_here
-        term = jnp.where(same, ext_ref[ahead : ahead + span], 0.0)
-        back = back + conv_ref[tap : tap + 1] * term
-        sums = sums + jnp.where(at == tap, jnp.sum(conv_in * term, axis=0, keepdims=True), 0.0)
-    convg_ref[...] += sums
+    convg_ref[...] += conv_back(
+        span,
+        width,
+        lambda here, lanes: dx_ref[here, lanes],
+        convsum_ref,
+        convin_ref,
+        conv_ref,
+        ext_ref,
+        lambda first, count: seg_ref[8 + first : 8 + first + count],
+        dval_ref,
+    )
     ext_ref[span : span + 8] = ext_ref[0:8]
-    dval = back.astype(BF16)
-    dval_ref[...] = dval
-    inacc_ref[...] += tn(hid, dval)
+    inacc_ref[...] += tn(hid, dval_ref[...])
 
     @pl.when(step == pl.num_programs(0) - 1)
     def _():
@@ -676,8 +728,11 @@
         def _():
             out_ref[...] = total.astype(BF16)
 
-    unit = hid_ref[...].astype(F32) / gain_ref[...]
-    gsum_ref[...] += jnp.sum(total * unit, axis=0, keepdims=True) + jnp.zeros(gsum_ref.shape, F32)
+    gain_sum = jnp.zeros(gain_ref.shape, F32)
+    for first in range(0, total.shape[0], 32):
+        here = slice(first, first + 32)
+        gain_sum = gain_sum + jnp.sum(total[here] * hid_ref[here].astype(F32), axis=0, keepdims=True)
+    gsum_ref[...] += gain_sum / gain_ref[...] + jnp.zeros(gsum_ref.shape, F32)
 
 
 def maps_back_kernel(
@@ -705,21 +760,18 @@
     small_ref,
 ):
     size, width = dmap_ref.shape
-    total = dbc_ref[...].astype(F32) + dbcfar_ref[...].astype(F32)
-    ext_ref[0:size] = total * silu_grad(convsum_ref[...])
     ext_ref[size : size + 8] = jnp.zeros((8, width), F32)
-    back = jnp.zeros((size, width), F32)
-    conv_in = convin_ref[...].astype(F32)
-    at = lax.broadcasted_iota(jnp.int32, (8, width), 0)
-    sums = jnp.where(at == CONV, jnp.sum(ext_ref[0:size], axis=0, keepdims=True), 0.0)
-    seg_here = segc_ref[8 : 8 + size]
-    for tap in range(CONV):
-        ahead = CONV - 1 - tap
-        same = segc_ref[8 + ahead : 8 + ahead + size] == seg_here
-        term = jnp.where(same, ext_ref[ahead : ahead + size], 0.0)
-        back = back + conv_ref[tap : tap + 1] * term
-        sums = sums + jnp.where(at == tap, jnp.sum(conv_in * term, axis=0, keepdims=True), 0.0)
-    dmap_ref[...] = back.astype(BF16)
+    sums = conv_back(
+        size,
+        width,
+        lambda here, lanes: dbc_ref[here, lanes].astype(F32) + dbcfar_ref[here, lanes].astype(F32),
+        convsum_ref,
+        convin_ref,
+        conv_ref,
+        ext_ref,
+        lambda first, count: segc_ref[8 + first : 8 + first + count],
+        dmap_ref,
+    )
     ctx = here_ref[2]
     acc_ref[...] = tn(hid_ref[...], dmap_ref[...])
     span = own_ref.shape[0]
@@ -757,15 +809,17 @@
 
 
 def input_back_kernel(part_refs, own_ref, tok_ref, gain_ref, cot_ref, out_ref):
-    grad = own_ref[...]
-    for ref in part_refs:
-        grad = grad + ref[...].astype(F32)
-    tok = tok_ref[...]
-    scale = lax.rsqrt(jnp.mean(tok * tok, axis=-1, keepdims=True) + NORM_EPS)
-    unit = tok * scale
-    scaled = grad * gain_ref[...]
-    mean = jnp.mean(scaled * unit, axis=-1, keepdims=True)
-    out_ref[...] = cot_ref[...] + scale * (scaled - unit * mean)
+    for first in range(0, out_ref.shape[0], 32):
+        here = slice(first, first + 32)
+        grad = own_ref[here]
+        for ref in part_refs:
+            grad = grad + ref[here].astype(F32)
+        tok = tok_ref[here]
+        scale = lax.rsqrt(jnp.mean(tok * tok, axis=-1, keepdims=True) + NORM_EPS)
+        unit = tok * scale
+        scaled = grad * gain_ref[...]
+        mean = jnp.mean(scaled * unit, axis=-1, keepdims=True)
+        out_ref[here] = cot_ref[here] + scale * (scaled - unit * mean)
 
 
 def with_rest(value, first):
@@ -970,15 +1024,12 @@
         w1, g2, cot_low = lax.optimization_barrier((w1, g2, cot_low))
         w1_came = swap(w1, "dp", 1)
         g2 = high_all_to_all(g2)
-        cot_far = swap(cot_low, "ctx", 2)
         w1, w1_came, tok_far = lax.optimization_barrier((w1, w1_came, tok_far))
         toks = [tok, tok_core, tok_far, swap(tok_far, "ctx", 1)]
-        w1, w1_came, toks, g2, cot_far, cot_low = lax.optimization_barrier(
-            (w1, w1_came, toks, g2, cot_far, cot_low)
-        )
+        w1, w1_came, toks, g2, cot_low = lax.optimization_barrier((w1, w1_came, toks, g2, cot_low))
         w1 = [w1, w1_came]
         g2 = [g2, swap(g2, "dp", 1)]
-        cots = [cot_low, swap(cot_low, "ctx", 1), cot_far, swap(cot_far, "ctx", 1)]
+        cots = fan_ctx(cot_low)
         at_rows = at_g2 = jnp.stack([d & 1, 1 - (d & 1)]).astype(jnp.int32)
     else:
         w1 = [lax.all_gather(w1[0], "dp", axis=0)]
@@ -1128,7 +1179,11 @@
                 rows_at(width),
                 full((8, width)),
             ],
-            scratch_shapes=[pltpu.VMEM((width, model), F32), pltpu.VMEM((model, width), F32)],
+            scratch_shapes=[
+                pltpu.VMEM((width, model), F32),
+                pltpu.VMEM((model, width), F32),
+                pltpu.VMEM((span, width), BF16),
+            ],
         ),
         out_shape=[
             [shape_of(span, model, dtype=BF16)] * nctx,
@@ -1207,14 +1262,12 @@
     if near:
         late_came = swap(late_send, "dp", 1)
         early_came, blocks_out, dval = lax.optimization_barrier((early_came, blocks_out, dval))
+        early_parts = (early_keep.astype(F32) + early_came.astype(F32)).astype(BF16)
+        early_parts = high_all_to_all(early_parts)
     dbc = (dbc.astype(F32) + dbc_came.astype(F32)).astype(BF16)
-    if near:
-        early_came, dbc = lax.optimization_barrier((early_came, dbc))
-        early_parts = (early_keep.astype(F32) + early_came.astype(F32)).astype(BF16)
+    dval, dbc = lax.optimization_barrier((dval, dbc))
     dbc_far = swap(dbc, "ctx", 2)
     if near:
-        dval, early_parts = lax.optimization_barrier((dval, early_parts))
-        early_parts = high_all_to_all(early_parts)
         dbc_far, late_came = lax.optimization_barrier((dbc_far, late_came))
 
     hidden_out, gain_sum = pl.pallas_call(
@@ -1344,7 +1397,6 @@
             compiler_params=params(),
             name="sum_late",
         )(late_parts)
-        late, hidden_out = lax.optimization_barrier((late, hidden_out))
         late = fan_ctx(late)
         input_grad = input_part(hidden_out, hidden_own)
         late, input_grad = lax.optimization_barrier((late, input_grad))

time: 271 us -> 244 us (0.900)
  waiting for transfers between devices: 100 us -> 75.9 us
  starting transfers between devices: 38.8 us -> 35.8 us
    ppermute x28, waiting for transfers between devices: 79.8 us -> 46.2 us  [swap(): return lax.ppermute(value, axis, [(at, at ^ bit) for at in range(count)])]
    all_to_all x4, waiting for transfers between devices: 20.6 us -> 29.7 us  [high_all_to_all(): return lax.all_to_all(value, 'dp', 0, 0, axis_index_groups=groups)]
    ppermute x28, starting transfers between devices: 21 us -> 17.6 us  [swap(): return lax.ppermute(value, axis, [(at, at ^ bit) for at in range(count)])]
    unnamed x89 -> x83, local copies, waits for them, and re-layouts: 6.65 us -> 5.68 us
  transfers between devices with their start and end apart: 32 -> 32, of which waited for: 16 -> 15; matrix products, arithmetic and copies ran while one was open for 3% -> 3% of each run, Pallas kernels for 26% -> 29%
where the time goes in v9:
time: 244 us; the launch traced here: 241 us
  Pallas kernels  108 us (44%)
  waiting for transfers between devices  75.9 us (31%)
  starting transfers between devices  35.8 us (15%)
  other arithmetic  10.6 us (4%)
  local copies, waits for them, and re-layouts  10.1 us (4%)
    ppermute x28, waiting for transfers between devices, swap(): return lax.ppermute(value, axis, [(at, at ^ bit) for at in range(count)])  46.2 us
    all_to_all x4, waiting for transfers between devices, high_all_to_all(): return lax.all_to_all(value, 'dp', 0, 0, axis_index_groups=groups)  29.7 us
    pallas_call x1, Pallas kernels, shards(): pl.pallas_call(scan_back_kernel, grid_spec=pltpu.PrefetchScalarGridSpec(n...  22.9 us
    pallas_call x1, Pallas kernels, shards(): pl.pallas_call(scan_forward_kernel, grid_spec=pltpu.PrefetchScalarGridSpe...  18.8 us
    all_to_all x4, starting transfers between devices, high_all_to_all(): return lax.all_to_all(value, 'dp', 0, 0, axis_index_groups=groups)  18.2 us
    ppermute x28, starting transfers between devices, swap(): return lax.ppermute(value, axis, [(at, at ^ bit) for at in range(count)])  17.6 us
    pallas_call x1, Pallas kernels, shards(): pl.pallas_call(norm_back_kernel, grid_spec=pltpu.PrefetchScalarGridSpec(n...  13.8 us
    pallas_call x1, Pallas kernels, shards(): pl.pallas_call(gate_kernel, grid_spec=pltpu.PrefetchScalarGridSpec(num_sc...  10.9 us
  transfers between devices with their start and end apart: 32, of which 15 were waited for; matrix products, arithmetic and copies ran while one was open for 3% of the time, Pallas kernels for 29%

profile of v9, /device:TPU:0, one launch (start us, length us, event | category | flops | bytes accessed | tf_op | source)
XLA Modules:
  0.0 241.4 jit_solution(5190363585511546572)
XLA Ops:
  0.7 0.6 pad_add_fusion.here_ref
  1.3 3.6 %pack.1 = (bf16[4,144,768]{2,1,0:T(8,128)(2,1)}, bf16[4,256,512]{2,1,0:T(8,128)(2,1)}) custom-call(s32[3]{0:T(128)} %pad_add_fusion.here_ref, f32[128,4352]{1,0:T(8,128)} %weight_ref.3, f32[256,1024]{1,0:T(8,128)} %weight_ref.2, f32[32,128]{1,0:T(8,128)} %dt_ref.1, f32[5,288]{1,0:T(8,128)} %conv_ref.1, f32[384]{0:T(512)} %gain_ref.1), custom_call_target="tpu_custom_call" | custom-call | tf_op jit(solution)/shard_map/pack/pallas_call | solution.py:1008
  4.8 6.3 %all-to-all-start = ((bf16[4,144,768]{2,1,0:T(8,128)(2,1)}), bf16[4,144,768]{2,1,0:T(8,128)(2,1)}, u32[]{:S(2)}, u32[]{:S(2)}) async-start(bf16[4,144,768]{2,1,0:T(8,128)(2,1)} %get-tuple-element.109), calls=%async_computation | async-start | bytes 1769472 | tf_op jit(solution)/shard_map/all_to_all | solution.py:931
  11.2 1.6 collective-permute-start.1
  12.8 20.6 %all-to-all-done.w1_pieces_0_ = bf16[4,144,768]{2,1,0:T(8,128)(2,1)} async-done(((bf16[4,144,768]{2,1,0:T(8,128)(2,1)}), bf16[4,144,768]{2,1,0:T(8,128)(2,1)}, u32[]{:S(2)}, u32[]{:S(2)}) %all-to-all-start) | async-done | bytes 884768 | tf_op jit(solution)/shard_map/all_to_all | solution.py:931
  33.5 1.5 collective-permute-start
  35.0 3.5 %all-to-all-start.1 = ((bf16[4,256,512]{2,1,0:T(8,128)(2,1)}), bf16[4,256,512]{2,1,0:T(8,128)(2,1)S(1)}, u32[]{:S(2)}, u32[]{:S(2)}) async-start(bf16[4,256,512]{2,1,0:T(8,128)(2,1)} %get-tuple-element.115), calls=%async_computation.1 | async-start | bytes 2097152 | tf_op jit(solution)/shard_map/all_to_all | solution.py:931
  38.6 15.7 %collective-permute-done.w1_pieces_1_ = bf16[4,144,768]{2,1,0:T(8,128)(2,1)S(1)} collective-permute-done((bf16[4,144,768]{2,1,0:T(8,128)(2,1)}, bf16[4,144,768]{2,1,0:T(8,128)(2,1)S(1)}, u32[]{:S(2)}, u32[]{:S(2)}) %collective-permute-start) | collective-permute-done | bytes 884768 | tf_op jit(solution)/shard_map/ppermute | solution.py:920
  54.3 9.1 %all-to-all-done.1.g2_pieces_0_ = bf16[4,256,512]{2,1,0:T(8,128)(2,1)S(1)} async-done(((bf16[4,256,512]{2,1,0:T(8,128)(2,1)}), bf16[4,256,512]{2,1,0:T(8,128)(2,1)S(1)}, u32[]{:S(2)}, u32[]{:S(2)}) %all-to-all-start.1) | async-done | bytes 1048608 | tf_op jit(solution)/shard_map/all_to_all | solution.py:931
  63.4 0.5 collective-permute-start.4
  64.0 1.5 collective-permute-start.6
  66.1 0.7 copy.66
  66.8 1.0 broadcast_in_dim.13.segc_ref
  67.8 0.6 pad_add_fusion.1.at_ref
  68.4 18.8 %scan_forward.1 = (bf16[1024,1024]{1,0:T(8,128)(2,1)}, f32[8,768]{1,0:T(8,128)}, f32[1,1024]{1,0:T(1,128)}, f32[1,512]{1,0:T(1,128)}, bf16[8,1024]{1,0:T(8,128)(...) custom-call(s32[3]{0:T(128)} %pad_add_fusion.here_ref, ...), custom_call_target="tpu_custom_call" | custom-call | tf_op jit(solution)/shard_map/scan_forward/pallas_call | solution.py:1059
  87.2 2.0 collective-permute-done.7.cot_pieces_3_
  89.3 1.0 copy-done.8
  90.2 10.9 %gate.1 = (bf16[1024,512]{1,0:T(8,128)(2,1)}, bf16[512,1024]{1,0:T(8,128)(2,1)}, bf16[4,256,1024]{2,1,0:T(8,128)(2,1)}, bf16[1024,512]{1,0:T(8,128)(2,1)}, f32[1024,512]{1,0:T(8,128)}, /*index=5*/f32[8,1024]{1,0:T(8,128)}) custom-call(s32[3]{0:T(128)} %pad_add_fusion.here_ref, s32[2]{0:T(128)} %pad_add_fusion.1.at_ref, ...), custom_call_target="tpu_custom_call" | custom-call | tf_op jit(solution)/shard_map/gate/pallas_call | solution.py:1124
  101.1 1.4 collective-permute-start.10
  102.8 0.5 collective-permute-start.9
  103.3 0.5 broadcast_xor_fusion.perm_ref
  103.8 0.9 collective-permute-done.10
  104.7 2.2 collective-permute-done.9
  106.9 1.4 add_add_fusion.1.stat_ref
  108.3 13.8 %norm_back.1 = (bf16[256,1024]{1,0:T(8,128)(2,1)}, bf16[256,1024]{1,0:T(8,128)(2,1)}, bf16[256,1024]{1,0:T(8,128)(2,1)}, bf16[256,1024]{1,0:T(8,128)(2,1)}, bf16...) custom-call(s32[4]{0:T(128)} %broadcast_xor_fusion.perm_ref, ...), custom_call_target="tpu_custom_call" | custom-call | tf_op jit(solution)/shard_map/norm_back/pallas_call | solution.py:1158
  122.1 1.6 collective-permute-start.11
  124.1 1.4 collective-permute-start.14
  125.5 22.9 %scan_back.1 = (bf16[4,128,512]{2,1,0:T(8,128)(2,1)}, bf16[4,128,512]{2,1,0:T(8,128)(2,1)}, bf16[1024,512]{1,0:T(8,128)(2,1)}, bf16[1024,256]{1,0:T(8,128)(2,1)}...) custom-call(s32[4]{0:T(128)} %broadcast_xor_fusion.perm_ref, ...), custom_call_target="tpu_custom_call" | custom-call | tf_op jit(solution)/shard_map/scan_back/pallas_call | solution.py:1205
  148.5 0.5 collective-permute-done.14
  149.8 1.3 add_convert_fusion
  151.1 3.5 %all-to-all-start.3 = ((bf16[4,256,512]{2,1,0:T(8,128)(2,1)}), bf16[4,256,512]{2,1,0:T(8,128)(2,1)S(1)}, u32[]{:S(2)}, u32[]{:S(2)}) async-start(bf16[4,256,512]{2,1,0:T(8,128)(2,1)} %add_convert_fusion), calls=%async_computation.3 | async-start | bytes 2097152 | tf_op jit(solution)/shard_map/all_to_all | solution.py:931
  154.9 0.5 collective-permute-start.17
  155.4 1.2 collective-permute-done.15
  156.8 0.6 collective-permute-start.16
  157.3 9.0 %hidden_back.1 = (bf16[256,1024]{1,0:T(8,128)(2,1)}, bf16[256,1024]{1,0:T(8,128)(2,1)}, bf16[256,1024]{1,0:T(8,128)(2,1)}, bf16[256,1024]{1,0:T(8,128)(2,1)}, f32[8,1024]{1,0:T(8,128)}) custom-call(s32[4]{0:T(128)} %broadcast_xor_fusion.perm_ref, bf16[1024,512]{1,0:T(8,128)(2,1)} %get-tuple-element.163.dgate_ref, ...), custom_call_target="tpu_custom_call" | custom-call | tf_op jit(solution)/shard_map/hidden_back/pallas_call | solution.py:1273
  166.3 2.7 %collective-permute-done.17.came_ref = bf16[4,128,512]{2,1,0:T(8,128)(2,1)S(1)} collective-permute-done((bf16[4,128,512]{2,1,0:T(8,128)(2,1)S(1)}, bf16[4,128,512]{2,1,0:T(8,128)(2,1)S(1)}, u32[]{:S(2)}, u32[]{:S(2)}) %collective-permute-start.17) | collective-permute-done | bytes 524320 | tf_op jit(solution)/shard_map/ppermute | solution.py:920
  169.0 1.8 collective-permute-done.16.dbcfar_ref
  170.9 0.8 copy-done.15
  171.7 6.5 %maps_back.1 = (bf16[160,512]{1,0:T(8,128)(2,1)}, bf16[160,512]{1,0:T(8,128)(2,1)}, f32[256,1024]{1,0:T(8,128)}) custom-call(s32[3]{0:T(128)} %pad_add_fusion.here_ref, bf16[1024,256]{1,0:T(8,128)(2,1)} %copy-done.7, bf16[1024,256]{1,0:T(8,128)(2,1)} %copy-done.15, f32[1024,768]{1,0:T(8,128)} %get-tuple-element.136.convsum_ref, ...), custom_call_target="tpu_custom_call" | custom-call | tf_op jit(solution)/shard_map/maps_back/pallas_call | solution.py:1301
  178.1 0.5 collective-permute-start.18
  178.7 5.2 %collective-permute-done.18.mcame_ref = bf16[160,512]{1,0:T(8,128)(2,1)S(1)} collective-permute-done((bf16[160,512]{1,0:T(8,128)(2,1)}, bf16[160,512]{1,0:T(8,128)(2,1)S(1)}, u32[]{:S(2)}, u32[]{:S(2)}) %collective-permute-start.18) | collective-permute-done | bytes 163872 | tf_op jit(solution)/shard_map/ppermute | solution.py:920
  183.9 0.7 copy-done.23
  184.5 2.4 pair_sum_late.1
  186.9 4.8 %all-to-all-start.2 = ((bf16[4,192,512]{2,1,0:T(8,128)(2,1)}), bf16[4,192,512]{2,1,0:T(8,128)(2,1)S(1)}, u32[]{:S(2)}, u32[]{:S(2)}) async-start(bf16[4,192,512]{2,1,0:T(8,128)(2,1)} %pair_sum_late.1), calls=%async_computation.2 | async-start | bytes 1572864 | tf_op jit(solution)/shard_map/all_to_all | solution.py:931
  192.0 0.6 collective-permute-start.20
  192.6 1.5 collective-permute-start.26
  194.7 6.3 %collective-permute-done.20.early_refs_2_ = bf16[256,512]{1,0:T(8,128)(2,1)S(1)} collective-permute-done((bf16[256,512]{1,0:T(8,128)(2,1)S(1)}, bf16[256,512]{1,0:T(8,128)(2,1)S(1)}, u32[]{:S(2)}, u32[]{:S(2)}) %collective-permute-start.20) | collective-permute-done | bytes 262176 | tf_op jit(solution)/shard_map/ppermute | solution.py:920
  201.0 3.0 %add_add_fusion = f32[256,1024]{1,0:T(8,128)} fusion(bf16[256,1024]{1,0:T(8,128)(2,1)} %get-tuple-element.174, bf16[256,1024]{1,0:T(8,128)(2,1)} %copy-done.19, bf16[256,1024]{1,0:T(8,128)(2,1)} %copy-done.18, bf16[256,1024]{1,0:T(8,128)(2,1)} %copy-done.17, f32[1,256,1024]{2,1,0:T(8,128)S(1)} %copy-done.1), kind=kLoop, calls=%fused_computation.2 | loop fusion | flops 2097152 | bytes 4194304 | tf_op jit(solution)/shard_map/add | solution.py:1353
  204.0 0.7 copy-done.11
  204.7 0.7 copy-done.12
  205.4 5.5 %adam_out.1 = (f32[256,1024]{1,0:T(8,128)}, f32[256,1024]{1,0:T(8,128)}, f32[256,1024]{1,0:T(8,128)}) custom-call(s32[3]{0:T(128)} %pad_add_fusion.here_ref, f32[256,1024]{1,0:T(8,128)} %weight_ref.2, f32[256,1024]{1,0:T(8,128)} %first_ref.2, f32[256,1024]{1,0:T(8,128)} %second_ref.2, bf16[256,512]{1,0:T(8,128)(2,1)} %copy-done.5, ...), custom_call_target="tpu_custom_call" | custom-call | tf_op jit(solution)/shard_map/adam_out/pallas_call | solution.py:1379
  211.0 0.9 copy-done.4
  211.8 1.9 sum_late.1.late_refs_0_
  214.2 1.5 collective-permute-start.24
  215.6 4.9 %collective-permute-done.27.part_refs_2_ = bf16[256,1024]{1,0:T(8,128)(2,1)} collective-permute-done((bf16[256,1024]{1,0:T(8,128)(2,1)}, bf16[256,1024]{1,0:T(8,128)(2,1)}, u32[]{:S(2)}, u32[]{:S(2)}) %collective-permute-start.27) | collective-permute-done | bytes 524320 | tf_op jit(solution)/shard_map/ppermute | solution.py:920
  220.5 4.1 %input_back.1 = f32[256,1024]{1,0:T(8,128)} custom-call(bf16[256,1024]{1,0:T(8,128)(2,1)} %collective-permute-done.25.part_refs_0_, bf16[256,1024]{1,0:T(8,128)(2,1)} %collective-permute-done.26.part_refs_1_, bf16[256,1024]{1,0:T(8,128)(2,1)} %collective-permute-done.27.part_refs_2_, bf16[256,1024]{1,0:T(8,128)(2,1)} %get-tuple-element.185.part_refs_3_, ...), custom_call_target="tpu_custom_call" | custom-call | tf_op jit(solution)/shard_map/input_back/pallas_call | solution.py:1355
  224.8 2.4 %collective-permute-done.23.late_refs_2_ = bf16[192,512]{1,0:T(8,128)(2,1)S(1)} collective-permute-done((bf16[192,512]{1,0:T(8,128)(2,1)}, bf16[192,512]{1,0:T(8,128)(2,1)S(1)}, u32[]{:S(2)}, u32[]{:S(2)}) %collective-permute-start.23) | collective-permute-done | bytes 196640 | tf_op jit(solution)/shard_map/ppermute | solution.py:920
  227.5 0.8 slice_bitcast_fusion.3
  228.3 0.6 gather_fusion
  230.2 0.6 multiply_subtract_fusion
  230.9 0.6 multiply_subtract_fusion.2
  231.5 0.7 multiply_subtract_fusion.3
  232.2 0.7 multiply_subtract_fusion.1
  232.9 8.3 %adam_in.1 = (f32[128,4352]{1,0:T(8,128)}, f32[128,4352]{1,0:T(8,128)}, f32[128,4352]{1,0:T(8,128)}) custom-call(s32[3]{0:T(128)} %pad_add_fusion.here_ref, f32[128,4352]{1,0:T(8,128)} %weight_ref.3, f32[128,4352]{1,0:T(8,128)} %first_ref.3, f32[128,4352]{1,0:T(8,128)} %second_ref.3, bf16[256,512]{1,0:T(8,128)(2,1)} %copy-done.5, ...), custom_call_target="tpu_custom_call" | custom-call | tf_op jit(solution)/shard_map/adam_in/pallas_call | solution.py:1404
  (143 shorter events, 5.8 us)
Async XLA Ops:
  1.3 9.9 %copy-start = (f32[1,256,1024]{2,1,0:T(8,128)S(1)}, f32[1,256,1024]{2,1,0:T(8,128)}, u32[]{:S(2)}) copy-start(f32[1,256,1024]{2,1,0:T(8,128)} %param.22) | copy-start | bytes 3145732
  1.3 11.5 %copy-start.3 = (f32[1,256,1024]{2,1,0:T(8,128)S(1)}, f32[1,256,1024]{2,1,0:T(8,128)}, u32[]{:S(2)}) copy-start(f32[1,256,1024]{2,1,0:T(8,128)} %param.24) | copy-start | bytes 3145732
  4.8 28.6 %all-to-all-start = ((bf16[4,144,768]{2,1,0:T(8,128)(2,1)}), bf16[4,144,768]{2,1,0:T(8,128)(2,1)}, u32[]{:S(2)}, u32[]{:S(2)}) async-start(bf16[4,144,768]{2,1,0:T(8,128)(2,1)} %get-tuple-element.109), calls=%async_computation | async-start | bytes 1769472 | tf_op jit(solution)/shard_map/all_to_all | solution.py:931
  11.2 54.7 %copy-start.33 = (f32[3,32]{1,0:T(4,128)S(1)}, f32[3,32]{1,0:T(4,128)}, u32[]{:S(2)}) copy-start(f32[3,32]{1,0:T(4,128)} %param.30) | copy-start | bytes 1156
  11.2 55.6 %copy-start.26 = (s32[1,1024]{1,0:T(1,128)S(1)}, s32[1,1024]{1,0:T(1,128)}, u32[]{:S(2)}) copy-start(s32[1,1024]{1,0:T(1,128)} %segr_ref.3) | copy-start | bytes 12292
  11.2 27.4 %collective-permute-start.1 = (f32[256,1024]{1,0:T(8,128)S(1)}, f32[256,1024]{1,0:T(8,128)}, u32[]{:S(2)}, u32[]{:S(2)}) collective-permute-start(f32[256,1024]{1,0:T(8,128)S(1)} %bitcast.46), channel_id=1, source_target_pairs={{0,2},{1,3},{2,0},{3,1},{4,6},{5,7},{6,4},{7,5},{8,10},{9,11},{10,... | collective-permute-start | bytes 3145736 | tf_op jit(solution)/shard_map/ppermute | solution.py:920
  12.8 74.4 %copy-start.6 = (bf16[256,1024]{1,0:T(8,128)(2,1)}, bf16[256,1024]{1,0:T(8,128)(2,1)S(1)}, u32[]{:S(2)}) copy-start(bf16[256,1024]{1,0:T(8,128)(2,1)S(1)} %bitcast_convert_fusion.cot_pieces_0_) | copy-start | bytes 1572868
  33.5 20.8 %collective-permute-start = (bf16[4,144,768]{2,1,0:T(8,128)(2,1)}, bf16[4,144,768]{2,1,0:T(8,128)(2,1)S(1)}, u32[]{:S(2)}, u32[]{:S(2)}) collective-permute-start(bf16[4,144,768]{2,1,0:T(8,128)(2,1)} %all-to-all-done.w1_pieces_0_), channel_id=1, source_target_pairs={{0,4},{4,0},{8,12},{12,8},{16,20},{20,16},{24,28},{28,24},{1,5},{5... | collective-permute-start | bytes 2654216 | tf_op jit(solution)/shard_map/ppermute | solution.py:920
  35.0 28.4 %all-to-all-start.1 = ((bf16[4,256,512]{2,1,0:T(8,128)(2,1)}), bf16[4,256,512]{2,1,0:T(8,128)(2,1)S(1)}, u32[]{:S(2)}, u32[]{:S(2)}) async-start(bf16[4,256,512]{2,1,0:T(8,128)(2,1)} %get-tuple-element.115), calls=%async_computation.1 | async-start | bytes 2097152 | tf_op jit(solution)/shard_map/all_to_all | solution.py:931
  38.5 15.8 %collective-permute-start.2 = (f32[256,1024]{1,0:T(8,128)S(1)}, f32[256,1024]{1,0:T(8,128)}, u32[]{:S(2)}, u32[]{:S(2)}) collective-permute-start(f32[256,1024]{1,0:T(8,128)S(1)} %bitcast.47), channel_id=1, source_target_pairs={{0,1},{1,0},{2,3},{3,2},{4,5},{5,4},{6,7},{7,6},{8,9},{9,8},{10,11... | collective-permute-start | bytes 3145736 | tf_op jit(solution)/shard_map/ppermute | solution.py:920
  54.3 14.1 %copy-start.13 = (bf16[4,144,768]{2,1,0:T(8,128)(2,1)}, bf16[4,144,768]{2,1,0:T(8,128)(2,1)S(1)}, u32[]{:S(2)}) copy-start(bf16[4,144,768]{2,1,0:T(8,128)(2,1)S(1)} %collective-permute-done.w1_pieces_1_) | copy-start | bytes 2654212
  54.3 9.1 %collective-permute-start.3 = (f32[256,1024]{1,0:T(8,128)}, f32[256,1024]{1,0:T(8,128)}, u32[]{:S(2)}, u32[]{:S(2)}) collective-permute-start(f32[256,1024]{1,0:T(8,128)} %collective-permute-done.1.tok_pieces_2_), channel_id=1, source_target_pairs={{0,1},{1,0},{2,3},{3,2},{4,5},{5,4},{6,7},{7,6},{8,9},{9,8},{10,11... | collective-permute-start | bytes 3145736 | tf_op jit(solution)/shard_map/ppermute | solution.py:920
  63.4 23.8 %copy-start.2 = (bf16[4,256,512]{2,1,0:T(8,128)(2,1)}, bf16[4,256,512]{2,1,0:T(8,128)(2,1)S(1)}, u32[]{:S(2)}) copy-start(bf16[4,256,512]{2,1,0:T(8,128)(2,1)S(1)} %all-to-all-done.1.g2_pieces_0_) | copy-start | bytes 3145732
  63.4 25.8 %collective-permute-start.4 = (bf16[4,256,512]{2,1,0:T(8,128)(2,1)S(1)}, bf16[4,256,512]{2,1,0:T(8,128)(2,1)S(1)}, u32[]{:S(2)}, u32[]{:S(2)}) collective-permute-start(bf16[4,256,512]{2,1,0:T(8,128)(2,1)S(1)} %all-to-all-done.1.g2_pieces_0_), channel_id=1, source_target_pairs={{0,4},{4,0},{8,12},{12,8},{16,20},{20,16},{24,28},{28,24},{1,5},{5... | collective-permute-start | bytes 3145736 | tf_op jit(solution)/shard_map/ppermute | solution.py:920
  64.0 23.3 %collective-permute-start.5 = (bf16[256,1024]{1,0:T(8,128)(2,1)S(1)}, bf16[256,1024]{1,0:T(8,128)(2,1)}, u32[]{:S(2)}, u32[]{:S(2)}) collective-permute-start(bf16[256,1024]{1,0:T(8,128)(2,1)S(1)} %bitcast_convert_fusion.cot_pieces_0_), channel_id=1, source_target_pairs={{0,1},{1,0},{2,3},{3,2},{4,5},{5,4},{6,7},{7,6},{8,9},{9,8},{10,11... | collective-permute-start | bytes 1572872 | tf_op jit(solution)/shard_map/ppermute | solution.py:920
  64.0 23.3 %collective-permute-start.6 = (bf16[256,1024]{1,0:T(8,128)(2,1)S(1)}, bf16[256,1024]{1,0:T(8,128)(2,1)}, u32[]{:S(2)}, u32[]{:S(2)}) collective-permute-start(bf16[256,1024]{1,0:T(8,128)(2,1)S(1)} %bitcast_convert_fusion.cot_pieces_0_), channel_id=1, source_target_pairs={{0,2},{1,3},{2,0},{3,1},{4,6},{5,7},{6,4},{7,5},{8,10},{9,11},{10,... | collective-permute-start | bytes 1572872 | tf_op jit(solution)/shard_map/ppermute | solution.py:920
  65.5 23.8 %collective-permute-start.7 = (bf16[256,1024]{1,0:T(8,128)(2,1)S(1)}, bf16[256,1024]{1,0:T(8,128)(2,1)}, u32[]{:S(2)}, u32[]{:S(2)}) collective-permute-start(bf16[256,1024]{1,0:T(8,128)(2,1)S(1)} %bitcast_convert_fusion.cot_pieces_0_), channel_id=1, source_target_pairs={{0,3},{1,2},{2,1},{3,0},{4,7},{5,6},{6,5},{7,4},{8,11},{9,10},{10,... | collective-permute-start | bytes 1572872 | tf_op jit(solution)/shard_map/ppermute | solution.py:920
  66.1 2.4 copy-start.27
  89.3 1.0 copy-start.8
  90.2 13.1 %copy-start.39 = (s32[4]{0:T(128)S(1)}, s32[4]{0:T(128)}, u32[]{:S(2)}) copy-start(s32[4]{0:T(128)} %constant.15.clone) | copy-start | bytes 52
  101.1 3.6 %collective-permute-start.10 = (f32[8,1024]{1,0:T(8,128)}, f32[8,1024]{1,0:T(8,128)S(1)}, u32[]{:S(2)}, u32[]{:S(2)}) collective-permute-start(f32[8,1024]{1,0:T(8,128)} %get-tuple-element.130), channel_id=1, source_target_pairs={{0,3},{1,2},{2,1},{3,0},{4,7},{5,6},{6,5},{7,4},{8,11},{9,10},{10,... | collective-permute-start | bytes 98312 | tf_op jit(solution)/shard_map/ppermute | solution.py:920
  102.5 2.2 collective-permute-start.8
  102.8 4.1 %collective-permute-start.9 = (f32[8,1024]{1,0:T(8,128)}, f32[8,1024]{1,0:T(8,128)S(1)}, u32[]{:S(2)}, u32[]{:S(2)}) collective-permute-start(f32[8,1024]{1,0:T(8,128)} %get-tuple-element.130), channel_id=1, source_target_pairs={{0,2},{1,3},{2,0},{3,1},{4,6},{5,7},{6,4},{7,5},{8,10},{9,11},{10,... | collective-permute-start | bytes 98312 | tf_op jit(solution)/shard_map/ppermute | solution.py:920
  122.1 27.0 %collective-permute-start.11 = (bf16[4,256,512]{2,1,0:T(8,128)(2,1)}, bf16[4,256,512]{2,1,0:T(8,128)(2,1)S(1)}, u32[]{:S(2)}, u32[]{:S(2)}) collective-permute-start(bf16[4,256,512]{2,1,0:T(8,128)(2,1)} %get-tuple-element.145), channel_id=1, source_target_pairs={{0,4},{4,0},{8,12},{12,8},{16,20},{20,16},{24,28},{28,24},{1,5},{5... | collective-permute-start | bytes 3145736 | tf_op jit(solution)/shard_map/ppermute | solution.py:920
  123.6 24.8 %collective-permute-start.12 = (bf16[256,1024]{1,0:T(8,128)(2,1)}, bf16[256,1024]{1,0:T(8,128)(2,1)S(1)}, u32[]{:S(2)}, u32[]{:S(2)}) collective-permute-start(bf16[256,1024]{1,0:T(8,128)(2,1)} %get-tuple-element.146), channel_id=1, source_target_pairs={{0,1},{1,0},{2,3},{3,2},{4,5},{5,4},{6,7},{7,6},{8,9},{9,8},{10,11... | collective-permute-start | bytes 1572872 | tf_op jit(solution)/shard_map/ppermute | solution.py:920
  123.6 24.8 %collective-permute-start.13 = (bf16[256,1024]{1,0:T(8,128)(2,1)}, bf16[256,1024]{1,0:T(8,128)(2,1)S(1)}, u32[]{:S(2)}, u32[]{:S(2)}) collective-permute-start(bf16[256,1024]{1,0:T(8,128)(2,1)} %get-tuple-element.147), channel_id=1, source_target_pairs={{0,2},{1,3},{2,0},{3,1},{4,6},{5,7},{6,4},{7,5},{8,10},{9,11},{10,... | collective-permute-start | bytes 1572872 | tf_op jit(solution)/shard_map/ppermute | solution.py:920
  124.1 24.9 %collective-permute-start.14 = (bf16[256,1024]{1,0:T(8,128)(2,1)}, bf16[256,1024]{1,0:T(8,128)(2,1)S(1)}, u32[]{:S(2)}, u32[]{:S(2)}) collective-permute-start(bf16[256,1024]{1,0:T(8,128)(2,1)} %get-tuple-element.148), channel_id=1, source_target_pairs={{0,3},{1,2},{2,1},{3,0},{4,7},{5,6},{6,5},{7,4},{8,11},{9,10},{10,... | collective-permute-start | bytes 1572872 | tf_op jit(solution)/shard_map/ppermute | solution.py:920
  125.5 24.3 %copy-start.9 = (bf16[4,256,512]{2,1,0:T(8,128)(2,1)S(1)}, bf16[4,256,512]{2,1,0:T(8,128)(2,1)}, u32[]{:S(2)}) copy-start(bf16[4,256,512]{2,1,0:T(8,128)(2,1)} %get-tuple-element.175) | copy-start | bytes 3145732
  149.8 4.8 %copy-start.14 = (bf16[1024,256]{1,0:T(8,128)(2,1)S(1)}, bf16[1024,256]{1,0:T(8,128)(2,1)}, u32[]{:S(2)}) copy-start(bf16[1024,256]{1,0:T(8,128)(2,1)} %get-tuple-element.152) | copy-start | bytes 1572868
  149.8 5.1 %copy-start.38 = (bf16[4,128,512]{2,1,0:T(8,128)(2,1)S(1)}, bf16[4,128,512]{2,1,0:T(8,128)(2,1)}, u32[]{:S(2)}) copy-start(bf16[4,128,512]{2,1,0:T(8,128)(2,1)} %get-tuple-element.154) | copy-start | bytes 1572868
  151.1 35.8 %all-to-all-start.3 = ((bf16[4,256,512]{2,1,0:T(8,128)(2,1)}), bf16[4,256,512]{2,1,0:T(8,128)(2,1)S(1)}, u32[]{:S(2)}, u32[]{:S(2)}) async-start(bf16[4,256,512]{2,1,0:T(8,128)(2,1)} %add_convert_fusion), calls=%async_computation.3 | async-start | bytes 2097152 | tf_op jit(solution)/shard_map/all_to_all | solution.py:931
  154.6 2.0 collective-permute-start.15
  154.9 14.1 %collective-permute-start.17 = (bf16[4,128,512]{2,1,0:T(8,128)(2,1)S(1)}, bf16[4,128,512]{2,1,0:T(8,128)(2,1)S(1)}, u32[]{:S(2)}, u32[]{:S(2)}) collective-permute-start(bf16[4,128,512]{2,1,0:T(8,128)(2,1)S(1)} %copy-done.38), channel_id=1, source_target_pairs={{0,4},{4,0},{8,12},{12,8},{16,20},{20,16},{24,28},{28,24},{1,5},{5... | collective-permute-start | bytes 1572872 | tf_op jit(solution)/shard_map/ppermute | solution.py:920
  156.7 9.5 %copy-start.7 = (bf16[1024,256]{1,0:T(8,128)(2,1)}, bf16[1024,256]{1,0:T(8,128)(2,1)S(1)}, u32[]{:S(2)}) copy-start(bf16[1024,256]{1,0:T(8,128)(2,1)S(1)} %add_convert_fusion.1.dbc_ref) | copy-start | bytes 1572868
  156.8 14.1 %collective-permute-start.16 = (bf16[1024,256]{1,0:T(8,128)(2,1)S(1)}, bf16[1024,256]{1,0:T(8,128)(2,1)S(1)}, u32[]{:S(2)}, u32[]{:S(2)}) collective-permute-start(bf16[1024,256]{1,0:T(8,128)(2,1)S(1)} %add_convert_fusion.1.dbc_ref), channel_id=1, source_target_pairs={{0,2},{1,3},{2,0},{3,1},{4,6},{5,7},{6,4},{7,5},{8,10},{9,11},{10,... | collective-permute-start | bytes 1572872 | tf_op jit(solution)/shard_map/ppermute | solution.py:920
  169.0 14.8 %copy-start.16 = (bf16[4,128,512]{2,1,0:T(8,128)(2,1)}, bf16[4,128,512]{2,1,0:T(8,128)(2,1)S(1)}, u32[]{:S(2)}) copy-start(bf16[4,128,512]{2,1,0:T(8,128)(2,1)S(1)} %collective-permute-done.17.came_ref) | copy-start | bytes 1572868
  178.1 5.7 %collective-permute-start.18 = (bf16[160,512]{1,0:T(8,128)(2,1)}, bf16[160,512]{1,0:T(8,128)(2,1)S(1)}, u32[]{:S(2)}, u32[]{:S(2)}) collective-permute-start(bf16[160,512]{1,0:T(8,128)(2,1)} %get-tuple-element.170), channel_id=1, source_target_pairs={{0,4},{4,0},{8,12},{12,8},{16,20},{20,16},{24,28},{28,24},{1,5},{5... | collective-permute-start | bytes 491528 | tf_op jit(solution)/shard_map/ppermute | solution.py:920
  184.5 16.5 %copy-start.1 = (f32[1,256,1024]{2,1,0:T(8,128)S(1)}, f32[1,256,1024]{2,1,0:T(8,128)}, u32[]{:S(2)}) copy-start(f32[1,256,1024]{2,1,0:T(8,128)} %param.22) | copy-start | bytes 3145732
  186.9 24.0 %all-to-all-start.2 = ((bf16[4,192,512]{2,1,0:T(8,128)(2,1)}), bf16[4,192,512]{2,1,0:T(8,128)(2,1)S(1)}, u32[]{:S(2)}, u32[]{:S(2)}) async-start(bf16[4,192,512]{2,1,0:T(8,128)(2,1)} %pair_sum_late.1), calls=%async_computation.2 | async-start | bytes 1572864 | tf_op jit(solution)/shard_map/all_to_all | solution.py:931
  192.0 12.0 %copy-start.5 = (bf16[256,512]{1,0:T(8,128)(2,1)}, bf16[256,512]{1,0:T(8,128)(2,1)S(1)}, u32[]{:S(2)}) copy-start(bf16[256,512]{1,0:T(8,128)(2,1)S(1)} %reduce_sum.30.early_refs_0_) | copy-start | bytes 786436
  192.0 9.0 %collective-permute-start.20 = (bf16[256,512]{1,0:T(8,128)(2,1)S(1)}, bf16[256,512]{1,0:T(8,128)(2,1)S(1)}, u32[]{:S(2)}, u32[]{:S(2)}) collective-permute-start(bf16[256,512]{1,0:T(8,128)(2,1)S(1)} %reduce_sum.30.early_refs_0_), channel_id=1, source_target_pairs={{0,2},{1,3},{2,0},{3,1},{4,6},{5,7},{6,4},{7,5},{8,10},{9,11},{10,... | collective-permute-start | bytes 786440 | tf_op jit(solution)/shard_map/ppermute | solution.py:920
  192.6 21.6 %collective-permute-start.25 = (bf16[256,1024]{1,0:T(8,128)(2,1)}, bf16[256,1024]{1,0:T(8,128)(2,1)}, u32[]{:S(2)}, u32[]{:S(2)}) collective-permute-start(bf16[256,1024]{1,0:T(8,128)(2,1)} %get-tuple-element.182), channel_id=1, source_target_pairs={{0,1},{1,0},{2,3},{3,2},{4,5},{5,4},{6,7},{7,6},{8,9},{9,8},{10,11... | collective-permute-start | bytes 1572872 | tf_op jit(solution)/shard_map/ppermute | solution.py:920
  192.6 23.0 %collective-permute-start.26 = (bf16[256,1024]{1,0:T(8,128)(2,1)}, bf16[256,1024]{1,0:T(8,128)(2,1)}, u32[]{:S(2)}, u32[]{:S(2)}) collective-permute-start(bf16[256,1024]{1,0:T(8,128)(2,1)} %get-tuple-element.183), channel_id=1, source_target_pairs={{0,2},{1,3},{2,0},{3,1},{4,6},{5,7},{6,4},{7,5},{8,10},{9,11},{10,... | collective-permute-start | bytes 1572872 | tf_op jit(solution)/shard_map/ppermute | solution.py:920
  194.1 26.4 %collective-permute-start.27 = (bf16[256,1024]{1,0:T(8,128)(2,1)}, bf16[256,1024]{1,0:T(8,128)(2,1)}, u32[]{:S(2)}, u32[]{:S(2)}) collective-permute-start(bf16[256,1024]{1,0:T(8,128)(2,1)} %get-tuple-element.184), channel_id=1, source_target_pairs={{0,3},{1,2},{2,1},{3,0},{4,7},{5,6},{6,5},{7,4},{8,11},{9,10},{10,... | collective-permute-start | bytes 1572872 | tf_op jit(solution)/shard_map/ppermute | solution.py:920
  194.4 9.6 %collective-permute-start.19 = (bf16[256,512]{1,0:T(8,128)(2,1)S(1)}, bf16[256,512]{1,0:T(8,128)(2,1)S(1)}, u32[]{:S(2)}, u32[]{:S(2)}) collective-permute-start(bf16[256,512]{1,0:T(8,128)(2,1)S(1)} %reduce_sum.30.early_refs_0_), channel_id=1, source_target_pairs={{0,1},{1,0},{2,3},{3,2},{4,5},{5,4},{6,7},{7,6},{8,9},{9,8},{10,11... | collective-permute-start | bytes 786440 | tf_op jit(solution)/shard_map/ppermute | solution.py:920
  201.0 3.0 %copy-start.10 = (bf16[256,512]{1,0:T(8,128)(2,1)}, bf16[256,512]{1,0:T(8,128)(2,1)S(1)}, u32[]{:S(2)}) copy-start(bf16[256,512]{1,0:T(8,128)(2,1)S(1)} %collective-permute-done.20.early_refs_2_) | copy-start | bytes 786436
  201.0 3.0 %collective-permute-start.21 = (bf16[256,512]{1,0:T(8,128)(2,1)S(1)}, bf16[256,512]{1,0:T(8,128)(2,1)S(1)}, u32[]{:S(2)}, u32[]{:S(2)}) collective-permute-start(bf16[256,512]{1,0:T(8,128)(2,1)S(1)} %collective-permute-done.20.early_refs_2_), channel_id=1, source_target_pairs={{0,1},{1,0},{2,3},{3,2},{4,5},{5,4},{6,7},{7,6},{8,9},{9,8},{10,11... | collective-permute-start | bytes 786440 | tf_op jit(solution)/shard_map/ppermute | solution.py:920
  213.7 11.0 %collective-permute-start.22 = (bf16[192,512]{1,0:T(8,128)(2,1)}, bf16[192,512]{1,0:T(8,128)(2,1)S(1)}, u32[]{:S(2)}, u32[]{:S(2)}) collective-permute-start(bf16[192,512]{1,0:T(8,128)(2,1)} %sum_late.1.late_refs_0_), channel_id=1, source_target_pairs={{0,1},{1,0},{2,3},{3,2},{4,5},{5,4},{6,7},{7,6},{8,9},{9,8},{10,11... | collective-permute-start | bytes 589832 | tf_op jit(solution)/shard_map/ppermute | solution.py:920
  214.1 13.1 %collective-permute-start.23 = (bf16[192,512]{1,0:T(8,128)(2,1)}, bf16[192,512]{1,0:T(8,128)(2,1)S(1)}, u32[]{:S(2)}, u32[]{:S(2)}) collective-permute-start(bf16[192,512]{1,0:T(8,128)(2,1)} %sum_late.1.late_refs_0_), channel_id=1, source_target_pairs={{0,2},{1,3},{2,0},{3,1},{4,6},{5,7},{6,4},{7,5},{8,10},{9,11},{10,... | collective-permute-start | bytes 589832 | tf_op jit(solution)/shard_map/ppermute | solution.py:920
  214.2 13.3 %collective-permute-start.24 = (bf16[192,512]{1,0:T(8,128)(2,1)}, bf16[192,512]{1,0:T(8,128)(2,1)S(1)}, u32[]{:S(2)}, u32[]{:S(2)}) collective-permute-start(bf16[192,512]{1,0:T(8,128)(2,1)} %sum_late.1.late_refs_0_), channel_id=1, source_target_pairs={{0,3},{1,2},{2,1},{3,0},{4,7},{5,6},{6,5},{7,4},{8,11},{9,10},{10,... | collective-permute-start | bytes 589832 | tf_op jit(solution)/shard_map/ppermute | solution.py:920
  224.7 5.5 %copy-start.24 = (f32[32,128]{1,0:T(8,128)S(1)}, f32[32,128]{1,0:T(8,128)}, u32[]{:S(2)}) copy-start(f32[32,128]{1,0:T(8,128)} %dt_ref.1) | copy-start | bytes 49156
  224.7 5.5 %copy-start.28 = (f32[32,128]{1,0:T(8,128)S(1)}, f32[32,128]{1,0:T(8,128)}, u32[]{:S(2)}) copy-start(f32[32,128]{1,0:T(8,128)} %param.33) | copy-start | bytes 49156
  224.7 5.5 %copy-start.29 = (f32[32,128]{1,0:T(8,128)S(1)}, f32[32,128]{1,0:T(8,128)}, u32[]{:S(2)}) copy-start(f32[32,128]{1,0:T(8,128)} %param.34) | copy-start | bytes 49156
  224.7 6.2 %copy-start.34 = (f32[3,32]{1,0:T(4,128)S(1)}, f32[3,32]{1,0:T(4,128)}, u32[]{:S(2)}) copy-start(f32[3,32]{1,0:T(4,128)} %param.41) | copy-start | bytes 1156
  224.7 6.2 %copy-start.35 = (f32[3,32]{1,0:T(4,128)S(1)}, f32[3,32]{1,0:T(4,128)}, u32[]{:S(2)}) copy-start(f32[3,32]{1,0:T(4,128)} %param.42) | copy-start | bytes 1156
  224.7 6.8 %copy-start.32 = (f32[384]{0:T(512)S(1)}, f32[384]{0:T(512)}, u32[]{:S(2)}) copy-start(f32[384]{0:T(512)} %gain_ref.1) | copy-start | bytes 4612
  224.7 6.8 %copy-start.36 = (f32[384]{0:T(512)S(1)}, f32[384]{0:T(512)}, u32[]{:S(2)}) copy-start(f32[384]{0:T(512)} %param.39) | copy-start | bytes 4612
  224.7 6.8 %copy-start.37 = (f32[384]{0:T(512)S(1)}, f32[384]{0:T(512)}, u32[]{:S(2)}) copy-start(f32[384]{0:T(512)} %param.40) | copy-start | bytes 4612
  224.7 7.4 %copy-start.25 = (f32[5,288]{1,0:T(8,128)S(1)}, f32[5,288]{1,0:T(8,128)}, u32[]{:S(2)}) copy-start(f32[5,288]{1,0:T(8,128)} %conv_ref.1) | copy-start | bytes 17284
  224.8 7.4 %copy-start.30 = (f32[5,288]{1,0:T(8,128)S(1)}, f32[5,288]{1,0:T(8,128)}, u32[]{:S(2)}) copy-start(f32[5,288]{1,0:T(8,128)} %param.37) | copy-start | bytes 17284
  224.8 7.4 %copy-start.31 = (f32[5,288]{1,0:T(8,128)S(1)}, f32[5,288]{1,0:T(8,128)}, u32[]{:S(2)}) copy-start(f32[5,288]{1,0:T(8,128)} %param.38) | copy-start | bytes 17284
  224.8 8.1 %copy-start.20 = (bf16[192,512]{1,0:T(8,128)(2,1)}, bf16[192,512]{1,0:T(8,128)(2,1)S(1)}, u32[]{:S(2)}) copy-start(bf16[192,512]{1,0:T(8,128)(2,1)S(1)} %collective-permute-done.22.late_refs_1_) | copy-start | bytes 589828
  227.2 5.7 %copy-start.21 = (bf16[192,512]{1,0:T(8,128)(2,1)}, bf16[192,512]{1,0:T(8,128)(2,1)S(1)}, u32[]{:S(2)}) copy-start(bf16[192,512]{1,0:T(8,128)(2,1)S(1)} %collective-permute-done.23.late_refs_2_) | copy-start | bytes 589828
  227.5 5.4 %copy-start.22 = (bf16[192,512]{1,0:T(8,128)(2,1)}, bf16[192,512]{1,0:T(8,128)(2,1)S(1)}, u32[]{:S(2)}) copy-start(bf16[192,512]{1,0:T(8,128)(2,1)S(1)} %collective-permute-done.24.late_refs_3_) | copy-start | bytes 589828
  (8 other events, 6.3 us)

commit v10 on v9

--- a/solution.py
+++ b/solution.py
@@ -185,7 +185,7 @@
     return jnp.concatenate(out, axis=1)
 
 
-def pack_kernel(here_ref, win_ref, wout_ref, dt_ref, conv_ref, gain_ref, w1_ref, g2_ref, tmp_ref):
+def pack_kernel(near, here_ref, win_ref, wout_ref, dt_ref, conv_ref, gain_ref, w1_ref, wg_ref, wo_ref, tmp_ref):
     ctx = here_ref[2]
     rows = win_ref.shape[0]
     heads = HEADS // 4
@@ -207,17 +207,15 @@
     tmp_ref[8 + CONV + 1 : 8 + CONV + 2, 0 : gain_ref.shape[0]] = gain_ref[...].reshape(1, -1)
     for copy in copies:
         w1_ref[copy, rows : rows + 16, :] = tmp_ref[...].astype(BF16)
-    copies = range(g2_ref.shape[0])
     for at, part in enumerate(pick_heads(win_ref, 0, ctx, heads)):
         part = part.astype(BF16)
         for copy in copies:
-            g2_ref[copy, 0:rows, at * 128 : (at + 1) * 128] = part
-    if g2_ref.shape[1] > rows:
-        some = wout_ref.shape[0] // 4
-        mine = wout_ref[pl.ds(pl.multiple_of(ctx * some, 8), some), :].astype(BF16)
+            wg_ref[copy, :, at * 128 : (at + 1) * 128] = part
+    if near:
+        mine = wout_ref[pl.ds(pl.multiple_of(ctx * HEAD_DIM, 8), HEAD_DIM), :].astype(BF16)
         for copy in copies:
-            g2_ref[copy, rows : rows + some] = mine[:, :width]
-            g2_ref[copy, rows + some : rows + 2 * some] = mine[:, width:]
+            wo_ref[copy, :HEAD_DIM] = mine[:, :width]
+            wo_ref[copy, HEAD_DIM:] = mine[:, width:]
 
 
 def scan_forward_kernel(
@@ -379,18 +377,43 @@
     state_ref[...] = state
 
 
-def gate_kernel(
+def row_stats(columns, at, stat_ref, before):
+    value = jnp.concatenate(columns, axis=0)
+    value = jnp.sum(jnp.where(diagonal(value.shape[0]), value, 0.0), axis=0, keepdims=True)
+    row = lax.broadcasted_iota(jnp.int32, stat_ref.shape, 0)
+    stat_ref[...] = jnp.where(row == at, value, before)
+
+
+def gate_kernel(at_ref, hid_ref, wg_pieces, inner_ref, wg_ref, gate_ref, stat_ref, sems):
+    rows = wg_pieces[0].shape[1]
+
+    @pl.when(pl.program_id(0) == 0)
+    def _():
+        copies = place(wg_pieces, at_ref, len(wg_pieces), sems, [(0, rows, rows_of(wg_ref, rows))])
+        for copy in copies:
+            copy.wait()
+
+    gate_ref[...] = nn(hid_ref[...], wg_ref[...]).astype(BF16)
+    squares = []
+    for first in range(0, gate_ref.shape[0], 32):
+        here = slice(first, first + 32)
+        gate = gate_ref[here].astype(F32)
+        gated = inner_ref[here] * (gate * sigmoid(gate))
+        squares.append(jnp.sum(gated * gated, axis=1, keepdims=True))
+    row_stats(squares, 0, stat_ref, 0.0)
+
+
+def normed_grad_kernel(
     here_ref,
     at_ref,
-    hid_ref,
-    g2_pieces,
+    wo_pieces,
     cot_pieces,
     inner_ref,
+    gate_ref,
+    before_ref,
     gain_ref,
-    wg_ref,
     wout_ref,
     cot_ref,
-    gate_ref,
     ng_ref,
     stat_ref,
     turned_ref,
@@ -398,21 +421,19 @@
     cot_sems,
 ):
     step = pl.program_id(0)
-    rows = wg_ref.shape[0] // (wout_ref.shape[0] // HEAD_DIM)
-    width = wg_ref.shape[1]
+    width = ng_ref.shape[1]
 
     @pl.when(step == 0)
     def _():
         some = rows_of(wout_ref, HEAD_DIM)
         copies = place(
-            g2_pieces,
+            wo_pieces,
             at_ref,
-            len(g2_pieces),
+            len(wo_pieces),
             sems,
             [
-                (0, rows, rows_of(wg_ref, rows)),
-                (rows, HEAD_DIM, lambda at: some(at).at[:, 0:width]),
-                (rows + HEAD_DIM, HEAD_DIM, lambda at: some(at).at[:, width : 2 * width]),
+                (0, HEAD_DIM, lambda at: some(at).at[:, 0:width]),
+                (HEAD_DIM, HEAD_DIM, lambda at: some(at).at[:, width : 2 * width]),
             ],
         )
         cots = [
@@ -425,23 +446,14 @@
             copy.wait()
         turned_ref[...] = wout_ref[...].T
 
-    gate_ref[...] = nn(hid_ref[...], wg_ref[...]).astype(BF16)
     ng_ref[...] = nn(cot_ref[step], turned_ref[...])
-    span = gate_ref.shape[0]
-    squares, crossed = [], []
-    for first in range(0, span, 32):
+    crossed = []
+    for first in range(0, ng_ref.shape[0], 32):
         here = slice(first, first + 32)
         gate = gate_ref[here].astype(F32)
         gated = inner_ref[here] * (gate * sigmoid(gate))
-        squares.append(jnp.sum(gated * gated, axis=1, keepdims=True))
         crossed.append(jnp.sum(gated * (ng_ref[here] * gain_ref[...]), axis=1, keepdims=True))
-    squares = jnp.concatenate(squares, axis=0)
-    crossed = jnp.concatenate(crossed, axis=0)
-    same = diagonal(span)
-    squares = jnp.sum(jnp.where(same, squares, 0.0), axis=0, keepdims=True)
-    crossed = jnp.sum(jnp.where(same, crossed, 0.0), axis=0, keepdims=True)
-    at = lax.broadcasted_iota(jnp.int32, stat_ref.shape, 0)
-    stat_ref[...] = jnp.where(at == 0, squares, crossed)
+    row_stats(crossed, 1, stat_ref, before_ref[...])
 
 
 def norm_back_kernel(
@@ -451,7 +463,7 @@
     inner_ref,
     gate_ref,
     ng_ref,
-    stat_ref,
+    stat_refs,
     gain_ref,
     mixed_ref,
     wout_ref,
@@ -476,8 +488,9 @@
         sums_ref[...] = jnp.zeros_like(sums_ref)
 
     same = diagonal(span)
-    squares = jnp.sum(jnp.where(same, stat_ref[0:1], 0.0), axis=1, keepdims=True)
-    cross = jnp.sum(jnp.where(same, stat_ref[1:2], 0.0), axis=1, keepdims=True)
+    stats = sum(ref[...] for ref in stat_refs)
+    squares = jnp.sum(jnp.where(same, stats[0:1], 0.0), axis=1, keepdims=True)
+    cross = jnp.sum(jnp.where(same, stats[1:2], 0.0), axis=1, keepdims=True)
     inv = lax.rsqrt(squares * (1.0 / INNER) + NORM_EPS)
     gain_sum = jnp.zeros((1, width), F32)
     skip_sum = jnp.zeros((1, width), F32)
@@ -1005,47 +1018,50 @@
     vmem = pl.BlockSpec(memory_space=pltpu.VMEM)
     anywhere = lambda pieces: [pl.BlockSpec(memory_space=pl.ANY)] * len(pieces)
 
-    w1, g2 = pl.pallas_call(
-        pack_kernel,
+    w1, wg, wo = pl.pallas_call(
+        functools.partial(pack_kernel, near),
         in_specs=[smem] + [vmem] * 5,
         out_shape=[
             shape_of(high if near else 1, rows_in + 16, wide, dtype=BF16),
-            shape_of(high if near else 1, rows_in + (2 * HEAD_DIM if near else 0), width, dtype=BF16),
+            shape_of(high if near else 1, rows_in, width, dtype=BF16),
+            shape_of(high if near else 1, 2 * HEAD_DIM, width, dtype=BF16),
         ],
         scratch_shapes=[pltpu.VMEM((16, wide), F32)],
         compiler_params=params(),
         name="pack",
     )(bits, in_weight, out_weight, dt_weight, conv_params, gains)
+    ids = segment_ids[0]
+    seg_col = jnp.pad(ids, (8, 8), constant_values=-1)[:, None]
+    seg_row = segment_ids
+    head_mine = lax.dynamic_index_in_dim(head_params.reshape(3, heads, nctx), c, 2, False)
+    head_col = head_mine.T
     cot_low = cotangent[0].astype(BF16)
     if near:
         tok_far = swap(tok, "ctx", 2)
         tok_core = swap(tok, "ctx", 1)
         w1 = high_all_to_all(w1)
-        w1, g2, cot_low = lax.optimization_barrier((w1, g2, cot_low))
+        at_rows = jnp.stack([d & 1, 1 - (d & 1)]).astype(jnp.int32)
+        w1, wg, wo, cot_low, seg_col, head_mine, head_col, at_rows, perm = lax.optimization_barrier(
+            (w1, wg, wo, cot_low, seg_col, head_mine, head_col, at_rows, perm)
+        )
         w1_came = swap(w1, "dp", 1)
-        g2 = high_all_to_all(g2)
+        wg = high_all_to_all(wg)
+        wo = high_all_to_all(wo)
         w1, w1_came, tok_far = lax.optimization_barrier((w1, w1_came, tok_far))
         toks = [tok, tok_core, tok_far, swap(tok_far, "ctx", 1)]
-        w1, w1_came, toks, g2, cot_low = lax.optimization_barrier((w1, w1_came, toks, g2, cot_low))
+        w1, w1_came, toks, wg, cot_low = lax.optimization_barrier((w1, w1_came, toks, wg, cot_low))
         w1 = [w1, w1_came]
-        g2 = [g2, swap(g2, "dp", 1)]
+        wg = [wg, swap(wg, "dp", 1)]
         cots = fan_ctx(cot_low)
-        at_rows = at_g2 = jnp.stack([d & 1, 1 - (d & 1)]).astype(jnp.int32)
     else:
         w1 = [lax.all_gather(w1[0], "dp", axis=0)]
         toks = gather_ctx(tok)
         cots = gather_ctx(cot_low)
-        wg = lax.all_gather(g2[0], "dp", axis=0, tiled=True).reshape(heads, block_in, width)
-        wout = lax.all_gather(out_weight.astype(BF16), "dp", axis=0, tiled=True)
-        wout = lax.dynamic_index_in_dim(wout.reshape(heads, nctx, HEAD_DIM, model), c, 1, False)
-        g2 = [jnp.concatenate([wg, wout[:, :, :width], wout[:, :, width:]], axis=1)]
-        at_rows = at_g2 = jnp.zeros((1,), jnp.int32)
-
-    ids = segment_ids[0]
-    seg_col = jnp.pad(ids, (8, 8), constant_values=-1)[:, None]
-    seg_row = segment_ids
-    head_mine = lax.dynamic_index_in_dim(head_params.reshape(3, heads, nctx), c, 2, False)
-    head_col = head_mine.T
+        wg = [lax.all_gather(wg[0], "dp", axis=0, tiled=True).reshape(heads, block_in, width)]
+        wo = lax.all_gather(out_weight.astype(BF16), "dp", axis=0, tiled=True)
+        wo = lax.dynamic_index_in_dim(wo.reshape(heads, nctx, HEAD_DIM, model), c, 1, False)
+        wo = [jnp.concatenate([wo[:, :, :width], wo[:, :, width:]], axis=1)]
+        at_rows = jnp.zeros((1,), jnp.int32)
 
     rows = lambda cols: pl.BlockSpec((span, cols), lambda i, *_: (i, 0))
     row_of = pl.BlockSpec((heads, span), lambda i, *_: (0, i))
@@ -1121,38 +1137,64 @@
         name="scan_forward",
     )(bits, at_rows, toks, w1, head_mine, head_col, seg_col, seg_row)
 
-    wg, wout, cot_all, gate, normed_grad, stats = pl.pallas_call(
+    if near:
+        wo, hid, cots = lax.optimization_barrier((wo, hid, cots))
+        wo = [wo, swap(wo, "dp", 1)]
+    stat_block = pl.BlockSpec((8, span), lambda i, *_: (0, i))
+    wg, gate, squares = pl.pallas_call(
         gate_kernel,
+        grid_spec=pltpu.PrefetchScalarGridSpec(
+            num_scalar_prefetch=1,
+            grid=(chunks,),
+            in_specs=[rows(model), anywhere(wg), rows(width)],
+            out_specs=[full((model, width)), rows(width), stat_block],
+            scratch_shapes=[pltpu.SemaphoreType.DMA((copies_of(wg, 1),))],
+        ),
+        out_shape=[
+            shape_of(model, width, dtype=BF16),
+            shape_of(length, width, dtype=BF16),
+            shape_of(8, length),
+        ],
+        compiler_params=params("arbitrary"),
+        name="gate",
+    )(at_rows, hid, wg, inner)
+    if near:
+        squares, wo = lax.optimization_barrier((squares, wo))
+    wout, cot_all, normed_grad, stats = pl.pallas_call(
+        normed_grad_kernel,
         grid_spec=pltpu.PrefetchScalarGridSpec(
             num_scalar_prefetch=2,
             grid=(chunks,),
-            in_specs=[rows(model), anywhere(g2), anywhere(cots), rows(width), full((1, width))],
+            in_specs=[
+                anywhere(wo),
+                anywhere(cots),
+                rows(width),
+                rows(width),
+                stat_block,
+                full((1, width)),
+            ],
             out_specs=[
-                full((model, width)),
                 full((width, model)),
                 full((nctx, span, model)),
                 rows(width),
-                rows(width),
-                pl.BlockSpec((8, span), lambda i, *_: (0, i)),
+                stat_block,
             ],
             scratch_shapes=[
                 pltpu.VMEM((model, width), BF16),
-                pltpu.SemaphoreType.DMA((copies_of(g2, 3),)),
+                pltpu.SemaphoreType.DMA((copies_of(wo, 2),)),
                 pltpu.SemaphoreType.DMA((nctx,)),
             ],
         ),
         out_shape=[
-            shape_of(model, width, dtype=BF16),
             shape_of(width, model, dtype=BF16),
             shape_of(nctx, span, model, dtype=BF16),
-            shape_of(length, width, dtype=BF16),
             shape_of(length, width),
             shape_of(8, length),
         ],
         compiler_params=params("arbitrary"),
-        name="gate",
-    )(bits, at_g2, hid, g2, cots, inner, gain_mine)
-    stats = sum(fan_ctx(stats))
+        name="normed_grad",
+    )(bits, at_rows, wo, cots, inner, gate, squares, gain_mine)
+    stats = fan_ctx(stats)
 
     early_rows = block_in + 2 * HEAD_DIM
     blocks_out, early_keep, early_send, dy, dgate, col_sums = pl.pallas_call(
@@ -1165,7 +1207,7 @@
                 rows_at(width),
                 rows_at(width),
                 rows_at(width),
-                pl.BlockSpec((8, span), lambda i, p, *_: (0, p[i])),
+                [pl.BlockSpec((8, span), lambda i, p, *_: (0, p[i]))] * nctx,
                 full((1, width)),
                 rows_at(width),
                 full((width, model)),
@@ -1267,8 +1309,6 @@
     dbc = (dbc.astype(F32) + dbc_came.astype(F32)).astype(BF16)
     dval, dbc = lax.optimization_barrier((dval, dbc))
     dbc_far = swap(dbc, "ctx", 2)
-    if near:
-        dbc_far, late_came = lax.optimization_barrier((dbc_far, late_came))
 
     hidden_out, gain_sum = pl.pallas_call(
         hidden_back_kernel,
@@ -1362,7 +1402,9 @@
 
     late_rows = block_in + 64
     if near:
+        early = jnp.sum(early_parts.astype(F32), axis=0).astype(BF16)
         map_came = swap(map_send, "dp", 1)
+        map_came, block_output, early = lax.optimization_barrier((map_came, block_output, early))
         late_parts = pl.pallas_call(
             pair_sum_late_kernel,
             out_shape=shape_of(high, late_rows, width, dtype=BF16),
@@ -1370,7 +1412,6 @@
             name="pair_sum_late",
         )(late_keep, late_came, map_keep, map_came)
         late_parts = high_all_to_all(late_parts)
-        early = jnp.sum(early_parts.astype(F32), axis=0).astype(BF16)
         early = gather_ctx(early)
         row_block = lambda ref_rows, cols: pl.BlockSpec((ref_rows, cols), lambda i, *_: (i, 0))
         out_block = row_block(out_weight.shape[0] // nctx, model)
@@ -1390,7 +1431,7 @@
             name="adam_out",
         )(bits, out_weight, out_first, out_second, early)
 
-        late_parts, block_output, out_new = lax.optimization_barrier((late_parts, block_output, out_new))
+        late_parts, out_new = lax.optimization_barrier((late_parts, out_new))
         late = pl.pallas_call(
             sum_late_kernel,
             out_shape=shape_of(late_rows, width, dtype=BF16),

time: 244 us -> 267 us (1.094)
  blocking collectives: 0 us -> 18.9 us
  Pallas kernels: 108 us -> 113 us
  starting transfers between devices: 35.8 us -> 40.5 us
  waiting for transfers between devices: 75.9 us -> 71.4 us
  other arithmetic: 10.6 us -> 7.68 us
    all_to_all x0 -> x1, blocking collectives: none -> 18.9 us  [high_all_to_all(): return lax.all_to_all(value, 'dp', 0, 0, axis_index_groups=groups)]
    pallas_call x1 -> x2, Pallas kernels: 3.58 us -> 12.2 us  [the longest x1 8.6 us: shards(): pl.pallas_call(normed_grad_kernel, grid_spec=pltpu.PrefetchScalarGridSpec...]
    all_to_all x4, waiting for transfers between devices: 29.7 us -> 22.8 us  [high_all_to_all(): return lax.all_to_all(value, 'dp', 0, 0, axis_index_groups=groups)]
    pallas_call x1, Pallas kernels: 10.9 us -> 7.54 us  [shards(): pl.pallas_call(gate_kernel, grid_spec=pltpu.PrefetchScalarGridSpec(num_sc...]
    ppermute x28 -> x29, starting transfers between devices: 17.6 us -> 20.8 us  [swap(): return lax.ppermute(value, axis, [(at, at ^ bit) for at in range(count)])]
    ppermute x28 -> x29, waiting for transfers between devices: 46.2 us -> 48.6 us  [swap(): return lax.ppermute(value, axis, [(at, at ^ bit) for at in range(count)])]
    unnamed x83 -> x99, local copies, waits for them, and re-layouts: 5.68 us -> 7.23 us
  transfers between devices with their start and end apart: 32 -> 33, of which waited for: 15 -> 17; matrix products, arithmetic and copies ran while one was open for 3% -> 2% of each run, Pallas kernels for 29% -> 29%
where the time goes in v10:
time: 267 us; the launch traced here: 265 us
  Pallas kernels  113 us (42%)
  waiting for transfers between devices  71.4 us (27%)
  starting transfers between devices  40.5 us (15%)
  blocking collectives  18.9 us (7%)
  local copies, waits for them, and re-layouts  11.6 us (4%)
  other arithmetic  7.68 us (3%)
    ppermute x29, waiting for transfers between devices, swap(): return lax.ppermute(value, axis, [(at, at ^ bit) for at in range(count)])  48.6 us
    pallas_call x1, Pallas kernels, shards(): pl.pallas_call(scan_back_kernel, grid_spec=pltpu.PrefetchScalarGridSpec(n...  22.9 us
    all_to_all x4, waiting for transfers between devices, high_all_to_all(): return lax.all_to_all(value, 'dp', 0, 0, axis_index_groups=groups)  22.8 us
    ppermute x29, starting transfers between devices, swap(): return lax.ppermute(value, axis, [(at, at ^ bit) for at in range(count)])  20.8 us
    all_to_all x4, starting transfers between devices, high_all_to_all(): return lax.all_to_all(value, 'dp', 0, 0, axis_index_groups=groups)  19.7 us
    all_to_all x1, blocking collectives, high_all_to_all(): return lax.all_to_all(value, 'dp', 0, 0, axis_index_groups=groups)  18.9 us
    pallas_call x1, Pallas kernels, shards(): pl.pallas_call(scan_forward_kernel, grid_spec=pltpu.PrefetchScalarGridSpe...  18.8 us
    pallas_call x1, Pallas kernels, shards(): pl.pallas_call(norm_back_kernel, grid_spec=pltpu.PrefetchScalarGridSpec(n...  14.2 us
  transfers between devices with their start and end apart: 33, of which 17 were waited for; matrix products, arithmetic and copies ran while one was open for 2% of the time, Pallas kernels for 29%

profile of v10, /device:TPU:0, one launch (start us, length us, event | category | flops | bytes accessed | tf_op | source)
XLA Modules:
  0.0 264.8 jit_solution(1727112583282293880)
XLA Ops:
  1.3 3.6 %pack.1 = (bf16[4,144,768]{2,1,0:T(8,128)(2,1)}, bf16[4,128,512]{2,1,0:T(8,128)(2,1)}, bf16[4,128,512]{2,1,0:T(8,128)(2,1)}) custom-call(s32[3]{0:T(128)} %pad_add_fusion.here_ref, f32[128,4352]{1,0:T(8,128)} %weight_ref.3, f32[256,1024]{1,0:T(8,128)} %weight_ref.2, f32[32,128]{1,0:T(8,128)} %dt_ref.1, f32[5,288]{1,0:T(8,128)} %conv_ref.1, f32[384]{0:T(512)} %gain_ref.1), custom_call_target="tpu_custom_call" | custom-call | tf_op jit(solution)/shard_map/pack/pallas_call | solution.py:1021
  4.8 6.5 %all-to-all-start = ((bf16[4,144,768]{2,1,0:T(8,128)(2,1)}), bf16[4,144,768]{2,1,0:T(8,128)(2,1)S(1)}, u32[]{:S(2)}, u32[]{:S(2)}) async-start(bf16[4,144,768]{2,1,0:T(8,128)(2,1)} %get-tuple-element.126), calls=%async_computation | async-start | bytes 1769472 | tf_op jit(solution)/shard_map/all_to_all | solution.py:944
  11.3 1.5 collective-permute-start.1
  13.7 0.7 copy.66
  15.1 18.4 %all-to-all-done.w1_pieces_0_ = bf16[4,144,768]{2,1,0:T(8,128)(2,1)S(1)} async-done(((bf16[4,144,768]{2,1,0:T(8,128)(2,1)}), bf16[4,144,768]{2,1,0:T(8,128)(2,1)S(1)}, u32[]{:S(2)}, u32[]{:S(2)}) %all-to-all-start) | async-done | bytes 884768 | tf_op jit(solution)/shard_map/all_to_all | solution.py:944
  33.5 1.5 collective-permute-start
  35.0 1.0 collective-permute-done.1.tok_pieces_2_
  36.0 18.1 %collective-permute-done.w1_pieces_1_ = bf16[4,144,768]{2,1,0:T(8,128)(2,1)S(1)} collective-permute-done((bf16[4,144,768]{2,1,0:T(8,128)(2,1)S(1)}, bf16[4,144,768]{2,1,0:T(8,128)(2,1)S(1)}, u32[]{:S(2)}, u32[]{:S(2)}) %collective-permute-start) | collective-permute-done | bytes 884768 | tf_op jit(solution)/shard_map/ppermute | solution.py:933
  54.1 0.9 copy-done.14
  55.1 18.9 %all_to_all.25.wg_pieces_0_ = bf16[4,128,512]{2,1,0:T(8,128)(2,1)S(1)} all-to-all(bf16[4,128,512]{2,1,0:T(8,128)(2,1)} %get-tuple-element.136), channel_id=1, replica_groups={{0,8,16,24},{4,12,20,28},{1,9,17,25},{5,13,21,29},{2,10,18,26},{6,14,22..., dimensions={0} | all-to-all | bytes 1048576 | tf_op jit(solution)/shard_map/all_to_all | solution.py:944
  73.9 3.5 %all-to-all-start.1 = ((bf16[4,128,512]{2,1,0:T(8,128)(2,1)}), bf16[4,128,512]{2,1,0:T(8,128)(2,1)S(1)}, u32[]{:S(2)}, u32[]{:S(2)}) async-start(bf16[4,128,512]{2,1,0:T(8,128)(2,1)} %get-tuple-element.130), calls=%async_computation.1 | async-start | bytes 1048576 | tf_op jit(solution)/shard_map/all_to_all | solution.py:944
  77.5 1.6 collective-permute-start.5
  79.4 1.0 copy.67.segc_ref
  80.4 1.5 collective-permute-start.7
  81.9 18.8 %scan_forward.1 = (bf16[1024,1024]{1,0:T(8,128)(2,1)}, f32[8,768]{1,0:T(8,128)}, f32[1,1024]{1,0:T(1,128)}, f32[1,512]{1,0:T(1,128)}, bf16[8,1024]{1,0:T(8,128)(...) custom-call(s32[3]{0:T(128)} %pad_add_fusion.here_ref, ...), custom_call_target="tpu_custom_call" | custom-call | tf_op jit(solution)/shard_map/scan_forward/pallas_call | solution.py:1075
  100.8 2.0 collective-permute-done.6.cot_pieces_3_
  102.7 1.5 collective-permute-start.8
  104.2 7.5 %gate.1 = (bf16[1024,512]{1,0:T(8,128)(2,1)}, bf16[1024,512]{1,0:T(8,128)(2,1)}, f32[8,1024]{1,0:T(8,128)}) custom-call(s32[2]{0:T(128)} %pad_add_fusion.1.at_ref, bf16[1024,1024]{1,0:T(8,128)(2,1)} %get-tuple-element.149.hid_ref, bf16[4,128,512]{2,1,0:T(8,128)(2,1)} %copy-done.9, bf16[4,128,512]{2,1,0:T(8,128)(2,1)} %collective-permute-done.7.wg_pieces_1_, ...), custom_call_target="tpu_custom_call" | custom-call | tf_op jit(solution)/shard_map/gate/pallas_call | solution.py:1144
  111.8 5.0 %collective-permute-done.8.wo_pieces_1_ = bf16[4,128,512]{2,1,0:T(8,128)(2,1)S(1)} collective-permute-done((bf16[4,128,512]{2,1,0:T(8,128)(2,1)S(1)}, bf16[4,128,512]{2,1,0:T(8,128)(2,1)S(1)}, u32[]{:S(2)}, u32[]{:S(2)}) %collective-permute-start.8) | collective-permute-done | bytes 524320 | tf_op jit(solution)/shard_map/ppermute | solution.py:933
  116.8 0.8 copy-done.19
  117.6 8.6 %normed_grad.1 = (bf16[512,1024]{1,0:T(8,128)(2,1)}, bf16[4,256,1024]{2,1,0:T(8,128)(2,1)}, f32[1024,512]{1,0:T(8,128)}, f32[8,1024]{1,0:T(8,128)}) custom-call(s32[3]{0:T(128)} %pad_add_fusion.here_ref, s32[2]{0:T(128)} %pad_add_fusion.1.at_ref, bf16[4,128,512]{2,1,0:T(8,128)(2,1)} %copy-done.8, bf16[4,128,512]{2,1,0:T(8,128)(2,1)} %copy-done.19, ...), custom_call_target="tpu_custom_call" | custom-call | tf_op jit(solution)/shard_map/normed_grad/pallas_call | solution.py:1163
  126.2 1.6 collective-permute-start.10
  128.5 2.0 collective-permute-done.10.stat_refs_2_
  130.4 1.0 collective-permute-done.11.stat_refs_3_
  132.0 14.2 %norm_back.1 = (bf16[256,1024]{1,0:T(8,128)(2,1)}, bf16[256,1024]{1,0:T(8,128)(2,1)}, bf16[256,1024]{1,0:T(8,128)(2,1)}, bf16[256,1024]{1,0:T(8,128)(2,1)}, bf16...) custom-call(s32[4]{0:T(128)} %broadcast_xor_fusion.perm_ref, ...), custom_call_target="tpu_custom_call" | custom-call | tf_op jit(solution)/shard_map/norm_back/pallas_call | solution.py:1200
  146.2 1.5 collective-permute-start.12
  147.8 0.9 collective-permute-start.14
  148.6 1.0 collective-permute-start.15
  149.6 22.9 %scan_back.1 = (bf16[4,128,512]{2,1,0:T(8,128)(2,1)}, bf16[4,128,512]{2,1,0:T(8,128)(2,1)}, bf16[1024,512]{1,0:T(8,128)(2,1)}, bf16[1024,256]{1,0:T(8,128)(2,1)}...) custom-call(s32[4]{0:T(128)} %broadcast_xor_fusion.perm_ref, ...), custom_call_target="tpu_custom_call" | custom-call | tf_op jit(solution)/shard_map/scan_back/pallas_call | solution.py:1247
  173.2 0.8 copy-done.22
  174.0 1.3 add_convert_fusion
  175.2 5.0 %all-to-all-start.3 = ((bf16[4,256,512]{2,1,0:T(8,128)(2,1)}), bf16[4,256,512]{2,1,0:T(8,128)(2,1)S(1)}, u32[]{:S(2)}, u32[]{:S(2)}) async-start(bf16[4,256,512]{2,1,0:T(8,128)(2,1)} %add_convert_fusion), calls=%async_computation.3 | async-start | bytes 2097152 | tf_op jit(solution)/shard_map/all_to_all | solution.py:944
  180.4 0.9 collective-permute-start.17
  181.8 8.9 %hidden_back.1 = (bf16[256,1024]{1,0:T(8,128)(2,1)}, bf16[256,1024]{1,0:T(8,128)(2,1)}, bf16[256,1024]{1,0:T(8,128)(2,1)}, bf16[256,1024]{1,0:T(8,128)(2,1)}, f32[8,1024]{1,0:T(8,128)}) custom-call(s32[4]{0:T(128)} %broadcast_xor_fusion.perm_ref, bf16[1024,512]{1,0:T(8,128)(2,1)} %get-tuple-element.193.dgate_ref, ...), custom_call_target="tpu_custom_call" | custom-call | tf_op jit(solution)/shard_map/hidden_back/pallas_call | solution.py:1313
  190.8 3.4 %collective-permute-done.17.dbcfar_ref = bf16[1024,256]{1,0:T(8,128)(2,1)S(1)} collective-permute-done((bf16[1024,256]{1,0:T(8,128)(2,1)S(1)}, bf16[1024,256]{1,0:T(8,128)(2,1)S(1)}, u32[]{:S(2)}, u32[]{:S(2)}) %collective-permute-start.17) | collective-permute-done | bytes 524320 | tf_op jit(solution)/shard_map/ppermute | solution.py:933
  194.2 0.8 copy-done.18
  195.0 6.6 %maps_back.1 = (bf16[160,512]{1,0:T(8,128)(2,1)}, bf16[160,512]{1,0:T(8,128)(2,1)}, f32[256,1024]{1,0:T(8,128)}) custom-call(s32[3]{0:T(128)} %pad_add_fusion.here_ref, bf16[1024,256]{1,0:T(8,128)(2,1)} %copy-done.7, bf16[1024,256]{1,0:T(8,128)(2,1)} %copy-done.18, f32[1024,768]{1,0:T(8,128)} %get-tuple-element.175.convsum_ref, ...), custom_call_target="tpu_custom_call" | custom-call | tf_op jit(solution)/shard_map/maps_back/pallas_call | solution.py:1341
  202.1 1.4 add_add_fusion
  203.5 2.8 %all-to-all-done.3 = bf16[4,256,512]{2,1,0:T(8,128)(2,1)S(1)} async-done(((bf16[4,256,512]{2,1,0:T(8,128)(2,1)}), bf16[4,256,512]{2,1,0:T(8,128)(2,1)S(1)}, u32[]{:S(2)}, u32[]{:S(2)}) %all-to-all-start.3) | async-done | bytes 1048608 | tf_op jit(solution)/shard_map/all_to_all | solution.py:944
  206.5 0.7 collective-permute-done.18.mcame_ref
  207.2 0.8 copy-done.20
  208.0 2.3 pair_sum_late.1
  210.3 4.8 %all-to-all-start.4 = ((bf16[4,192,512]{2,1,0:T(8,128)(2,1)}), bf16[4,192,512]{2,1,0:T(8,128)(2,1)S(1)}, u32[]{:S(2)}, u32[]{:S(2)}) async-start(bf16[4,192,512]{2,1,0:T(8,128)(2,1)} %pair_sum_late.1), calls=%async_computation.4 | async-start | bytes 1572864 | tf_op jit(solution)/shard_map/all_to_all | solution.py:944
  215.1 0.9 collective-permute-start.21
  216.0 1.2 collective-permute-start.27
  217.2 0.7 collective-permute-start.28
  218.1 5.6 %collective-permute-done.21.early_refs_2_ = bf16[256,512]{1,0:T(8,128)(2,1)S(1)} collective-permute-done((bf16[256,512]{1,0:T(8,128)(2,1)S(1)}, bf16[256,512]{1,0:T(8,128)(2,1)S(1)}, u32[]{:S(2)}, u32[]{:S(2)}) %collective-permute-start.21) | collective-permute-done | bytes 262176 | tf_op jit(solution)/shard_map/ppermute | solution.py:933
  223.8 1.5 collective-permute-done.22.early_refs_3_
  225.3 0.7 copy-done.13
  226.0 5.5 %adam_out.1 = (f32[256,1024]{1,0:T(8,128)}, f32[256,1024]{1,0:T(8,128)}, f32[256,1024]{1,0:T(8,128)}) custom-call(s32[3]{0:T(128)} %pad_add_fusion.here_ref, f32[256,1024]{1,0:T(8,128)} %weight_ref.2, f32[256,1024]{1,0:T(8,128)} %first_ref.2, f32[256,1024]{1,0:T(8,128)} %second_ref.2, bf16[256,512]{1,0:T(8,128)(2,1)} %copy-done.5, ...), custom_call_target="tpu_custom_call" | custom-call | tf_op jit(solution)/shard_map/adam_out/pallas_call | solution.py:1420
  231.5 1.5 all-to-all-done.4.parts_ref
  233.0 0.9 copy-done.4
  233.9 1.9 sum_late.1.late_refs_0_
  235.8 0.9 collective-permute-start.24
  236.7 1.0 collective-permute-start.25
  237.7 6.7 %collective-permute-done.28.part_refs_2_ = bf16[256,1024]{1,0:T(8,128)(2,1)S(1)} collective-permute-done((bf16[256,1024]{1,0:T(8,128)(2,1)}, bf16[256,1024]{1,0:T(8,128)(2,1)S(1)}, u32[]{:S(2)}, u32[]{:S(2)}) %collective-permute-start.28) | collective-permute-done | bytes 524320 | tf_op jit(solution)/shard_map/ppermute | solution.py:933
  244.4 0.8 copy-done.26
  245.2 4.1 %input_back.1 = f32[256,1024]{1,0:T(8,128)} custom-call(bf16[256,1024]{1,0:T(8,128)(2,1)} %copy-done.24, bf16[256,1024]{1,0:T(8,128)(2,1)} %copy-done.25, bf16[256,1024]{1,0:T(8,128)(2,1)} %copy-done.26, bf16[256,1024]{1,0:T(8,128)(2,1)} %get-tuple-element.219.part_refs_3_, f32[256,1024]{1,0:T(8,128)} %get-tuple-element.220.own_ref, f32[256,1024]{1,0:T(8,128)} %bitcast.45, ...), custom_call_target="tpu_custom_call" | custom-call | tf_op jit(solution)/shard_map/input_back/pallas_call | solution.py:1395
  249.4 0.8 collective-permute-done.24.late_refs_2_
  250.9 0.8 slice_bitcast_fusion.3
  253.6 0.6 multiply_subtract_fusion
  254.9 0.7 multiply_subtract_fusion.3
  255.6 0.7 multiply_subtract_fusion.1
  256.3 8.3 %adam_in.1 = (f32[128,4352]{1,0:T(8,128)}, f32[128,4352]{1,0:T(8,128)}, f32[128,4352]{1,0:T(8,128)}) custom-call(s32[3]{0:T(128)} %pad_add_fusion.here_ref, f32[128,4352]{1,0:T(8,128)} %weight_ref.3, f32[128,4352]{1,0:T(8,128)} %first_ref.3, f32[128,4352]{1,0:T(8,128)} %second_ref.3, bf16[256,512]{1,0:T(8,128)(2,1)} %copy-done.5, ...), custom_call_target="tpu_custom_call" | custom-call | tf_op jit(solution)/shard_map/adam_in/pallas_call | solution.py:1445
  (163 shorter events, 9.3 us)
Async XLA Ops:
  1.3 10.1 %copy-start = (f32[1,256,1024]{2,1,0:T(8,128)S(1)}, f32[1,256,1024]{2,1,0:T(8,128)}, u32[]{:S(2)}) copy-start(f32[1,256,1024]{2,1,0:T(8,128)} %param.22) | copy-start | bytes 3145732
  1.3 11.6 %copy-start.2 = (f32[1,256,1024]{2,1,0:T(8,128)S(1)}, f32[1,256,1024]{2,1,0:T(8,128)}, u32[]{:S(2)}) copy-start(f32[1,256,1024]{2,1,0:T(8,128)} %param.24) | copy-start | bytes 3145732
  4.8 8.1 %copy-start.47 = (s32[4]{0:T(128)S(1)}, s32[4]{0:T(128)}, u32[]{:S(2)}) copy-start(s32[4]{0:T(128)} %constant.15.clone) | copy-start | bytes 52
  4.8 8.7 %copy-start.42 = (f32[3,32]{1,0:T(4,128)S(1)}, f32[3,32]{1,0:T(4,128)}, u32[]{:S(2)}) copy-start(f32[3,32]{1,0:T(4,128)} %param.30) | copy-start | bytes 1156
  4.8 9.6 %copy-start.32 = (s32[1,1024]{1,0:T(1,128)S(1)}, s32[1,1024]{1,0:T(1,128)}, u32[]{:S(2)}) copy-start(s32[1,1024]{1,0:T(1,128)} %segr_ref.3) | copy-start | bytes 12292
  4.8 28.7 %all-to-all-start = ((bf16[4,144,768]{2,1,0:T(8,128)(2,1)}), bf16[4,144,768]{2,1,0:T(8,128)(2,1)S(1)}, u32[]{:S(2)}, u32[]{:S(2)}) async-start(bf16[4,144,768]{2,1,0:T(8,128)(2,1)} %get-tuple-element.126), calls=%async_computation | async-start | bytes 1769472 | tf_op jit(solution)/shard_map/all_to_all | solution.py:944
  11.3 24.7 %collective-permute-start.1 = (f32[256,1024]{1,0:T(8,128)S(1)}, f32[256,1024]{1,0:T(8,128)}, u32[]{:S(2)}, u32[]{:S(2)}) collective-permute-start(f32[256,1024]{1,0:T(8,128)S(1)} %bitcast.46), channel_id=1, source_target_pairs={{0,2},{1,3},{2,0},{3,1},{4,6},{5,7},{6,4},{7,5},{8,10},{9,11},{10,... | collective-permute-start | bytes 3145736 | tf_op jit(solution)/shard_map/ppermute | solution.py:933
  12.9 87.7 %copy-start.6 = (bf16[256,1024]{1,0:T(8,128)(2,1)}, bf16[256,1024]{1,0:T(8,128)(2,1)S(1)}, u32[]{:S(2)}) copy-start(bf16[256,1024]{1,0:T(8,128)(2,1)S(1)} %bitcast_convert_fusion.cot_pieces_0_) | copy-start | bytes 1572868
  13.7 68.2 %copy-start.33 = (f32[3,8]{1,0:T(4,128)}, f32[3,8]{1,0:T(4,128)S(1)}, u32[]{:S(2)}) copy-start(f32[3,8]{1,0:T(4,128)S(1)} %dynamic-slice_reduce_fusion.hrow_ref) | copy-start | bytes 292
  33.5 48.4 %copy-start.3 = (bf16[4,144,768]{2,1,0:T(8,128)(2,1)}, bf16[4,144,768]{2,1,0:T(8,128)(2,1)S(1)}, u32[]{:S(2)}) copy-start(bf16[4,144,768]{2,1,0:T(8,128)(2,1)S(1)} %all-to-all-done.w1_pieces_0_) | copy-start | bytes 2654212
  33.5 20.6 %collective-permute-start = (bf16[4,144,768]{2,1,0:T(8,128)(2,1)S(1)}, bf16[4,144,768]{2,1,0:T(8,128)(2,1)S(1)}, u32[]{:S(2)}, u32[]{:S(2)}) collective-permute-start(bf16[4,144,768]{2,1,0:T(8,128)(2,1)S(1)} %all-to-all-done.w1_pieces_0_), channel_id=1, source_target_pairs={{0,4},{4,0},{8,12},{12,8},{16,20},{20,16},{24,28},{28,24},{1,5},{5... | collective-permute-start | bytes 2654216 | tf_op jit(solution)/shard_map/ppermute | solution.py:933
  35.0 42.4 %collective-permute-start.2 = (f32[256,1024]{1,0:T(8,128)S(1)}, f32[256,1024]{1,0:T(8,128)}, u32[]{:S(2)}, u32[]{:S(2)}) collective-permute-start(f32[256,1024]{1,0:T(8,128)S(1)} %bitcast.47), channel_id=1, source_target_pairs={{0,1},{1,0},{2,3},{3,2},{4,5},{5,4},{6,7},{7,6},{8,9},{9,8},{10,11... | collective-permute-start | bytes 3145736 | tf_op jit(solution)/shard_map/ppermute | solution.py:933
  55.0 22.4 %collective-permute-start.3 = (f32[256,1024]{1,0:T(8,128)}, f32[256,1024]{1,0:T(8,128)}, u32[]{:S(2)}, u32[]{:S(2)}) collective-permute-start(f32[256,1024]{1,0:T(8,128)} %collective-permute-done.1.tok_pieces_2_), channel_id=1, source_target_pairs={{0,1},{1,0},{2,3},{3,2},{4,5},{5,4},{6,7},{7,6},{8,9},{9,8},{10,11... | collective-permute-start | bytes 3145736 | tf_op jit(solution)/shard_map/ppermute | solution.py:933
  73.9 26.7 %copy-start.9 = (bf16[4,128,512]{2,1,0:T(8,128)(2,1)}, bf16[4,128,512]{2,1,0:T(8,128)(2,1)S(1)}, u32[]{:S(2)}) copy-start(bf16[4,128,512]{2,1,0:T(8,128)(2,1)S(1)} %all_to_all.25.wg_pieces_0_) | copy-start | bytes 1572868
  73.9 26.8 %all-to-all-start.1 = ((bf16[4,128,512]{2,1,0:T(8,128)(2,1)}), bf16[4,128,512]{2,1,0:T(8,128)(2,1)S(1)}, u32[]{:S(2)}, u32[]{:S(2)}) async-start(bf16[4,128,512]{2,1,0:T(8,128)(2,1)} %get-tuple-element.130), calls=%async_computation.1 | async-start | bytes 1048576 | tf_op jit(solution)/shard_map/all_to_all | solution.py:944
  77.4 23.3 %collective-permute-start.4 = (bf16[256,1024]{1,0:T(8,128)(2,1)S(1)}, bf16[256,1024]{1,0:T(8,128)(2,1)S(1)}, u32[]{:S(2)}, u32[]{:S(2)}) collective-permute-start(bf16[256,1024]{1,0:T(8,128)(2,1)S(1)} %bitcast_convert_fusion.cot_pieces_0_), channel_id=1, source_target_pairs={{0,1},{1,0},{2,3},{3,2},{4,5},{5,4},{6,7},{7,6},{8,9},{9,8},{10,11... | collective-permute-start | bytes 1572872 | tf_op jit(solution)/shard_map/ppermute | solution.py:933
  77.5 23.2 %collective-permute-start.5 = (bf16[256,1024]{1,0:T(8,128)(2,1)S(1)}, bf16[256,1024]{1,0:T(8,128)(2,1)S(1)}, u32[]{:S(2)}, u32[]{:S(2)}) collective-permute-start(bf16[256,1024]{1,0:T(8,128)(2,1)S(1)} %bitcast_convert_fusion.cot_pieces_0_), channel_id=1, source_target_pairs={{0,2},{1,3},{2,0},{3,1},{4,6},{5,7},{6,4},{7,5},{8,10},{9,11},{10,... | collective-permute-start | bytes 1572872 | tf_op jit(solution)/shard_map/ppermute | solution.py:933
  79.1 23.6 %collective-permute-start.6 = (bf16[256,1024]{1,0:T(8,128)(2,1)S(1)}, bf16[256,1024]{1,0:T(8,128)(2,1)}, u32[]{:S(2)}, u32[]{:S(2)}) collective-permute-start(bf16[256,1024]{1,0:T(8,128)(2,1)S(1)} %bitcast_convert_fusion.cot_pieces_0_), channel_id=1, source_target_pairs={{0,3},{1,2},{2,1},{3,0},{4,7},{5,6},{6,5},{7,4},{8,11},{9,10},{10,... | collective-permute-start | bytes 1572872 | tf_op jit(solution)/shard_map/ppermute | solution.py:933
  80.4 23.8 %collective-permute-start.7 = (bf16[4,128,512]{2,1,0:T(8,128)(2,1)S(1)}, bf16[4,128,512]{2,1,0:T(8,128)(2,1)}, u32[]{:S(2)}, u32[]{:S(2)}) collective-permute-start(bf16[4,128,512]{2,1,0:T(8,128)(2,1)S(1)} %all_to_all.25.wg_pieces_0_), channel_id=1, source_target_pairs={{0,4},{4,0},{8,12},{12,8},{16,20},{20,16},{24,28},{28,24},{1,5},{5... | collective-permute-start | bytes 1572872 | tf_op jit(solution)/shard_map/ppermute | solution.py:933
  100.7 11.1 %copy-start.8 = (bf16[4,128,512]{2,1,0:T(8,128)(2,1)}, bf16[4,128,512]{2,1,0:T(8,128)(2,1)S(1)}, u32[]{:S(2)}) copy-start(bf16[4,128,512]{2,1,0:T(8,128)(2,1)S(1)} %all-to-all-done.1.wo_pieces_0_) | copy-start | bytes 1572868
  100.7 11.1 %copy-start.15 = (bf16[256,1024]{1,0:T(8,128)(2,1)}, bf16[256,1024]{1,0:T(8,128)(2,1)S(1)}, u32[]{:S(2)}) copy-start(bf16[256,1024]{1,0:T(8,128)(2,1)S(1)} %collective-permute-done.4.cot_pieces_1_) | copy-start | bytes 1572868
  100.7 11.1 %copy-start.16 = (bf16[256,1024]{1,0:T(8,128)(2,1)}, bf16[256,1024]{1,0:T(8,128)(2,1)S(1)}, u32[]{:S(2)}) copy-start(bf16[256,1024]{1,0:T(8,128)(2,1)S(1)} %collective-permute-done.5.cot_pieces_2_) | copy-start | bytes 1572868
  102.7 14.1 %collective-permute-start.8 = (bf16[4,128,512]{2,1,0:T(8,128)(2,1)S(1)}, bf16[4,128,512]{2,1,0:T(8,128)(2,1)S(1)}, u32[]{:S(2)}, u32[]{:S(2)}) collective-permute-start(bf16[4,128,512]{2,1,0:T(8,128)(2,1)S(1)} %all-to-all-done.1.wo_pieces_0_), channel_id=1, source_target_pairs={{0,4},{4,0},{8,12},{12,8},{16,20},{20,16},{24,28},{28,24},{1,5},{5... | collective-permute-start | bytes 1572872 | tf_op jit(solution)/shard_map/ppermute | solution.py:933
  126.2 4.2 %collective-permute-start.10 = (f32[8,1024]{1,0:T(8,128)}, f32[8,1024]{1,0:T(8,128)S(1)}, u32[]{:S(2)}, u32[]{:S(2)}) collective-permute-start(f32[8,1024]{1,0:T(8,128)} %get-tuple-element.164.stat_refs_0_), channel_id=1, source_target_pairs={{0,2},{1,3},{2,0},{3,1},{4,6},{5,7},{6,4},{7,5},{8,10},{9,11},{10,... | collective-permute-start | bytes 98312 | tf_op jit(solution)/shard_map/ppermute | solution.py:933
  127.8 3.6 %collective-permute-start.11 = (f32[8,1024]{1,0:T(8,128)}, f32[8,1024]{1,0:T(8,128)S(1)}, u32[]{:S(2)}, u32[]{:S(2)}) collective-permute-start(f32[8,1024]{1,0:T(8,128)} %get-tuple-element.164.stat_refs_0_), channel_id=1, source_target_pairs={{0,3},{1,2},{2,1},{3,0},{4,7},{5,6},{6,5},{7,4},{8,11},{9,10},{10,... | collective-permute-start | bytes 98312 | tf_op jit(solution)/shard_map/ppermute | solution.py:933
  127.8 3.6 %collective-permute-start.9 = (f32[8,1024]{1,0:T(8,128)}, f32[8,1024]{1,0:T(8,128)S(1)}, u32[]{:S(2)}, u32[]{:S(2)}) collective-permute-start(f32[8,1024]{1,0:T(8,128)} %get-tuple-element.164.stat_refs_0_), channel_id=1, source_target_pairs={{0,1},{1,0},{2,3},{3,2},{4,5},{5,4},{6,7},{7,6},{8,9},{9,8},{10,11... | collective-permute-start | bytes 98312 | tf_op jit(solution)/shard_map/ppermute | solution.py:933
  146.2 26.9 %collective-permute-start.12 = (bf16[4,256,512]{2,1,0:T(8,128)(2,1)}, bf16[4,256,512]{2,1,0:T(8,128)(2,1)S(1)}, u32[]{:S(2)}, u32[]{:S(2)}) collective-permute-start(bf16[4,256,512]{2,1,0:T(8,128)(2,1)} %get-tuple-element.168), channel_id=1, source_target_pairs={{0,4},{4,0},{8,12},{12,8},{16,20},{20,16},{24,28},{28,24},{1,5},{5... | collective-permute-start | bytes 3145736 | tf_op jit(solution)/shard_map/ppermute | solution.py:933
  147.8 25.2 %collective-permute-start.13 = (bf16[256,1024]{1,0:T(8,128)(2,1)}, bf16[256,1024]{1,0:T(8,128)(2,1)S(1)}, u32[]{:S(2)}, u32[]{:S(2)}) collective-permute-start(bf16[256,1024]{1,0:T(8,128)(2,1)} %get-tuple-element.169), channel_id=1, source_target_pairs={{0,1},{1,0},{2,3},{3,2},{4,5},{5,4},{6,7},{7,6},{8,9},{9,8},{10,11... | collective-permute-start | bytes 1572872 | tf_op jit(solution)/shard_map/ppermute | solution.py:933
  147.8 25.2 %collective-permute-start.14 = (bf16[256,1024]{1,0:T(8,128)(2,1)}, bf16[256,1024]{1,0:T(8,128)(2,1)S(1)}, u32[]{:S(2)}, u32[]{:S(2)}) collective-permute-start(bf16[256,1024]{1,0:T(8,128)(2,1)} %get-tuple-element.170), channel_id=1, source_target_pairs={{0,2},{1,3},{2,0},{3,1},{4,6},{5,7},{6,4},{7,5},{8,10},{9,11},{10,... | collective-permute-start | bytes 1572872 | tf_op jit(solution)/shard_map/ppermute | solution.py:933
  148.6 24.5 %collective-permute-start.15 = (bf16[256,1024]{1,0:T(8,128)(2,1)}, bf16[256,1024]{1,0:T(8,128)(2,1)S(1)}, u32[]{:S(2)}, u32[]{:S(2)}) collective-permute-start(bf16[256,1024]{1,0:T(8,128)(2,1)} %get-tuple-element.171), channel_id=1, source_target_pairs={{0,3},{1,2},{2,1},{3,0},{4,7},{5,6},{6,5},{7,4},{8,11},{9,10},{10,... | collective-permute-start | bytes 1572872 | tf_op jit(solution)/shard_map/ppermute | solution.py:933
  149.6 24.3 %copy-start.10 = (bf16[4,256,512]{2,1,0:T(8,128)(2,1)S(1)}, bf16[4,256,512]{2,1,0:T(8,128)(2,1)}, u32[]{:S(2)}) copy-start(bf16[4,256,512]{2,1,0:T(8,128)(2,1)} %get-tuple-element.204) | copy-start | bytes 3145732
  172.6 7.6 %collective-permute-start.16 = (bf16[1024,256]{1,0:T(8,128)(2,1)}, bf16[1024,256]{1,0:T(8,128)(2,1)S(1)}, u32[]{:S(2)}, u32[]{:S(2)}) collective-permute-start(bf16[1024,256]{1,0:T(8,128)(2,1)} %get-tuple-element.185), channel_id=1, source_target_pairs={{0,1},{1,0},{2,3},{3,2},{4,5},{5,4},{6,7},{7,6},{8,9},{9,8},{10,11... | collective-permute-start | bytes 1572872 | tf_op jit(solution)/shard_map/ppermute | solution.py:933
  173.9 6.2 %copy-start.17 = (bf16[1024,256]{1,0:T(8,128)(2,1)S(1)}, bf16[1024,256]{1,0:T(8,128)(2,1)}, u32[]{:S(2)}) copy-start(bf16[1024,256]{1,0:T(8,128)(2,1)} %get-tuple-element.185) | copy-start | bytes 1572868
  175.2 31.1 %all-to-all-start.3 = ((bf16[4,256,512]{2,1,0:T(8,128)(2,1)}), bf16[4,256,512]{2,1,0:T(8,128)(2,1)S(1)}, u32[]{:S(2)}, u32[]{:S(2)}) async-start(bf16[4,256,512]{2,1,0:T(8,128)(2,1)} %add_convert_fusion), calls=%async_computation.3 | async-start | bytes 2097152 | tf_op jit(solution)/shard_map/all_to_all | solution.py:944
  180.3 10.4 %copy-start.7 = (bf16[1024,256]{1,0:T(8,128)(2,1)}, bf16[1024,256]{1,0:T(8,128)(2,1)S(1)}, u32[]{:S(2)}) copy-start(bf16[1024,256]{1,0:T(8,128)(2,1)S(1)} %add_convert_fusion.1.dbc_ref) | copy-start | bytes 1572868
  180.4 13.8 %collective-permute-start.17 = (bf16[1024,256]{1,0:T(8,128)(2,1)S(1)}, bf16[1024,256]{1,0:T(8,128)(2,1)S(1)}, u32[]{:S(2)}, u32[]{:S(2)}) collective-permute-start(bf16[1024,256]{1,0:T(8,128)(2,1)S(1)} %add_convert_fusion.1.dbc_ref), channel_id=1, source_target_pairs={{0,2},{1,3},{2,0},{3,1},{4,6},{5,7},{6,4},{7,5},{8,10},{9,11},{10,... | collective-permute-start | bytes 1572872 | tf_op jit(solution)/shard_map/ppermute | solution.py:933
  181.3 25.9 %collective-permute-start.19 = (bf16[4,128,512]{2,1,0:T(8,128)(2,1)}, bf16[4,128,512]{2,1,0:T(8,128)(2,1)S(1)}, u32[]{:S(2)}, u32[]{:S(2)}) collective-permute-start(bf16[4,128,512]{2,1,0:T(8,128)(2,1)} %get-tuple-element.208), channel_id=1, source_target_pairs={{0,4},{4,0},{8,12},{12,8},{16,20},{20,16},{24,28},{28,24},{1,5},{5... | collective-permute-start | bytes 1572872 | tf_op jit(solution)/shard_map/ppermute | solution.py:933
  195.0 7.1 %copy-start.1 = (f32[1,256,1024]{2,1,0:T(8,128)S(1)}, f32[1,256,1024]{2,1,0:T(8,128)}, u32[]{:S(2)}) copy-start(f32[1,256,1024]{2,1,0:T(8,128)} %param.22) | copy-start | bytes 3145732
  195.0 7.1 %copy-start.21 = (bf16[256,1024]{1,0:T(8,128)(2,1)S(1)}, bf16[256,1024]{1,0:T(8,128)(2,1)}, u32[]{:S(2)}) copy-start(bf16[256,1024]{1,0:T(8,128)(2,1)} %get-tuple-element.203) | copy-start | bytes 1572868
  195.0 7.1 %copy-start.23 = (bf16[256,1024]{1,0:T(8,128)(2,1)S(1)}, bf16[256,1024]{1,0:T(8,128)(2,1)}, u32[]{:S(2)}) copy-start(bf16[256,1024]{1,0:T(8,128)(2,1)} %copy-done.22) | copy-start | bytes 1572868
  201.6 5.6 %collective-permute-start.18 = (bf16[160,512]{1,0:T(8,128)(2,1)}, bf16[160,512]{1,0:T(8,128)(2,1)}, u32[]{:S(2)}, u32[]{:S(2)}) collective-permute-start(bf16[160,512]{1,0:T(8,128)(2,1)} %get-tuple-element.199), channel_id=1, source_target_pairs={{0,4},{4,0},{8,12},{12,8},{16,20},{20,16},{24,28},{28,24},{1,5},{5... | collective-permute-start | bytes 491528 | tf_op jit(solution)/shard_map/ppermute | solution.py:933
  206.5 18.7 %copy-start.5 = (bf16[256,512]{1,0:T(8,128)(2,1)}, bf16[256,512]{1,0:T(8,128)(2,1)S(1)}, u32[]{:S(2)}) copy-start(bf16[256,512]{1,0:T(8,128)(2,1)S(1)} %reduce_sum.30.early_refs_0_) | copy-start | bytes 786436
  210.3 22.7 %all-to-all-start.4 = ((bf16[4,192,512]{2,1,0:T(8,128)(2,1)}), bf16[4,192,512]{2,1,0:T(8,128)(2,1)S(1)}, u32[]{:S(2)}, u32[]{:S(2)}) async-start(bf16[4,192,512]{2,1,0:T(8,128)(2,1)} %pair_sum_late.1), calls=%async_computation.4 | async-start | bytes 1572864 | tf_op jit(solution)/shard_map/all_to_all | solution.py:944
  215.1 8.6 %collective-permute-start.21 = (bf16[256,512]{1,0:T(8,128)(2,1)S(1)}, bf16[256,512]{1,0:T(8,128)(2,1)S(1)}, u32[]{:S(2)}, u32[]{:S(2)}) collective-permute-start(bf16[256,512]{1,0:T(8,128)(2,1)S(1)} %reduce_sum.30.early_refs_0_), channel_id=1, source_target_pairs={{0,2},{1,3},{2,0},{3,1},{4,6},{5,7},{6,4},{7,5},{8,10},{9,11},{10,... | collective-permute-start | bytes 786440 | tf_op jit(solution)/shard_map/ppermute | solution.py:933
  216.0 20.7 %collective-permute-start.26 = (bf16[256,1024]{1,0:T(8,128)(2,1)}, bf16[256,1024]{1,0:T(8,128)(2,1)S(1)}, u32[]{:S(2)}, u32[]{:S(2)}) collective-permute-start(bf16[256,1024]{1,0:T(8,128)(2,1)} %get-tuple-element.216), channel_id=1, source_target_pairs={{0,1},{1,0},{2,3},{3,2},{4,5},{5,4},{6,7},{7,6},{8,9},{9,8},{10,11... | collective-permute-start | bytes 1572872 | tf_op jit(solution)/shard_map/ppermute | solution.py:933
  216.0 21.7 %collective-permute-start.27 = (bf16[256,1024]{1,0:T(8,128)(2,1)}, bf16[256,1024]{1,0:T(8,128)(2,1)S(1)}, u32[]{:S(2)}, u32[]{:S(2)}) collective-permute-start(bf16[256,1024]{1,0:T(8,128)(2,1)} %get-tuple-element.217), channel_id=1, source_target_pairs={{0,2},{1,3},{2,0},{3,1},{4,6},{5,7},{6,4},{7,5},{8,10},{9,11},{10,... | collective-permute-start | bytes 1572872 | tf_op jit(solution)/shard_map/ppermute | solution.py:933
  217.2 27.2 %collective-permute-start.28 = (bf16[256,1024]{1,0:T(8,128)(2,1)}, bf16[256,1024]{1,0:T(8,128)(2,1)S(1)}, u32[]{:S(2)}, u32[]{:S(2)}) collective-permute-start(bf16[256,1024]{1,0:T(8,128)(2,1)} %get-tuple-element.218), channel_id=1, source_target_pairs={{0,3},{1,2},{2,1},{3,0},{4,7},{5,6},{6,5},{7,4},{8,11},{9,10},{10,... | collective-permute-start | bytes 1572872 | tf_op jit(solution)/shard_map/ppermute | solution.py:933
  217.9 5.9 %collective-permute-start.20 = (bf16[256,512]{1,0:T(8,128)(2,1)S(1)}, bf16[256,512]{1,0:T(8,128)(2,1)S(1)}, u32[]{:S(2)}, u32[]{:S(2)}) collective-permute-start(bf16[256,512]{1,0:T(8,128)(2,1)S(1)} %reduce_sum.30.early_refs_0_), channel_id=1, source_target_pairs={{0,1},{1,0},{2,3},{3,2},{4,5},{5,4},{6,7},{7,6},{8,9},{9,8},{10,11... | collective-permute-start | bytes 786440 | tf_op jit(solution)/shard_map/ppermute | solution.py:933
  223.7 1.5 collective-permute-start.22
  235.8 13.6 %collective-permute-start.23 = (bf16[192,512]{1,0:T(8,128)(2,1)}, bf16[192,512]{1,0:T(8,128)(2,1)S(1)}, u32[]{:S(2)}, u32[]{:S(2)}) collective-permute-start(bf16[192,512]{1,0:T(8,128)(2,1)} %sum_late.1.late_refs_0_), channel_id=1, source_target_pairs={{0,1},{1,0},{2,3},{3,2},{4,5},{5,4},{6,7},{7,6},{8,9},{9,8},{10,11... | collective-permute-start | bytes 589832 | tf_op jit(solution)/shard_map/ppermute | solution.py:933
  235.8 14.5 %collective-permute-start.24 = (bf16[192,512]{1,0:T(8,128)(2,1)}, bf16[192,512]{1,0:T(8,128)(2,1)S(1)}, u32[]{:S(2)}, u32[]{:S(2)}) collective-permute-start(bf16[192,512]{1,0:T(8,128)(2,1)} %sum_late.1.late_refs_0_), channel_id=1, source_target_pairs={{0,2},{1,3},{2,0},{3,1},{4,6},{5,7},{6,4},{7,5},{8,10},{9,11},{10,... | collective-permute-start | bytes 589832 | tf_op jit(solution)/shard_map/ppermute | solution.py:933
  236.7 7.7 %copy-start.24 = (bf16[256,1024]{1,0:T(8,128)(2,1)}, bf16[256,1024]{1,0:T(8,128)(2,1)S(1)}, u32[]{:S(2)}) copy-start(bf16[256,1024]{1,0:T(8,128)(2,1)S(1)} %collective-permute-done.26.part_refs_0_) | copy-start | bytes 1572868
  236.7 14.2 %collective-permute-start.25 = (bf16[192,512]{1,0:T(8,128)(2,1)}, bf16[192,512]{1,0:T(8,128)(2,1)S(1)}, u32[]{:S(2)}, u32[]{:S(2)}) collective-permute-start(bf16[192,512]{1,0:T(8,128)(2,1)} %sum_late.1.late_refs_0_), channel_id=1, source_target_pairs={{0,3},{1,2},{2,1},{3,0},{4,7},{5,6},{6,5},{7,4},{8,11},{9,10},{10,... | collective-permute-start | bytes 589832 | tf_op jit(solution)/shard_map/ppermute | solution.py:933
  237.7 6.7 %copy-start.25 = (bf16[256,1024]{1,0:T(8,128)(2,1)}, bf16[256,1024]{1,0:T(8,128)(2,1)S(1)}, u32[]{:S(2)}) copy-start(bf16[256,1024]{1,0:T(8,128)(2,1)S(1)} %collective-permute-done.27.part_refs_1_) | copy-start | bytes 1572868
  249.3 5.0 %copy-start.43 = (f32[3,32]{1,0:T(4,128)S(1)}, f32[3,32]{1,0:T(4,128)}, u32[]{:S(2)}) copy-start(f32[3,32]{1,0:T(4,128)} %param.41) | copy-start | bytes 1156
  249.4 5.6 %copy-start.41 = (f32[384]{0:T(512)S(1)}, f32[384]{0:T(512)}, u32[]{:S(2)}) copy-start(f32[384]{0:T(512)} %gain_ref.1) | copy-start | bytes 4612
  249.4 5.5 %copy-start.45 = (f32[384]{0:T(512)S(1)}, f32[384]{0:T(512)}, u32[]{:S(2)}) copy-start(f32[384]{0:T(512)} %param.39) | copy-start | bytes 4612
  249.4 5.5 %copy-start.46 = (f32[384]{0:T(512)S(1)}, f32[384]{0:T(512)}, u32[]{:S(2)}) copy-start(f32[384]{0:T(512)} %param.40) | copy-start | bytes 4612
  249.4 6.2 %copy-start.31 = (f32[5,288]{1,0:T(8,128)S(1)}, f32[5,288]{1,0:T(8,128)}, u32[]{:S(2)}) copy-start(f32[5,288]{1,0:T(8,128)} %conv_ref.1) | copy-start | bytes 17284
  249.4 6.2 %copy-start.39 = (f32[5,288]{1,0:T(8,128)S(1)}, f32[5,288]{1,0:T(8,128)}, u32[]{:S(2)}) copy-start(f32[5,288]{1,0:T(8,128)} %param.37) | copy-start | bytes 17284
  249.4 6.2 %copy-start.40 = (f32[5,288]{1,0:T(8,128)S(1)}, f32[5,288]{1,0:T(8,128)}, u32[]{:S(2)}) copy-start(f32[5,288]{1,0:T(8,128)} %param.38) | copy-start | bytes 17284
  249.4 6.9 %copy-start.27 = (bf16[192,512]{1,0:T(8,128)(2,1)}, bf16[192,512]{1,0:T(8,128)(2,1)S(1)}, u32[]{:S(2)}) copy-start(bf16[192,512]{1,0:T(8,128)(2,1)S(1)} %collective-permute-done.23.late_refs_1_) | copy-start | bytes 589828
  250.3 6.1 %copy-start.28 = (bf16[192,512]{1,0:T(8,128)(2,1)}, bf16[192,512]{1,0:T(8,128)(2,1)S(1)}, u32[]{:S(2)}) copy-start(bf16[192,512]{1,0:T(8,128)(2,1)S(1)} %collective-permute-done.24.late_refs_2_) | copy-start | bytes 589828
  250.9 5.4 %copy-start.29 = (bf16[192,512]{1,0:T(8,128)(2,1)}, bf16[192,512]{1,0:T(8,128)(2,1)S(1)}, u32[]{:S(2)}) copy-start(bf16[192,512]{1,0:T(8,128)(2,1)S(1)} %collective-permute-done.25.late_refs_3_) | copy-start | bytes 589828
  (17 other events, 29.6 us)

commit v11 on v9

--- a/solution.py
+++ b/solution.py
@@ -451,7 +451,7 @@
     inner_ref,
     gate_ref,
     ng_ref,
-    stat_ref,
+    stat_refs,
     gain_ref,
     mixed_ref,
     wout_ref,
@@ -476,8 +476,9 @@
         sums_ref[...] = jnp.zeros_like(sums_ref)
 
     same = diagonal(span)
-    squares = jnp.sum(jnp.where(same, stat_ref[0:1], 0.0), axis=1, keepdims=True)
-    cross = jnp.sum(jnp.where(same, stat_ref[1:2], 0.0), axis=1, keepdims=True)
+    stats = sum(ref[...] for ref in stat_refs)
+    squares = jnp.sum(jnp.where(same, stats[0:1], 0.0), axis=1, keepdims=True)
+    cross = jnp.sum(jnp.where(same, stats[1:2], 0.0), axis=1, keepdims=True)
     inv = lax.rsqrt(squares * (1.0 / INNER) + NORM_EPS)
     gain_sum = jnp.zeros((1, width), F32)
     skip_sum = jnp.zeros((1, width), F32)
@@ -1016,12 +1017,21 @@
         compiler_params=params(),
         name="pack",
     )(bits, in_weight, out_weight, dt_weight, conv_params, gains)
+    ids = segment_ids[0]
+    seg_col = jnp.pad(ids, (8, 8), constant_values=-1)[:, None]
+    seg_row = segment_ids
+    head_mine = lax.dynamic_index_in_dim(head_params.reshape(3, heads, nctx), c, 2, False)
+    head_col = head_mine.T
     cot_low = cotangent[0].astype(BF16)
     if near:
         tok_far = swap(tok, "ctx", 2)
         tok_core = swap(tok, "ctx", 1)
         w1 = high_all_to_all(w1)
-        w1, g2, cot_low = lax.optimization_barrier((w1, g2, cot_low))
+        at_rows = jnp.stack([d & 1, 1 - (d & 1)]).astype(jnp.int32)
+        w1, g2, cot_low, seg_col, head_mine, head_col, at_rows, perm = lax.optimization_barrier(
+            (w1, g2, cot_low, seg_col, head_mine, head_col, at_rows, perm)
+        )
+        at_g2 = at_rows
         w1_came = swap(w1, "dp", 1)
         g2 = high_all_to_all(g2)
         w1, w1_came, tok_far = lax.optimization_barrier((w1, w1_came, tok_far))
@@ -1030,7 +1040,6 @@
         w1 = [w1, w1_came]
         g2 = [g2, swap(g2, "dp", 1)]
         cots = fan_ctx(cot_low)
-        at_rows = at_g2 = jnp.stack([d & 1, 1 - (d & 1)]).astype(jnp.int32)
     else:
         w1 = [lax.all_gather(w1[0], "dp", axis=0)]
         toks = gather_ctx(tok)
@@ -1040,12 +1049,6 @@
         wout = lax.dynamic_index_in_dim(wout.reshape(heads, nctx, HEAD_DIM, model), c, 1, False)
         g2 = [jnp.concatenate([wg, wout[:, :, :width], wout[:, :, width:]], axis=1)]
         at_rows = at_g2 = jnp.zeros((1,), jnp.int32)
-
-    ids = segment_ids[0]
-    seg_col = jnp.pad(ids, (8, 8), constant_values=-1)[:, None]
-    seg_row = segment_ids
-    head_mine = lax.dynamic_index_in_dim(head_params.reshape(3, heads, nctx), c, 2, False)
-    head_col = head_mine.T
 
     rows = lambda cols: pl.BlockSpec((span, cols), lambda i, *_: (i, 0))
     row_of = pl.BlockSpec((heads, span), lambda i, *_: (0, i))
@@ -1152,7 +1155,7 @@
         compiler_params=params("arbitrary"),
         name="gate",
     )(bits, at_g2, hid, g2, cots, inner, gain_mine)
-    stats = sum(fan_ctx(stats))
+    stats = fan_ctx(stats)
 
     early_rows = block_in + 2 * HEAD_DIM
     blocks_out, early_keep, early_send, dy, dgate, col_sums = pl.pallas_call(
@@ -1165,7 +1168,7 @@
                 rows_at(width),
                 rows_at(width),
                 rows_at(width),
-                pl.BlockSpec((8, span), lambda i, p, *_: (0, p[i])),
+                [pl.BlockSpec((8, span), lambda i, p, *_: (0, p[i]))] * nctx,
                 full((1, width)),
                 rows_at(width),
                 full((width, model)),
@@ -1267,8 +1270,6 @@
     dbc = (dbc.astype(F32) + dbc_came.astype(F32)).astype(BF16)
     dval, dbc = lax.optimization_barrier((dval, dbc))
     dbc_far = swap(dbc, "ctx", 2)
-    if near:
-        dbc_far, late_came = lax.optimization_barrier((dbc_far, late_came))
 
     hidden_out, gain_sum = pl.pallas_call(
         hidden_back_kernel,
@@ -1362,7 +1363,11 @@
 
     late_rows = block_in + 64
     if near:
+        early = jnp.sum(early_parts.astype(F32), axis=0).astype(BF16)
         map_came = swap(map_send, "dp", 1)
+        map_came, block_output, early, hidden_out = lax.optimization_barrier(
+            (map_came, block_output, early, hidden_out)
+        )
         late_parts = pl.pallas_call(
             pair_sum_late_kernel,
             out_shape=shape_of(high, late_rows, width, dtype=BF16),
@@ -1370,8 +1375,8 @@
             name="pair_sum_late",
         )(late_keep, late_came, map_keep, map_came)
         late_parts = high_all_to_all(late_parts)
-        early = jnp.sum(early_parts.astype(F32), axis=0).astype(BF16)
         early = gather_ctx(early)
+        input_grad = input_part(hidden_out, hidden_own)
         row_block = lambda ref_rows, cols: pl.BlockSpec((ref_rows, cols), lambda i, *_: (i, 0))
         out_block = row_block(out_weight.shape[0] // nctx, model)
         early_spec = [full((early_rows, width))] * nctx
@@ -1390,7 +1395,7 @@
             name="adam_out",
         )(bits, out_weight, out_first, out_second, early)
 
-        late_parts, block_output, out_new = lax.optimization_barrier((late_parts, block_output, out_new))
+        late_parts, input_grad, out_new = lax.optimization_barrier((late_parts, input_grad, out_new))
         late = pl.pallas_call(
             sum_late_kernel,
             out_shape=shape_of(late_rows, width, dtype=BF16),
@@ -1398,8 +1403,6 @@
             name="sum_late",
         )(late_parts)
         late = fan_ctx(late)
-        input_grad = input_part(hidden_out, hidden_own)
-        late, input_grad = lax.optimization_barrier((late, input_grad))
         in_block = row_block(32, in_weight.shape[1])
         in_new = pl.pallas_call(
             adam_in_kernel,

time: 244 us -> 248 us (1.016)
  waiting for transfers between devices: 75.9 us -> 82.4 us
  other arithmetic: 10.6 us -> 7.74 us
    ppermute x28, waiting for transfers between devices: 46.2 us -> 51.6 us  [swap(): return lax.ppermute(value, axis, [(at, at ^ bit) for at in range(count)])]
    unnamed x83 -> x99, local copies, waits for them, and re-layouts: 5.68 us -> 6.6 us
  transfers between devices with their start and end apart: 32 -> 32, of which waited for: 15 -> 14; matrix products, arithmetic and copies ran while one was open for 3% -> 3% of each run, Pallas kernels for 29% -> 27%
where the time goes in v11:
time: 248 us; the launch traced here: 247 us
  Pallas kernels  108 us (44%)
  waiting for transfers between devices  82.4 us (33%)
  starting transfers between devices  36 us (15%)
  local copies, waits for them, and re-layouts  11 us (4%)
  other arithmetic  7.74 us (3%)
    ppermute x28, waiting for transfers between devices, swap(): return lax.ppermute(value, axis, [(at, at ^ bit) for at in range(count)])  51.6 us
    all_to_all x4, waiting for transfers between devices, high_all_to_all(): return lax.all_to_all(value, 'dp', 0, 0, axis_index_groups=groups)  30.8 us
    pallas_call x1, Pallas kernels, shards(): pl.pallas_call(scan_back_kernel, grid_spec=pltpu.PrefetchScalarGridSpec(n...  22.9 us
    pallas_call x1, Pallas kernels, shards(): pl.pallas_call(scan_forward_kernel, grid_spec=pltpu.PrefetchScalarGridSpe...  18.8 us
    all_to_all x4, starting transfers between devices, high_all_to_all(): return lax.all_to_all(value, 'dp', 0, 0, axis_index_groups=groups)  18.1 us
    ppermute x28, starting transfers between devices, swap(): return lax.ppermute(value, axis, [(at, at ^ bit) for at in range(count)])  17.9 us
    pallas_call x1, Pallas kernels, shards(): pl.pallas_call(norm_back_kernel, grid_spec=pltpu.PrefetchScalarGridSpec(n...  14.2 us
    pallas_call x1, Pallas kernels, shards(): pl.pallas_call(gate_kernel, grid_spec=pltpu.PrefetchScalarGridSpec(num_sc...  10.7 us
  transfers between devices with their start and end apart: 32, of which 14 were waited for; matrix products, arithmetic and copies ran while one was open for 3% of the time, Pallas kernels for 27%

profile of v11, /device:TPU:0, one launch (start us, length us, event | category | flops | bytes accessed | tf_op | source)
XLA Modules:
  0.0 246.7 jit_solution(7513936263294763998)
XLA Ops:
  0.7 0.7 pad_add_fusion.here_ref
  1.3 3.6 %pack.1 = (bf16[4,144,768]{2,1,0:T(8,128)(2,1)}, bf16[4,256,512]{2,1,0:T(8,128)(2,1)}) custom-call(s32[3]{0:T(128)} %pad_add_fusion.here_ref, f32[128,4352]{1,0:T(8,128)} %weight_ref.3, f32[256,1024]{1,0:T(8,128)} %weight_ref.2, f32[32,128]{1,0:T(8,128)} %dt_ref.1, f32[5,288]{1,0:T(8,128)} %conv_ref.1, f32[384]{0:T(512)} %gain_ref.1), custom_call_target="tpu_custom_call" | custom-call | tf_op jit(solution)/shard_map/pack/pallas_call | solution.py:1009
  4.9 6.5 %all-to-all-start = ((bf16[4,144,768]{2,1,0:T(8,128)(2,1)}), bf16[4,144,768]{2,1,0:T(8,128)(2,1)}, u32[]{:S(2)}, u32[]{:S(2)}) async-start(bf16[4,144,768]{2,1,0:T(8,128)(2,1)} %get-tuple-element.114), calls=%async_computation | async-start | bytes 1769472 | tf_op jit(solution)/shard_map/all_to_all | solution.py:932
  11.4 1.5 collective-permute-start.1
  13.0 0.6 broadcast_xor_fusion.perm_ref
  13.8 0.7 copy.66
  14.6 0.6 pad_add_fusion.1.at_ref
  15.1 18.5 %all-to-all-done.w1_pieces_0_ = bf16[4,144,768]{2,1,0:T(8,128)(2,1)} async-done(((bf16[4,144,768]{2,1,0:T(8,128)(2,1)}), bf16[4,144,768]{2,1,0:T(8,128)(2,1)}, u32[]{:S(2)}, u32[]{:S(2)}) %all-to-all-start) | async-done | bytes 884768 | tf_op jit(solution)/shard_map/all_to_all | solution.py:932
  33.7 1.5 collective-permute-start
  35.2 3.5 %all-to-all-start.1 = ((bf16[4,256,512]{2,1,0:T(8,128)(2,1)}), bf16[4,256,512]{2,1,0:T(8,128)(2,1)S(1)}, u32[]{:S(2)}, u32[]{:S(2)}) async-start(bf16[4,256,512]{2,1,0:T(8,128)(2,1)} %get-tuple-element.122), calls=%async_computation.1 | async-start | bytes 2097152 | tf_op jit(solution)/shard_map/all_to_all | solution.py:932
  38.8 15.7 %collective-permute-done.w1_pieces_1_ = bf16[4,144,768]{2,1,0:T(8,128)(2,1)S(1)} collective-permute-done((bf16[4,144,768]{2,1,0:T(8,128)(2,1)}, bf16[4,144,768]{2,1,0:T(8,128)(2,1)S(1)}, u32[]{:S(2)}, u32[]{:S(2)}) %collective-permute-start) | collective-permute-done | bytes 884768 | tf_op jit(solution)/shard_map/ppermute | solution.py:921
  54.5 9.1 %all-to-all-done.1.g2_pieces_0_ = bf16[4,256,512]{2,1,0:T(8,128)(2,1)S(1)} async-done(((bf16[4,256,512]{2,1,0:T(8,128)(2,1)}), bf16[4,256,512]{2,1,0:T(8,128)(2,1)S(1)}, u32[]{:S(2)}, u32[]{:S(2)}) %all-to-all-start.1) | async-done | bytes 1048608 | tf_op jit(solution)/shard_map/all_to_all | solution.py:932
  63.6 0.5 collective-permute-start.4
  64.2 1.5 collective-permute-start.6
  66.0 1.0 copy.67.segc_ref
  67.1 18.8 %scan_forward.1 = (bf16[1024,1024]{1,0:T(8,128)(2,1)}, f32[8,768]{1,0:T(8,128)}, f32[1,1024]{1,0:T(1,128)}, f32[1,512]{1,0:T(1,128)}, bf16[8,1024]{1,0:T(8,128)(...) custom-call(s32[3]{0:T(128)} %pad_add_fusion.here_ref, ...), custom_call_target="tpu_custom_call" | custom-call | tf_op jit(solution)/shard_map/scan_forward/pallas_call | solution.py:1062
  85.9 3.6 %collective-permute-done.7.cot_pieces_3_ = bf16[256,1024]{1,0:T(8,128)(2,1)} collective-permute-done((bf16[256,1024]{1,0:T(8,128)(2,1)S(1)}, bf16[256,1024]{1,0:T(8,128)(2,1)}, u32[]{:S(2)}, u32[]{:S(2)}) %collective-permute-start.7) | collective-permute-done | bytes 524320 | tf_op jit(solution)/shard_map/ppermute | solution.py:921
  89.5 1.0 copy-done.9
  90.4 10.7 %gate.1 = (bf16[1024,512]{1,0:T(8,128)(2,1)}, bf16[512,1024]{1,0:T(8,128)(2,1)}, bf16[4,256,1024]{2,1,0:T(8,128)(2,1)}, bf16[1024,512]{1,0:T(8,128)(2,1)}, f32[1024,512]{1,0:T(8,128)}, /*index=5*/f32[8,1024]{1,0:T(8,128)}) custom-call(s32[3]{0:T(128)} %pad_add_fusion.here_ref, s32[2]{0:T(128)} %pad_add_fusion.1.at_ref, ...), custom_call_target="tpu_custom_call" | custom-call | tf_op jit(solution)/shard_map/gate/pallas_call | solution.py:1127
  101.2 1.4 collective-permute-start.10
  103.4 1.4 collective-permute-done.10.stat_refs_3_
  104.8 2.2 collective-permute-done.9.stat_refs_2_
  107.0 0.6 copy-done.36
  107.6 14.2 %norm_back.1 = (bf16[256,1024]{1,0:T(8,128)(2,1)}, bf16[256,1024]{1,0:T(8,128)(2,1)}, bf16[256,1024]{1,0:T(8,128)(2,1)}, bf16[256,1024]{1,0:T(8,128)(2,1)}, bf16...) custom-call(s32[4]{0:T(128)} %broadcast_xor_fusion.perm_ref, ...), custom_call_target="tpu_custom_call" | custom-call | tf_op jit(solution)/shard_map/norm_back/pallas_call | solution.py:1161
  121.8 1.6 collective-permute-start.11
  123.9 1.4 collective-permute-start.14
  125.3 22.9 %scan_back.1 = (bf16[4,128,512]{2,1,0:T(8,128)(2,1)}, bf16[4,128,512]{2,1,0:T(8,128)(2,1)}, bf16[1024,512]{1,0:T(8,128)(2,1)}, bf16[1024,256]{1,0:T(8,128)(2,1)}...) custom-call(s32[4]{0:T(128)} %broadcast_xor_fusion.perm_ref, ...), custom_call_target="tpu_custom_call" | custom-call | tf_op jit(solution)/shard_map/scan_back/pallas_call | solution.py:1208
  148.8 0.6 copy-done.21
  149.7 1.3 add_convert_fusion
  151.0 3.5 %all-to-all-start.2 = ((bf16[4,256,512]{2,1,0:T(8,128)(2,1)}), bf16[4,256,512]{2,1,0:T(8,128)(2,1)S(1)}, u32[]{:S(2)}, u32[]{:S(2)}) async-start(bf16[4,256,512]{2,1,0:T(8,128)(2,1)} %add_convert_fusion), calls=%async_computation.2 | async-start | bytes 2097152 | tf_op jit(solution)/shard_map/all_to_all | solution.py:932
  154.7 0.5 collective-permute-start.16
  155.2 9.0 %hidden_back.1 = (bf16[256,1024]{1,0:T(8,128)(2,1)}, bf16[256,1024]{1,0:T(8,128)(2,1)}, bf16[256,1024]{1,0:T(8,128)(2,1)}, bf16[256,1024]{1,0:T(8,128)(2,1)}, f32[8,1024]{1,0:T(8,128)}) custom-call(s32[4]{0:T(128)} %broadcast_xor_fusion.perm_ref, bf16[1024,512]{1,0:T(8,128)(2,1)} %get-tuple-element.169.dgate_ref, ...), custom_call_target="tpu_custom_call" | custom-call | tf_op jit(solution)/shard_map/hidden_back/pallas_call | solution.py:1274
  164.2 1.6 collective-permute-start.19
  166.1 0.6 collective-permute-start.21
  166.7 2.8 %collective-permute-done.16.dbcfar_ref = bf16[1024,256]{1,0:T(8,128)(2,1)S(1)} collective-permute-done((bf16[1024,256]{1,0:T(8,128)(2,1)S(1)}, bf16[1024,256]{1,0:T(8,128)(2,1)S(1)}, u32[]{:S(2)}, u32[]{:S(2)}) %collective-permute-start.16) | collective-permute-done | bytes 524320 | tf_op jit(solution)/shard_map/ppermute | solution.py:921
  169.5 0.8 copy-done.15
  170.3 6.6 %maps_back.1 = (bf16[160,512]{1,0:T(8,128)(2,1)}, bf16[160,512]{1,0:T(8,128)(2,1)}, f32[256,1024]{1,0:T(8,128)}) custom-call(s32[3]{0:T(128)} %pad_add_fusion.here_ref, bf16[1024,256]{1,0:T(8,128)(2,1)} %copy-done.7, bf16[1024,256]{1,0:T(8,128)(2,1)} %copy-done.15, f32[1024,768]{1,0:T(8,128)} %get-tuple-element.151.convsum_ref, ...), custom_call_target="tpu_custom_call" | custom-call | tf_op jit(solution)/shard_map/maps_back/pallas_call | solution.py:1302
  176.9 0.5 collective-permute-start.17
  177.5 1.4 add_add_fusion
  178.8 2.0 all-to-all-done.2
  181.1 9.4 %collective-permute-done.20.part_refs_2_ = bf16[256,1024]{1,0:T(8,128)(2,1)S(1)} collective-permute-done((bf16[256,1024]{1,0:T(8,128)(2,1)}, bf16[256,1024]{1,0:T(8,128)(2,1)S(1)}, u32[]{:S(2)}, u32[]{:S(2)}) %collective-permute-start.20) | collective-permute-done | bytes 524320 | tf_op jit(solution)/shard_map/ppermute | solution.py:921
  190.6 0.8 copy-done.16
  191.4 2.3 pair_sum_late.1
  193.7 4.6 %all-to-all-start.3 = ((bf16[4,192,512]{2,1,0:T(8,128)(2,1)}), bf16[4,192,512]{2,1,0:T(8,128)(2,1)S(1)}, u32[]{:S(2)}, u32[]{:S(2)}) async-start(bf16[4,192,512]{2,1,0:T(8,128)(2,1)} %pair_sum_late.1), calls=%async_computation.3 | async-start | bytes 1572864 | tf_op jit(solution)/shard_map/all_to_all | solution.py:932
  198.3 1.0 collective-permute-start.23
  199.3 7.6 %collective-permute-done.23.early_refs_2_ = bf16[256,512]{1,0:T(8,128)(2,1)S(1)} collective-permute-done((bf16[256,512]{1,0:T(8,128)(2,1)S(1)}, bf16[256,512]{1,0:T(8,128)(2,1)S(1)}, u32[]{:S(2)}, u32[]{:S(2)}) %collective-permute-start.23) | collective-permute-done | bytes 262176 | tf_op jit(solution)/shard_map/ppermute | solution.py:921
  207.0 4.2 %input_back.1 = f32[256,1024]{1,0:T(8,128)} custom-call(bf16[256,1024]{1,0:T(8,128)(2,1)} %copy-done.18, bf16[256,1024]{1,0:T(8,128)(2,1)} %copy-done.19, bf16[256,1024]{1,0:T(8,128)(2,1)} %copy-done.20, bf16[256,1024]{1,0:T(8,128)(2,1)} %get-tuple-element.194.part_refs_3_, f32[256,1024]{1,0:T(8,128)} %get-tuple-element.195.own_ref, f32[256,1024]{1,0:T(8,128)} %bitcast.45, ...), custom_call_target="tpu_custom_call" | custom-call | tf_op jit(solution)/shard_map/input_back/pallas_call | solution.py:1356
  211.2 0.7 copy-done.11
  211.9 0.7 copy-done.12
  212.6 5.5 %adam_out.1 = (f32[256,1024]{1,0:T(8,128)}, f32[256,1024]{1,0:T(8,128)}, f32[256,1024]{1,0:T(8,128)}) custom-call(s32[3]{0:T(128)} %pad_add_fusion.here_ref, f32[256,1024]{1,0:T(8,128)} %weight_ref.2, f32[256,1024]{1,0:T(8,128)} %first_ref.2, f32[256,1024]{1,0:T(8,128)} %second_ref.2, bf16[256,512]{1,0:T(8,128)(2,1)} %copy-done.5, ...), custom_call_target="tpu_custom_call" | custom-call | tf_op jit(solution)/shard_map/adam_out/pallas_call | solution.py:1384
  218.2 1.1 all-to-all-done.3.parts_ref
  219.3 0.9 copy-done.4
  220.2 2.0 sum_late.1.late_refs_0_
  222.2 1.3 collective-permute-start.26
  223.5 0.6 collective-permute-start.25
  224.1 0.8 slice_bitcast_fusion.4
  224.8 4.8 %collective-permute-done.27.late_refs_3_ = bf16[192,512]{1,0:T(8,128)(2,1)S(1)} collective-permute-done((bf16[192,512]{1,0:T(8,128)(2,1)}, bf16[192,512]{1,0:T(8,128)(2,1)S(1)}, u32[]{:S(2)}, u32[]{:S(2)}) %collective-permute-start.27) | collective-permute-done | bytes 196640 | tf_op jit(solution)/shard_map/ppermute | solution.py:921
  229.6 3.8 %collective-permute-done.26.late_refs_2_ = bf16[192,512]{1,0:T(8,128)(2,1)S(1)} collective-permute-done((bf16[192,512]{1,0:T(8,128)(2,1)}, bf16[192,512]{1,0:T(8,128)(2,1)S(1)}, u32[]{:S(2)}, u32[]{:S(2)}) %collective-permute-start.26) | collective-permute-done | bytes 196640 | tf_op jit(solution)/shard_map/ppermute | solution.py:921
  233.5 0.6 gather_fusion
  235.5 0.6 multiply_subtract_fusion
  236.1 0.6 multiply_subtract_fusion.2
  236.8 0.7 multiply_subtract_fusion.3
  237.5 0.7 multiply_subtract_fusion.1
  238.2 8.3 %adam_in.1 = (f32[128,4352]{1,0:T(8,128)}, f32[128,4352]{1,0:T(8,128)}, f32[128,4352]{1,0:T(8,128)}) custom-call(s32[3]{0:T(128)} %pad_add_fusion.here_ref, f32[128,4352]{1,0:T(8,128)} %weight_ref.3, f32[128,4352]{1,0:T(8,128)} %first_ref.3, f32[128,4352]{1,0:T(8,128)} %second_ref.3, bf16[256,512]{1,0:T(8,128)(2,1)} %copy-done.5, ...), custom_call_target="tpu_custom_call" | custom-call | tf_op jit(solution)/shard_map/adam_in/pallas_call | solution.py:1407
  (161 shorter events, 5.2 us)
Async XLA Ops:
  1.3 10.1 %copy-start = (f32[1,256,1024]{2,1,0:T(8,128)S(1)}, f32[1,256,1024]{2,1,0:T(8,128)}, u32[]{:S(2)}) copy-start(f32[1,256,1024]{2,1,0:T(8,128)} %param.22) | copy-start | bytes 3145732
  1.3 11.6 %copy-start.3 = (f32[1,256,1024]{2,1,0:T(8,128)S(1)}, f32[1,256,1024]{2,1,0:T(8,128)}, u32[]{:S(2)}) copy-start(f32[1,256,1024]{2,1,0:T(8,128)} %param.24) | copy-start | bytes 3145732
  4.9 8.1 %copy-start.47 = (s32[4]{0:T(128)S(1)}, s32[4]{0:T(128)}, u32[]{:S(2)}) copy-start(s32[4]{0:T(128)} %constant.15.clone) | copy-start | bytes 52
  4.9 8.7 %copy-start.42 = (f32[3,32]{1,0:T(4,128)S(1)}, f32[3,32]{1,0:T(4,128)}, u32[]{:S(2)}) copy-start(f32[3,32]{1,0:T(4,128)} %param.30) | copy-start | bytes 1156
  4.9 9.6 %copy-start.32 = (s32[1,1024]{1,0:T(1,128)S(1)}, s32[1,1024]{1,0:T(1,128)}, u32[]{:S(2)}) copy-start(s32[1,1024]{1,0:T(1,128)} %segr_ref.3) | copy-start | bytes 12292
  4.9 28.8 %all-to-all-start = ((bf16[4,144,768]{2,1,0:T(8,128)(2,1)}), bf16[4,144,768]{2,1,0:T(8,128)(2,1)}, u32[]{:S(2)}, u32[]{:S(2)}) async-start(bf16[4,144,768]{2,1,0:T(8,128)(2,1)} %get-tuple-element.114), calls=%async_computation | async-start | bytes 1769472 | tf_op jit(solution)/shard_map/all_to_all | solution.py:932
  11.4 27.4 %collective-permute-start.1 = (f32[256,1024]{1,0:T(8,128)S(1)}, f32[256,1024]{1,0:T(8,128)}, u32[]{:S(2)}, u32[]{:S(2)}) collective-permute-start(f32[256,1024]{1,0:T(8,128)S(1)} %bitcast.46), channel_id=1, source_target_pairs={{0,2},{1,3},{2,0},{3,1},{4,6},{5,7},{6,4},{7,5},{8,10},{9,11},{10,... | collective-permute-start | bytes 3145736 | tf_op jit(solution)/shard_map/ppermute | solution.py:921
  13.0 72.9 %copy-start.6 = (bf16[256,1024]{1,0:T(8,128)(2,1)}, bf16[256,1024]{1,0:T(8,128)(2,1)S(1)}, u32[]{:S(2)}) copy-start(bf16[256,1024]{1,0:T(8,128)(2,1)S(1)} %bitcast_convert_fusion.cot_pieces_0_) | copy-start | bytes 1572868
  13.8 53.3 %copy-start.33 = (f32[3,8]{1,0:T(4,128)}, f32[3,8]{1,0:T(4,128)S(1)}, u32[]{:S(2)}) copy-start(f32[3,8]{1,0:T(4,128)S(1)} %dynamic-slice_reduce_fusion.hrow_ref) | copy-start | bytes 292
  33.7 20.8 %collective-permute-start = (bf16[4,144,768]{2,1,0:T(8,128)(2,1)}, bf16[4,144,768]{2,1,0:T(8,128)(2,1)S(1)}, u32[]{:S(2)}, u32[]{:S(2)}) collective-permute-start(bf16[4,144,768]{2,1,0:T(8,128)(2,1)} %all-to-all-done.w1_pieces_0_), channel_id=1, source_target_pairs={{0,4},{4,0},{8,12},{12,8},{16,20},{20,16},{24,28},{28,24},{1,5},{5... | collective-permute-start | bytes 2654216 | tf_op jit(solution)/shard_map/ppermute | solution.py:921
  35.2 28.4 %all-to-all-start.1 = ((bf16[4,256,512]{2,1,0:T(8,128)(2,1)}), bf16[4,256,512]{2,1,0:T(8,128)(2,1)S(1)}, u32[]{:S(2)}, u32[]{:S(2)}) async-start(bf16[4,256,512]{2,1,0:T(8,128)(2,1)} %get-tuple-element.122), calls=%async_computation.1 | async-start | bytes 2097152 | tf_op jit(solution)/shard_map/all_to_all | solution.py:932
  38.7 15.8 %collective-permute-start.2 = (f32[256,1024]{1,0:T(8,128)S(1)}, f32[256,1024]{1,0:T(8,128)}, u32[]{:S(2)}, u32[]{:S(2)}) collective-permute-start(f32[256,1024]{1,0:T(8,128)S(1)} %bitcast.47), channel_id=1, source_target_pairs={{0,1},{1,0},{2,3},{3,2},{4,5},{5,4},{6,7},{7,6},{8,9},{9,8},{10,11... | collective-permute-start | bytes 3145736 | tf_op jit(solution)/shard_map/ppermute | solution.py:921
  54.5 12.6 %copy-start.13 = (bf16[4,144,768]{2,1,0:T(8,128)(2,1)}, bf16[4,144,768]{2,1,0:T(8,128)(2,1)S(1)}, u32[]{:S(2)}) copy-start(bf16[4,144,768]{2,1,0:T(8,128)(2,1)S(1)} %collective-permute-done.w1_pieces_1_) | copy-start | bytes 2654212
  54.5 9.1 %collective-permute-start.3 = (f32[256,1024]{1,0:T(8,128)}, f32[256,1024]{1,0:T(8,128)}, u32[]{:S(2)}, u32[]{:S(2)}) collective-permute-start(f32[256,1024]{1,0:T(8,128)} %collective-permute-done.1.tok_pieces_2_), channel_id=1, source_target_pairs={{0,1},{1,0},{2,3},{3,2},{4,5},{5,4},{6,7},{7,6},{8,9},{9,8},{10,11... | collective-permute-start | bytes 3145736 | tf_op jit(solution)/shard_map/ppermute | solution.py:921
  63.6 22.2 %copy-start.2 = (bf16[4,256,512]{2,1,0:T(8,128)(2,1)}, bf16[4,256,512]{2,1,0:T(8,128)(2,1)S(1)}, u32[]{:S(2)}) copy-start(bf16[4,256,512]{2,1,0:T(8,128)(2,1)S(1)} %all-to-all-done.1.g2_pieces_0_) | copy-start | bytes 3145732
  63.6 25.8 %collective-permute-start.4 = (bf16[4,256,512]{2,1,0:T(8,128)(2,1)S(1)}, bf16[4,256,512]{2,1,0:T(8,128)(2,1)S(1)}, u32[]{:S(2)}, u32[]{:S(2)}) collective-permute-start(bf16[4,256,512]{2,1,0:T(8,128)(2,1)S(1)} %all-to-all-done.1.g2_pieces_0_), channel_id=1, source_target_pairs={{0,4},{4,0},{8,12},{12,8},{16,20},{20,16},{24,28},{28,24},{1,5},{5... | collective-permute-start | bytes 3145736 | tf_op jit(solution)/shard_map/ppermute | solution.py:921
  64.2 21.7 %collective-permute-start.5 = (bf16[256,1024]{1,0:T(8,128)(2,1)S(1)}, bf16[256,1024]{1,0:T(8,128)(2,1)}, u32[]{:S(2)}, u32[]{:S(2)}) collective-permute-start(bf16[256,1024]{1,0:T(8,128)(2,1)S(1)} %bitcast_convert_fusion.cot_pieces_0_), channel_id=1, source_target_pairs={{0,1},{1,0},{2,3},{3,2},{4,5},{5,4},{6,7},{7,6},{8,9},{9,8},{10,11... | collective-permute-start | bytes 1572872 | tf_op jit(solution)/shard_map/ppermute | solution.py:921
  64.2 21.7 %collective-permute-start.6 = (bf16[256,1024]{1,0:T(8,128)(2,1)S(1)}, bf16[256,1024]{1,0:T(8,128)(2,1)}, u32[]{:S(2)}, u32[]{:S(2)}) collective-permute-start(bf16[256,1024]{1,0:T(8,128)(2,1)S(1)} %bitcast_convert_fusion.cot_pieces_0_), channel_id=1, source_target_pairs={{0,2},{1,3},{2,0},{3,1},{4,6},{5,7},{6,4},{7,5},{8,10},{9,11},{10,... | collective-permute-start | bytes 1572872 | tf_op jit(solution)/shard_map/ppermute | solution.py:921
  65.7 23.8 %collective-permute-start.7 = (bf16[256,1024]{1,0:T(8,128)(2,1)S(1)}, bf16[256,1024]{1,0:T(8,128)(2,1)}, u32[]{:S(2)}, u32[]{:S(2)}) collective-permute-start(bf16[256,1024]{1,0:T(8,128)(2,1)S(1)} %bitcast_convert_fusion.cot_pieces_0_), channel_id=1, source_target_pairs={{0,3},{1,2},{2,1},{3,0},{4,7},{5,6},{6,5},{7,4},{8,11},{9,10},{10,... | collective-permute-start | bytes 1572872 | tf_op jit(solution)/shard_map/ppermute | solution.py:921
  101.2 3.6 %collective-permute-start.10 = (f32[8,1024]{1,0:T(8,128)}, f32[8,1024]{1,0:T(8,128)S(1)}, u32[]{:S(2)}, u32[]{:S(2)}) collective-permute-start(f32[8,1024]{1,0:T(8,128)} %get-tuple-element.140.stat_refs_0_), channel_id=1, source_target_pairs={{0,3},{1,2},{2,1},{3,0},{4,7},{5,6},{6,5},{7,4},{8,11},{9,10},{10,... | collective-permute-start | bytes 98312 | tf_op jit(solution)/shard_map/ppermute | solution.py:921
  102.6 2.2 collective-permute-start.8
  102.9 4.1 %collective-permute-start.9 = (f32[8,1024]{1,0:T(8,128)}, f32[8,1024]{1,0:T(8,128)S(1)}, u32[]{:S(2)}, u32[]{:S(2)}) collective-permute-start(f32[8,1024]{1,0:T(8,128)} %get-tuple-element.140.stat_refs_0_), channel_id=1, source_target_pairs={{0,2},{1,3},{2,0},{3,1},{4,6},{5,7},{6,4},{7,5},{8,10},{9,11},{10,... | collective-permute-start | bytes 98312 | tf_op jit(solution)/shard_map/ppermute | solution.py:921
  121.8 27.0 %collective-permute-start.11 = (bf16[4,256,512]{2,1,0:T(8,128)(2,1)}, bf16[4,256,512]{2,1,0:T(8,128)(2,1)S(1)}, u32[]{:S(2)}, u32[]{:S(2)}) collective-permute-start(bf16[4,256,512]{2,1,0:T(8,128)(2,1)} %get-tuple-element.144), channel_id=1, source_target_pairs={{0,4},{4,0},{8,12},{12,8},{16,20},{20,16},{24,28},{28,24},{1,5},{5... | collective-permute-start | bytes 3145736 | tf_op jit(solution)/shard_map/ppermute | solution.py:921
  123.4 25.2 %collective-permute-start.12 = (bf16[256,1024]{1,0:T(8,128)(2,1)}, bf16[256,1024]{1,0:T(8,128)(2,1)S(1)}, u32[]{:S(2)}, u32[]{:S(2)}) collective-permute-start(bf16[256,1024]{1,0:T(8,128)(2,1)} %get-tuple-element.145), channel_id=1, source_target_pairs={{0,1},{1,0},{2,3},{3,2},{4,5},{5,4},{6,7},{7,6},{8,9},{9,8},{10,11... | collective-permute-start | bytes 1572872 | tf_op jit(solution)/shard_map/ppermute | solution.py:921
  123.4 25.2 %collective-permute-start.13 = (bf16[256,1024]{1,0:T(8,128)(2,1)}, bf16[256,1024]{1,0:T(8,128)(2,1)S(1)}, u32[]{:S(2)}, u32[]{:S(2)}) collective-permute-start(bf16[256,1024]{1,0:T(8,128)(2,1)} %get-tuple-element.146), channel_id=1, source_target_pairs={{0,2},{1,3},{2,0},{3,1},{4,6},{5,7},{6,4},{7,5},{8,10},{9,11},{10,... | collective-permute-start | bytes 1572872 | tf_op jit(solution)/shard_map/ppermute | solution.py:921
  123.9 24.9 %collective-permute-start.14 = (bf16[256,1024]{1,0:T(8,128)(2,1)}, bf16[256,1024]{1,0:T(8,128)(2,1)S(1)}, u32[]{:S(2)}, u32[]{:S(2)}) collective-permute-start(bf16[256,1024]{1,0:T(8,128)(2,1)} %get-tuple-element.147), channel_id=1, source_target_pairs={{0,3},{1,2},{2,1},{3,0},{4,7},{5,6},{6,5},{7,4},{8,11},{9,10},{10,... | collective-permute-start | bytes 1572872 | tf_op jit(solution)/shard_map/ppermute | solution.py:921
  125.2 24.4 %copy-start.8 = (bf16[4,256,512]{2,1,0:T(8,128)(2,1)S(1)}, bf16[4,256,512]{2,1,0:T(8,128)(2,1)}, u32[]{:S(2)}) copy-start(bf16[4,256,512]{2,1,0:T(8,128)(2,1)} %get-tuple-element.180) | copy-start | bytes 3145732
  148.2 6.3 %collective-permute-start.15 = (bf16[1024,256]{1,0:T(8,128)(2,1)}, bf16[1024,256]{1,0:T(8,128)(2,1)S(1)}, u32[]{:S(2)}, u32[]{:S(2)}) collective-permute-start(bf16[1024,256]{1,0:T(8,128)(2,1)} %get-tuple-element.161), channel_id=1, source_target_pairs={{0,1},{1,0},{2,3},{3,2},{4,5},{5,4},{6,7},{7,6},{8,9},{9,8},{10,11... | collective-permute-start | bytes 1572872 | tf_op jit(solution)/shard_map/ppermute | solution.py:921
  151.0 29.9 %all-to-all-start.2 = ((bf16[4,256,512]{2,1,0:T(8,128)(2,1)}), bf16[4,256,512]{2,1,0:T(8,128)(2,1)S(1)}, u32[]{:S(2)}, u32[]{:S(2)}) async-start(bf16[4,256,512]{2,1,0:T(8,128)(2,1)} %add_convert_fusion), calls=%async_computation.2 | async-start | bytes 2097152 | tf_op jit(solution)/shard_map/all_to_all | solution.py:932
  154.6 9.5 %copy-start.7 = (bf16[1024,256]{1,0:T(8,128)(2,1)}, bf16[1024,256]{1,0:T(8,128)(2,1)S(1)}, u32[]{:S(2)}) copy-start(bf16[1024,256]{1,0:T(8,128)(2,1)S(1)} %add_convert_fusion.1.dbc_ref) | copy-start | bytes 1572868
  154.7 14.8 %collective-permute-start.16 = (bf16[1024,256]{1,0:T(8,128)(2,1)S(1)}, bf16[1024,256]{1,0:T(8,128)(2,1)S(1)}, u32[]{:S(2)}, u32[]{:S(2)}) collective-permute-start(bf16[1024,256]{1,0:T(8,128)(2,1)S(1)} %add_convert_fusion.1.dbc_ref), channel_id=1, source_target_pairs={{0,2},{1,3},{2,0},{3,1},{4,6},{5,7},{6,4},{7,5},{8,10},{9,11},{10,... | collective-permute-start | bytes 1572872 | tf_op jit(solution)/shard_map/ppermute | solution.py:921
  164.2 16.9 %collective-permute-start.18 = (bf16[256,1024]{1,0:T(8,128)(2,1)}, bf16[256,1024]{1,0:T(8,128)(2,1)S(1)}, u32[]{:S(2)}, u32[]{:S(2)}) collective-permute-start(bf16[256,1024]{1,0:T(8,128)(2,1)} %get-tuple-element.182), channel_id=1, source_target_pairs={{0,1},{1,0},{2,3},{3,2},{4,5},{5,4},{6,7},{7,6},{8,9},{9,8},{10,11... | collective-permute-start | bytes 1572872 | tf_op jit(solution)/shard_map/ppermute | solution.py:921
  164.2 16.9 %collective-permute-start.19 = (bf16[256,1024]{1,0:T(8,128)(2,1)}, bf16[256,1024]{1,0:T(8,128)(2,1)S(1)}, u32[]{:S(2)}, u32[]{:S(2)}) collective-permute-start(bf16[256,1024]{1,0:T(8,128)(2,1)} %get-tuple-element.183), channel_id=1, source_target_pairs={{0,2},{1,3},{2,0},{3,1},{4,6},{5,7},{6,4},{7,5},{8,10},{9,11},{10,... | collective-permute-start | bytes 1572872 | tf_op jit(solution)/shard_map/ppermute | solution.py:921
  165.9 24.7 %collective-permute-start.20 = (bf16[256,1024]{1,0:T(8,128)(2,1)}, bf16[256,1024]{1,0:T(8,128)(2,1)S(1)}, u32[]{:S(2)}, u32[]{:S(2)}) collective-permute-start(bf16[256,1024]{1,0:T(8,128)(2,1)} %get-tuple-element.184), channel_id=1, source_target_pairs={{0,3},{1,2},{2,1},{3,0},{4,7},{5,6},{6,5},{7,4},{8,11},{9,10},{10,... | collective-permute-start | bytes 1572872 | tf_op jit(solution)/shard_map/ppermute | solution.py:921
  166.1 24.4 %collective-permute-start.21 = (bf16[4,128,512]{2,1,0:T(8,128)(2,1)}, bf16[4,128,512]{2,1,0:T(8,128)(2,1)S(1)}, u32[]{:S(2)}, u32[]{:S(2)}) collective-permute-start(bf16[4,128,512]{2,1,0:T(8,128)(2,1)} %get-tuple-element.188), channel_id=1, source_target_pairs={{0,4},{4,0},{8,12},{12,8},{16,20},{20,16},{24,28},{28,24},{1,5},{5... | collective-permute-start | bytes 1572872 | tf_op jit(solution)/shard_map/ppermute | solution.py:921
  170.3 7.2 %copy-start.1 = (f32[1,256,1024]{2,1,0:T(8,128)S(1)}, f32[1,256,1024]{2,1,0:T(8,128)}, u32[]{:S(2)}) copy-start(f32[1,256,1024]{2,1,0:T(8,128)} %param.22) | copy-start | bytes 3145732
  170.3 7.2 %copy-start.17 = (bf16[256,1024]{1,0:T(8,128)(2,1)S(1)}, bf16[256,1024]{1,0:T(8,128)(2,1)}, u32[]{:S(2)}) copy-start(bf16[256,1024]{1,0:T(8,128)(2,1)} %get-tuple-element.179) | copy-start | bytes 1572868
  170.3 7.2 %copy-start.22 = (bf16[256,1024]{1,0:T(8,128)(2,1)S(1)}, bf16[256,1024]{1,0:T(8,128)(2,1)}, u32[]{:S(2)}) copy-start(bf16[256,1024]{1,0:T(8,128)(2,1)} %copy-done.21) | copy-start | bytes 1572868
  170.3 7.2 %copy-start.24 = (bf16[256,1024]{1,0:T(8,128)(2,1)S(1)}, bf16[256,1024]{1,0:T(8,128)(2,1)}, u32[]{:S(2)}) copy-start(bf16[256,1024]{1,0:T(8,128)(2,1)} %copy-done.23) | copy-start | bytes 1572868
  170.3 7.2 %copy-start.26 = (bf16[256,1024]{1,0:T(8,128)(2,1)S(1)}, bf16[256,1024]{1,0:T(8,128)(2,1)}, u32[]{:S(2)}) copy-start(bf16[256,1024]{1,0:T(8,128)(2,1)} %copy-done.25) | copy-start | bytes 1572868
  176.9 13.6 %collective-permute-start.17 = (bf16[160,512]{1,0:T(8,128)(2,1)}, bf16[160,512]{1,0:T(8,128)(2,1)}, u32[]{:S(2)}, u32[]{:S(2)}) collective-permute-start(bf16[160,512]{1,0:T(8,128)(2,1)} %get-tuple-element.175), channel_id=1, source_target_pairs={{0,4},{4,0},{8,12},{12,8},{16,20},{20,16},{24,28},{28,24},{1,5},{5... | collective-permute-start | bytes 491528 | tf_op jit(solution)/shard_map/ppermute | solution.py:921
  181.1 30.1 %copy-start.5 = (bf16[256,512]{1,0:T(8,128)(2,1)}, bf16[256,512]{1,0:T(8,128)(2,1)S(1)}, u32[]{:S(2)}) copy-start(bf16[256,512]{1,0:T(8,128)(2,1)S(1)} %reduce_sum.30.early_refs_0_) | copy-start | bytes 786436
  181.1 25.9 %copy-start.18 = (bf16[256,1024]{1,0:T(8,128)(2,1)}, bf16[256,1024]{1,0:T(8,128)(2,1)S(1)}, u32[]{:S(2)}) copy-start(bf16[256,1024]{1,0:T(8,128)(2,1)S(1)} %collective-permute-done.18.part_refs_0_) | copy-start | bytes 1572868
  181.1 25.9 %copy-start.19 = (bf16[256,1024]{1,0:T(8,128)(2,1)}, bf16[256,1024]{1,0:T(8,128)(2,1)S(1)}, u32[]{:S(2)}) copy-start(bf16[256,1024]{1,0:T(8,128)(2,1)S(1)} %collective-permute-done.19.part_refs_1_) | copy-start | bytes 1572868
  190.5 16.5 %copy-start.20 = (bf16[256,1024]{1,0:T(8,128)(2,1)}, bf16[256,1024]{1,0:T(8,128)(2,1)S(1)}, u32[]{:S(2)}) copy-start(bf16[256,1024]{1,0:T(8,128)(2,1)S(1)} %collective-permute-done.20.part_refs_2_) | copy-start | bytes 1572868
  193.7 25.6 %all-to-all-start.3 = ((bf16[4,192,512]{2,1,0:T(8,128)(2,1)}), bf16[4,192,512]{2,1,0:T(8,128)(2,1)S(1)}, u32[]{:S(2)}, u32[]{:S(2)}) async-start(bf16[4,192,512]{2,1,0:T(8,128)(2,1)} %pair_sum_late.1), calls=%async_computation.3 | async-start | bytes 1572864 | tf_op jit(solution)/shard_map/all_to_all | solution.py:932
  198.3 8.6 %collective-permute-start.23 = (bf16[256,512]{1,0:T(8,128)(2,1)S(1)}, bf16[256,512]{1,0:T(8,128)(2,1)S(1)}, u32[]{:S(2)}, u32[]{:S(2)}) collective-permute-start(bf16[256,512]{1,0:T(8,128)(2,1)S(1)} %reduce_sum.30.early_refs_0_), channel_id=1, source_target_pairs={{0,2},{1,3},{2,0},{3,1},{4,6},{5,7},{6,4},{7,5},{8,10},{9,11},{10,... | collective-permute-start | bytes 786440 | tf_op jit(solution)/shard_map/ppermute | solution.py:921
  199.3 11.9 %collective-permute-start.22 = (bf16[256,512]{1,0:T(8,128)(2,1)S(1)}, bf16[256,512]{1,0:T(8,128)(2,1)S(1)}, u32[]{:S(2)}, u32[]{:S(2)}) collective-permute-start(bf16[256,512]{1,0:T(8,128)(2,1)S(1)} %reduce_sum.30.early_refs_0_), channel_id=1, source_target_pairs={{0,1},{1,0},{2,3},{3,2},{4,5},{5,4},{6,7},{7,6},{8,9},{9,8},{10,11... | collective-permute-start | bytes 786440 | tf_op jit(solution)/shard_map/ppermute | solution.py:921
  207.0 4.3 %collective-permute-start.24 = (bf16[256,512]{1,0:T(8,128)(2,1)S(1)}, bf16[256,512]{1,0:T(8,128)(2,1)S(1)}, u32[]{:S(2)}, u32[]{:S(2)}) collective-permute-start(bf16[256,512]{1,0:T(8,128)(2,1)S(1)} %collective-permute-done.23.early_refs_2_), channel_id=1, source_target_pairs={{0,1},{1,0},{2,3},{3,2},{4,5},{5,4},{6,7},{7,6},{8,9},{9,8},{10,11... | collective-permute-start | bytes 786440 | tf_op jit(solution)/shard_map/ppermute | solution.py:921
  218.1 17.3 %copy-start.30 = (f32[32,128]{1,0:T(8,128)S(1)}, f32[32,128]{1,0:T(8,128)}, u32[]{:S(2)}) copy-start(f32[32,128]{1,0:T(8,128)} %dt_ref.1) | copy-start | bytes 49156
  218.1 17.3 %copy-start.37 = (f32[32,128]{1,0:T(8,128)S(1)}, f32[32,128]{1,0:T(8,128)}, u32[]{:S(2)}) copy-start(f32[32,128]{1,0:T(8,128)} %param.33) | copy-start | bytes 49156
  218.2 17.3 %copy-start.38 = (f32[32,128]{1,0:T(8,128)S(1)}, f32[32,128]{1,0:T(8,128)}, u32[]{:S(2)}) copy-start(f32[32,128]{1,0:T(8,128)} %param.34) | copy-start | bytes 49156
  220.2 16.0 %copy-start.43 = (f32[3,32]{1,0:T(4,128)S(1)}, f32[3,32]{1,0:T(4,128)}, u32[]{:S(2)}) copy-start(f32[3,32]{1,0:T(4,128)} %param.41) | copy-start | bytes 1156
  220.2 16.0 %copy-start.44 = (f32[3,32]{1,0:T(4,128)S(1)}, f32[3,32]{1,0:T(4,128)}, u32[]{:S(2)}) copy-start(f32[3,32]{1,0:T(4,128)} %param.42) | copy-start | bytes 1156
  220.2 16.6 %copy-start.41 = (f32[384]{0:T(512)S(1)}, f32[384]{0:T(512)}, u32[]{:S(2)}) copy-start(f32[384]{0:T(512)} %gain_ref.1) | copy-start | bytes 4612
  220.2 16.6 %copy-start.45 = (f32[384]{0:T(512)S(1)}, f32[384]{0:T(512)}, u32[]{:S(2)}) copy-start(f32[384]{0:T(512)} %param.39) | copy-start | bytes 4612
  220.2 16.6 %copy-start.46 = (f32[384]{0:T(512)S(1)}, f32[384]{0:T(512)}, u32[]{:S(2)}) copy-start(f32[384]{0:T(512)} %param.40) | copy-start | bytes 4612
  220.2 17.3 %copy-start.31 = (f32[5,288]{1,0:T(8,128)S(1)}, f32[5,288]{1,0:T(8,128)}, u32[]{:S(2)}) copy-start(f32[5,288]{1,0:T(8,128)} %conv_ref.1) | copy-start | bytes 17284
  220.2 17.2 %copy-start.39 = (f32[5,288]{1,0:T(8,128)S(1)}, f32[5,288]{1,0:T(8,128)}, u32[]{:S(2)}) copy-start(f32[5,288]{1,0:T(8,128)} %param.37) | copy-start | bytes 17284
  220.2 17.2 %copy-start.40 = (f32[5,288]{1,0:T(8,128)S(1)}, f32[5,288]{1,0:T(8,128)}, u32[]{:S(2)}) copy-start(f32[5,288]{1,0:T(8,128)} %param.38) | copy-start | bytes 17284
  222.2 7.4 %collective-permute-start.27 = (bf16[192,512]{1,0:T(8,128)(2,1)}, bf16[192,512]{1,0:T(8,128)(2,1)S(1)}, u32[]{:S(2)}, u32[]{:S(2)}) collective-permute-start(bf16[192,512]{1,0:T(8,128)(2,1)} %sum_late.1.late_refs_0_), channel_id=1, source_target_pairs={{0,3},{1,2},{2,1},{3,0},{4,7},{5,6},{6,5},{7,4},{8,11},{9,10},{10,... | collective-permute-start | bytes 589832 | tf_op jit(solution)/shard_map/ppermute | solution.py:921
  222.2 11.3 %collective-permute-start.26 = (bf16[192,512]{1,0:T(8,128)(2,1)}, bf16[192,512]{1,0:T(8,128)(2,1)S(1)}, u32[]{:S(2)}, u32[]{:S(2)}) collective-permute-start(bf16[192,512]{1,0:T(8,128)(2,1)} %sum_late.1.late_refs_0_), channel_id=1, source_target_pairs={{0,2},{1,3},{2,0},{3,1},{4,6},{5,7},{6,4},{7,5},{8,10},{9,11},{10,... | collective-permute-start | bytes 589832 | tf_op jit(solution)/shard_map/ppermute | solution.py:921
  223.5 10.0 %collective-permute-start.25 = (bf16[192,512]{1,0:T(8,128)(2,1)}, bf16[192,512]{1,0:T(8,128)(2,1)S(1)}, u32[]{:S(2)}, u32[]{:S(2)}) collective-permute-start(bf16[192,512]{1,0:T(8,128)(2,1)} %sum_late.1.late_refs_0_), channel_id=1, source_target_pairs={{0,1},{1,0},{2,3},{3,2},{4,5},{5,4},{6,7},{7,6},{8,9},{9,8},{10,11... | collective-permute-start | bytes 589832 | tf_op jit(solution)/shard_map/ppermute | solution.py:921
  229.6 8.5 %copy-start.27 = (bf16[192,512]{1,0:T(8,128)(2,1)}, bf16[192,512]{1,0:T(8,128)(2,1)S(1)}, u32[]{:S(2)}) copy-start(bf16[192,512]{1,0:T(8,128)(2,1)S(1)} %collective-permute-done.27.late_refs_3_) | copy-start | bytes 589828
  (16 other events, 31.1 us)

commit v12 on v11

--- a/solution.py
+++ b/solution.py
@@ -1296,7 +1296,9 @@
         compiler_params=params("arbitrary"),
         name="hidden_back",
     )(perm, dgate, dval, dstep, wg, w1, dt_mine, hid, gain_pre)
-    hidden_out = from_owners(hidden_out)
+    hidden_near = swap(hidden_out[0], "ctx", 1)
+    hidden_far = (hidden_out[1].astype(F32) + swap(hidden_out[2], "ctx", 1).astype(F32)).astype(BF16)
+    hidden_out = [hidden_out[3], hidden_near]
     map_rows = 32 + 32 * high
     map_cols = lambda size: pl.BlockSpec((size, maps), lambda i: (0, width // maps))
     map_keep, map_send, hidden_own = pl.pallas_call(
@@ -1355,7 +1357,7 @@
 
     input_part = lambda parts, own: pl.pallas_call(
         input_back_kernel,
-        in_specs=[[vmem] * nctx] + [vmem] * 4,
+        in_specs=[[vmem] * (nctx - 1)] + [vmem] * 4,
         out_shape=shape_of(span, model),
         compiler_params=params(),
         name="input_back",
@@ -1365,9 +1367,11 @@
     if near:
         early = jnp.sum(early_parts.astype(F32), axis=0).astype(BF16)
         map_came = swap(map_send, "dp", 1)
-        map_came, block_output, early, hidden_out = lax.optimization_barrier(
-            (map_came, block_output, early, hidden_out)
+        map_came, block_output, early, hidden_far = lax.optimization_barrier(
+            (map_came, block_output, early, hidden_far)
         )
+    hidden_out = hidden_out + [swap(hidden_far, "ctx", 2)]
+    if near:
         late_parts = pl.pallas_call(
             pair_sum_late_kernel,
             out_shape=shape_of(high, late_rows, width, dtype=BF16),
@@ -1376,7 +1380,6 @@
         )(late_keep, late_came, map_keep, map_came)
         late_parts = high_all_to_all(late_parts)
         early = gather_ctx(early)
-        input_grad = input_part(hidden_out, hidden_own)
         row_block = lambda ref_rows, cols: pl.BlockSpec((ref_rows, cols), lambda i, *_: (i, 0))
         out_block = row_block(out_weight.shape[0] // nctx, model)
         early_spec = [full((early_rows, width))] * nctx
@@ -1395,7 +1398,7 @@
             name="adam_out",
         )(bits, out_weight, out_first, out_second, early)
 
-        late_parts, input_grad, out_new = lax.optimization_barrier((late_parts, input_grad, out_new))
+        late_parts, out_new = lax.optimization_barrier((late_parts, out_new))
         late = pl.pallas_call(
             sum_late_kernel,
             out_shape=shape_of(late_rows, width, dtype=BF16),
@@ -1403,6 +1406,8 @@
             name="sum_late",
         )(late_parts)
         late = fan_ctx(late)
+        input_grad = input_part(hidden_out, hidden_own)
+        late, input_grad = lax.optimization_barrier((late, input_grad))
         in_block = row_block(32, in_weight.shape[1])
         in_new = pl.pallas_call(
             adam_in_kernel,

time: 248 us -> 239 us (0.964)
  waiting for transfers between devices: 82.4 us -> 74.2 us
    ppermute x28, waiting for transfers between devices: 51.6 us -> 39.8 us  [swap(): return lax.ppermute(value, axis, [(at, at ^ bit) for at in range(count)])]
    all_to_all x4, waiting for transfers between devices: 30.8 us -> 34.4 us  [high_all_to_all(): return lax.all_to_all(value, 'dp', 0, 0, axis_index_groups=groups)]
    unnamed x99 -> x97, local copies, waits for them, and re-layouts: 6.6 us -> 6.71 us
  transfers between devices with their start and end apart: 32 -> 32, of which waited for: 14 -> 15; matrix products, arithmetic and copies ran while one was open for 3% -> 3% of each run, Pallas kernels for 27% -> 29%
where the time goes in v12:
time: 239 us; the launch traced here: 238 us
  Pallas kernels  108 us (45%)
  waiting for transfers between devices  74.2 us (31%)
  starting transfers between devices  35.9 us (15%)
  local copies, waits for them, and re-layouts  11.1 us (5%)
  other arithmetic  7.83 us (3%)
    ppermute x28, waiting for transfers between devices, swap(): return lax.ppermute(value, axis, [(at, at ^ bit) for at in range(count)])  39.8 us
    all_to_all x4, waiting for transfers between devices, high_all_to_all(): return lax.all_to_all(value, 'dp', 0, 0, axis_index_groups=groups)  34.4 us
    pallas_call x1, Pallas kernels, shards(): pl.pallas_call(scan_back_kernel, grid_spec=pltpu.PrefetchScalarGridSpec(n...  22.9 us
    pallas_call x1, Pallas kernels, shards(): pl.pallas_call(scan_forward_kernel, grid_spec=pltpu.PrefetchScalarGridSpe...  18.8 us
    all_to_all x4, starting transfers between devices, high_all_to_all(): return lax.all_to_all(value, 'dp', 0, 0, axis_index_groups=groups)  18.5 us
    ppermute x28, starting transfers between devices, swap(): return lax.ppermute(value, axis, [(at, at ^ bit) for at in range(count)])  17.4 us
    pallas_call x1, Pallas kernels, shards(): pl.pallas_call(norm_back_kernel, grid_spec=pltpu.PrefetchScalarGridSpec(n...  14.2 us
    pallas_call x1, Pallas kernels, shards(): pl.pallas_call(gate_kernel, grid_spec=pltpu.PrefetchScalarGridSpec(num_sc...  10.7 us
  transfers between devices with their start and end apart: 32, of which 15 were waited for; matrix products, arithmetic and copies ran while one was open for 3% of the time, Pallas kernels for 29%

profile of v12, /device:TPU:0, one launch (start us, length us, event | category | flops | bytes accessed | tf_op | source)
XLA Modules:
  0.0 238.3 jit_solution(16383670223535006909)
XLA Ops:
  0.7 0.6 pad_add_fusion.here_ref
  1.2 3.6 %pack.1 = (bf16[4,144,768]{2,1,0:T(8,128)(2,1)}, bf16[4,256,512]{2,1,0:T(8,128)(2,1)}) custom-call(s32[3]{0:T(128)} %pad_add_fusion.here_ref, f32[128,4352]{1,0:T(8,128)} %weight_ref.3, f32[256,1024]{1,0:T(8,128)} %weight_ref.2, f32[32,128]{1,0:T(8,128)} %dt_ref.1, f32[5,288]{1,0:T(8,128)} %conv_ref.1, f32[384]{0:T(512)} %gain_ref.1), custom_call_target="tpu_custom_call" | custom-call | tf_op jit(solution)/shard_map/pack/pallas_call | solution.py:1009
  4.8 6.5 %all-to-all-start = ((bf16[4,144,768]{2,1,0:T(8,128)(2,1)}), bf16[4,144,768]{2,1,0:T(8,128)(2,1)S(1)}, u32[]{:S(2)}, u32[]{:S(2)}) async-start(bf16[4,144,768]{2,1,0:T(8,128)(2,1)} %get-tuple-element.115), calls=%async_computation | async-start | bytes 1769472 | tf_op jit(solution)/shard_map/all_to_all | solution.py:932
  11.3 1.5 collective-permute-start.1
  12.9 0.6 broadcast_xor_fusion.perm_ref
  13.7 0.7 copy.66
  14.5 0.6 pad_add_fusion.1.at_ref
  15.0 18.4 %all-to-all-done.w1_pieces_0_ = bf16[4,144,768]{2,1,0:T(8,128)(2,1)S(1)} async-done(((bf16[4,144,768]{2,1,0:T(8,128)(2,1)}), bf16[4,144,768]{2,1,0:T(8,128)(2,1)S(1)}, u32[]{:S(2)}, u32[]{:S(2)}) %all-to-all-start) | async-done | bytes 884768 | tf_op jit(solution)/shard_map/all_to_all | solution.py:932
  33.5 1.5 collective-permute-start
  35.0 3.5 %all-to-all-start.1 = ((bf16[4,256,512]{2,1,0:T(8,128)(2,1)}), bf16[4,256,512]{2,1,0:T(8,128)(2,1)S(1)}, u32[]{:S(2)}, u32[]{:S(2)}) async-start(bf16[4,256,512]{2,1,0:T(8,128)(2,1)} %get-tuple-element.123), calls=%async_computation.1 | async-start | bytes 2097152 | tf_op jit(solution)/shard_map/all_to_all | solution.py:932
  38.6 15.6 %collective-permute-done.w1_pieces_1_ = bf16[4,144,768]{2,1,0:T(8,128)(2,1)} collective-permute-done((bf16[4,144,768]{2,1,0:T(8,128)(2,1)S(1)}, bf16[4,144,768]{2,1,0:T(8,128)(2,1)}, u32[]{:S(2)}, u32[]{:S(2)}) %collective-permute-start) | collective-permute-done | bytes 884768 | tf_op jit(solution)/shard_map/ppermute | solution.py:921
  54.2 9.2 %all-to-all-done.1.g2_pieces_0_ = bf16[4,256,512]{2,1,0:T(8,128)(2,1)S(1)} async-done(((bf16[4,256,512]{2,1,0:T(8,128)(2,1)}), bf16[4,256,512]{2,1,0:T(8,128)(2,1)S(1)}, u32[]{:S(2)}, u32[]{:S(2)}) %all-to-all-start.1) | async-done | bytes 1048608 | tf_op jit(solution)/shard_map/all_to_all | solution.py:932
  63.4 0.5 collective-permute-start.4
  64.0 1.5 collective-permute-start.6
  65.8 1.0 copy.67.segc_ref
  66.9 18.8 %scan_forward.1 = (bf16[1024,1024]{1,0:T(8,128)(2,1)}, f32[8,768]{1,0:T(8,128)}, f32[1,1024]{1,0:T(1,128)}, f32[1,512]{1,0:T(1,128)}, bf16[8,1024]{1,0:T(8,128)(...) custom-call(s32[3]{0:T(128)} %pad_add_fusion.here_ref, ...), custom_call_target="tpu_custom_call" | custom-call | tf_op jit(solution)/shard_map/scan_forward/pallas_call | solution.py:1062
  85.7 3.6 %collective-permute-done.7.cot_pieces_3_ = bf16[256,1024]{1,0:T(8,128)(2,1)} collective-permute-done((bf16[256,1024]{1,0:T(8,128)(2,1)S(1)}, bf16[256,1024]{1,0:T(8,128)(2,1)}, u32[]{:S(2)}, u32[]{:S(2)}) %collective-permute-start.7) | collective-permute-done | bytes 524320 | tf_op jit(solution)/shard_map/ppermute | solution.py:921
  89.3 1.0 copy-done.10
  90.2 10.7 %gate.1 = (bf16[1024,512]{1,0:T(8,128)(2,1)}, bf16[512,1024]{1,0:T(8,128)(2,1)}, bf16[4,256,1024]{2,1,0:T(8,128)(2,1)}, bf16[1024,512]{1,0:T(8,128)(2,1)}, f32[1024,512]{1,0:T(8,128)}, /*index=5*/f32[8,1024]{1,0:T(8,128)}) custom-call(s32[3]{0:T(128)} %pad_add_fusion.here_ref, s32[2]{0:T(128)} %pad_add_fusion.1.at_ref, ...), custom_call_target="tpu_custom_call" | custom-call | tf_op jit(solution)/shard_map/gate/pallas_call | solution.py:1127
  101.0 1.4 collective-permute-start.10
  102.7 0.5 collective-permute-start.9
  103.2 1.4 collective-permute-done.10.stat_refs_3_
  104.6 2.2 collective-permute-done.9.stat_refs_2_
  106.8 0.6 copy-done.35
  107.4 14.2 %norm_back.1 = (bf16[256,1024]{1,0:T(8,128)(2,1)}, bf16[256,1024]{1,0:T(8,128)(2,1)}, bf16[256,1024]{1,0:T(8,128)(2,1)}, bf16[256,1024]{1,0:T(8,128)(2,1)}, bf16...) custom-call(s32[4]{0:T(128)} %broadcast_xor_fusion.perm_ref, ...), custom_call_target="tpu_custom_call" | custom-call | tf_op jit(solution)/shard_map/norm_back/pallas_call | solution.py:1161
  121.7 1.6 collective-permute-start.11
  123.7 1.4 collective-permute-start.14
  125.1 22.9 %scan_back.1 = (bf16[4,128,512]{2,1,0:T(8,128)(2,1)}, bf16[4,128,512]{2,1,0:T(8,128)(2,1)}, bf16[1024,512]{1,0:T(8,128)(2,1)}, bf16[1024,256]{1,0:T(8,128)(2,1)}...) custom-call(s32[4]{0:T(128)} %broadcast_xor_fusion.perm_ref, ...), custom_call_target="tpu_custom_call" | custom-call | tf_op jit(solution)/shard_map/scan_back/pallas_call | solution.py:1208
  148.6 0.8 copy-done.23
  149.4 1.3 add_convert_fusion
  150.7 3.5 %all-to-all-start.2 = ((bf16[4,256,512]{2,1,0:T(8,128)(2,1)}), bf16[4,256,512]{2,1,0:T(8,128)(2,1)S(1)}, u32[]{:S(2)}, u32[]{:S(2)}) async-start(bf16[4,256,512]{2,1,0:T(8,128)(2,1)} %add_convert_fusion), calls=%async_computation.2 | async-start | bytes 2097152 | tf_op jit(solution)/shard_map/all_to_all | solution.py:932
  154.4 0.5 collective-permute-start.16
  154.9 9.1 %hidden_back.1 = (bf16[256,1024]{1,0:T(8,128)(2,1)}, bf16[256,1024]{1,0:T(8,128)(2,1)}, bf16[256,1024]{1,0:T(8,128)(2,1)}, bf16[256,1024]{1,0:T(8,128)(2,1)}, f32[8,1024]{1,0:T(8,128)}) custom-call(s32[4]{0:T(128)} %broadcast_xor_fusion.perm_ref, bf16[1024,512]{1,0:T(8,128)(2,1)} %get-tuple-element.170.dgate_ref, ...), custom_call_target="tpu_custom_call" | custom-call | tf_op jit(solution)/shard_map/hidden_back/pallas_call | solution.py:1274
  164.1 0.6 collective-permute-start.19
  164.7 1.4 add_add_fusion
  166.1 2.4 %collective-permute-done.16.dbcfar_ref = bf16[1024,256]{1,0:T(8,128)(2,1)S(1)} collective-permute-done((bf16[1024,256]{1,0:T(8,128)(2,1)S(1)}, bf16[1024,256]{1,0:T(8,128)(2,1)S(1)}, u32[]{:S(2)}, u32[]{:S(2)}) %collective-permute-start.16) | collective-permute-done | bytes 524320 | tf_op jit(solution)/shard_map/ppermute | solution.py:921
  168.5 0.8 copy-done.18
  169.3 6.5 %maps_back.1 = (bf16[160,512]{1,0:T(8,128)(2,1)}, bf16[160,512]{1,0:T(8,128)(2,1)}, f32[256,1024]{1,0:T(8,128)}) custom-call(s32[3]{0:T(128)} %pad_add_fusion.here_ref, bf16[1024,256]{1,0:T(8,128)(2,1)} %copy-done.8, bf16[1024,256]{1,0:T(8,128)(2,1)} %copy-done.18, f32[1024,768]{1,0:T(8,128)} %get-tuple-element.152.convsum_ref, ...), custom_call_target="tpu_custom_call" | custom-call | tf_op jit(solution)/shard_map/maps_back/pallas_call | solution.py:1304
  175.8 0.5 collective-permute-start.17
  176.5 4.0 %all-to-all-done.2 = bf16[4,256,512]{2,1,0:T(8,128)(2,1)S(1)} async-done(((bf16[4,256,512]{2,1,0:T(8,128)(2,1)}), bf16[4,256,512]{2,1,0:T(8,128)(2,1)S(1)}, u32[]{:S(2)}, u32[]{:S(2)}) %all-to-all-start.2) | async-done | bytes 1048608 | tf_op jit(solution)/shard_map/all_to_all | solution.py:932
  180.8 1.4 collective-permute-done.17.mcame_ref
  182.2 0.7 copy-done.28
  183.0 2.3 pair_sum_late.1
  185.3 5.0 %all-to-all-start.3 = ((bf16[4,192,512]{2,1,0:T(8,128)(2,1)}), bf16[4,192,512]{2,1,0:T(8,128)(2,1)S(1)}, u32[]{:S(2)}, u32[]{:S(2)}) async-start(bf16[4,192,512]{2,1,0:T(8,128)(2,1)} %pair_sum_late.1), calls=%async_computation.3 | async-start | bytes 1572864 | tf_op jit(solution)/shard_map/all_to_all | solution.py:932
  190.4 1.6 collective-permute-start.21
  192.6 7.0 %collective-permute-done.21.early_refs_2_ = bf16[256,512]{1,0:T(8,128)(2,1)S(1)} collective-permute-done((bf16[256,512]{1,0:T(8,128)(2,1)S(1)}, bf16[256,512]{1,0:T(8,128)(2,1)S(1)}, u32[]{:S(2)}, u32[]{:S(2)}) %collective-permute-start.21) | collective-permute-done | bytes 262176 | tf_op jit(solution)/shard_map/ppermute | solution.py:921
  199.6 1.5 collective-permute-done.22.early_refs_3_
  201.2 0.7 copy-done.13
  201.9 5.5 %adam_out.1 = (f32[256,1024]{1,0:T(8,128)}, f32[256,1024]{1,0:T(8,128)}, f32[256,1024]{1,0:T(8,128)}) custom-call(s32[3]{0:T(128)} %pad_add_fusion.here_ref, f32[256,1024]{1,0:T(8,128)} %weight_ref.2, f32[256,1024]{1,0:T(8,128)} %first_ref.2, f32[256,1024]{1,0:T(8,128)} %second_ref.2, bf16[256,512]{1,0:T(8,128)(2,1)} %copy-done.6, ...), custom_call_target="tpu_custom_call" | custom-call | tf_op jit(solution)/shard_map/adam_out/pallas_call | solution.py:1387
  207.4 2.7 %all-to-all-done.3.parts_ref = bf16[4,192,512]{2,1,0:T(8,128)(2,1)S(1)} async-done(((bf16[4,192,512]{2,1,0:T(8,128)(2,1)}), bf16[4,192,512]{2,1,0:T(8,128)(2,1)S(1)}, u32[]{:S(2)}, u32[]{:S(2)}) %all-to-all-start.3) | async-done | bytes 786464 | tf_op jit(solution)/shard_map/all_to_all | solution.py:932
  210.1 0.9 copy-done.5
  210.9 1.9 sum_late.1.late_refs_0_
  212.9 1.8 collective-permute-start.24
  214.9 0.8 copy-done.14
  215.8 3.9 %input_back.1 = f32[256,1024]{1,0:T(8,128)} custom-call(bf16[256,1024]{1,0:T(8,128)(2,1)} %get-tuple-element.195.part_refs_0_, bf16[256,1024]{1,0:T(8,128)(2,1)} %copy-done.14, bf16[256,1024]{1,0:T(8,128)(2,1)} %copy-done.15, f32[256,1024]{1,0:T(8,128)} %get-tuple-element.198.own_ref, f32[256,1024]{1,0:T(8,128)} %bitcast.45, ...), custom_call_target="tpu_custom_call" | custom-call | tf_op jit(solution)/shard_map/input_back/pallas_call | solution.py:1358
  219.9 0.9 collective-permute-done.24.late_refs_2_
  220.8 3.6 %collective-permute-done.25.late_refs_3_ = bf16[192,512]{1,0:T(8,128)(2,1)S(1)} collective-permute-done((bf16[192,512]{1,0:T(8,128)(2,1)}, bf16[192,512]{1,0:T(8,128)(2,1)S(1)}, u32[]{:S(2)}, u32[]{:S(2)}) %collective-permute-start.25) | collective-permute-done | bytes 196640 | tf_op jit(solution)/shard_map/ppermute | solution.py:921
  224.4 0.8 slice_bitcast_fusion.3
  225.2 0.6 gather_fusion
  227.1 0.6 multiply_subtract_fusion
  227.7 0.6 multiply_subtract_fusion.2
  228.4 0.7 multiply_subtract_fusion.3
  229.1 0.7 multiply_subtract_fusion.1
  229.8 8.3 %adam_in.1 = (f32[128,4352]{1,0:T(8,128)}, f32[128,4352]{1,0:T(8,128)}, f32[128,4352]{1,0:T(8,128)}) custom-call(s32[3]{0:T(128)} %pad_add_fusion.here_ref, f32[128,4352]{1,0:T(8,128)} %weight_ref.3, f32[128,4352]{1,0:T(8,128)} %first_ref.3, f32[128,4352]{1,0:T(8,128)} %second_ref.3, bf16[256,512]{1,0:T(8,128)(2,1)} %copy-done.6, ...), custom_call_target="tpu_custom_call" | custom-call | tf_op jit(solution)/shard_map/adam_in/pallas_call | solution.py:1412
  (158 shorter events, 5.5 us)
Async XLA Ops:
  1.2 10.1 %copy-start = (f32[1,256,1024]{2,1,0:T(8,128)S(1)}, f32[1,256,1024]{2,1,0:T(8,128)}, u32[]{:S(2)}) copy-start(f32[1,256,1024]{2,1,0:T(8,128)} %param.22) | copy-start | bytes 3145732
  1.2 11.6 %copy-start.2 = (f32[1,256,1024]{2,1,0:T(8,128)S(1)}, f32[1,256,1024]{2,1,0:T(8,128)}, u32[]{:S(2)}) copy-start(f32[1,256,1024]{2,1,0:T(8,128)} %param.24) | copy-start | bytes 3145732
  4.8 8.1 %copy-start.46 = (s32[4]{0:T(128)S(1)}, s32[4]{0:T(128)}, u32[]{:S(2)}) copy-start(s32[4]{0:T(128)} %constant.15.clone) | copy-start | bytes 52
  4.8 8.7 %copy-start.41 = (f32[3,32]{1,0:T(4,128)S(1)}, f32[3,32]{1,0:T(4,128)}, u32[]{:S(2)}) copy-start(f32[3,32]{1,0:T(4,128)} %param.30) | copy-start | bytes 1156
  4.8 9.6 %copy-start.31 = (s32[1,1024]{1,0:T(1,128)S(1)}, s32[1,1024]{1,0:T(1,128)}, u32[]{:S(2)}) copy-start(s32[1,1024]{1,0:T(1,128)} %segr_ref.3) | copy-start | bytes 12292
  4.8 28.7 %all-to-all-start = ((bf16[4,144,768]{2,1,0:T(8,128)(2,1)}), bf16[4,144,768]{2,1,0:T(8,128)(2,1)S(1)}, u32[]{:S(2)}, u32[]{:S(2)}) async-start(bf16[4,144,768]{2,1,0:T(8,128)(2,1)} %get-tuple-element.115), calls=%async_computation | async-start | bytes 1769472 | tf_op jit(solution)/shard_map/all_to_all | solution.py:932
  11.3 27.3 %collective-permute-start.1 = (f32[256,1024]{1,0:T(8,128)S(1)}, f32[256,1024]{1,0:T(8,128)}, u32[]{:S(2)}, u32[]{:S(2)}) collective-permute-start(f32[256,1024]{1,0:T(8,128)S(1)} %bitcast.46), channel_id=1, source_target_pairs={{0,2},{1,3},{2,0},{3,1},{4,6},{5,7},{6,4},{7,5},{8,10},{9,11},{10,... | collective-permute-start | bytes 3145736 | tf_op jit(solution)/shard_map/ppermute | solution.py:921
  12.9 72.7 %copy-start.7 = (bf16[256,1024]{1,0:T(8,128)(2,1)}, bf16[256,1024]{1,0:T(8,128)(2,1)S(1)}, u32[]{:S(2)}) copy-start(bf16[256,1024]{1,0:T(8,128)(2,1)S(1)} %bitcast_convert_fusion.cot_pieces_0_) | copy-start | bytes 1572868
  13.7 53.2 %copy-start.32 = (f32[3,8]{1,0:T(4,128)}, f32[3,8]{1,0:T(4,128)S(1)}, u32[]{:S(2)}) copy-start(f32[3,8]{1,0:T(4,128)S(1)} %dynamic-slice_reduce_fusion.hrow_ref) | copy-start | bytes 292
  33.5 33.4 %copy-start.4 = (bf16[4,144,768]{2,1,0:T(8,128)(2,1)}, bf16[4,144,768]{2,1,0:T(8,128)(2,1)S(1)}, u32[]{:S(2)}) copy-start(bf16[4,144,768]{2,1,0:T(8,128)(2,1)S(1)} %all-to-all-done.w1_pieces_0_) | copy-start | bytes 2654212
  33.5 20.7 %collective-permute-start = (bf16[4,144,768]{2,1,0:T(8,128)(2,1)S(1)}, bf16[4,144,768]{2,1,0:T(8,128)(2,1)}, u32[]{:S(2)}, u32[]{:S(2)}) collective-permute-start(bf16[4,144,768]{2,1,0:T(8,128)(2,1)S(1)} %all-to-all-done.w1_pieces_0_), channel_id=1, source_target_pairs={{0,4},{4,0},{8,12},{12,8},{16,20},{20,16},{24,28},{28,24},{1,5},{5... | collective-permute-start | bytes 2654216 | tf_op jit(solution)/shard_map/ppermute | solution.py:921
  35.0 28.4 %all-to-all-start.1 = ((bf16[4,256,512]{2,1,0:T(8,128)(2,1)}), bf16[4,256,512]{2,1,0:T(8,128)(2,1)S(1)}, u32[]{:S(2)}, u32[]{:S(2)}) async-start(bf16[4,256,512]{2,1,0:T(8,128)(2,1)} %get-tuple-element.123), calls=%async_computation.1 | async-start | bytes 2097152 | tf_op jit(solution)/shard_map/all_to_all | solution.py:932
  38.5 15.7 %collective-permute-start.2 = (f32[256,1024]{1,0:T(8,128)S(1)}, f32[256,1024]{1,0:T(8,128)}, u32[]{:S(2)}, u32[]{:S(2)}) collective-permute-start(f32[256,1024]{1,0:T(8,128)S(1)} %bitcast.47), channel_id=1, source_target_pairs={{0,1},{1,0},{2,3},{3,2},{4,5},{5,4},{6,7},{7,6},{8,9},{9,8},{10,11... | collective-permute-start | bytes 3145736 | tf_op jit(solution)/shard_map/ppermute | solution.py:921
  54.2 9.2 %collective-permute-start.3 = (f32[256,1024]{1,0:T(8,128)}, f32[256,1024]{1,0:T(8,128)}, u32[]{:S(2)}, u32[]{:S(2)}) collective-permute-start(f32[256,1024]{1,0:T(8,128)} %collective-permute-done.1.tok_pieces_2_), channel_id=1, source_target_pairs={{0,1},{1,0},{2,3},{3,2},{4,5},{5,4},{6,7},{7,6},{8,9},{9,8},{10,11... | collective-permute-start | bytes 3145736 | tf_op jit(solution)/shard_map/ppermute | solution.py:921
  63.4 22.2 %copy-start.3 = (bf16[4,256,512]{2,1,0:T(8,128)(2,1)}, bf16[4,256,512]{2,1,0:T(8,128)(2,1)S(1)}, u32[]{:S(2)}) copy-start(bf16[4,256,512]{2,1,0:T(8,128)(2,1)S(1)} %all-to-all-done.1.g2_pieces_0_) | copy-start | bytes 3145732
  63.4 25.8 %collective-permute-start.4 = (bf16[4,256,512]{2,1,0:T(8,128)(2,1)S(1)}, bf16[4,256,512]{2,1,0:T(8,128)(2,1)S(1)}, u32[]{:S(2)}, u32[]{:S(2)}) collective-permute-start(bf16[4,256,512]{2,1,0:T(8,128)(2,1)S(1)} %all-to-all-done.1.g2_pieces_0_), channel_id=1, source_target_pairs={{0,4},{4,0},{8,12},{12,8},{16,20},{20,16},{24,28},{28,24},{1,5},{5... | collective-permute-start | bytes 3145736 | tf_op jit(solution)/shard_map/ppermute | solution.py:921
  64.0 21.7 %collective-permute-start.5 = (bf16[256,1024]{1,0:T(8,128)(2,1)S(1)}, bf16[256,1024]{1,0:T(8,128)(2,1)}, u32[]{:S(2)}, u32[]{:S(2)}) collective-permute-start(bf16[256,1024]{1,0:T(8,128)(2,1)S(1)} %bitcast_convert_fusion.cot_pieces_0_), channel_id=1, source_target_pairs={{0,1},{1,0},{2,3},{3,2},{4,5},{5,4},{6,7},{7,6},{8,9},{9,8},{10,11... | collective-permute-start | bytes 1572872 | tf_op jit(solution)/shard_map/ppermute | solution.py:921
  64.0 21.7 %collective-permute-start.6 = (bf16[256,1024]{1,0:T(8,128)(2,1)S(1)}, bf16[256,1024]{1,0:T(8,128)(2,1)}, u32[]{:S(2)}, u32[]{:S(2)}) collective-permute-start(bf16[256,1024]{1,0:T(8,128)(2,1)S(1)} %bitcast_convert_fusion.cot_pieces_0_), channel_id=1, source_target_pairs={{0,2},{1,3},{2,0},{3,1},{4,6},{5,7},{6,4},{7,5},{8,10},{9,11},{10,... | collective-permute-start | bytes 1572872 | tf_op jit(solution)/shard_map/ppermute | solution.py:921
  65.5 23.8 %collective-permute-start.7 = (bf16[256,1024]{1,0:T(8,128)(2,1)S(1)}, bf16[256,1024]{1,0:T(8,128)(2,1)}, u32[]{:S(2)}, u32[]{:S(2)}) collective-permute-start(bf16[256,1024]{1,0:T(8,128)(2,1)S(1)} %bitcast_convert_fusion.cot_pieces_0_), channel_id=1, source_target_pairs={{0,3},{1,2},{2,1},{3,0},{4,7},{5,6},{6,5},{7,4},{8,11},{9,10},{10,... | collective-permute-start | bytes 1572872 | tf_op jit(solution)/shard_map/ppermute | solution.py:921
  101.0 3.6 %collective-permute-start.10 = (f32[8,1024]{1,0:T(8,128)}, f32[8,1024]{1,0:T(8,128)S(1)}, u32[]{:S(2)}, u32[]{:S(2)}) collective-permute-start(f32[8,1024]{1,0:T(8,128)} %get-tuple-element.141.stat_refs_0_), channel_id=1, source_target_pairs={{0,3},{1,2},{2,1},{3,0},{4,7},{5,6},{6,5},{7,4},{8,11},{9,10},{10,... | collective-permute-start | bytes 98312 | tf_op jit(solution)/shard_map/ppermute | solution.py:921
  102.4 2.2 collective-permute-start.8
  102.7 4.1 %collective-permute-start.9 = (f32[8,1024]{1,0:T(8,128)}, f32[8,1024]{1,0:T(8,128)S(1)}, u32[]{:S(2)}, u32[]{:S(2)}) collective-permute-start(f32[8,1024]{1,0:T(8,128)} %get-tuple-element.141.stat_refs_0_), channel_id=1, source_target_pairs={{0,2},{1,3},{2,0},{3,1},{4,6},{5,7},{6,4},{7,5},{8,10},{9,11},{10,... | collective-permute-start | bytes 98312 | tf_op jit(solution)/shard_map/ppermute | solution.py:921
  121.7 27.0 %collective-permute-start.11 = (bf16[4,256,512]{2,1,0:T(8,128)(2,1)}, bf16[4,256,512]{2,1,0:T(8,128)(2,1)S(1)}, u32[]{:S(2)}, u32[]{:S(2)}) collective-permute-start(bf16[4,256,512]{2,1,0:T(8,128)(2,1)} %get-tuple-element.145), channel_id=1, source_target_pairs={{0,4},{4,0},{8,12},{12,8},{16,20},{20,16},{24,28},{28,24},{1,5},{5... | collective-permute-start | bytes 3145736 | tf_op jit(solution)/shard_map/ppermute | solution.py:921
  123.2 25.2 %collective-permute-start.12 = (bf16[256,1024]{1,0:T(8,128)(2,1)}, bf16[256,1024]{1,0:T(8,128)(2,1)S(1)}, u32[]{:S(2)}, u32[]{:S(2)}) collective-permute-start(bf16[256,1024]{1,0:T(8,128)(2,1)} %get-tuple-element.146), channel_id=1, source_target_pairs={{0,1},{1,0},{2,3},{3,2},{4,5},{5,4},{6,7},{7,6},{8,9},{9,8},{10,11... | collective-permute-start | bytes 1572872 | tf_op jit(solution)/shard_map/ppermute | solution.py:921
  123.2 25.2 %collective-permute-start.13 = (bf16[256,1024]{1,0:T(8,128)(2,1)}, bf16[256,1024]{1,0:T(8,128)(2,1)S(1)}, u32[]{:S(2)}, u32[]{:S(2)}) collective-permute-start(bf16[256,1024]{1,0:T(8,128)(2,1)} %get-tuple-element.147), channel_id=1, source_target_pairs={{0,2},{1,3},{2,0},{3,1},{4,6},{5,7},{6,4},{7,5},{8,10},{9,11},{10,... | collective-permute-start | bytes 1572872 | tf_op jit(solution)/shard_map/ppermute | solution.py:921
  123.7 24.9 %collective-permute-start.14 = (bf16[256,1024]{1,0:T(8,128)(2,1)}, bf16[256,1024]{1,0:T(8,128)(2,1)S(1)}, u32[]{:S(2)}, u32[]{:S(2)}) collective-permute-start(bf16[256,1024]{1,0:T(8,128)(2,1)} %get-tuple-element.148), channel_id=1, source_target_pairs={{0,3},{1,2},{2,1},{3,0},{4,7},{5,6},{6,5},{7,4},{8,11},{9,10},{10,... | collective-permute-start | bytes 1572872 | tf_op jit(solution)/shard_map/ppermute | solution.py:921
  125.1 24.3 %copy-start.9 = (bf16[4,256,512]{2,1,0:T(8,128)(2,1)S(1)}, bf16[4,256,512]{2,1,0:T(8,128)(2,1)}, u32[]{:S(2)}) copy-start(bf16[4,256,512]{2,1,0:T(8,128)(2,1)} %get-tuple-element.181) | copy-start | bytes 3145732
  148.0 6.2 %collective-permute-start.15 = (bf16[1024,256]{1,0:T(8,128)(2,1)}, bf16[1024,256]{1,0:T(8,128)(2,1)S(1)}, u32[]{:S(2)}, u32[]{:S(2)}) collective-permute-start(bf16[1024,256]{1,0:T(8,128)(2,1)} %get-tuple-element.162), channel_id=1, source_target_pairs={{0,1},{1,0},{2,3},{3,2},{4,5},{5,4},{6,7},{7,6},{8,9},{9,8},{10,11... | collective-permute-start | bytes 1572872 | tf_op jit(solution)/shard_map/ppermute | solution.py:921
  149.4 4.8 %copy-start.17 = (bf16[1024,256]{1,0:T(8,128)(2,1)S(1)}, bf16[1024,256]{1,0:T(8,128)(2,1)}, u32[]{:S(2)}) copy-start(bf16[1024,256]{1,0:T(8,128)(2,1)} %get-tuple-element.162) | copy-start | bytes 1572868
  150.7 29.9 %all-to-all-start.2 = ((bf16[4,256,512]{2,1,0:T(8,128)(2,1)}), bf16[4,256,512]{2,1,0:T(8,128)(2,1)S(1)}, u32[]{:S(2)}, u32[]{:S(2)}) async-start(bf16[4,256,512]{2,1,0:T(8,128)(2,1)} %add_convert_fusion), calls=%async_computation.2 | async-start | bytes 2097152 | tf_op jit(solution)/shard_map/all_to_all | solution.py:932
  154.4 9.7 %copy-start.8 = (bf16[1024,256]{1,0:T(8,128)(2,1)}, bf16[1024,256]{1,0:T(8,128)(2,1)S(1)}, u32[]{:S(2)}) copy-start(bf16[1024,256]{1,0:T(8,128)(2,1)S(1)} %add_convert_fusion.2.dbc_ref) | copy-start | bytes 1572868
  154.4 14.1 %collective-permute-start.16 = (bf16[1024,256]{1,0:T(8,128)(2,1)S(1)}, bf16[1024,256]{1,0:T(8,128)(2,1)S(1)}, u32[]{:S(2)}, u32[]{:S(2)}) collective-permute-start(bf16[1024,256]{1,0:T(8,128)(2,1)S(1)} %add_convert_fusion.2.dbc_ref), channel_id=1, source_target_pairs={{0,2},{1,3},{2,0},{3,1},{4,6},{5,7},{6,4},{7,5},{8,10},{9,11},{10,... | collective-permute-start | bytes 1572872 | tf_op jit(solution)/shard_map/ppermute | solution.py:921
  154.9 9.8 %copy-start.1 = (f32[1,256,1024]{2,1,0:T(8,128)S(1)}, f32[1,256,1024]{2,1,0:T(8,128)}, u32[]{:S(2)}) copy-start(f32[1,256,1024]{2,1,0:T(8,128)} %param.22) | copy-start | bytes 3145732
  154.9 9.8 %copy-start.20 = (bf16[256,1024]{1,0:T(8,128)(2,1)S(1)}, bf16[256,1024]{1,0:T(8,128)(2,1)}, u32[]{:S(2)}) copy-start(bf16[256,1024]{1,0:T(8,128)(2,1)} %get-tuple-element.180) | copy-start | bytes 1572868
  154.9 9.8 %copy-start.22 = (bf16[256,1024]{1,0:T(8,128)(2,1)S(1)}, bf16[256,1024]{1,0:T(8,128)(2,1)}, u32[]{:S(2)}) copy-start(bf16[256,1024]{1,0:T(8,128)(2,1)} %copy-done.21) | copy-start | bytes 1572868
  154.9 9.8 %copy-start.24 = (bf16[256,1024]{1,0:T(8,128)(2,1)S(1)}, bf16[256,1024]{1,0:T(8,128)(2,1)}, u32[]{:S(2)}) copy-start(bf16[256,1024]{1,0:T(8,128)(2,1)} %copy-done.23) | copy-start | bytes 1572868
  164.0 12.3 %collective-permute-start.18 = (bf16[256,1024]{1,0:T(8,128)(2,1)}, bf16[256,1024]{1,0:T(8,128)(2,1)S(1)}, u32[]{:S(2)}, u32[]{:S(2)}) collective-permute-start(bf16[256,1024]{1,0:T(8,128)(2,1)} %get-tuple-element.184), channel_id=1, source_target_pairs={{0,1},{1,0},{2,3},{3,2},{4,5},{5,4},{6,7},{7,6},{8,9},{9,8},{10,11... | collective-permute-start | bytes 1572872 | tf_op jit(solution)/shard_map/ppermute | solution.py:921
  164.1 18.1 %collective-permute-start.19 = (bf16[4,128,512]{2,1,0:T(8,128)(2,1)}, bf16[4,128,512]{2,1,0:T(8,128)(2,1)S(1)}, u32[]{:S(2)}, u32[]{:S(2)}) collective-permute-start(bf16[4,128,512]{2,1,0:T(8,128)(2,1)} %get-tuple-element.187), channel_id=1, source_target_pairs={{0,4},{4,0},{8,12},{12,8},{16,20},{20,16},{24,28},{28,24},{1,5},{5... | collective-permute-start | bytes 1572872 | tf_op jit(solution)/shard_map/ppermute | solution.py:921
  169.3 7.1 %copy-start.16 = (bf16[256,1024]{1,0:T(8,128)(2,1)S(1)}, bf16[256,1024]{1,0:T(8,128)(2,1)}, u32[]{:S(2)}) copy-start(bf16[256,1024]{1,0:T(8,128)(2,1)} %get-tuple-element.183) | copy-start | bytes 1572868
  175.8 6.4 %collective-permute-start.17 = (bf16[160,512]{1,0:T(8,128)(2,1)}, bf16[160,512]{1,0:T(8,128)(2,1)S(1)}, u32[]{:S(2)}, u32[]{:S(2)}) collective-permute-start(bf16[160,512]{1,0:T(8,128)(2,1)} %get-tuple-element.176), channel_id=1, source_target_pairs={{0,4},{4,0},{8,12},{12,8},{16,20},{20,16},{24,28},{28,24},{1,5},{5... | collective-permute-start | bytes 491528 | tf_op jit(solution)/shard_map/ppermute | solution.py:921
  180.8 20.4 %copy-start.6 = (bf16[256,512]{1,0:T(8,128)(2,1)}, bf16[256,512]{1,0:T(8,128)(2,1)S(1)}, u32[]{:S(2)}) copy-start(bf16[256,512]{1,0:T(8,128)(2,1)S(1)} %reduce_sum.30.early_refs_0_) | copy-start | bytes 786436
  185.3 24.7 %all-to-all-start.3 = ((bf16[4,192,512]{2,1,0:T(8,128)(2,1)}), bf16[4,192,512]{2,1,0:T(8,128)(2,1)S(1)}, u32[]{:S(2)}, u32[]{:S(2)}) async-start(bf16[4,192,512]{2,1,0:T(8,128)(2,1)} %pair_sum_late.1), calls=%async_computation.3 | async-start | bytes 1572864 | tf_op jit(solution)/shard_map/all_to_all | solution.py:932
  190.4 9.2 %collective-permute-start.21 = (bf16[256,512]{1,0:T(8,128)(2,1)S(1)}, bf16[256,512]{1,0:T(8,128)(2,1)S(1)}, u32[]{:S(2)}, u32[]{:S(2)}) collective-permute-start(bf16[256,512]{1,0:T(8,128)(2,1)S(1)} %reduce_sum.30.early_refs_0_), channel_id=1, source_target_pairs={{0,2},{1,3},{2,0},{3,1},{4,6},{5,7},{6,4},{7,5},{8,10},{9,11},{10,... | collective-permute-start | bytes 786440 | tf_op jit(solution)/shard_map/ppermute | solution.py:921
  191.9 22.9 %collective-permute-start.26 = (bf16[256,1024]{1,0:T(8,128)(2,1)}, bf16[256,1024]{1,0:T(8,128)(2,1)S(1)}, u32[]{:S(2)}, u32[]{:S(2)}) collective-permute-start(bf16[256,1024]{1,0:T(8,128)(2,1)} %get-tuple-element.196), channel_id=1, source_target_pairs={{0,1},{1,0},{2,3},{3,2},{4,5},{5,4},{6,7},{7,6},{8,9},{9,8},{10,11... | collective-permute-start | bytes 1572872 | tf_op jit(solution)/shard_map/ppermute | solution.py:921
  191.9 22.9 %collective-permute-start.27 = (bf16[256,1024]{1,0:T(8,128)(2,1)S(1)}, bf16[256,1024]{1,0:T(8,128)(2,1)S(1)}, u32[]{:S(2)}, u32[]{:S(2)}) collective-permute-start(bf16[256,1024]{1,0:T(8,128)(2,1)S(1)} %add_convert_fusion.1), channel_id=1, source_target_pairs={{0,2},{1,3},{2,0},{3,1},{4,6},{5,7},{6,4},{7,5},{8,10},{9,11},{10,... | collective-permute-start | bytes 1572872 | tf_op jit(solution)/shard_map/ppermute | solution.py:921
  192.4 7.2 %collective-permute-start.20 = (bf16[256,512]{1,0:T(8,128)(2,1)S(1)}, bf16[256,512]{1,0:T(8,128)(2,1)S(1)}, u32[]{:S(2)}, u32[]{:S(2)}) collective-permute-start(bf16[256,512]{1,0:T(8,128)(2,1)S(1)} %reduce_sum.30.early_refs_0_), channel_id=1, source_target_pairs={{0,1},{1,0},{2,3},{3,2},{4,5},{5,4},{6,7},{7,6},{8,9},{9,8},{10,11... | collective-permute-start | bytes 786440 | tf_op jit(solution)/shard_map/ppermute | solution.py:921
  199.6 1.5 collective-permute-start.22
  212.9 7.0 %collective-permute-start.23 = (bf16[192,512]{1,0:T(8,128)(2,1)}, bf16[192,512]{1,0:T(8,128)(2,1)S(1)}, u32[]{:S(2)}, u32[]{:S(2)}) collective-permute-start(bf16[192,512]{1,0:T(8,128)(2,1)} %sum_late.1.late_refs_0_), channel_id=1, source_target_pairs={{0,1},{1,0},{2,3},{3,2},{4,5},{5,4},{6,7},{7,6},{8,9},{9,8},{10,11... | collective-permute-start | bytes 589832 | tf_op jit(solution)/shard_map/ppermute | solution.py:921
  212.9 7.9 %collective-permute-start.24 = (bf16[192,512]{1,0:T(8,128)(2,1)}, bf16[192,512]{1,0:T(8,128)(2,1)S(1)}, u32[]{:S(2)}, u32[]{:S(2)}) collective-permute-start(bf16[192,512]{1,0:T(8,128)(2,1)} %sum_late.1.late_refs_0_), channel_id=1, source_target_pairs={{0,2},{1,3},{2,0},{3,1},{4,6},{5,7},{6,4},{7,5},{8,10},{9,11},{10,... | collective-permute-start | bytes 589832 | tf_op jit(solution)/shard_map/ppermute | solution.py:921
  214.7 9.7 %collective-permute-start.25 = (bf16[192,512]{1,0:T(8,128)(2,1)}, bf16[192,512]{1,0:T(8,128)(2,1)S(1)}, u32[]{:S(2)}, u32[]{:S(2)}) collective-permute-start(bf16[192,512]{1,0:T(8,128)(2,1)} %sum_late.1.late_refs_0_), channel_id=1, source_target_pairs={{0,3},{1,2},{2,1},{3,0},{4,7},{5,6},{6,5},{7,4},{8,11},{9,10},{10,... | collective-permute-start | bytes 589832 | tf_op jit(solution)/shard_map/ppermute | solution.py:921
  219.7 7.3 %copy-start.29 = (f32[32,128]{1,0:T(8,128)S(1)}, f32[32,128]{1,0:T(8,128)}, u32[]{:S(2)}) copy-start(f32[32,128]{1,0:T(8,128)} %dt_ref.1) | copy-start | bytes 49156
  219.7 7.4 %copy-start.36 = (f32[32,128]{1,0:T(8,128)S(1)}, f32[32,128]{1,0:T(8,128)}, u32[]{:S(2)}) copy-start(f32[32,128]{1,0:T(8,128)} %param.33) | copy-start | bytes 49156
  219.7 7.4 %copy-start.37 = (f32[32,128]{1,0:T(8,128)S(1)}, f32[32,128]{1,0:T(8,128)}, u32[]{:S(2)}) copy-start(f32[32,128]{1,0:T(8,128)} %param.34) | copy-start | bytes 49156
  219.7 8.0 %copy-start.42 = (f32[3,32]{1,0:T(4,128)S(1)}, f32[3,32]{1,0:T(4,128)}, u32[]{:S(2)}) copy-start(f32[3,32]{1,0:T(4,128)} %param.41) | copy-start | bytes 1156
  219.7 8.0 %copy-start.43 = (f32[3,32]{1,0:T(4,128)S(1)}, f32[3,32]{1,0:T(4,128)}, u32[]{:S(2)}) copy-start(f32[3,32]{1,0:T(4,128)} %param.42) | copy-start | bytes 1156
  219.8 8.6 %copy-start.40 = (f32[384]{0:T(512)S(1)}, f32[384]{0:T(512)}, u32[]{:S(2)}) copy-start(f32[384]{0:T(512)} %gain_ref.1) | copy-start | bytes 4612
  219.8 8.6 %copy-start.44 = (f32[384]{0:T(512)S(1)}, f32[384]{0:T(512)}, u32[]{:S(2)}) copy-start(f32[384]{0:T(512)} %param.39) | copy-start | bytes 4612
  219.8 8.6 %copy-start.45 = (f32[384]{0:T(512)S(1)}, f32[384]{0:T(512)}, u32[]{:S(2)}) copy-start(f32[384]{0:T(512)} %param.40) | copy-start | bytes 4612
  219.8 9.3 %copy-start.30 = (f32[5,288]{1,0:T(8,128)S(1)}, f32[5,288]{1,0:T(8,128)}, u32[]{:S(2)}) copy-start(f32[5,288]{1,0:T(8,128)} %conv_ref.1) | copy-start | bytes 17284
  219.8 9.3 %copy-start.38 = (f32[5,288]{1,0:T(8,128)S(1)}, f32[5,288]{1,0:T(8,128)}, u32[]{:S(2)}) copy-start(f32[5,288]{1,0:T(8,128)} %param.37) | copy-start | bytes 17284
  219.8 9.2 %copy-start.39 = (f32[5,288]{1,0:T(8,128)S(1)}, f32[5,288]{1,0:T(8,128)}, u32[]{:S(2)}) copy-start(f32[5,288]{1,0:T(8,128)} %param.38) | copy-start | bytes 17284
  219.8 10.0 %copy-start.25 = (bf16[192,512]{1,0:T(8,128)(2,1)}, bf16[192,512]{1,0:T(8,128)(2,1)S(1)}, u32[]{:S(2)}) copy-start(bf16[192,512]{1,0:T(8,128)(2,1)S(1)} %collective-permute-done.23.late_refs_1_) | copy-start | bytes 589828
  220.8 9.0 %copy-start.26 = (bf16[192,512]{1,0:T(8,128)(2,1)}, bf16[192,512]{1,0:T(8,128)(2,1)S(1)}, u32[]{:S(2)}) copy-start(bf16[192,512]{1,0:T(8,128)(2,1)S(1)} %collective-permute-done.24.late_refs_2_) | copy-start | bytes 589828
  224.3 5.4 %copy-start.27 = (bf16[192,512]{1,0:T(8,128)(2,1)}, bf16[192,512]{1,0:T(8,128)(2,1)S(1)}, u32[]{:S(2)}) copy-start(bf16[192,512]{1,0:T(8,128)(2,1)S(1)} %collective-permute-done.25.late_refs_3_) | copy-start | bytes 589828
  (15 other events, 17.8 us)
